TPU v7x, 32 devices: a whole 2x2x4 slice. The times are simulated.
32 devices in a mesh: req: 8 (over y, x, core), mlp: 4 (over z).
Axes of the slice: x: 2, y: 2, z: 4, core: 2. Of those that a mesh axis runs over, the one named last changes fastest.
Arguments:
- layer_input: bfloat16 [1024, 4096], P(('req', 'mlp')), may hold values from -6 to 6
- request_lengths: int32 [8, 4], P('req'), may hold values from 1 to 80, 128 in all within a row
- request_adapter: int32 [8, 4], P('req'), may hold values from 0 to 63, as said below
- slot_adapter_index: int32 [8], replicated, may hold values from 0 to 63, as said below
- query_weight: bfloat16 [4096, 2048], P(None, 'mlp'), may hold values from -0.09375 to 0.09375
- key_weight: bfloat16 [4096, 2048], P(None, 'mlp'), may hold values from -0.09375 to 0.09375
- value_weight: bfloat16 [4096, 2048], P(None, 'mlp'), may hold values from -0.09375 to 0.09375
- output_weight: bfloat16 [2048, 4096], P('mlp'), may hold values from -0.125 to 0.125
- query_norm_gain: float32 [2048], P('mlp'), may hold values from 0.1 to 1.9
- key_norm_gain: float32 [2048], P('mlp'), may hold values from 0.1 to 1.9
- query_down_factors: bfloat16 [4096, 128], replicated, may hold values from -0.09375 to 0.09375
- value_down_factors: bfloat16 [4096, 128], replicated, may hold values from -0.09375 to 0.09375
- query_up_factors: bfloat16 [128, 2048], P(None, 'mlp'), may hold values from -1.5 to 1.5
- value_up_factors: bfloat16 [128, 2048], P(None, 'mlp'), may hold values from -1.5 to 1.5
- attention_norm_gain: float32 [4096], replicated, may hold values from 0.1 to 1.9
- feedforward_norm_gain: float32 [4096], replicated, may hold values from 0.1 to 1.9
- gate_weight: bfloat16 [4096, 6144], P(None, ('req', 'mlp')), may hold values from -0.09375 to 0.09375
- up_weight: bfloat16 [4096, 6144], P(None, ('req', 'mlp')), may hold values from -0.09375 to 0.09375
- down_weight_transposed: bfloat16 [4096, 6144], P(None, ('req', 'mlp')), may hold values from -0.078125 to 0.078125
Outputs:
- layer_out: bfloat16 [1024, 4096], P(('req', 'mlp'))
Inputs may be any that keep to these rules, and one draw needn't show every extreme that they name: `request_lengths`: the lengths of a group's requests sum to 128, and the longest request of every group has exactly 80 tokens. `slot_adapter_index`: 8 distinct adapter numbers. `request_adapter`: every request's adapter is one of the numbers in slot_adapter_index.
All inputs are finite; a program needn't handle non-finite values.
Results may differ from a plain program's by a relative error of at most 0.024.
Values may be sent and summed in bfloat16 or wider, within the bound.
No kernel may reach another device: no remote copies, remote signals or barrier semaphores. Data moves between devices by JAX's collectives and lax.ppermute only.
A program may use at most 128 MiB of HBM per device.

v0:
```python
import jax
import jax.numpy as jnp
from jax import lax
from jax.sharding import PartitionSpec as P

HEAD_SIZE = 128
ADAPTER_RANK = 16
ADAPTER_SLOTS = 8
SINKS = 4


epsilon = 1e-06
adapter_scale = 0.5
rope_theta = 500000.0


def rms_scale(inputs):
    return inputs * lax.rsqrt(jnp.mean(inputs * inputs, axis=-1, keepdims=True) + epsilon)


def rotary(inputs, position):
    half_dim = inputs.shape[-1] // 2
    exponent = jnp.arange(half_dim, dtype=jnp.float32) * (2.0 / inputs.shape[-1])
    frequency = rope_theta ** (-exponent)
    angles = position.astype(jnp.float32)[:, None] * frequency[None, :]
    cosine = jnp.cos(angles)[:, None, :]
    sine_part = jnp.sin(angles)[:, None, :]
    first_half = inputs[..., :half_dim]
    second = inputs[..., half_dim:]
    return jnp.concatenate(
        [first_half * cosine - second * sine_part, second * cosine + first_half * sine_part],
        axis=-1,
    )


def layout(lengths, adapters, slot_adapter_index, row_count):
    req_ends = jnp.cumsum(lengths)
    starts = req_ends - lengths
    places = jnp.arange(row_count, dtype=jnp.int32)
    member = ((places[:, None] >= starts[None, :]) & (places[:, None] < req_ends[None, :])).astype(
        jnp.int32
    )
    request = jnp.sum(member * jnp.arange(lengths.shape[0], dtype=jnp.int32)[None, :], axis=1)
    position = places - jnp.sum(member * starts[None, :], axis=1)
    chosen = jnp.sum(member * adapters[None, :], axis=1)
    slot_ids = jnp.arange(slot_adapter_index.shape[0], dtype=jnp.int32)
    token_slot = jnp.sum(
        (chosen[:, None] == slot_adapter_index[None, :]).astype(jnp.int32) * slot_ids[None, :],
        axis=1,
    )
    return (request, position, token_slot)


def attention(queries, key_heads, value_heads, request, position, window):
    scores = jnp.einsum(
        "qhd,khd->hqk", queries, key_heads, preferred_element_type=jnp.float32
    ) * HEAD_SIZE ** (-0.5)
    distance = position[:, None] - position[None, :]
    allowed = (
        (request[:, None] == request[None, :])
        & (distance >= 0)
        & ((distance < window) | (position[None, :] < SINKS))
    )
    scores = jnp.where(allowed[None, :, :], scores, -1e30)
    row_peak = jnp.max(scores, axis=-1, keepdims=True)
    weights = jnp.exp(scores - row_peak)
    weights = (weights / jnp.sum(weights, axis=-1, keepdims=True)).astype(jnp.bfloat16)
    context = jnp.einsum("hqk,khd->qhd", weights, value_heads, preferred_element_type=jnp.float32)
    return context.astype(jnp.bfloat16)


def feed_forward(states, gate_cols, up_cols, down_cols):
    gate_act = jnp.dot(states, gate_cols, preferred_element_type=jnp.float32)
    up_act = jnp.dot(states, up_cols, preferred_element_type=jnp.float32)
    hidden_act = (jax.nn.silu(gate_act) * up_act).astype(jnp.bfloat16)
    return lax.dot_general(
        hidden_act, down_cols, (((1,), (1,)), ((), ())), preferred_element_type=jnp.float32
    )


def shards(
    layer_input,
    request_lengths,
    request_adapter,
    slot_adapter_index,
    query_weight,
    key_weight,
    value_weight,
    output_weight,
    query_norm_gain,
    key_norm_gain,
    query_down_factors,
    value_down_factors,
    query_up_factors,
    value_up_factors,
    attention_norm_gain,
    feedforward_norm_gain,
    gate_weight,
    up_weight,
    down_weight_transposed,
):
    tok_dev = layer_input.shape[0]
    tok_group = tok_dev * lax.axis_size("mlp")
    window = tok_group * 3 // 8
    heads_local = query_weight.shape[1] // HEAD_SIZE
    request, position, token_slot = layout(
        request_lengths[0], request_adapter[0], slot_adapter_index, tok_group
    )
    group_token_rows = lax.all_gather(layer_input, "mlp", axis=0, tiled=True)
    columns = jnp.arange(ADAPTER_SLOTS * ADAPTER_RANK, dtype=jnp.int32) // ADAPTER_RANK
    slot_match_mask = (columns[None, :] == token_slot[:, None]).astype(jnp.bfloat16)
    query_reduced = (
        jnp.dot(group_token_rows, query_down_factors, preferred_element_type=jnp.float32).astype(
            jnp.bfloat16
        )
        * slot_match_mask
    )
    value_reduced = (
        jnp.dot(group_token_rows, value_down_factors, preferred_element_type=jnp.float32).astype(
            jnp.bfloat16
        )
        * slot_match_mask
    )
    query_before_norm = jnp.dot(
        group_token_rows, query_weight, preferred_element_type=jnp.float32
    ) + adapter_scale * jnp.dot(query_reduced, query_up_factors, preferred_element_type=jnp.float32)
    key_pre = jnp.dot(group_token_rows, key_weight, preferred_element_type=jnp.float32)
    value_before_adapter = jnp.dot(
        group_token_rows, value_weight, preferred_element_type=jnp.float32
    ) + adapter_scale * jnp.dot(value_reduced, value_up_factors, preferred_element_type=jnp.float32)
    queries = rotary(
        rms_scale(query_before_norm.reshape(tok_group, heads_local, HEAD_SIZE))
        * query_norm_gain.reshape(heads_local, HEAD_SIZE),
        position,
    ).astype(jnp.bfloat16)
    key_heads = rotary(
        rms_scale(key_pre.reshape(tok_group, heads_local, HEAD_SIZE))
        * key_norm_gain.reshape(heads_local, HEAD_SIZE),
        position,
    ).astype(jnp.bfloat16)
    value_heads = value_before_adapter.astype(jnp.bfloat16).reshape(
        tok_group, heads_local, HEAD_SIZE
    )
    context = attention(queries, key_heads, value_heads, request, position, window).reshape(
        tok_group, heads_local * HEAD_SIZE
    )
    attn_own = lax.psum_scatter(
        jnp.dot(context, output_weight, preferred_element_type=jnp.float32).astype(jnp.bfloat16),
        "mlp",
        scatter_dimension=0,
        tiled=True,
    ).astype(jnp.float32)
    residual_own = (
        layer_input.astype(jnp.float32) + rms_scale(attn_own) * attention_norm_gain
    ).astype(jnp.bfloat16)
    residual_all = lax.all_gather(residual_own, "mlp", axis=0, tiled=True)
    partial_value = feed_forward(
        residual_all,
        lax.all_gather(gate_weight, "req", axis=1, tiled=True),
        lax.all_gather(up_weight, "req", axis=1, tiled=True),
        lax.all_gather(down_weight_transposed, "req", axis=1, tiled=True),
    )
    mlp_own = lax.psum_scatter(
        partial_value.astype(jnp.bfloat16), "mlp", scatter_dimension=0, tiled=True
    ).astype(jnp.float32)
    return (residual_own.astype(jnp.float32) + rms_scale(mlp_own) * feedforward_norm_gain).astype(
        jnp.bfloat16
    )


def solution(mesh):
    return jax.shard_map(
        shards,
        mesh=mesh,
        in_specs=(
            P(("req", "mlp"), None),
            P("req", None),
            P("req", None),
            P(),
            P(None, "mlp"),
            P(None, "mlp"),
            P(None, "mlp"),
            P("mlp", None),
            P("mlp"),
            P("mlp"),
            P(),
            P(),
            P(None, "mlp"),
            P(None, "mlp"),
            P(),
            P(),
            P(None, ("req", "mlp")),
            P(None, ("req", "mlp")),
            P(None, ("req", "mlp")),
        ),
        out_specs=P(("req", "mlp"), None),
        check_vma=False,
    )
```

profile of v0, /device:TPU:0, one launch (start us, length us, event | category | flops | bytes accessed | tf_op | source)
XLA Modules:
  0.0 387.4 jit_solution(2803297482719864840)
XLA Ops:
  6.5 0.7 all-gather.6.cloned.1.call-update
  7.3 0.0 reduce-scatter.3.cloned.1.call-start
  7.3 0.8 reduce-window.4
  8.2 0.7 fusion.44
  8.8 0.7 select_reduce_fusion.2
  9.6 0.7 select_reduce_fusion
  10.3 0.1 fusion.31
  10.4 0.3 multiply_cosine_fusion
  10.8 28.8 %all-gather.6.cloned.1.call-done = bf16[128,4096]{1,0:T(8,128)(2,1)} async-done(((bf16[32,4096]{1,0:T(8,128)(2,1)}), bf16[128,4096]{1,0:T(8,128)(2,1)}) %all-gather.6.cloned.1.call-update) | async-done | bytes 1048592 | tf_op jit(solution)/shard_map/all_gather | solution.py:109
  39.6 3.3 fusion.61
  42.9 0.6 fusion.4
  43.5 0.1 reshape.228
  43.6 0.2 multiply_reduce_fusion.1
  43.9 0.1 copy.36
  43.9 2.9 fusion.62
  46.9 0.1 reshape.229
  47.0 0.2 multiply_reduce_fusion
  47.2 0.1 copy.38
  47.3 0.2 fusion.19
  47.5 0.3 subtract_convert_fusion
  47.8 0.3 fusion.3
  48.1 0.9 fusion.55
  49.0 2.9 fusion.60
  52.0 0.6 fusion.7
  52.6 0.1 copy.43
  52.7 0.2 convolution_convert_fusion.2
  52.9 3.9 %convolution_convert_fusion.1 = bf16[128,4096]{1,0:T(8,128)(2,1)} fusion(bf16[128,512]{0,1:T(8,128)(2,1)S(1)} %bitcast.51, bf16[512,4096]{1,0:T(8,128)(2,1)} %param.26), kind=kOutput, calls=%fused_computation.2 | convolution fusion | flops 537395200 | bytes 5373952 | tf_op jit(solution)/shard_map/dot_general | solution.py:148
  56.8 0.0 reduce-scatter.3.cloned.1.call-update
  56.8 0.0 all-gather.8.cloned.1.call-start
  56.9 26.7 %reduce-scatter.3.cloned.1.call-done = bf16[32,4096]{1,0:T(8,128)(2,1)} async-done(((bf16[128,4096]{1,0:T(8,128)(2,1)}), bf16[32,4096]{1,0:T(8,128)(2,1)}) %reduce-scatter.3.cloned.1.call-update) | async-done | bytes 262160 | tf_op jit(solution)/shard_map/reduce_scatter | solution.py:147
  83.6 1.1 fusion.10
  84.7 1.8 fusion.13
  86.6 0.0 all-gather.10.cloned.1.call-start
  86.6 0.5 all-gather.10.cloned.1.call-update
  87.2 0.0 all-gather.12.cloned.1.call-start
  87.2 0.5 all-gather.12.cloned.1.call-update
  87.8 0.0 all-gather.14.cloned.1.call-start
  87.8 0.5 all-gather.14.cloned.1.call-update
  88.3 0.2 reduce-scatter.5.cloned.1.call-start
  88.6 24.8 %all-gather.8.cloned.1.call-done = bf16[128,4096]{1,0:T(8,128)(2,1)} async-done(((bf16[32,4096]{1,0:T(8,128)(2,1)}), bf16[128,4096]{1,0:T(8,128)(2,1)}) %all-gather.8.cloned.1.call-update) | async-done | bytes 1048592 | tf_op jit(solution)/shard_map/all_gather | solution.py:156
  113.4 73.6 %all-gather.10.cloned.1.call-done = bf16[4096,1536]{0,1:T(8,128)(2,1)} async-done(((bf16[4096,192]{0,1:T(8,128)(2,1)}), bf16[4096,1536]{0,1:T(8,128)(2,1)}) %all-gather.10.cloned.1.call-update) | async-done | bytes 12582928 | tf_op jit(solution)/shard_map/all_gather | solution.py:159
  186.9 9.2 %fusion.63 = f32[128,1536]{1,0:T(8,128)S(1)} fusion(bf16[128,4096]{1,0:T(8,128)(2,1)} %all-gather.8.cloned.1.call-done, bf16[4096,1536]{0,1:T(8,128)(2,1)} %all-gather.10.cloned.1.call-done), kind=kOutput, calls=%fused_computation.98 | convolution fusion | flops 1610612736 | bytes 14417920 | tf_op jit(solution)/shard_map/dot_general | solution.py:73
  196.1 64.8 %all-gather.12.cloned.1.call-done = bf16[4096,1536]{0,1:T(8,128)(2,1)} async-done(((bf16[4096,192]{0,1:T(8,128)(2,1)}), bf16[4096,1536]{0,1:T(8,128)(2,1)}) %all-gather.12.cloned.1.call-update) | async-done | bytes 12582928 | tf_op jit(solution)/shard_map/all_gather | solution.py:160
  261.0 74.1 %all-gather.14.cloned.1.call-done = bf16[4096,1536]{0,1:T(8,128)(2,1)} async-done(((bf16[4096,192]{0,1:T(8,128)(2,1)}), bf16[4096,1536]{0,1:T(8,128)(2,1)}) %all-gather.14.cloned.1.call-update) | async-done | bytes 12582928 | tf_op jit(solution)/shard_map/all_gather | solution.py:161
  335.0 15.2 %convolution_convert_fusion = bf16[128,4096]{1,0:T(8,128)(2,1)} fusion(bf16[4096,1536]{0,1:T(8,128)(2,1)} %all-gather.14.cloned.1.call-done, bf16[128,4096]{1,0:T(8,128)(2,1)S(1)} %copy-done.3, bf16[4096,1536]{0,1:T(8,128)(2,1)} %all-gather.12.cloned.1.call-done, f32[128,1536]{1,0:T(8,128)S(1)} %fusion.63), kind=kOutput, calls=%fused_computation.1 | convolution fusion | flops 3222929408 | bytes 28049408 | tf_op jit(solution)/shard_map/dot_general | solution.py:76
  350.3 27.3 %reduce-scatter.5.cloned.1.call-done = bf16[32,4096]{1,0:T(8,128)(2,1)} async-done(((bf16[128,4096]{1,0:T(8,128)(2,1)}), bf16[32,4096]{1,0:T(8,128)(2,1)}) %reduce-scatter.5.cloned.1.call-update) | async-done | bytes 262160 | tf_op jit(solution)/shard_map/reduce_scatter | solution.py:163
  377.6 1.1 fusion.14
  378.7 1.8 fusion.17
  (47 shorter events, 0.2 us)
Async XLA Ops:
  6.5 36.4 %copy-start = (bf16[4096,128]{1,0:T(8,128)(2,1)S(1)}, bf16[4096,128]{1,0:T(8,128)(2,1)}, u32[]{:S(2)}) copy-start(bf16[4096,128]{1,0:T(8,128)(2,1)} %param.29) | copy-start | bytes 3145732
  6.5 36.4 %copy-start.7 = (bf16[128,512]{1,0:T(8,128)(2,1)S(1)}, bf16[128,512]{1,0:T(8,128)(2,1)}, u32[]{:S(2)}) copy-start(bf16[128,512]{1,0:T(8,128)(2,1)} %param.31) | copy-start | bytes 393220
  6.5 33.1 %all-gather.6.cloned.1.call-start = ((), (), s32[]{:S(2)}) async-start(), calls=%async_computation.2 | async-start | bytes 1310720 | tf_op jit(solution)/shard_map/all_gather | solution.py:109
  7.3 76.3 %reduce-scatter.3.cloned.1.call-start = ((), (), s32[]{:S(2)}) async-start(), calls=%async_computation.3 | async-start | bytes 1310720 | tf_op jit(solution)/shard_map/reduce_scatter | solution.py:147
  8.1 35.4 %copy-start.13 = (s32[128]{0:T(128)}, s32[128]{0:T(128)S(1)}, u32[]{:S(2)}) copy-start(s32[128]{0:T(128)S(1)} %and_select_fusion) | copy-start | bytes 1540
  10.3 33.2 %copy-start.15 = (s32[128]{0:T(128)}, s32[128]{0:T(128)S(1)}, u32[]{:S(2)}) copy-start(s32[128]{0:T(128)S(1)} %select_reduce_fusion) | copy-start | bytes 1540
  39.6 3.3 copy-start.2
  43.5 3.7 copy-start.11
  43.5 3.7 copy-start.12
  47.5 4.4 %copy-start.5 = (bf16[4096,128]{1,0:T(8,128)(2,1)S(1)}, bf16[4096,128]{1,0:T(8,128)(2,1)}, u32[]{:S(2)}) copy-start(bf16[4096,128]{1,0:T(8,128)(2,1)} %param.30) | copy-start | bytes 3145732
  47.5 4.4 %copy-start.8 = (bf16[128,512]{1,0:T(8,128)(2,1)S(1)}, bf16[128,512]{1,0:T(8,128)(2,1)}, u32[]{:S(2)}) copy-start(bf16[128,512]{1,0:T(8,128)(2,1)} %param.32) | copy-start | bytes 393220
  47.8 4.2 %copy-start.14 = (s32[128]{0:T(128)S(1)}, s32[128]{0:T(128)}, u32[]{:S(2)}) copy-start(s32[128]{0:T(128)} %copy-done.13) | copy-start | bytes 1540
  47.8 4.2 %copy-start.16 = (s32[128]{0:T(128)S(1)}, s32[128]{0:T(128)}, u32[]{:S(2)}) copy-start(s32[128]{0:T(128)} %copy-done.15) | copy-start | bytes 1540
  49.0 3.7 copy-start.17
  52.5 32.2 %copy-start.6 = (bf16[32,4096]{1,0:T(8,128)(2,1)S(1)}, bf16[32,4096]{1,0:T(8,128)(2,1)}, u32[]{:S(2)}) copy-start(bf16[32,4096]{1,0:T(8,128)(2,1)} %param.19) | copy-start | bytes 786436
  52.5 32.2 %copy-start.9 = (f32[4096]{0:T(1024)S(1)}, f32[4096]{0:T(1024)}, u32[]{:S(2)}) copy-start(f32[4096]{0:T(1024)} %param.33) | copy-start | bytes 49156
  56.8 56.5 %all-gather.8.cloned.1.call-start = ((), (), s32[]{:S(2)}) async-start(), calls=%async_computation.4 | async-start | bytes 1310720 | tf_op jit(solution)/shard_map/all_gather | solution.py:156
  86.6 100.3 %all-gather.10.cloned.1.call-start = ((), (), s32[]{:S(2)}) async-start(), calls=%async_computation.5 | async-start | bytes 14155776 | tf_op jit(solution)/shard_map/all_gather | solution.py:159
  87.2 173.8 %all-gather.12.cloned.1.call-start = ((), (), s32[]{:S(2)}) async-start(), calls=%async_computation.6 | async-start | bytes 14155776 | tf_op jit(solution)/shard_map/all_gather | solution.py:160
  87.8 247.3 %all-gather.14.cloned.1.call-start = ((), (), s32[]{:S(2)}) async-start(), calls=%async_computation.7 | async-start | bytes 14155776 | tf_op jit(solution)/shard_map/all_gather | solution.py:161
  88.3 289.3 %reduce-scatter.5.cloned.1.call-start = ((), (), s32[]{:S(2)}) async-start(), calls=%async_computation.8 | async-start | bytes 1310720 | tf_op jit(solution)/shard_map/reduce_scatter | solution.py:163
  113.4 221.7 %copy-start.3 = (bf16[128,4096]{1,0:T(8,128)(2,1)S(1)}, bf16[128,4096]{1,0:T(8,128)(2,1)}, u32[]{:S(2)}) copy-start(bf16[128,4096]{1,0:T(8,128)(2,1)} %all-gather.8.cloned.1.call-done) | copy-start | bytes 3145732
  196.1 182.6 %copy-start.4 = (bf16[32,4096]{1,0:T(8,128)(2,1)S(1)}, bf16[32,4096]{1,0:T(8,128)(2,1)}, u32[]{:S(2)}) copy-start(bf16[32,4096]{1,0:T(8,128)(2,1)} %fusion.13) | copy-start | bytes 786436
  196.1 182.6 %copy-start.10 = (f32[4096]{0:T(1024)S(1)}, f32[4096]{0:T(1024)}, u32[]{:S(2)}) copy-start(f32[4096]{0:T(1024)} %param.34) | copy-start | bytes 49156
  335.0 45.5 %copy-start.1 = (bf16[4096,128]{1,0:T(8,128)(2,1)S(1)}, bf16[4096,128]{1,0:T(8,128)(2,1)}, u32[]{:S(2)}) copy-start(bf16[4096,128]{1,0:T(8,128)(2,1)} %param.29) | copy-start | bytes 3145732
Sparse Core Ops, SparseCore 0:
  8.9 30.6 all-gather.5
  57.0 26.5 reduce-scatter.2
  86.7 26.5 all-gather.7
  115.3 71.6 all-gather.9
  188.8 72.1 all-gather.11
  262.9 72.1 all-gather.13
  350.4 27.1 reduce-scatter.4
where the time goes:
time: 388 us; the launch traced here: 387 us
  waiting for transfers between devices  322 us (83%)
  matrix products  40 us (10%)
  between operations  13.8 us (4%)
  other arithmetic  10.2 us (3%)
    all_gather x1, waiting for transfers between devices, shards(): lax.all_gather(down_weight_transposed, 'req', axis=1, tiled=True)  74.1 us
    all_gather x1, waiting for transfers between devices, shards(): lax.all_gather(gate_weight, 'req', axis=1, tiled=True)  73.6 us
    all_gather x1, waiting for transfers between devices, shards(): lax.all_gather(up_weight, 'req', axis=1, tiled=True)  64.8 us
    all_gather x1, waiting for transfers between devices, shards(): group_token_rows = lax.all_gather(layer_input, 'mlp', axis=0, tiled=True)  28.8 us
    reduce_scatter x1, waiting for transfers between devices, shards(): lax.psum_scatter(partial_value.astype(jnp.bfloat16), 'mlp', scatter_dimen...  27.3 us
    reduce_scatter x1, waiting for transfers between devices, shards(): lax.psum_scatter(jnp.dot(context, output_weight, preferred_element_type=j...  26.7 us
    all_gather x1, waiting for transfers between devices, shards(): residual_all = lax.all_gather(residual_own, 'mlp', axis=0, tiled=True)  24.8 us
    dot_general x1, matrix products, feed_forward(): lax.dot_general(hidden_act, down_cols, (((1,), (1,)), ((), ())), preferre...  15.2 us
  transfers between devices with their start and end apart: 7, of which 7 were waited for; matrix products, arithmetic and copies ran while one was open for 3% of the time, Pallas kernels for 0%

commit v1 on v0

--- a/solution.py
+++ b/solution.py
@@ -1,12 +1,16 @@
+import math
+
 import jax
 import jax.numpy as jnp
 from jax import lax
-from jax.sharding import PartitionSpec as P
+from jax.sharding import Mesh, PartitionSpec as P
 
 HEAD_SIZE = 128
 ADAPTER_RANK = 16
 ADAPTER_SLOTS = 8
 SINKS = 4
+REQ = ("y", "x", "core")
+STATIONARY_TOKENS = 2048
 
 
 epsilon = 1e-06
@@ -69,12 +73,16 @@
     return context.astype(jnp.bfloat16)
 
 
-def feed_forward(states, gate_cols, up_cols, down_cols):
-    gate_act = jnp.dot(states, gate_cols, preferred_element_type=jnp.float32)
-    up_act = jnp.dot(states, up_cols, preferred_element_type=jnp.float32)
-    hidden_act = (jax.nn.silu(gate_act) * up_act).astype(jnp.bfloat16)
-    return lax.dot_general(
-        hidden_act, down_cols, (((1,), (1,)), ((), ())), preferred_element_type=jnp.float32
+def hidden_units(states, gate_rows, up_rows):
+    contract = (((1,), (1,)), ((), ()))
+    gate_act = lax.dot_general(states, gate_rows, contract, preferred_element_type=jnp.float32)
+    up_act = lax.dot_general(states, up_rows, contract, preferred_element_type=jnp.float32)
+    return (jax.nn.silu(gate_act) * up_act).astype(jnp.bfloat16)
+
+
+def feed_forward(states, gate_rows, up_rows, down_rows):
+    return jnp.dot(
+        hidden_units(states, gate_rows, up_rows), down_rows, preferred_element_type=jnp.float32
     )
 
 
@@ -153,15 +161,23 @@
     residual_own = (
         layer_input.astype(jnp.float32) + rms_scale(attn_own) * attention_norm_gain
     ).astype(jnp.bfloat16)
-    residual_all = lax.all_gather(residual_own, "mlp", axis=0, tiled=True)
-    partial_value = feed_forward(
-        residual_all,
-        lax.all_gather(gate_weight, "req", axis=1, tiled=True),
-        lax.all_gather(up_weight, "req", axis=1, tiled=True),
-        lax.all_gather(down_weight_transposed, "req", axis=1, tiled=True),
-    )
+    gate_rows, up_rows, down_rows = gate_weight.T, up_weight.T, down_weight_transposed.T
+    if tok_group * lax.axis_size(REQ) <= STATIONARY_TOKENS:
+        token_axes = ("y", "x", "mlp")
+        swap = [(0, 1), (1, 0)]
+        gate_rows, up_rows, down_rows = (
+            jnp.concatenate([rows, lax.ppermute(rows, "core", swap)])
+            for rows in (gate_rows, up_rows, down_rows)
+        )
+    else:
+        token_axes = ("mlp",)
+        gate_rows, up_rows, down_rows = (
+            lax.all_gather(rows, REQ, axis=0, tiled=True) for rows in (gate_rows, up_rows, down_rows)
+        )
+    residual_all = lax.all_gather(residual_own, token_axes, axis=0, tiled=True)
+    partial_value = feed_forward(residual_all, gate_rows, up_rows, down_rows)
     mlp_own = lax.psum_scatter(
-        partial_value.astype(jnp.bfloat16), "mlp", scatter_dimension=0, tiled=True
+        partial_value.astype(jnp.bfloat16), token_axes, scatter_dimension=0, tiled=True
     ).astype(jnp.float32)
     return (residual_own.astype(jnp.float32) + rms_scale(mlp_own) * feedforward_norm_gain).astype(
         jnp.bfloat16
@@ -169,13 +185,16 @@
 
 
 def solution(mesh):
+    req, mlp = mesh.devices.shape
+    side = math.isqrt(req // 2)
+    fine = Mesh(mesh.devices.reshape(req // 2 // side, side, 2, mlp), ("y", "x", "core", "mlp"))
     return jax.shard_map(
         shards,
-        mesh=mesh,
+        mesh=fine,
         in_specs=(
-            P(("req", "mlp"), None),
-            P("req", None),
-            P("req", None),
+            P((*REQ, "mlp"), None),
+            P(REQ, None),
+            P(REQ, None),
             P(),
             P(None, "mlp"),
             P(None, "mlp"),
@@ -189,10 +208,10 @@
             P(None, "mlp"),
             P(),
             P(),
-            P(None, ("req", "mlp")),
-            P(None, ("req", "mlp")),
-            P(None, ("req", "mlp")),
+            P(None, (*REQ, "mlp")),
+            P(None, (*REQ, "mlp")),
+            P(None, (*REQ, "mlp")),
         ),
-        out_specs=P(("req", "mlp"), None),
+        out_specs=P((*REQ, "mlp"), None),
         check_vma=False,
     )

time: 388 us -> 289 us (0.74)
  waiting for transfers between devices: 322 us -> 225 us
    all_gather x4 -> x1, waiting for transfers between devices: 237 us -> 69.6 us  [shards(): residual_all = lax.all_gather(residual_own, token_axes, axis=0, tiled=True)]
    reduce_scatter x1, waiting for transfers between devices: 27.3 us -> 95.1 us  [shards(): lax.psum_scatter(partial_value.astype(jnp.bfloat16), token_axes, scatter_...]
    dot_general x2, matrix products: 24.4 us -> 16.7 us  [the longest x1 10.8 us: feed_forward(): jnp.dot(hidden_units(states, gate_rows, up_rows), down_rows, preferred_el...]
    ppermute x0 -> x3, waiting for transfers between devices: none -> 4.4 us  [shards(): lax.ppermute(rows, 'core', swap)]
  transfers between devices with their start and end apart: 7 -> 7, of which waited for: 7 -> 5; matrix products, arithmetic and copies ran while one was open for 3% -> 3% of each run, Pallas kernels for 0% -> 0%
where the time goes in v1:
time: 289 us
  waiting for transfers between devices  225 us (78%)
  matrix products  36.8 us (13%)
  between operations  13.4 us (5%)
  other arithmetic  12.4 us (4%)
    reduce_scatter x1, waiting for transfers between devices, shards(): lax.psum_scatter(partial_value.astype(jnp.bfloat16), token_axes, scatter_...  95.1 us
    all_gather x1, waiting for transfers between devices, shards(): residual_all = lax.all_gather(residual_own, token_axes, axis=0, tiled=True)  69.6 us
    all_gather x1, waiting for transfers between devices, shards(): group_token_rows = lax.all_gather(layer_input, 'mlp', axis=0, tiled=True)  28.2 us
    reduce_scatter x1, waiting for transfers between devices, shards(): lax.psum_scatter(jnp.dot(context, output_weight, preferred_element_type=j...  26.7 us
    dot_general x1, matrix products, feed_forward(): jnp.dot(hidden_units(states, gate_rows, up_rows), down_rows, preferred_el...  10.8 us
    dot_general x1, matrix products, hidden_units(): lax.dot_general(states, gate_rows, contract, preferred_element_type=jnp.f...  5.9 us
  transfers between devices with their start and end apart: 7, of which 5 were waited for; matrix products, arithmetic and copies ran while one was open for 3% of the time, Pallas kernels for 0%

profile of v1, /device:TPU:0, one launch (start us, length us, event | category | flops | bytes accessed | tf_op | source)
XLA Modules:
  0.0 288.8 jit_solution(5284186134971861276)
XLA Ops:
  6.5 0.7 all-gather.3.cloned.1.call-update
  7.3 0.0 reduce-scatter.3.cloned.1.call-start
  7.3 0.8 reduce-window.4
  8.2 0.7 fusion.58
  8.8 0.7 select_reduce_fusion.2
  9.6 0.7 select_reduce_fusion
  10.3 0.1 fusion.45
  10.4 1.0 multiply_cosine_fusion
  11.4 28.2 %all-gather.3.cloned.1.call-done = bf16[128,4096]{1,0:T(8,128)(2,1)} async-done(((bf16[32,4096]{1,0:T(8,128)(2,1)}), bf16[128,4096]{1,0:T(8,128)(2,1)}) %all-gather.3.cloned.1.call-update) | async-done | bytes 1048592 | tf_op jit(solution)/shard_map/all_gather | solution.py:117
  39.6 3.3 %fusion.79 = f32[128,512]{1,0:T(8,128)S(1)} fusion(bf16[128,4096]{1,0:T(8,128)(2,1)} %all-gather.3.cloned.1.call-done, bf16[4096,512]{1,0:T(8,128)(2,1)} %param.24), kind=kOutput, calls=%fused_computation.109 | convolution fusion | flops 536870912 | bytes 5505024 | tf_op jit(solution)/shard_map/dot_general | solution.py:135
  42.9 0.1 reshape.229
  43.0 0.2 multiply_reduce_fusion
  43.2 0.1 copy.38
  43.3 0.0 copy-done.1
  43.3 0.0 copy-start.9
  43.3 2.9 %fusion.78 = f32[128,512]{1,0:T(8,128)S(1)} fusion(bf16[128,4096]{1,0:T(8,128)(2,1)S(1)} %copy-done.1, bf16[4096,512]{1,0:T(8,128)(2,1)} %param.23), kind=kOutput, calls=%fused_computation.108 | convolution fusion | flops 536870912 | bytes 5505024 | tf_op jit(solution)/shard_map/dot_general | solution.py:132
  46.3 0.6 fusion.14
  46.9 0.1 reshape.228
  47.0 0.2 multiply_reduce_fusion.1
  47.2 0.1 copy.36
  47.3 0.0 copy-done.8
  47.3 0.2 fusion.33
  47.5 1.8 subtract_convert_fusion
  49.3 1.8 fusion.72
  51.1 1.9 fusion.13
  53.0 2.9 %fusion.77 = f32[128,512]{1,0:T(8,128)S(1)} fusion(bf16[128,4096]{1,0:T(8,128)(2,1)S(1)} %copy-done.1, bf16[4096,512]{1,0:T(8,128)(2,1)} %param.25), kind=kOutput, calls=%fused_computation.107 | convolution fusion | flops 536870912 | bytes 5505024 | tf_op jit(solution)/shard_map/dot_general | solution.py:136
  56.0 1.5 fusion.17
  57.5 0.1 copy.43
  57.6 1.4 convolution_convert_fusion.2
  59.0 3.9 %convolution_convert_fusion.1 = bf16[128,4096]{1,0:T(8,128)(2,1)} fusion(bf16[128,512]{0,1:T(8,128)(2,1)S(1)} %bitcast.51, bf16[512,4096]{1,0:T(8,128)(2,1)} %param.26), kind=kOutput, calls=%fused_computation.2 | convolution fusion | flops 537395200 | bytes 5373952 | tf_op jit(solution)/shard_map/dot_general | solution.py:156
  62.9 0.0 reduce-scatter.3.cloned.1.call-update
  62.9 0.0 all-gather.5.cloned.1.call-start
  63.0 26.7 %reduce-scatter.3.cloned.1.call-done = bf16[32,4096]{1,0:T(8,128)(2,1)} async-done(((bf16[128,4096]{1,0:T(8,128)(2,1)}), bf16[32,4096]{1,0:T(8,128)(2,1)}) %reduce-scatter.3.cloned.1.call-update) | async-done | bytes 262160 | tf_op jit(solution)/shard_map/reduce_scatter | solution.py:155
  89.7 1.1 fusion.20
  90.9 1.8 fusion.23
  92.7 0.0 all-gather.5.cloned.1.call-update
  92.7 0.0 reduce-scatter.5.cloned.1.call-start
  92.8 0.1 collective-permute-start
  92.9 0.5 collective-permute-start.1
  93.4 0.1 collective-permute-start.2
  93.4 4.4 %collective-permute-done = bf16[192,4096]{1,0:T(8,128)(2,1)} collective-permute-done((bf16[192,4096]{1,0:T(8,128)(2,1)S(1)}, bf16[192,4096]{1,0:T(8,128)(2,1)}, u32[]{:S(2)}, u32[]{:S(2)}) %collective-permute-start) | collective-permute-done | bytes 1572896 | tf_op jit(solution)/shard_map/ppermute | solution.py:169
  97.8 69.6 %all-gather.5.cloned.1.call-done = bf16[512,4096]{1,0:T(8,128)(2,1)} async-done(((bf16[32,4096]{1,0:T(8,128)(2,1)}), bf16[512,4096]{1,0:T(8,128)(2,1)}) %all-gather.5.cloned.1.call-update) | async-done | bytes 4194320 | tf_op jit(solution)/shard_map/all_gather | solution.py:177
  167.5 5.9 %fusion.1 = f32[512,384]{1,0:T(8,128)} fusion(bf16[512,4096]{1,0:T(8,128)(2,1)} %all-gather.5.cloned.1.call-done, bf16[192,4096]{1,0:T(8,128)(2,1)} %collective-permute-done, bf16[192,4096]{1,0:T(8,128)(2,1)S(1)} %bitcast.57), kind=kOutput, calls=%fused_computation.3 | convolution fusion | flops 1616904192 | bytes 8126464 | tf_op jit(solution)/shard_map/dot_general | solution.py:78
  173.4 10.8 %convolution_convert_fusion = bf16[512,4096]{1,0:T(8,128)(2,1)} fusion(bf16[192,4096]{1,0:T(8,128)(2,1)} %collective-permute-done.2, bf16[192,4096]{1,0:T(8,128)(2,1)} %bitcast.59, f32[512,384]{1,0:T(8,128)} %fusion.1, bf16[512,4096]{1,0:T(8,128)(2,1)} %all-gather.5.cloned.1.call-done, bf16[192,4096]{1,0:T(8,128)(2,1)} %collective-permute-done.1, ...), kind=kOutput, calls=%fused_computation.1 | convolution fusion | flops 3237085184 | bytes 15466496 | tf_op jit(solution)/shard_map/dot_general | solution.py:84
  184.1 0.0 reduce-scatter.5.cloned.1.call-update
  184.2 95.1 %reduce-scatter.5.cloned.1.call-done = bf16[32,4096]{1,0:T(8,128)(2,1)} async-done(((bf16[512,4096]{1,0:T(8,128)(2,1)}), bf16[32,4096]{1,0:T(8,128)(2,1)}) %reduce-scatter.5.cloned.1.call-update) | async-done | bytes 262160 | tf_op jit(solution)/shard_map/reduce_scatter | solution.py:179
  279.3 1.1 fusion.24
  280.4 1.8 fusion.27
  (40 shorter events, 0.1 us)
Async XLA Ops:
  6.5 39.8 %copy-start = (bf16[4096,128]{1,0:T(8,128)(2,1)S(1)}, bf16[4096,128]{1,0:T(8,128)(2,1)}, u32[]{:S(2)}) copy-start(bf16[4096,128]{1,0:T(8,128)(2,1)} %param.29) | copy-start | bytes 3145732
  6.5 33.1 %all-gather.3.cloned.1.call-start = ((), (), s32[]{:S(2)}) async-start(), calls=%async_computation.2 | async-start | bytes 1310720 | tf_op jit(solution)/shard_map/all_gather | solution.py:117
  7.3 82.5 %reduce-scatter.3.cloned.1.call-start = ((), (), s32[]{:S(2)}) async-start(), calls=%async_computation.3 | async-start | bytes 1310720 | tf_op jit(solution)/shard_map/reduce_scatter | solution.py:155
  8.1 38.1 %copy-start.10 = (s32[128]{0:T(128)}, s32[128]{0:T(128)S(1)}, u32[]{:S(2)}) copy-start(s32[128]{0:T(128)S(1)} %and_select_fusion) | copy-start | bytes 1540
  10.3 36.0 %copy-start.12 = (s32[128]{0:T(128)}, s32[128]{0:T(128)S(1)}, u32[]{:S(2)}) copy-start(s32[128]{0:T(128)S(1)} %select_reduce_fusion) | copy-start | bytes 1540
  39.6 3.7 %copy-start.1 = (bf16[128,4096]{1,0:T(8,128)(2,1)S(1)}, bf16[128,4096]{1,0:T(8,128)(2,1)}, u32[]{:S(2)}) copy-start(bf16[128,4096]{1,0:T(8,128)(2,1)} %all-gather.3.cloned.1.call-done) | copy-start | bytes 3145732
  42.9 3.4 %copy-start.5 = (bf16[128,512]{1,0:T(8,128)(2,1)S(1)}, bf16[128,512]{1,0:T(8,128)(2,1)}, u32[]{:S(2)}) copy-start(bf16[128,512]{1,0:T(8,128)(2,1)} %param.31) | copy-start | bytes 393220
  43.3 3.9 %copy-start.8 = (f32[512]{0:T(512)S(1)}, f32[512]{0:T(512)}, u32[]{:S(2)}) copy-start(f32[512]{0:T(512)} %param.28) | copy-start | bytes 6148
  43.3 3.9 %copy-start.9 = (f32[512]{0:T(512)S(1)}, f32[512]{0:T(512)}, u32[]{:S(2)}) copy-start(f32[512]{0:T(512)} %param.27) | copy-start | bytes 6148
  47.5 8.5 %copy-start.3 = (bf16[4096,128]{1,0:T(8,128)(2,1)S(1)}, bf16[4096,128]{1,0:T(8,128)(2,1)}, u32[]{:S(2)}) copy-start(bf16[4096,128]{1,0:T(8,128)(2,1)} %param.30) | copy-start | bytes 3145732
  53.0 2.9 %copy-start.11 = (s32[128]{0:T(128)S(1)}, s32[128]{0:T(128)}, u32[]{:S(2)}) copy-start(s32[128]{0:T(128)} %copy-done.10) | copy-start | bytes 1540
  53.0 2.9 %copy-start.13 = (s32[128]{0:T(128)S(1)}, s32[128]{0:T(128)}, u32[]{:S(2)}) copy-start(s32[128]{0:T(128)} %copy-done.12) | copy-start | bytes 1540
  53.0 4.6 %copy-start.15 = (f32[4,128]{1,0:T(4,128)S(1)}, f32[4,128]{1,0:T(4,128)}, u32[]{:S(2)}) copy-start(f32[4,128]{1,0:T(4,128)} %fusion.72) | copy-start | bytes 6148
  57.5 33.4 %copy-start.4 = (bf16[32,4096]{1,0:T(8,128)(2,1)S(1)}, bf16[32,4096]{1,0:T(8,128)(2,1)}, u32[]{:S(2)}) copy-start(bf16[32,4096]{1,0:T(8,128)(2,1)} %param.19) | copy-start | bytes 786436
  57.5 33.4 %copy-start.6 = (f32[4096]{0:T(1024)S(1)}, f32[4096]{0:T(1024)}, u32[]{:S(2)}) copy-start(f32[4096]{0:T(1024)} %param.33) | copy-start | bytes 49156
  57.6 35.2 %copy-start.14 = (bf16[4096,192]{0,1:T(8,128)(2,1)S(1)}, bf16[4096,192]{0,1:T(8,128)(2,1)}, u32[]{:S(2)}) copy-start(bf16[4096,192]{0,1:T(8,128)(2,1)} %param.35) | copy-start | bytes 4718596
  62.9 104.5 %all-gather.5.cloned.1.call-start = ((), (), s32[]{:S(2)}) async-start(), calls=%async_computation.4 | async-start | bytes 4456448 | tf_op jit(solution)/shard_map/all_gather | solution.py:177
  92.7 186.6 %reduce-scatter.5.cloned.1.call-start = ((), (), s32[]{:S(2)}) async-start(), calls=%async_computation.5 | async-start | bytes 4456448 | tf_op jit(solution)/shard_map/reduce_scatter | solution.py:179
  92.8 5.1 %collective-permute-start = (bf16[192,4096]{1,0:T(8,128)(2,1)S(1)}, bf16[192,4096]{1,0:T(8,128)(2,1)}, u32[]{:S(2)}, u32[]{:S(2)}) collective-permute-start(bf16[192,4096]{1,0:T(8,128)(2,1)S(1)} %bitcast.56), channel_id=1, source_target_pairs={{0,4},{4,0},{1,5},{5,1},{2,6},{6,2},{3,7},{7,3},{8,12},{12,8},{9,1... | collective-permute-start | bytes 4718600 | tf_op jit(solution)/shard_map/ppermute | solution.py:169
  92.9 80.5 %collective-permute-start.1 = (bf16[192,4096]{1,0:T(8,128)(2,1)}, bf16[192,4096]{1,0:T(8,128)(2,1)}, u32[]{:S(2)}, u32[]{:S(2)}) collective-permute-start(bf16[192,4096]{1,0:T(8,128)(2,1)} %bitcast.60), channel_id=1, source_target_pairs={{0,4},{4,0},{1,5},{5,1},{2,6},{6,2},{3,7},{7,3},{8,12},{12,8},{9,1... | collective-permute-start | bytes 4718600 | tf_op jit(solution)/shard_map/ppermute | solution.py:169
  93.4 80.0 %collective-permute-start.2 = (bf16[192,4096]{1,0:T(8,128)(2,1)}, bf16[192,4096]{1,0:T(8,128)(2,1)}, u32[]{:S(2)}, u32[]{:S(2)}) collective-permute-start(bf16[192,4096]{1,0:T(8,128)(2,1)} %bitcast.58), channel_id=1, source_target_pairs={{0,4},{4,0},{1,5},{5,1},{2,6},{6,2},{3,7},{7,3},{8,12},{12,8},{9,1... | collective-permute-start | bytes 4718600 | tf_op jit(solution)/shard_map/ppermute | solution.py:169
  184.1 96.3 %copy-start.2 = (bf16[32,4096]{1,0:T(8,128)(2,1)S(1)}, bf16[32,4096]{1,0:T(8,128)(2,1)}, u32[]{:S(2)}) copy-start(bf16[32,4096]{1,0:T(8,128)(2,1)} %fusion.23) | copy-start | bytes 786436
  184.1 96.3 %copy-start.7 = (f32[4096]{0:T(1024)S(1)}, f32[4096]{0:T(1024)}, u32[]{:S(2)}) copy-start(f32[4096]{0:T(1024)} %param.34) | copy-start | bytes 49156
Sparse Core Ops, SparseCore 0:
  8.9 30.6 all-gather.2
  63.1 26.6 reduce-scatter.2
  92.9 74.5 all-gather.4
  184.3 94.9 reduce-scatter.4

commit v2 on v1

--- a/solution.py
+++ b/solution.py
@@ -10,7 +10,6 @@
 ADAPTER_SLOTS = 8
 SINKS = 4
 REQ = ("y", "x", "core")
-STATIONARY_TOKENS = 2048
 
 
 epsilon = 1e-06
@@ -37,10 +36,9 @@
     )
 
 
-def layout(lengths, adapters, slot_adapter_index, row_count):
+def layout(lengths, adapters, slot_adapter_index, places):
     req_ends = jnp.cumsum(lengths)
     starts = req_ends - lengths
-    places = jnp.arange(row_count, dtype=jnp.int32)
     member = ((places[:, None] >= starts[None, :]) & (places[:, None] < req_ends[None, :])).astype(
         jnp.int32
     )
@@ -80,10 +78,58 @@
     return (jax.nn.silu(gate_act) * up_act).astype(jnp.bfloat16)
 
 
-def feed_forward(states, gate_rows, up_rows, down_rows):
-    return jnp.dot(
-        hidden_units(states, gate_rows, up_rows), down_rows, preferred_element_type=jnp.float32
-    )
+def exchange(block, axis):
+    return lax.ppermute(block, axis, [(0, 1), (1, 0)])
+
+
+def line_gather(block):
+    index = lax.axis_index("mlp")
+    from_right = lax.ppermute(block, "mlp", [(1, 0), (2, 1), (3, 2)])
+    from_left = lax.ppermute(block, "mlp", [(0, 1), (1, 2), (2, 3)])
+    across = lax.ppermute(block, "mlp", [(0, 2), (1, 3), (2, 0), (3, 1)])
+    far = lax.ppermute(across, "mlp", [(1, 0), (2, 3)])
+    return [
+        block,
+        jnp.where(index == 3, far, from_right),
+        across,
+        jnp.where(index == 0, far, from_left),
+    ]
+
+
+def line_scatter(parts):
+    index = lax.axis_index("mlp")
+    far = lax.ppermute(jnp.where(index == 0, parts[3], parts[1]), "mlp", [(0, 1), (3, 2)])
+    to_right = lax.ppermute(parts[1], "mlp", [(0, 1), (1, 2), (2, 3)])
+    to_left = lax.ppermute(parts[3], "mlp", [(1, 0), (2, 1), (3, 2)])
+    across = (parts[2].astype(jnp.float32) + far.astype(jnp.float32)).astype(parts[2].dtype)
+    across = lax.ppermute(across, "mlp", [(0, 2), (1, 3), (2, 0), (3, 1)])
+    return sum(part.astype(jnp.float32) for part in (parts[0], to_right, to_left, across))
+
+
+def gather_group(block, direct):
+    if direct:
+        return jnp.concatenate(line_gather(block))
+    return lax.all_gather(block, "mlp", axis=0, tiled=True)
+
+
+def scatter_group(rows, direct):
+    if direct:
+        return line_scatter(jnp.split(rows, 4))
+    return lax.psum_scatter(rows, "mlp", scatter_dimension=0, tiled=True).astype(jnp.float32)
+
+
+def spread_weights(gate_rows, up_rows, down_rows):
+    gate_x, up_x = exchange(gate_rows, "x"), exchange(up_rows, "x")
+    half = down_rows.shape[1] // 2
+    y = lax.axis_index("y")
+    own = lax.dynamic_slice_in_dim(down_rows, y * half, half, axis=1)
+    other = exchange(lax.dynamic_slice_in_dim(down_rows, (1 - y) * half, half, axis=1), "y")
+    own_x, other_x = exchange(own, "x"), exchange(other, "x")
+
+    def quad(rows, rows_x):
+        return jnp.concatenate([rows, exchange(rows, "core"), rows_x, exchange(rows_x, "core")])
+
+    return quad(gate_rows, gate_x), quad(up_rows, up_x), quad(own, own_x), quad(other, other_x)
 
 
 def shards(
@@ -111,10 +157,17 @@
     tok_group = tok_dev * lax.axis_size("mlp")
     window = tok_group * 3 // 8
     heads_local = query_weight.shape[1] // HEAD_SIZE
+    direct = [lax.axis_size(axis) for axis in (*REQ, "mlp")] == [2, 2, 2, 4]
+    places = jnp.arange(tok_group, dtype=jnp.int32)
+    if direct:
+        places = (places + lax.axis_index("mlp") * tok_dev) % tok_group
     request, position, token_slot = layout(
-        request_lengths[0], request_adapter[0], slot_adapter_index, tok_group
-    )
-    group_token_rows = lax.all_gather(layer_input, "mlp", axis=0, tiled=True)
+        request_lengths[0], request_adapter[0], slot_adapter_index, places
+    )
+    gate_rows, up_rows, down_rows = gate_weight.T, up_weight.T, down_weight_transposed.T
+    if direct:
+        gate_rows, up_rows, down_near, down_far = spread_weights(gate_rows, up_rows, down_rows)
+    group_token_rows = gather_group(layer_input, direct)
     columns = jnp.arange(ADAPTER_SLOTS * ADAPTER_RANK, dtype=jnp.int32) // ADAPTER_RANK
     slot_match_mask = (columns[None, :] == token_slot[:, None]).astype(jnp.bfloat16)
     query_reduced = (
@@ -152,33 +205,38 @@
     context = attention(queries, key_heads, value_heads, request, position, window).reshape(
         tok_group, heads_local * HEAD_SIZE
     )
-    attn_own = lax.psum_scatter(
+    attn_own = scatter_group(
         jnp.dot(context, output_weight, preferred_element_type=jnp.float32).astype(jnp.bfloat16),
-        "mlp",
-        scatter_dimension=0,
-        tiled=True,
-    ).astype(jnp.float32)
+        direct,
+    )
     residual_own = (
         layer_input.astype(jnp.float32) + rms_scale(attn_own) * attention_norm_gain
     ).astype(jnp.bfloat16)
-    gate_rows, up_rows, down_rows = gate_weight.T, up_weight.T, down_weight_transposed.T
-    if tok_group * lax.axis_size(REQ) <= STATIONARY_TOKENS:
-        token_axes = ("y", "x", "mlp")
-        swap = [(0, 1), (1, 0)]
-        gate_rows, up_rows, down_rows = (
-            jnp.concatenate([rows, lax.ppermute(rows, "core", swap)])
-            for rows in (gate_rows, up_rows, down_rows)
+    if direct:
+        line = line_gather(residual_own)
+        other = [exchange(block, "y") for block in line]
+        states = jnp.concatenate(line + other)
+        hidden = hidden_units(states, gate_rows, up_rows)
+        hidden_other = jnp.concatenate(
+            [exchange(hidden[tok_group:], "y"), exchange(hidden[:tok_group], "y")]
+        )
+        part = jnp.dot(hidden, down_near, preferred_element_type=jnp.float32)
+        part = part + jnp.dot(hidden_other, down_far, preferred_element_type=jnp.float32)
+        part = part.astype(jnp.bfloat16).reshape(2, 4, tok_dev, -1)
+        summed = line_scatter([part[:, k] for k in range(4)])
+        own_half = summed[0]
+        other_half = exchange(summed[1].astype(jnp.bfloat16), "y").astype(jnp.float32)
+        upper = lax.axis_index("y") == 1
+        mlp_own = jnp.concatenate(
+            [jnp.where(upper, other_half, own_half), jnp.where(upper, own_half, other_half)], axis=1
         )
     else:
-        token_axes = ("mlp",)
         gate_rows, up_rows, down_rows = (
             lax.all_gather(rows, REQ, axis=0, tiled=True) for rows in (gate_rows, up_rows, down_rows)
         )
-    residual_all = lax.all_gather(residual_own, token_axes, axis=0, tiled=True)
-    partial_value = feed_forward(residual_all, gate_rows, up_rows, down_rows)
-    mlp_own = lax.psum_scatter(
-        partial_value.astype(jnp.bfloat16), token_axes, scatter_dimension=0, tiled=True
-    ).astype(jnp.float32)
+        hidden = hidden_units(gather_group(residual_own, direct), gate_rows, up_rows)
+        part = jnp.dot(hidden, down_rows, preferred_element_type=jnp.float32)
+        mlp_own = scatter_group(part.astype(jnp.bfloat16), direct)
     return (residual_own.astype(jnp.float32) + rms_scale(mlp_own) * feedforward_norm_gain).astype(
         jnp.bfloat16
     )

time: 289 us -> 240 us (0.83)
  waiting for transfers between devices: 225 us -> 143 us
  starting transfers between devices: 0.77 us -> 55.4 us
  between operations: 13.4 us -> 0.58 us
  other arithmetic: 12.4 us -> 7.07 us
  matrix products: 36.8 us -> 32.5 us
    ppermute x3 -> x36, waiting for transfers between devices: 4.4 us -> 143 us  [the longest x20 77.1 us: exchange(): return lax.ppermute(block, axis, [(0, 1), (1, 0)])]
    reduce_scatter x2 -> x0, waiting for transfers between devices: 122 us -> none  [the longest x1 95.1 us: shards(): lax.psum_scatter(partial_value.astype(jnp.bfloat16), token_axes, scatter_...]
    all_gather x2 -> x0, waiting for transfers between devices: 97.8 us -> none  [the longest x1 69.6 us: shards(): residual_all = lax.all_gather(residual_own, token_axes, axis=0, tiled=True)]
    ppermute x3 -> x36, starting transfers between devices: 0.65 us -> 55.4 us  [the longest x20 16 us: exchange(): return lax.ppermute(block, axis, [(0, 1), (1, 0)])]
    dot_general x1 -> x3, matrix products: 10.8 us -> 9.61 us  [the longest x1 7.26 us: hidden_units(): lax.dot_general(states, up_rows, contract, preferred_element_type=jnp.flo...]
  transfers between devices with their start and end apart: 7 -> 36, of which waited for: 5 -> 22; matrix products, arithmetic and copies ran while one was open for 3% -> 8% of each run, Pallas kernels for 0% -> 0%
where the time goes in v2:
time: 240 us
  waiting for transfers between devices  143 us (60%)
  starting transfers between devices  55.4 us (23%)
  matrix products  32.5 us (14%)
  other arithmetic  7.07 us (3%)
    ppermute x20, waiting for transfers between devices, exchange(): return lax.ppermute(block, axis, [(0, 1), (1, 0)])  77.1 us
    ppermute x2, waiting for transfers between devices, line_scatter(): across = lax.ppermute(across, 'mlp', [(0, 2), (1, 3), (2, 0), (3, 1)])  28.4 us
    ppermute x20, starting transfers between devices, exchange(): return lax.ppermute(block, axis, [(0, 1), (1, 0)])  16 us
    ppermute x2, starting transfers between devices, line_scatter(): lax.ppermute(jnp.where(index == 0, parts[3], parts[1]), 'mlp', [(0, 1), (...  12.8 us
    ppermute x2, waiting for transfers between devices, line_gather(): far = lax.ppermute(across, 'mlp', [(1, 0), (2, 3)])  9.06 us
    ppermute x2, waiting for transfers between devices, line_gather(): across = lax.ppermute(block, 'mlp', [(0, 2), (1, 3), (2, 0), (3, 1)])  7.86 us
    ppermute x2, starting transfers between devices, line_gather(): from_left = lax.ppermute(block, 'mlp', [(0, 1), (1, 2), (2, 3)])  7.67 us
    ppermute x2, waiting for transfers between devices, line_scatter(): lax.ppermute(jnp.where(index == 0, parts[3], parts[1]), 'mlp', [(0, 1), (...  7.56 us
  transfers between devices with their start and end apart: 36, of which 22 were waited for; matrix products, arithmetic and copies ran while one was open for 8% of the time, Pallas kernels for 0%

profile of v2, /device:TPU:0, one launch (start us, length us, event | category | flops | bytes accessed | tf_op | source)
XLA Modules:
  0.0 239.5 jit_solution(5910179469184027694)
XLA Ops:
  0.0 4.0 %collective-permute-start = (bf16[32,4096]{1,0:T(8,128)(2,1)}, bf16[32,4096]{1,0:T(8,128)(2,1)S(1)}, u32[]{:S(2)}, u32[]{:S(2)}) collective-permute-start(bf16[32,4096]{1,0:T(8,128)(2,1)} %param.19), channel_id=1, source_target_pairs={{0,2},{1,3},{2,0},{3,1},{4,6},{5,7},{6,4},{7,5},{8,10},{9,11},{10,... | collective-permute-start | bytes 786440 | tf_op jit(solution)/shard_map/ppermute | solution.py:89
  5.3 4.6 %collective-permute-start.3 = (bf16[32,4096]{1,0:T(8,128)(2,1)}, bf16[32,4096]{1,0:T(8,128)(2,1)S(1)}, u32[]{:S(2)}, u32[]{:S(2)}) collective-permute-start(bf16[32,4096]{1,0:T(8,128)(2,1)} %param.19), channel_id=1, source_target_pairs={{0,1},{1,2},{2,3},{4,5},{5,6},{6,7},{8,9},{9,10},{10,11},{12,13},{... | collective-permute-start | bytes 786440 | tf_op jit(solution)/shard_map/ppermute | solution.py:88
  13.0 4.0 %collective-permute-done = bf16[32,4096]{1,0:T(8,128)(2,1)S(1)} collective-permute-done((bf16[32,4096]{1,0:T(8,128)(2,1)}, bf16[32,4096]{1,0:T(8,128)(2,1)S(1)}, u32[]{:S(2)}, u32[]{:S(2)}) %collective-permute-start) | collective-permute-done | bytes 262176 | tf_op jit(solution)/shard_map/ppermute | solution.py:89
  18.7 6.9 %collective-permute-done.1 = bf16[32,4096]{1,0:T(8,128)(2,1)S(1)} collective-permute-done((bf16[32,4096]{1,0:T(8,128)(2,1)S(1)}, bf16[32,4096]{1,0:T(8,128)(2,1)S(1)}, u32[]{:S(2)}, u32[]{:S(2)}) %collective-permute-start.1) | collective-permute-done | bytes 262176 | tf_op jit(solution)/shard_map/ppermute | solution.py:90
  25.7 1.6 convolution_multiply_fusion.1
  27.3 2.9 %convolution_add_fusion = f32[128,512]{1,0:T(8,128)S(1)} fusion(f32[128,512]{1,0:T(8,128)S(1)} %convolution_multiply_fusion.1, bf16[4096,512]{1,0:T(8,128)(2,1)} %param.23, bf16[32,4096]{1,0:T(8,128)(2,1)S(1)} %get-tuple-element.32, bf16[32,4096]{1,0:T(8,128)(2,1)S(1)} %collective-permute-done, bf16[32,4096]{1,0:T(8,128)(2,1)S(1)} %get-tuple-element.31, ...), kind=kOutput, calls=%fused_computation.42 | convolution fusion | flops 541130752 | bytes 5767168 | tf_op jit(solution)/shard_map/dot_general | solution.py:185
  30.6 2.9 %fusion.93 = f32[128,512]{1,0:T(8,128)S(1)} fusion(bf16[4096,512]{1,0:T(8,128)(2,1)} %param.24, bf16[32,4096]{1,0:T(8,128)(2,1)S(1)} %get-tuple-element.32, bf16[32,4096]{1,0:T(8,128)(2,1)S(1)} %collective-permute-done, bf16[32,4096]{1,0:T(8,128)(2,1)S(1)} %get-tuple-element.31, bf16[32,4096]{1,0:T(8,128)(2,1)S(1)} %copy-done.2), kind=kOutput, calls=%fused_computation.158 | convolution fusion | flops 541065216 | bytes 5505024 | tf_op jit(solution)/shard_map/dot_general | solution.py:188
  35.1 1.8 convolution_multiply_fusion.2
  36.8 2.9 %fusion.42 = bf16[128,512]{1,0:T(8,128)(2,1)S(1)} fusion(f32[128,512]{1,0:T(8,128)S(1)} %convolution_multiply_fusion.2, bf16[4096,512]{1,0:T(8,128)(2,1)} %param.25, bf16[32,4096]{1,0:T(8,128)(2,1)S(1)} %get-tuple-element.32, bf16[32,4096]{1,0:T(8,128)(2,1)S(1)} %collective-permute-done, bf16[32,4096]{1,0:T(8,128)(2,1)S(1)} %get-tuple-element.31, ...), kind=kOutput, calls=%fused_computation.45 | convolution fusion | flops 541196288 | bytes 5636096 | tf_op jit(solution)/shard_map/dot_general | solution.py:189
  40.1 2.9 %convolution_convert_fusion = bf16[128,4096]{1,0:T(8,128)(2,1)S(1)} fusion(bf16[128,512]{0,1:T(8,128)(2,1)S(1)} %bitcast.89, bf16[512,4096]{1,0:T(8,128)(2,1)} %param.26), kind=kOutput, calls=%fused_computation.17 | convolution fusion | flops 537395200 | bytes 5373952 | tf_op jit(solution)/shard_map/dot_general | solution.py:209
  43.1 1.6 collective-permute-start.6
  44.7 1.3 collective-permute-start.4
  47.3 3.5 %collective-permute-done.6 = bf16[32,4096]{1,0:T(8,128)(2,1)S(1)} collective-permute-done((bf16[32,4096]{1,0:T(8,128)(2,1)S(1)}, bf16[32,4096]{1,0:T(8,128)(2,1)S(1)}, u32[]{:S(2)}, u32[]{:S(2)}) %collective-permute-start.6) | collective-permute-done | bytes 262176 | tf_op jit(solution)/shard_map/ppermute | solution.py:101
  51.0 4.3 %collective-permute-start.7 = (bf16[32,4096]{1,0:T(8,128)(2,1)S(1)}, bf16[32,4096]{1,0:T(8,128)(2,1)S(1)}, u32[]{:S(2)}, u32[]{:S(2)}) collective-permute-start(bf16[32,4096]{1,0:T(8,128)(2,1)S(1)} %add_convert_fusion.2), channel_id=1, source_target_pairs={{0,2},{1,3},{2,0},{3,1},{4,6},{5,7},{6,4},{7,5},{8,10},{9,11},{10,... | collective-permute-start | bytes 786440 | tf_op jit(solution)/shard_map/ppermute | solution.py:105
  55.3 1.5 collective-permute-done.5
  56.8 18.9 %collective-permute-done.7 = bf16[32,4096]{1,0:T(8,128)(2,1)S(1)} collective-permute-done((bf16[32,4096]{1,0:T(8,128)(2,1)S(1)}, bf16[32,4096]{1,0:T(8,128)(2,1)S(1)}, u32[]{:S(2)}, u32[]{:S(2)}) %collective-permute-start.7) | collective-permute-done | bytes 262176 | tf_op jit(solution)/shard_map/ppermute | solution.py:105
  76.8 1.4 collective-permute-start.17
  78.9 1.4 collective-permute-start.10
  80.3 3.9 %collective-permute-done.8 = bf16[32,4096]{1,0:T(8,128)(2,1)S(1)} collective-permute-done((bf16[32,4096]{1,0:T(8,128)(2,1)S(1)}, bf16[32,4096]{1,0:T(8,128)(2,1)S(1)}, u32[]{:S(2)}, u32[]{:S(2)}) %collective-permute-start.8) | collective-permute-done | bytes 262176 | tf_op jit(solution)/shard_map/ppermute | solution.py:89
  85.6 4.5 %collective-permute-done.10 = bf16[32,4096]{1,0:T(8,128)(2,1)S(1)} collective-permute-done((bf16[32,4096]{1,0:T(8,128)(2,1)S(1)}, bf16[32,4096]{1,0:T(8,128)(2,1)S(1)}, u32[]{:S(2)}, u32[]{:S(2)}) %collective-permute-start.10) | collective-permute-done | bytes 262176 | tf_op jit(solution)/shard_map/ppermute | solution.py:87
  90.1 3.1 %collective-permute-start.11 = (bf16[32,4096]{1,0:T(8,128)(2,1)S(1)}, bf16[32,4096]{1,0:T(8,128)(2,1)S(1)}, u32[]{:S(2)}, u32[]{:S(2)}) collective-permute-start(bf16[32,4096]{1,0:T(8,128)(2,1)S(1)} %get-tuple-element.13), channel_id=1, source_target_pairs={{0,1},{1,2},{2,3},{4,5},{5,6},{6,7},{8,9},{9,10},{10,11},{12,13},{... | collective-permute-start | bytes 786440 | tf_op jit(solution)/shard_map/ppermute | solution.py:88
  93.2 2.2 collective-permute-done.9
  95.3 1.4 collective-permute-start.12
  96.9 1.6 collective-permute-done.11
  98.5 1.4 collective-permute-start.14
  100.0 4.5 %collective-permute-done.12 = bf16[32,4096]{1,0:T(8,128)(2,1)S(1)} collective-permute-done((bf16[32,4096]{1,0:T(8,128)(2,1)S(1)}, bf16[32,4096]{1,0:T(8,128)(2,1)S(1)}, u32[]{:S(2)}, u32[]{:S(2)}) %collective-permute-start.12) | collective-permute-done | bytes 262176 | tf_op jit(solution)/shard_map/ppermute | solution.py:82
  104.5 1.4 collective-permute-start.13
  106.0 8.5 %collective-permute-done.17 = bf16[192,4096]{1,0:T(8,128)(2,1)} collective-permute-done((bf16[192,4096]{1,0:T(8,128)(2,1)}, bf16[192,4096]{1,0:T(8,128)(2,1)}, u32[]{:S(2)}, u32[]{:S(2)}) %collective-permute-start.17) | collective-permute-done | bytes 1572896 | tf_op jit(solution)/shard_map/ppermute | solution.py:82
  114.7 1.4 collective-permute-start.15
  116.4 22.8 %collective-permute-done.20 = bf16[192,4096]{1,0:T(8,128)(2,1)} collective-permute-done((bf16[192,4096]{1,0:T(8,128)(2,1)}, bf16[192,4096]{1,0:T(8,128)(2,1)}, u32[]{:S(2)}, u32[]{:S(2)}) %collective-permute-start.20) | collective-permute-done | bytes 1572896 | tf_op jit(solution)/shard_map/ppermute | solution.py:82
  139.2 1.5 collective-permute-start.27
  140.8 10.4 %collective-permute-done.27 = bf16[192,2048]{1,0:T(8,128)(2,1)S(1)} collective-permute-done((bf16[192,2048]{1,0:T(8,128)(2,1)S(1)}, bf16[192,2048]{1,0:T(8,128)(2,1)S(1)}, u32[]{:S(2)}, u32[]{:S(2)}) %collective-permute-start.27) | collective-permute-done | bytes 786464 | tf_op jit(solution)/shard_map/ppermute | solution.py:82
  151.2 1.5 collective-permute-start.23
  153.3 7.1 %fusion.1 = f32[256,768]{1,0:T(8,128)S(1)} fusion(bf16[256,4096]{1,0:T(8,128)(2,1)S(1)} %constant_dynamic-update-slice_fusion, bf16[192,4096]{1,0:T(8,128)(2,1)S(1)} %collective-permute-done.18, bf16[192,4096]{1,0:T(8,128)(2,1)} %collective-permute-done.17, bf16[192,4096]{1,0:T(8,128)(2,1)} %collective-permute-done.16, bf16[192,4096]{1,0:T(8,128)(2,1)} %bitcast.10), kind=kOutput, calls=%fused_computation.1 | convolution fusion | flops 1635778560 | bytes 9175040 | tf_op jit(solution)/shard_map/dot_general | solution.py:76
  160.4 10.2 %collective-permute-done.23 = bf16[192,2048]{1,0:T(8,128)(2,1)S(1)} collective-permute-done((bf16[192,2048]{1,0:T(8,128)(2,1)S(1)}, bf16[192,2048]{1,0:T(8,128)(2,1)S(1)}, u32[]{:S(2)}, u32[]{:S(2)}) %collective-permute-start.23) | collective-permute-done | bytes 786464 | tf_op jit(solution)/shard_map/ppermute | solution.py:82
  171.1 9.0 %collective-permute-done.29 = bf16[192,2048]{1,0:T(8,128)(2,1)S(1)} collective-permute-done((bf16[192,2048]{1,0:T(8,128)(2,1)S(1)}, bf16[192,2048]{1,0:T(8,128)(2,1)S(1)}, u32[]{:S(2)}, u32[]{:S(2)}) %collective-permute-start.29) | collective-permute-done | bytes 786464 | tf_op jit(solution)/shard_map/ppermute | solution.py:82
  180.0 7.3 %multiply_convert_fusion = bf16[256,768]{1,0:T(8,128)(2,1)S(1)} fusion(f32[256,768]{1,0:T(8,128)S(1)} %fusion.1, bf16[256,4096]{1,0:T(8,128)(2,1)S(1)} %constant_dynamic-update-slice_fusion, bf16[192,4096]{1,0:T(8,128)(2,1)S(1)} %collective-permute-done.21, bf16[192,4096]{1,0:T(8,128)(2,1)} %collective-permute-done.20, ...), kind=kOutput, calls=%fused_computation.53 | convolution fusion | flops 1636958208 | bytes 9568256 | tf_op jit(solution)/shard_map/dot_general | solution.py:77
  187.3 1.6 collective-permute-start.25
  190.6 4.5 %collective-permute-done.25 = bf16[128,768]{1,0:T(8,128)(2,1)S(1)} collective-permute-done((bf16[128,768]{1,0:T(8,128)(2,1)S(1)}, bf16[128,768]{1,0:T(8,128)(2,1)S(1)}, u32[]{:S(2)}, u32[]{:S(2)}) %collective-permute-start.25) | collective-permute-done | bytes 196640 | tf_op jit(solution)/shard_map/ppermute | solution.py:82
  195.1 3.8 %collective-permute-done.26 = bf16[128,768]{1,0:T(8,128)(2,1)S(1)} collective-permute-done((bf16[128,768]{1,0:T(8,128)(2,1)S(1)}, bf16[128,768]{1,0:T(8,128)(2,1)S(1)}, u32[]{:S(2)}, u32[]{:S(2)}) %collective-permute-start.26) | collective-permute-done | bytes 196640 | tf_op jit(solution)/shard_map/ppermute | solution.py:82
  200.1 11.3 %collective-permute-start.33 = (bf16[2,32,2048]{2,1,0:T(8,128)(2,1)S(1)}, bf16[2,32,2048]{2,1,0:T(8,128)(2,1)S(1)}, u32[]{:S(2)}, u32[]{:S(2)}) collective-permute-start(bf16[2,32,2048]{2,1,0:T(8,128)(2,1)S(1)} %broadcast_select_fusion), channel_id=1, source_target_pairs={{0,1},{3,2},{4,5},{7,6},{8,9},{11,10},{12,13},{15,14},{16,17},{19,... | collective-permute-start | bytes 786440 | tf_op jit(solution)/shard_map/ppermute | solution.py:101
  211.5 1.3 collective-permute-start.31
  212.8 1.3 collective-permute-start.32
  214.1 4.0 %collective-permute-done.33 = bf16[2,32,2048]{2,1,0:T(8,128)(2,1)S(1)} collective-permute-done((bf16[2,32,2048]{2,1,0:T(8,128)(2,1)S(1)}, bf16[2,32,2048]{2,1,0:T(8,128)(2,1)S(1)}, u32[]{:S(2)}, u32[]{:S(2)}) %collective-permute-start.33) | collective-permute-done | bytes 262176 | tf_op jit(solution)/shard_map/ppermute | solution.py:101
  218.2 5.5 %collective-permute-done.31 = bf16[2,32,2048]{2,1,0:T(8,128)(2,1)S(1)} collective-permute-done((bf16[2,32,2048]{2,1,0:T(8,128)(2,1)S(1)}, bf16[2,32,2048]{2,1,0:T(8,128)(2,1)S(1)}, u32[]{:S(2)}, u32[]{:S(2)}) %collective-permute-start.31) | collective-permute-done | bytes 262176 | tf_op jit(solution)/shard_map/ppermute | solution.py:102
  223.7 9.6 %collective-permute-done.34 = bf16[2,32,2048]{2,1,0:T(8,128)(2,1)S(1)} collective-permute-done((bf16[2,32,2048]{2,1,0:T(8,128)(2,1)S(1)}, bf16[2,32,2048]{2,1,0:T(8,128)(2,1)S(1)}, u32[]{:S(2)}, u32[]{:S(2)}) %collective-permute-start.34) | collective-permute-done | bytes 262176 | tf_op jit(solution)/shard_map/ppermute | solution.py:105
  233.4 1.8 collective-permute-start.35
  235.2 3.3 %collective-permute-done.35 = bf16[32,2048]{1,0:T(8,128)(2,1)S(1)} collective-permute-done((bf16[32,2048]{1,0:T(8,128)(2,1)S(1)}, bf16[32,2048]{1,0:T(8,128)(2,1)S(1)}, u32[]{:S(2)}, u32[]{:S(2)}) %collective-permute-start.35) | collective-permute-done | bytes 131104 | tf_op jit(solution)/shard_map/ppermute | solution.py:82
  (101 shorter events, 18.9 us)
Async XLA Ops:
  0.0 25.6 %copy-start = (bf16[4096,128]{1,0:T(8,128)(2,1)S(1)}, bf16[4096,128]{1,0:T(8,128)(2,1)}, u32[]{:S(2)}) copy-start(bf16[4096,128]{1,0:T(8,128)(2,1)} %param.29) | copy-start | bytes 3145732
  0.0 17.0 %collective-permute-start = (bf16[32,4096]{1,0:T(8,128)(2,1)}, bf16[32,4096]{1,0:T(8,128)(2,1)S(1)}, u32[]{:S(2)}, u32[]{:S(2)}) collective-permute-start(bf16[32,4096]{1,0:T(8,128)(2,1)} %param.19), channel_id=1, source_target_pairs={{0,2},{1,3},{2,0},{3,1},{4,6},{5,7},{6,4},{7,5},{8,10},{9,11},{10,... | collective-permute-start | bytes 786440 | tf_op jit(solution)/shard_map/ppermute | solution.py:89
  4.0 14.6 %collective-permute-start.2 = (bf16[32,4096]{1,0:T(8,128)(2,1)}, bf16[32,4096]{1,0:T(8,128)(2,1)S(1)}, u32[]{:S(2)}, u32[]{:S(2)}) collective-permute-start(bf16[32,4096]{1,0:T(8,128)(2,1)} %param.19), channel_id=1, source_target_pairs={{1,0},{2,1},{3,2},{5,4},{6,5},{7,6},{9,8},{10,9},{11,10},{13,12},{... | collective-permute-start | bytes 786440 | tf_op jit(solution)/shard_map/ppermute | solution.py:87
  5.3 13.4 %collective-permute-start.3 = (bf16[32,4096]{1,0:T(8,128)(2,1)}, bf16[32,4096]{1,0:T(8,128)(2,1)S(1)}, u32[]{:S(2)}, u32[]{:S(2)}) collective-permute-start(bf16[32,4096]{1,0:T(8,128)(2,1)} %param.19), channel_id=1, source_target_pairs={{0,1},{1,2},{2,3},{4,5},{5,6},{6,7},{8,9},{9,10},{10,11},{12,13},{... | collective-permute-start | bytes 786440 | tf_op jit(solution)/shard_map/ppermute | solution.py:88
  17.0 8.5 %collective-permute-start.1 = (bf16[32,4096]{1,0:T(8,128)(2,1)S(1)}, bf16[32,4096]{1,0:T(8,128)(2,1)S(1)}, u32[]{:S(2)}, u32[]{:S(2)}) collective-permute-start(bf16[32,4096]{1,0:T(8,128)(2,1)S(1)} %collective-permute-done), channel_id=1, source_target_pairs={{1,0},{2,3},{5,4},{6,7},{9,8},{10,11},{13,12},{14,15},{17,16},{18,... | collective-permute-start | bytes 786440 | tf_op jit(solution)/shard_map/ppermute | solution.py:90
  25.6 1.6 copy-start.2
  30.6 3.4 %copy-start.6 = (f32[512]{0:T(512)S(1)}, f32[512]{0:T(512)}, u32[]{:S(2)}) copy-start(f32[512]{0:T(512)} %param.28) | copy-start | bytes 6148
  30.6 3.4 %copy-start.7 = (f32[512]{0:T(512)S(1)}, f32[512]{0:T(512)}, u32[]{:S(2)}) copy-start(f32[512]{0:T(512)} %param.27) | copy-start | bytes 6148
  33.9 1.1 copy-start.8
  43.0 32.9 %copy-start.4 = (f32[4096]{0:T(1024)S(1)}, f32[4096]{0:T(1024)}, u32[]{:S(2)}) copy-start(f32[4096]{0:T(1024)} %param.33) | copy-start | bytes 49156
  43.1 42.3 %copy-start.1 = (bf16[4096,192]{0,1:T(8,128)(2,1)S(1)}, bf16[4096,192]{0,1:T(8,128)(2,1)}, u32[]{:S(2)}) copy-start(bf16[4096,192]{0,1:T(8,128)(2,1)} %param.37) | copy-start | bytes 4718596
  43.1 7.8 %collective-permute-start.6 = (bf16[32,4096]{1,0:T(8,128)(2,1)S(1)}, bf16[32,4096]{1,0:T(8,128)(2,1)S(1)}, u32[]{:S(2)}, u32[]{:S(2)}) collective-permute-start(bf16[32,4096]{1,0:T(8,128)(2,1)S(1)} %get-tuple-element.21), channel_id=1, source_target_pairs={{0,1},{3,2},{4,5},{7,6},{8,9},{11,10},{12,13},{15,14},{16,17},{19,... | collective-permute-start | bytes 786440 | tf_op jit(solution)/shard_map/ppermute | solution.py:101
  44.7 10.6 %collective-permute-start.4 = (bf16[32,4096]{1,0:T(8,128)(2,1)S(1)}, bf16[32,4096]{1,0:T(8,128)(2,1)S(1)}, u32[]{:S(2)}, u32[]{:S(2)}) collective-permute-start(bf16[32,4096]{1,0:T(8,128)(2,1)S(1)} %get-tuple-element.20), channel_id=1, source_target_pairs={{0,1},{1,2},{2,3},{4,5},{5,6},{6,7},{8,9},{9,10},{10,11},{12,13},{... | collective-permute-start | bytes 786440 | tf_op jit(solution)/shard_map/ppermute | solution.py:102
  46.0 10.7 %collective-permute-start.5 = (bf16[32,4096]{1,0:T(8,128)(2,1)S(1)}, bf16[32,4096]{1,0:T(8,128)(2,1)S(1)}, u32[]{:S(2)}, u32[]{:S(2)}) collective-permute-start(bf16[32,4096]{1,0:T(8,128)(2,1)S(1)} %get-tuple-element.22), channel_id=1, source_target_pairs={{1,0},{2,1},{3,2},{5,4},{6,5},{7,6},{9,8},{10,9},{11,10},{13,12},{... | collective-permute-start | bytes 786440 | tf_op jit(solution)/shard_map/ppermute | solution.py:103
  51.0 24.7 %collective-permute-start.7 = (bf16[32,4096]{1,0:T(8,128)(2,1)S(1)}, bf16[32,4096]{1,0:T(8,128)(2,1)S(1)}, u32[]{:S(2)}, u32[]{:S(2)}) collective-permute-start(bf16[32,4096]{1,0:T(8,128)(2,1)S(1)} %add_convert_fusion.2), channel_id=1, source_target_pairs={{0,2},{1,3},{2,0},{3,1},{4,6},{5,7},{6,4},{7,5},{8,10},{9,11},{10,... | collective-permute-start | bytes 786440 | tf_op jit(solution)/shard_map/ppermute | solution.py:105
  76.8 7.3 %collective-permute-start.8 = (bf16[32,4096]{1,0:T(8,128)(2,1)S(1)}, bf16[32,4096]{1,0:T(8,128)(2,1)S(1)}, u32[]{:S(2)}, u32[]{:S(2)}) collective-permute-start(bf16[32,4096]{1,0:T(8,128)(2,1)S(1)} %get-tuple-element.13), channel_id=1, source_target_pairs={{0,2},{1,3},{2,0},{3,1},{4,6},{5,7},{6,4},{7,5},{8,10},{9,11},{10,... | collective-permute-start | bytes 786440 | tf_op jit(solution)/shard_map/ppermute | solution.py:89
  76.8 37.6 %collective-permute-start.17 = (bf16[192,4096]{1,0:T(8,128)(2,1)}, bf16[192,4096]{1,0:T(8,128)(2,1)}, u32[]{:S(2)}, u32[]{:S(2)}) collective-permute-start(bf16[192,4096]{1,0:T(8,128)(2,1)} %bitcast.10), channel_id=1, source_target_pairs={{0,8},{8,0},{1,9},{9,1},{2,10},{10,2},{3,11},{11,3},{4,12},{12,4},... | collective-permute-start | bytes 4718600 | tf_op jit(solution)/shard_map/ppermute | solution.py:82
  78.3 74.4 %collective-permute-start.16 = (bf16[192,4096]{1,0:T(8,128)(2,1)}, bf16[192,4096]{1,0:T(8,128)(2,1)}, u32[]{:S(2)}, u32[]{:S(2)}) collective-permute-start(bf16[192,4096]{1,0:T(8,128)(2,1)} %bitcast.10), channel_id=1, source_target_pairs={{0,4},{4,0},{1,5},{5,1},{2,6},{6,2},{3,7},{7,3},{8,12},{12,8},{9,1... | collective-permute-start | bytes 4718600 | tf_op jit(solution)/shard_map/ppermute | solution.py:82
  78.3 60.9 %collective-permute-start.20 = (bf16[192,4096]{1,0:T(8,128)(2,1)}, bf16[192,4096]{1,0:T(8,128)(2,1)}, u32[]{:S(2)}, u32[]{:S(2)}) collective-permute-start(bf16[192,4096]{1,0:T(8,128)(2,1)} %bitcast.11), channel_id=1, source_target_pairs={{0,8},{8,0},{1,9},{9,1},{2,10},{10,2},{3,11},{11,3},{4,12},{12,4},... | collective-permute-start | bytes 4718600 | tf_op jit(solution)/shard_map/ppermute | solution.py:82
  78.9 17.9 %copy-start.3 = (bf16[256,4096]{1,0:T(8,128)(2,1)S(1)}, bf16[256,4096]{1,0:T(8,128)(2,1)}, u32[]{:S(2)}) copy-start(bf16[256,4096]{1,0:T(8,128)(2,1)} %get-tuple-element.12) | copy-start | bytes 6291460
  78.9 11.2 %collective-permute-start.10 = (bf16[32,4096]{1,0:T(8,128)(2,1)S(1)}, bf16[32,4096]{1,0:T(8,128)(2,1)S(1)}, u32[]{:S(2)}, u32[]{:S(2)}) collective-permute-start(bf16[32,4096]{1,0:T(8,128)(2,1)S(1)} %get-tuple-element.13), channel_id=1, source_target_pairs={{1,0},{2,1},{3,2},{5,4},{6,5},{7,6},{9,8},{10,9},{11,10},{13,12},{... | collective-permute-start | bytes 786440 | tf_op jit(solution)/shard_map/ppermute | solution.py:87
  84.2 11.2 %collective-permute-start.9 = (bf16[32,4096]{1,0:T(8,128)(2,1)S(1)}, bf16[32,4096]{1,0:T(8,128)(2,1)S(1)}, u32[]{:S(2)}, u32[]{:S(2)}) collective-permute-start(bf16[32,4096]{1,0:T(8,128)(2,1)S(1)} %collective-permute-done.8), channel_id=1, source_target_pairs={{1,0},{2,3},{5,4},{6,7},{9,8},{10,11},{13,12},{14,15},{17,16},{18,... | collective-permute-start | bytes 786440 | tf_op jit(solution)/shard_map/ppermute | solution.py:90
  90.1 8.5 %collective-permute-start.11 = (bf16[32,4096]{1,0:T(8,128)(2,1)S(1)}, bf16[32,4096]{1,0:T(8,128)(2,1)S(1)}, u32[]{:S(2)}, u32[]{:S(2)}) collective-permute-start(bf16[32,4096]{1,0:T(8,128)(2,1)S(1)} %get-tuple-element.13), channel_id=1, source_target_pairs={{0,1},{1,2},{2,3},{4,5},{5,6},{6,7},{8,9},{9,10},{10,11},{12,13},{... | collective-permute-start | bytes 786440 | tf_op jit(solution)/shard_map/ppermute | solution.py:88
  95.3 9.2 %collective-permute-start.12 = (bf16[32,4096]{1,0:T(8,128)(2,1)S(1)}, bf16[32,4096]{1,0:T(8,128)(2,1)S(1)}, u32[]{:S(2)}, u32[]{:S(2)}) collective-permute-start(bf16[32,4096]{1,0:T(8,128)(2,1)S(1)} %get-tuple-element.13), channel_id=1, source_target_pairs={{0,16},{16,0},{1,17},{17,1},{2,18},{18,2},{3,19},{19,3},{4,20},{20... | collective-permute-start | bytes 786440 | tf_op jit(solution)/shard_map/ppermute | solution.py:82
  98.5 17.6 %collective-permute-start.14 = (bf16[32,4096]{1,0:T(8,128)(2,1)S(1)}, bf16[32,4096]{1,0:T(8,128)(2,1)S(1)}, u32[]{:S(2)}, u32[]{:S(2)}) collective-permute-start(bf16[32,4096]{1,0:T(8,128)(2,1)S(1)} %collective-permute-done.8), channel_id=1, source_target_pairs={{0,16},{16,0},{1,17},{17,1},{2,18},{18,2},{3,19},{19,3},{4,20},{20... | collective-permute-start | bytes 786440 | tf_op jit(solution)/shard_map/ppermute | solution.py:82
  104.5 10.1 %collective-permute-start.13 = (bf16[32,4096]{1,0:T(8,128)(2,1)S(1)}, bf16[32,4096]{1,0:T(8,128)(2,1)S(1)}, u32[]{:S(2)}, u32[]{:S(2)}) collective-permute-start(bf16[32,4096]{1,0:T(8,128)(2,1)S(1)} %get-tuple-element.11), channel_id=1, source_target_pairs={{0,16},{16,0},{1,17},{17,1},{2,18},{18,2},{3,19},{19,3},{4,20},{20... | collective-permute-start | bytes 786440 | tf_op jit(solution)/shard_map/ppermute | solution.py:82
  114.5 38.2 %collective-permute-start.18 = (bf16[192,4096]{1,0:T(8,128)(2,1)}, bf16[192,4096]{1,0:T(8,128)(2,1)S(1)}, u32[]{:S(2)}, u32[]{:S(2)}) collective-permute-start(bf16[192,4096]{1,0:T(8,128)(2,1)} %collective-permute-done.17), channel_id=1, source_target_pairs={{0,4},{4,0},{1,5},{5,1},{2,6},{6,2},{3,7},{7,3},{8,12},{12,8},{9,1... | collective-permute-start | bytes 4718600 | tf_op jit(solution)/shard_map/ppermute | solution.py:82
  114.7 26.1 %collective-permute-start.15 = (bf16[32,4096]{1,0:T(8,128)(2,1)S(1)}, bf16[32,4096]{1,0:T(8,128)(2,1)S(1)}, u32[]{:S(2)}, u32[]{:S(2)}) collective-permute-start(bf16[32,4096]{1,0:T(8,128)(2,1)S(1)} %get-tuple-element.9), channel_id=1, source_target_pairs={{0,16},{16,0},{1,17},{17,1},{2,18},{18,2},{3,19},{19,3},{4,20},{20... | collective-permute-start | bytes 786440 | tf_op jit(solution)/shard_map/ppermute | solution.py:82
  116.1 54.4 %collective-permute-start.19 = (bf16[192,4096]{1,0:T(8,128)(2,1)}, bf16[192,4096]{1,0:T(8,128)(2,1)S(1)}, u32[]{:S(2)}, u32[]{:S(2)}) collective-permute-start(bf16[192,4096]{1,0:T(8,128)(2,1)} %bitcast.11), channel_id=1, source_target_pairs={{0,4},{4,0},{1,5},{5,1},{2,6},{6,2},{3,7},{7,3},{8,12},{12,8},{9,1... | collective-permute-start | bytes 4718600 | tf_op jit(solution)/shard_map/ppermute | solution.py:82
  139.2 12.0 %collective-permute-start.27 = (bf16[192,2048]{1,0:T(8,128)(2,1)S(1)}, bf16[192,2048]{1,0:T(8,128)(2,1)S(1)}, u32[]{:S(2)}, u32[]{:S(2)}) collective-permute-start(bf16[192,2048]{1,0:T(8,128)(2,1)S(1)} %get-tuple-element.16), channel_id=1, source_target_pairs={{0,16},{16,0},{1,17},{17,1},{2,18},{18,2},{3,19},{19,3},{4,20},{20... | collective-permute-start | bytes 2359304 | tf_op jit(solution)/shard_map/ppermute | solution.py:82
  140.7 39.3 %collective-permute-start.21 = (bf16[192,4096]{1,0:T(8,128)(2,1)}, bf16[192,4096]{1,0:T(8,128)(2,1)S(1)}, u32[]{:S(2)}, u32[]{:S(2)}) collective-permute-start(bf16[192,4096]{1,0:T(8,128)(2,1)} %collective-permute-done.20), channel_id=1, source_target_pairs={{0,4},{4,0},{1,5},{5,1},{2,6},{6,2},{3,7},{7,3},{8,12},{12,8},{9,1... | collective-permute-start | bytes 4718600 | tf_op jit(solution)/shard_map/ppermute | solution.py:82
  151.2 19.4 %collective-permute-start.23 = (bf16[192,2048]{1,0:T(8,128)(2,1)S(1)}, bf16[192,2048]{1,0:T(8,128)(2,1)S(1)}, u32[]{:S(2)}, u32[]{:S(2)}) collective-permute-start(bf16[192,2048]{1,0:T(8,128)(2,1)S(1)} %get-tuple-element.17), channel_id=1, source_target_pairs={{0,8},{8,0},{1,9},{9,1},{2,10},{10,2},{3,11},{11,3},{4,12},{12,4},... | collective-permute-start | bytes 2359304 | tf_op jit(solution)/shard_map/ppermute | solution.py:82
  152.7 36.2 %collective-permute-start.22 = (bf16[192,2048]{1,0:T(8,128)(2,1)S(1)}, bf16[192,2048]{1,0:T(8,128)(2,1)S(1)}, u32[]{:S(2)}, u32[]{:S(2)}) collective-permute-start(bf16[192,2048]{1,0:T(8,128)(2,1)S(1)} %get-tuple-element.17), channel_id=1, source_target_pairs={{0,4},{4,0},{1,5},{5,1},{2,6},{6,2},{3,7},{7,3},{8,12},{12,8},{9,1... | collective-permute-start | bytes 2359304 | tf_op jit(solution)/shard_map/ppermute | solution.py:82
  152.7 27.3 %collective-permute-start.29 = (bf16[192,2048]{1,0:T(8,128)(2,1)S(1)}, bf16[192,2048]{1,0:T(8,128)(2,1)S(1)}, u32[]{:S(2)}, u32[]{:S(2)}) collective-permute-start(bf16[192,2048]{1,0:T(8,128)(2,1)S(1)} %collective-permute-done.27), channel_id=1, source_target_pairs={{0,8},{8,0},{1,9},{9,1},{2,10},{10,2},{3,11},{11,3},{4,12},{12,4},... | collective-permute-start | bytes 2359304 | tf_op jit(solution)/shard_map/ppermute | solution.py:82
  170.6 20.1 %collective-permute-start.28 = (bf16[192,2048]{1,0:T(8,128)(2,1)S(1)}, bf16[192,2048]{1,0:T(8,128)(2,1)S(1)}, u32[]{:S(2)}, u32[]{:S(2)}) collective-permute-start(bf16[192,2048]{1,0:T(8,128)(2,1)S(1)} %collective-permute-done.27), channel_id=1, source_target_pairs={{0,4},{4,0},{1,5},{5,1},{2,6},{6,2},{3,7},{7,3},{8,12},{12,8},{9,1... | collective-permute-start | bytes 2359304 | tf_op jit(solution)/shard_map/ppermute | solution.py:82
  170.6 18.9 %collective-permute-start.24 = (bf16[192,2048]{1,0:T(8,128)(2,1)S(1)}, bf16[192,2048]{1,0:T(8,128)(2,1)S(1)}, u32[]{:S(2)}, u32[]{:S(2)}) collective-permute-start(bf16[192,2048]{1,0:T(8,128)(2,1)S(1)} %collective-permute-done.23), channel_id=1, source_target_pairs={{0,4},{4,0},{1,5},{5,1},{2,6},{6,2},{3,7},{7,3},{8,12},{12,8},{9,1... | collective-permute-start | bytes 2359304 | tf_op jit(solution)/shard_map/ppermute | solution.py:82
  180.0 10.6 %collective-permute-start.30 = (bf16[192,2048]{1,0:T(8,128)(2,1)S(1)}, bf16[192,2048]{1,0:T(8,128)(2,1)S(1)}, u32[]{:S(2)}, u32[]{:S(2)}) collective-permute-start(bf16[192,2048]{1,0:T(8,128)(2,1)S(1)} %collective-permute-done.29), channel_id=1, source_target_pairs={{0,4},{4,0},{1,5},{5,1},{2,6},{6,2},{3,7},{7,3},{8,12},{12,8},{9,1... | collective-permute-start | bytes 2359304 | tf_op jit(solution)/shard_map/ppermute | solution.py:82
  187.3 7.8 %collective-permute-start.25 = (bf16[128,768]{1,0:T(8,128)(2,1)S(1)}, bf16[128,768]{1,0:T(8,128)(2,1)S(1)}, u32[]{:S(2)}, u32[]{:S(2)}) collective-permute-start(bf16[128,768]{1,0:T(8,128)(2,1)S(1)} %get-tuple-element.25), channel_id=1, source_target_pairs={{0,16},{16,0},{1,17},{17,1},{2,18},{18,2},{3,19},{19,3},{4,20},{20... | collective-permute-start | bytes 589832 | tf_op jit(solution)/shard_map/ppermute | solution.py:82
  188.9 10.0 %collective-permute-start.26 = (bf16[128,768]{1,0:T(8,128)(2,1)S(1)}, bf16[128,768]{1,0:T(8,128)(2,1)S(1)}, u32[]{:S(2)}, u32[]{:S(2)}) collective-permute-start(bf16[128,768]{1,0:T(8,128)(2,1)S(1)} %get-tuple-element.26), channel_id=1, source_target_pairs={{0,16},{16,0},{1,17},{17,1},{2,18},{18,2},{3,19},{19,3},{4,20},{20... | collective-permute-start | bytes 589832 | tf_op jit(solution)/shard_map/ppermute | solution.py:82
  200.1 18.0 %collective-permute-start.33 = (bf16[2,32,2048]{2,1,0:T(8,128)(2,1)S(1)}, bf16[2,32,2048]{2,1,0:T(8,128)(2,1)S(1)}, u32[]{:S(2)}, u32[]{:S(2)}) collective-permute-start(bf16[2,32,2048]{2,1,0:T(8,128)(2,1)S(1)} %broadcast_select_fusion), channel_id=1, source_target_pairs={{0,1},{3,2},{4,5},{7,6},{8,9},{11,10},{12,13},{15,14},{16,17},{19,... | collective-permute-start | bytes 786440 | tf_op jit(solution)/shard_map/ppermute | solution.py:101
  211.4 27.2 %copy-start.5 = (f32[4096]{0:T(1024)S(1)}, f32[4096]{0:T(1024)}, u32[]{:S(2)}) copy-start(f32[4096]{0:T(1024)} %param.34) | copy-start | bytes 49156
  211.5 12.2 %collective-permute-start.31 = (bf16[2,32,2048]{2,1,0:T(8,128)(2,1)S(1)}, bf16[2,32,2048]{2,1,0:T(8,128)(2,1)S(1)}, u32[]{:S(2)}, u32[]{:S(2)}) collective-permute-start(bf16[2,32,2048]{2,1,0:T(8,128)(2,1)S(1)} %get-tuple-element.18), channel_id=1, source_target_pairs={{0,1},{1,2},{2,3},{4,5},{5,6},{6,7},{8,9},{9,10},{10,11},{12,13},{... | collective-permute-start | bytes 786440 | tf_op jit(solution)/shard_map/ppermute | solution.py:102
  212.8 10.9 %collective-permute-start.32 = (bf16[2,32,2048]{2,1,0:T(8,128)(2,1)S(1)}, bf16[2,32,2048]{2,1,0:T(8,128)(2,1)S(1)}, u32[]{:S(2)}, u32[]{:S(2)}) collective-permute-start(bf16[2,32,2048]{2,1,0:T(8,128)(2,1)S(1)} %get-tuple-element.19), channel_id=1, source_target_pairs={{1,0},{2,1},{3,2},{5,4},{6,5},{7,6},{9,8},{10,9},{11,10},{13,12},{... | collective-permute-start | bytes 786440 | tf_op jit(solution)/shard_map/ppermute | solution.py:103
  218.2 15.1 %collective-permute-start.34 = (bf16[2,32,2048]{2,1,0:T(8,128)(2,1)S(1)}, bf16[2,32,2048]{2,1,0:T(8,128)(2,1)S(1)}, u32[]{:S(2)}, u32[]{:S(2)}) collective-permute-start(bf16[2,32,2048]{2,1,0:T(8,128)(2,1)S(1)} %fusion.45), channel_id=1, source_target_pairs={{0,2},{1,3},{2,0},{3,1},{4,6},{5,7},{6,4},{7,5},{8,10},{9,11},{10,... | collective-permute-start | bytes 786440 | tf_op jit(solution)/shard_map/ppermute | solution.py:105
  233.4 5.0 %collective-permute-start.35 = (bf16[32,2048]{1,0:T(8,128)(2,1)S(1)}, bf16[32,2048]{1,0:T(8,128)(2,1)S(1)}, u32[]{:S(2)}, u32[]{:S(2)}) collective-permute-start(bf16[32,2048]{1,0:T(8,128)(2,1)S(1)} %fusion.53), channel_id=1, source_target_pairs={{0,16},{16,0},{1,17},{17,1},{2,18},{18,2},{3,19},{19,3},{4,20},{20... | collective-permute-start | bytes 393224 | tf_op jit(solution)/shard_map/ppermute | solution.py:82

commit v3 on v2

--- a/solution.py
+++ b/solution.py
@@ -82,28 +82,19 @@
     return lax.ppermute(block, axis, [(0, 1), (1, 0)])
 
 
+def shift(block, hops):
+    return lax.ppermute(block, "mlp", [((k + hops) % 4, k) for k in range(4)])
+
+
 def line_gather(block):
-    index = lax.axis_index("mlp")
-    from_right = lax.ppermute(block, "mlp", [(1, 0), (2, 1), (3, 2)])
-    from_left = lax.ppermute(block, "mlp", [(0, 1), (1, 2), (2, 3)])
-    across = lax.ppermute(block, "mlp", [(0, 2), (1, 3), (2, 0), (3, 1)])
-    far = lax.ppermute(across, "mlp", [(1, 0), (2, 3)])
-    return [
-        block,
-        jnp.where(index == 3, far, from_right),
-        across,
-        jnp.where(index == 0, far, from_left),
-    ]
+    across = shift(block, 2)
+    return [block, shift(block, 1), across, shift(block, 3)]
 
 
 def line_scatter(parts):
-    index = lax.axis_index("mlp")
-    far = lax.ppermute(jnp.where(index == 0, parts[3], parts[1]), "mlp", [(0, 1), (3, 2)])
-    to_right = lax.ppermute(parts[1], "mlp", [(0, 1), (1, 2), (2, 3)])
-    to_left = lax.ppermute(parts[3], "mlp", [(1, 0), (2, 1), (3, 2)])
-    across = (parts[2].astype(jnp.float32) + far.astype(jnp.float32)).astype(parts[2].dtype)
-    across = lax.ppermute(across, "mlp", [(0, 2), (1, 3), (2, 0), (3, 1)])
-    return sum(part.astype(jnp.float32) for part in (parts[0], to_right, to_left, across))
+    across = shift(parts[2], 2)
+    arrived = (parts[0], shift(parts[3], 1), across, shift(parts[1], 3))
+    return sum(part.astype(jnp.float32) for part in arrived)
 
 
 def gather_group(block, direct):
@@ -118,18 +109,12 @@
     return lax.psum_scatter(rows, "mlp", scatter_dimension=0, tiled=True).astype(jnp.float32)
 
 
-def spread_weights(gate_rows, up_rows, down_rows):
-    gate_x, up_x = exchange(gate_rows, "x"), exchange(up_rows, "x")
-    half = down_rows.shape[1] // 2
-    y = lax.axis_index("y")
-    own = lax.dynamic_slice_in_dim(down_rows, y * half, half, axis=1)
-    other = exchange(lax.dynamic_slice_in_dim(down_rows, (1 - y) * half, half, axis=1), "y")
-    own_x, other_x = exchange(own, "x"), exchange(other, "x")
-
-    def quad(rows, rows_x):
-        return jnp.concatenate([rows, exchange(rows, "core"), rows_x, exchange(rows_x, "core")])
-
-    return quad(gate_rows, gate_x), quad(up_rows, up_x), quad(own, own_x), quad(other, other_x)
+def after(value, *events):
+    return lax.optimization_barrier((value, *events))[0]
+
+
+def both_cores(rows, rows_x):
+    return jnp.concatenate([rows, exchange(rows, "core"), rows_x, exchange(rows_x, "core")])
 
 
 def shards(
@@ -166,7 +151,11 @@
     )
     gate_rows, up_rows, down_rows = gate_weight.T, up_weight.T, down_weight_transposed.T
     if direct:
-        gate_rows, up_rows, down_near, down_far = spread_weights(gate_rows, up_rows, down_rows)
+        gate_x = exchange(gate_rows, "x")
+        half = down_rows.shape[1] // 2
+        y = lax.axis_index("y")
+        near = lax.dynamic_slice_in_dim(down_rows, y * half, half, axis=1)
+        far = exchange(lax.dynamic_slice_in_dim(down_rows, (1 - y) * half, half, axis=1), "y")
     group_token_rows = gather_group(layer_input, direct)
     columns = jnp.arange(ADAPTER_SLOTS * ADAPTER_RANK, dtype=jnp.int32) // ADAPTER_RANK
     slot_match_mask = (columns[None, :] == token_slot[:, None]).astype(jnp.bfloat16)
@@ -205,23 +194,32 @@
     context = attention(queries, key_heads, value_heads, request, position, window).reshape(
         tok_group, heads_local * HEAD_SIZE
     )
+    if direct:
+        context = after(context, gate_x, far)
+        up_x = exchange(after(up_rows, gate_x), "x")
     attn_own = scatter_group(
         jnp.dot(context, output_weight, preferred_element_type=jnp.float32).astype(jnp.bfloat16),
         direct,
     )
+    if direct:
+        attn_own = after(attn_own, up_x)
+        near_x = exchange(after(near, up_x), "x")
+        far_x = exchange(after(far, up_x), "x")
     residual_own = (
         layer_input.astype(jnp.float32) + rms_scale(attn_own) * attention_norm_gain
     ).astype(jnp.bfloat16)
     if direct:
         line = line_gather(residual_own)
         other = [exchange(block, "y") for block in line]
-        states = jnp.concatenate(line + other)
-        hidden = hidden_units(states, gate_rows, up_rows)
+        states = after(jnp.concatenate(line + other), near_x, far_x)
+        hidden = hidden_units(states, both_cores(gate_rows, gate_x), both_cores(up_rows, up_x))
         hidden_other = jnp.concatenate(
             [exchange(hidden[tok_group:], "y"), exchange(hidden[:tok_group], "y")]
         )
-        part = jnp.dot(hidden, down_near, preferred_element_type=jnp.float32)
-        part = part + jnp.dot(hidden_other, down_far, preferred_element_type=jnp.float32)
+        part = jnp.dot(hidden, both_cores(near, near_x), preferred_element_type=jnp.float32)
+        part = part + jnp.dot(
+            hidden_other, both_cores(far, far_x), preferred_element_type=jnp.float32
+        )
         part = part.astype(jnp.bfloat16).reshape(2, 4, tok_dev, -1)
         summed = line_scatter([part[:, k] for k in range(4)])
         own_half = summed[0]

time: 240 us -> 199 us (0.83)
  starting transfers between devices: 55.4 us -> 35.5 us
  waiting for transfers between devices: 143 us -> 125 us
  matrix products: 32.5 us -> 27.2 us
  local copies, waits for them, and re-layouts: 0.77 us -> 4.4 us
    ppermute x20, waiting for transfers between devices: 77.1 us -> 50.4 us  [exchange(): return lax.ppermute(block, axis, [(0, 1), (1, 0)])]
    ppermute x16 -> x12, starting transfers between devices: 39.4 us -> 20.2 us  [shift(): return lax.ppermute(block, 'mlp', [((k + hops) % 4, k) for k in range(4)])]
    ppermute x16 -> x12, waiting for transfers between devices: 66 us -> 74.7 us  [shift(): return lax.ppermute(block, 'mlp', [((k + hops) % 4, k) for k in range(4)])]
    dot_general x1, matrix products: 7.26 us -> 1.86 us  [hidden_units(): lax.dot_general(states, up_rows, contract, preferred_element_type=jnp.flo...]
    dynamic_slice x1, local copies, waits for them, and re-layouts: 0.11 us -> 2.69 us  [shards(): near = lax.dynamic_slice_in_dim(down_rows, y * half, half, axis=1)]
  transfers between devices with their start and end apart: 36 -> 32, of which waited for: 22 -> 16; matrix products, arithmetic and copies ran while one was open for 8% -> 18% of each run, Pallas kernels for 0% -> 0%
where the time goes in v3:
time: 199 us
  waiting for transfers between devices  125 us (63%)
  starting transfers between devices  35.5 us (18%)
  matrix products  27.2 us (14%)
  other arithmetic  6.17 us (3%)
  local copies, waits for them, and re-layouts  4.4 us (2%)
    ppermute x12, waiting for transfers between devices, shift(): return lax.ppermute(block, 'mlp', [((k + hops) % 4, k) for k in range(4)])  74.7 us
    ppermute x20, waiting for transfers between devices, exchange(): return lax.ppermute(block, axis, [(0, 1), (1, 0)])  50.4 us
    ppermute x12, starting transfers between devices, shift(): return lax.ppermute(block, 'mlp', [((k + hops) % 4, k) for k in range(4)])  20.2 us
    ppermute x20, starting transfers between devices, exchange(): return lax.ppermute(block, axis, [(0, 1), (1, 0)])  15.3 us
    dot_general x1, matrix products, hidden_units(): lax.dot_general(states, gate_rows, contract, preferred_element_type=jnp.f...  7.17 us
  transfers between devices with their start and end apart: 32, of which 16 were waited for; matrix products, arithmetic and copies ran while one was open for 18% of the time, Pallas kernels for 0%

profile of v3, /device:TPU:0, one launch (start us, length us, event | category | flops | bytes accessed | tf_op | source)
XLA Modules:
  0.0 198.7 jit_solution(6618908317174704965)
XLA Ops:
  0.0 5.1 %collective-permute-start = (bf16[32,4096]{1,0:T(8,128)(2,1)}, bf16[32,4096]{1,0:T(8,128)(2,1)S(1)}, u32[]{:S(2)}, u32[]{:S(2)}) collective-permute-start(bf16[32,4096]{1,0:T(8,128)(2,1)} %param.19), channel_id=1, source_target_pairs={{1,0},{2,1},{3,2},{0,3},{5,4},{6,5},{7,6},{4,7},{9,8},{10,9},{11,1... | collective-permute-start | bytes 786440 | tf_op jit(solution)/shard_map/ppermute | solution.py:86
  5.1 1.0 collective-permute-start.2
  6.2 2.7 %dynamic-slice_bitcast_fusion = (bf16[192,2048]{1,0:T(8,128)(2,1)}, bf16[192,2048]{1,0:T(8,128)(2,1)}) fusion(bf16[4096,192]{0,1:T(8,128)(2,1)} %param.37, s32[]{:T(128)S(6)} %select_n.60, s32[]{:T(128)S(6)} %select_n.58), kind=kLoop, calls=%fused_computation.51 | loop fusion | bytes 3145736 | tf_op jit(solution)/shard_map/dynamic_slice | solution.py:157
  8.8 1.5 collective-permute-start.4
  10.4 1.5 collective-permute-start.3
  12.5 1.0 multiply_cosine_fusion
  13.5 14.2 %collective-permute-done.1 = bf16[32,4096]{1,0:T(8,128)(2,1)S(1)} collective-permute-done((bf16[32,4096]{1,0:T(8,128)(2,1)}, bf16[32,4096]{1,0:T(8,128)(2,1)S(1)}, u32[]{:S(2)}, u32[]{:S(2)}) %collective-permute-start.1) | collective-permute-done | bytes 262176 | tf_op jit(solution)/shard_map/ppermute | solution.py:86
  28.3 2.9 %convolution_add_fusion = f32[128,512]{1,0:T(8,128)S(1)} fusion(f32[128,512]{1,0:T(8,128)S(1)} %convolution_multiply_fusion.1, bf16[128,4096]{1,0:T(8,128)(2,1)S(1)} %constant_dynamic-update-slice_fusion, bf16[4096,512]{1,0:T(8,128)(2,1)} %param.23), kind=kOutput, calls=%fused_computation.42 | convolution fusion | flops 536936448 | bytes 5767168 | tf_op jit(solution)/shard_map/dot_general | solution.py:174
  32.2 2.9 %fusion.100 = f32[128,512]{1,0:T(8,128)S(1)} fusion(bf16[128,4096]{1,0:T(8,128)(2,1)S(1)} %constant_dynamic-update-slice_fusion, bf16[4096,512]{1,0:T(8,128)(2,1)} %param.24), kind=kOutput, calls=%fused_computation.155 | convolution fusion | flops 536870912 | bytes 5505024 | tf_op jit(solution)/shard_map/dot_general | solution.py:177
  35.2 1.8 convolution_multiply_fusion.2
  37.0 2.9 %fusion.42 = bf16[128,512]{1,0:T(8,128)(2,1)S(1)} fusion(f32[128,512]{1,0:T(8,128)S(1)} %convolution_multiply_fusion.2, bf16[128,4096]{1,0:T(8,128)(2,1)S(1)} %constant_dynamic-update-slice_fusion, bf16[4096,512]{1,0:T(8,128)(2,1)} %param.25), kind=kOutput, calls=%fused_computation.45 | convolution fusion | flops 537001984 | bytes 5636096 | tf_op jit(solution)/shard_map/dot_general | solution.py:178
  40.1 0.9 copy.52
  41.3 0.9 fusion.50
  42.2 1.1 subtract_convert_fusion
  44.2 1.5 collective-permute-done.3
  45.7 1.5 collective-permute-start.8
  47.2 2.9 %convolution_convert_fusion = bf16[128,4096]{1,0:T(8,128)(2,1)S(1)} fusion(bf16[128,512]{0,1:T(8,128)(2,1)S(1)} %bitcast.85, bf16[512,4096]{1,0:T(8,128)(2,1)} %param.26), kind=kOutput, calls=%fused_computation.17 | convolution fusion | flops 537395200 | bytes 5373952 | tf_op jit(solution)/shard_map/dot_general | solution.py:201
  50.2 3.1 %collective-permute-start.5 = (bf16[32,4096]{1,0:T(8,128)(2,1)S(1)}, bf16[32,4096]{1,0:T(8,128)(2,1)S(1)}, u32[]{:S(2)}, u32[]{:S(2)}) collective-permute-start(bf16[32,4096]{1,0:T(8,128)(2,1)S(1)} %get-tuple-element.29), channel_id=1, source_target_pairs={{1,0},{2,1},{3,2},{0,3},{5,4},{6,5},{7,6},{4,7},{9,8},{10,9},{11,1... | collective-permute-start | bytes 786440 | tf_op jit(solution)/shard_map/ppermute | solution.py:86
  54.5 5.6 %collective-permute-done.5 = bf16[32,4096]{1,0:T(8,128)(2,1)S(1)} collective-permute-done((bf16[32,4096]{1,0:T(8,128)(2,1)S(1)}, bf16[32,4096]{1,0:T(8,128)(2,1)S(1)}, u32[]{:S(2)}, u32[]{:S(2)}) %collective-permute-start.5) | collective-permute-done | bytes 262176 | tf_op jit(solution)/shard_map/ppermute | solution.py:86
  60.1 14.6 %collective-permute-done.6 = bf16[32,4096]{1,0:T(8,128)(2,1)S(1)} collective-permute-done((bf16[32,4096]{1,0:T(8,128)(2,1)S(1)}, bf16[32,4096]{1,0:T(8,128)(2,1)S(1)}, u32[]{:S(2)}, u32[]{:S(2)}) %collective-permute-start.6) | collective-permute-done | bytes 262176 | tf_op jit(solution)/shard_map/ppermute | solution.py:86
  74.9 5.1 %collective-permute-done.8 = bf16[192,4096]{1,0:T(8,128)(2,1)S(1)} collective-permute-done((bf16[192,4096]{1,0:T(8,128)(2,1)}, bf16[192,4096]{1,0:T(8,128)(2,1)S(1)}, u32[]{:S(2)}, u32[]{:S(2)}) %collective-permute-start.8) | collective-permute-done | bytes 1572896 | tf_op jit(solution)/shard_map/ppermute | solution.py:82
  80.3 3.4 %collective-permute-start.9 = (bf16[32,4096]{1,0:T(8,128)(2,1)S(1)}, bf16[32,4096]{1,0:T(8,128)(2,1)S(1)}, u32[]{:S(2)}, u32[]{:S(2)}) collective-permute-start(bf16[32,4096]{1,0:T(8,128)(2,1)S(1)} %get-tuple-element.21), channel_id=1, source_target_pairs={{1,0},{2,1},{3,2},{0,3},{5,4},{6,5},{7,6},{4,7},{9,8},{10,9},{11,1... | collective-permute-start | bytes 786440 | tf_op jit(solution)/shard_map/ppermute | solution.py:86
  84.8 0.9 collective-permute-start.11
  85.8 4.6 %collective-permute-done.9 = bf16[32,4096]{1,0:T(8,128)(2,1)S(1)} collective-permute-done((bf16[32,4096]{1,0:T(8,128)(2,1)S(1)}, bf16[32,4096]{1,0:T(8,128)(2,1)S(1)}, u32[]{:S(2)}, u32[]{:S(2)}) %collective-permute-start.9) | collective-permute-done | bytes 262176 | tf_op jit(solution)/shard_map/ppermute | solution.py:86
  90.8 14.7 %collective-permute-done.10 = bf16[32,4096]{1,0:T(8,128)(2,1)S(1)} collective-permute-done((bf16[32,4096]{1,0:T(8,128)(2,1)S(1)}, bf16[32,4096]{1,0:T(8,128)(2,1)S(1)}, u32[]{:S(2)}, u32[]{:S(2)}) %collective-permute-start.10) | collective-permute-done | bytes 262176 | tf_op jit(solution)/shard_map/ppermute | solution.py:86
  105.5 1.5 collective-permute-start.17
  107.0 1.0 collective-permute-start.13
  108.1 1.1 collective-permute-start.14
  109.2 7.1 %collective-permute-done.13 = bf16[32,4096]{1,0:T(8,128)(2,1)S(1)} collective-permute-done((bf16[32,4096]{1,0:T(8,128)(2,1)S(1)}, bf16[32,4096]{1,0:T(8,128)(2,1)S(1)}, u32[]{:S(2)}, u32[]{:S(2)}) %collective-permute-start.13) | collective-permute-done | bytes 262176 | tf_op jit(solution)/shard_map/ppermute | solution.py:82
  116.3 1.0 collective-permute-start.15
  117.3 4.6 %collective-permute-done.14 = bf16[32,4096]{1,0:T(8,128)(2,1)S(1)} collective-permute-done((bf16[32,4096]{1,0:T(8,128)(2,1)S(1)}, bf16[32,4096]{1,0:T(8,128)(2,1)S(1)}, u32[]{:S(2)}, u32[]{:S(2)}) %collective-permute-start.14) | collective-permute-done | bytes 262176 | tf_op jit(solution)/shard_map/ppermute | solution.py:82
  122.0 2.9 %collective-permute-done.15 = bf16[32,4096]{1,0:T(8,128)(2,1)S(1)} collective-permute-done((bf16[32,4096]{1,0:T(8,128)(2,1)S(1)}, bf16[32,4096]{1,0:T(8,128)(2,1)S(1)}, u32[]{:S(2)}, u32[]{:S(2)}) %collective-permute-start.15) | collective-permute-done | bytes 262176 | tf_op jit(solution)/shard_map/ppermute | solution.py:82
  125.5 16.4 %collective-permute-done.16 = bf16[192,2048]{1,0:T(8,128)(2,1)S(1)} collective-permute-done((bf16[192,2048]{1,0:T(8,128)(2,1)S(1)}, bf16[192,2048]{1,0:T(8,128)(2,1)S(1)}, u32[]{:S(2)}, u32[]{:S(2)}) %collective-permute-start.16) | collective-permute-done | bytes 786464 | tf_op jit(solution)/shard_map/ppermute | solution.py:82
  142.5 7.2 %fusion.1 = f32[256,768]{1,0:T(8,128)S(1)} fusion(bf16[256,4096]{1,0:T(8,128)(2,1)S(1)} %constant_dynamic-update-slice_fusion.4, bf16[192,4096]{1,0:T(8,128)(2,1)S(1)} %collective-permute-done.19, bf16[192,4096]{1,0:T(8,128)(2,1)} %collective-permute-done.3, bf16[192,4096]{1,0:T(8,128)(2,1)S(1)} %collective-permute-done.18, bf16[192,4096]{1,0:T(8,128)(2,1)} %bitcast.10), kind=kOutput, calls=%fused_computation.1 | convolution fusion | flops 1635778560 | bytes 9175040 | tf_op jit(solution)/shard_map/dot_general | solution.py:76
  150.2 1.9 multiply_convert_fusion
  152.1 1.2 collective-permute-start.24
  153.3 0.9 collective-permute-start.25
  154.2 5.7 %collective-permute-done.24 = bf16[128,768]{1,0:T(8,128)(2,1)S(1)} collective-permute-done((bf16[128,768]{1,0:T(8,128)(2,1)S(1)}, bf16[128,768]{1,0:T(8,128)(2,1)S(1)}, u32[]{:S(2)}, u32[]{:S(2)}) %collective-permute-start.24) | collective-permute-done | bytes 196640 | tf_op jit(solution)/shard_map/ppermute | solution.py:82
  159.9 3.3 %collective-permute-done.25 = bf16[128,768]{1,0:T(8,128)(2,1)S(1)} collective-permute-done((bf16[128,768]{1,0:T(8,128)(2,1)S(1)}, bf16[128,768]{1,0:T(8,128)(2,1)S(1)}, u32[]{:S(2)}, u32[]{:S(2)}) %collective-permute-start.25) | collective-permute-done | bytes 196640 | tf_op jit(solution)/shard_map/ppermute | solution.py:82
  163.3 2.1 %fusion.25 = f32[256,2048]{1,0:T(8,128)S(1)} fusion(bf16[192,2048]{1,0:T(8,128)(2,1)S(1)} %collective-permute-done.27, bf16[192,2048]{1,0:T(8,128)(2,1)S(1)} %collective-permute-done.17, bf16[192,2048]{1,0:T(8,128)(2,1)S(1)} %collective-permute-done.26, bf16[192,2048]{1,0:T(8,128)(2,1)} %collective-permute-done.4, ...), kind=kOutput, calls=%fused_computation.26 | convolution fusion | flops 818675712 | bytes 5636096 | tf_op jit(solution)/shard_map/dot_general | solution.py:220
  165.4 1.2 fusion.36
  166.8 3.4 %collective-permute-start.29 = (bf16[2,32,2048]{2,1,0:T(8,128)(2,1)S(1)}, bf16[2,32,2048]{2,1,0:T(8,128)(2,1)S(1)}, u32[]{:S(2)}, u32[]{:S(2)}) collective-permute-start(bf16[2,32,2048]{2,1,0:T(8,128)(2,1)S(1)} %get-tuple-element.27), channel_id=1, source_target_pairs={{2,0},{3,1},{0,2},{1,3},{6,4},{7,5},{4,6},{5,7},{10,8},{11,9},{8,1... | collective-permute-start | bytes 786440 | tf_op jit(solution)/shard_map/ppermute | solution.py:86
  170.2 1.4 collective-permute-start.30
  171.6 3.4 %collective-permute-done.28 = bf16[2,32,2048]{2,1,0:T(8,128)(2,1)S(1)} collective-permute-done((bf16[2,32,2048]{2,1,0:T(8,128)(2,1)S(1)}, bf16[2,32,2048]{2,1,0:T(8,128)(2,1)S(1)}, u32[]{:S(2)}, u32[]{:S(2)}) %collective-permute-start.28) | collective-permute-done | bytes 262176 | tf_op jit(solution)/shard_map/ppermute | solution.py:86
  175.0 17.5 %collective-permute-done.29 = bf16[2,32,2048]{2,1,0:T(8,128)(2,1)S(1)} collective-permute-done((bf16[2,32,2048]{2,1,0:T(8,128)(2,1)S(1)}, bf16[2,32,2048]{2,1,0:T(8,128)(2,1)S(1)}, u32[]{:S(2)}, u32[]{:S(2)}) %collective-permute-start.29) | collective-permute-done | bytes 262176 | tf_op jit(solution)/shard_map/ppermute | solution.py:86
  192.6 1.5 collective-permute-start.31
  194.1 3.6 %collective-permute-done.31 = bf16[32,2048]{1,0:T(8,128)(2,1)S(1)} collective-permute-done((bf16[32,2048]{1,0:T(8,128)(2,1)S(1)}, bf16[32,2048]{1,0:T(8,128)(2,1)S(1)}, u32[]{:S(2)}, u32[]{:S(2)}) %collective-permute-start.31) | collective-permute-done | bytes 131104 | tf_op jit(solution)/shard_map/ppermute | solution.py:82
  197.9 0.9 add_convert_fusion
  (102 shorter events, 8.9 us)
Async XLA Ops:
  0.0 27.7 %copy-start = (bf16[4096,128]{1,0:T(8,128)(2,1)S(1)}, bf16[4096,128]{1,0:T(8,128)(2,1)}, u32[]{:S(2)}) copy-start(bf16[4096,128]{1,0:T(8,128)(2,1)} %param.29) | copy-start | bytes 3145732
  0.0 11.9 %copy-start.1 = (bf16[32,4096]{1,0:T(8,128)(2,1)S(1)}, bf16[32,4096]{1,0:T(8,128)(2,1)}, u32[]{:S(2)}) copy-start(bf16[32,4096]{1,0:T(8,128)(2,1)} %param.19) | copy-start | bytes 786436
  0.0 11.9 %copy-start.11 = (s32[1,4]{1,0:T(1,128)S(1)}, s32[1,4]{1,0:T(1,128)}, u32[]{:S(2)}) copy-start(s32[1,4]{1,0:T(1,128)} %param.20) | copy-start | bytes 52
  0.0 12.1 %copy-start.9 = (s32[1,4]{1,0:T(1,128)S(1)}, s32[1,4]{1,0:T(1,128)}, u32[]{:S(2)}) copy-start(s32[1,4]{1,0:T(1,128)} %param.21) | copy-start | bytes 52
  0.0 12.2 %copy-start.12 = (s32[8]{0:T(128)S(1)}, s32[8]{0:T(128)}, u32[]{:S(2)}) copy-start(s32[8]{0:T(128)} %param.22) | copy-start | bytes 100
  0.0 27.7 %copy-start.3 = (bf16[128,512]{1,0:T(8,128)(2,1)S(1)}, bf16[128,512]{1,0:T(8,128)(2,1)}, u32[]{:S(2)}) copy-start(bf16[128,512]{1,0:T(8,128)(2,1)} %param.31) | copy-start | bytes 393220
  0.0 13.4 %collective-permute-start = (bf16[32,4096]{1,0:T(8,128)(2,1)}, bf16[32,4096]{1,0:T(8,128)(2,1)S(1)}, u32[]{:S(2)}, u32[]{:S(2)}) collective-permute-start(bf16[32,4096]{1,0:T(8,128)(2,1)} %param.19), channel_id=1, source_target_pairs={{1,0},{2,1},{3,2},{0,3},{5,4},{6,5},{7,6},{4,7},{9,8},{10,9},{11,1... | collective-permute-start | bytes 786440 | tf_op jit(solution)/shard_map/ppermute | solution.py:86
  5.1 22.5 %collective-permute-start.1 = (bf16[32,4096]{1,0:T(8,128)(2,1)}, bf16[32,4096]{1,0:T(8,128)(2,1)S(1)}, u32[]{:S(2)}, u32[]{:S(2)}) collective-permute-start(bf16[32,4096]{1,0:T(8,128)(2,1)} %param.19), channel_id=1, source_target_pairs={{2,0},{3,1},{0,2},{1,3},{6,4},{7,5},{4,6},{5,7},{10,8},{11,9},{8,1... | collective-permute-start | bytes 786440 | tf_op jit(solution)/shard_map/ppermute | solution.py:86
  5.1 22.5 %collective-permute-start.2 = (bf16[32,4096]{1,0:T(8,128)(2,1)}, bf16[32,4096]{1,0:T(8,128)(2,1)S(1)}, u32[]{:S(2)}, u32[]{:S(2)}) collective-permute-start(bf16[32,4096]{1,0:T(8,128)(2,1)} %param.19), channel_id=1, source_target_pairs={{3,0},{0,1},{1,2},{2,3},{7,4},{4,5},{5,6},{6,7},{11,8},{8,9},{9,10... | collective-permute-start | bytes 786440 | tf_op jit(solution)/shard_map/ppermute | solution.py:86
  8.8 35.3 %collective-permute-start.4 = (bf16[192,2048]{1,0:T(8,128)(2,1)}, bf16[192,2048]{1,0:T(8,128)(2,1)}, u32[]{:S(2)}, u32[]{:S(2)}) collective-permute-start(bf16[192,2048]{1,0:T(8,128)(2,1)} %get-tuple-element.25), channel_id=1, source_target_pairs={{0,16},{16,0},{1,17},{17,1},{2,18},{18,2},{3,19},{19,3},{4,20},{20... | collective-permute-start | bytes 2359304 | tf_op jit(solution)/shard_map/ppermute | solution.py:82
  10.4 35.3 %collective-permute-start.3 = (bf16[192,4096]{1,0:T(8,128)(2,1)}, bf16[192,4096]{1,0:T(8,128)(2,1)}, u32[]{:S(2)}, u32[]{:S(2)}) collective-permute-start(bf16[192,4096]{1,0:T(8,128)(2,1)} %bitcast.10), channel_id=1, source_target_pairs={{0,8},{8,0},{1,9},{9,1},{2,10},{10,2},{3,11},{11,3},{4,12},{12,4},... | collective-permute-start | bytes 4718600 | tf_op jit(solution)/shard_map/ppermute | solution.py:82
  11.9 19.3 %copy-start.7 = (s32[128]{0:T(128)}, s32[128]{0:T(128)S(1)}, u32[]{:S(2)}) copy-start(s32[128]{0:T(128)S(1)} %and_select_fusion.1) | copy-start | bytes 1540
  12.3 18.9 %copy-start.8 = (s32[128]{0:T(128)}, s32[128]{0:T(128)S(1)}, u32[]{:S(2)}) copy-start(s32[128]{0:T(128)S(1)} %select_reduce_fusion) | copy-start | bytes 1540
  31.3 3.9 %copy-start.4 = (bf16[128,512]{1,0:T(8,128)(2,1)S(1)}, bf16[128,512]{1,0:T(8,128)(2,1)}, u32[]{:S(2)}) copy-start(bf16[128,512]{1,0:T(8,128)(2,1)} %param.32) | copy-start | bytes 393220
  45.7 34.3 %collective-permute-start.8 = (bf16[192,4096]{1,0:T(8,128)(2,1)}, bf16[192,4096]{1,0:T(8,128)(2,1)S(1)}, u32[]{:S(2)}, u32[]{:S(2)}) collective-permute-start(bf16[192,4096]{1,0:T(8,128)(2,1)} %bitcast.90), channel_id=1, source_target_pairs={{0,8},{8,0},{1,9},{9,1},{2,10},{10,2},{3,11},{11,3},{4,12},{12,4},... | collective-permute-start | bytes 4718600 | tf_op jit(solution)/shard_map/ppermute | solution.py:82
  50.1 30.0 %copy-start.5 = (f32[4096]{0:T(1024)S(1)}, f32[4096]{0:T(1024)}, u32[]{:S(2)}) copy-start(f32[4096]{0:T(1024)} %param.33) | copy-start | bytes 49156
  50.2 71.8 %copy-start.10 = (bf16[4096,192]{0,1:T(8,128)(2,1)S(1)}, bf16[4096,192]{0,1:T(8,128)(2,1)}, u32[]{:S(2)}) copy-start(bf16[4096,192]{0,1:T(8,128)(2,1)} %param.36) | copy-start | bytes 4718596
  50.2 74.7 %copy-start.2 = (bf16[192,2048]{1,0:T(8,128)(2,1)S(1)}, bf16[192,2048]{1,0:T(8,128)(2,1)}, u32[]{:S(2)}) copy-start(bf16[192,2048]{1,0:T(8,128)(2,1)} %get-tuple-element.14) | copy-start | bytes 2359300
  50.2 9.9 %collective-permute-start.5 = (bf16[32,4096]{1,0:T(8,128)(2,1)S(1)}, bf16[32,4096]{1,0:T(8,128)(2,1)S(1)}, u32[]{:S(2)}, u32[]{:S(2)}) collective-permute-start(bf16[32,4096]{1,0:T(8,128)(2,1)S(1)} %get-tuple-element.29), channel_id=1, source_target_pairs={{1,0},{2,1},{3,2},{0,3},{5,4},{6,5},{7,6},{4,7},{9,8},{10,9},{11,1... | collective-permute-start | bytes 786440 | tf_op jit(solution)/shard_map/ppermute | solution.py:86
  53.4 21.4 %collective-permute-start.6 = (bf16[32,4096]{1,0:T(8,128)(2,1)S(1)}, bf16[32,4096]{1,0:T(8,128)(2,1)S(1)}, u32[]{:S(2)}, u32[]{:S(2)}) collective-permute-start(bf16[32,4096]{1,0:T(8,128)(2,1)S(1)} %get-tuple-element.31), channel_id=1, source_target_pairs={{2,0},{3,1},{0,2},{1,3},{6,4},{7,5},{4,6},{5,7},{10,8},{11,9},{8,1... | collective-permute-start | bytes 786440 | tf_op jit(solution)/shard_map/ppermute | solution.py:86
  54.2 20.6 %collective-permute-start.7 = (bf16[32,4096]{1,0:T(8,128)(2,1)S(1)}, bf16[32,4096]{1,0:T(8,128)(2,1)S(1)}, u32[]{:S(2)}, u32[]{:S(2)}) collective-permute-start(bf16[32,4096]{1,0:T(8,128)(2,1)S(1)} %get-tuple-element.30), channel_id=1, source_target_pairs={{3,0},{0,1},{1,2},{2,3},{7,4},{4,5},{5,6},{6,7},{11,8},{8,9},{9,10... | collective-permute-start | bytes 786440 | tf_op jit(solution)/shard_map/ppermute | solution.py:86
  80.3 10.1 %collective-permute-start.9 = (bf16[32,4096]{1,0:T(8,128)(2,1)S(1)}, bf16[32,4096]{1,0:T(8,128)(2,1)S(1)}, u32[]{:S(2)}, u32[]{:S(2)}) collective-permute-start(bf16[32,4096]{1,0:T(8,128)(2,1)S(1)} %get-tuple-element.21), channel_id=1, source_target_pairs={{1,0},{2,1},{3,2},{0,3},{5,4},{6,5},{7,6},{4,7},{9,8},{10,9},{11,1... | collective-permute-start | bytes 786440 | tf_op jit(solution)/shard_map/ppermute | solution.py:86
  83.7 58.2 %collective-permute-start.18 = (bf16[192,4096]{1,0:T(8,128)(2,1)}, bf16[192,4096]{1,0:T(8,128)(2,1)S(1)}, u32[]{:S(2)}, u32[]{:S(2)}) collective-permute-start(bf16[192,4096]{1,0:T(8,128)(2,1)} %bitcast.10), channel_id=1, source_target_pairs={{0,4},{4,0},{1,5},{5,1},{2,6},{6,2},{3,7},{7,3},{8,12},{12,8},{9,1... | collective-permute-start | bytes 4718600 | tf_op jit(solution)/shard_map/ppermute | solution.py:82
  83.7 58.7 %collective-permute-start.19 = (bf16[192,4096]{1,0:T(8,128)(2,1)}, bf16[192,4096]{1,0:T(8,128)(2,1)S(1)}, u32[]{:S(2)}, u32[]{:S(2)}) collective-permute-start(bf16[192,4096]{1,0:T(8,128)(2,1)} %collective-permute-done.3), channel_id=1, source_target_pairs={{0,4},{4,0},{1,5},{5,1},{2,6},{6,2},{3,7},{7,3},{8,12},{12,8},{9,1... | collective-permute-start | bytes 4718600 | tf_op jit(solution)/shard_map/ppermute | solution.py:82
  84.3 21.3 %collective-permute-start.10 = (bf16[32,4096]{1,0:T(8,128)(2,1)S(1)}, bf16[32,4096]{1,0:T(8,128)(2,1)S(1)}, u32[]{:S(2)}, u32[]{:S(2)}) collective-permute-start(bf16[32,4096]{1,0:T(8,128)(2,1)S(1)} %get-tuple-element.21), channel_id=1, source_target_pairs={{2,0},{3,1},{0,2},{1,3},{6,4},{7,5},{4,6},{5,7},{10,8},{11,9},{8,1... | collective-permute-start | bytes 786440 | tf_op jit(solution)/shard_map/ppermute | solution.py:86
  84.8 22.2 %collective-permute-start.11 = (bf16[32,4096]{1,0:T(8,128)(2,1)S(1)}, bf16[32,4096]{1,0:T(8,128)(2,1)S(1)}, u32[]{:S(2)}, u32[]{:S(2)}) collective-permute-start(bf16[32,4096]{1,0:T(8,128)(2,1)S(1)} %get-tuple-element.21), channel_id=1, source_target_pairs={{3,0},{0,1},{1,2},{2,3},{7,4},{4,5},{5,6},{6,7},{11,8},{8,9},{9,10... | collective-permute-start | bytes 786440 | tf_op jit(solution)/shard_map/ppermute | solution.py:86
  90.4 17.7 %collective-permute-start.12 = (bf16[32,4096]{1,0:T(8,128)(2,1)S(1)}, bf16[32,4096]{1,0:T(8,128)(2,1)S(1)}, u32[]{:S(2)}, u32[]{:S(2)}) collective-permute-start(bf16[32,4096]{1,0:T(8,128)(2,1)S(1)} %get-tuple-element.21), channel_id=1, source_target_pairs={{0,16},{16,0},{1,17},{17,1},{2,18},{18,2},{3,19},{19,3},{4,20},{20... | collective-permute-start | bytes 786440 | tf_op jit(solution)/shard_map/ppermute | solution.py:82
  105.5 19.9 %collective-permute-start.17 = (bf16[192,2048]{1,0:T(8,128)(2,1)}, bf16[192,2048]{1,0:T(8,128)(2,1)S(1)}, u32[]{:S(2)}, u32[]{:S(2)}) collective-permute-start(bf16[192,2048]{1,0:T(8,128)(2,1)} %collective-permute-done.4), channel_id=1, source_target_pairs={{0,8},{8,0},{1,9},{9,1},{2,10},{10,2},{3,11},{11,3},{4,12},{12,4},... | collective-permute-start | bytes 2359304 | tf_op jit(solution)/shard_map/ppermute | solution.py:82
  107.0 9.3 %collective-permute-start.13 = (bf16[32,4096]{1,0:T(8,128)(2,1)S(1)}, bf16[32,4096]{1,0:T(8,128)(2,1)S(1)}, u32[]{:S(2)}, u32[]{:S(2)}) collective-permute-start(bf16[32,4096]{1,0:T(8,128)(2,1)S(1)} %collective-permute-done.9), channel_id=1, source_target_pairs={{0,16},{16,0},{1,17},{17,1},{2,18},{18,2},{3,19},{19,3},{4,20},{20... | collective-permute-start | bytes 786440 | tf_op jit(solution)/shard_map/ppermute | solution.py:82
  108.1 13.8 %collective-permute-start.14 = (bf16[32,4096]{1,0:T(8,128)(2,1)S(1)}, bf16[32,4096]{1,0:T(8,128)(2,1)S(1)}, u32[]{:S(2)}, u32[]{:S(2)}) collective-permute-start(bf16[32,4096]{1,0:T(8,128)(2,1)S(1)} %collective-permute-done.10), channel_id=1, source_target_pairs={{0,16},{16,0},{1,17},{17,1},{2,18},{18,2},{3,19},{19,3},{4,20},{20... | collective-permute-start | bytes 786440 | tf_op jit(solution)/shard_map/ppermute | solution.py:82
  116.3 8.5 %collective-permute-start.15 = (bf16[32,4096]{1,0:T(8,128)(2,1)S(1)}, bf16[32,4096]{1,0:T(8,128)(2,1)S(1)}, u32[]{:S(2)}, u32[]{:S(2)}) collective-permute-start(bf16[32,4096]{1,0:T(8,128)(2,1)S(1)} %collective-permute-done.11), channel_id=1, source_target_pairs={{0,16},{16,0},{1,17},{17,1},{2,18},{18,2},{3,19},{19,3},{4,20},{20... | collective-permute-start | bytes 786440 | tf_op jit(solution)/shard_map/ppermute | solution.py:82
  122.0 27.7 %collective-permute-start.20 = (bf16[192,4096]{1,0:T(8,128)(2,1)S(1)}, bf16[192,4096]{1,0:T(8,128)(2,1)S(1)}, u32[]{:S(2)}, u32[]{:S(2)}) collective-permute-start(bf16[192,4096]{1,0:T(8,128)(2,1)S(1)} %bitcast.91), channel_id=1, source_target_pairs={{0,4},{4,0},{1,5},{5,1},{2,6},{6,2},{3,7},{7,3},{8,12},{12,8},{9,1... | collective-permute-start | bytes 4718600 | tf_op jit(solution)/shard_map/ppermute | solution.py:82
  124.9 17.0 %collective-permute-start.16 = (bf16[192,2048]{1,0:T(8,128)(2,1)S(1)}, bf16[192,2048]{1,0:T(8,128)(2,1)S(1)}, u32[]{:S(2)}, u32[]{:S(2)}) collective-permute-start(bf16[192,2048]{1,0:T(8,128)(2,1)S(1)} %copy-done.2), channel_id=1, source_target_pairs={{0,8},{8,0},{1,9},{9,1},{2,10},{10,2},{3,11},{11,3},{4,12},{12,4},... | collective-permute-start | bytes 2359304 | tf_op jit(solution)/shard_map/ppermute | solution.py:82
  125.4 24.8 %collective-permute-start.21 = (bf16[192,4096]{1,0:T(8,128)(2,1)S(1)}, bf16[192,4096]{1,0:T(8,128)(2,1)S(1)}, u32[]{:S(2)}, u32[]{:S(2)}) collective-permute-start(bf16[192,4096]{1,0:T(8,128)(2,1)S(1)} %collective-permute-done.8), channel_id=1, source_target_pairs={{0,4},{4,0},{1,5},{5,1},{2,6},{6,2},{3,7},{7,3},{8,12},{12,8},{9,1... | collective-permute-start | bytes 4718600 | tf_op jit(solution)/shard_map/ppermute | solution.py:82
  141.9 23.5 %collective-permute-start.22 = (bf16[192,2048]{1,0:T(8,128)(2,1)S(1)}, bf16[192,2048]{1,0:T(8,128)(2,1)S(1)}, u32[]{:S(2)}, u32[]{:S(2)}) collective-permute-start(bf16[192,2048]{1,0:T(8,128)(2,1)S(1)} %copy-done.2), channel_id=1, source_target_pairs={{0,4},{4,0},{1,5},{5,1},{2,6},{6,2},{3,7},{7,3},{8,12},{12,8},{9,1... | collective-permute-start | bytes 2359304 | tf_op jit(solution)/shard_map/ppermute | solution.py:82
  141.9 11.4 %collective-permute-start.26 = (bf16[192,2048]{1,0:T(8,128)(2,1)}, bf16[192,2048]{1,0:T(8,128)(2,1)S(1)}, u32[]{:S(2)}, u32[]{:S(2)}) collective-permute-start(bf16[192,2048]{1,0:T(8,128)(2,1)} %collective-permute-done.4), channel_id=1, source_target_pairs={{0,4},{4,0},{1,5},{5,1},{2,6},{6,2},{3,7},{7,3},{8,12},{12,8},{9,1... | collective-permute-start | bytes 2359304 | tf_op jit(solution)/shard_map/ppermute | solution.py:82
  142.4 11.8 %collective-permute-start.27 = (bf16[192,2048]{1,0:T(8,128)(2,1)S(1)}, bf16[192,2048]{1,0:T(8,128)(2,1)S(1)}, u32[]{:S(2)}, u32[]{:S(2)}) collective-permute-start(bf16[192,2048]{1,0:T(8,128)(2,1)S(1)} %collective-permute-done.17), channel_id=1, source_target_pairs={{0,4},{4,0},{1,5},{5,1},{2,6},{6,2},{3,7},{7,3},{8,12},{12,8},{9,1... | collective-permute-start | bytes 2359304 | tf_op jit(solution)/shard_map/ppermute | solution.py:82
  149.7 15.7 %collective-permute-start.23 = (bf16[192,2048]{1,0:T(8,128)(2,1)S(1)}, bf16[192,2048]{1,0:T(8,128)(2,1)S(1)}, u32[]{:S(2)}, u32[]{:S(2)}) collective-permute-start(bf16[192,2048]{1,0:T(8,128)(2,1)S(1)} %collective-permute-done.16), channel_id=1, source_target_pairs={{0,4},{4,0},{1,5},{5,1},{2,6},{6,2},{3,7},{7,3},{8,12},{12,8},{9,1... | collective-permute-start | bytes 2359304 | tf_op jit(solution)/shard_map/ppermute | solution.py:82
  152.1 7.8 %collective-permute-start.24 = (bf16[128,768]{1,0:T(8,128)(2,1)S(1)}, bf16[128,768]{1,0:T(8,128)(2,1)S(1)}, u32[]{:S(2)}, u32[]{:S(2)}) collective-permute-start(bf16[128,768]{1,0:T(8,128)(2,1)S(1)} %get-tuple-element.34), channel_id=1, source_target_pairs={{0,16},{16,0},{1,17},{17,1},{2,18},{18,2},{3,19},{19,3},{4,20},{20... | collective-permute-start | bytes 589832 | tf_op jit(solution)/shard_map/ppermute | solution.py:82
  153.3 10.0 %collective-permute-start.25 = (bf16[128,768]{1,0:T(8,128)(2,1)S(1)}, bf16[128,768]{1,0:T(8,128)(2,1)S(1)}, u32[]{:S(2)}, u32[]{:S(2)}) collective-permute-start(bf16[128,768]{1,0:T(8,128)(2,1)S(1)} %get-tuple-element.35), channel_id=1, source_target_pairs={{0,16},{16,0},{1,17},{17,1},{2,18},{18,2},{3,19},{19,3},{4,20},{20... | collective-permute-start | bytes 589832 | tf_op jit(solution)/shard_map/ppermute | solution.py:82
  166.6 31.2 %copy-start.6 = (f32[4096]{0:T(1024)S(1)}, f32[4096]{0:T(1024)}, u32[]{:S(2)}) copy-start(f32[4096]{0:T(1024)} %param.34) | copy-start | bytes 49156
  166.7 8.3 %collective-permute-start.28 = (bf16[2,32,2048]{2,1,0:T(8,128)(2,1)S(1)}, bf16[2,32,2048]{2,1,0:T(8,128)(2,1)S(1)}, u32[]{:S(2)}, u32[]{:S(2)}) collective-permute-start(bf16[2,32,2048]{2,1,0:T(8,128)(2,1)S(1)} %get-tuple-element.26), channel_id=1, source_target_pairs={{1,0},{2,1},{3,2},{0,3},{5,4},{6,5},{7,6},{4,7},{9,8},{10,9},{11,1... | collective-permute-start | bytes 786440 | tf_op jit(solution)/shard_map/ppermute | solution.py:86
  166.8 25.7 %collective-permute-start.29 = (bf16[2,32,2048]{2,1,0:T(8,128)(2,1)S(1)}, bf16[2,32,2048]{2,1,0:T(8,128)(2,1)S(1)}, u32[]{:S(2)}, u32[]{:S(2)}) collective-permute-start(bf16[2,32,2048]{2,1,0:T(8,128)(2,1)S(1)} %get-tuple-element.27), channel_id=1, source_target_pairs={{2,0},{3,1},{0,2},{1,3},{6,4},{7,5},{4,6},{5,7},{10,8},{11,9},{8,1... | collective-permute-start | bytes 786440 | tf_op jit(solution)/shard_map/ppermute | solution.py:86
  170.2 22.3 %collective-permute-start.30 = (bf16[2,32,2048]{2,1,0:T(8,128)(2,1)S(1)}, bf16[2,32,2048]{2,1,0:T(8,128)(2,1)S(1)}, u32[]{:S(2)}, u32[]{:S(2)}) collective-permute-start(bf16[2,32,2048]{2,1,0:T(8,128)(2,1)S(1)} %get-tuple-element.28), channel_id=1, source_target_pairs={{3,0},{0,1},{1,2},{2,3},{7,4},{4,5},{5,6},{6,7},{11,8},{8,9},{9,10... | collective-permute-start | bytes 786440 | tf_op jit(solution)/shard_map/ppermute | solution.py:86
  192.6 5.0 %collective-permute-start.31 = (bf16[32,2048]{1,0:T(8,128)(2,1)S(1)}, bf16[32,2048]{1,0:T(8,128)(2,1)S(1)}, u32[]{:S(2)}, u32[]{:S(2)}) collective-permute-start(bf16[32,2048]{1,0:T(8,128)(2,1)S(1)} %fusion.52), channel_id=1, source_target_pairs={{0,16},{16,0},{1,17},{17,1},{2,18},{18,2},{3,19},{19,3},{4,20},{20... | collective-permute-start | bytes 393224 | tf_op jit(solution)/shard_map/ppermute | solution.py:82

commit v4 on v3

--- a/solution.py
+++ b/solution.py
@@ -97,6 +97,44 @@
     return sum(part.astype(jnp.float32) for part in arrived)
 
 
+def line_relay(block, beside):
+    index = lax.axis_index("mlp")
+    end = (index == 0) | (index == 3)
+    other, fetched = [exchange(block, "y")], [exchange(beside[0], "x")]
+    from_right = lax.ppermute(block, "mlp", [(1, 0), (2, 1), (3, 2)])
+    from_left = lax.ppermute(block, "mlp", [(0, 1), (1, 2), (2, 3)])
+    from_right, from_left, fetched[0], beside[1] = together(
+        from_right, from_left, fetched[0], beside[1]
+    )
+    first = jnp.where(index < 2, from_right, from_left)
+    other.append(exchange(first, "y"))
+    fetched.append(exchange(beside[1], "x"))
+    across = jnp.where(
+        index < 2,
+        lax.ppermute(from_right, "mlp", [(1, 0), (2, 1)]),
+        lax.ppermute(from_left, "mlp", [(1, 2), (2, 3)]),
+    )
+    across, fetched[1], other[0], beside[2] = together(across, fetched[1], other[0], beside[2])
+    second = jnp.where(end, across, jnp.where(index == 1, from_left, from_right))
+    other.append(exchange(second, "y"))
+    fetched.append(exchange(beside[2], "x"))
+    last = lax.ppermute(across, "mlp", [(1, 0), (2, 3)])
+    last, fetched[2], other[1], beside[3] = together(last, fetched[2], other[1], beside[3])
+    third = jnp.where(end, last, across)
+    other.append(exchange(third, "y"))
+    fetched.append(exchange(beside[3], "x"))
+    return [block, *by_distance(first, second, third), other[0], *by_distance(*other[1:])], fetched
+
+
+def by_distance(first, second, third):
+    index = lax.axis_index("mlp")
+    return [
+        jnp.where(index < 2, first, jnp.where(index == 2, second, third)),
+        jnp.where((index == 0) | (index == 3), second, third),
+        jnp.where(index > 1, first, jnp.where(index == 1, second, third)),
+    ]
+
+
 def gather_group(block, direct):
     if direct:
         return jnp.concatenate(line_gather(block))
@@ -109,8 +147,8 @@
     return lax.psum_scatter(rows, "mlp", scatter_dimension=0, tiled=True).astype(jnp.float32)
 
 
-def after(value, *events):
-    return lax.optimization_barrier((value, *events))[0]
+def together(*values):
+    return lax.optimization_barrier(values)
 
 
 def both_cores(rows, rows_x):
@@ -154,8 +192,6 @@
         gate_x = exchange(gate_rows, "x")
         half = down_rows.shape[1] // 2
         y = lax.axis_index("y")
-        near = lax.dynamic_slice_in_dim(down_rows, y * half, half, axis=1)
-        far = exchange(lax.dynamic_slice_in_dim(down_rows, (1 - y) * half, half, axis=1), "y")
     group_token_rows = gather_group(layer_input, direct)
     columns = jnp.arange(ADAPTER_SLOTS * ADAPTER_RANK, dtype=jnp.int32) // ADAPTER_RANK
     slot_match_mask = (columns[None, :] == token_slot[:, None]).astype(jnp.bfloat16)
@@ -195,23 +231,23 @@
         tok_group, heads_local * HEAD_SIZE
     )
     if direct:
-        context = after(context, gate_x, far)
-        up_x = exchange(after(up_rows, gate_x), "x")
+        context, gate_x, down_rows, up_rows_late = together(context, gate_x, down_rows, up_rows)
+        near = lax.dynamic_slice_in_dim(down_rows, y * half, half, axis=1)
+        far = exchange(lax.dynamic_slice_in_dim(down_rows, (1 - y) * half, half, axis=1), "y")
+        up_x = exchange(up_rows_late, "x")
     attn_own = scatter_group(
         jnp.dot(context, output_weight, preferred_element_type=jnp.float32).astype(jnp.bfloat16),
         direct,
     )
     if direct:
-        attn_own = after(attn_own, up_x)
-        near_x = exchange(after(near, up_x), "x")
-        far_x = exchange(after(far, up_x), "x")
+        attn_own, near, far, up_x = together(attn_own, near, far, up_x)
     residual_own = (
         layer_input.astype(jnp.float32) + rms_scale(attn_own) * attention_norm_gain
     ).astype(jnp.bfloat16)
     if direct:
-        line = line_gather(residual_own)
-        other = [exchange(block, "y") for block in line]
-        states = after(jnp.concatenate(line + other), near_x, far_x)
+        blocks, fetched = line_relay(residual_own, [*jnp.split(near, 2), *jnp.split(far, 2)])
+        states = jnp.concatenate(blocks)
+        near_x, far_x = jnp.concatenate(fetched[:2]), jnp.concatenate(fetched[2:])
         hidden = hidden_units(states, both_cores(gate_rows, gate_x), both_cores(up_rows, up_x))
         hidden_other = jnp.concatenate(
             [exchange(hidden[tok_group:], "y"), exchange(hidden[:tok_group], "y")]

time: 199 us -> 200 us (level)
  starting transfers between devices: 35.5 us -> 40.5 us
    ppermute x0 -> x5, waiting for transfers between devices: none -> 20.2 us  [the longest x1 8.7 us: line_relay(): lax.ppermute(from_right, 'mlp', [(1, 0), (2, 1)])]
    ppermute x12 -> x9, waiting for transfers between devices: 74.7 us -> 55.6 us  [shift(): return lax.ppermute(block, 'mlp', [((k + hops) % 4, k) for k in range(4)])]
    ppermute x0 -> x5, starting transfers between devices: none -> 11.1 us  [the longest x1 6.22 us: line_relay(): from_left = lax.ppermute(block, 'mlp', [(0, 1), (1, 2), (2, 3)])]
    ppermute x12 -> x9, starting transfers between devices: 20.2 us -> 12.4 us  [shift(): return lax.ppermute(block, 'mlp', [((k + hops) % 4, k) for k in range(4)])]
    ppermute x20 -> x22, waiting for transfers between devices: 50.4 us -> 47.8 us  [exchange(): return lax.ppermute(block, axis, [(0, 1), (1, 0)])]
    dynamic_slice x1, local copies, waits for them, and re-layouts: 2.69 us -> 0.1 us  [shards(): lax.dynamic_slice_in_dim(down_rows, (1 - y) * half, half, axis=1)]
    ppermute x20 -> x22, starting transfers between devices: 15.3 us -> 17 us  [exchange(): return lax.ppermute(block, axis, [(0, 1), (1, 0)])]
  transfers between devices with their start and end apart: 32 -> 36, of which waited for: 16 -> 21; matrix products, arithmetic and copies ran while one was open for 18% -> 16% of each run, Pallas kernels for 0% -> 0%
where the time goes in v4:
time: 200 us; the launch traced here: 199 us
  waiting for transfers between devices  124 us (62%)
  starting transfers between devices  40.5 us (20%)
  matrix products  25.3 us (13%)
  other arithmetic  6.73 us (3%)
  local copies, waits for them, and re-layouts  2.44 us (1%)
    ppermute x9, waiting for transfers between devices, shift(): return lax.ppermute(block, 'mlp', [((k + hops) % 4, k) for k in range(4)])  55.6 us
    ppermute x22, waiting for transfers between devices, exchange(): return lax.ppermute(block, axis, [(0, 1), (1, 0)])  47.8 us
    ppermute x22, starting transfers between devices, exchange(): return lax.ppermute(block, axis, [(0, 1), (1, 0)])  17 us
    ppermute x9, starting transfers between devices, shift(): return lax.ppermute(block, 'mlp', [((k + hops) % 4, k) for k in range(4)])  12.4 us
    ppermute x1, waiting for transfers between devices, line_relay(): lax.ppermute(from_right, 'mlp', [(1, 0), (2, 1)])  8.7 us
    ppermute x1, waiting for transfers between devices, line_relay(): last = lax.ppermute(across, 'mlp', [(1, 0), (2, 3)])  7.11 us
    dot_general x1, matrix products, hidden_units(): lax.dot_general(states, gate_rows, contract, preferred_element_type=jnp.f...  6.83 us
    ppermute x1, starting transfers between devices, line_relay(): from_left = lax.ppermute(block, 'mlp', [(0, 1), (1, 2), (2, 3)])  6.22 us
  transfers between devices with their start and end apart: 36, of which 21 were waited for; matrix products, arithmetic and copies ran while one was open for 16% of the time, Pallas kernels for 0%

profile of v4, /device:TPU:0, one launch (start us, length us, event | category | flops | bytes accessed | tf_op | source)
XLA Modules:
  0.0 199.3 jit_solution(12082217367155313908)
XLA Ops:
  0.0 5.0 %collective-permute-start = (bf16[32,4096]{1,0:T(8,128)(2,1)}, bf16[32,4096]{1,0:T(8,128)(2,1)S(1)}, u32[]{:S(2)}, u32[]{:S(2)}) collective-permute-start(bf16[32,4096]{1,0:T(8,128)(2,1)} %param.19), channel_id=1, source_target_pairs={{1,0},{2,1},{3,2},{0,3},{5,4},{6,5},{7,6},{4,7},{9,8},{10,9},{11,1... | collective-permute-start | bytes 786440 | tf_op jit(solution)/shard_map/ppermute | solution.py:86
  5.1 1.0 collective-permute-start.2
  6.1 1.5 collective-permute-start.3
  7.6 1.0 constant_dynamic-update-slice_fusion.3
  8.6 0.8 reduce-window.4
  12.1 15.4 %collective-permute-done.1 = bf16[32,4096]{1,0:T(8,128)(2,1)S(1)} collective-permute-done((bf16[32,4096]{1,0:T(8,128)(2,1)}, bf16[32,4096]{1,0:T(8,128)(2,1)S(1)}, u32[]{:S(2)}, u32[]{:S(2)}) %collective-permute-start.1) | collective-permute-done | bytes 262176 | tf_op jit(solution)/shard_map/ppermute | solution.py:86
  27.6 1.5 convolution_multiply_fusion.1
  29.1 2.9 %convolution_add_fusion.1 = f32[128,512]{1,0:T(8,128)S(1)} fusion(f32[128,512]{1,0:T(8,128)S(1)} %convolution_multiply_fusion.1, bf16[128,4096]{1,0:T(8,128)(2,1)S(1)} %constant_dynamic-update-slice_fusion, bf16[4096,512]{1,0:T(8,128)(2,1)} %param.23), kind=kOutput, calls=%fused_computation.26 | convolution fusion | flops 536936448 | bytes 5767168 | tf_op jit(solution)/shard_map/dot_general | solution.py:210
  32.4 3.0 %fusion.81 = f32[128,512]{1,0:T(8,128)S(1)} fusion(bf16[128,4096]{1,0:T(8,128)(2,1)S(1)} %constant_dynamic-update-slice_fusion, bf16[4096,512]{1,0:T(8,128)(2,1)} %param.24), kind=kOutput, calls=%fused_computation.157 | convolution fusion | flops 536870912 | bytes 5505024 | tf_op jit(solution)/shard_map/dot_general | solution.py:213
  36.1 2.9 %fusion.21 = bf16[128,512]{1,0:T(8,128)(2,1)S(1)} fusion(f32[128,512]{1,0:T(8,128)S(1)} %convolution_multiply_fusion.2, bf16[128,4096]{1,0:T(8,128)(2,1)S(1)} %constant_dynamic-update-slice_fusion, bf16[4096,512]{1,0:T(8,128)(2,1)} %param.25), kind=kOutput, calls=%fused_computation.29 | convolution fusion | flops 537001984 | bytes 5636096 | tf_op jit(solution)/shard_map/dot_general | solution.py:214
  40.9 0.8 collective-permute-done.3
  41.7 1.5 collective-permute-start.8
  43.2 2.9 %convolution_convert_fusion = bf16[128,4096]{1,0:T(8,128)(2,1)S(1)} fusion(bf16[128,512]{0,1:T(8,128)(2,1)S(1)} %bitcast.85, bf16[512,4096]{1,0:T(8,128)(2,1)} %param.26), kind=kOutput, calls=%fused_computation.17 | convolution fusion | flops 537395200 | bytes 5373952 | tf_op jit(solution)/shard_map/dot_general | solution.py:239
  46.2 3.1 %collective-permute-start.4 = (bf16[32,4096]{1,0:T(8,128)(2,1)S(1)}, bf16[32,4096]{1,0:T(8,128)(2,1)S(1)}, u32[]{:S(2)}, u32[]{:S(2)}) collective-permute-start(bf16[32,4096]{1,0:T(8,128)(2,1)S(1)} %get-tuple-element.60), channel_id=1, source_target_pairs={{1,0},{2,1},{3,2},{0,3},{5,4},{6,5},{7,6},{4,7},{9,8},{10,9},{11,1... | collective-permute-start | bytes 786440 | tf_op jit(solution)/shard_map/ppermute | solution.py:86
  49.3 0.8 collective-permute-start.5
  50.6 5.5 %collective-permute-done.4 = bf16[32,4096]{1,0:T(8,128)(2,1)S(1)} collective-permute-done((bf16[32,4096]{1,0:T(8,128)(2,1)S(1)}, bf16[32,4096]{1,0:T(8,128)(2,1)S(1)}, u32[]{:S(2)}, u32[]{:S(2)}) %collective-permute-start.4) | collective-permute-done | bytes 262176 | tf_op jit(solution)/shard_map/ppermute | solution.py:86
  56.1 1.5 collective-permute-start.7
  57.6 13.4 %collective-permute-done.5 = bf16[32,4096]{1,0:T(8,128)(2,1)S(1)} collective-permute-done((bf16[32,4096]{1,0:T(8,128)(2,1)S(1)}, bf16[32,4096]{1,0:T(8,128)(2,1)S(1)}, u32[]{:S(2)}, u32[]{:S(2)}) %collective-permute-start.5) | collective-permute-done | bytes 262176 | tf_op jit(solution)/shard_map/ppermute | solution.py:86
  71.1 5.3 %collective-permute-done.8 = bf16[192,4096]{1,0:T(8,128)(2,1)S(1)} collective-permute-done((bf16[192,4096]{1,0:T(8,128)(2,1)}, bf16[192,4096]{1,0:T(8,128)(2,1)S(1)}, u32[]{:S(2)}, u32[]{:S(2)}) %collective-permute-start.8) | collective-permute-done | bytes 1572896 | tf_op jit(solution)/shard_map/ppermute | solution.py:82
  76.8 6.2 %collective-permute-start.10 = (bf16[32,4096]{1,0:T(8,128)(2,1)S(1)}, bf16[32,4096]{1,0:T(8,128)(2,1)S(1)}, u32[]{:S(2)}, u32[]{:S(2)}) collective-permute-start(bf16[32,4096]{1,0:T(8,128)(2,1)S(1)} %get-tuple-element.52), channel_id=1, source_target_pairs={{0,1},{1,2},{2,3},{4,5},{5,6},{6,7},{8,9},{9,10},{10,11},{12,13},{... | collective-permute-start | bytes 786440 | tf_op jit(solution)/shard_map/ppermute | solution.py:105
  83.0 1.3 collective-permute-start.9
  85.4 1.5 collective-permute-done.10
  86.9 1.5 collective-permute-start.15
  88.4 2.9 %collective-permute-done.9 = bf16[32,4096]{1,0:T(8,128)(2,1)S(1)} collective-permute-done((bf16[32,4096]{1,0:T(8,128)(2,1)S(1)}, bf16[32,4096]{1,0:T(8,128)(2,1)S(1)}, u32[]{:S(2)}, u32[]{:S(2)}) %collective-permute-start.9) | collective-permute-done | bytes 262176 | tf_op jit(solution)/shard_map/ppermute | solution.py:104
  91.3 4.8 %collective-permute-done.11 = bf16[96,2048]{1,0:T(8,128)(2,1)S(1)} collective-permute-done((bf16[96,2048]{1,0:T(8,128)(2,1)S(1)}, bf16[96,2048]{1,0:T(8,128)(2,1)S(1)}, u32[]{:S(2)}, u32[]{:S(2)}) %collective-permute-start.11) | collective-permute-done | bytes 393248 | tf_op jit(solution)/shard_map/ppermute | solution.py:82
  96.0 1.4 collective-permute-start.12
  98.2 8.7 %collective-permute-done.12 = bf16[32,4096]{1,0:T(8,128)(2,1)S(1)} collective-permute-done((bf16[32,4096]{1,0:T(8,128)(2,1)S(1)}, bf16[32,4096]{1,0:T(8,128)(2,1)S(1)}, u32[]{:S(2)}, u32[]{:S(2)}) %collective-permute-start.12) | collective-permute-done | bytes 262176 | tf_op jit(solution)/shard_map/ppermute | solution.py:114
  107.6 1.6 collective-permute-start.18
  109.2 9.2 %collective-permute-done.14 = bf16[96,2048]{1,0:T(8,128)(2,1)S(1)} collective-permute-done((bf16[96,2048]{1,0:T(8,128)(2,1)S(1)}, bf16[96,2048]{1,0:T(8,128)(2,1)S(1)}, u32[]{:S(2)}, u32[]{:S(2)}) %collective-permute-start.14) | collective-permute-done | bytes 393248 | tf_op jit(solution)/shard_map/ppermute | solution.py:82
  119.1 1.5 collective-permute-start.16
  121.5 7.1 %collective-permute-done.16 = bf16[32,4096]{1,0:T(8,128)(2,1)S(1)} collective-permute-done((bf16[32,4096]{1,0:T(8,128)(2,1)S(1)}, bf16[32,4096]{1,0:T(8,128)(2,1)S(1)}, u32[]{:S(2)}, u32[]{:S(2)}) %collective-permute-start.16) | collective-permute-done | bytes 262176 | tf_op jit(solution)/shard_map/ppermute | solution.py:121
  129.4 1.6 collective-permute-start.19
  131.7 7.0 %collective-permute-done.19 = bf16[32,4096]{1,0:T(8,128)(2,1)S(1)} collective-permute-done((bf16[32,4096]{1,0:T(8,128)(2,1)S(1)}, bf16[32,4096]{1,0:T(8,128)(2,1)S(1)}, u32[]{:S(2)}, u32[]{:S(2)}) %collective-permute-start.19) | collective-permute-done | bytes 262176 | tf_op jit(solution)/shard_map/ppermute | solution.py:82
  138.7 3.4 %collective-permute-done.20 = bf16[32,4096]{1,0:T(8,128)(2,1)S(1)} collective-permute-done((bf16[32,4096]{1,0:T(8,128)(2,1)S(1)}, bf16[32,4096]{1,0:T(8,128)(2,1)S(1)}, u32[]{:S(2)}, u32[]{:S(2)}) %collective-permute-start.20) | collective-permute-done | bytes 262176 | tf_op jit(solution)/shard_map/ppermute | solution.py:82
  143.2 6.8 %fusion.1 = f32[256,768]{1,0:T(8,128)S(1)} fusion(bf16[256,4096]{1,0:T(8,128)(2,1)S(1)} %select_dynamic-update-slice_fusion, bf16[192,4096]{1,0:T(8,128)(2,1)S(1)} %collective-permute-done.22, bf16[192,4096]{1,0:T(8,128)(2,1)} %collective-permute-done.3, bf16[192,4096]{1,0:T(8,128)(2,1)} %collective-permute-done.21, bf16[192,4096]{1,0:T(8,128)(2,1)S(1)} %bitcast.92), kind=kOutput, calls=%fused_computation.1 | convolution fusion | flops 1635778560 | bytes 9175040 | tf_op jit(solution)/shard_map/dot_general | solution.py:76
  150.0 4.0 %collective-permute-done.30 = bf16[96,2048]{1,0:T(8,128)(2,1)S(1)} collective-permute-done((bf16[96,2048]{1,0:T(8,128)(2,1)S(1)}, bf16[96,2048]{1,0:T(8,128)(2,1)S(1)}, u32[]{:S(2)}, u32[]{:S(2)}) %collective-permute-start.30) | collective-permute-done | bytes 393248 | tf_op jit(solution)/shard_map/ppermute | solution.py:82
  154.2 1.9 multiply_convert_fusion
  156.1 1.6 collective-permute-start.27
  158.4 5.5 %collective-permute-done.27 = bf16[128,768]{1,0:T(8,128)(2,1)S(1)} collective-permute-done((bf16[128,768]{1,0:T(8,128)(2,1)S(1)}, bf16[128,768]{1,0:T(8,128)(2,1)S(1)}, u32[]{:S(2)}, u32[]{:S(2)}) %collective-permute-start.27) | collective-permute-done | bytes 196640 | tf_op jit(solution)/shard_map/ppermute | solution.py:82
  163.9 3.8 %collective-permute-done.28 = bf16[128,768]{1,0:T(8,128)(2,1)S(1)} collective-permute-done((bf16[128,768]{1,0:T(8,128)(2,1)S(1)}, bf16[128,768]{1,0:T(8,128)(2,1)S(1)}, u32[]{:S(2)}, u32[]{:S(2)}) %collective-permute-start.28) | collective-permute-done | bytes 196640 | tf_op jit(solution)/shard_map/ppermute | solution.py:82
  167.7 1.0 fusion.26
  168.7 1.0 fusion.17
  170.3 1.5 collective-permute-start.34
  171.9 6.3 %collective-permute-done.32 = bf16[2,32,2048]{2,1,0:T(8,128)(2,1)S(1)} collective-permute-done((bf16[2,32,2048]{2,1,0:T(8,128)(2,1)S(1)}, bf16[2,32,2048]{2,1,0:T(8,128)(2,1)S(1)}, u32[]{:S(2)}, u32[]{:S(2)}) %collective-permute-start.32) | collective-permute-done | bytes 262176 | tf_op jit(solution)/shard_map/ppermute | solution.py:86
  178.2 14.9 %collective-permute-done.33 = bf16[2,32,2048]{2,1,0:T(8,128)(2,1)S(1)} collective-permute-done((bf16[2,32,2048]{2,1,0:T(8,128)(2,1)S(1)}, bf16[2,32,2048]{2,1,0:T(8,128)(2,1)S(1)}, u32[]{:S(2)}, u32[]{:S(2)}) %collective-permute-start.33) | collective-permute-done | bytes 262176 | tf_op jit(solution)/shard_map/ppermute | solution.py:86
  193.2 1.6 collective-permute-start.35
  194.8 3.4 %collective-permute-done.35 = bf16[32,2048]{1,0:T(8,128)(2,1)S(1)} collective-permute-done((bf16[32,2048]{1,0:T(8,128)(2,1)S(1)}, bf16[32,2048]{1,0:T(8,128)(2,1)S(1)}, u32[]{:S(2)}, u32[]{:S(2)}) %collective-permute-start.35) | collective-permute-done | bytes 131104 | tf_op jit(solution)/shard_map/ppermute | solution.py:82
  198.5 0.9 add_convert_fusion
  (124 shorter events, 14.7 us)
Async XLA Ops:
  0.0 27.6 %copy-start = (bf16[4096,128]{1,0:T(8,128)(2,1)S(1)}, bf16[4096,128]{1,0:T(8,128)(2,1)}, u32[]{:S(2)}) copy-start(bf16[4096,128]{1,0:T(8,128)(2,1)} %param.29) | copy-start | bytes 3145732
  0.0 12.1 %collective-permute-start = (bf16[32,4096]{1,0:T(8,128)(2,1)}, bf16[32,4096]{1,0:T(8,128)(2,1)S(1)}, u32[]{:S(2)}, u32[]{:S(2)}) collective-permute-start(bf16[32,4096]{1,0:T(8,128)(2,1)} %param.19), channel_id=1, source_target_pairs={{1,0},{2,1},{3,2},{0,3},{5,4},{6,5},{7,6},{4,7},{9,8},{10,9},{11,1... | collective-permute-start | bytes 786440 | tf_op jit(solution)/shard_map/ppermute | solution.py:86
  5.1 22.5 %collective-permute-start.1 = (bf16[32,4096]{1,0:T(8,128)(2,1)}, bf16[32,4096]{1,0:T(8,128)(2,1)S(1)}, u32[]{:S(2)}, u32[]{:S(2)}) collective-permute-start(bf16[32,4096]{1,0:T(8,128)(2,1)} %param.19), channel_id=1, source_target_pairs={{2,0},{3,1},{0,2},{1,3},{6,4},{7,5},{4,6},{5,7},{10,8},{11,9},{8,1... | collective-permute-start | bytes 786440 | tf_op jit(solution)/shard_map/ppermute | solution.py:86
  5.1 22.5 %collective-permute-start.2 = (bf16[32,4096]{1,0:T(8,128)(2,1)}, bf16[32,4096]{1,0:T(8,128)(2,1)S(1)}, u32[]{:S(2)}, u32[]{:S(2)}) collective-permute-start(bf16[32,4096]{1,0:T(8,128)(2,1)} %param.19), channel_id=1, source_target_pairs={{3,0},{0,1},{1,2},{2,3},{7,4},{4,5},{5,6},{6,7},{11,8},{8,9},{9,10... | collective-permute-start | bytes 786440 | tf_op jit(solution)/shard_map/ppermute | solution.py:86
  6.1 35.6 %collective-permute-start.3 = (bf16[192,4096]{1,0:T(8,128)(2,1)}, bf16[192,4096]{1,0:T(8,128)(2,1)}, u32[]{:S(2)}, u32[]{:S(2)}) collective-permute-start(bf16[192,4096]{1,0:T(8,128)(2,1)} %bitcast.90), channel_id=1, source_target_pairs={{0,8},{8,0},{1,9},{9,1},{2,10},{10,2},{3,11},{11,3},{4,12},{12,4},... | collective-permute-start | bytes 4718600 | tf_op jit(solution)/shard_map/ppermute | solution.py:82
  7.6 134.9 %collective-permute-start.21 = (bf16[192,4096]{1,0:T(8,128)(2,1)}, bf16[192,4096]{1,0:T(8,128)(2,1)}, u32[]{:S(2)}, u32[]{:S(2)}) collective-permute-start(bf16[192,4096]{1,0:T(8,128)(2,1)} %bitcast.91), channel_id=1, source_target_pairs={{0,4},{4,0},{1,5},{5,1},{2,6},{6,2},{3,7},{7,3},{8,12},{12,8},{9,1... | collective-permute-start | bytes 4718600 | tf_op jit(solution)/shard_map/ppermute | solution.py:82
  32.1 3.4 %copy-start.4 = (bf16[4096,128]{1,0:T(8,128)(2,1)S(1)}, bf16[4096,128]{1,0:T(8,128)(2,1)}, u32[]{:S(2)}) copy-start(bf16[4096,128]{1,0:T(8,128)(2,1)} %param.30) | copy-start | bytes 3145732
  32.1 3.4 %copy-start.5 = (bf16[128,512]{1,0:T(8,128)(2,1)S(1)}, bf16[128,512]{1,0:T(8,128)(2,1)}, u32[]{:S(2)}) copy-start(bf16[128,512]{1,0:T(8,128)(2,1)} %param.32) | copy-start | bytes 393220
  36.1 3.5 %copy-start.8 = (f32[512]{0:T(512)S(1)}, f32[512]{0:T(512)}, u32[]{:S(2)}) copy-start(f32[512]{0:T(512)} %param.28) | copy-start | bytes 6148
  36.1 3.5 %copy-start.9 = (f32[512]{0:T(512)S(1)}, f32[512]{0:T(512)}, u32[]{:S(2)}) copy-start(f32[512]{0:T(512)} %param.27) | copy-start | bytes 6148
  41.7 8.8 %copy-start.2 = (bf16[4096,192]{0,1:T(8,128)(2,1)S(1)}, bf16[4096,192]{0,1:T(8,128)(2,1)}, u32[]{:S(2)}) copy-start(bf16[4096,192]{0,1:T(8,128)(2,1)} %param.37) | copy-start | bytes 4718596
  41.7 34.8 %collective-permute-start.8 = (bf16[192,4096]{1,0:T(8,128)(2,1)}, bf16[192,4096]{1,0:T(8,128)(2,1)S(1)}, u32[]{:S(2)}, u32[]{:S(2)}) collective-permute-start(bf16[192,4096]{1,0:T(8,128)(2,1)} %bitcast.93), channel_id=1, source_target_pairs={{0,8},{8,0},{1,9},{9,1},{2,10},{10,2},{3,11},{11,3},{4,12},{12,4},... | collective-permute-start | bytes 4718600 | tf_op jit(solution)/shard_map/ppermute | solution.py:82
  46.1 30.5 %copy-start.3 = (bf16[32,4096]{1,0:T(8,128)(2,1)S(1)}, bf16[32,4096]{1,0:T(8,128)(2,1)}, u32[]{:S(2)}) copy-start(bf16[32,4096]{1,0:T(8,128)(2,1)} %param.19) | copy-start | bytes 786436
  46.1 30.5 %copy-start.6 = (f32[4096]{0:T(1024)S(1)}, f32[4096]{0:T(1024)}, u32[]{:S(2)}) copy-start(f32[4096]{0:T(1024)} %param.33) | copy-start | bytes 49156
  46.2 9.9 %collective-permute-start.4 = (bf16[32,4096]{1,0:T(8,128)(2,1)S(1)}, bf16[32,4096]{1,0:T(8,128)(2,1)S(1)}, u32[]{:S(2)}, u32[]{:S(2)}) collective-permute-start(bf16[32,4096]{1,0:T(8,128)(2,1)S(1)} %get-tuple-element.60), channel_id=1, source_target_pairs={{1,0},{2,1},{3,2},{0,3},{5,4},{6,5},{7,6},{4,7},{9,8},{10,9},{11,1... | collective-permute-start | bytes 786440 | tf_op jit(solution)/shard_map/ppermute | solution.py:86
  49.3 21.7 %collective-permute-start.5 = (bf16[32,4096]{1,0:T(8,128)(2,1)S(1)}, bf16[32,4096]{1,0:T(8,128)(2,1)S(1)}, u32[]{:S(2)}, u32[]{:S(2)}) collective-permute-start(bf16[32,4096]{1,0:T(8,128)(2,1)S(1)} %get-tuple-element.62), channel_id=1, source_target_pairs={{2,0},{3,1},{0,2},{1,3},{6,4},{7,5},{4,6},{5,7},{10,8},{11,9},{8,1... | collective-permute-start | bytes 786440 | tf_op jit(solution)/shard_map/ppermute | solution.py:86
  50.2 20.8 %collective-permute-start.6 = (bf16[32,4096]{1,0:T(8,128)(2,1)S(1)}, bf16[32,4096]{1,0:T(8,128)(2,1)S(1)}, u32[]{:S(2)}, u32[]{:S(2)}) collective-permute-start(bf16[32,4096]{1,0:T(8,128)(2,1)S(1)} %get-tuple-element.61), channel_id=1, source_target_pairs={{3,0},{0,1},{1,2},{2,3},{7,4},{4,5},{5,6},{6,7},{11,8},{8,9},{9,10... | collective-permute-start | bytes 786440 | tf_op jit(solution)/shard_map/ppermute | solution.py:86
  56.1 15.0 %collective-permute-start.7 = (bf16[192,2048]{1,0:T(8,128)(2,1)S(1)}, bf16[192,2048]{1,0:T(8,128)(2,1)S(1)}, u32[]{:S(2)}, u32[]{:S(2)}) collective-permute-start(bf16[192,2048]{1,0:T(8,128)(2,1)S(1)} %get-tuple-element.55), channel_id=1, source_target_pairs={{0,16},{16,0},{1,17},{17,1},{2,18},{18,2},{3,19},{19,3},{4,20},{20... | collective-permute-start | bytes 2359304 | tf_op jit(solution)/shard_map/ppermute | solution.py:82
  76.8 10.1 %collective-permute-start.10 = (bf16[32,4096]{1,0:T(8,128)(2,1)S(1)}, bf16[32,4096]{1,0:T(8,128)(2,1)S(1)}, u32[]{:S(2)}, u32[]{:S(2)}) collective-permute-start(bf16[32,4096]{1,0:T(8,128)(2,1)S(1)} %get-tuple-element.52), channel_id=1, source_target_pairs={{0,1},{1,2},{2,3},{4,5},{5,6},{6,7},{8,9},{9,10},{10,11},{12,13},{... | collective-permute-start | bytes 786440 | tf_op jit(solution)/shard_map/ppermute | solution.py:105
  83.0 8.3 %collective-permute-start.9 = (bf16[32,4096]{1,0:T(8,128)(2,1)S(1)}, bf16[32,4096]{1,0:T(8,128)(2,1)S(1)}, u32[]{:S(2)}, u32[]{:S(2)}) collective-permute-start(bf16[32,4096]{1,0:T(8,128)(2,1)S(1)} %get-tuple-element.52), channel_id=1, source_target_pairs={{1,0},{2,1},{3,2},{5,4},{6,5},{7,6},{9,8},{10,9},{11,10},{13,12},{... | collective-permute-start | bytes 786440 | tf_op jit(solution)/shard_map/ppermute | solution.py:104
  84.3 34.8 %collective-permute-start.25 = (bf16[192,2048]{1,0:T(8,128)(2,1)S(1)}, bf16[192,2048]{1,0:T(8,128)(2,1)S(1)}, u32[]{:S(2)}, u32[]{:S(2)}) collective-permute-start(bf16[192,2048]{1,0:T(8,128)(2,1)S(1)} %get-tuple-element.29), channel_id=1, source_target_pairs={{0,4},{4,0},{1,5},{5,1},{2,6},{6,2},{3,7},{7,3},{8,12},{12,8},{9,1... | collective-permute-start | bytes 2359304 | tf_op jit(solution)/shard_map/ppermute | solution.py:82
  84.5 11.6 %collective-permute-start.11 = (bf16[96,2048]{1,0:T(8,128)(2,1)S(1)}, bf16[96,2048]{1,0:T(8,128)(2,1)S(1)}, u32[]{:S(2)}, u32[]{:S(2)}) collective-permute-start(bf16[96,2048]{1,0:T(8,128)(2,1)S(1)} %get-tuple-element.66), channel_id=1, source_target_pairs={{0,8},{8,0},{1,9},{9,1},{2,10},{10,2},{3,11},{11,3},{4,12},{12,4},... | collective-permute-start | bytes 1179656 | tf_op jit(solution)/shard_map/ppermute | solution.py:82
  86.9 20.7 %collective-permute-start.15 = (bf16[32,4096]{1,0:T(8,128)(2,1)S(1)}, bf16[32,4096]{1,0:T(8,128)(2,1)S(1)}, u32[]{:S(2)}, u32[]{:S(2)}) collective-permute-start(bf16[32,4096]{1,0:T(8,128)(2,1)S(1)} %get-tuple-element.52), channel_id=1, source_target_pairs={{0,16},{16,0},{1,17},{17,1},{2,18},{18,2},{3,19},{19,3},{4,20},{20... | collective-permute-start | bytes 786440 | tf_op jit(solution)/shard_map/ppermute | solution.py:82
  96.0 24.8 %copy-start.11 = (bf16[4096,192]{0,1:T(8,128)(2,1)S(1)}, bf16[4096,192]{0,1:T(8,128)(2,1)}, u32[]{:S(2)}) copy-start(bf16[4096,192]{0,1:T(8,128)(2,1)} %param.36) | copy-start | bytes 4718596
  96.0 10.8 %collective-permute-start.12 = (bf16[32,4096]{1,0:T(8,128)(2,1)S(1)}, bf16[32,4096]{1,0:T(8,128)(2,1)S(1)}, u32[]{:S(2)}, u32[]{:S(2)}) collective-permute-start(bf16[32,4096]{1,0:T(8,128)(2,1)S(1)} %collective-permute-done.9), channel_id=1, source_target_pairs={{1,0},{2,1},{5,4},{6,5},{9,8},{10,9},{13,12},{14,13},{17,16},{18,1... | collective-permute-start | bytes 786440 | tf_op jit(solution)/shard_map/ppermute | solution.py:114
  97.5 9.4 %collective-permute-start.13 = (bf16[32,4096]{1,0:T(8,128)(2,1)S(1)}, bf16[32,4096]{1,0:T(8,128)(2,1)S(1)}, u32[]{:S(2)}, u32[]{:S(2)}) collective-permute-start(bf16[32,4096]{1,0:T(8,128)(2,1)S(1)} %collective-permute-done.10), channel_id=1, source_target_pairs={{1,2},{2,3},{5,6},{6,7},{9,10},{10,11},{13,14},{14,15},{17,18},{18... | collective-permute-start | bytes 786440 | tf_op jit(solution)/shard_map/ppermute | solution.py:115
  106.9 13.9 %collective-permute-start.29 = (bf16[192,2048]{1,0:T(8,128)(2,1)S(1)}, bf16[192,2048]{1,0:T(8,128)(2,1)S(1)}, u32[]{:S(2)}, u32[]{:S(2)}) collective-permute-start(bf16[192,2048]{1,0:T(8,128)(2,1)S(1)} %collective-permute-done.7), channel_id=1, source_target_pairs={{0,4},{4,0},{1,5},{5,1},{2,6},{6,2},{3,7},{7,3},{8,12},{12,8},{9,1... | collective-permute-start | bytes 2359304 | tf_op jit(solution)/shard_map/ppermute | solution.py:82
  106.9 11.5 %collective-permute-start.14 = (bf16[96,2048]{1,0:T(8,128)(2,1)S(1)}, bf16[96,2048]{1,0:T(8,128)(2,1)S(1)}, u32[]{:S(2)}, u32[]{:S(2)}) collective-permute-start(bf16[96,2048]{1,0:T(8,128)(2,1)S(1)} %get-tuple-element.32), channel_id=1, source_target_pairs={{0,8},{8,0},{1,9},{9,1},{2,10},{10,2},{3,11},{11,3},{4,12},{12,4},... | collective-permute-start | bytes 1179656 | tf_op jit(solution)/shard_map/ppermute | solution.py:82
  107.6 13.3 %collective-permute-start.18 = (bf16[32,4096]{1,0:T(8,128)(2,1)S(1)}, bf16[32,4096]{1,0:T(8,128)(2,1)S(1)}, u32[]{:S(2)}, u32[]{:S(2)}) collective-permute-start(bf16[32,4096]{1,0:T(8,128)(2,1)S(1)} %broadcast_select_fusion.2), channel_id=1, source_target_pairs={{0,16},{16,0},{1,17},{17,1},{2,18},{18,2},{3,19},{19,3},{4,20},{20... | collective-permute-start | bytes 786440 | tf_op jit(solution)/shard_map/ppermute | solution.py:82
  118.4 10.7 %collective-permute-start.17 = (bf16[96,2048]{1,0:T(8,128)(2,1)S(1)}, bf16[96,2048]{1,0:T(8,128)(2,1)S(1)}, u32[]{:S(2)}, u32[]{:S(2)}) collective-permute-start(bf16[96,2048]{1,0:T(8,128)(2,1)S(1)} %get-tuple-element.35), channel_id=1, source_target_pairs={{0,8},{8,0},{1,9},{9,1},{2,10},{10,2},{3,11},{11,3},{4,12},{12,4},... | collective-permute-start | bytes 1179656 | tf_op jit(solution)/shard_map/ppermute | solution.py:82
  119.1 9.5 %collective-permute-start.16 = (bf16[32,4096]{1,0:T(8,128)(2,1)S(1)}, bf16[32,4096]{1,0:T(8,128)(2,1)S(1)}, u32[]{:S(2)}, u32[]{:S(2)}) collective-permute-start(bf16[32,4096]{1,0:T(8,128)(2,1)S(1)} %broadcast_select_fusion.1), channel_id=1, source_target_pairs={{1,0},{2,3},{5,4},{6,7},{9,8},{10,11},{13,12},{14,15},{17,16},{18,... | collective-permute-start | bytes 786440 | tf_op jit(solution)/shard_map/ppermute | solution.py:121
  120.8 33.4 %collective-permute-start.23 = (bf16[192,4096]{1,0:T(8,128)(2,1)S(1)}, bf16[192,4096]{1,0:T(8,128)(2,1)S(1)}, u32[]{:S(2)}, u32[]{:S(2)}) collective-permute-start(bf16[192,4096]{1,0:T(8,128)(2,1)S(1)} %bitcast.94), channel_id=1, source_target_pairs={{0,4},{4,0},{1,5},{5,1},{2,6},{6,2},{3,7},{7,3},{8,12},{12,8},{9,1... | collective-permute-start | bytes 4718600 | tf_op jit(solution)/shard_map/ppermute | solution.py:82
  121.0 22.2 %collective-permute-start.22 = (bf16[192,4096]{1,0:T(8,128)(2,1)}, bf16[192,4096]{1,0:T(8,128)(2,1)S(1)}, u32[]{:S(2)}, u32[]{:S(2)}) collective-permute-start(bf16[192,4096]{1,0:T(8,128)(2,1)} %collective-permute-done.3), channel_id=1, source_target_pairs={{0,4},{4,0},{1,5},{5,1},{2,6},{6,2},{3,7},{7,3},{8,12},{12,8},{9,1... | collective-permute-start | bytes 4718600 | tf_op jit(solution)/shard_map/ppermute | solution.py:82
  129.4 13.8 %copy-start.10 = (bf16[4096,192]{0,1:T(8,128)(2,1)S(1)}, bf16[4096,192]{0,1:T(8,128)(2,1)}, u32[]{:S(2)}) copy-start(bf16[4096,192]{0,1:T(8,128)(2,1)} %param.35) | copy-start | bytes 4718596
  129.4 9.3 %collective-permute-start.19 = (bf16[32,4096]{1,0:T(8,128)(2,1)S(1)}, bf16[32,4096]{1,0:T(8,128)(2,1)S(1)}, u32[]{:S(2)}, u32[]{:S(2)}) collective-permute-start(bf16[32,4096]{1,0:T(8,128)(2,1)S(1)} %get-tuple-element.50), channel_id=1, source_target_pairs={{0,16},{16,0},{1,17},{17,1},{2,18},{18,2},{3,19},{19,3},{4,20},{20... | collective-permute-start | bytes 786440 | tf_op jit(solution)/shard_map/ppermute | solution.py:82
  131.0 11.1 %collective-permute-start.20 = (bf16[32,4096]{1,0:T(8,128)(2,1)S(1)}, bf16[32,4096]{1,0:T(8,128)(2,1)S(1)}, u32[]{:S(2)}, u32[]{:S(2)}) collective-permute-start(bf16[32,4096]{1,0:T(8,128)(2,1)S(1)} %get-tuple-element.49), channel_id=1, source_target_pairs={{0,16},{16,0},{1,17},{17,1},{2,18},{18,2},{3,19},{19,3},{4,20},{20... | collective-permute-start | bytes 786440 | tf_op jit(solution)/shard_map/ppermute | solution.py:82
  138.7 15.5 %collective-permute-start.24 = (bf16[192,4096]{1,0:T(8,128)(2,1)S(1)}, bf16[192,4096]{1,0:T(8,128)(2,1)S(1)}, u32[]{:S(2)}, u32[]{:S(2)}) collective-permute-start(bf16[192,4096]{1,0:T(8,128)(2,1)S(1)} %collective-permute-done.8), channel_id=1, source_target_pairs={{0,4},{4,0},{1,5},{5,1},{2,6},{6,2},{3,7},{7,3},{8,12},{12,8},{9,1... | collective-permute-start | bytes 4718600 | tf_op jit(solution)/shard_map/ppermute | solution.py:82
  142.1 16.1 %collective-permute-start.26 = (bf16[192,2048]{1,0:T(8,128)(2,1)S(1)}, bf16[192,2048]{1,0:T(8,128)(2,1)S(1)}, u32[]{:S(2)}, u32[]{:S(2)}) collective-permute-start(bf16[192,2048]{1,0:T(8,128)(2,1)S(1)} %pad_maximum_fusion), channel_id=1, source_target_pairs={{0,4},{4,0},{1,5},{5,1},{2,6},{6,2},{3,7},{7,3},{8,12},{12,8},{9,1... | collective-permute-start | bytes 2359304 | tf_op jit(solution)/shard_map/ppermute | solution.py:82
  142.4 11.6 %collective-permute-start.30 = (bf16[96,2048]{1,0:T(8,128)(2,1)S(1)}, bf16[96,2048]{1,0:T(8,128)(2,1)S(1)}, u32[]{:S(2)}, u32[]{:S(2)}) collective-permute-start(bf16[96,2048]{1,0:T(8,128)(2,1)S(1)} %get-tuple-element.44), channel_id=1, source_target_pairs={{0,8},{8,0},{1,9},{9,1},{2,10},{10,2},{3,11},{11,3},{4,12},{12,4},... | collective-permute-start | bytes 1179656 | tf_op jit(solution)/shard_map/ppermute | solution.py:82
  154.1 4.2 %collective-permute-start.31 = (bf16[192,2048]{1,0:T(8,128)(2,1)S(1)}, bf16[192,2048]{1,0:T(8,128)(2,1)S(1)}, u32[]{:S(2)}, u32[]{:S(2)}) collective-permute-start(bf16[192,2048]{1,0:T(8,128)(2,1)S(1)} %pad_maximum_fusion.1), channel_id=1, source_target_pairs={{0,4},{4,0},{1,5},{5,1},{2,6},{6,2},{3,7},{7,3},{8,12},{12,8},{9,1... | collective-permute-start | bytes 2359304 | tf_op jit(solution)/shard_map/ppermute | solution.py:82
  156.1 7.8 %collective-permute-start.27 = (bf16[128,768]{1,0:T(8,128)(2,1)S(1)}, bf16[128,768]{1,0:T(8,128)(2,1)S(1)}, u32[]{:S(2)}, u32[]{:S(2)}) collective-permute-start(bf16[128,768]{1,0:T(8,128)(2,1)S(1)} %get-tuple-element.69), channel_id=1, source_target_pairs={{0,16},{16,0},{1,17},{17,1},{2,18},{18,2},{3,19},{19,3},{4,20},{20... | collective-permute-start | bytes 589832 | tf_op jit(solution)/shard_map/ppermute | solution.py:82
  157.7 10.0 %collective-permute-start.28 = (bf16[128,768]{1,0:T(8,128)(2,1)S(1)}, bf16[128,768]{1,0:T(8,128)(2,1)S(1)}, u32[]{:S(2)}, u32[]{:S(2)}) collective-permute-start(bf16[128,768]{1,0:T(8,128)(2,1)S(1)} %get-tuple-element.70), channel_id=1, source_target_pairs={{0,16},{16,0},{1,17},{17,1},{2,18},{18,2},{3,19},{19,3},{4,20},{20... | collective-permute-start | bytes 589832 | tf_op jit(solution)/shard_map/ppermute | solution.py:82
  168.7 30.7 %copy-start.1 = (bf16[4096,128]{1,0:T(8,128)(2,1)S(1)}, bf16[4096,128]{1,0:T(8,128)(2,1)}, u32[]{:S(2)}) copy-start(bf16[4096,128]{1,0:T(8,128)(2,1)} %param.29) | copy-start | bytes 3145732
  169.7 28.8 %copy-start.7 = (f32[4096]{0:T(1024)S(1)}, f32[4096]{0:T(1024)}, u32[]{:S(2)}) copy-start(f32[4096]{0:T(1024)} %param.34) | copy-start | bytes 49156
  169.8 8.4 %collective-permute-start.32 = (bf16[2,32,2048]{2,1,0:T(8,128)(2,1)S(1)}, bf16[2,32,2048]{2,1,0:T(8,128)(2,1)S(1)}, u32[]{:S(2)}, u32[]{:S(2)}) collective-permute-start(bf16[2,32,2048]{2,1,0:T(8,128)(2,1)S(1)} %get-tuple-element.57), channel_id=1, source_target_pairs={{1,0},{2,1},{3,2},{0,3},{5,4},{6,5},{7,6},{4,7},{9,8},{10,9},{11,1... | collective-permute-start | bytes 786440 | tf_op jit(solution)/shard_map/ppermute | solution.py:86
  169.9 23.2 %collective-permute-start.33 = (bf16[2,32,2048]{2,1,0:T(8,128)(2,1)S(1)}, bf16[2,32,2048]{2,1,0:T(8,128)(2,1)S(1)}, u32[]{:S(2)}, u32[]{:S(2)}) collective-permute-start(bf16[2,32,2048]{2,1,0:T(8,128)(2,1)S(1)} %get-tuple-element.58), channel_id=1, source_target_pairs={{2,0},{3,1},{0,2},{1,3},{6,4},{7,5},{4,6},{5,7},{10,8},{11,9},{8,1... | collective-permute-start | bytes 786440 | tf_op jit(solution)/shard_map/ppermute | solution.py:86
  170.3 22.7 %collective-permute-start.34 = (bf16[2,32,2048]{2,1,0:T(8,128)(2,1)S(1)}, bf16[2,32,2048]{2,1,0:T(8,128)(2,1)S(1)}, u32[]{:S(2)}, u32[]{:S(2)}) collective-permute-start(bf16[2,32,2048]{2,1,0:T(8,128)(2,1)S(1)} %get-tuple-element.59), channel_id=1, source_target_pairs={{3,0},{0,1},{1,2},{2,3},{7,4},{4,5},{5,6},{6,7},{11,8},{8,9},{9,10... | collective-permute-start | bytes 786440 | tf_op jit(solution)/shard_map/ppermute | solution.py:86
  193.2 5.0 %collective-permute-start.35 = (bf16[32,2048]{1,0:T(8,128)(2,1)S(1)}, bf16[32,2048]{1,0:T(8,128)(2,1)S(1)}, u32[]{:S(2)}, u32[]{:S(2)}) collective-permute-start(bf16[32,2048]{1,0:T(8,128)(2,1)S(1)} %fusion.32), channel_id=1, source_target_pairs={{0,16},{16,0},{1,17},{17,1},{2,18},{18,2},{3,19},{19,3},{4,20},{20... | collective-permute-start | bytes 393224 | tf_op jit(solution)/shard_map/ppermute | solution.py:82

commit v5 on v1

--- a/solution.py
+++ b/solution.py
@@ -3,6 +3,8 @@
 import jax
 import jax.numpy as jnp
 from jax import lax
+from jax.experimental import pallas as pl
+from jax.experimental.pallas import tpu as pltpu
 from jax.sharding import Mesh, PartitionSpec as P
 
 HEAD_SIZE = 128
@@ -10,7 +12,6 @@
 ADAPTER_SLOTS = 8
 SINKS = 4
 REQ = ("y", "x", "core")
-STATIONARY_TOKENS = 2048
 
 
 epsilon = 1e-06
@@ -22,11 +23,15 @@
     return inputs * lax.rsqrt(jnp.mean(inputs * inputs, axis=-1, keepdims=True) + epsilon)
 
 
+def rotary_angles(position):
+    exponent = jnp.arange(HEAD_SIZE // 2, dtype=jnp.float32) * (2.0 / HEAD_SIZE)
+    frequency = rope_theta ** (-exponent)
+    return position.astype(jnp.float32)[:, None] * frequency[None, :]
+
+
 def rotary(inputs, position):
     half_dim = inputs.shape[-1] // 2
-    exponent = jnp.arange(half_dim, dtype=jnp.float32) * (2.0 / inputs.shape[-1])
-    frequency = rope_theta ** (-exponent)
-    angles = position.astype(jnp.float32)[:, None] * frequency[None, :]
+    angles = rotary_angles(position)
     cosine = jnp.cos(angles)[:, None, :]
     sine_part = jnp.sin(angles)[:, None, :]
     first_half = inputs[..., :half_dim]
@@ -37,10 +42,9 @@
     )
 
 
-def layout(lengths, adapters, slot_adapter_index, row_count):
+def layout(lengths, adapters, slot_adapter_index, places):
     req_ends = jnp.cumsum(lengths)
     starts = req_ends - lengths
-    places = jnp.arange(row_count, dtype=jnp.int32)
     member = ((places[:, None] >= starts[None, :]) & (places[:, None] < req_ends[None, :])).astype(
         jnp.int32
     )
@@ -55,16 +59,20 @@
     return (request, position, token_slot)
 
 
+def allowed_keys(request, position, window):
+    distance = position[:, None] - position[None, :]
+    return (
+        (request[:, None] == request[None, :])
+        & (distance >= 0)
+        & ((distance < window) | (position[None, :] < SINKS))
+    )
+
+
 def attention(queries, key_heads, value_heads, request, position, window):
     scores = jnp.einsum(
         "qhd,khd->hqk", queries, key_heads, preferred_element_type=jnp.float32
     ) * HEAD_SIZE ** (-0.5)
-    distance = position[:, None] - position[None, :]
-    allowed = (
-        (request[:, None] == request[None, :])
-        & (distance >= 0)
-        & ((distance < window) | (position[None, :] < SINKS))
-    )
+    allowed = allowed_keys(request, position, window)
     scores = jnp.where(allowed[None, :, :], scores, -1e30)
     row_peak = jnp.max(scores, axis=-1, keepdims=True)
     weights = jnp.exp(scores - row_peak)
@@ -80,10 +88,226 @@
     return (jax.nn.silu(gate_act) * up_act).astype(jnp.bfloat16)
 
 
-def feed_forward(states, gate_rows, up_rows, down_rows):
-    return jnp.dot(
-        hidden_units(states, gate_rows, up_rows), down_rows, preferred_element_type=jnp.float32
-    )
+def exchange(block, axis):
+    return lax.ppermute(block, axis, [(0, 1), (1, 0)])
+
+
+def shift(block, hops):
+    return lax.ppermute(block, "mlp", [((k + hops) % 4, k) for k in range(4)])
+
+
+def line_gather(block):
+    across = shift(block, 2)
+    return [block, shift(block, 1), across, shift(block, 3)]
+
+
+def line_scatter(parts):
+    across = shift(parts[2], 2)
+    arrived = (parts[0], shift(parts[3], 1), across, shift(parts[1], 3))
+    return sum(part.astype(jnp.float32) for part in arrived)
+
+
+def together(*values):
+    return lax.optimization_barrier(values)
+
+
+def both_cores(rows, rows_x):
+    return jnp.concatenate([rows, exchange(rows, "core"), rows_x, exchange(rows_x, "core")])
+
+
+def in_vmem(*arrays):
+    return [pltpu.with_memory_space_constraint(array, pltpu.VMEM) for array in arrays]
+
+
+def vmem_call(kernel, outs, scratch, operands, vmem_mib):
+    whole = pl.BlockSpec(memory_space=pltpu.VMEM)
+    return pl.pallas_call(
+        kernel,
+        out_shape=outs,
+        in_specs=[whole] * len(operands),
+        out_specs=[whole] * len(outs),
+        scratch_shapes=scratch,
+        compiler_params=pltpu.CompilerParams(vmem_limit_bytes=vmem_mib << 20),
+        cost_estimate=pl.CostEstimate(flops=1 << 20, bytes_accessed=1 << 20, transcendentals=0),
+    )(*operands)
+
+
+NT = (((1,), (1,)), ((), ()))
+
+
+def attention_kernel(
+    block_0,
+    block_1,
+    block_2,
+    block_3,
+    query_weight,
+    key_weight,
+    value_weight,
+    output_weight,
+    query_down,
+    value_down,
+    query_up,
+    value_up,
+    query_gain,
+    key_gain,
+    cosine,
+    sine,
+    slot_mask,
+    allowed,
+    out_0,
+    out_1,
+    out_2,
+    out_3,
+    rows,
+    context,
+):
+    tok_dev = block_0.shape[0]
+    for k, block in enumerate((block_0, block_1, block_2, block_3)):
+        rows[k * tok_dev : (k + 1) * tok_dev, :] = block[...]
+
+    def project(weight):
+        return jnp.dot(rows[...], weight[...], preferred_element_type=jnp.float32)
+
+    def adapted(weight, down, up):
+        low = project(down).astype(jnp.bfloat16) * slot_mask[...]
+        return project(weight) + adapter_scale * jnp.dot(
+            low, up[...], preferred_element_type=jnp.float32
+        )
+
+    def heads(inputs, gain):
+        inputs = rms_scale(inputs) * gain
+        turned = pltpu.roll(inputs, HEAD_SIZE // 2, 1)
+        return (inputs * cosine[...] + turned * sine[...]).astype(jnp.bfloat16)
+
+    queries = adapted(query_weight, query_down, query_up)
+    keys = project(key_weight)
+    values = adapted(value_weight, value_down, value_up).astype(jnp.bfloat16)
+    for start in range(0, queries.shape[1], HEAD_SIZE):
+        at = slice(start, start + HEAD_SIZE)
+        scores = lax.dot_general(
+            heads(queries[:, at], query_gain[:, at]),
+            heads(keys[:, at], key_gain[:, at]),
+            NT,
+            preferred_element_type=jnp.float32,
+        ) * HEAD_SIZE ** (-0.5)
+        scores = jnp.where(allowed[...] > 0, scores, -1e30)
+        weights = jnp.exp(scores - jnp.max(scores, axis=-1, keepdims=True))
+        weights = (weights / jnp.sum(weights, axis=-1, keepdims=True)).astype(jnp.bfloat16)
+        context[:, at] = jnp.dot(
+            weights, values[:, at], preferred_element_type=jnp.float32
+        ).astype(jnp.bfloat16)
+    step = 1024
+    for start in range(0, output_weight.shape[1], step):
+        at = slice(start, start + step)
+        part = jnp.dot(context[...], output_weight[:, at], preferred_element_type=jnp.float32)
+        part = part.astype(jnp.bfloat16)
+        for k, out in enumerate((out_0, out_1, out_2, out_3)):
+            out[:, at] = part[k * tok_dev : (k + 1) * tok_dev]
+
+
+def hidden_kernel(states, gate_rows, up_rows, hidden_own, hidden_other):
+    half = hidden_own.shape[0]
+    step = 256
+    for start in range(0, gate_rows.shape[0], step):
+        at = slice(start, start + step)
+        gate_act = lax.dot_general(
+            states[...], gate_rows[at, :], NT, preferred_element_type=jnp.float32
+        )
+        up_act = lax.dot_general(
+            states[...], up_rows[at, :], NT, preferred_element_type=jnp.float32
+        )
+        hidden = (gate_act / (1.0 + jnp.exp(-gate_act)) * up_act).astype(jnp.bfloat16)
+        hidden_own[:, at] = hidden[:half]
+        hidden_other[:, at] = hidden[half:]
+
+
+def down_kernel(own, other, far_own, far_other, near_rows, far_rows, out_0, out_1, out_2, out_3):
+    tok_dev = out_0.shape[0] // 2
+    step = 512
+    for start in range(0, near_rows.shape[1], step):
+        at = slice(start, start + step)
+        for side, (near, far) in enumerate(((own, far_own), (other, far_other))):
+            part = jnp.dot(near[...], near_rows[:, at], preferred_element_type=jnp.float32)
+            part += jnp.dot(far[...], far_rows[:, at], preferred_element_type=jnp.float32)
+            part = part.astype(jnp.bfloat16)
+            for k, out in enumerate((out_0, out_1, out_2, out_3)):
+                out[side * tok_dev : (side + 1) * tok_dev, at] = part[
+                    k * tok_dev : (k + 1) * tok_dev
+                ]
+
+
+def add_normed(base, added, gain):
+    return (base.astype(jnp.float32) + rms_scale(added) * gain).astype(jnp.bfloat16)
+
+
+def layer_direct(
+    layer_input, angles, slot_mask, allowed, projections, adapters, head_gains, gains, ffn_rows
+):
+    tok_dev, width = layer_input.shape
+    gate_rows, up_rows, down_rows = ffn_rows
+    y = lax.axis_index("y")
+    half = width // 2
+    gate_x, up_x = exchange(gate_rows, "x"), exchange(up_rows, "x")
+    cosine, sine = jnp.cos(angles), jnp.sin(angles)
+    block = jax.ShapeDtypeStruct((tok_dev, width), jnp.bfloat16)
+    parts = vmem_call(
+        attention_kernel,
+        [block] * 4,
+        [
+            pltpu.VMEM((4 * tok_dev, width), jnp.bfloat16),
+            pltpu.VMEM((4 * tok_dev, projections[0].shape[1]), jnp.bfloat16),
+        ],
+        [
+            *line_gather(layer_input),
+            *in_vmem(*projections, *adapters[:2]),
+            *adapters[2:],
+            *head_gains,
+            jnp.concatenate([cosine, cosine], axis=1),
+            jnp.concatenate([-sine, sine], axis=1),
+            slot_mask,
+            allowed,
+        ],
+        24,
+    )
+    *parts, down_rows = together(*parts, down_rows)
+    near = lax.dynamic_slice_in_dim(down_rows, y * half, half, axis=1)
+    far = exchange(lax.dynamic_slice_in_dim(down_rows, (1 - y) * half, half, axis=1), "y")
+    near_x, far_x = exchange(near, "x"), exchange(far, "x")
+    attn_own, gate_x = together(line_scatter(parts), gate_x)
+    residual_own = add_normed(layer_input, attn_own, gains[0])
+    *line, other, up_x, near_x = together(
+        *line_gather(residual_own), exchange(residual_own, "y"), up_x, near_x
+    )
+    *others, far_x = together(*[exchange(rows, "y") for rows in line[1:]], far_x)
+    states = jnp.concatenate([*line, other, *others])
+    group = jax.ShapeDtypeStruct((4 * tok_dev, 4 * gate_rows.shape[0]), jnp.bfloat16)
+    hidden_own, hidden_other = vmem_call(
+        hidden_kernel,
+        [group] * 2,
+        [],
+        [states, *in_vmem(both_cores(gate_rows, gate_x), both_cores(up_rows, up_x))],
+        24,
+    )
+    parts = vmem_call(
+        down_kernel,
+        [jax.ShapeDtypeStruct((2 * tok_dev, half), jnp.bfloat16)] * 4,
+        [],
+        [
+            hidden_own,
+            hidden_other,
+            exchange(hidden_other, "y"),
+            exchange(hidden_own, "y"),
+            *in_vmem(both_cores(near, near_x), both_cores(far, far_x)),
+        ],
+        24,
+    )
+    summed = line_scatter(parts)
+    own_half = summed[:tok_dev]
+    other_half = exchange(summed[tok_dev:].astype(jnp.bfloat16), "y").astype(jnp.float32)
+    mlp_own = jnp.concatenate(
+        [jnp.where(y == 1, other_half, own_half), jnp.where(y == 1, own_half, other_half)], axis=1
+    )
+    return add_normed(residual_own, mlp_own, gains[1])
 
 
 def shards(
@@ -111,12 +335,29 @@
     tok_group = tok_dev * lax.axis_size("mlp")
     window = tok_group * 3 // 8
     heads_local = query_weight.shape[1] // HEAD_SIZE
+    direct = [lax.axis_size(axis) for axis in (*REQ, "mlp")] == [2, 2, 2, 4]
+    places = jnp.arange(tok_group, dtype=jnp.int32)
+    if direct:
+        places = (places + lax.axis_index("mlp") * tok_dev) % tok_group
     request, position, token_slot = layout(
-        request_lengths[0], request_adapter[0], slot_adapter_index, tok_group
-    )
-    group_token_rows = lax.all_gather(layer_input, "mlp", axis=0, tiled=True)
+        request_lengths[0], request_adapter[0], slot_adapter_index, places
+    )
     columns = jnp.arange(ADAPTER_SLOTS * ADAPTER_RANK, dtype=jnp.int32) // ADAPTER_RANK
     slot_match_mask = (columns[None, :] == token_slot[:, None]).astype(jnp.bfloat16)
+    gate_rows, up_rows, down_rows = gate_weight.T, up_weight.T, down_weight_transposed.T
+    if direct:
+        return layer_direct(
+            layer_input,
+            rotary_angles(position),
+            slot_match_mask,
+            allowed_keys(request, position, window).astype(jnp.float32),
+            (query_weight, key_weight, value_weight, output_weight),
+            (query_down_factors, value_down_factors, query_up_factors, value_up_factors),
+            (query_norm_gain[None, :], key_norm_gain[None, :]),
+            (attention_norm_gain, feedforward_norm_gain),
+            (gate_rows, up_rows, down_rows),
+        )
+    group_token_rows = lax.all_gather(layer_input, "mlp", axis=0, tiled=True)
     query_reduced = (
         jnp.dot(group_token_rows, query_down_factors, preferred_element_type=jnp.float32).astype(
             jnp.bfloat16
@@ -158,30 +399,18 @@
         scatter_dimension=0,
         tiled=True,
     ).astype(jnp.float32)
-    residual_own = (
-        layer_input.astype(jnp.float32) + rms_scale(attn_own) * attention_norm_gain
-    ).astype(jnp.bfloat16)
-    gate_rows, up_rows, down_rows = gate_weight.T, up_weight.T, down_weight_transposed.T
-    if tok_group * lax.axis_size(REQ) <= STATIONARY_TOKENS:
-        token_axes = ("y", "x", "mlp")
-        swap = [(0, 1), (1, 0)]
-        gate_rows, up_rows, down_rows = (
-            jnp.concatenate([rows, lax.ppermute(rows, "core", swap)])
-            for rows in (gate_rows, up_rows, down_rows)
-        )
-    else:
-        token_axes = ("mlp",)
-        gate_rows, up_rows, down_rows = (
-            lax.all_gather(rows, REQ, axis=0, tiled=True) for rows in (gate_rows, up_rows, down_rows)
-        )
-    residual_all = lax.all_gather(residual_own, token_axes, axis=0, tiled=True)
-    partial_value = feed_forward(residual_all, gate_rows, up_rows, down_rows)
+    residual_own = add_normed(layer_input, attn_own, attention_norm_gain)
+    gate_rows, up_rows, down_rows = (
+        lax.all_gather(rows, REQ, axis=0, tiled=True) for rows in (gate_rows, up_rows, down_rows)
+    )
+    hidden = hidden_units(
+        lax.all_gather(residual_own, "mlp", axis=0, tiled=True), gate_rows, up_rows
+    )
+    part = jnp.dot(hidden, down_rows, preferred_element_type=jnp.float32)
     mlp_own = lax.psum_scatter(
-        partial_value.astype(jnp.bfloat16), token_axes, scatter_dimension=0, tiled=True
+        part.astype(jnp.bfloat16), "mlp", scatter_dimension=0, tiled=True
     ).astype(jnp.float32)
-    return (residual_own.astype(jnp.float32) + rms_scale(mlp_own) * feedforward_norm_gain).astype(
-        jnp.bfloat16
-    )
+    return add_normed(residual_own, mlp_own, feedforward_norm_gain)
 
 
 def solution(mesh):

time: 289 us -> 179 us (0.62)
  waiting for transfers between devices: 225 us -> 97.9 us
  starting transfers between devices: 0.77 us -> 42.6 us
  matrix products: 36.8 us -> 0 us
  local copies, waits for them, and re-layouts: 0.51 us -> 15.6 us
  between operations: 13.4 us -> 0.29 us
  Pallas kernels: 0 us -> 9.64 us
    reduce_scatter x2 -> x0, waiting for transfers between devices: 122 us -> none  [the longest x1 95.1 us: shards(): lax.psum_scatter(partial_value.astype(jnp.bfloat16), token_axes, scatter_...]
    all_gather x2 -> x0, waiting for transfers between devices: 97.8 us -> none  [the longest x1 69.6 us: shards(): residual_all = lax.all_gather(residual_own, token_axes, axis=0, tiled=True)]
    ppermute x3 -> x32, waiting for transfers between devices: 4.4 us -> 97.9 us  [the longest x20 49.8 us: exchange(): return lax.ppermute(block, axis, [(0, 1), (1, 0)])]
    ppermute x3 -> x32, starting transfers between devices: 0.65 us -> 42.6 us  [the longest x12 26.3 us: shift(): return lax.ppermute(block, 'mlp', [((k + hops) % 4, k) for k in range(4)])]
    dot_general x10 -> x0, matrix products: 35 us -> none  [the longest x1 10.8 us: feed_forward(): jnp.dot(hidden_units(states, gate_rows, up_rows), down_rows, preferred_el...]
    unnamed x32 -> x39, local copies, waits for them, and re-layouts: 0.09 us -> 15.5 us
    pallas_call x0 -> x3, Pallas kernels: none -> 9.64 us  [vmem_call(): pl.pallas_call(kernel, out_shape=outs, in_specs=[whole] * len(operands),...]
    concatenate x0 -> x5, other arithmetic: none -> 5.52 us  [the longest x4 5.42 us: both_cores(): jnp.concatenate([rows, exchange(rows, 'core'), rows_x, exchange(rows_x, '...]
  transfers between devices with their start and end apart: 7 -> 32, of which waited for: 5 -> 15; matrix products, arithmetic and copies ran while one was open for 3% -> 5% of each run, Pallas kernels for 0% -> 4%
where the time goes in v5:
time: 179 us; the launch traced here: 177 us
  waiting for transfers between devices  97.9 us (55%)
  starting transfers between devices  42.6 us (24%)
  local copies, waits for them, and re-layouts  15.6 us (9%)
  other arithmetic  10.6 us (6%)
  Pallas kernels  9.64 us (5%)
    ppermute x20, waiting for transfers between devices, exchange(): return lax.ppermute(block, axis, [(0, 1), (1, 0)])  49.8 us
    ppermute x12, waiting for transfers between devices, shift(): return lax.ppermute(block, 'mlp', [((k + hops) % 4, k) for k in range(4)])  48.1 us
    ppermute x12, starting transfers between devices, shift(): return lax.ppermute(block, 'mlp', [((k + hops) % 4, k) for k in range(4)])  26.3 us
    ppermute x20, starting transfers between devices, exchange(): return lax.ppermute(block, axis, [(0, 1), (1, 0)])  16.3 us
    unnamed x39, local copies, waits for them, and re-layouts  15.5 us
    pallas_call x3, Pallas kernels, vmem_call(): pl.pallas_call(kernel, out_shape=outs, in_specs=[whole] * len(operands),...  9.64 us
    concatenate x4, other arithmetic, both_cores(): jnp.concatenate([rows, exchange(rows, 'core'), rows_x, exchange(rows_x, '...  5.42 us
  transfers between devices with their start and end apart: 32, of which 15 were waited for; matrix products, arithmetic and copies ran while one was open for 5% of the time, Pallas kernels for 4%

profile of v5, /device:TPU:0, one launch (start us, length us, event | category | flops | bytes accessed | tf_op | source)
XLA Modules:
  0.0 176.6 jit_solution(15132505784189187686)
XLA Ops:
  0.0 5.0 %collective-permute-start = (bf16[32,4096]{1,0:T(8,128)(2,1)}, bf16[32,4096]{1,0:T(8,128)(2,1)S(1)}, u32[]{:S(2)}, u32[]{:S(2)}) collective-permute-start(bf16[32,4096]{1,0:T(8,128)(2,1)} %block_0.1), channel_id=1, source_target_pairs={{1,0},{2,1},{3,2},{0,3},{5,4},{6,5},{7,6},{4,7},{9,8},{10,9},{11,1... | collective-permute-start | bytes 786440 | tf_op jit(solution)/shard_map/ppermute | solution.py:96
  5.1 1.0 collective-permute-start.2
  6.1 1.5 collective-permute-start.6
  8.1 0.8 reduce-window.4
  9.6 0.7 select_reduce_fusion.1
  12.1 15.4 %collective-permute-done.1.block_2 = bf16[32,4096]{1,0:T(8,128)(2,1)S(1)} collective-permute-done((bf16[32,4096]{1,0:T(8,128)(2,1)}, bf16[32,4096]{1,0:T(8,128)(2,1)S(1)}, u32[]{:S(2)}, u32[]{:S(2)}) %collective-permute-start.1) | collective-permute-done | bytes 262176 | tf_op jit(solution)/shard_map/ppermute | solution.py:96
  27.6 2.2 %copy-done = bf16[4096,512]{1,0:T(8,128)(2,1)S(1)} copy-done((bf16[4096,512]{1,0:T(8,128)(2,1)S(1)}, bf16[4096,512]{1,0:T(8,128)(2,1)}, u32[]{:S(2)}) %copy-start) | copy-done | bytes 4194328
  29.8 2.2 %copy-done.1 = bf16[4096,512]{1,0:T(8,128)(2,1)S(1)} copy-done((bf16[4096,512]{1,0:T(8,128)(2,1)S(1)}, bf16[4096,512]{1,0:T(8,128)(2,1)}, u32[]{:S(2)}) %copy-start.1) | copy-done | bytes 4194328
  32.0 2.2 %copy-done.2 = bf16[4096,512]{1,0:T(8,128)(2,1)S(1)} copy-done((bf16[4096,512]{1,0:T(8,128)(2,1)S(1)}, bf16[4096,512]{1,0:T(8,128)(2,1)}, u32[]{:S(2)}) %copy-start.2) | copy-done | bytes 4194328
  34.1 2.2 %copy-done.3 = bf16[512,4096]{1,0:T(8,128)(2,1)S(1)} copy-done((bf16[512,4096]{1,0:T(8,128)(2,1)S(1)}, bf16[512,4096]{1,0:T(8,128)(2,1)}, u32[]{:S(2)}) %copy-start.3) | copy-done | bytes 4194328
  36.3 0.9 copy-done.4
  37.3 1.2 copy-done.5
  38.5 1.2 copy-done.6
  39.7 0.9 copy-done.7
  40.6 0.9 copy-done.8
  42.9 4.3 %shard_map.181 = (bf16[32,4096]{1,0:T(8,128)(2,1)S(1)}, bf16[32,4096]{1,0:T(8,128)(2,1)S(1)}, bf16[32,4096]{1,0:T(8,128)(2,1)S(1)}, bf16[32,4096]{1,0:T(8,128)(2,1)S(1)}) custom-call(bf16[32,4096]{1,0:T(8,128)(2,1)S(1)} %copy-done.4, bf16[32,4096]{1,0:T(8,128)(2,1)S(1)} %collective-permute-done.block_1, bf16[32,4096]{1,0:T(8,128)(2,1)S(1)} %collective-permute-done.1.block_2, ...), custom_call_target="tpu_custom_call" | custom-call | flops 1048576 | bytes 1048576 | tf_op jit(solution)/shard_map/pallas_call | solution.py:124
  47.2 1.0 collective-permute-start.5
  48.2 1.9 %collective-permute-start.4 = (bf16[32,4096]{1,0:T(8,128)(2,1)S(1)}, bf16[32,4096]{1,0:T(8,128)(2,1)S(1)}, u32[]{:S(2)}, u32[]{:S(2)}) collective-permute-start(bf16[32,4096]{1,0:T(8,128)(2,1)S(1)} %get-tuple-element.39), channel_id=1, source_target_pairs={{2,0},{3,1},{0,2},{1,3},{6,4},{7,5},{4,6},{5,7},{10,8},{11,9},{8,1... | collective-permute-start | bytes 786440 | tf_op jit(solution)/shard_map/ppermute | solution.py:96
  50.1 2.8 %collective-permute-start.3 = (bf16[32,4096]{1,0:T(8,128)(2,1)S(1)}, bf16[32,4096]{1,0:T(8,128)(2,1)S(1)}, u32[]{:S(2)}, u32[]{:S(2)}) collective-permute-start(bf16[32,4096]{1,0:T(8,128)(2,1)S(1)} %get-tuple-element.38), channel_id=1, source_target_pairs={{1,0},{2,1},{3,2},{0,3},{5,4},{6,5},{7,6},{4,7},{9,8},{10,9},{11,1... | collective-permute-start | bytes 786440 | tf_op jit(solution)/shard_map/ppermute | solution.py:96
  53.2 5.3 %collective-permute-done.5 = bf16[32,4096]{1,0:T(8,128)(2,1)S(1)} collective-permute-done((bf16[32,4096]{1,0:T(8,128)(2,1)S(1)}, bf16[32,4096]{1,0:T(8,128)(2,1)S(1)}, u32[]{:S(2)}, u32[]{:S(2)}) %collective-permute-start.5) | collective-permute-done | bytes 262176 | tf_op jit(solution)/shard_map/ppermute | solution.py:96
  58.4 1.5 collective-permute-start.12
  59.9 7.7 %collective-permute-done.4 = bf16[32,4096]{1,0:T(8,128)(2,1)S(1)} collective-permute-done((bf16[32,4096]{1,0:T(8,128)(2,1)S(1)}, bf16[32,4096]{1,0:T(8,128)(2,1)S(1)}, u32[]{:S(2)}, u32[]{:S(2)}) %collective-permute-start.4) | collective-permute-done | bytes 262176 | tf_op jit(solution)/shard_map/ppermute | solution.py:96
  67.6 1.5 collective-permute-start.16
  69.6 7.8 %collective-permute-start.7 = (bf16[32,4096]{1,0:T(8,128)(2,1)S(1)}, bf16[32,4096]{1,0:T(8,128)(2,1)S(1)}, u32[]{:S(2)}, u32[]{:S(2)}) collective-permute-start(bf16[32,4096]{1,0:T(8,128)(2,1)S(1)} %add_convert_fusion.1), channel_id=1, source_target_pairs={{1,0},{2,1},{3,2},{0,3},{5,4},{6,5},{7,6},{4,7},{9,8},{10,9},{11,1... | collective-permute-start | bytes 786440 | tf_op jit(solution)/shard_map/ppermute | solution.py:96
  77.4 14.7 %collective-permute-done.12 = bf16[192,2048]{1,0:T(8,128)(2,1)S(1)} collective-permute-done((bf16[192,2048]{1,0:T(8,128)(2,1)S(1)}, bf16[192,2048]{1,0:T(8,128)(2,1)S(1)}, u32[]{:S(2)}, u32[]{:S(2)}) %collective-permute-start.12) | collective-permute-done | bytes 786464 | tf_op jit(solution)/shard_map/ppermute | solution.py:92
  92.1 2.5 %collective-permute-start.9 = (bf16[32,4096]{1,0:T(8,128)(2,1)S(1)}, bf16[32,4096]{1,0:T(8,128)(2,1)S(1)}, u32[]{:S(2)}, u32[]{:S(2)}) collective-permute-start(bf16[32,4096]{1,0:T(8,128)(2,1)S(1)} %add_convert_fusion.1), channel_id=1, source_target_pairs={{3,0},{0,1},{1,2},{2,3},{7,4},{4,5},{5,6},{6,7},{11,8},{8,9},{9,10... | collective-permute-start | bytes 786440 | tf_op jit(solution)/shard_map/ppermute | solution.py:96
  94.6 1.5 collective-permute-start.10
  96.1 1.6 collective-permute-start.17
  97.7 2.6 %collective-permute-done.9 = bf16[32,4096]{1,0:T(8,128)(2,1)S(1)} collective-permute-done((bf16[32,4096]{1,0:T(8,128)(2,1)S(1)}, bf16[32,4096]{1,0:T(8,128)(2,1)S(1)}, u32[]{:S(2)}, u32[]{:S(2)}) %collective-permute-start.9) | collective-permute-done | bytes 262176 | tf_op jit(solution)/shard_map/ppermute | solution.py:96
  100.3 1.0 collective-permute-done.10
  101.3 1.6 collective-permute-start.13
  103.5 1.6 collective-permute-start.15
  105.2 10.9 %collective-permute-done.17 = bf16[192,2048]{1,0:T(8,128)(2,1)S(1)} collective-permute-done((bf16[192,2048]{1,0:T(8,128)(2,1)S(1)}, bf16[192,2048]{1,0:T(8,128)(2,1)S(1)}, u32[]{:S(2)}, u32[]{:S(2)}) %collective-permute-start.17) | collective-permute-done | bytes 786464 | tf_op jit(solution)/shard_map/ppermute | solution.py:92
  116.7 1.1 collective-permute-done.15
  118.5 8.9 %collective-permute-done.25 = bf16[192,2048]{1,0:T(8,128)(2,1)S(1)} collective-permute-done((bf16[192,2048]{1,0:T(8,128)(2,1)S(1)}, bf16[192,2048]{1,0:T(8,128)(2,1)S(1)}, u32[]{:S(2)}, u32[]{:S(2)}) %collective-permute-start.25) | collective-permute-done | bytes 786464 | tf_op jit(solution)/shard_map/ppermute | solution.py:92
  128.4 3.1 %pad_maximum_fusion.gate_rows = bf16[768,4096]{1,0:T(8,128)(2,1)S(1)} fusion(bf16[192,4096]{1,0:T(8,128)(2,1)S(1)} %collective-permute-done.19, bf16[192,4096]{1,0:T(8,128)(2,1)} %collective-permute-done.6, bf16[192,4096]{1,0:T(8,128)(2,1)S(1)} %collective-permute-done.18, bf16[192,4096]{1,0:T(8,128)(2,1)S(1)} %bitcast.18), kind=kLoop, calls=%fused_computation | loop fusion | flops 25165824 | bytes 12582912 | tf_op jit(solution)/shard_map/concatenate | solution.py:115
  131.5 1.4 pad_maximum_fusion.1.up_rows
  133.0 3.5 %shard_map.182 = (bf16[128,768]{1,0:T(8,128)(2,1)S(1)}, bf16[128,768]{1,0:T(8,128)(2,1)S(1)}) custom-call(bf16[256,4096]{1,0:T(8,128)(2,1)S(1)} %constant_dynamic-update-slice_fusion.states, bf16[768,4096]{1,0:T(8,128)(2,1)S(1)} %pad_maximum_fusion.gate_rows, bf16[768,4096]{1,0:T(8,128)(2,1)S(1)} %pad_maximum_fusion.1.up_rows), custom_call_target="tpu_custom_call" | custom-call | flops 1048576 | bytes 1048576 | tf_op jit(solution)/shard_map/pallas_call | solution.py:124
  137.1 1.5 collective-permute-start.23
  139.0 5.3 %collective-permute-done.22.far_own = bf16[128,768]{1,0:T(8,128)(2,1)S(1)} collective-permute-done((bf16[128,768]{1,0:T(8,128)(2,1)S(1)}, bf16[128,768]{1,0:T(8,128)(2,1)S(1)}, u32[]{:S(2)}, u32[]{:S(2)}) %collective-permute-start.22) | collective-permute-done | bytes 196640 | tf_op jit(solution)/shard_map/ppermute | solution.py:92
  144.3 3.4 %collective-permute-done.23.far_other = bf16[128,768]{1,0:T(8,128)(2,1)S(1)} collective-permute-done((bf16[128,768]{1,0:T(8,128)(2,1)S(1)}, bf16[128,768]{1,0:T(8,128)(2,1)S(1)}, u32[]{:S(2)}, u32[]{:S(2)}) %collective-permute-start.23) | collective-permute-done | bytes 196640 | tf_op jit(solution)/shard_map/ppermute | solution.py:92
  147.7 1.9 %shard_map.183 = (bf16[64,2048]{1,0:T(8,128)(2,1)S(1)}, bf16[64,2048]{1,0:T(8,128)(2,1)S(1)}, bf16[64,2048]{1,0:T(8,128)(2,1)S(1)}, bf16[64,2048]{1,0:T(8,128)(2,1)S(1)}) custom-call(bf16[128,768]{1,0:T(8,128)(2,1)S(1)} %get-tuple-element.53.own, bf16[128,768]{1,0:T(8,128)(2,1)S(1)} %get-tuple-element.54.other, ...), custom_call_target="tpu_custom_call" | custom-call | flops 1048576 | bytes 1048576 | tf_op jit(solution)/shard_map/pallas_call | solution.py:124
  149.9 1.6 collective-permute-start.29
  151.5 2.2 %collective-permute-start.28 = (bf16[64,2048]{1,0:T(8,128)(2,1)S(1)}, bf16[64,2048]{1,0:T(8,128)(2,1)S(1)}, u32[]{:S(2)}, u32[]{:S(2)}) collective-permute-start(bf16[64,2048]{1,0:T(8,128)(2,1)S(1)} %get-tuple-element.58), channel_id=1, source_target_pairs={{1,0},{2,1},{3,2},{0,3},{5,4},{6,5},{7,6},{4,7},{9,8},{10,9},{11,1... | collective-permute-start | bytes 786440 | tf_op jit(solution)/shard_map/ppermute | solution.py:96
  153.7 7.0 %collective-permute-done.30 = bf16[64,2048]{1,0:T(8,128)(2,1)S(1)} collective-permute-done((bf16[64,2048]{1,0:T(8,128)(2,1)S(1)}, bf16[64,2048]{1,0:T(8,128)(2,1)S(1)}, u32[]{:S(2)}, u32[]{:S(2)}) %collective-permute-start.30) | collective-permute-done | bytes 262176 | tf_op jit(solution)/shard_map/ppermute | solution.py:96
  160.8 9.6 %collective-permute-done.29 = bf16[64,2048]{1,0:T(8,128)(2,1)S(1)} collective-permute-done((bf16[64,2048]{1,0:T(8,128)(2,1)S(1)}, bf16[64,2048]{1,0:T(8,128)(2,1)S(1)}, u32[]{:S(2)}, u32[]{:S(2)}) %collective-permute-start.29) | collective-permute-done | bytes 262176 | tf_op jit(solution)/shard_map/ppermute | solution.py:96
  171.1 4.4 %collective-permute-done.31 = bf16[32,2048]{1,0:T(8,128)(2,1)S(1)} collective-permute-done((bf16[32,2048]{1,0:T(8,128)(2,1)S(1)}, bf16[32,2048]{1,0:T(8,128)(2,1)S(1)}, u32[]{:S(2)}, u32[]{:S(2)}) %collective-permute-start.31) | collective-permute-done | bytes 131104 | tf_op jit(solution)/shard_map/ppermute | solution.py:92
  175.8 0.9 add_convert_fusion
  (86 shorter events, 10.1 us)
Async XLA Ops:
  0.0 12.1 %collective-permute-start = (bf16[32,4096]{1,0:T(8,128)(2,1)}, bf16[32,4096]{1,0:T(8,128)(2,1)S(1)}, u32[]{:S(2)}, u32[]{:S(2)}) collective-permute-start(bf16[32,4096]{1,0:T(8,128)(2,1)} %block_0.1), channel_id=1, source_target_pairs={{1,0},{2,1},{3,2},{0,3},{5,4},{6,5},{7,6},{4,7},{9,8},{10,9},{11,1... | collective-permute-start | bytes 786440 | tf_op jit(solution)/shard_map/ppermute | solution.py:96
  5.0 22.5 %collective-permute-start.1 = (bf16[32,4096]{1,0:T(8,128)(2,1)}, bf16[32,4096]{1,0:T(8,128)(2,1)S(1)}, u32[]{:S(2)}, u32[]{:S(2)}) collective-permute-start(bf16[32,4096]{1,0:T(8,128)(2,1)} %block_0.1), channel_id=1, source_target_pairs={{2,0},{3,1},{0,2},{1,3},{6,4},{7,5},{4,6},{5,7},{10,8},{11,9},{8,1... | collective-permute-start | bytes 786440 | tf_op jit(solution)/shard_map/ppermute | solution.py:96
  5.1 22.5 %collective-permute-start.2 = (bf16[32,4096]{1,0:T(8,128)(2,1)}, bf16[32,4096]{1,0:T(8,128)(2,1)S(1)}, u32[]{:S(2)}, u32[]{:S(2)}) collective-permute-start(bf16[32,4096]{1,0:T(8,128)(2,1)} %block_0.1), channel_id=1, source_target_pairs={{3,0},{0,1},{1,2},{2,3},{7,4},{4,5},{5,6},{6,7},{11,8},{8,9},{9,10... | collective-permute-start | bytes 786440 | tf_op jit(solution)/shard_map/ppermute | solution.py:96
  6.1 63.2 %collective-permute-start.6 = (bf16[192,4096]{1,0:T(8,128)(2,1)}, bf16[192,4096]{1,0:T(8,128)(2,1)}, u32[]{:S(2)}, u32[]{:S(2)}) collective-permute-start(bf16[192,4096]{1,0:T(8,128)(2,1)} %bitcast.16), channel_id=1, source_target_pairs={{0,8},{8,0},{1,9},{9,1},{2,10},{10,2},{3,11},{11,3},{4,12},{12,4},... | collective-permute-start | bytes 4718600 | tf_op jit(solution)/shard_map/ppermute | solution.py:92
  7.6 88.6 %collective-permute-start.11 = (bf16[192,4096]{1,0:T(8,128)(2,1)}, bf16[192,4096]{1,0:T(8,128)(2,1)S(1)}, u32[]{:S(2)}, u32[]{:S(2)}) collective-permute-start(bf16[192,4096]{1,0:T(8,128)(2,1)} %bitcast.19), channel_id=1, source_target_pairs={{0,8},{8,0},{1,9},{9,1},{2,10},{10,2},{3,11},{11,3},{4,12},{12,4},... | collective-permute-start | bytes 4718600 | tf_op jit(solution)/shard_map/ppermute | solution.py:92
  27.6 2.2 %copy-start = (bf16[4096,512]{1,0:T(8,128)(2,1)S(1)}, bf16[4096,512]{1,0:T(8,128)(2,1)}, u32[]{:S(2)}) copy-start(bf16[4096,512]{1,0:T(8,128)(2,1)} %query_weight.1) | copy-start | bytes 12582916
  29.8 2.2 %copy-start.1 = (bf16[4096,512]{1,0:T(8,128)(2,1)S(1)}, bf16[4096,512]{1,0:T(8,128)(2,1)}, u32[]{:S(2)}) copy-start(bf16[4096,512]{1,0:T(8,128)(2,1)} %key_weight.1) | copy-start | bytes 12582916
  32.0 2.2 %copy-start.2 = (bf16[4096,512]{1,0:T(8,128)(2,1)S(1)}, bf16[4096,512]{1,0:T(8,128)(2,1)}, u32[]{:S(2)}) copy-start(bf16[4096,512]{1,0:T(8,128)(2,1)} %value_weight.1) | copy-start | bytes 12582916
  34.1 2.2 %copy-start.3 = (bf16[512,4096]{1,0:T(8,128)(2,1)S(1)}, bf16[512,4096]{1,0:T(8,128)(2,1)}, u32[]{:S(2)}) copy-start(bf16[512,4096]{1,0:T(8,128)(2,1)} %output_weight.1) | copy-start | bytes 12582916
  36.3 0.9 copy-start.4
  37.3 1.2 copy-start.5
  38.5 1.2 copy-start.6
  39.7 0.9 copy-start.7
  40.6 0.9 copy-start.8
  41.5 0.7 copy-start.9
  42.2 0.7 copy-start.10
  42.9 10.1 %copy-start.13 = (bf16[4096,192]{0,1:T(8,128)(2,1)S(1)}, bf16[4096,192]{0,1:T(8,128)(2,1)}, u32[]{:S(2)}) copy-start(bf16[4096,192]{0,1:T(8,128)(2,1)} %param.37) | copy-start | bytes 4718596
  47.2 22.2 %copy-start.14 = (f32[4096]{0:T(1024)S(1)}, f32[4096]{0:T(1024)}, u32[]{:S(2)}) copy-start(f32[4096]{0:T(1024)} %param.33) | copy-start | bytes 49156
  47.2 11.2 %collective-permute-start.5 = (bf16[32,4096]{1,0:T(8,128)(2,1)S(1)}, bf16[32,4096]{1,0:T(8,128)(2,1)S(1)}, u32[]{:S(2)}, u32[]{:S(2)}) collective-permute-start(bf16[32,4096]{1,0:T(8,128)(2,1)S(1)} %get-tuple-element.40), channel_id=1, source_target_pairs={{3,0},{0,1},{1,2},{2,3},{7,4},{4,5},{5,6},{6,7},{11,8},{8,9},{9,10... | collective-permute-start | bytes 786440 | tf_op jit(solution)/shard_map/ppermute | solution.py:96
  48.2 19.4 %collective-permute-start.4 = (bf16[32,4096]{1,0:T(8,128)(2,1)S(1)}, bf16[32,4096]{1,0:T(8,128)(2,1)S(1)}, u32[]{:S(2)}, u32[]{:S(2)}) collective-permute-start(bf16[32,4096]{1,0:T(8,128)(2,1)S(1)} %get-tuple-element.39), channel_id=1, source_target_pairs={{2,0},{3,1},{0,2},{1,3},{6,4},{7,5},{4,6},{5,7},{10,8},{11,9},{8,1... | collective-permute-start | bytes 786440 | tf_op jit(solution)/shard_map/ppermute | solution.py:96
  50.1 19.0 %collective-permute-start.3 = (bf16[32,4096]{1,0:T(8,128)(2,1)S(1)}, bf16[32,4096]{1,0:T(8,128)(2,1)S(1)}, u32[]{:S(2)}, u32[]{:S(2)}) collective-permute-start(bf16[32,4096]{1,0:T(8,128)(2,1)S(1)} %get-tuple-element.38), channel_id=1, source_target_pairs={{1,0},{2,1},{3,2},{0,3},{5,4},{6,5},{7,6},{4,7},{9,8},{10,9},{11,1... | collective-permute-start | bytes 786440 | tf_op jit(solution)/shard_map/ppermute | solution.py:96
  53.1 63.0 %copy-start.11 = (bf16[4096,192]{0,1:T(8,128)(2,1)S(1)}, bf16[4096,192]{0,1:T(8,128)(2,1)}, u32[]{:S(2)}) copy-start(bf16[4096,192]{0,1:T(8,128)(2,1)} %param.35) | copy-start | bytes 4718596
  53.1 63.0 %copy-start.12 = (bf16[4096,192]{0,1:T(8,128)(2,1)S(1)}, bf16[4096,192]{0,1:T(8,128)(2,1)}, u32[]{:S(2)}) copy-start(bf16[4096,192]{0,1:T(8,128)(2,1)} %param.36) | copy-start | bytes 4718596
  58.4 33.7 %collective-permute-start.12 = (bf16[192,2048]{1,0:T(8,128)(2,1)S(1)}, bf16[192,2048]{1,0:T(8,128)(2,1)S(1)}, u32[]{:S(2)}, u32[]{:S(2)}) collective-permute-start(bf16[192,2048]{1,0:T(8,128)(2,1)S(1)} %get-tuple-element.67), channel_id=1, source_target_pairs={{0,8},{8,0},{1,9},{9,1},{2,10},{10,2},{3,11},{11,3},{4,12},{12,4},... | collective-permute-start | bytes 2359304 | tf_op jit(solution)/shard_map/ppermute | solution.py:92
  67.6 27.0 %collective-permute-start.16 = (bf16[192,2048]{1,0:T(8,128)(2,1)S(1)}, bf16[192,2048]{1,0:T(8,128)(2,1)S(1)}, u32[]{:S(2)}, u32[]{:S(2)}) collective-permute-start(bf16[192,2048]{1,0:T(8,128)(2,1)S(1)} %get-tuple-element.66), channel_id=1, source_target_pairs={{0,16},{16,0},{1,17},{17,1},{2,18},{18,2},{3,19},{19,3},{4,20},{20... | collective-permute-start | bytes 2359304 | tf_op jit(solution)/shard_map/ppermute | solution.py:92
  69.6 26.5 %collective-permute-start.7 = (bf16[32,4096]{1,0:T(8,128)(2,1)S(1)}, bf16[32,4096]{1,0:T(8,128)(2,1)S(1)}, u32[]{:S(2)}, u32[]{:S(2)}) collective-permute-start(bf16[32,4096]{1,0:T(8,128)(2,1)S(1)} %add_convert_fusion.1), channel_id=1, source_target_pairs={{1,0},{2,1},{3,2},{0,3},{5,4},{6,5},{7,6},{4,7},{9,8},{10,9},{11,1... | collective-permute-start | bytes 786440 | tf_op jit(solution)/shard_map/ppermute | solution.py:96
  77.4 20.3 %collective-permute-start.8 = (bf16[32,4096]{1,0:T(8,128)(2,1)S(1)}, bf16[32,4096]{1,0:T(8,128)(2,1)S(1)}, u32[]{:S(2)}, u32[]{:S(2)}) collective-permute-start(bf16[32,4096]{1,0:T(8,128)(2,1)S(1)} %add_convert_fusion.1), channel_id=1, source_target_pairs={{2,0},{3,1},{0,2},{1,3},{6,4},{7,5},{4,6},{5,7},{10,8},{11,9},{8,1... | collective-permute-start | bytes 786440 | tf_op jit(solution)/shard_map/ppermute | solution.py:96
  92.1 8.2 %collective-permute-start.9 = (bf16[32,4096]{1,0:T(8,128)(2,1)S(1)}, bf16[32,4096]{1,0:T(8,128)(2,1)S(1)}, u32[]{:S(2)}, u32[]{:S(2)}) collective-permute-start(bf16[32,4096]{1,0:T(8,128)(2,1)S(1)} %add_convert_fusion.1), channel_id=1, source_target_pairs={{3,0},{0,1},{1,2},{2,3},{7,4},{4,5},{5,6},{6,7},{11,8},{8,9},{9,10... | collective-permute-start | bytes 786440 | tf_op jit(solution)/shard_map/ppermute | solution.py:96
  94.6 6.7 %collective-permute-start.10 = (bf16[32,4096]{1,0:T(8,128)(2,1)S(1)}, bf16[32,4096]{1,0:T(8,128)(2,1)S(1)}, u32[]{:S(2)}, u32[]{:S(2)}) collective-permute-start(bf16[32,4096]{1,0:T(8,128)(2,1)S(1)} %add_convert_fusion.1), channel_id=1, source_target_pairs={{0,16},{16,0},{1,17},{17,1},{2,18},{18,2},{3,19},{19,3},{4,20},{20... | collective-permute-start | bytes 786440 | tf_op jit(solution)/shard_map/ppermute | solution.py:92
  96.1 21.7 %collective-permute-start.24 = (bf16[192,2048]{1,0:T(8,128)(2,1)S(1)}, bf16[192,2048]{1,0:T(8,128)(2,1)S(1)}, u32[]{:S(2)}, u32[]{:S(2)}) collective-permute-start(bf16[192,2048]{1,0:T(8,128)(2,1)S(1)} %get-tuple-element.67), channel_id=1, source_target_pairs={{0,4},{4,0},{1,5},{5,1},{2,6},{6,2},{3,7},{7,3},{8,12},{12,8},{9,1... | collective-permute-start | bytes 2359304 | tf_op jit(solution)/shard_map/ppermute | solution.py:92
  96.1 20.0 %collective-permute-start.17 = (bf16[192,2048]{1,0:T(8,128)(2,1)S(1)}, bf16[192,2048]{1,0:T(8,128)(2,1)S(1)}, u32[]{:S(2)}, u32[]{:S(2)}) collective-permute-start(bf16[192,2048]{1,0:T(8,128)(2,1)S(1)} %collective-permute-done.16), channel_id=1, source_target_pairs={{0,8},{8,0},{1,9},{9,1},{2,10},{10,2},{3,11},{11,3},{4,12},{12,4},... | collective-permute-start | bytes 2359304 | tf_op jit(solution)/shard_map/ppermute | solution.py:92
  101.3 14.8 %collective-permute-start.13 = (bf16[32,4096]{1,0:T(8,128)(2,1)S(1)}, bf16[32,4096]{1,0:T(8,128)(2,1)S(1)}, u32[]{:S(2)}, u32[]{:S(2)}) collective-permute-start(bf16[32,4096]{1,0:T(8,128)(2,1)S(1)} %collective-permute-done.7), channel_id=1, source_target_pairs={{0,16},{16,0},{1,17},{17,1},{2,18},{18,2},{3,19},{19,3},{4,20},{20... | collective-permute-start | bytes 786440 | tf_op jit(solution)/shard_map/ppermute | solution.py:92
  102.9 13.7 %collective-permute-start.14 = (bf16[32,4096]{1,0:T(8,128)(2,1)S(1)}, bf16[32,4096]{1,0:T(8,128)(2,1)S(1)}, u32[]{:S(2)}, u32[]{:S(2)}) collective-permute-start(bf16[32,4096]{1,0:T(8,128)(2,1)S(1)} %collective-permute-done.8), channel_id=1, source_target_pairs={{0,16},{16,0},{1,17},{17,1},{2,18},{18,2},{3,19},{19,3},{4,20},{20... | collective-permute-start | bytes 786440 | tf_op jit(solution)/shard_map/ppermute | solution.py:92
  103.5 14.3 %collective-permute-start.15 = (bf16[32,4096]{1,0:T(8,128)(2,1)S(1)}, bf16[32,4096]{1,0:T(8,128)(2,1)S(1)}, u32[]{:S(2)}, u32[]{:S(2)}) collective-permute-start(bf16[32,4096]{1,0:T(8,128)(2,1)S(1)} %collective-permute-done.9), channel_id=1, source_target_pairs={{0,16},{16,0},{1,17},{17,1},{2,18},{18,2},{3,19},{19,3},{4,20},{20... | collective-permute-start | bytes 786440 | tf_op jit(solution)/shard_map/ppermute | solution.py:92
  116.1 11.8 %collective-permute-start.18 = (bf16[192,4096]{1,0:T(8,128)(2,1)S(1)}, bf16[192,4096]{1,0:T(8,128)(2,1)S(1)}, u32[]{:S(2)}, u32[]{:S(2)}) collective-permute-start(bf16[192,4096]{1,0:T(8,128)(2,1)S(1)} %bitcast.17), channel_id=1, source_target_pairs={{0,4},{4,0},{1,5},{5,1},{2,6},{6,2},{3,7},{7,3},{8,12},{12,8},{9,1... | collective-permute-start | bytes 4718600 | tf_op jit(solution)/shard_map/ppermute | solution.py:92
  116.1 15.4 %collective-permute-start.20 = (bf16[192,4096]{1,0:T(8,128)(2,1)S(1)}, bf16[192,4096]{1,0:T(8,128)(2,1)S(1)}, u32[]{:S(2)}, u32[]{:S(2)}) collective-permute-start(bf16[192,4096]{1,0:T(8,128)(2,1)S(1)} %bitcast.20), channel_id=1, source_target_pairs={{0,4},{4,0},{1,5},{5,1},{2,6},{6,2},{3,7},{7,3},{8,12},{12,8},{9,1... | collective-permute-start | bytes 4718600 | tf_op jit(solution)/shard_map/ppermute | solution.py:92
  116.6 11.8 %collective-permute-start.19 = (bf16[192,4096]{1,0:T(8,128)(2,1)}, bf16[192,4096]{1,0:T(8,128)(2,1)S(1)}, u32[]{:S(2)}, u32[]{:S(2)}) collective-permute-start(bf16[192,4096]{1,0:T(8,128)(2,1)} %collective-permute-done.6), channel_id=1, source_target_pairs={{0,4},{4,0},{1,5},{5,1},{2,6},{6,2},{3,7},{7,3},{8,12},{12,8},{9,1... | collective-permute-start | bytes 4718600 | tf_op jit(solution)/shard_map/ppermute | solution.py:92
  117.8 13.7 %collective-permute-start.21 = (bf16[192,4096]{1,0:T(8,128)(2,1)S(1)}, bf16[192,4096]{1,0:T(8,128)(2,1)S(1)}, u32[]{:S(2)}, u32[]{:S(2)}) collective-permute-start(bf16[192,4096]{1,0:T(8,128)(2,1)S(1)} %collective-permute-done.11), channel_id=1, source_target_pairs={{0,4},{4,0},{1,5},{5,1},{2,6},{6,2},{3,7},{7,3},{8,12},{12,8},{9,1... | collective-permute-start | bytes 4718600 | tf_op jit(solution)/shard_map/ppermute | solution.py:92
  117.9 9.5 %collective-permute-start.25 = (bf16[192,2048]{1,0:T(8,128)(2,1)S(1)}, bf16[192,2048]{1,0:T(8,128)(2,1)S(1)}, u32[]{:S(2)}, u32[]{:S(2)}) collective-permute-start(bf16[192,2048]{1,0:T(8,128)(2,1)S(1)} %collective-permute-done.12), channel_id=1, source_target_pairs={{0,4},{4,0},{1,5},{5,1},{2,6},{6,2},{3,7},{7,3},{8,12},{12,8},{9,1... | collective-permute-start | bytes 2359304 | tf_op jit(solution)/shard_map/ppermute | solution.py:92
  127.4 11.2 %collective-permute-start.26 = (bf16[192,2048]{1,0:T(8,128)(2,1)S(1)}, bf16[192,2048]{1,0:T(8,128)(2,1)S(1)}, u32[]{:S(2)}, u32[]{:S(2)}) collective-permute-start(bf16[192,2048]{1,0:T(8,128)(2,1)S(1)} %collective-permute-done.16), channel_id=1, source_target_pairs={{0,4},{4,0},{1,5},{5,1},{2,6},{6,2},{3,7},{7,3},{8,12},{12,8},{9,1... | collective-permute-start | bytes 2359304 | tf_op jit(solution)/shard_map/ppermute | solution.py:92
  127.9 10.6 %collective-permute-start.27 = (bf16[192,2048]{1,0:T(8,128)(2,1)S(1)}, bf16[192,2048]{1,0:T(8,128)(2,1)S(1)}, u32[]{:S(2)}, u32[]{:S(2)}) collective-permute-start(bf16[192,2048]{1,0:T(8,128)(2,1)S(1)} %collective-permute-done.17), channel_id=1, source_target_pairs={{0,4},{4,0},{1,5},{5,1},{2,6},{6,2},{3,7},{7,3},{8,12},{12,8},{9,1... | collective-permute-start | bytes 2359304 | tf_op jit(solution)/shard_map/ppermute | solution.py:92
  136.5 7.8 %collective-permute-start.22 = (bf16[128,768]{1,0:T(8,128)(2,1)S(1)}, bf16[128,768]{1,0:T(8,128)(2,1)S(1)}, u32[]{:S(2)}, u32[]{:S(2)}) collective-permute-start(bf16[128,768]{1,0:T(8,128)(2,1)S(1)} %get-tuple-element.54.other), channel_id=1, source_target_pairs={{0,16},{16,0},{1,17},{17,1},{2,18},{18,2},{3,19},{19,3},{4,20},{20... | collective-permute-start | bytes 589832 | tf_op jit(solution)/shard_map/ppermute | solution.py:92
  137.1 10.7 %collective-permute-start.23 = (bf16[128,768]{1,0:T(8,128)(2,1)S(1)}, bf16[128,768]{1,0:T(8,128)(2,1)S(1)}, u32[]{:S(2)}, u32[]{:S(2)}) collective-permute-start(bf16[128,768]{1,0:T(8,128)(2,1)S(1)} %get-tuple-element.53.own), channel_id=1, source_target_pairs={{0,16},{16,0},{1,17},{17,1},{2,18},{18,2},{3,19},{19,3},{4,20},{20... | collective-permute-start | bytes 589832 | tf_op jit(solution)/shard_map/ppermute | solution.py:92
  149.6 26.2 %copy-start.15 = (f32[4096]{0:T(1024)S(1)}, f32[4096]{0:T(1024)}, u32[]{:S(2)}) copy-start(f32[4096]{0:T(1024)} %param.34) | copy-start | bytes 49156
  149.6 11.2 %collective-permute-start.30 = (bf16[64,2048]{1,0:T(8,128)(2,1)S(1)}, bf16[64,2048]{1,0:T(8,128)(2,1)S(1)}, u32[]{:S(2)}, u32[]{:S(2)}) collective-permute-start(bf16[64,2048]{1,0:T(8,128)(2,1)S(1)} %get-tuple-element.60), channel_id=1, source_target_pairs={{3,0},{0,1},{1,2},{2,3},{7,4},{4,5},{5,6},{6,7},{11,8},{8,9},{9,10... | collective-permute-start | bytes 786440 | tf_op jit(solution)/shard_map/ppermute | solution.py:96
  149.9 20.5 %collective-permute-start.29 = (bf16[64,2048]{1,0:T(8,128)(2,1)S(1)}, bf16[64,2048]{1,0:T(8,128)(2,1)S(1)}, u32[]{:S(2)}, u32[]{:S(2)}) collective-permute-start(bf16[64,2048]{1,0:T(8,128)(2,1)S(1)} %get-tuple-element.59), channel_id=1, source_target_pairs={{2,0},{3,1},{0,2},{1,3},{6,4},{7,5},{4,6},{5,7},{10,8},{11,9},{8,1... | collective-permute-start | bytes 786440 | tf_op jit(solution)/shard_map/ppermute | solution.py:96
  151.5 18.8 %collective-permute-start.28 = (bf16[64,2048]{1,0:T(8,128)(2,1)S(1)}, bf16[64,2048]{1,0:T(8,128)(2,1)S(1)}, u32[]{:S(2)}, u32[]{:S(2)}) collective-permute-start(bf16[64,2048]{1,0:T(8,128)(2,1)S(1)} %get-tuple-element.58), channel_id=1, source_target_pairs={{1,0},{2,1},{3,2},{0,3},{5,4},{6,5},{7,6},{4,7},{9,8},{10,9},{11,1... | collective-permute-start | bytes 786440 | tf_op jit(solution)/shard_map/ppermute | solution.py:96
  170.5 5.0 %collective-permute-start.31 = (bf16[32,2048]{1,0:T(8,128)(2,1)S(1)}, bf16[32,2048]{1,0:T(8,128)(2,1)S(1)}, u32[]{:S(2)}, u32[]{:S(2)}) collective-permute-start(bf16[32,2048]{1,0:T(8,128)(2,1)S(1)} %slice.14), channel_id=1, source_target_pairs={{0,16},{16,0},{1,17},{17,1},{2,18},{18,2},{3,19},{19,3},{4,20},{20... | collective-permute-start | bytes 393224 | tf_op jit(solution)/shard_map/ppermute | solution.py:92

commit v6 on v5

--- a/solution.py
+++ b/solution.py
@@ -111,12 +111,8 @@
     return lax.optimization_barrier(values)
 
 
-def both_cores(rows, rows_x):
-    return jnp.concatenate([rows, exchange(rows, "core"), rows_x, exchange(rows_x, "core")])
-
-
-def in_vmem(*arrays):
-    return [pltpu.with_memory_space_constraint(array, pltpu.VMEM) for array in arrays]
+def four_pieces(rows, rows_x, place=lambda rows: rows):
+    return [place(rows), exchange(rows, "core"), rows_x, exchange(rows_x, "core")]
 
 
 def vmem_call(kernel, outs, scratch, operands, vmem_mib):
@@ -130,6 +126,40 @@
         compiler_params=pltpu.CompilerParams(vmem_limit_bytes=vmem_mib << 20),
         cost_estimate=pl.CostEstimate(flops=1 << 20, bytes_accessed=1 << 20, transcendentals=0),
     )(*operands)
+
+
+def in_hbm(array):
+    return pltpu.with_memory_space_constraint(array, pltpu.HBM)
+
+
+def staged(*groups):
+    arrays = [array for group in groups for array in group]
+
+    def kernel(*refs):
+        sources, targets, sems = refs[: len(arrays)], refs[len(arrays) : -1], refs[-1]
+        copies = []
+        for group, target in zip(groups, targets):
+            start = 0
+            for array in group:
+                at = len(copies)
+                rows = target.at[pl.ds(start, array.shape[0]), :]
+                copies.append(pltpu.make_async_copy(sources[at], rows, sems.at[at]))
+                copies[-1].start()
+                start += array.shape[0]
+        for copy in copies:
+            copy.wait()
+
+    outs = [(sum(array.shape[0] for array in group), group[0].shape[1]) for group in groups]
+    size = sum(array.size * array.dtype.itemsize for array in arrays)
+    return pl.pallas_call(
+        kernel,
+        out_shape=[pltpu.VMEM(shape, group[0].dtype) for shape, group in zip(outs, groups)],
+        in_specs=[pl.BlockSpec(memory_space=pl.ANY)] * len(arrays),
+        out_specs=[pl.BlockSpec(memory_space=pltpu.VMEM)] * len(groups),
+        scratch_shapes=[pltpu.SemaphoreType.DMA((len(arrays),))],
+        compiler_params=pltpu.CompilerParams(vmem_limit_bytes=1 << 20),
+        cost_estimate=pl.CostEstimate(flops=0, bytes_accessed=2 * size, transcendentals=0),
+    )(*arrays)
 
 
 NT = (((1,), (1,)), ((), ()))
@@ -250,6 +280,9 @@
     gate_x, up_x = exchange(gate_rows, "x"), exchange(up_rows, "x")
     cosine, sine = jnp.cos(angles), jnp.sin(angles)
     block = jax.ShapeDtypeStruct((tok_dev, width), jnp.bfloat16)
+    *staged_rows, own_block = staged(
+        *([in_hbm(array)] for array in (*projections, *adapters, *head_gains, layer_input))
+    )
     parts = vmem_call(
         attention_kernel,
         [block] * 4,
@@ -258,48 +291,49 @@
             pltpu.VMEM((4 * tok_dev, projections[0].shape[1]), jnp.bfloat16),
         ],
         [
-            *line_gather(layer_input),
-            *in_vmem(*projections, *adapters[:2]),
-            *adapters[2:],
-            *head_gains,
+            own_block,
+            *line_gather(layer_input)[1:],
+            *staged_rows,
             jnp.concatenate([cosine, cosine], axis=1),
             jnp.concatenate([-sine, sine], axis=1),
             slot_mask,
             allowed,
         ],
-        24,
+        8,
     )
     *parts, down_rows = together(*parts, down_rows)
     near = lax.dynamic_slice_in_dim(down_rows, y * half, half, axis=1)
     far = exchange(lax.dynamic_slice_in_dim(down_rows, (1 - y) * half, half, axis=1), "y")
     near_x, far_x = exchange(near, "x"), exchange(far, "x")
-    attn_own, gate_x = together(line_scatter(parts), gate_x)
+    attn_own, gate_x, near, far = together(line_scatter(parts), gate_x, near, far)
     residual_own = add_normed(layer_input, attn_own, gains[0])
-    *line, other, up_x, near_x = together(
-        *line_gather(residual_own), exchange(residual_own, "y"), up_x, near_x
-    )
-    *others, far_x = together(*[exchange(rows, "y") for rows in line[1:]], far_x)
-    states = jnp.concatenate([*line, other, *others])
+    *line, other = together(*line_gather(residual_own), exchange(residual_own, "y"))
+    *line, gate_x, up_x, near_x = together(*line, gate_x, up_x, near_x)
+    (gate_all,) = staged(four_pieces(gate_rows, gate_x, in_hbm))
+    (up_all,) = staged(four_pieces(up_rows, up_x, in_hbm))
+    *others, gate_all, up_all, far_x = together(
+        *[exchange(rows, "y") for rows in line[1:]], gate_all, up_all, far_x
+    )
     group = jax.ShapeDtypeStruct((4 * tok_dev, 4 * gate_rows.shape[0]), jnp.bfloat16)
     hidden_own, hidden_other = vmem_call(
         hidden_kernel,
         [group] * 2,
         [],
-        [states, *in_vmem(both_cores(gate_rows, gate_x), both_cores(up_rows, up_x))],
-        24,
+        [jnp.concatenate([*line, other, *others]), gate_all, up_all],
+        8,
+    )
+    hidden_own, hidden_other, near_x, far_x = together(hidden_own, hidden_other, near_x, far_x)
+    (near_all,) = staged(four_pieces(near, near_x))
+    (far_all,) = staged(four_pieces(far, far_x))
+    from_other, from_own, near_all, far_all = together(
+        exchange(hidden_other, "y"), exchange(hidden_own, "y"), near_all, far_all
     )
     parts = vmem_call(
         down_kernel,
         [jax.ShapeDtypeStruct((2 * tok_dev, half), jnp.bfloat16)] * 4,
         [],
-        [
-            hidden_own,
-            hidden_other,
-            exchange(hidden_other, "y"),
-            exchange(hidden_own, "y"),
-            *in_vmem(both_cores(near, near_x), both_cores(far, far_x)),
-        ],
-        24,
+        [hidden_own, hidden_other, from_other, from_own, near_all, far_all],
+        8,
     )
     summed = line_scatter(parts)
     own_half = summed[:tok_dev]

time: 179 us -> 165 us (0.922); the launches traced: 177 us -> 165 us
  local copies, waits for them, and re-layouts: 15.6 us -> 0.34 us
  Pallas kernels: 9.64 us -> 20.8 us
  waiting for transfers between devices: 97.9 us -> 90.4 us
  other arithmetic: 10.6 us -> 5.67 us
  starting transfers between devices: 42.6 us -> 47.2 us
    ppermute x20, waiting for transfers between devices: 49.8 us -> 31 us  [exchange(): return lax.ppermute(block, axis, [(0, 1), (1, 0)])]
    unnamed x39 -> x21, local copies, waits for them, and re-layouts: 15.5 us -> 0.17 us
    ppermute x12, waiting for transfers between devices: 48.1 us -> 59.4 us  [shift(): return lax.ppermute(block, 'mlp', [((k + hops) % 4, k) for k in range(4)])]
    pallas_call x0 -> x5, Pallas kernels: none -> 9.99 us  [staged(): pl.pallas_call(kernel, out_shape=[pltpu.VMEM(shape, group[0].dtype) for s...]
    ppermute x12, starting transfers between devices: 26.3 us -> 31.7 us  [shift(): return lax.ppermute(block, 'mlp', [((k + hops) % 4, k) for k in range(4)])]
    concatenate x4 -> x0, other arithmetic: 5.42 us -> none  [both_cores(): jnp.concatenate([rows, exchange(rows, 'core'), rows_x, exchange(rows_x, '...]
  transfers between devices with their start and end apart: 32 -> 32, of which waited for: 15 -> 17; matrix products, arithmetic and copies ran while one was open for 5% -> 3% of each run, Pallas kernels for 4% -> 12%
where the time goes in v6:
time: 165 us
  waiting for transfers between devices  90.4 us (55%)
  starting transfers between devices  47.2 us (29%)
  Pallas kernels  20.8 us (13%)
  other arithmetic  5.67 us (3%)
    ppermute x12, waiting for transfers between devices, shift(): return lax.ppermute(block, 'mlp', [((k + hops) % 4, k) for k in range(4)])  59.4 us
    ppermute x12, starting transfers between devices, shift(): return lax.ppermute(block, 'mlp', [((k + hops) % 4, k) for k in range(4)])  31.7 us
    ppermute x20, waiting for transfers between devices, exchange(): return lax.ppermute(block, axis, [(0, 1), (1, 0)])  31 us
    ppermute x20, starting transfers between devices, exchange(): return lax.ppermute(block, axis, [(0, 1), (1, 0)])  15.5 us
    pallas_call x3, Pallas kernels, vmem_call(): pl.pallas_call(kernel, out_shape=outs, in_specs=[whole] * len(operands),...  10.8 us
    pallas_call x5, Pallas kernels, staged(): pl.pallas_call(kernel, out_shape=[pltpu.VMEM(shape, group[0].dtype) for s...  9.99 us
  transfers between devices with their start and end apart: 32, of which 17 were waited for; matrix products, arithmetic and copies ran while one was open for 3% of the time, Pallas kernels for 12%

profile of v6, /device:TPU:0, one launch (start us, length us, event | category | flops | bytes accessed | tf_op | source)
XLA Modules:
  0.0 164.8 jit_solution(11799573831291296254)
XLA Ops:
  0.0 5.0 %collective-permute-start = (bf16[32,4096]{1,0:T(8,128)(2,1)}, bf16[32,4096]{1,0:T(8,128)(2,1)S(1)}, u32[]{:S(2)}, u32[]{:S(2)}) collective-permute-start(bf16[32,4096]{1,0:T(8,128)(2,1)} %refs_10_.1), channel_id=1, source_target_pairs={{1,0},{2,1},{3,2},{0,3},{5,4},{6,5},{7,6},{4,7},{9,8},{10,9},{11,1... | collective-permute-start | bytes 786440 | tf_op jit(solution)/shard_map/ppermute | solution.py:96
  5.1 1.0 collective-permute-start.2
  6.1 1.5 collective-permute-start.6
  7.6 0.5 collective-permute-start.12
  8.1 0.8 reduce-window.4
  8.9 0.7 fusion.6
  9.6 0.7 select_reduce_fusion.1
  10.8 0.7 select_reduce_fusion
  11.5 0.5 and_select_fusion
  12.0 6.6 %shard_map.181 = (bf16[4096,512]{1,0:T(8,128)(2,1)S(1)}, bf16[4096,512]{1,0:T(8,128)(2,1)S(1)}, bf16[4096,512]{1,0:T(8,128)(2,1)S(1)}, bf16[512,4096]{1,0:T(8,12...) custom-call(bf16[4096,512]{1,0:T(8,128)(2,1)} %refs_0_.1, ...), custom_call_target="tpu_custom_call" | custom-call | bytes 38805504 | tf_op jit(solution)/shard_map/pallas_call | solution.py:154
  18.8 8.9 %collective-permute-done.1.block_2 = bf16[32,4096]{1,0:T(8,128)(2,1)} collective-permute-done((bf16[32,4096]{1,0:T(8,128)(2,1)}, bf16[32,4096]{1,0:T(8,128)(2,1)}, u32[]{:S(2)}, u32[]{:S(2)}) %collective-permute-start.1) | collective-permute-done | bytes 262176 | tf_op jit(solution)/shard_map/ppermute | solution.py:96
  27.7 5.5 %shard_map.182 = (bf16[32,4096]{1,0:T(8,128)(2,1)S(1)}, bf16[32,4096]{1,0:T(8,128)(2,1)S(1)}, bf16[32,4096]{1,0:T(8,128)(2,1)S(1)}, bf16[32,4096]{1,0:T(8,128)(2,1)S(1)}) custom-call(bf16[32,4096]{1,0:T(8,128)(2,1)S(1)} %get-tuple-element.61.block_0, bf16[32,4096]{1,0:T(8,128)(2,1)S(1)} %collective-permute-done.block_1, ...), custom_call_target="tpu_custom_call" | custom-call | flops 1048576 | bytes 1048576 | tf_op jit(solution)/shard_map/pallas_call | solution.py:120
  33.2 2.9 %collective-permute-start.4 = (bf16[32,4096]{1,0:T(8,128)(2,1)S(1)}, bf16[32,4096]{1,0:T(8,128)(2,1)S(1)}, u32[]{:S(2)}, u32[]{:S(2)}) collective-permute-start(bf16[32,4096]{1,0:T(8,128)(2,1)S(1)} %get-tuple-element.78), channel_id=1, source_target_pairs={{2,0},{3,1},{0,2},{1,3},{6,4},{7,5},{4,6},{5,7},{10,8},{11,9},{8,1... | collective-permute-start | bytes 786440 | tf_op jit(solution)/shard_map/ppermute | solution.py:96
  36.1 1.9 %collective-permute-start.5 = (bf16[32,4096]{1,0:T(8,128)(2,1)S(1)}, bf16[32,4096]{1,0:T(8,128)(2,1)S(1)}, u32[]{:S(2)}, u32[]{:S(2)}) collective-permute-start(bf16[32,4096]{1,0:T(8,128)(2,1)S(1)} %get-tuple-element.79), channel_id=1, source_target_pairs={{3,0},{0,1},{1,2},{2,3},{7,4},{4,5},{5,6},{6,7},{11,8},{8,9},{9,10... | collective-permute-start | bytes 786440 | tf_op jit(solution)/shard_map/ppermute | solution.py:96
  38.2 2.4 %collective-permute-done.3 = bf16[32,4096]{1,0:T(8,128)(2,1)S(1)} collective-permute-done((bf16[32,4096]{1,0:T(8,128)(2,1)S(1)}, bf16[32,4096]{1,0:T(8,128)(2,1)S(1)}, u32[]{:S(2)}, u32[]{:S(2)}) %collective-permute-start.3) | collective-permute-done | bytes 262176 | tf_op jit(solution)/shard_map/ppermute | solution.py:96
  40.6 1.5 collective-permute-start.7
  42.1 16.5 %collective-permute-done.4 = bf16[32,4096]{1,0:T(8,128)(2,1)S(1)} collective-permute-done((bf16[32,4096]{1,0:T(8,128)(2,1)S(1)}, bf16[32,4096]{1,0:T(8,128)(2,1)S(1)}, u32[]{:S(2)}, u32[]{:S(2)}) %collective-permute-start.4) | collective-permute-done | bytes 262176 | tf_op jit(solution)/shard_map/ppermute | solution.py:96
  58.6 1.5 collective-permute-start.13
  60.6 9.7 %collective-permute-start.10 = (bf16[32,4096]{1,0:T(8,128)(2,1)S(1)}, bf16[32,4096]{1,0:T(8,128)(2,1)S(1)}, u32[]{:S(2)}, u32[]{:S(2)}) collective-permute-start(bf16[32,4096]{1,0:T(8,128)(2,1)S(1)} %add_convert_fusion.1), channel_id=1, source_target_pairs={{3,0},{0,1},{1,2},{2,3},{7,4},{4,5},{5,6},{6,7},{11,8},{8,9},{9,10... | collective-permute-start | bytes 786440 | tf_op jit(solution)/shard_map/ppermute | solution.py:96
  70.2 1.5 collective-permute-start.11
  71.8 2.4 %collective-permute-done.10 = bf16[32,4096]{1,0:T(8,128)(2,1)S(1)} collective-permute-done((bf16[32,4096]{1,0:T(8,128)(2,1)S(1)}, bf16[32,4096]{1,0:T(8,128)(2,1)S(1)}, u32[]{:S(2)}, u32[]{:S(2)}) %collective-permute-start.10) | collective-permute-done | bytes 262176 | tf_op jit(solution)/shard_map/ppermute | solution.py:96
  74.1 7.1 %collective-permute-start.9 = (bf16[32,4096]{1,0:T(8,128)(2,1)S(1)}, bf16[32,4096]{1,0:T(8,128)(2,1)S(1)}, u32[]{:S(2)}, u32[]{:S(2)}) collective-permute-start(bf16[32,4096]{1,0:T(8,128)(2,1)S(1)} %add_convert_fusion.1), channel_id=1, source_target_pairs={{2,0},{3,1},{0,2},{1,3},{6,4},{7,5},{4,6},{5,7},{10,8},{11,9},{8,1... | collective-permute-start | bytes 786440 | tf_op jit(solution)/shard_map/ppermute | solution.py:96
  81.8 6.6 %collective-permute-done.9 = bf16[32,4096]{1,0:T(8,128)(2,1)S(1)} collective-permute-done((bf16[32,4096]{1,0:T(8,128)(2,1)S(1)}, bf16[32,4096]{1,0:T(8,128)(2,1)S(1)}, u32[]{:S(2)}, u32[]{:S(2)}) %collective-permute-start.9) | collective-permute-done | bytes 262176 | tf_op jit(solution)/shard_map/ppermute | solution.py:96
  88.4 5.8 %collective-permute-done.13.refs_2_ = bf16[192,2048]{1,0:T(8,128)(2,1)S(1)} collective-permute-done((bf16[192,2048]{1,0:T(8,128)(2,1)S(1)}, bf16[192,2048]{1,0:T(8,128)(2,1)S(1)}, u32[]{:S(2)}, u32[]{:S(2)}) %collective-permute-start.13) | collective-permute-done | bytes 786464 | tf_op jit(solution)/shard_map/ppermute | solution.py:92
  94.2 0.5 collective-permute-start.18
  94.8 1.6 collective-permute-start.14
  96.9 0.7 collective-permute-done.20.refs_3_
  97.6 1.5 collective-permute-start.16
  99.1 1.5 shard_map.184.up_rows
  100.7 1.5 shard_map.183.gate_rows
  102.1 6.8 %collective-permute-done.21.refs_2_ = bf16[192,2048]{1,0:T(8,128)(2,1)S(1)} collective-permute-done((bf16[192,2048]{1,0:T(8,128)(2,1)S(1)}, bf16[192,2048]{1,0:T(8,128)(2,1)S(1)}, u32[]{:S(2)}, u32[]{:S(2)}) %collective-permute-start.21) | collective-permute-done | bytes 786464 | tf_op jit(solution)/shard_map/ppermute | solution.py:92
  109.0 0.7 collective-permute-done.15
  109.7 4.7 %collective-permute-done.16 = bf16[32,4096]{1,0:T(8,128)(2,1)S(1)} collective-permute-done((bf16[32,4096]{1,0:T(8,128)(2,1)S(1)}, bf16[32,4096]{1,0:T(8,128)(2,1)S(1)}, u32[]{:S(2)}, u32[]{:S(2)}) %collective-permute-start.16) | collective-permute-done | bytes 262176 | tf_op jit(solution)/shard_map/ppermute | solution.py:92
  114.4 3.5 %shard_map.185 = (bf16[128,768]{1,0:T(8,128)(2,1)S(1)}, bf16[128,768]{1,0:T(8,128)(2,1)S(1)}) custom-call(bf16[256,4096]{1,0:T(8,128)(2,1)S(1)} %constant_dynamic-update-slice_fusion.states, bf16[768,4096]{1,0:T(8,128)(2,1)S(1)} %shard_map.183.gate_rows, bf16[768,4096]{1,0:T(8,128)(2,1)S(1)} %shard_map.184.up_rows), custom_call_target="tpu_custom_call" | custom-call | flops 1048576 | bytes 1048576 | tf_op jit(solution)/shard_map/pallas_call | solution.py:120
  118.6 1.5 collective-permute-start.22
  120.1 0.5 collective-permute-start.23
  120.9 0.5 collective-permute-done.24.refs_1_
  121.4 1.1 collective-permute-done.25.refs_3_
  122.8 3.5 %collective-permute-done.22.far_own = bf16[128,768]{1,0:T(8,128)(2,1)S(1)} collective-permute-done((bf16[128,768]{1,0:T(8,128)(2,1)S(1)}, bf16[128,768]{1,0:T(8,128)(2,1)S(1)}, u32[]{:S(2)}, u32[]{:S(2)}) %collective-permute-start.22) | collective-permute-done | bytes 196640 | tf_op jit(solution)/shard_map/ppermute | solution.py:92
  126.3 3.8 %collective-permute-done.23.far_other = bf16[128,768]{1,0:T(8,128)(2,1)S(1)} collective-permute-done((bf16[128,768]{1,0:T(8,128)(2,1)S(1)}, bf16[128,768]{1,0:T(8,128)(2,1)S(1)}, u32[]{:S(2)}, u32[]{:S(2)}) %collective-permute-start.23) | collective-permute-done | bytes 196640 | tf_op jit(solution)/shard_map/ppermute | solution.py:92
  130.0 1.8 %shard_map.188 = (bf16[64,2048]{1,0:T(8,128)(2,1)S(1)}, bf16[64,2048]{1,0:T(8,128)(2,1)S(1)}, bf16[64,2048]{1,0:T(8,128)(2,1)S(1)}, bf16[64,2048]{1,0:T(8,128)(2,1)S(1)}) custom-call(bf16[128,768]{1,0:T(8,128)(2,1)S(1)} %get-tuple-element.103.own, bf16[128,768]{1,0:T(8,128)(2,1)S(1)} %get-tuple-element.104.other, ...), custom_call_target="tpu_custom_call" | custom-call | flops 1048576 | bytes 1048576 | tf_op jit(solution)/shard_map/pallas_call | solution.py:120
  131.9 2.9 %collective-permute-start.28 = (bf16[64,2048]{1,0:T(8,128)(2,1)S(1)}, bf16[64,2048]{1,0:T(8,128)(2,1)S(1)}, u32[]{:S(2)}, u32[]{:S(2)}) collective-permute-start(bf16[64,2048]{1,0:T(8,128)(2,1)S(1)} %get-tuple-element.114), channel_id=1, source_target_pairs={{1,0},{2,1},{3,2},{0,3},{5,4},{6,5},{7,6},{4,7},{9,8},{10,9},{11,1... | collective-permute-start | bytes 786440 | tf_op jit(solution)/shard_map/ppermute | solution.py:96
  134.7 1.1 collective-permute-start.29
  135.8 5.7 %collective-permute-done.28 = bf16[64,2048]{1,0:T(8,128)(2,1)S(1)} collective-permute-done((bf16[64,2048]{1,0:T(8,128)(2,1)S(1)}, bf16[64,2048]{1,0:T(8,128)(2,1)S(1)}, u32[]{:S(2)}, u32[]{:S(2)}) %collective-permute-start.28) | collective-permute-done | bytes 262176 | tf_op jit(solution)/shard_map/ppermute | solution.py:96
  141.5 17.0 %collective-permute-done.29 = bf16[64,2048]{1,0:T(8,128)(2,1)S(1)} collective-permute-done((bf16[64,2048]{1,0:T(8,128)(2,1)S(1)}, bf16[64,2048]{1,0:T(8,128)(2,1)S(1)}, u32[]{:S(2)}, u32[]{:S(2)}) %collective-permute-start.29) | collective-permute-done | bytes 262176 | tf_op jit(solution)/shard_map/ppermute | solution.py:96
  158.7 1.6 collective-permute-start.31
  160.3 3.4 %collective-permute-done.31 = bf16[32,2048]{1,0:T(8,128)(2,1)S(1)} collective-permute-done((bf16[32,2048]{1,0:T(8,128)(2,1)S(1)}, bf16[32,2048]{1,0:T(8,128)(2,1)S(1)}, u32[]{:S(2)}, u32[]{:S(2)}) %collective-permute-start.31) | collective-permute-done | bytes 131104 | tf_op jit(solution)/shard_map/ppermute | solution.py:92
  163.9 0.9 add_convert_fusion
  (69 shorter events, 4.0 us)
Async XLA Ops:
  0.0 18.8 %collective-permute-start = (bf16[32,4096]{1,0:T(8,128)(2,1)}, bf16[32,4096]{1,0:T(8,128)(2,1)S(1)}, u32[]{:S(2)}, u32[]{:S(2)}) collective-permute-start(bf16[32,4096]{1,0:T(8,128)(2,1)} %refs_10_.1), channel_id=1, source_target_pairs={{1,0},{2,1},{3,2},{0,3},{5,4},{6,5},{7,6},{4,7},{9,8},{10,9},{11,1... | collective-permute-start | bytes 786440 | tf_op jit(solution)/shard_map/ppermute | solution.py:96
  5.0 22.6 %collective-permute-start.1 = (bf16[32,4096]{1,0:T(8,128)(2,1)}, bf16[32,4096]{1,0:T(8,128)(2,1)}, u32[]{:S(2)}, u32[]{:S(2)}) collective-permute-start(bf16[32,4096]{1,0:T(8,128)(2,1)} %refs_10_.1), channel_id=1, source_target_pairs={{2,0},{3,1},{0,2},{1,3},{6,4},{7,5},{4,6},{5,7},{10,8},{11,9},{8,1... | collective-permute-start | bytes 786440 | tf_op jit(solution)/shard_map/ppermute | solution.py:96
  5.1 22.6 %collective-permute-start.2 = (bf16[32,4096]{1,0:T(8,128)(2,1)}, bf16[32,4096]{1,0:T(8,128)(2,1)}, u32[]{:S(2)}, u32[]{:S(2)}) collective-permute-start(bf16[32,4096]{1,0:T(8,128)(2,1)} %refs_10_.1), channel_id=1, source_target_pairs={{3,0},{0,1},{1,2},{2,3},{7,4},{4,5},{5,6},{6,7},{11,8},{8,9},{9,10... | collective-permute-start | bytes 786440 | tf_op jit(solution)/shard_map/ppermute | solution.py:96
  6.1 54.2 %collective-permute-start.6 = (bf16[192,4096]{1,0:T(8,128)(2,1)}, bf16[192,4096]{1,0:T(8,128)(2,1)S(1)}, u32[]{:S(2)}, u32[]{:S(2)}) collective-permute-start(bf16[192,4096]{1,0:T(8,128)(2,1)} %bitcast.17), channel_id=1, source_target_pairs={{0,8},{8,0},{1,9},{9,1},{2,10},{10,2},{3,11},{11,3},{4,12},{12,4},... | collective-permute-start | bytes 4718600 | tf_op jit(solution)/shard_map/ppermute | solution.py:92
  7.6 86.6 %collective-permute-start.12 = (bf16[192,4096]{1,0:T(8,128)(2,1)}, bf16[192,4096]{1,0:T(8,128)(2,1)S(1)}, u32[]{:S(2)}, u32[]{:S(2)}) collective-permute-start(bf16[192,4096]{1,0:T(8,128)(2,1)} %bitcast.14), channel_id=1, source_target_pairs={{0,8},{8,0},{1,9},{9,1},{2,10},{10,2},{3,11},{11,3},{4,12},{12,4},... | collective-permute-start | bytes 4718600 | tf_op jit(solution)/shard_map/ppermute | solution.py:92
  12.0 6.6 %copy-start.6 = (s32[128]{0:T(128)S(1)}, s32[128]{0:T(128)}, u32[]{:S(2)}) copy-start(s32[128]{0:T(128)} %and_select_fusion) | copy-start | bytes 1540
  27.7 10.4 %copy-start.2 = (bf16[4096,192]{0,1:T(8,128)(2,1)S(1)}, bf16[4096,192]{0,1:T(8,128)(2,1)}, u32[]{:S(2)}) copy-start(bf16[4096,192]{0,1:T(8,128)(2,1)} %param.37) | copy-start | bytes 4718596
  33.2 27.2 %copy-start.3 = (bf16[32,4096]{1,0:T(8,128)(2,1)S(1)}, bf16[32,4096]{1,0:T(8,128)(2,1)}, u32[]{:S(2)}) copy-start(bf16[32,4096]{1,0:T(8,128)(2,1)} %refs_10_.1) | copy-start | bytes 786436
  33.2 27.2 %copy-start.4 = (f32[4096]{0:T(1024)S(1)}, f32[4096]{0:T(1024)}, u32[]{:S(2)}) copy-start(f32[4096]{0:T(1024)} %param.33) | copy-start | bytes 49156
  33.2 7.4 %collective-permute-start.3 = (bf16[32,4096]{1,0:T(8,128)(2,1)S(1)}, bf16[32,4096]{1,0:T(8,128)(2,1)S(1)}, u32[]{:S(2)}, u32[]{:S(2)}) collective-permute-start(bf16[32,4096]{1,0:T(8,128)(2,1)S(1)} %get-tuple-element.77), channel_id=1, source_target_pairs={{1,0},{2,1},{3,2},{0,3},{5,4},{6,5},{7,6},{4,7},{9,8},{10,9},{11,1... | collective-permute-start | bytes 786440 | tf_op jit(solution)/shard_map/ppermute | solution.py:96
  33.2 25.3 %collective-permute-start.4 = (bf16[32,4096]{1,0:T(8,128)(2,1)S(1)}, bf16[32,4096]{1,0:T(8,128)(2,1)S(1)}, u32[]{:S(2)}, u32[]{:S(2)}) collective-permute-start(bf16[32,4096]{1,0:T(8,128)(2,1)S(1)} %get-tuple-element.78), channel_id=1, source_target_pairs={{2,0},{3,1},{0,2},{1,3},{6,4},{7,5},{4,6},{5,7},{10,8},{11,9},{8,1... | collective-permute-start | bytes 786440 | tf_op jit(solution)/shard_map/ppermute | solution.py:96
  36.1 24.0 %collective-permute-start.5 = (bf16[32,4096]{1,0:T(8,128)(2,1)S(1)}, bf16[32,4096]{1,0:T(8,128)(2,1)S(1)}, u32[]{:S(2)}, u32[]{:S(2)}) collective-permute-start(bf16[32,4096]{1,0:T(8,128)(2,1)S(1)} %get-tuple-element.79), channel_id=1, source_target_pairs={{3,0},{0,1},{1,2},{2,3},{7,4},{4,5},{5,6},{6,7},{11,8},{8,9},{9,10... | collective-permute-start | bytes 786440 | tf_op jit(solution)/shard_map/ppermute | solution.py:96
  38.2 43.0 %copy-start = (bf16[4096,192]{0,1:T(8,128)(2,1)S(1)}, bf16[4096,192]{0,1:T(8,128)(2,1)}, u32[]{:S(2)}) copy-start(bf16[4096,192]{0,1:T(8,128)(2,1)} %param.36) | copy-start | bytes 4718596
  38.2 43.1 %copy-start.1 = (bf16[4096,192]{0,1:T(8,128)(2,1)S(1)}, bf16[4096,192]{0,1:T(8,128)(2,1)}, u32[]{:S(2)}) copy-start(bf16[4096,192]{0,1:T(8,128)(2,1)} %param.35) | copy-start | bytes 4718596
  40.6 19.6 %collective-permute-start.7 = (bf16[192,2048]{1,0:T(8,128)(2,1)S(1)}, bf16[192,2048]{1,0:T(8,128)(2,1)S(1)}, u32[]{:S(2)}, u32[]{:S(2)}) collective-permute-start(bf16[192,2048]{1,0:T(8,128)(2,1)S(1)} %get-tuple-element.122), channel_id=1, source_target_pairs={{0,16},{16,0},{1,17},{17,1},{2,18},{18,2},{3,19},{19,3},{4,20},{20... | collective-permute-start | bytes 2359304 | tf_op jit(solution)/shard_map/ppermute | solution.py:92
  58.6 35.6 %collective-permute-start.13 = (bf16[192,2048]{1,0:T(8,128)(2,1)S(1)}, bf16[192,2048]{1,0:T(8,128)(2,1)S(1)}, u32[]{:S(2)}, u32[]{:S(2)}) collective-permute-start(bf16[192,2048]{1,0:T(8,128)(2,1)S(1)} %get-tuple-element.105.refs_0_), channel_id=1, source_target_pairs={{0,8},{8,0},{1,9},{9,1},{2,10},{10,2},{3,11},{11,3},{4,12},{12,4},... | collective-permute-start | bytes 2359304 | tf_op jit(solution)/shard_map/ppermute | solution.py:92
  60.6 13.6 %collective-permute-start.10 = (bf16[32,4096]{1,0:T(8,128)(2,1)S(1)}, bf16[32,4096]{1,0:T(8,128)(2,1)S(1)}, u32[]{:S(2)}, u32[]{:S(2)}) collective-permute-start(bf16[32,4096]{1,0:T(8,128)(2,1)S(1)} %add_convert_fusion.1), channel_id=1, source_target_pairs={{3,0},{0,1},{1,2},{2,3},{7,4},{4,5},{5,6},{6,7},{11,8},{8,9},{9,10... | collective-permute-start | bytes 786440 | tf_op jit(solution)/shard_map/ppermute | solution.py:96
  70.2 11.0 %collective-permute-start.11 = (bf16[32,4096]{1,0:T(8,128)(2,1)S(1)}, bf16[32,4096]{1,0:T(8,128)(2,1)S(1)}, u32[]{:S(2)}, u32[]{:S(2)}) collective-permute-start(bf16[32,4096]{1,0:T(8,128)(2,1)S(1)} %add_convert_fusion.1), channel_id=1, source_target_pairs={{0,16},{16,0},{1,17},{17,1},{2,18},{18,2},{3,19},{19,3},{4,20},{20... | collective-permute-start | bytes 786440 | tf_op jit(solution)/shard_map/ppermute | solution.py:92
  71.8 9.5 %collective-permute-start.8 = (bf16[32,4096]{1,0:T(8,128)(2,1)S(1)}, bf16[32,4096]{1,0:T(8,128)(2,1)S(1)}, u32[]{:S(2)}, u32[]{:S(2)}) collective-permute-start(bf16[32,4096]{1,0:T(8,128)(2,1)S(1)} %add_convert_fusion.1), channel_id=1, source_target_pairs={{1,0},{2,1},{3,2},{0,3},{5,4},{6,5},{7,6},{4,7},{9,8},{10,9},{11,1... | collective-permute-start | bytes 786440 | tf_op jit(solution)/shard_map/ppermute | solution.py:96
  74.1 14.3 %collective-permute-start.9 = (bf16[32,4096]{1,0:T(8,128)(2,1)S(1)}, bf16[32,4096]{1,0:T(8,128)(2,1)S(1)}, u32[]{:S(2)}, u32[]{:S(2)}) collective-permute-start(bf16[32,4096]{1,0:T(8,128)(2,1)S(1)} %add_convert_fusion.1), channel_id=1, source_target_pairs={{2,0},{3,1},{0,2},{1,3},{6,4},{7,5},{4,6},{5,7},{10,8},{11,9},{8,1... | collective-permute-start | bytes 786440 | tf_op jit(solution)/shard_map/ppermute | solution.py:96
  81.3 13.5 %collective-permute-start.19 = (bf16[192,4096]{1,0:T(8,128)(2,1)S(1)}, bf16[192,4096]{1,0:T(8,128)(2,1)S(1)}, u32[]{:S(2)}, u32[]{:S(2)}) collective-permute-start(bf16[192,4096]{1,0:T(8,128)(2,1)S(1)} %bitcast.16), channel_id=1, source_target_pairs={{0,4},{4,0},{1,5},{5,1},{2,6},{6,2},{3,7},{7,3},{8,12},{12,8},{9,1... | collective-permute-start | bytes 4718600 | tf_op jit(solution)/shard_map/ppermute | solution.py:92
  81.3 15.1 %collective-permute-start.17 = (bf16[192,4096]{1,0:T(8,128)(2,1)S(1)}, bf16[192,4096]{1,0:T(8,128)(2,1)S(1)}, u32[]{:S(2)}, u32[]{:S(2)}) collective-permute-start(bf16[192,4096]{1,0:T(8,128)(2,1)S(1)} %bitcast.19), channel_id=1, source_target_pairs={{0,4},{4,0},{1,5},{5,1},{2,6},{6,2},{3,7},{7,3},{8,12},{12,8},{9,1... | collective-permute-start | bytes 4718600 | tf_op jit(solution)/shard_map/ppermute | solution.py:92
  88.4 20.6 %collective-permute-start.21 = (bf16[192,2048]{1,0:T(8,128)(2,1)S(1)}, bf16[192,2048]{1,0:T(8,128)(2,1)S(1)}, u32[]{:S(2)}, u32[]{:S(2)}) collective-permute-start(bf16[192,2048]{1,0:T(8,128)(2,1)S(1)} %collective-permute-done.7.refs_0_), channel_id=1, source_target_pairs={{0,8},{8,0},{1,9},{9,1},{2,10},{10,2},{3,11},{11,3},{4,12},{12,4},... | collective-permute-start | bytes 2359304 | tf_op jit(solution)/shard_map/ppermute | solution.py:92
  94.2 3.4 %collective-permute-start.20 = (bf16[192,4096]{1,0:T(8,128)(2,1)S(1)}, bf16[192,4096]{1,0:T(8,128)(2,1)S(1)}, u32[]{:S(2)}, u32[]{:S(2)}) collective-permute-start(bf16[192,4096]{1,0:T(8,128)(2,1)S(1)} %collective-permute-done.12.refs_2_), channel_id=1, source_target_pairs={{0,4},{4,0},{1,5},{5,1},{2,6},{6,2},{3,7},{7,3},{8,12},{12,8},{9,1... | collective-permute-start | bytes 4718600 | tf_op jit(solution)/shard_map/ppermute | solution.py:92
  94.2 6.4 %collective-permute-start.18 = (bf16[192,4096]{1,0:T(8,128)(2,1)S(1)}, bf16[192,4096]{1,0:T(8,128)(2,1)S(1)}, u32[]{:S(2)}, u32[]{:S(2)}) collective-permute-start(bf16[192,4096]{1,0:T(8,128)(2,1)S(1)} %collective-permute-done.6.refs_2_), channel_id=1, source_target_pairs={{0,4},{4,0},{1,5},{5,1},{2,6},{6,2},{3,7},{7,3},{8,12},{12,8},{9,1... | collective-permute-start | bytes 4718600 | tf_op jit(solution)/shard_map/ppermute | solution.py:92
  94.8 14.2 %collective-permute-start.14 = (bf16[32,4096]{1,0:T(8,128)(2,1)S(1)}, bf16[32,4096]{1,0:T(8,128)(2,1)S(1)}, u32[]{:S(2)}, u32[]{:S(2)}) collective-permute-start(bf16[32,4096]{1,0:T(8,128)(2,1)S(1)} %collective-permute-done.8), channel_id=1, source_target_pairs={{0,16},{16,0},{1,17},{17,1},{2,18},{18,2},{3,19},{19,3},{4,20},{20... | collective-permute-start | bytes 786440 | tf_op jit(solution)/shard_map/ppermute | solution.py:92
  96.4 13.3 %collective-permute-start.15 = (bf16[32,4096]{1,0:T(8,128)(2,1)S(1)}, bf16[32,4096]{1,0:T(8,128)(2,1)S(1)}, u32[]{:S(2)}, u32[]{:S(2)}) collective-permute-start(bf16[32,4096]{1,0:T(8,128)(2,1)S(1)} %collective-permute-done.9), channel_id=1, source_target_pairs={{0,16},{16,0},{1,17},{17,1},{2,18},{18,2},{3,19},{19,3},{4,20},{20... | collective-permute-start | bytes 786440 | tf_op jit(solution)/shard_map/ppermute | solution.py:92
  97.6 16.7 %collective-permute-start.16 = (bf16[32,4096]{1,0:T(8,128)(2,1)S(1)}, bf16[32,4096]{1,0:T(8,128)(2,1)S(1)}, u32[]{:S(2)}, u32[]{:S(2)}) collective-permute-start(bf16[32,4096]{1,0:T(8,128)(2,1)S(1)} %collective-permute-done.10), channel_id=1, source_target_pairs={{0,16},{16,0},{1,17},{17,1},{2,18},{18,2},{3,19},{19,3},{4,20},{20... | collective-permute-start | bytes 786440 | tf_op jit(solution)/shard_map/ppermute | solution.py:92
  100.6 19.5 %collective-permute-start.26 = (bf16[192,2048]{1,0:T(8,128)(2,1)S(1)}, bf16[192,2048]{1,0:T(8,128)(2,1)S(1)}, u32[]{:S(2)}, u32[]{:S(2)}) collective-permute-start(bf16[192,2048]{1,0:T(8,128)(2,1)S(1)} %collective-permute-done.7.refs_0_), channel_id=1, source_target_pairs={{0,4},{4,0},{1,5},{5,1},{2,6},{6,2},{3,7},{7,3},{8,12},{12,8},{9,1... | collective-permute-start | bytes 2359304 | tf_op jit(solution)/shard_map/ppermute | solution.py:92
  117.9 2.7 %collective-permute-start.27 = (bf16[192,2048]{1,0:T(8,128)(2,1)S(1)}, bf16[192,2048]{1,0:T(8,128)(2,1)S(1)}, u32[]{:S(2)}, u32[]{:S(2)}) collective-permute-start(bf16[192,2048]{1,0:T(8,128)(2,1)S(1)} %collective-permute-done.21.refs_2_), channel_id=1, source_target_pairs={{0,4},{4,0},{1,5},{5,1},{2,6},{6,2},{3,7},{7,3},{8,12},{12,8},{9,1... | collective-permute-start | bytes 2359304 | tf_op jit(solution)/shard_map/ppermute | solution.py:92
  118.0 3.4 %collective-permute-start.24 = (bf16[192,2048]{1,0:T(8,128)(2,1)S(1)}, bf16[192,2048]{1,0:T(8,128)(2,1)S(1)}, u32[]{:S(2)}, u32[]{:S(2)}) collective-permute-start(bf16[192,2048]{1,0:T(8,128)(2,1)S(1)} %get-tuple-element.105.refs_0_), channel_id=1, source_target_pairs={{0,4},{4,0},{1,5},{5,1},{2,6},{6,2},{3,7},{7,3},{8,12},{12,8},{9,1... | collective-permute-start | bytes 2359304 | tf_op jit(solution)/shard_map/ppermute | solution.py:92
  118.5 4.0 %collective-permute-start.25 = (bf16[192,2048]{1,0:T(8,128)(2,1)S(1)}, bf16[192,2048]{1,0:T(8,128)(2,1)S(1)}, u32[]{:S(2)}, u32[]{:S(2)}) collective-permute-start(bf16[192,2048]{1,0:T(8,128)(2,1)S(1)} %collective-permute-done.13.refs_2_), channel_id=1, source_target_pairs={{0,4},{4,0},{1,5},{5,1},{2,6},{6,2},{3,7},{7,3},{8,12},{12,8},{9,1... | collective-permute-start | bytes 2359304 | tf_op jit(solution)/shard_map/ppermute | solution.py:92
  118.6 7.7 %collective-permute-start.22 = (bf16[128,768]{1,0:T(8,128)(2,1)S(1)}, bf16[128,768]{1,0:T(8,128)(2,1)S(1)}, u32[]{:S(2)}, u32[]{:S(2)}) collective-permute-start(bf16[128,768]{1,0:T(8,128)(2,1)S(1)} %get-tuple-element.104.other), channel_id=1, source_target_pairs={{0,16},{16,0},{1,17},{17,1},{2,18},{18,2},{3,19},{19,3},{4,20},{20... | collective-permute-start | bytes 589832 | tf_op jit(solution)/shard_map/ppermute | solution.py:92
  120.1 9.9 %collective-permute-start.23 = (bf16[128,768]{1,0:T(8,128)(2,1)S(1)}, bf16[128,768]{1,0:T(8,128)(2,1)S(1)}, u32[]{:S(2)}, u32[]{:S(2)}) collective-permute-start(bf16[128,768]{1,0:T(8,128)(2,1)S(1)} %get-tuple-element.103.own), channel_id=1, source_target_pairs={{0,16},{16,0},{1,17},{17,1},{2,18},{18,2},{3,19},{19,3},{4,20},{20... | collective-permute-start | bytes 589832 | tf_op jit(solution)/shard_map/ppermute | solution.py:92
  131.8 32.1 %copy-start.5 = (f32[4096]{0:T(1024)S(1)}, f32[4096]{0:T(1024)}, u32[]{:S(2)}) copy-start(f32[4096]{0:T(1024)} %param.34) | copy-start | bytes 49156
  131.9 9.7 %collective-permute-start.28 = (bf16[64,2048]{1,0:T(8,128)(2,1)S(1)}, bf16[64,2048]{1,0:T(8,128)(2,1)S(1)}, u32[]{:S(2)}, u32[]{:S(2)}) collective-permute-start(bf16[64,2048]{1,0:T(8,128)(2,1)S(1)} %get-tuple-element.114), channel_id=1, source_target_pairs={{1,0},{2,1},{3,2},{0,3},{5,4},{6,5},{7,6},{4,7},{9,8},{10,9},{11,1... | collective-permute-start | bytes 786440 | tf_op jit(solution)/shard_map/ppermute | solution.py:96
  134.7 23.8 %collective-permute-start.29 = (bf16[64,2048]{1,0:T(8,128)(2,1)S(1)}, bf16[64,2048]{1,0:T(8,128)(2,1)S(1)}, u32[]{:S(2)}, u32[]{:S(2)}) collective-permute-start(bf16[64,2048]{1,0:T(8,128)(2,1)S(1)} %get-tuple-element.115), channel_id=1, source_target_pairs={{2,0},{3,1},{0,2},{1,3},{6,4},{7,5},{4,6},{5,7},{10,8},{11,9},{8,1... | collective-permute-start | bytes 786440 | tf_op jit(solution)/shard_map/ppermute | solution.py:96
  135.8 22.7 %collective-permute-start.30 = (bf16[64,2048]{1,0:T(8,128)(2,1)S(1)}, bf16[64,2048]{1,0:T(8,128)(2,1)S(1)}, u32[]{:S(2)}, u32[]{:S(2)}) collective-permute-start(bf16[64,2048]{1,0:T(8,128)(2,1)S(1)} %get-tuple-element.116), channel_id=1, source_target_pairs={{3,0},{0,1},{1,2},{2,3},{7,4},{4,5},{5,6},{6,7},{11,8},{8,9},{9,10... | collective-permute-start | bytes 786440 | tf_op jit(solution)/shard_map/ppermute | solution.py:96
  158.7 5.0 %collective-permute-start.31 = (bf16[32,2048]{1,0:T(8,128)(2,1)S(1)}, bf16[32,2048]{1,0:T(8,128)(2,1)S(1)}, u32[]{:S(2)}, u32[]{:S(2)}) collective-permute-start(bf16[32,2048]{1,0:T(8,128)(2,1)S(1)} %slice.14), channel_id=1, source_target_pairs={{0,16},{16,0},{1,17},{17,1},{2,18},{18,2},{3,19},{19,3},{4,20},{20... | collective-permute-start | bytes 393224 | tf_op jit(solution)/shard_map/ppermute | solution.py:92

commit v7 on v6

--- a/solution.py
+++ b/solution.py
@@ -97,14 +97,12 @@
 
 
 def line_gather(block):
-    across = shift(block, 2)
-    return [block, shift(block, 1), across, shift(block, 3)]
+    copies = jnp.broadcast_to(block[None], (lax.axis_size("mlp"), *block.shape))
+    return lax.all_to_all(copies, "mlp", 0, 0, tiled=True).reshape(-1, block.shape[1])
 
 
 def line_scatter(parts):
-    across = shift(parts[2], 2)
-    arrived = (parts[0], shift(parts[3], 1), across, shift(parts[1], 3))
-    return sum(part.astype(jnp.float32) for part in arrived)
+    return jnp.sum(lax.all_to_all(parts, "mlp", 0, 0, tiled=True).astype(jnp.float32), axis=0)
 
 
 def together(*values):
@@ -184,14 +182,11 @@
     sine,
     slot_mask,
     allowed,
-    out_0,
-    out_1,
-    out_2,
-    out_3,
+    out,
     rows,
     context,
 ):
-    tok_dev = block_0.shape[0]
+    tok_dev = out.shape[1]
     for k, block in enumerate((block_0, block_1, block_2, block_3)):
         rows[k * tok_dev : (k + 1) * tok_dev, :] = block[...]
 
@@ -231,8 +226,9 @@
         at = slice(start, start + step)
         part = jnp.dot(context[...], output_weight[:, at], preferred_element_type=jnp.float32)
         part = part.astype(jnp.bfloat16)
-        for k, out in enumerate((out_0, out_1, out_2, out_3)):
-            out[:, at] = part[k * tok_dev : (k + 1) * tok_dev]
+        for k in range(4):
+            owner = lax.rem(lax.axis_index("mlp") + k, 4)
+            out[owner, :, at] = part[k * tok_dev : (k + 1) * tok_dev]
 
 
 def hidden_kernel(states, gate_rows, up_rows, hidden_own, hidden_other):
@@ -251,8 +247,8 @@
         hidden_other[:, at] = hidden[half:]
 
 
-def down_kernel(own, other, far_own, far_other, near_rows, far_rows, out_0, out_1, out_2, out_3):
-    tok_dev = out_0.shape[0] // 2
+def down_kernel(own, other, far_own, far_other, near_rows, far_rows, out):
+    tok_dev = out.shape[1] // 2
     step = 512
     for start in range(0, near_rows.shape[1], step):
         at = slice(start, start + step)
@@ -260,8 +256,8 @@
             part = jnp.dot(near[...], near_rows[:, at], preferred_element_type=jnp.float32)
             part += jnp.dot(far[...], far_rows[:, at], preferred_element_type=jnp.float32)
             part = part.astype(jnp.bfloat16)
-            for k, out in enumerate((out_0, out_1, out_2, out_3)):
-                out[side * tok_dev : (side + 1) * tok_dev, at] = part[
+            for k in range(out.shape[0]):
+                out[k, side * tok_dev : (side + 1) * tok_dev, at] = part[
                     k * tok_dev : (k + 1) * tok_dev
                 ]
 
@@ -279,20 +275,17 @@
     half = width // 2
     gate_x, up_x = exchange(gate_rows, "x"), exchange(up_rows, "x")
     cosine, sine = jnp.cos(angles), jnp.sin(angles)
-    block = jax.ShapeDtypeStruct((tok_dev, width), jnp.bfloat16)
-    *staged_rows, own_block = staged(
-        *([in_hbm(array)] for array in (*projections, *adapters, *head_gains, layer_input))
-    )
-    parts = vmem_call(
+    staged_rows = staged(*([in_hbm(array)] for array in (*projections, *adapters, *head_gains)))
+    blocks = [layer_input, *(shift(layer_input, hops) for hops in (1, 2, 3))]
+    (parts,) = vmem_call(
         attention_kernel,
-        [block] * 4,
+        [jax.ShapeDtypeStruct((4, tok_dev, width), jnp.bfloat16)],
         [
             pltpu.VMEM((4 * tok_dev, width), jnp.bfloat16),
             pltpu.VMEM((4 * tok_dev, projections[0].shape[1]), jnp.bfloat16),
         ],
         [
-            own_block,
-            *line_gather(layer_input)[1:],
+            *blocks,
             *staged_rows,
             jnp.concatenate([cosine, cosine], axis=1),
             jnp.concatenate([-sine, sine], axis=1),
@@ -301,25 +294,23 @@
         ],
         8,
     )
-    *parts, down_rows = together(*parts, down_rows)
+    parts, down_rows = together(parts, down_rows)
     near = lax.dynamic_slice_in_dim(down_rows, y * half, half, axis=1)
     far = exchange(lax.dynamic_slice_in_dim(down_rows, (1 - y) * half, half, axis=1), "y")
     near_x, far_x = exchange(near, "x"), exchange(far, "x")
-    attn_own, gate_x, near, far = together(line_scatter(parts), gate_x, near, far)
+    attn_own, near, far = together(line_scatter(parts), near, far)
     residual_own = add_normed(layer_input, attn_own, gains[0])
-    *line, other = together(*line_gather(residual_own), exchange(residual_own, "y"))
-    *line, gate_x, up_x, near_x = together(*line, gate_x, up_x, near_x)
+    line = line_gather(residual_own)
+    line, gate_x, up_x, near_x = together(line, gate_x, up_x, near_x)
     (gate_all,) = staged(four_pieces(gate_rows, gate_x, in_hbm))
     (up_all,) = staged(four_pieces(up_rows, up_x, in_hbm))
-    *others, gate_all, up_all, far_x = together(
-        *[exchange(rows, "y") for rows in line[1:]], gate_all, up_all, far_x
-    )
+    others, gate_all, up_all, far_x = together(exchange(line, "y"), gate_all, up_all, far_x)
     group = jax.ShapeDtypeStruct((4 * tok_dev, 4 * gate_rows.shape[0]), jnp.bfloat16)
     hidden_own, hidden_other = vmem_call(
         hidden_kernel,
         [group] * 2,
         [],
-        [jnp.concatenate([*line, other, *others]), gate_all, up_all],
+        [jnp.concatenate([line, others]), gate_all, up_all],
         8,
     )
     hidden_own, hidden_other, near_x, far_x = together(hidden_own, hidden_other, near_x, far_x)
@@ -328,9 +319,9 @@
     from_other, from_own, near_all, far_all = together(
         exchange(hidden_other, "y"), exchange(hidden_own, "y"), near_all, far_all
     )
-    parts = vmem_call(
+    (parts,) = vmem_call(
         down_kernel,
-        [jax.ShapeDtypeStruct((2 * tok_dev, half), jnp.bfloat16)] * 4,
+        [jax.ShapeDtypeStruct((4, 2 * tok_dev, half), jnp.bfloat16)],
         [],
         [hidden_own, hidden_other, from_other, from_own, near_all, far_all],
         8,

time: 165 us -> 209 us (1.27)
  blocking collectives: 0 us -> 30.1 us
  waiting for transfers between devices: 90.4 us -> 119 us
  starting transfers between devices: 47.2 us -> 25.8 us
  local copies, waits for them, and re-layouts: 0.34 us -> 3.77 us
  other arithmetic: 5.67 us -> 7.91 us
    ppermute x20 -> x17, waiting for transfers between devices: 31 us -> 86.4 us  [exchange(): return lax.ppermute(block, axis, [(0, 1), (1, 0)])]
    ppermute x12 -> x3, waiting for transfers between devices: 59.4 us -> 11.4 us  [shift(): return lax.ppermute(block, 'mlp', [((k + hops) % 4, k) for k in range(4)])]
    all_to_all x0 -> x1, blocking collectives: none -> 30.1 us  [line_scatter(): lax.all_to_all(parts, 'mlp', 0, 0, tiled=True).astype(jnp.float32)]
    ppermute x12 -> x3, starting transfers between devices: 31.7 us -> 6.06 us  [shift(): return lax.ppermute(block, 'mlp', [((k + hops) % 4, k) for k in range(4)])]
    all_to_all x0 -> x2, waiting for transfers between devices: none -> 21 us  [the longest x1 21 us: line_scatter(): lax.all_to_all(parts, 'mlp', 0, 0, tiled=True).astype(jnp.float32)]
    all_to_all x0 -> x2, starting transfers between devices: none -> 8.63 us  [the longest x1 4.39 us: line_scatter(): lax.all_to_all(parts, 'mlp', 0, 0, tiled=True).astype(jnp.float32)]
    ppermute x20 -> x17, starting transfers between devices: 15.5 us -> 11.1 us  [exchange(): return lax.ppermute(block, axis, [(0, 1), (1, 0)])]
  transfers between devices with their start and end apart: 32 -> 22, of which waited for: 17 -> 12; matrix products, arithmetic and copies ran while one was open for 3% -> 4% of each run, Pallas kernels for 12% -> 7%
where the time goes in v7:
time: 209 us; the launch traced here: 208 us
  waiting for transfers between devices  119 us (57%)
  blocking collectives  30.1 us (14%)
  starting transfers between devices  25.8 us (12%)
  Pallas kernels  21.6 us (10%)
  other arithmetic  7.91 us (4%)
  local copies, waits for them, and re-layouts  3.77 us (2%)
    ppermute x17, waiting for transfers between devices, exchange(): return lax.ppermute(block, axis, [(0, 1), (1, 0)])  86.4 us
    all_to_all x1, blocking collectives, line_scatter(): lax.all_to_all(parts, 'mlp', 0, 0, tiled=True).astype(jnp.float32)  30.1 us
    all_to_all x1, waiting for transfers between devices, line_scatter(): lax.all_to_all(parts, 'mlp', 0, 0, tiled=True).astype(jnp.float32)  21 us
    ppermute x3, waiting for transfers between devices, shift(): return lax.ppermute(block, 'mlp', [((k + hops) % 4, k) for k in range(4)])  11.4 us
    ppermute x17, starting transfers between devices, exchange(): return lax.ppermute(block, axis, [(0, 1), (1, 0)])  11.1 us
    pallas_call x5, Pallas kernels, staged(): pl.pallas_call(kernel, out_shape=[pltpu.VMEM(shape, group[0].dtype) for s...  10.9 us
    pallas_call x3, Pallas kernels, vmem_call(): pl.pallas_call(kernel, out_shape=outs, in_specs=[whole] * len(operands),...  10.7 us
    ppermute x3, starting transfers between devices, shift(): return lax.ppermute(block, 'mlp', [((k + hops) % 4, k) for k in range(4)])  6.06 us
  transfers between devices with their start and end apart: 22, of which 12 were waited for; matrix products, arithmetic and copies ran while one was open for 4% of the time, Pallas kernels for 7%

profile of v7, /device:TPU:0, one launch (start us, length us, event | category | flops | bytes accessed | tf_op | source)
XLA Modules:
  0.0 208.2 jit_solution(16218948806301614214)
XLA Ops:
  0.0 5.0 %collective-permute-start = (bf16[32,4096]{1,0:T(8,128)(2,1)}, bf16[32,4096]{1,0:T(8,128)(2,1)S(1)}, u32[]{:S(2)}, u32[]{:S(2)}) collective-permute-start(bf16[32,4096]{1,0:T(8,128)(2,1)} %block_0.1), channel_id=1, source_target_pairs={{1,0},{2,1},{3,2},{0,3},{5,4},{6,5},{7,6},{4,7},{9,8},{10,9},{11,1... | collective-permute-start | bytes 786440 | tf_op jit(solution)/shard_map/ppermute | solution.py:96
  5.1 1.0 collective-permute-start.2
  6.1 0.8 reduce-window.4
  6.9 0.7 fusion.6
  7.6 0.7 select_reduce_fusion.1
  8.3 0.3 fusion.4
  8.7 0.7 select_reduce_fusion
  9.5 6.5 %shard_map.181 = (bf16[4096,512]{1,0:T(8,128)(2,1)S(1)}, bf16[4096,512]{1,0:T(8,128)(2,1)S(1)}, bf16[4096,512]{1,0:T(8,128)(2,1)S(1)}, bf16[512,4096]{1,0:T(8,12...) custom-call(bf16[4096,512]{1,0:T(8,128)(2,1)} %refs_0_.1, ...), custom_call_target="tpu_custom_call" | custom-call | bytes 38281216 | tf_op jit(solution)/shard_map/pallas_call | solution.py:152
  16.2 11.4 %collective-permute-done.1.block_2 = bf16[32,4096]{1,0:T(8,128)(2,1)S(1)} collective-permute-done((bf16[32,4096]{1,0:T(8,128)(2,1)}, bf16[32,4096]{1,0:T(8,128)(2,1)S(1)}, u32[]{:S(2)}, u32[]{:S(2)}) %collective-permute-start.1) | collective-permute-done | bytes 262176 | tf_op jit(solution)/shard_map/ppermute | solution.py:96
  27.6 5.4 %shard_map.182 = bf16[4,32,4096]{2,1,0:T(8,128)(2,1)} custom-call(bf16[32,4096]{1,0:T(8,128)(2,1)S(1)} %copy-done, bf16[32,4096]{1,0:T(8,128)(2,1)S(1)} %collective-permute-done.block_1, bf16[32,4096]{1,0:T(8,128)(2,1)S(1)} %collective-permute-done.1.block_2, bf16[32,4096]{1,0:T(8,128)(2,1)S(1)} %collective-permute-done.2.block_3, ...), custom_call_target="tpu_custom_call" | custom-call | flops 1048576 | bytes 1048576 | tf_op jit(solution)/shard_map/pallas_call | solution.py:118
  33.0 4.4 %all-to-all-start = ((bf16[4,32,4096]{2,1,0:T(8,128)(2,1)}), bf16[4,32,4096]{2,1,0:T(8,128)(2,1)}, u32[]{:S(2)}, u32[]{:S(2)}) async-start(bf16[4,32,4096]{2,1,0:T(8,128)(2,1)} %shard_map.182), calls=%async_computation | async-start | bytes 2097152 | tf_op jit(solution)/shard_map/all_to_all | solution.py:105
  37.4 1.0 constant_dynamic-slice_fusion.1
  38.5 1.5 collective-permute-start.3
  40.0 1.5 collective-permute-start.4
  41.5 0.5 collective-permute-start.5
  42.0 21.0 %all-to-all-done = bf16[4,32,4096]{2,1,0:T(8,128)(2,1)} async-done(((bf16[4,32,4096]{2,1,0:T(8,128)(2,1)}), bf16[4,32,4096]{2,1,0:T(8,128)(2,1)}, u32[]{:S(2)}, u32[]{:S(2)}) %all-to-all-start) | async-done | bytes 1048608 | tf_op jit(solution)/shard_map/all_to_all | solution.py:105
  63.0 1.4 convert_reduce_fusion.1
  64.8 0.7 copy-done.3
  65.5 1.1 broadcast_in_dim.8
  66.6 4.2 %all-to-all-start.1 = ((bf16[4,32,4096]{2,1,0:T(8,128)(2,1)}), bf16[4,32,4096]{2,1,0:T(8,128)(2,1)}, u32[]{:S(2)}, u32[]{:S(2)}) async-start(bf16[4,32,4096]{2,1,0:T(8,128)(2,1)} %broadcast_in_dim.8), calls=%async_computation.1 | async-start | bytes 2097152 | tf_op jit(solution)/shard_map/all_to_all | solution.py:101
  70.8 1.6 collective-permute-start.6
  72.4 53.4 %collective-permute-done.6.refs_2_ = bf16[192,2048]{1,0:T(8,128)(2,1)S(1)} collective-permute-done((bf16[192,2048]{1,0:T(8,128)(2,1)S(1)}, bf16[192,2048]{1,0:T(8,128)(2,1)S(1)}, u32[]{:S(2)}, u32[]{:S(2)}) %collective-permute-start.6) | collective-permute-done | bytes 786464 | tf_op jit(solution)/shard_map/ppermute | solution.py:92
  125.7 0.9 copy-done.1
  126.7 0.5 collective-permute-start.8
  127.2 0.5 collective-permute-start.7
  127.8 1.5 collective-permute-start.12
  129.3 1.0 collective-permute-done.11.refs_3_
  130.4 2.4 %shard_map.184.up_rows = bf16[768,4096]{1,0:T(8,128)(2,1)S(1)} custom-call(bf16[192,4096]{1,0:T(8,128)(2,1)} %bitcast.17, bf16[192,4096]{1,0:T(8,128)(2,1)} %collective-permute-done.10.refs_1_, bf16[192,4096]{1,0:T(8,128)(2,1)} %collective-permute-done.5.refs_2_, bf16[192,4096]{1,0:T(8,128)(2,1)S(1)} %collective-permute-done.11.refs_3_), custom_call_target="tpu_custom_call" | custom-call | bytes 12582912 | tf_op jit(solution)/shard_map/pallas_call | solution.py:152
  132.8 2.0 collective-permute-done.8.refs_1_
  134.8 1.4 shard_map.183.gate_rows
  136.2 11.1 %collective-permute-done.12.refs_2_ = bf16[192,2048]{1,0:T(8,128)(2,1)S(1)} collective-permute-done((bf16[192,2048]{1,0:T(8,128)(2,1)S(1)}, bf16[192,2048]{1,0:T(8,128)(2,1)S(1)}, u32[]{:S(2)}, u32[]{:S(2)}) %collective-permute-start.12) | collective-permute-done | bytes 786464 | tf_op jit(solution)/shard_map/ppermute | solution.py:92
  147.4 5.6 %collective-permute-done.7 = bf16[128,4096]{1,0:T(8,128)(2,1)S(1)} collective-permute-done((bf16[128,4096]{1,0:T(8,128)(2,1)}, bf16[128,4096]{1,0:T(8,128)(2,1)S(1)}, u32[]{:S(2)}, u32[]{:S(2)}) %collective-permute-start.7) | collective-permute-done | bytes 1048608 | tf_op jit(solution)/shard_map/ppermute | solution.py:92
  153.0 1.4 pad_maximum_fusion.states
  154.4 3.5 %shard_map.185 = (bf16[128,768]{1,0:T(8,128)(2,1)S(1)}, bf16[128,768]{1,0:T(8,128)(2,1)S(1)}) custom-call(bf16[256,4096]{1,0:T(8,128)(2,1)S(1)} %pad_maximum_fusion.states, bf16[768,4096]{1,0:T(8,128)(2,1)S(1)} %shard_map.183.gate_rows, bf16[768,4096]{1,0:T(8,128)(2,1)S(1)} %shard_map.184.up_rows), custom_call_target="tpu_custom_call" | custom-call | flops 1048576 | bytes 1048576 | tf_op jit(solution)/shard_map/pallas_call | solution.py:118
  158.0 0.5 collective-permute-start.15
  158.5 0.5 collective-permute-start.13
  159.1 1.5 collective-permute-start.14
  160.6 0.3 shard_map.187.far_rows
  160.8 0.5 collective-permute-done.15.refs_1_
  161.4 1.1 collective-permute-done.16.refs_3_
  162.5 0.3 shard_map.186.near_rows
  162.8 3.5 %collective-permute-done.13.far_own = bf16[128,768]{1,0:T(8,128)(2,1)S(1)} collective-permute-done((bf16[128,768]{1,0:T(8,128)(2,1)S(1)}, bf16[128,768]{1,0:T(8,128)(2,1)S(1)}, u32[]{:S(2)}, u32[]{:S(2)}) %collective-permute-start.13) | collective-permute-done | bytes 196640 | tf_op jit(solution)/shard_map/ppermute | solution.py:92
  166.2 3.8 %collective-permute-done.14.far_other = bf16[128,768]{1,0:T(8,128)(2,1)S(1)} collective-permute-done((bf16[128,768]{1,0:T(8,128)(2,1)S(1)}, bf16[128,768]{1,0:T(8,128)(2,1)S(1)}, u32[]{:S(2)}, u32[]{:S(2)}) %collective-permute-start.14) | collective-permute-done | bytes 196640 | tf_op jit(solution)/shard_map/ppermute | solution.py:92
  170.0 1.8 shard_map.188
  171.8 30.1 %all_to_all.15 = bf16[4,64,2048]{2,1,0:T(8,128)(2,1)S(1)} all-to-all(bf16[4,64,2048]{2,1,0:T(8,128)(2,1)S(1)} %shard_map.188), channel_id=1, replica_groups=mesh['y'=2,'x'=2,'core'=2,'mlp'=4] {'mlp'}, dimensions={0} | all-to-all | bytes 2097152 | tf_op jit(solution)/shard_map/all_to_all | solution.py:105
  202.1 0.6 collective-permute-start.19
  202.7 4.5 %collective-permute-done.19 = bf16[32,2048]{1,0:T(8,128)(2,1)S(1)} collective-permute-done((bf16[32,2048]{1,0:T(8,128)(2,1)S(1)}, bf16[32,2048]{1,0:T(8,128)(2,1)S(1)}, u32[]{:S(2)}, u32[]{:S(2)}) %collective-permute-start.19) | collective-permute-done | bytes 131104 | tf_op jit(solution)/shard_map/ppermute | solution.py:92
  207.4 0.8 add_convert_fusion
  (46 shorter events, 1.4 us)
Async XLA Ops:
  0.0 16.2 %collective-permute-start = (bf16[32,4096]{1,0:T(8,128)(2,1)}, bf16[32,4096]{1,0:T(8,128)(2,1)S(1)}, u32[]{:S(2)}, u32[]{:S(2)}) collective-permute-start(bf16[32,4096]{1,0:T(8,128)(2,1)} %block_0.1), channel_id=1, source_target_pairs={{1,0},{2,1},{3,2},{0,3},{5,4},{6,5},{7,6},{4,7},{9,8},{10,9},{11,1... | collective-permute-start | bytes 786440 | tf_op jit(solution)/shard_map/ppermute | solution.py:96
  5.0 22.5 %collective-permute-start.1 = (bf16[32,4096]{1,0:T(8,128)(2,1)}, bf16[32,4096]{1,0:T(8,128)(2,1)S(1)}, u32[]{:S(2)}, u32[]{:S(2)}) collective-permute-start(bf16[32,4096]{1,0:T(8,128)(2,1)} %block_0.1), channel_id=1, source_target_pairs={{2,0},{3,1},{0,2},{1,3},{6,4},{7,5},{4,6},{5,7},{10,8},{11,9},{8,1... | collective-permute-start | bytes 786440 | tf_op jit(solution)/shard_map/ppermute | solution.py:96
  5.1 22.5 %collective-permute-start.2 = (bf16[32,4096]{1,0:T(8,128)(2,1)}, bf16[32,4096]{1,0:T(8,128)(2,1)S(1)}, u32[]{:S(2)}, u32[]{:S(2)}) collective-permute-start(bf16[32,4096]{1,0:T(8,128)(2,1)} %block_0.1), channel_id=1, source_target_pairs={{3,0},{0,1},{1,2},{2,3},{7,4},{4,5},{5,6},{6,7},{11,8},{8,9},{9,10... | collective-permute-start | bytes 786440 | tf_op jit(solution)/shard_map/ppermute | solution.py:96
  9.5 18.1 %copy-start = (bf16[32,4096]{1,0:T(8,128)(2,1)S(1)}, bf16[32,4096]{1,0:T(8,128)(2,1)}, u32[]{:S(2)}) copy-start(bf16[32,4096]{1,0:T(8,128)(2,1)} %block_0.1) | copy-start | bytes 786436
  33.0 4.4 %copy-start.5 = (bf16[4096,192]{0,1:T(8,128)(2,1)S(1)}, bf16[4096,192]{0,1:T(8,128)(2,1)}, u32[]{:S(2)}) copy-start(bf16[4096,192]{0,1:T(8,128)(2,1)} %param.37) | copy-start | bytes 4718596
  33.0 30.0 %all-to-all-start = ((bf16[4,32,4096]{2,1,0:T(8,128)(2,1)}), bf16[4,32,4096]{2,1,0:T(8,128)(2,1)}, u32[]{:S(2)}, u32[]{:S(2)}) async-start(bf16[4,32,4096]{2,1,0:T(8,128)(2,1)} %shard_map.182), calls=%async_computation | async-start | bytes 2097152 | tf_op jit(solution)/shard_map/all_to_all | solution.py:105
  37.4 27.2 %copy-start.6 = (f32[4096]{0:T(1024)S(1)}, f32[4096]{0:T(1024)}, u32[]{:S(2)}) copy-start(f32[4096]{0:T(1024)} %param.33) | copy-start | bytes 49156
  38.5 26.0 %collective-permute-start.3 = (bf16[192,2048]{1,0:T(8,128)(2,1)}, bf16[192,2048]{1,0:T(8,128)(2,1)S(1)}, u32[]{:S(2)}, u32[]{:S(2)}) collective-permute-start(bf16[192,2048]{1,0:T(8,128)(2,1)} %get-tuple-element.76), channel_id=1, source_target_pairs={{0,16},{16,0},{1,17},{17,1},{2,18},{18,2},{3,19},{19,3},{4,20},{20... | collective-permute-start | bytes 2359304 | tf_op jit(solution)/shard_map/ppermute | solution.py:92
  40.0 85.8 %collective-permute-start.4 = (bf16[192,4096]{1,0:T(8,128)(2,1)}, bf16[192,4096]{1,0:T(8,128)(2,1)S(1)}, u32[]{:S(2)}, u32[]{:S(2)}) collective-permute-start(bf16[192,4096]{1,0:T(8,128)(2,1)} %bitcast.18), channel_id=1, source_target_pairs={{0,8},{8,0},{1,9},{9,1},{2,10},{10,2},{3,11},{11,3},{4,12},{12,4},... | collective-permute-start | bytes 4718600 | tf_op jit(solution)/shard_map/ppermute | solution.py:92
  41.5 85.2 %collective-permute-start.5 = (bf16[192,4096]{1,0:T(8,128)(2,1)}, bf16[192,4096]{1,0:T(8,128)(2,1)}, u32[]{:S(2)}, u32[]{:S(2)}) collective-permute-start(bf16[192,4096]{1,0:T(8,128)(2,1)} %bitcast.15), channel_id=1, source_target_pairs={{0,8},{8,0},{1,9},{9,1},{2,10},{10,2},{3,11},{11,3},{4,12},{12,4},... | collective-permute-start | bytes 4718600 | tf_op jit(solution)/shard_map/ppermute | solution.py:92
  64.8 0.7 copy-start.3
  66.6 60.1 %all-to-all-start.1 = ((bf16[4,32,4096]{2,1,0:T(8,128)(2,1)}), bf16[4,32,4096]{2,1,0:T(8,128)(2,1)}, u32[]{:S(2)}, u32[]{:S(2)}) async-start(bf16[4,32,4096]{2,1,0:T(8,128)(2,1)} %broadcast_in_dim.8), calls=%async_computation.1 | async-start | bytes 2097152 | tf_op jit(solution)/shard_map/all_to_all | solution.py:101
  70.8 54.9 %collective-permute-start.6 = (bf16[192,2048]{1,0:T(8,128)(2,1)S(1)}, bf16[192,2048]{1,0:T(8,128)(2,1)S(1)}, u32[]{:S(2)}, u32[]{:S(2)}) collective-permute-start(bf16[192,2048]{1,0:T(8,128)(2,1)S(1)} %get-tuple-element.63.refs_0_), channel_id=1, source_target_pairs={{0,8},{8,0},{1,9},{9,1},{2,10},{10,2},{3,11},{11,3},{4,12},{12,4},... | collective-permute-start | bytes 2359304 | tf_op jit(solution)/shard_map/ppermute | solution.py:92
  72.4 55.4 %collective-permute-start.10 = (bf16[192,4096]{1,0:T(8,128)(2,1)}, bf16[192,4096]{1,0:T(8,128)(2,1)}, u32[]{:S(2)}, u32[]{:S(2)}) collective-permute-start(bf16[192,4096]{1,0:T(8,128)(2,1)} %bitcast.16), channel_id=1, source_target_pairs={{0,4},{4,0},{1,5},{5,1},{2,6},{6,2},{3,7},{7,3},{8,12},{12,8},{9,1... | collective-permute-start | bytes 4718600 | tf_op jit(solution)/shard_map/ppermute | solution.py:92
  125.7 0.9 copy-start.1
  126.7 3.6 %collective-permute-start.11 = (bf16[192,4096]{1,0:T(8,128)(2,1)}, bf16[192,4096]{1,0:T(8,128)(2,1)S(1)}, u32[]{:S(2)}, u32[]{:S(2)}) collective-permute-start(bf16[192,4096]{1,0:T(8,128)(2,1)} %collective-permute-done.5.refs_2_), channel_id=1, source_target_pairs={{0,4},{4,0},{1,5},{5,1},{2,6},{6,2},{3,7},{7,3},{8,12},{12,8},{9,1... | collective-permute-start | bytes 4718600 | tf_op jit(solution)/shard_map/ppermute | solution.py:92
  126.7 8.1 %collective-permute-start.8 = (bf16[192,4096]{1,0:T(8,128)(2,1)}, bf16[192,4096]{1,0:T(8,128)(2,1)S(1)}, u32[]{:S(2)}, u32[]{:S(2)}) collective-permute-start(bf16[192,4096]{1,0:T(8,128)(2,1)} %bitcast.19), channel_id=1, source_target_pairs={{0,4},{4,0},{1,5},{5,1},{2,6},{6,2},{3,7},{7,3},{8,12},{12,8},{9,1... | collective-permute-start | bytes 4718600 | tf_op jit(solution)/shard_map/ppermute | solution.py:92
  127.2 7.6 %collective-permute-start.9 = (bf16[192,4096]{1,0:T(8,128)(2,1)S(1)}, bf16[192,4096]{1,0:T(8,128)(2,1)S(1)}, u32[]{:S(2)}, u32[]{:S(2)}) collective-permute-start(bf16[192,4096]{1,0:T(8,128)(2,1)S(1)} %collective-permute-done.4.refs_2_), channel_id=1, source_target_pairs={{0,4},{4,0},{1,5},{5,1},{2,6},{6,2},{3,7},{7,3},{8,12},{12,8},{9,1... | collective-permute-start | bytes 4718600 | tf_op jit(solution)/shard_map/ppermute | solution.py:92
  127.2 25.7 %collective-permute-start.7 = (bf16[128,4096]{1,0:T(8,128)(2,1)}, bf16[128,4096]{1,0:T(8,128)(2,1)S(1)}, u32[]{:S(2)}, u32[]{:S(2)}) collective-permute-start(bf16[128,4096]{1,0:T(8,128)(2,1)} %bitcast.8), channel_id=1, source_target_pairs={{0,16},{16,0},{1,17},{17,1},{2,18},{18,2},{3,19},{19,3},{4,20},{20... | collective-permute-start | bytes 3145736 | tf_op jit(solution)/shard_map/ppermute | solution.py:92
  127.8 19.6 %collective-permute-start.12 = (bf16[192,2048]{1,0:T(8,128)(2,1)S(1)}, bf16[192,2048]{1,0:T(8,128)(2,1)S(1)}, u32[]{:S(2)}, u32[]{:S(2)}) collective-permute-start(bf16[192,2048]{1,0:T(8,128)(2,1)S(1)} %collective-permute-done.3.refs_0_), channel_id=1, source_target_pairs={{0,8},{8,0},{1,9},{9,1},{2,10},{10,2},{3,11},{11,3},{4,12},{12,4},... | collective-permute-start | bytes 2359304 | tf_op jit(solution)/shard_map/ppermute | solution.py:92
  130.3 28.8 %collective-permute-start.17 = (bf16[192,2048]{1,0:T(8,128)(2,1)S(1)}, bf16[192,2048]{1,0:T(8,128)(2,1)S(1)}, u32[]{:S(2)}, u32[]{:S(2)}) collective-permute-start(bf16[192,2048]{1,0:T(8,128)(2,1)S(1)} %collective-permute-done.3.refs_0_), channel_id=1, source_target_pairs={{0,4},{4,0},{1,5},{5,1},{2,6},{6,2},{3,7},{7,3},{8,12},{12,8},{9,1... | collective-permute-start | bytes 2359304 | tf_op jit(solution)/shard_map/ppermute | solution.py:92
  154.4 4.1 %copy-start.2 = (bf16[192,2048]{1,0:T(8,128)(2,1)S(1)}, bf16[192,2048]{1,0:T(8,128)(2,1)}, u32[]{:S(2)}) copy-start(bf16[192,2048]{1,0:T(8,128)(2,1)} %copy-done.1) | copy-start | bytes 2359300
  157.9 2.7 %collective-permute-start.18 = (bf16[192,2048]{1,0:T(8,128)(2,1)S(1)}, bf16[192,2048]{1,0:T(8,128)(2,1)S(1)}, u32[]{:S(2)}, u32[]{:S(2)}) collective-permute-start(bf16[192,2048]{1,0:T(8,128)(2,1)S(1)} %collective-permute-done.12.refs_2_), channel_id=1, source_target_pairs={{0,4},{4,0},{1,5},{5,1},{2,6},{6,2},{3,7},{7,3},{8,12},{12,8},{9,1... | collective-permute-start | bytes 2359304 | tf_op jit(solution)/shard_map/ppermute | solution.py:92
  158.0 3.4 %collective-permute-start.15 = (bf16[192,2048]{1,0:T(8,128)(2,1)S(1)}, bf16[192,2048]{1,0:T(8,128)(2,1)S(1)}, u32[]{:S(2)}, u32[]{:S(2)}) collective-permute-start(bf16[192,2048]{1,0:T(8,128)(2,1)S(1)} %get-tuple-element.63.refs_0_), channel_id=1, source_target_pairs={{0,4},{4,0},{1,5},{5,1},{2,6},{6,2},{3,7},{7,3},{8,12},{12,8},{9,1... | collective-permute-start | bytes 2359304 | tf_op jit(solution)/shard_map/ppermute | solution.py:92
  158.5 4.0 %collective-permute-start.16 = (bf16[192,2048]{1,0:T(8,128)(2,1)S(1)}, bf16[192,2048]{1,0:T(8,128)(2,1)S(1)}, u32[]{:S(2)}, u32[]{:S(2)}) collective-permute-start(bf16[192,2048]{1,0:T(8,128)(2,1)S(1)} %copy-done.2), channel_id=1, source_target_pairs={{0,4},{4,0},{1,5},{5,1},{2,6},{6,2},{3,7},{7,3},{8,12},{12,8},{9,1... | collective-permute-start | bytes 2359304 | tf_op jit(solution)/shard_map/ppermute | solution.py:92
  158.5 7.7 %collective-permute-start.13 = (bf16[128,768]{1,0:T(8,128)(2,1)S(1)}, bf16[128,768]{1,0:T(8,128)(2,1)S(1)}, u32[]{:S(2)}, u32[]{:S(2)}) collective-permute-start(bf16[128,768]{1,0:T(8,128)(2,1)S(1)} %get-tuple-element.62.other), channel_id=1, source_target_pairs={{0,16},{16,0},{1,17},{17,1},{2,18},{18,2},{3,19},{19,3},{4,20},{20... | collective-permute-start | bytes 589832 | tf_op jit(solution)/shard_map/ppermute | solution.py:92
  159.1 11.0 %collective-permute-start.14 = (bf16[128,768]{1,0:T(8,128)(2,1)S(1)}, bf16[128,768]{1,0:T(8,128)(2,1)S(1)}, u32[]{:S(2)}, u32[]{:S(2)}) collective-permute-start(bf16[128,768]{1,0:T(8,128)(2,1)S(1)} %get-tuple-element.61.own), channel_id=1, source_target_pairs={{0,16},{16,0},{1,17},{17,1},{2,18},{18,2},{3,19},{19,3},{4,20},{20... | collective-permute-start | bytes 589832 | tf_op jit(solution)/shard_map/ppermute | solution.py:92
  201.9 5.4 %copy-start.4 = (bf16[32,4096]{1,0:T(8,128)(2,1)S(1)}, bf16[32,4096]{1,0:T(8,128)(2,1)}, u32[]{:S(2)}) copy-start(bf16[32,4096]{1,0:T(8,128)(2,1)} %copy-done.3) | copy-start | bytes 786436
  201.9 5.4 %copy-start.7 = (f32[4096]{0:T(1024)S(1)}, f32[4096]{0:T(1024)}, u32[]{:S(2)}) copy-start(f32[4096]{0:T(1024)} %param.34) | copy-start | bytes 49156
  202.1 5.0 %collective-permute-start.19 = (bf16[32,2048]{1,0:T(8,128)(2,1)S(1)}, bf16[32,2048]{1,0:T(8,128)(2,1)S(1)}, u32[]{:S(2)}, u32[]{:S(2)}) collective-permute-start(bf16[32,2048]{1,0:T(8,128)(2,1)S(1)} %slice.14), channel_id=1, source_target_pairs={{0,16},{16,0},{1,17},{17,1},{2,18},{18,2},{3,19},{19,3},{4,20},{20... | collective-permute-start | bytes 393224 | tf_op jit(solution)/shard_map/ppermute | solution.py:92

commit v8 on v6

--- a/solution.py
+++ b/solution.py
@@ -235,8 +235,7 @@
             out[:, at] = part[k * tok_dev : (k + 1) * tok_dev]
 
 
-def hidden_kernel(states, gate_rows, up_rows, hidden_own, hidden_other):
-    half = hidden_own.shape[0]
+def hidden_kernel(states, gate_rows, up_rows, out):
     step = 256
     for start in range(0, gate_rows.shape[0], step):
         at = slice(start, start + step)
@@ -246,9 +245,8 @@
         up_act = lax.dot_general(
             states[...], up_rows[at, :], NT, preferred_element_type=jnp.float32
         )
-        hidden = (gate_act / (1.0 + jnp.exp(-gate_act)) * up_act).astype(jnp.bfloat16)
-        hidden_own[:, at] = hidden[:half]
-        hidden_other[:, at] = hidden[half:]
+        hidden = gate_act / (1.0 + jnp.exp(-gate_act)) * up_act
+        out[:, at] = hidden.astype(jnp.bfloat16)
 
 
 def down_kernel(own, other, far_own, far_other, near_rows, far_rows, out_0, out_1, out_2, out_3):
@@ -305,29 +303,31 @@
     near = lax.dynamic_slice_in_dim(down_rows, y * half, half, axis=1)
     far = exchange(lax.dynamic_slice_in_dim(down_rows, (1 - y) * half, half, axis=1), "y")
     near_x, far_x = exchange(near, "x"), exchange(far, "x")
-    attn_own, gate_x, near, far = together(line_scatter(parts), gate_x, near, far)
+    attn_own, near, far = together(line_scatter(parts), near, far)
     residual_own = add_normed(layer_input, attn_own, gains[0])
-    *line, other = together(*line_gather(residual_own), exchange(residual_own, "y"))
-    *line, gate_x, up_x, near_x = together(*line, gate_x, up_x, near_x)
+    own, *line, other = together(*line_gather(residual_own), exchange(residual_own, "y"))
+    line, gate_x, up_x, near_x = together(jnp.concatenate(line), gate_x, up_x, near_x)
     (gate_all,) = staged(four_pieces(gate_rows, gate_x, in_hbm))
     (up_all,) = staged(four_pieces(up_rows, up_x, in_hbm))
-    *others, gate_all, up_all, far_x = together(
-        *[exchange(rows, "y") for rows in line[1:]], gate_all, up_all, far_x
-    )
-    group = jax.ShapeDtypeStruct((4 * tok_dev, 4 * gate_rows.shape[0]), jnp.bfloat16)
-    hidden_own, hidden_other = vmem_call(
-        hidden_kernel,
-        [group] * 2,
-        [],
-        [jnp.concatenate([*line, other, *others]), gate_all, up_all],
-        8,
-    )
-    hidden_own, hidden_other, near_x, far_x = together(hidden_own, hidden_other, near_x, far_x)
+
+    def hidden_units_of(first, others):
+        (hidden,) = vmem_call(
+            hidden_kernel,
+            [jax.ShapeDtypeStruct((4 * tok_dev, gate_all.shape[0]), jnp.bfloat16)],
+            [],
+            [jnp.concatenate([first, others]), gate_all, up_all],
+            8,
+        )
+        return hidden
+
+    line_other = exchange(line, "y")
+    hidden_own = hidden_units_of(own, line)
+    line_other, hidden_own, far_x = together(line_other, hidden_own, far_x)
+    from_own = exchange(hidden_own, "y")
+    hidden_other = hidden_units_of(other, line_other)
+    from_other = exchange(hidden_other, "y")
     (near_all,) = staged(four_pieces(near, near_x))
     (far_all,) = staged(four_pieces(far, far_x))
-    from_other, from_own, near_all, far_all = together(
-        exchange(hidden_other, "y"), exchange(hidden_own, "y"), near_all, far_all
-    )
     parts = vmem_call(
         down_kernel,
         [jax.ShapeDtypeStruct((2 * tok_dev, half), jnp.bfloat16)] * 4,

time: 165 us -> 163 us (0.988)
  the two profiles are of different devices: /device:TPU:0 before, /device:TPU:8 now
where the time goes in v8:
time: 163 us
  waiting for transfers between devices  99.4 us (61%)
  starting transfers between devices  30.9 us (19%)
  Pallas kernels  25.9 us (16%)
  other arithmetic  5.89 us (4%)
    ppermute x12, waiting for transfers between devices, shift(): return lax.ppermute(block, 'mlp', [((k + hops) % 4, k) for k in range(4)])  60.8 us
    ppermute x18, waiting for transfers between devices, exchange(): return lax.ppermute(block, axis, [(0, 1), (1, 0)])  38.7 us
    ppermute x12, starting transfers between devices, shift(): return lax.ppermute(block, 'mlp', [((k + hops) % 4, k) for k in range(4)])  16.8 us
    pallas_call x4, Pallas kernels, vmem_call(): pl.pallas_call(kernel, out_shape=outs, in_specs=[whole] * len(operands),...  15.9 us
    ppermute x18, starting transfers between devices, exchange(): return lax.ppermute(block, axis, [(0, 1), (1, 0)])  14.1 us
    pallas_call x5, Pallas kernels, staged(): pl.pallas_call(kernel, out_shape=[pltpu.VMEM(shape, group[0].dtype) for s...  9.99 us
  transfers between devices with their start and end apart: 30, of which 22 were waited for; matrix products, arithmetic and copies ran while one was open for 3% of the time, Pallas kernels for 15%

profile of v8, /device:TPU:8, one launch (start us, length us, event | category | flops | bytes accessed | tf_op | source)
XLA Modules:
  0.0 162.6 jit_solution(12090598870862178984)
XLA Ops:
  0.0 3.0 %collective-permute-start.1 = (bf16[32,4096]{1,0:T(8,128)(2,1)}, bf16[32,4096]{1,0:T(8,128)(2,1)}, u32[]{:S(2)}, u32[]{:S(2)}) collective-permute-start(bf16[32,4096]{1,0:T(8,128)(2,1)} %refs_10_.1), channel_id=1, source_target_pairs={{2,0},{3,1},{0,2},{1,3},{6,4},{7,5},{4,6},{5,7},{10,8},{11,9},{8,1... | collective-permute-start | bytes 786440 | tf_op jit(solution)/shard_map/ppermute | solution.py:96
  3.0 2.5 %collective-permute-start.2 = (bf16[32,4096]{1,0:T(8,128)(2,1)}, bf16[32,4096]{1,0:T(8,128)(2,1)}, u32[]{:S(2)}, u32[]{:S(2)}) collective-permute-start(bf16[32,4096]{1,0:T(8,128)(2,1)} %refs_10_.1), channel_id=1, source_target_pairs={{3,0},{0,1},{1,2},{2,3},{7,4},{4,5},{5,6},{6,7},{11,8},{8,9},{9,10... | collective-permute-start | bytes 786440 | tf_op jit(solution)/shard_map/ppermute | solution.py:96
  5.5 1.5 collective-permute-start.11
  7.0 0.5 collective-permute-start.12
  7.6 0.8 reduce-window.4
  8.4 0.7 fusion.6
  9.1 0.7 select_reduce_fusion.1
  10.1 0.7 select_reduce_fusion
  11.5 6.6 %shard_map.181 = (bf16[4096,512]{1,0:T(8,128)(2,1)S(1)}, bf16[4096,512]{1,0:T(8,128)(2,1)S(1)}, bf16[4096,512]{1,0:T(8,128)(2,1)S(1)}, bf16[512,4096]{1,0:T(8,12...) custom-call(bf16[4096,512]{1,0:T(8,128)(2,1)} %refs_0_.1, ...), custom_call_target="tpu_custom_call" | custom-call | bytes 38805504 | tf_op jit(solution)/shard_map/pallas_call | solution.py:154
  18.2 2.4 %collective-permute-done.block_1 = bf16[32,4096]{1,0:T(8,128)(2,1)S(1)} collective-permute-done((bf16[32,4096]{1,0:T(8,128)(2,1)}, bf16[32,4096]{1,0:T(8,128)(2,1)S(1)}, u32[]{:S(2)}, u32[]{:S(2)}) %collective-permute-start) | collective-permute-done | bytes 262176 | tf_op jit(solution)/shard_map/ppermute | solution.py:96
  20.8 4.7 %collective-permute-done.2.block_3 = bf16[32,4096]{1,0:T(8,128)(2,1)} collective-permute-done((bf16[32,4096]{1,0:T(8,128)(2,1)}, bf16[32,4096]{1,0:T(8,128)(2,1)}, u32[]{:S(2)}, u32[]{:S(2)}) %collective-permute-start.2) | collective-permute-done | bytes 262176 | tf_op jit(solution)/shard_map/ppermute | solution.py:96
  25.5 5.5 %shard_map.182 = (bf16[32,4096]{1,0:T(8,128)(2,1)S(1)}, bf16[32,4096]{1,0:T(8,128)(2,1)S(1)}, bf16[32,4096]{1,0:T(8,128)(2,1)S(1)}, bf16[32,4096]{1,0:T(8,128)(2,1)S(1)}) custom-call(bf16[32,4096]{1,0:T(8,128)(2,1)S(1)} %get-tuple-element.44.block_0, bf16[32,4096]{1,0:T(8,128)(2,1)S(1)} %collective-permute-done.block_1, ...), custom_call_target="tpu_custom_call" | custom-call | flops 1048576 | bytes 1048576 | tf_op jit(solution)/shard_map/pallas_call | solution.py:120
  31.0 2.5 %collective-permute-start.5 = (bf16[32,4096]{1,0:T(8,128)(2,1)S(1)}, bf16[32,4096]{1,0:T(8,128)(2,1)S(1)}, u32[]{:S(2)}, u32[]{:S(2)}) collective-permute-start(bf16[32,4096]{1,0:T(8,128)(2,1)S(1)} %get-tuple-element.62), channel_id=1, source_target_pairs={{3,0},{0,1},{1,2},{2,3},{7,4},{4,5},{5,6},{6,7},{11,8},{8,9},{9,10... | collective-permute-start | bytes 786440 | tf_op jit(solution)/shard_map/ppermute | solution.py:96
  33.6 1.0 collective-permute-start.4
  35.2 16.3 %collective-permute-done.5 = bf16[32,4096]{1,0:T(8,128)(2,1)S(1)} collective-permute-done((bf16[32,4096]{1,0:T(8,128)(2,1)S(1)}, bf16[32,4096]{1,0:T(8,128)(2,1)S(1)}, u32[]{:S(2)}, u32[]{:S(2)}) %collective-permute-start.5) | collective-permute-done | bytes 262176 | tf_op jit(solution)/shard_map/ppermute | solution.py:96
  51.6 1.5 collective-permute-start.6
  53.1 2.3 %collective-permute-done.4 = bf16[32,4096]{1,0:T(8,128)(2,1)S(1)} collective-permute-done((bf16[32,4096]{1,0:T(8,128)(2,1)S(1)}, bf16[32,4096]{1,0:T(8,128)(2,1)S(1)}, u32[]{:S(2)}, u32[]{:S(2)}) %collective-permute-start.4) | collective-permute-done | bytes 262176 | tf_op jit(solution)/shard_map/ppermute | solution.py:96
  55.4 1.2 collective-permute-done.3
  56.7 6.8 %collective-permute-done.6.refs_0_ = bf16[192,2048]{1,0:T(8,128)(2,1)S(1)} collective-permute-done((bf16[192,2048]{1,0:T(8,128)(2,1)S(1)}, bf16[192,2048]{1,0:T(8,128)(2,1)S(1)}, u32[]{:S(2)}, u32[]{:S(2)}) %collective-permute-start.6) | collective-permute-done | bytes 786464 | tf_op jit(solution)/shard_map/ppermute | solution.py:92
  64.0 3.9 %collective-permute-start.8 = (bf16[32,4096]{1,0:T(8,128)(2,1)S(1)}, bf16[32,4096]{1,0:T(8,128)(2,1)S(1)}, u32[]{:S(2)}, u32[]{:S(2)}) collective-permute-start(bf16[32,4096]{1,0:T(8,128)(2,1)S(1)} %add_convert_fusion.1), channel_id=1, source_target_pairs={{2,0},{3,1},{0,2},{1,3},{6,4},{7,5},{4,6},{5,7},{10,8},{11,9},{8,1... | collective-permute-start | bytes 786440 | tf_op jit(solution)/shard_map/ppermute | solution.py:96
  67.9 1.5 collective-permute-start.13
  69.4 7.2 %collective-permute-done.7 = bf16[32,4096]{1,0:T(8,128)(2,1)S(1)} collective-permute-done((bf16[32,4096]{1,0:T(8,128)(2,1)S(1)}, bf16[32,4096]{1,0:T(8,128)(2,1)S(1)}, u32[]{:S(2)}, u32[]{:S(2)}) %collective-permute-start.7) | collective-permute-done | bytes 262176 | tf_op jit(solution)/shard_map/ppermute | solution.py:96
  76.6 0.6 collective-permute-done.8
  77.3 1.5 collective-permute-start.10
  78.8 4.2 %collective-permute-done.9 = bf16[32,4096]{1,0:T(8,128)(2,1)S(1)} collective-permute-done((bf16[32,4096]{1,0:T(8,128)(2,1)S(1)}, bf16[32,4096]{1,0:T(8,128)(2,1)S(1)}, u32[]{:S(2)}, u32[]{:S(2)}) %collective-permute-start.9) | collective-permute-done | bytes 262176 | tf_op jit(solution)/shard_map/ppermute | solution.py:96
  83.0 0.6 collective-permute-done.10
  83.7 7.9 %collective-permute-done.13.refs_2_ = bf16[192,2048]{1,0:T(8,128)(2,1)S(1)} collective-permute-done((bf16[192,2048]{1,0:T(8,128)(2,1)S(1)}, bf16[192,2048]{1,0:T(8,128)(2,1)S(1)}, u32[]{:S(2)}, u32[]{:S(2)}) %collective-permute-start.13) | collective-permute-done | bytes 786464 | tf_op jit(solution)/shard_map/ppermute | solution.py:92
  92.2 1.5 collective-permute-start.19
  93.7 1.5 collective-permute-start.14
  95.3 1.5 shard_map.183.gate_rows
  97.4 2.1 %collective-permute-done.18.refs_3_ = bf16[192,4096]{1,0:T(8,128)(2,1)S(1)} collective-permute-done((bf16[192,4096]{1,0:T(8,128)(2,1)S(1)}, bf16[192,4096]{1,0:T(8,128)(2,1)S(1)}, u32[]{:S(2)}, u32[]{:S(2)}) %collective-permute-start.18) | collective-permute-done | bytes 1572896 | tf_op jit(solution)/shard_map/ppermute | solution.py:92
  99.6 1.4 shard_map.184.up_rows
  101.1 4.3 %shard_map.185.own = bf16[128,768]{1,0:T(8,128)(2,1)S(1)} custom-call(bf16[128,4096]{1,0:T(8,128)(2,1)S(1)} %pad_maximum_fusion.states, bf16[768,4096]{1,0:T(8,128)(2,1)S(1)} %shard_map.183.gate_rows, bf16[768,4096]{1,0:T(8,128)(2,1)S(1)} %shard_map.184.up_rows), custom_call_target="tpu_custom_call" | custom-call | flops 1048576 | bytes 1048576 | tf_op jit(solution)/shard_map/pallas_call | solution.py:120
  105.4 6.7 %collective-permute-done.19.refs_2_ = bf16[192,2048]{1,0:T(8,128)(2,1)S(1)} collective-permute-done((bf16[192,2048]{1,0:T(8,128)(2,1)S(1)}, bf16[192,2048]{1,0:T(8,128)(2,1)S(1)}, u32[]{:S(2)}, u32[]{:S(2)}) %collective-permute-start.19) | collective-permute-done | bytes 786464 | tf_op jit(solution)/shard_map/ppermute | solution.py:92
  112.1 1.2 collective-permute-done.14
  113.4 4.3 %shard_map.186.other = bf16[128,768]{1,0:T(8,128)(2,1)S(1)} custom-call(bf16[128,4096]{1,0:T(8,128)(2,1)S(1)} %pad_maximum_fusion.1.states, bf16[768,4096]{1,0:T(8,128)(2,1)S(1)} %shard_map.183.gate_rows, bf16[768,4096]{1,0:T(8,128)(2,1)S(1)} %shard_map.184.up_rows), custom_call_target="tpu_custom_call" | custom-call | flops 1048576 | bytes 1048576 | tf_op jit(solution)/shard_map/pallas_call | solution.py:120
  117.7 1.6 collective-permute-start.20
  120.3 5.1 %collective-permute-done.20.far_own = bf16[128,768]{1,0:T(8,128)(2,1)S(1)} collective-permute-done((bf16[128,768]{1,0:T(8,128)(2,1)S(1)}, bf16[128,768]{1,0:T(8,128)(2,1)S(1)}, u32[]{:S(2)}, u32[]{:S(2)}) %collective-permute-start.20) | collective-permute-done | bytes 196640 | tf_op jit(solution)/shard_map/ppermute | solution.py:92
  125.5 3.8 %collective-permute-done.21.far_other = bf16[128,768]{1,0:T(8,128)(2,1)S(1)} collective-permute-done((bf16[128,768]{1,0:T(8,128)(2,1)S(1)}, bf16[128,768]{1,0:T(8,128)(2,1)S(1)}, u32[]{:S(2)}, u32[]{:S(2)}) %collective-permute-start.21) | collective-permute-done | bytes 196640 | tf_op jit(solution)/shard_map/ppermute | solution.py:92
  129.3 1.8 %shard_map.189 = (bf16[64,2048]{1,0:T(8,128)(2,1)S(1)}, bf16[64,2048]{1,0:T(8,128)(2,1)S(1)}, bf16[64,2048]{1,0:T(8,128)(2,1)S(1)}, bf16[64,2048]{1,0:T(8,128)(2,1)S(1)}) custom-call(bf16[128,768]{1,0:T(8,128)(2,1)S(1)} %shard_map.185.own, bf16[128,768]{1,0:T(8,128)(2,1)S(1)} %shard_map.186.other, bf16[128,768]{1,0:T(8,128)(2,1)S(1)} %collective-permute-done.20.far_own, ...), custom_call_target="tpu_custom_call" | custom-call | flops 1048576 | bytes 1048576 | tf_op jit(solution)/shard_map/pallas_call | solution.py:120
  131.5 1.6 collective-permute-start.27
  133.1 1.3 collective-permute-start.26
  134.4 6.0 %collective-permute-done.28 = bf16[64,2048]{1,0:T(8,128)(2,1)S(1)} collective-permute-done((bf16[64,2048]{1,0:T(8,128)(2,1)S(1)}, bf16[64,2048]{1,0:T(8,128)(2,1)S(1)}, u32[]{:S(2)}, u32[]{:S(2)}) %collective-permute-start.28) | collective-permute-done | bytes 262176 | tf_op jit(solution)/shard_map/ppermute | solution.py:96
  140.4 13.4 %collective-permute-done.27 = bf16[64,2048]{1,0:T(8,128)(2,1)S(1)} collective-permute-done((bf16[64,2048]{1,0:T(8,128)(2,1)S(1)}, bf16[64,2048]{1,0:T(8,128)(2,1)S(1)}, u32[]{:S(2)}, u32[]{:S(2)}) %collective-permute-start.27) | collective-permute-done | bytes 262176 | tf_op jit(solution)/shard_map/ppermute | solution.py:96
  153.8 2.1 %collective-permute-done.26 = bf16[64,2048]{1,0:T(8,128)(2,1)S(1)} collective-permute-done((bf16[64,2048]{1,0:T(8,128)(2,1)S(1)}, bf16[64,2048]{1,0:T(8,128)(2,1)S(1)}, u32[]{:S(2)}, u32[]{:S(2)}) %collective-permute-start.26) | collective-permute-done | bytes 262176 | tf_op jit(solution)/shard_map/ppermute | solution.py:96
  156.1 1.6 collective-permute-start.29
  157.6 3.9 %collective-permute-done.29 = bf16[32,2048]{1,0:T(8,128)(2,1)S(1)} collective-permute-done((bf16[32,2048]{1,0:T(8,128)(2,1)S(1)}, bf16[32,2048]{1,0:T(8,128)(2,1)S(1)}, u32[]{:S(2)}, u32[]{:S(2)}) %collective-permute-start.29) | collective-permute-done | bytes 131104 | tf_op jit(solution)/shard_map/ppermute | solution.py:92
  161.8 0.9 add_convert_fusion
  (61 shorter events, 5.7 us)
Async XLA Ops:
  0.0 20.6 %collective-permute-start = (bf16[32,4096]{1,0:T(8,128)(2,1)}, bf16[32,4096]{1,0:T(8,128)(2,1)S(1)}, u32[]{:S(2)}, u32[]{:S(2)}) collective-permute-start(bf16[32,4096]{1,0:T(8,128)(2,1)} %refs_10_.1), channel_id=1, source_target_pairs={{1,0},{2,1},{3,2},{0,3},{5,4},{6,5},{7,6},{4,7},{9,8},{10,9},{11,1... | collective-permute-start | bytes 786440 | tf_op jit(solution)/shard_map/ppermute | solution.py:96
  0.0 20.8 %collective-permute-start.1 = (bf16[32,4096]{1,0:T(8,128)(2,1)}, bf16[32,4096]{1,0:T(8,128)(2,1)}, u32[]{:S(2)}, u32[]{:S(2)}) collective-permute-start(bf16[32,4096]{1,0:T(8,128)(2,1)} %refs_10_.1), channel_id=1, source_target_pairs={{2,0},{3,1},{0,2},{1,3},{6,4},{7,5},{4,6},{5,7},{10,8},{11,9},{8,1... | collective-permute-start | bytes 786440 | tf_op jit(solution)/shard_map/ppermute | solution.py:96
  3.0 22.5 %collective-permute-start.2 = (bf16[32,4096]{1,0:T(8,128)(2,1)}, bf16[32,4096]{1,0:T(8,128)(2,1)}, u32[]{:S(2)}, u32[]{:S(2)}) collective-permute-start(bf16[32,4096]{1,0:T(8,128)(2,1)} %refs_10_.1), channel_id=1, source_target_pairs={{3,0},{0,1},{1,2},{2,3},{7,4},{4,5},{5,6},{6,7},{11,8},{8,9},{9,10... | collective-permute-start | bytes 786440 | tf_op jit(solution)/shard_map/ppermute | solution.py:96
  5.5 86.1 %collective-permute-start.11 = (bf16[192,4096]{1,0:T(8,128)(2,1)}, bf16[192,4096]{1,0:T(8,128)(2,1)S(1)}, u32[]{:S(2)}, u32[]{:S(2)}) collective-permute-start(bf16[192,4096]{1,0:T(8,128)(2,1)} %bitcast.14), channel_id=1, source_target_pairs={{0,8},{8,0},{1,9},{9,1},{2,10},{10,2},{3,11},{11,3},{4,12},{12,4},... | collective-permute-start | bytes 4718600 | tf_op jit(solution)/shard_map/ppermute | solution.py:92
  7.0 84.6 %collective-permute-start.12 = (bf16[192,4096]{1,0:T(8,128)(2,1)}, bf16[192,4096]{1,0:T(8,128)(2,1)S(1)}, u32[]{:S(2)}, u32[]{:S(2)}) collective-permute-start(bf16[192,4096]{1,0:T(8,128)(2,1)} %bitcast.17), channel_id=1, source_target_pairs={{0,8},{8,0},{1,9},{9,1},{2,10},{10,2},{3,11},{11,3},{4,12},{12,4},... | collective-permute-start | bytes 4718600 | tf_op jit(solution)/shard_map/ppermute | solution.py:92
  11.5 6.6 %copy-start.6 = (s32[128]{0:T(128)S(1)}, s32[128]{0:T(128)}, u32[]{:S(2)}) copy-start(s32[128]{0:T(128)} %and_select_fusion) | copy-start | bytes 1540
  25.5 9.6 %copy-start.2 = (bf16[4096,192]{0,1:T(8,128)(2,1)S(1)}, bf16[4096,192]{0,1:T(8,128)(2,1)}, u32[]{:S(2)}) copy-start(bf16[4096,192]{0,1:T(8,128)(2,1)} %param.37) | copy-start | bytes 4718596
  31.0 32.7 %copy-start.3 = (bf16[32,4096]{1,0:T(8,128)(2,1)S(1)}, bf16[32,4096]{1,0:T(8,128)(2,1)}, u32[]{:S(2)}) copy-start(bf16[32,4096]{1,0:T(8,128)(2,1)} %refs_10_.1) | copy-start | bytes 786436
  31.0 32.7 %copy-start.4 = (f32[4096]{0:T(1024)S(1)}, f32[4096]{0:T(1024)}, u32[]{:S(2)}) copy-start(f32[4096]{0:T(1024)} %param.33) | copy-start | bytes 49156
  31.0 20.5 %collective-permute-start.5 = (bf16[32,4096]{1,0:T(8,128)(2,1)S(1)}, bf16[32,4096]{1,0:T(8,128)(2,1)S(1)}, u32[]{:S(2)}, u32[]{:S(2)}) collective-permute-start(bf16[32,4096]{1,0:T(8,128)(2,1)S(1)} %get-tuple-element.62), channel_id=1, source_target_pairs={{3,0},{0,1},{1,2},{2,3},{7,4},{4,5},{5,6},{6,7},{11,8},{8,9},{9,10... | collective-permute-start | bytes 786440 | tf_op jit(solution)/shard_map/ppermute | solution.py:96
  33.6 21.8 %collective-permute-start.4 = (bf16[32,4096]{1,0:T(8,128)(2,1)S(1)}, bf16[32,4096]{1,0:T(8,128)(2,1)S(1)}, u32[]{:S(2)}, u32[]{:S(2)}) collective-permute-start(bf16[32,4096]{1,0:T(8,128)(2,1)S(1)} %get-tuple-element.61), channel_id=1, source_target_pairs={{2,0},{3,1},{0,2},{1,3},{6,4},{7,5},{4,6},{5,7},{10,8},{11,9},{8,1... | collective-permute-start | bytes 786440 | tf_op jit(solution)/shard_map/ppermute | solution.py:96
  34.6 22.0 %collective-permute-start.3 = (bf16[32,4096]{1,0:T(8,128)(2,1)S(1)}, bf16[32,4096]{1,0:T(8,128)(2,1)S(1)}, u32[]{:S(2)}, u32[]{:S(2)}) collective-permute-start(bf16[32,4096]{1,0:T(8,128)(2,1)S(1)} %get-tuple-element.60), channel_id=1, source_target_pairs={{1,0},{2,1},{3,2},{0,3},{5,4},{6,5},{7,6},{4,7},{9,8},{10,9},{11,1... | collective-permute-start | bytes 786440 | tf_op jit(solution)/shard_map/ppermute | solution.py:96
  35.2 47.8 %copy-start = (bf16[4096,192]{0,1:T(8,128)(2,1)S(1)}, bf16[4096,192]{0,1:T(8,128)(2,1)}, u32[]{:S(2)}) copy-start(bf16[4096,192]{0,1:T(8,128)(2,1)} %param.35) | copy-start | bytes 4718596
  51.6 40.0 %copy-start.1 = (bf16[4096,192]{0,1:T(8,128)(2,1)S(1)}, bf16[4096,192]{0,1:T(8,128)(2,1)}, u32[]{:S(2)}) copy-start(bf16[4096,192]{0,1:T(8,128)(2,1)} %param.36) | copy-start | bytes 4718596
  51.6 12.0 %collective-permute-start.6 = (bf16[192,2048]{1,0:T(8,128)(2,1)S(1)}, bf16[192,2048]{1,0:T(8,128)(2,1)S(1)}, u32[]{:S(2)}, u32[]{:S(2)}) collective-permute-start(bf16[192,2048]{1,0:T(8,128)(2,1)S(1)} %get-tuple-element.88), channel_id=1, source_target_pairs={{0,16},{16,0},{1,17},{17,1},{2,18},{18,2},{3,19},{19,3},{4,20},{20... | collective-permute-start | bytes 2359304 | tf_op jit(solution)/shard_map/ppermute | solution.py:92
  63.9 12.7 %collective-permute-start.7 = (bf16[32,4096]{1,0:T(8,128)(2,1)S(1)}, bf16[32,4096]{1,0:T(8,128)(2,1)S(1)}, u32[]{:S(2)}, u32[]{:S(2)}) collective-permute-start(bf16[32,4096]{1,0:T(8,128)(2,1)S(1)} %add_convert_fusion.1), channel_id=1, source_target_pairs={{1,0},{2,1},{3,2},{0,3},{5,4},{6,5},{7,6},{4,7},{9,8},{10,9},{11,1... | collective-permute-start | bytes 786440 | tf_op jit(solution)/shard_map/ppermute | solution.py:96
  64.0 13.3 %collective-permute-start.8 = (bf16[32,4096]{1,0:T(8,128)(2,1)S(1)}, bf16[32,4096]{1,0:T(8,128)(2,1)S(1)}, u32[]{:S(2)}, u32[]{:S(2)}) collective-permute-start(bf16[32,4096]{1,0:T(8,128)(2,1)S(1)} %add_convert_fusion.1), channel_id=1, source_target_pairs={{2,0},{3,1},{0,2},{1,3},{6,4},{7,5},{4,6},{5,7},{10,8},{11,9},{8,1... | collective-permute-start | bytes 786440 | tf_op jit(solution)/shard_map/ppermute | solution.py:96
  67.9 23.7 %collective-permute-start.13 = (bf16[192,2048]{1,0:T(8,128)(2,1)S(1)}, bf16[192,2048]{1,0:T(8,128)(2,1)S(1)}, u32[]{:S(2)}, u32[]{:S(2)}) collective-permute-start(bf16[192,2048]{1,0:T(8,128)(2,1)S(1)} %get-tuple-element.75.refs_0_), channel_id=1, source_target_pairs={{0,8},{8,0},{1,9},{9,1},{2,10},{10,2},{3,11},{11,3},{4,12},{12,4},... | collective-permute-start | bytes 2359304 | tf_op jit(solution)/shard_map/ppermute | solution.py:92
  76.6 6.4 %collective-permute-start.9 = (bf16[32,4096]{1,0:T(8,128)(2,1)S(1)}, bf16[32,4096]{1,0:T(8,128)(2,1)S(1)}, u32[]{:S(2)}, u32[]{:S(2)}) collective-permute-start(bf16[32,4096]{1,0:T(8,128)(2,1)S(1)} %add_convert_fusion.1), channel_id=1, source_target_pairs={{3,0},{0,1},{1,2},{2,3},{7,4},{4,5},{5,6},{6,7},{11,8},{8,9},{9,10... | collective-permute-start | bytes 786440 | tf_op jit(solution)/shard_map/ppermute | solution.py:96
  77.3 6.4 %collective-permute-start.10 = (bf16[32,4096]{1,0:T(8,128)(2,1)S(1)}, bf16[32,4096]{1,0:T(8,128)(2,1)S(1)}, u32[]{:S(2)}, u32[]{:S(2)}) collective-permute-start(bf16[32,4096]{1,0:T(8,128)(2,1)S(1)} %add_convert_fusion.1), channel_id=1, source_target_pairs={{0,16},{16,0},{1,17},{17,1},{2,18},{18,2},{3,19},{19,3},{4,20},{20... | collective-permute-start | bytes 786440 | tf_op jit(solution)/shard_map/ppermute | solution.py:92
  83.0 10.7 %collective-permute-start.15 = (bf16[192,4096]{1,0:T(8,128)(2,1)S(1)}, bf16[192,4096]{1,0:T(8,128)(2,1)S(1)}, u32[]{:S(2)}, u32[]{:S(2)}) collective-permute-start(bf16[192,4096]{1,0:T(8,128)(2,1)S(1)} %bitcast.16), channel_id=1, source_target_pairs={{0,4},{4,0},{1,5},{5,1},{2,6},{6,2},{3,7},{7,3},{8,12},{12,8},{9,1... | collective-permute-start | bytes 4718600 | tf_op jit(solution)/shard_map/ppermute | solution.py:92
  91.6 3.6 %collective-permute-start.16 = (bf16[192,4096]{1,0:T(8,128)(2,1)S(1)}, bf16[192,4096]{1,0:T(8,128)(2,1)S(1)}, u32[]{:S(2)}, u32[]{:S(2)}) collective-permute-start(bf16[192,4096]{1,0:T(8,128)(2,1)S(1)} %collective-permute-done.11.refs_2_), channel_id=1, source_target_pairs={{0,4},{4,0},{1,5},{5,1},{2,6},{6,2},{3,7},{7,3},{8,12},{12,8},{9,1... | collective-permute-start | bytes 4718600 | tf_op jit(solution)/shard_map/ppermute | solution.py:92
  91.6 5.6 %collective-permute-start.17 = (bf16[192,4096]{1,0:T(8,128)(2,1)S(1)}, bf16[192,4096]{1,0:T(8,128)(2,1)S(1)}, u32[]{:S(2)}, u32[]{:S(2)}) collective-permute-start(bf16[192,4096]{1,0:T(8,128)(2,1)S(1)} %bitcast.19), channel_id=1, source_target_pairs={{0,4},{4,0},{1,5},{5,1},{2,6},{6,2},{3,7},{7,3},{8,12},{12,8},{9,1... | collective-permute-start | bytes 4718600 | tf_op jit(solution)/shard_map/ppermute | solution.py:92
  92.1 7.4 %collective-permute-start.18 = (bf16[192,4096]{1,0:T(8,128)(2,1)S(1)}, bf16[192,4096]{1,0:T(8,128)(2,1)S(1)}, u32[]{:S(2)}, u32[]{:S(2)}) collective-permute-start(bf16[192,4096]{1,0:T(8,128)(2,1)S(1)} %collective-permute-done.12.refs_2_), channel_id=1, source_target_pairs={{0,4},{4,0},{1,5},{5,1},{2,6},{6,2},{3,7},{7,3},{8,12},{12,8},{9,1... | collective-permute-start | bytes 4718600 | tf_op jit(solution)/shard_map/ppermute | solution.py:92
  92.2 19.9 %collective-permute-start.19 = (bf16[192,2048]{1,0:T(8,128)(2,1)S(1)}, bf16[192,2048]{1,0:T(8,128)(2,1)S(1)}, u32[]{:S(2)}, u32[]{:S(2)}) collective-permute-start(bf16[192,2048]{1,0:T(8,128)(2,1)S(1)} %collective-permute-done.6.refs_0_), channel_id=1, source_target_pairs={{0,8},{8,0},{1,9},{9,1},{2,10},{10,2},{3,11},{11,3},{4,12},{12,4},... | collective-permute-start | bytes 2359304 | tf_op jit(solution)/shard_map/ppermute | solution.py:92
  93.7 19.6 %collective-permute-start.14 = (bf16[96,4096]{1,0:T(8,128)(2,1)S(1)}, bf16[96,4096]{1,0:T(8,128)(2,1)S(1)}, u32[]{:S(2)}, u32[]{:S(2)}) collective-permute-start(bf16[96,4096]{1,0:T(8,128)(2,1)S(1)} %pad_maximum_fusion.2), channel_id=1, source_target_pairs={{0,16},{16,0},{1,17},{17,1},{2,18},{18,2},{3,19},{19,3},{4,20},{20... | collective-permute-start | bytes 2359304 | tf_op jit(solution)/shard_map/ppermute | solution.py:92
  95.2 24.1 %collective-permute-start.22 = (bf16[192,2048]{1,0:T(8,128)(2,1)S(1)}, bf16[192,2048]{1,0:T(8,128)(2,1)S(1)}, u32[]{:S(2)}, u32[]{:S(2)}) collective-permute-start(bf16[192,2048]{1,0:T(8,128)(2,1)S(1)} %get-tuple-element.75.refs_0_), channel_id=1, source_target_pairs={{0,4},{4,0},{1,5},{5,1},{2,6},{6,2},{3,7},{7,3},{8,12},{12,8},{9,1... | collective-permute-start | bytes 2359304 | tf_op jit(solution)/shard_map/ppermute | solution.py:92
  97.2 22.8 %collective-permute-start.24 = (bf16[192,2048]{1,0:T(8,128)(2,1)S(1)}, bf16[192,2048]{1,0:T(8,128)(2,1)S(1)}, u32[]{:S(2)}, u32[]{:S(2)}) collective-permute-start(bf16[192,2048]{1,0:T(8,128)(2,1)S(1)} %collective-permute-done.6.refs_0_), channel_id=1, source_target_pairs={{0,4},{4,0},{1,5},{5,1},{2,6},{6,2},{3,7},{7,3},{8,12},{12,8},{9,1... | collective-permute-start | bytes 2359304 | tf_op jit(solution)/shard_map/ppermute | solution.py:92
  99.5 20.3 %collective-permute-start.23 = (bf16[192,2048]{1,0:T(8,128)(2,1)S(1)}, bf16[192,2048]{1,0:T(8,128)(2,1)S(1)}, u32[]{:S(2)}, u32[]{:S(2)}) collective-permute-start(bf16[192,2048]{1,0:T(8,128)(2,1)S(1)} %collective-permute-done.13.refs_2_), channel_id=1, source_target_pairs={{0,4},{4,0},{1,5},{5,1},{2,6},{6,2},{3,7},{7,3},{8,12},{12,8},{9,1... | collective-permute-start | bytes 2359304 | tf_op jit(solution)/shard_map/ppermute | solution.py:92
  113.3 6.8 %collective-permute-start.25 = (bf16[192,2048]{1,0:T(8,128)(2,1)S(1)}, bf16[192,2048]{1,0:T(8,128)(2,1)S(1)}, u32[]{:S(2)}, u32[]{:S(2)}) collective-permute-start(bf16[192,2048]{1,0:T(8,128)(2,1)S(1)} %collective-permute-done.19.refs_2_), channel_id=1, source_target_pairs={{0,4},{4,0},{1,5},{5,1},{2,6},{6,2},{3,7},{7,3},{8,12},{12,8},{9,1... | collective-permute-start | bytes 2359304 | tf_op jit(solution)/shard_map/ppermute | solution.py:92
  117.7 7.8 %collective-permute-start.20 = (bf16[128,768]{1,0:T(8,128)(2,1)S(1)}, bf16[128,768]{1,0:T(8,128)(2,1)S(1)}, u32[]{:S(2)}, u32[]{:S(2)}) collective-permute-start(bf16[128,768]{1,0:T(8,128)(2,1)S(1)} %shard_map.186.other), channel_id=1, source_target_pairs={{0,16},{16,0},{1,17},{17,1},{2,18},{18,2},{3,19},{19,3},{4,20},{20... | collective-permute-start | bytes 589832 | tf_op jit(solution)/shard_map/ppermute | solution.py:92
  119.3 10.0 %collective-permute-start.21 = (bf16[128,768]{1,0:T(8,128)(2,1)S(1)}, bf16[128,768]{1,0:T(8,128)(2,1)S(1)}, u32[]{:S(2)}, u32[]{:S(2)}) collective-permute-start(bf16[128,768]{1,0:T(8,128)(2,1)S(1)} %shard_map.185.own), channel_id=1, source_target_pairs={{0,16},{16,0},{1,17},{17,1},{2,18},{18,2},{3,19},{19,3},{4,20},{20... | collective-permute-start | bytes 589832 | tf_op jit(solution)/shard_map/ppermute | solution.py:92
  131.1 30.6 %copy-start.5 = (f32[4096]{0:T(1024)S(1)}, f32[4096]{0:T(1024)}, u32[]{:S(2)}) copy-start(f32[4096]{0:T(1024)} %param.34) | copy-start | bytes 49156
  131.1 9.3 %collective-permute-start.28 = (bf16[64,2048]{1,0:T(8,128)(2,1)S(1)}, bf16[64,2048]{1,0:T(8,128)(2,1)S(1)}, u32[]{:S(2)}, u32[]{:S(2)}) collective-permute-start(bf16[64,2048]{1,0:T(8,128)(2,1)S(1)} %get-tuple-element.82), channel_id=1, source_target_pairs={{3,0},{0,1},{1,2},{2,3},{7,4},{4,5},{5,6},{6,7},{11,8},{8,9},{9,10... | collective-permute-start | bytes 786440 | tf_op jit(solution)/shard_map/ppermute | solution.py:96
  131.5 22.3 %collective-permute-start.27 = (bf16[64,2048]{1,0:T(8,128)(2,1)S(1)}, bf16[64,2048]{1,0:T(8,128)(2,1)S(1)}, u32[]{:S(2)}, u32[]{:S(2)}) collective-permute-start(bf16[64,2048]{1,0:T(8,128)(2,1)S(1)} %get-tuple-element.81), channel_id=1, source_target_pairs={{2,0},{3,1},{0,2},{1,3},{6,4},{7,5},{4,6},{5,7},{10,8},{11,9},{8,1... | collective-permute-start | bytes 786440 | tf_op jit(solution)/shard_map/ppermute | solution.py:96
  133.1 22.8 %collective-permute-start.26 = (bf16[64,2048]{1,0:T(8,128)(2,1)S(1)}, bf16[64,2048]{1,0:T(8,128)(2,1)S(1)}, u32[]{:S(2)}, u32[]{:S(2)}) collective-permute-start(bf16[64,2048]{1,0:T(8,128)(2,1)S(1)} %get-tuple-element.80), channel_id=1, source_target_pairs={{1,0},{2,1},{3,2},{0,3},{5,4},{6,5},{7,6},{4,7},{9,8},{10,9},{11,1... | collective-permute-start | bytes 786440 | tf_op jit(solution)/shard_map/ppermute | solution.py:96
  156.1 5.5 %collective-permute-start.29 = (bf16[32,2048]{1,0:T(8,128)(2,1)S(1)}, bf16[32,2048]{1,0:T(8,128)(2,1)S(1)}, u32[]{:S(2)}, u32[]{:S(2)}) collective-permute-start(bf16[32,2048]{1,0:T(8,128)(2,1)S(1)} %slice.14), channel_id=1, source_target_pairs={{0,16},{16,0},{1,17},{17,1},{2,18},{18,2},{3,19},{19,3},{4,20},{20... | collective-permute-start | bytes 393224 | tf_op jit(solution)/shard_map/ppermute | solution.py:92

commit v9 on v8

--- a/solution.py
+++ b/solution.py
@@ -111,8 +111,8 @@
     return lax.optimization_barrier(values)
 
 
-def four_pieces(rows, rows_x, place=lambda rows: rows):
-    return [place(rows), exchange(rows, "core"), rows_x, exchange(rows_x, "core")]
+def four_pieces(rows, rows_x):
+    return [rows, exchange(rows, "core"), rows_x, exchange(rows_x, "core")]
 
 
 def vmem_call(kernel, outs, scratch, operands, vmem_mib):
@@ -133,32 +133,48 @@
 
 
 def staged(*groups):
-    arrays = [array for group in groups for array in group]
+    groups = [
+        [piece if isinstance(piece, tuple) else (piece, 0, piece.shape[0]) for piece in group]
+        for group in groups
+    ]
+    arrays = []
+    for piece in (piece for group in groups for piece in group):
+        if not any(piece[0] is array for array in arrays):
+            arrays.append(piece[0])
+    places = [
+        [next(k for k, array in enumerate(arrays) if array is piece[0]) for piece in group]
+        for group in groups
+    ]
+    count = sum(len(group) for group in groups)
 
     def kernel(*refs):
         sources, targets, sems = refs[: len(arrays)], refs[len(arrays) : -1], refs[-1]
         copies = []
-        for group, target in zip(groups, targets):
-            start = 0
-            for array in group:
-                at = len(copies)
-                rows = target.at[pl.ds(start, array.shape[0]), :]
-                copies.append(pltpu.make_async_copy(sources[at], rows, sems.at[at]))
+        for group, place, target in zip(groups, places, targets):
+            at = 0
+            for (_, start, rows), k in zip(group, place):
+                copies.append(
+                    pltpu.make_async_copy(
+                        sources[k].at[pl.ds(start, rows), :],
+                        target.at[pl.ds(at, rows), :],
+                        sems.at[len(copies)],
+                    )
+                )
                 copies[-1].start()
-                start += array.shape[0]
+                at += rows
         for copy in copies:
             copy.wait()
 
-    outs = [(sum(array.shape[0] for array in group), group[0].shape[1]) for group in groups]
-    size = sum(array.size * array.dtype.itemsize for array in arrays)
+    outs = [(sum(piece[2] for piece in group), group[0][0].shape[1]) for group in groups]
+    size = sum(rows * columns for rows, columns in outs)
     return pl.pallas_call(
         kernel,
-        out_shape=[pltpu.VMEM(shape, group[0].dtype) for shape, group in zip(outs, groups)],
+        out_shape=[pltpu.VMEM(shape, group[0][0].dtype) for shape, group in zip(outs, groups)],
         in_specs=[pl.BlockSpec(memory_space=pl.ANY)] * len(arrays),
         out_specs=[pl.BlockSpec(memory_space=pltpu.VMEM)] * len(groups),
-        scratch_shapes=[pltpu.SemaphoreType.DMA((len(arrays),))],
+        scratch_shapes=[pltpu.SemaphoreType.DMA((count,))],
         compiler_params=pltpu.CompilerParams(vmem_limit_bytes=1 << 20),
-        cost_estimate=pl.CostEstimate(flops=0, bytes_accessed=2 * size, transcendentals=0),
+        cost_estimate=pl.CostEstimate(flops=0, bytes_accessed=4 * size, transcendentals=0),
     )(*arrays)
 
 
@@ -275,7 +291,9 @@
     gate_rows, up_rows, down_rows = ffn_rows
     y = lax.axis_index("y")
     half = width // 2
-    gate_x, up_x = exchange(gate_rows, "x"), exchange(up_rows, "x")
+    units = gate_rows.shape[0]
+    (gate_up,) = staged([in_hbm(gate_rows), in_hbm(up_rows)])
+    gate_up_x = exchange(gate_up, "x")
     cosine, sine = jnp.cos(angles), jnp.sin(angles)
     block = jax.ShapeDtypeStruct((tok_dev, width), jnp.bfloat16)
     *staged_rows, own_block = staged(
@@ -306,9 +324,12 @@
     attn_own, near, far = together(line_scatter(parts), near, far)
     residual_own = add_normed(layer_input, attn_own, gains[0])
     own, *line, other = together(*line_gather(residual_own), exchange(residual_own, "y"))
-    line, gate_x, up_x, near_x = together(jnp.concatenate(line), gate_x, up_x, near_x)
-    (gate_all,) = staged(four_pieces(gate_rows, gate_x, in_hbm))
-    (up_all,) = staged(four_pieces(up_rows, up_x, in_hbm))
+    line, gate_up_x, near_x = together(jnp.concatenate(line), gate_up_x, near_x)
+    pieces = [exchange(gate_up, "core"), gate_up_x, exchange(gate_up_x, "core")]
+    gate_all, up_all = staged(
+        [in_hbm(gate_rows), *((piece, 0, units) for piece in pieces)],
+        [in_hbm(up_rows), *((piece, units, units) for piece in pieces)],
+    )
 
     def hidden_units_of(first, others):
         (hidden,) = vmem_call(

time: 163 us -> 166 us (1.018)
  the two profiles are of different devices: /device:TPU:8 before, /device:TPU:0 now
where the time goes in v9:
time: 166 us
  waiting for transfers between devices  105 us (63%)
  starting transfers between devices  28.8 us (17%)
  Pallas kernels  27.9 us (17%)
  other arithmetic  3.27 us (2%)
    ppermute x12, waiting for transfers between devices, shift(): return lax.ppermute(block, 'mlp', [((k + hops) % 4, k) for k in range(4)])  70.2 us
    ppermute x15, waiting for transfers between devices, exchange(): return lax.ppermute(block, axis, [(0, 1), (1, 0)])  35.2 us
    pallas_call x4, Pallas kernels, vmem_call(): pl.pallas_call(kernel, out_shape=outs, in_specs=[whole] * len(operands),...  15.9 us
    ppermute x12, starting transfers between devices, shift(): return lax.ppermute(block, 'mlp', [((k + hops) % 4, k) for k in range(4)])  15.2 us
    ppermute x15, starting transfers between devices, exchange(): return lax.ppermute(block, axis, [(0, 1), (1, 0)])  13.6 us
    pallas_call x5, Pallas kernels, staged(): pl.pallas_call(kernel, out_shape=[pltpu.VMEM(shape, group[0][0].dtype) fo...  12 us
  transfers between devices with their start and end apart: 27, of which 15 were waited for; matrix products, arithmetic and copies ran while one was open for 1% of the time, Pallas kernels for 16%

profile of v9, /device:TPU:0, one launch (start us, length us, event | category | flops | bytes accessed | tf_op | source)
XLA Modules:
  0.0 166.0 jit_solution(9951562233343376311)
XLA Ops:
  0.0 5.0 %collective-permute-start = (bf16[32,4096]{1,0:T(8,128)(2,1)}, bf16[32,4096]{1,0:T(8,128)(2,1)S(1)}, u32[]{:S(2)}, u32[]{:S(2)}) collective-permute-start(bf16[32,4096]{1,0:T(8,128)(2,1)} %refs_10_.1), channel_id=1, source_target_pairs={{1,0},{2,1},{3,2},{0,3},{5,4},{6,5},{7,6},{4,7},{9,8},{10,9},{11,1... | collective-permute-start | bytes 786440 | tf_op jit(solution)/shard_map/ppermute | solution.py:96
  5.1 1.0 collective-permute-start.2
  6.1 1.9 %shard_map.183 = bf16[384,4096]{1,0:T(8,128)(2,1)S(1)} custom-call(bf16[192,4096]{1,0:T(8,128)(2,1)} %bitcast.14, bf16[192,4096]{1,0:T(8,128)(2,1)} %bitcast.16), custom_call_target="tpu_custom_call" | custom-call | bytes 6291456 | tf_op jit(solution)/shard_map/pallas_call | solution.py:170
  8.0 1.6 collective-permute-start.11
  9.6 0.2 reduce-window.4
  9.9 0.3 fusion.4
  10.4 0.5 and_select_fusion
  10.9 6.6 %shard_map.181 = (bf16[4096,512]{1,0:T(8,128)(2,1)S(1)}, bf16[4096,512]{1,0:T(8,128)(2,1)S(1)}, bf16[4096,512]{1,0:T(8,128)(2,1)S(1)}, bf16[512,4096]{1,0:T(8,12...) custom-call(bf16[4096,512]{1,0:T(8,128)(2,1)} %refs_0_.1, ...), custom_call_target="tpu_custom_call" | custom-call | bytes 38801408 | tf_op jit(solution)/shard_map/pallas_call | solution.py:170
  17.7 10.0 %collective-permute-done.1.block_2 = bf16[32,4096]{1,0:T(8,128)(2,1)} collective-permute-done((bf16[32,4096]{1,0:T(8,128)(2,1)}, bf16[32,4096]{1,0:T(8,128)(2,1)}, u32[]{:S(2)}, u32[]{:S(2)}) %collective-permute-start.1) | collective-permute-done | bytes 262176 | tf_op jit(solution)/shard_map/ppermute | solution.py:96
  27.7 5.5 %shard_map.182 = (bf16[32,4096]{1,0:T(8,128)(2,1)S(1)}, bf16[32,4096]{1,0:T(8,128)(2,1)S(1)}, bf16[32,4096]{1,0:T(8,128)(2,1)S(1)}, bf16[32,4096]{1,0:T(8,128)(2,1)S(1)}) custom-call(bf16[32,4096]{1,0:T(8,128)(2,1)S(1)} %get-tuple-element.45.block_0, bf16[32,4096]{1,0:T(8,128)(2,1)S(1)} %collective-permute-done.block_1, ...), custom_call_target="tpu_custom_call" | custom-call | flops 1048576 | bytes 1048576 | tf_op jit(solution)/shard_map/pallas_call | solution.py:120
  33.2 2.9 %collective-permute-start.4 = (bf16[32,4096]{1,0:T(8,128)(2,1)S(1)}, bf16[32,4096]{1,0:T(8,128)(2,1)S(1)}, u32[]{:S(2)}, u32[]{:S(2)}) collective-permute-start(bf16[32,4096]{1,0:T(8,128)(2,1)S(1)} %get-tuple-element.62), channel_id=1, source_target_pairs={{2,0},{3,1},{0,2},{1,3},{6,4},{7,5},{4,6},{5,7},{10,8},{11,9},{8,1... | collective-permute-start | bytes 786440 | tf_op jit(solution)/shard_map/ppermute | solution.py:96
  36.1 1.9 %collective-permute-start.5 = (bf16[32,4096]{1,0:T(8,128)(2,1)S(1)}, bf16[32,4096]{1,0:T(8,128)(2,1)S(1)}, u32[]{:S(2)}, u32[]{:S(2)}) collective-permute-start(bf16[32,4096]{1,0:T(8,128)(2,1)S(1)} %get-tuple-element.63), channel_id=1, source_target_pairs={{3,0},{0,1},{1,2},{2,3},{7,4},{4,5},{5,6},{6,7},{11,8},{8,9},{9,10... | collective-permute-start | bytes 786440 | tf_op jit(solution)/shard_map/ppermute | solution.py:96
  38.1 0.2 constant_dynamic-slice_fusion.1
  38.2 1.6 collective-permute-start.6
  39.8 0.8 collective-permute-done.3
  40.6 18.0 %collective-permute-done.4 = bf16[32,4096]{1,0:T(8,128)(2,1)S(1)} collective-permute-done((bf16[32,4096]{1,0:T(8,128)(2,1)S(1)}, bf16[32,4096]{1,0:T(8,128)(2,1)S(1)}, u32[]{:S(2)}, u32[]{:S(2)}) %collective-permute-start.4) | collective-permute-done | bytes 262176 | tf_op jit(solution)/shard_map/ppermute | solution.py:96
  58.7 0.2 multiply_reduce_fusion.1
  59.1 1.6 collective-permute-start.10
  60.7 1.5 collective-permute-start.12
  62.2 3.8 %collective-permute-done.10 = bf16[32,4096]{1,0:T(8,128)(2,1)S(1)} collective-permute-done((bf16[32,4096]{1,0:T(8,128)(2,1)S(1)}, bf16[32,4096]{1,0:T(8,128)(2,1)S(1)}, u32[]{:S(2)}, u32[]{:S(2)}) %collective-permute-start.10) | collective-permute-done | bytes 262176 | tf_op jit(solution)/shard_map/ppermute | solution.py:92
  66.0 3.4 %collective-permute-done.7 = bf16[32,4096]{1,0:T(8,128)(2,1)S(1)} collective-permute-done((bf16[32,4096]{1,0:T(8,128)(2,1)S(1)}, bf16[32,4096]{1,0:T(8,128)(2,1)S(1)}, u32[]{:S(2)}, u32[]{:S(2)}) %collective-permute-start.7) | collective-permute-done | bytes 262176 | tf_op jit(solution)/shard_map/ppermute | solution.py:96
  69.3 15.6 %collective-permute-done.8 = bf16[32,4096]{1,0:T(8,128)(2,1)S(1)} collective-permute-done((bf16[32,4096]{1,0:T(8,128)(2,1)S(1)}, bf16[32,4096]{1,0:T(8,128)(2,1)S(1)}, u32[]{:S(2)}, u32[]{:S(2)}) %collective-permute-start.8) | collective-permute-done | bytes 262176 | tf_op jit(solution)/shard_map/ppermute | solution.py:96
  85.0 9.0 %collective-permute-done.12.refs_2_ = bf16[192,2048]{1,0:T(8,128)(2,1)S(1)} collective-permute-done((bf16[192,2048]{1,0:T(8,128)(2,1)S(1)}, bf16[192,2048]{1,0:T(8,128)(2,1)S(1)}, u32[]{:S(2)}, u32[]{:S(2)}) %collective-permute-start.12) | collective-permute-done | bytes 786464 | tf_op jit(solution)/shard_map/ppermute | solution.py:92
  93.9 1.5 collective-permute-start.16
  95.4 1.5 collective-permute-start.13
  97.1 0.6 collective-permute-start.21
  97.6 2.2 %collective-permute-done.15.refs_3_ = bf16[384,4096]{1,0:T(8,128)(2,1)S(1)} collective-permute-done((bf16[384,4096]{1,0:T(8,128)(2,1)}, bf16[384,4096]{1,0:T(8,128)(2,1)S(1)}, u32[]{:S(2)}, u32[]{:S(2)}) %collective-permute-start.15) | collective-permute-done | bytes 3145760 | tf_op jit(solution)/shard_map/ppermute | solution.py:92
  99.9 3.0 %shard_map.184 = (bf16[768,4096]{1,0:T(8,128)(2,1)S(1)}, bf16[768,4096]{1,0:T(8,128)(2,1)S(1)}) custom-call(bf16[192,4096]{1,0:T(8,128)(2,1)} %bitcast.15, bf16[384,4096]{1,0:T(8,128)(2,1)S(1)} %collective-permute-done.14.refs_1_, bf16[384,4096]{1,0:T(8,128)(2,1)} %collective-permute-done.11.refs_2_, bf16[384,4096]{1,0:T(8,128)(2,1)S(1)} %collective-permute-done.15.refs_3_, ...), custom_call_target="tpu_custom_call" | custom-call | bytes 25165824 | tf_op jit(solution)/shard_map/pallas_call | solution.py:170
  102.9 4.3 %shard_map.185.own = bf16[128,768]{1,0:T(8,128)(2,1)S(1)} custom-call(bf16[128,4096]{1,0:T(8,128)(2,1)S(1)} %pad_maximum_fusion.states, bf16[768,4096]{1,0:T(8,128)(2,1)S(1)} %get-tuple-element.72.gate_rows, bf16[768,4096]{1,0:T(8,128)(2,1)S(1)} %get-tuple-element.73.up_rows), custom_call_target="tpu_custom_call" | custom-call | flops 1048576 | bytes 1048576 | tf_op jit(solution)/shard_map/pallas_call | solution.py:120
  107.3 6.6 %collective-permute-done.16.refs_2_ = bf16[192,2048]{1,0:T(8,128)(2,1)S(1)} collective-permute-done((bf16[192,2048]{1,0:T(8,128)(2,1)S(1)}, bf16[192,2048]{1,0:T(8,128)(2,1)S(1)}, u32[]{:S(2)}, u32[]{:S(2)}) %collective-permute-start.16) | collective-permute-done | bytes 786464 | tf_op jit(solution)/shard_map/ppermute | solution.py:92
  113.9 1.2 collective-permute-done.13
  115.2 4.3 %shard_map.186.other = bf16[128,768]{1,0:T(8,128)(2,1)S(1)} custom-call(bf16[128,4096]{1,0:T(8,128)(2,1)S(1)} %pad_maximum_fusion.1.states, bf16[768,4096]{1,0:T(8,128)(2,1)S(1)} %get-tuple-element.72.gate_rows, bf16[768,4096]{1,0:T(8,128)(2,1)S(1)} %get-tuple-element.73.up_rows), custom_call_target="tpu_custom_call" | custom-call | flops 1048576 | bytes 1048576 | tf_op jit(solution)/shard_map/pallas_call | solution.py:120
  119.5 1.6 collective-permute-start.17
  121.1 0.5 collective-permute-start.18
  121.6 0.3 shard_map.187.near_rows
  121.9 0.3 shard_map.188.far_rows
  122.2 5.1 %collective-permute-done.17.far_own = bf16[128,768]{1,0:T(8,128)(2,1)S(1)} collective-permute-done((bf16[128,768]{1,0:T(8,128)(2,1)S(1)}, bf16[128,768]{1,0:T(8,128)(2,1)S(1)}, u32[]{:S(2)}, u32[]{:S(2)}) %collective-permute-start.17) | collective-permute-done | bytes 196640 | tf_op jit(solution)/shard_map/ppermute | solution.py:92
  127.3 3.8 %collective-permute-done.18.far_other = bf16[128,768]{1,0:T(8,128)(2,1)S(1)} collective-permute-done((bf16[128,768]{1,0:T(8,128)(2,1)S(1)}, bf16[128,768]{1,0:T(8,128)(2,1)S(1)}, u32[]{:S(2)}, u32[]{:S(2)}) %collective-permute-start.18) | collective-permute-done | bytes 196640 | tf_op jit(solution)/shard_map/ppermute | solution.py:92
  131.1 1.8 %shard_map.189 = (bf16[64,2048]{1,0:T(8,128)(2,1)S(1)}, bf16[64,2048]{1,0:T(8,128)(2,1)S(1)}, bf16[64,2048]{1,0:T(8,128)(2,1)S(1)}, bf16[64,2048]{1,0:T(8,128)(2,1)S(1)}) custom-call(bf16[128,768]{1,0:T(8,128)(2,1)S(1)} %shard_map.185.own, bf16[128,768]{1,0:T(8,128)(2,1)S(1)} %shard_map.186.other, bf16[128,768]{1,0:T(8,128)(2,1)S(1)} %collective-permute-done.17.far_own, ...), custom_call_target="tpu_custom_call" | custom-call | flops 1048576 | bytes 1048576 | tf_op jit(solution)/shard_map/pallas_call | solution.py:120
  133.0 3.1 %collective-permute-start.23 = (bf16[64,2048]{1,0:T(8,128)(2,1)S(1)}, bf16[64,2048]{1,0:T(8,128)(2,1)S(1)}, u32[]{:S(2)}, u32[]{:S(2)}) collective-permute-start(bf16[64,2048]{1,0:T(8,128)(2,1)S(1)} %get-tuple-element.82), channel_id=1, source_target_pairs={{1,0},{2,1},{3,2},{0,3},{5,4},{6,5},{7,6},{4,7},{9,8},{10,9},{11,1... | collective-permute-start | bytes 786440 | tf_op jit(solution)/shard_map/ppermute | solution.py:96
  136.1 0.8 collective-permute-start.24
  136.9 0.3 collective-permute-start.25
  137.2 5.7 %collective-permute-done.23 = bf16[64,2048]{1,0:T(8,128)(2,1)S(1)} collective-permute-done((bf16[64,2048]{1,0:T(8,128)(2,1)S(1)}, bf16[64,2048]{1,0:T(8,128)(2,1)S(1)}, u32[]{:S(2)}, u32[]{:S(2)}) %collective-permute-start.23) | collective-permute-done | bytes 262176 | tf_op jit(solution)/shard_map/ppermute | solution.py:96
  142.9 16.8 %collective-permute-done.24 = bf16[64,2048]{1,0:T(8,128)(2,1)S(1)} collective-permute-done((bf16[64,2048]{1,0:T(8,128)(2,1)S(1)}, bf16[64,2048]{1,0:T(8,128)(2,1)S(1)}, u32[]{:S(2)}, u32[]{:S(2)}) %collective-permute-start.24) | collective-permute-done | bytes 262176 | tf_op jit(solution)/shard_map/ppermute | solution.py:96
  159.9 1.6 collective-permute-start.26
  161.4 3.4 %collective-permute-done.26 = bf16[32,2048]{1,0:T(8,128)(2,1)S(1)} collective-permute-done((bf16[32,2048]{1,0:T(8,128)(2,1)S(1)}, bf16[32,2048]{1,0:T(8,128)(2,1)S(1)}, u32[]{:S(2)}, u32[]{:S(2)}) %collective-permute-start.26) | collective-permute-done | bytes 131104 | tf_op jit(solution)/shard_map/ppermute | solution.py:92
  164.9 0.2 multiply_reduce_fusion
  165.1 0.9 add_convert_fusion
  (57 shorter events, 1.4 us)
Async XLA Ops:
  0.0 17.7 %collective-permute-start = (bf16[32,4096]{1,0:T(8,128)(2,1)}, bf16[32,4096]{1,0:T(8,128)(2,1)S(1)}, u32[]{:S(2)}, u32[]{:S(2)}) collective-permute-start(bf16[32,4096]{1,0:T(8,128)(2,1)} %refs_10_.1), channel_id=1, source_target_pairs={{1,0},{2,1},{3,2},{0,3},{5,4},{6,5},{7,6},{4,7},{9,8},{10,9},{11,1... | collective-permute-start | bytes 786440 | tf_op jit(solution)/shard_map/ppermute | solution.py:96
  5.0 22.6 %collective-permute-start.1 = (bf16[32,4096]{1,0:T(8,128)(2,1)}, bf16[32,4096]{1,0:T(8,128)(2,1)}, u32[]{:S(2)}, u32[]{:S(2)}) collective-permute-start(bf16[32,4096]{1,0:T(8,128)(2,1)} %refs_10_.1), channel_id=1, source_target_pairs={{2,0},{3,1},{0,2},{1,3},{6,4},{7,5},{4,6},{5,7},{10,8},{11,9},{8,1... | collective-permute-start | bytes 786440 | tf_op jit(solution)/shard_map/ppermute | solution.py:96
  5.1 22.6 %collective-permute-start.2 = (bf16[32,4096]{1,0:T(8,128)(2,1)}, bf16[32,4096]{1,0:T(8,128)(2,1)}, u32[]{:S(2)}, u32[]{:S(2)}) collective-permute-start(bf16[32,4096]{1,0:T(8,128)(2,1)} %refs_10_.1), channel_id=1, source_target_pairs={{3,0},{0,1},{1,2},{2,3},{7,4},{4,5},{5,6},{6,7},{11,8},{8,9},{9,10... | collective-permute-start | bytes 786440 | tf_op jit(solution)/shard_map/ppermute | solution.py:96
  6.1 3.5 %copy-start.6 = (s32[1,4]{1,0:T(1,128)S(1)}, s32[1,4]{1,0:T(1,128)}, u32[]{:S(2)}) copy-start(s32[1,4]{1,0:T(1,128)} %param.20) | copy-start | bytes 52
  6.1 3.7 %copy-start.5 = (s32[1,4]{1,0:T(1,128)S(1)}, s32[1,4]{1,0:T(1,128)}, u32[]{:S(2)}) copy-start(s32[1,4]{1,0:T(1,128)} %param.21) | copy-start | bytes 52
  6.1 4.2 %copy-start.7 = (s32[8]{0:T(128)S(1)}, s32[8]{0:T(128)}, u32[]{:S(2)}) copy-start(s32[8]{0:T(128)} %param.22) | copy-start | bytes 100
  8.0 85.9 %collective-permute-start.11 = (bf16[384,4096]{1,0:T(8,128)(2,1)S(1)}, bf16[384,4096]{1,0:T(8,128)(2,1)}, u32[]{:S(2)}, u32[]{:S(2)}) collective-permute-start(bf16[384,4096]{1,0:T(8,128)(2,1)S(1)} %shard_map.183), channel_id=1, source_target_pairs={{0,8},{8,0},{1,9},{9,1},{2,10},{10,2},{3,11},{11,3},{4,12},{12,4},... | collective-permute-start | bytes 9437192 | tf_op jit(solution)/shard_map/ppermute | solution.py:92
  10.9 6.6 %copy-start.4 = (s32[128]{0:T(128)S(1)}, s32[128]{0:T(128)}, u32[]{:S(2)}) copy-start(s32[128]{0:T(128)} %and_select_fusion) | copy-start | bytes 1540
  27.7 10.4 %copy-start = (bf16[4096,192]{0,1:T(8,128)(2,1)S(1)}, bf16[4096,192]{0,1:T(8,128)(2,1)}, u32[]{:S(2)}) copy-start(bf16[4096,192]{0,1:T(8,128)(2,1)} %param.37) | copy-start | bytes 4718596
  33.2 25.8 %copy-start.1 = (bf16[32,4096]{1,0:T(8,128)(2,1)S(1)}, bf16[32,4096]{1,0:T(8,128)(2,1)}, u32[]{:S(2)}) copy-start(bf16[32,4096]{1,0:T(8,128)(2,1)} %refs_10_.1) | copy-start | bytes 786436
  33.2 25.7 %copy-start.2 = (f32[4096]{0:T(1024)S(1)}, f32[4096]{0:T(1024)}, u32[]{:S(2)}) copy-start(f32[4096]{0:T(1024)} %param.33) | copy-start | bytes 49156
  33.2 7.4 %collective-permute-start.3 = (bf16[32,4096]{1,0:T(8,128)(2,1)S(1)}, bf16[32,4096]{1,0:T(8,128)(2,1)S(1)}, u32[]{:S(2)}, u32[]{:S(2)}) collective-permute-start(bf16[32,4096]{1,0:T(8,128)(2,1)S(1)} %get-tuple-element.61), channel_id=1, source_target_pairs={{1,0},{2,1},{3,2},{0,3},{5,4},{6,5},{7,6},{4,7},{9,8},{10,9},{11,1... | collective-permute-start | bytes 786440 | tf_op jit(solution)/shard_map/ppermute | solution.py:96
  33.2 25.3 %collective-permute-start.4 = (bf16[32,4096]{1,0:T(8,128)(2,1)S(1)}, bf16[32,4096]{1,0:T(8,128)(2,1)S(1)}, u32[]{:S(2)}, u32[]{:S(2)}) collective-permute-start(bf16[32,4096]{1,0:T(8,128)(2,1)S(1)} %get-tuple-element.62), channel_id=1, source_target_pairs={{2,0},{3,1},{0,2},{1,3},{6,4},{7,5},{4,6},{5,7},{10,8},{11,9},{8,1... | collective-permute-start | bytes 786440 | tf_op jit(solution)/shard_map/ppermute | solution.py:96
  36.1 22.5 %collective-permute-start.5 = (bf16[32,4096]{1,0:T(8,128)(2,1)S(1)}, bf16[32,4096]{1,0:T(8,128)(2,1)S(1)}, u32[]{:S(2)}, u32[]{:S(2)}) collective-permute-start(bf16[32,4096]{1,0:T(8,128)(2,1)S(1)} %get-tuple-element.63), channel_id=1, source_target_pairs={{3,0},{0,1},{1,2},{2,3},{7,4},{4,5},{5,6},{6,7},{11,8},{8,9},{9,10... | collective-permute-start | bytes 786440 | tf_op jit(solution)/shard_map/ppermute | solution.py:96
  38.2 20.5 %collective-permute-start.6 = (bf16[192,2048]{1,0:T(8,128)(2,1)S(1)}, bf16[192,2048]{1,0:T(8,128)(2,1)S(1)}, u32[]{:S(2)}, u32[]{:S(2)}) collective-permute-start(bf16[192,2048]{1,0:T(8,128)(2,1)S(1)} %get-tuple-element.90), channel_id=1, source_target_pairs={{0,16},{16,0},{1,17},{17,1},{2,18},{18,2},{3,19},{19,3},{4,20},{20... | collective-permute-start | bytes 2359304 | tf_op jit(solution)/shard_map/ppermute | solution.py:92
  59.1 6.9 %collective-permute-start.10 = (bf16[32,4096]{1,0:T(8,128)(2,1)S(1)}, bf16[32,4096]{1,0:T(8,128)(2,1)S(1)}, u32[]{:S(2)}, u32[]{:S(2)}) collective-permute-start(bf16[32,4096]{1,0:T(8,128)(2,1)S(1)} %add_convert_fusion.1), channel_id=1, source_target_pairs={{0,16},{16,0},{1,17},{17,1},{2,18},{18,2},{3,19},{19,3},{4,20},{20... | collective-permute-start | bytes 786440 | tf_op jit(solution)/shard_map/ppermute | solution.py:92
  60.7 33.3 %collective-permute-start.12 = (bf16[192,2048]{1,0:T(8,128)(2,1)S(1)}, bf16[192,2048]{1,0:T(8,128)(2,1)S(1)}, u32[]{:S(2)}, u32[]{:S(2)}) collective-permute-start(bf16[192,2048]{1,0:T(8,128)(2,1)S(1)} %get-tuple-element.77.refs_0_), channel_id=1, source_target_pairs={{0,8},{8,0},{1,9},{9,1},{2,10},{10,2},{3,11},{11,3},{4,12},{12,4},... | collective-permute-start | bytes 2359304 | tf_op jit(solution)/shard_map/ppermute | solution.py:92
  62.1 7.2 %collective-permute-start.7 = (bf16[32,4096]{1,0:T(8,128)(2,1)S(1)}, bf16[32,4096]{1,0:T(8,128)(2,1)S(1)}, u32[]{:S(2)}, u32[]{:S(2)}) collective-permute-start(bf16[32,4096]{1,0:T(8,128)(2,1)S(1)} %add_convert_fusion.1), channel_id=1, source_target_pairs={{1,0},{2,1},{3,2},{0,3},{5,4},{6,5},{7,6},{4,7},{9,8},{10,9},{11,1... | collective-permute-start | bytes 786440 | tf_op jit(solution)/shard_map/ppermute | solution.py:96
  62.1 22.8 %collective-permute-start.8 = (bf16[32,4096]{1,0:T(8,128)(2,1)S(1)}, bf16[32,4096]{1,0:T(8,128)(2,1)S(1)}, u32[]{:S(2)}, u32[]{:S(2)}) collective-permute-start(bf16[32,4096]{1,0:T(8,128)(2,1)S(1)} %add_convert_fusion.1), channel_id=1, source_target_pairs={{2,0},{3,1},{0,2},{1,3},{6,4},{7,5},{4,6},{5,7},{10,8},{11,9},{8,1... | collective-permute-start | bytes 786440 | tf_op jit(solution)/shard_map/ppermute | solution.py:96
  65.9 19.0 %collective-permute-start.9 = (bf16[32,4096]{1,0:T(8,128)(2,1)S(1)}, bf16[32,4096]{1,0:T(8,128)(2,1)S(1)}, u32[]{:S(2)}, u32[]{:S(2)}) collective-permute-start(bf16[32,4096]{1,0:T(8,128)(2,1)S(1)} %add_convert_fusion.1), channel_id=1, source_target_pairs={{3,0},{0,1},{1,2},{2,3},{7,4},{4,5},{5,6},{6,7},{11,8},{8,9},{9,10... | collective-permute-start | bytes 786440 | tf_op jit(solution)/shard_map/ppermute | solution.py:96
  69.3 27.7 %collective-permute-start.14 = (bf16[384,4096]{1,0:T(8,128)(2,1)S(1)}, bf16[384,4096]{1,0:T(8,128)(2,1)S(1)}, u32[]{:S(2)}, u32[]{:S(2)}) collective-permute-start(bf16[384,4096]{1,0:T(8,128)(2,1)S(1)} %shard_map.183), channel_id=1, source_target_pairs={{0,4},{4,0},{1,5},{5,1},{2,6},{6,2},{3,7},{7,3},{8,12},{12,8},{9,1... | collective-permute-start | bytes 9437192 | tf_op jit(solution)/shard_map/ppermute | solution.py:92
  93.9 5.9 %collective-permute-start.15 = (bf16[384,4096]{1,0:T(8,128)(2,1)}, bf16[384,4096]{1,0:T(8,128)(2,1)S(1)}, u32[]{:S(2)}, u32[]{:S(2)}) collective-permute-start(bf16[384,4096]{1,0:T(8,128)(2,1)} %collective-permute-done.11.refs_2_), channel_id=1, source_target_pairs={{0,4},{4,0},{1,5},{5,1},{2,6},{6,2},{3,7},{7,3},{8,12},{12,8},{9,1... | collective-permute-start | bytes 9437192 | tf_op jit(solution)/shard_map/ppermute | solution.py:92
  93.9 20.0 %collective-permute-start.16 = (bf16[192,2048]{1,0:T(8,128)(2,1)S(1)}, bf16[192,2048]{1,0:T(8,128)(2,1)S(1)}, u32[]{:S(2)}, u32[]{:S(2)}) collective-permute-start(bf16[192,2048]{1,0:T(8,128)(2,1)S(1)} %collective-permute-done.6.refs_0_), channel_id=1, source_target_pairs={{0,8},{8,0},{1,9},{9,1},{2,10},{10,2},{3,11},{11,3},{4,12},{12,4},... | collective-permute-start | bytes 2359304 | tf_op jit(solution)/shard_map/ppermute | solution.py:92
  95.4 19.7 %collective-permute-start.13 = (bf16[96,4096]{1,0:T(8,128)(2,1)S(1)}, bf16[96,4096]{1,0:T(8,128)(2,1)S(1)}, u32[]{:S(2)}, u32[]{:S(2)}) collective-permute-start(bf16[96,4096]{1,0:T(8,128)(2,1)S(1)} %pad_maximum_fusion.2), channel_id=1, source_target_pairs={{0,16},{16,0},{1,17},{17,1},{2,18},{18,2},{3,19},{19,3},{4,20},{20... | collective-permute-start | bytes 2359304 | tf_op jit(solution)/shard_map/ppermute | solution.py:92
  97.0 24.1 %collective-permute-start.19 = (bf16[192,2048]{1,0:T(8,128)(2,1)S(1)}, bf16[192,2048]{1,0:T(8,128)(2,1)S(1)}, u32[]{:S(2)}, u32[]{:S(2)}) collective-permute-start(bf16[192,2048]{1,0:T(8,128)(2,1)S(1)} %get-tuple-element.77.refs_0_), channel_id=1, source_target_pairs={{0,4},{4,0},{1,5},{5,1},{2,6},{6,2},{3,7},{7,3},{8,12},{12,8},{9,1... | collective-permute-start | bytes 2359304 | tf_op jit(solution)/shard_map/ppermute | solution.py:92
  97.1 24.8 %collective-permute-start.21 = (bf16[192,2048]{1,0:T(8,128)(2,1)S(1)}, bf16[192,2048]{1,0:T(8,128)(2,1)S(1)}, u32[]{:S(2)}, u32[]{:S(2)}) collective-permute-start(bf16[192,2048]{1,0:T(8,128)(2,1)S(1)} %collective-permute-done.6.refs_0_), channel_id=1, source_target_pairs={{0,4},{4,0},{1,5},{5,1},{2,6},{6,2},{3,7},{7,3},{8,12},{12,8},{9,1... | collective-permute-start | bytes 2359304 | tf_op jit(solution)/shard_map/ppermute | solution.py:92
  99.8 21.8 %collective-permute-start.20 = (bf16[192,2048]{1,0:T(8,128)(2,1)S(1)}, bf16[192,2048]{1,0:T(8,128)(2,1)S(1)}, u32[]{:S(2)}, u32[]{:S(2)}) collective-permute-start(bf16[192,2048]{1,0:T(8,128)(2,1)S(1)} %collective-permute-done.12.refs_2_), channel_id=1, source_target_pairs={{0,4},{4,0},{1,5},{5,1},{2,6},{6,2},{3,7},{7,3},{8,12},{12,8},{9,1... | collective-permute-start | bytes 2359304 | tf_op jit(solution)/shard_map/ppermute | solution.py:92
  115.1 6.8 %collective-permute-start.22 = (bf16[192,2048]{1,0:T(8,128)(2,1)S(1)}, bf16[192,2048]{1,0:T(8,128)(2,1)S(1)}, u32[]{:S(2)}, u32[]{:S(2)}) collective-permute-start(bf16[192,2048]{1,0:T(8,128)(2,1)S(1)} %collective-permute-done.16.refs_2_), channel_id=1, source_target_pairs={{0,4},{4,0},{1,5},{5,1},{2,6},{6,2},{3,7},{7,3},{8,12},{12,8},{9,1... | collective-permute-start | bytes 2359304 | tf_op jit(solution)/shard_map/ppermute | solution.py:92
  119.5 7.8 %collective-permute-start.17 = (bf16[128,768]{1,0:T(8,128)(2,1)S(1)}, bf16[128,768]{1,0:T(8,128)(2,1)S(1)}, u32[]{:S(2)}, u32[]{:S(2)}) collective-permute-start(bf16[128,768]{1,0:T(8,128)(2,1)S(1)} %shard_map.186.other), channel_id=1, source_target_pairs={{0,16},{16,0},{1,17},{17,1},{2,18},{18,2},{3,19},{19,3},{4,20},{20... | collective-permute-start | bytes 589832 | tf_op jit(solution)/shard_map/ppermute | solution.py:92
  121.1 10.0 %collective-permute-start.18 = (bf16[128,768]{1,0:T(8,128)(2,1)S(1)}, bf16[128,768]{1,0:T(8,128)(2,1)S(1)}, u32[]{:S(2)}, u32[]{:S(2)}) collective-permute-start(bf16[128,768]{1,0:T(8,128)(2,1)S(1)} %shard_map.185.own), channel_id=1, source_target_pairs={{0,16},{16,0},{1,17},{17,1},{2,18},{18,2},{3,19},{19,3},{4,20},{20... | collective-permute-start | bytes 589832 | tf_op jit(solution)/shard_map/ppermute | solution.py:92
  132.9 32.1 %copy-start.3 = (f32[4096]{0:T(1024)S(1)}, f32[4096]{0:T(1024)}, u32[]{:S(2)}) copy-start(f32[4096]{0:T(1024)} %param.34) | copy-start | bytes 49156
  133.0 9.9 %collective-permute-start.23 = (bf16[64,2048]{1,0:T(8,128)(2,1)S(1)}, bf16[64,2048]{1,0:T(8,128)(2,1)S(1)}, u32[]{:S(2)}, u32[]{:S(2)}) collective-permute-start(bf16[64,2048]{1,0:T(8,128)(2,1)S(1)} %get-tuple-element.82), channel_id=1, source_target_pairs={{1,0},{2,1},{3,2},{0,3},{5,4},{6,5},{7,6},{4,7},{9,8},{10,9},{11,1... | collective-permute-start | bytes 786440 | tf_op jit(solution)/shard_map/ppermute | solution.py:96
  136.1 23.6 %collective-permute-start.24 = (bf16[64,2048]{1,0:T(8,128)(2,1)S(1)}, bf16[64,2048]{1,0:T(8,128)(2,1)S(1)}, u32[]{:S(2)}, u32[]{:S(2)}) collective-permute-start(bf16[64,2048]{1,0:T(8,128)(2,1)S(1)} %get-tuple-element.83), channel_id=1, source_target_pairs={{2,0},{3,1},{0,2},{1,3},{6,4},{7,5},{4,6},{5,7},{10,8},{11,9},{8,1... | collective-permute-start | bytes 786440 | tf_op jit(solution)/shard_map/ppermute | solution.py:96
  136.9 22.8 %collective-permute-start.25 = (bf16[64,2048]{1,0:T(8,128)(2,1)S(1)}, bf16[64,2048]{1,0:T(8,128)(2,1)S(1)}, u32[]{:S(2)}, u32[]{:S(2)}) collective-permute-start(bf16[64,2048]{1,0:T(8,128)(2,1)S(1)} %get-tuple-element.84), channel_id=1, source_target_pairs={{3,0},{0,1},{1,2},{2,3},{7,4},{4,5},{5,6},{6,7},{11,8},{8,9},{9,10... | collective-permute-start | bytes 786440 | tf_op jit(solution)/shard_map/ppermute | solution.py:96
  159.9 5.0 %collective-permute-start.26 = (bf16[32,2048]{1,0:T(8,128)(2,1)S(1)}, bf16[32,2048]{1,0:T(8,128)(2,1)S(1)}, u32[]{:S(2)}, u32[]{:S(2)}) collective-permute-start(bf16[32,2048]{1,0:T(8,128)(2,1)S(1)} %slice.14), channel_id=1, source_target_pairs={{0,16},{16,0},{1,17},{17,1},{2,18},{18,2},{3,19},{19,3},{4,20},{20... | collective-permute-start | bytes 393224 | tf_op jit(solution)/shard_map/ppermute | solution.py:92

commit v10 on v9

--- a/solution.py
+++ b/solution.py
@@ -132,7 +132,7 @@
     return pltpu.with_memory_space_constraint(array, pltpu.HBM)
 
 
-def staged(*groups):
+def staged(*groups, space=pltpu.VMEM):
     groups = [
         [piece if isinstance(piece, tuple) else (piece, 0, piece.shape[0]) for piece in group]
         for group in groups
@@ -169,9 +169,9 @@
     size = sum(rows * columns for rows, columns in outs)
     return pl.pallas_call(
         kernel,
-        out_shape=[pltpu.VMEM(shape, group[0][0].dtype) for shape, group in zip(outs, groups)],
+        out_shape=[space(shape, group[0][0].dtype) for shape, group in zip(outs, groups)],
         in_specs=[pl.BlockSpec(memory_space=pl.ANY)] * len(arrays),
-        out_specs=[pl.BlockSpec(memory_space=pltpu.VMEM)] * len(groups),
+        out_specs=[pl.BlockSpec(memory_space=space)] * len(groups),
         scratch_shapes=[pltpu.SemaphoreType.DMA((count,))],
         compiler_params=pltpu.CompilerParams(vmem_limit_bytes=1 << 20),
         cost_estimate=pl.CostEstimate(flops=0, bytes_accessed=4 * size, transcendentals=0),
@@ -292,13 +292,16 @@
     y = lax.axis_index("y")
     half = width // 2
     units = gate_rows.shape[0]
-    (gate_up,) = staged([in_hbm(gate_rows), in_hbm(up_rows)])
+    near = lax.dynamic_slice_in_dim(down_rows, y * half, half, axis=1)
+    far = exchange(lax.dynamic_slice_in_dim(down_rows, (1 - y) * half, half, axis=1), "y")
+    (gate_up,) = staged([in_hbm(gate_rows), in_hbm(up_rows)], space=pltpu.HBM)
     gate_up_x = exchange(gate_up, "x")
     cosine, sine = jnp.cos(angles), jnp.sin(angles)
     block = jax.ShapeDtypeStruct((tok_dev, width), jnp.bfloat16)
     *staged_rows, own_block = staged(
         *([in_hbm(array)] for array in (*projections, *adapters, *head_gains, layer_input))
     )
+    *blocks, far = together(*line_gather(layer_input)[1:], far)
     parts = vmem_call(
         attention_kernel,
         [block] * 4,
@@ -308,7 +311,7 @@
         ],
         [
             own_block,
-            *line_gather(layer_input)[1:],
+            *blocks,
             *staged_rows,
             jnp.concatenate([cosine, cosine], axis=1),
             jnp.concatenate([-sine, sine], axis=1),
@@ -317,14 +320,12 @@
         ],
         8,
     )
-    *parts, down_rows = together(*parts, down_rows)
-    near = lax.dynamic_slice_in_dim(down_rows, y * half, half, axis=1)
-    far = exchange(lax.dynamic_slice_in_dim(down_rows, (1 - y) * half, half, axis=1), "y")
-    near_x, far_x = exchange(near, "x"), exchange(far, "x")
-    attn_own, near, far = together(line_scatter(parts), near, far)
+    near_x = [exchange(rows, "x") for rows in jnp.split(near, 2)]
+    attn_own = line_scatter(parts)
     residual_own = add_normed(layer_input, attn_own, gains[0])
     own, *line, other = together(*line_gather(residual_own), exchange(residual_own, "y"))
-    line, gate_up_x, near_x = together(jnp.concatenate(line), gate_up_x, near_x)
+    line, gate_up_x, near_x[0] = together(jnp.concatenate(line), gate_up_x, near_x[0])
+    far_x = exchange(far, "x")
     pieces = [exchange(gate_up, "core"), gate_up_x, exchange(gate_up_x, "core")]
     gate_all, up_all = staged(
         [in_hbm(gate_rows), *((piece, 0, units) for piece in pieces)],
@@ -345,10 +346,12 @@
     hidden_own = hidden_units_of(own, line)
     line_other, hidden_own, far_x = together(line_other, hidden_own, far_x)
     from_own = exchange(hidden_own, "y")
-    hidden_other = hidden_units_of(other, line_other)
+    far_pieces = four_pieces(far, far_x)
+    hidden_other, near_x[1] = together(hidden_units_of(other, line_other), near_x[1])
     from_other = exchange(hidden_other, "y")
-    (near_all,) = staged(four_pieces(near, near_x))
-    (far_all,) = staged(four_pieces(far, far_x))
+    near_pieces = four_pieces(near, jnp.concatenate(near_x))
+    from_own, *pieces = together(from_own, *near_pieces, *far_pieces)
+    near_all, far_all = staged(pieces[:4], pieces[4:])
     parts = vmem_call(
         down_kernel,
         [jax.ShapeDtypeStruct((2 * tok_dev, half), jnp.bfloat16)] * 4,

time: 166 us -> 258 us (1.55)
  Pallas kernels: 27.9 us -> 121 us
    pallas_call x5 -> x4, Pallas kernels: 12 us -> 106 us  [staged(): pl.pallas_call(kernel, out_shape=[space(shape, group[0][0].dtype) for sha...]
    ppermute x12, waiting for transfers between devices: 70.2 us -> 61.1 us  [shift(): return lax.ppermute(block, 'mlp', [((k + hops) % 4, k) for k in range(4)])]
    ppermute x15 -> x16, waiting for transfers between devices: 35.2 us -> 42.2 us  [exchange(): return lax.ppermute(block, axis, [(0, 1), (1, 0)])]
    ppermute x15 -> x16, starting transfers between devices: 13.6 us -> 10.2 us  [exchange(): return lax.ppermute(block, axis, [(0, 1), (1, 0)])]
    ppermute x12, starting transfers between devices: 15.2 us -> 17.9 us  [shift(): return lax.ppermute(block, 'mlp', [((k + hops) % 4, k) for k in range(4)])]
  transfers between devices with their start and end apart: 27 -> 28, of which waited for: 15 -> 15; matrix products, arithmetic and copies ran while one was open for 1% -> 1% of each run, Pallas kernels for 16% -> 46%
where the time goes in v10:
time: 258 us; the launch traced here: 257 us
  Pallas kernels  121 us (47%)
  waiting for transfers between devices  103 us (40%)
  starting transfers between devices  28 us (11%)
  other arithmetic  2.82 us (1%)
    pallas_call x4, Pallas kernels, staged(): pl.pallas_call(kernel, out_shape=[space(shape, group[0][0].dtype) for sha...  106 us
    ppermute x12, waiting for transfers between devices, shift(): return lax.ppermute(block, 'mlp', [((k + hops) % 4, k) for k in range(4)])  61.1 us
    ppermute x16, waiting for transfers between devices, exchange(): return lax.ppermute(block, axis, [(0, 1), (1, 0)])  42.2 us
    ppermute x12, starting transfers between devices, shift(): return lax.ppermute(block, 'mlp', [((k + hops) % 4, k) for k in range(4)])  17.9 us
    pallas_call x4, Pallas kernels, vmem_call(): pl.pallas_call(kernel, out_shape=outs, in_specs=[whole] * len(operands),...  14.9 us
    ppermute x16, starting transfers between devices, exchange(): return lax.ppermute(block, axis, [(0, 1), (1, 0)])  10.2 us
  transfers between devices with their start and end apart: 28, of which 15 were waited for; matrix products, arithmetic and copies ran while one was open for 1% of the time, Pallas kernels for 46%

profile of v10, /device:TPU:0, one launch (start us, length us, event | category | flops | bytes accessed | tf_op | source)
XLA Modules:
  0.0 257.5 jit_solution(10066304316040618218)
XLA Ops:
  0.0 5.0 %collective-permute-start = (bf16[32,4096]{1,0:T(8,128)(2,1)}, bf16[32,4096]{1,0:T(8,128)(2,1)S(1)}, u32[]{:S(2)}, u32[]{:S(2)}) collective-permute-start(bf16[32,4096]{1,0:T(8,128)(2,1)} %refs_10_.1), channel_id=1, source_target_pairs={{1,0},{2,1},{3,2},{0,3},{5,4},{6,5},{7,6},{4,7},{9,8},{10,9},{11,1... | collective-permute-start | bytes 786440 | tf_op jit(solution)/shard_map/ppermute | solution.py:96
  5.1 1.0 collective-permute-start.2
  6.1 1.5 dynamic-slice_bitcast_fusion
  7.6 1.6 collective-permute-start.3
  9.2 96.4 %shard_map.183 = bf16[384,4096]{1,0:T(8,128)(2,1)} custom-call(bf16[192,4096]{1,0:T(8,128)(2,1)} %bitcast.17, bf16[192,4096]{1,0:T(8,128)(2,1)} %bitcast.19), custom_call_target="tpu_custom_call" | custom-call | bytes 6291456 | tf_op jit(solution)/shard_map/pallas_call | solution.py:170
  105.6 1.6 collective-permute-start.11
  107.5 0.3 fusion.4
  108.0 6.6 %shard_map.181 = (bf16[4096,512]{1,0:T(8,128)(2,1)S(1)}, bf16[4096,512]{1,0:T(8,128)(2,1)S(1)}, bf16[4096,512]{1,0:T(8,128)(2,1)S(1)}, bf16[512,4096]{1,0:T(8,12...) custom-call(bf16[4096,512]{1,0:T(8,128)(2,1)} %refs_0_.1, ...), custom_call_target="tpu_custom_call" | custom-call | bytes 38801408 | tf_op jit(solution)/shard_map/pallas_call | solution.py:170
  114.8 4.5 %shard_map.182 = (bf16[32,4096]{1,0:T(8,128)(2,1)S(1)}, bf16[32,4096]{1,0:T(8,128)(2,1)S(1)}, bf16[32,4096]{1,0:T(8,128)(2,1)S(1)}, bf16[32,4096]{1,0:T(8,128)(2,1)S(1)}) custom-call(bf16[32,4096]{1,0:T(8,128)(2,1)S(1)} %get-tuple-element.54.block_0, bf16[32,4096]{1,0:T(8,128)(2,1)S(1)} %collective-permute-done.block_1, ...), custom_call_target="tpu_custom_call" | custom-call | flops 1048576 | bytes 1048576 | tf_op jit(solution)/shard_map/pallas_call | solution.py:120
  119.3 2.9 %collective-permute-start.4 = (bf16[32,4096]{1,0:T(8,128)(2,1)S(1)}, bf16[32,4096]{1,0:T(8,128)(2,1)S(1)}, u32[]{:S(2)}, u32[]{:S(2)}) collective-permute-start(bf16[32,4096]{1,0:T(8,128)(2,1)S(1)} %get-tuple-element.69), channel_id=1, source_target_pairs={{1,0},{2,1},{3,2},{0,3},{5,4},{6,5},{7,6},{4,7},{9,8},{10,9},{11,1... | collective-permute-start | bytes 786440 | tf_op jit(solution)/shard_map/ppermute | solution.py:96
  122.1 1.1 collective-permute-start.5
  123.3 5.7 %collective-permute-done.4 = bf16[32,4096]{1,0:T(8,128)(2,1)S(1)} collective-permute-done((bf16[32,4096]{1,0:T(8,128)(2,1)S(1)}, bf16[32,4096]{1,0:T(8,128)(2,1)S(1)}, u32[]{:S(2)}, u32[]{:S(2)}) %collective-permute-start.4) | collective-permute-done | bytes 262176 | tf_op jit(solution)/shard_map/ppermute | solution.py:96
  128.9 15.8 %collective-permute-done.5 = bf16[32,4096]{1,0:T(8,128)(2,1)S(1)} collective-permute-done((bf16[32,4096]{1,0:T(8,128)(2,1)S(1)}, bf16[32,4096]{1,0:T(8,128)(2,1)S(1)}, u32[]{:S(2)}, u32[]{:S(2)}) %collective-permute-start.5) | collective-permute-done | bytes 262176 | tf_op jit(solution)/shard_map/ppermute | solution.py:96
  144.7 0.3 multiply_reduce_fusion.1
  145.0 0.2 add_convert_fusion.1
  145.3 0.6 collective-permute-start.10
  145.8 1.5 collective-permute-start.8
  147.3 2.0 collective-permute-start.9
  149.4 2.3 collective-permute-done.10
  151.7 1.1 collective-permute-done.7
  152.8 0.5 collective-permute-start.12
  153.3 16.5 %collective-permute-done.8 = bf16[32,4096]{1,0:T(8,128)(2,1)S(1)} collective-permute-done((bf16[32,4096]{1,0:T(8,128)(2,1)S(1)}, bf16[32,4096]{1,0:T(8,128)(2,1)S(1)}, u32[]{:S(2)}, u32[]{:S(2)}) %collective-permute-start.8) | collective-permute-done | bytes 262176 | tf_op jit(solution)/shard_map/ppermute | solution.py:96
  169.9 13.1 %collective-permute-done.12 = bf16[96,2048]{1,0:T(8,128)(2,1)S(1)} collective-permute-done((bf16[96,2048]{1,0:T(8,128)(2,1)S(1)}, bf16[96,2048]{1,0:T(8,128)(2,1)S(1)}, u32[]{:S(2)}, u32[]{:S(2)}) %collective-permute-start.12) | collective-permute-done | bytes 393248 | tf_op jit(solution)/shard_map/ppermute | solution.py:92
  183.0 1.5 collective-permute-start.16
  184.5 0.5 collective-permute-start.13
  185.2 0.6 collective-permute-start.17
  185.8 3.1 %collective-permute-done.15.refs_3_ = bf16[384,4096]{1,0:T(8,128)(2,1)S(1)} collective-permute-done((bf16[384,4096]{1,0:T(8,128)(2,1)}, bf16[384,4096]{1,0:T(8,128)(2,1)S(1)}, u32[]{:S(2)}, u32[]{:S(2)}) %collective-permute-start.15) | collective-permute-done | bytes 3145760 | tf_op jit(solution)/shard_map/ppermute | solution.py:92
  189.0 3.0 %shard_map.184 = (bf16[768,4096]{1,0:T(8,128)(2,1)S(1)}, bf16[768,4096]{1,0:T(8,128)(2,1)S(1)}) custom-call(bf16[192,4096]{1,0:T(8,128)(2,1)} %bitcast.18, bf16[384,4096]{1,0:T(8,128)(2,1)S(1)} %collective-permute-done.14.refs_1_, bf16[384,4096]{1,0:T(8,128)(2,1)} %collective-permute-done.11.refs_2_, bf16[384,4096]{1,0:T(8,128)(2,1)S(1)} %collective-permute-done.15.refs_3_, ...), custom_call_target="tpu_custom_call" | custom-call | bytes 25165824 | tf_op jit(solution)/shard_map/pallas_call | solution.py:170
  192.0 4.3 %shard_map.185.own = bf16[128,768]{1,0:T(8,128)(2,1)S(1)} custom-call(bf16[128,4096]{1,0:T(8,128)(2,1)S(1)} %pad_maximum_fusion.states, bf16[768,4096]{1,0:T(8,128)(2,1)S(1)} %get-tuple-element.78.gate_rows, bf16[768,4096]{1,0:T(8,128)(2,1)S(1)} %get-tuple-element.79.up_rows), custom_call_target="tpu_custom_call" | custom-call | flops 1048576 | bytes 1048576 | tf_op jit(solution)/shard_map/pallas_call | solution.py:120
  196.3 7.0 %collective-permute-done.16.refs_6_ = bf16[192,2048]{1,0:T(8,128)(2,1)S(1)} collective-permute-done((bf16[192,2048]{1,0:T(8,128)(2,1)S(1)}, bf16[192,2048]{1,0:T(8,128)(2,1)S(1)}, u32[]{:S(2)}, u32[]{:S(2)}) %collective-permute-start.16) | collective-permute-done | bytes 786464 | tf_op jit(solution)/shard_map/ppermute | solution.py:92
  203.4 0.8 collective-permute-done.13
  204.3 4.3 %shard_map.186.other = bf16[128,768]{1,0:T(8,128)(2,1)S(1)} custom-call(bf16[128,4096]{1,0:T(8,128)(2,1)S(1)} %pad_maximum_fusion.1.states, bf16[768,4096]{1,0:T(8,128)(2,1)S(1)} %get-tuple-element.78.gate_rows, bf16[768,4096]{1,0:T(8,128)(2,1)S(1)} %get-tuple-element.79.up_rows), custom_call_target="tpu_custom_call" | custom-call | flops 1048576 | bytes 1048576 | tf_op jit(solution)/shard_map/pallas_call | solution.py:120
  208.6 2.8 %collective-permute-done.17 = bf16[96,2048]{1,0:T(8,128)(2,1)S(1)} collective-permute-done((bf16[96,2048]{1,0:T(8,128)(2,1)S(1)}, bf16[96,2048]{1,0:T(8,128)(2,1)S(1)}, u32[]{:S(2)}, u32[]{:S(2)}) %collective-permute-start.17) | collective-permute-done | bytes 393248 | tf_op jit(solution)/shard_map/ppermute | solution.py:92
  211.5 0.5 collective-permute-start.23
  212.0 0.5 collective-permute-start.19
  212.5 1.5 collective-permute-start.18
  214.0 5.7 %collective-permute-done.19.far_other = bf16[128,768]{1,0:T(8,128)(2,1)S(1)} collective-permute-done((bf16[128,768]{1,0:T(8,128)(2,1)S(1)}, bf16[128,768]{1,0:T(8,128)(2,1)S(1)}, u32[]{:S(2)}, u32[]{:S(2)}) %collective-permute-start.19) | collective-permute-done | bytes 196640 | tf_op jit(solution)/shard_map/ppermute | solution.py:92
  219.8 0.5 shard_map.187
  220.3 2.8 %collective-permute-done.18.far_own = bf16[128,768]{1,0:T(8,128)(2,1)S(1)} collective-permute-done((bf16[128,768]{1,0:T(8,128)(2,1)S(1)}, bf16[128,768]{1,0:T(8,128)(2,1)S(1)}, u32[]{:S(2)}, u32[]{:S(2)}) %collective-permute-start.18) | collective-permute-done | bytes 196640 | tf_op jit(solution)/shard_map/ppermute | solution.py:92
  223.1 1.8 shard_map.188
  224.9 3.1 %collective-permute-start.24 = (bf16[64,2048]{1,0:T(8,128)(2,1)S(1)}, bf16[64,2048]{1,0:T(8,128)(2,1)S(1)}, u32[]{:S(2)}, u32[]{:S(2)}) collective-permute-start(bf16[64,2048]{1,0:T(8,128)(2,1)S(1)} %get-tuple-element.100), channel_id=1, source_target_pairs={{1,0},{2,1},{3,2},{0,3},{5,4},{6,5},{7,6},{4,7},{9,8},{10,9},{11,1... | collective-permute-start | bytes 786440 | tf_op jit(solution)/shard_map/ppermute | solution.py:96
  228.1 0.8 collective-permute-start.25
  228.9 0.3 collective-permute-start.26
  229.2 5.7 %collective-permute-done.24 = bf16[64,2048]{1,0:T(8,128)(2,1)S(1)} collective-permute-done((bf16[64,2048]{1,0:T(8,128)(2,1)S(1)}, bf16[64,2048]{1,0:T(8,128)(2,1)S(1)}, u32[]{:S(2)}, u32[]{:S(2)}) %collective-permute-start.24) | collective-permute-done | bytes 262176 | tf_op jit(solution)/shard_map/ppermute | solution.py:96
  234.9 16.3 %collective-permute-done.25 = bf16[64,2048]{1,0:T(8,128)(2,1)S(1)} collective-permute-done((bf16[64,2048]{1,0:T(8,128)(2,1)S(1)}, bf16[64,2048]{1,0:T(8,128)(2,1)S(1)}, u32[]{:S(2)}, u32[]{:S(2)}) %collective-permute-start.25) | collective-permute-done | bytes 262176 | tf_op jit(solution)/shard_map/ppermute | solution.py:96
  251.4 0.6 collective-permute-start.27
  251.9 4.5 %collective-permute-done.27 = bf16[32,2048]{1,0:T(8,128)(2,1)S(1)} collective-permute-done((bf16[32,2048]{1,0:T(8,128)(2,1)S(1)}, bf16[32,2048]{1,0:T(8,128)(2,1)S(1)}, u32[]{:S(2)}, u32[]{:S(2)}) %collective-permute-start.27) | collective-permute-done | bytes 131104 | tf_op jit(solution)/shard_map/ppermute | solution.py:92
  256.6 0.9 add_convert_fusion
  (58 shorter events, 1.6 us)
Async XLA Ops:
  0.0 114.7 %collective-permute-start = (bf16[32,4096]{1,0:T(8,128)(2,1)}, bf16[32,4096]{1,0:T(8,128)(2,1)S(1)}, u32[]{:S(2)}, u32[]{:S(2)}) collective-permute-start(bf16[32,4096]{1,0:T(8,128)(2,1)} %refs_10_.1), channel_id=1, source_target_pairs={{1,0},{2,1},{3,2},{0,3},{5,4},{6,5},{7,6},{4,7},{9,8},{10,9},{11,1... | collective-permute-start | bytes 786440 | tf_op jit(solution)/shard_map/ppermute | solution.py:96
  5.0 109.7 %collective-permute-start.1 = (bf16[32,4096]{1,0:T(8,128)(2,1)}, bf16[32,4096]{1,0:T(8,128)(2,1)S(1)}, u32[]{:S(2)}, u32[]{:S(2)}) collective-permute-start(bf16[32,4096]{1,0:T(8,128)(2,1)} %refs_10_.1), channel_id=1, source_target_pairs={{2,0},{3,1},{0,2},{1,3},{6,4},{7,5},{4,6},{5,7},{10,8},{11,9},{8,1... | collective-permute-start | bytes 786440 | tf_op jit(solution)/shard_map/ppermute | solution.py:96
  5.1 109.7 %collective-permute-start.2 = (bf16[32,4096]{1,0:T(8,128)(2,1)}, bf16[32,4096]{1,0:T(8,128)(2,1)S(1)}, u32[]{:S(2)}, u32[]{:S(2)}) collective-permute-start(bf16[32,4096]{1,0:T(8,128)(2,1)} %refs_10_.1), channel_id=1, source_target_pairs={{3,0},{0,1},{1,2},{2,3},{7,4},{4,5},{5,6},{6,7},{11,8},{8,9},{9,10... | collective-permute-start | bytes 786440 | tf_op jit(solution)/shard_map/ppermute | solution.py:96
  7.6 107.2 %collective-permute-start.3 = (bf16[192,2048]{1,0:T(8,128)(2,1)S(1)}, bf16[192,2048]{1,0:T(8,128)(2,1)S(1)}, u32[]{:S(2)}, u32[]{:S(2)}) collective-permute-start(bf16[192,2048]{1,0:T(8,128)(2,1)S(1)} %get-tuple-element.109), channel_id=1, source_target_pairs={{0,16},{16,0},{1,17},{17,1},{2,18},{18,2},{3,19},{19,3},{4,20},{20... | collective-permute-start | bytes 2359304 | tf_op jit(solution)/shard_map/ppermute | solution.py:92
  9.2 98.0 %copy-start.5 = (s32[1,4]{1,0:T(1,128)S(1)}, s32[1,4]{1,0:T(1,128)}, u32[]{:S(2)}) copy-start(s32[1,4]{1,0:T(1,128)} %param.20) | copy-start | bytes 52
  9.2 98.2 %copy-start.4 = (s32[1,4]{1,0:T(1,128)S(1)}, s32[1,4]{1,0:T(1,128)}, u32[]{:S(2)}) copy-start(s32[1,4]{1,0:T(1,128)} %param.21) | copy-start | bytes 52
  9.2 98.6 %copy-start.6 = (s32[8]{0:T(128)S(1)}, s32[8]{0:T(128)}, u32[]{:S(2)}) copy-start(s32[8]{0:T(128)} %param.22) | copy-start | bytes 100
  105.6 77.4 %collective-permute-start.11 = (bf16[384,4096]{1,0:T(8,128)(2,1)}, bf16[384,4096]{1,0:T(8,128)(2,1)}, u32[]{:S(2)}, u32[]{:S(2)}) collective-permute-start(bf16[384,4096]{1,0:T(8,128)(2,1)} %shard_map.183), channel_id=1, source_target_pairs={{0,8},{8,0},{1,9},{9,1},{2,10},{10,2},{3,11},{11,3},{4,12},{12,4},... | collective-permute-start | bytes 9437192 | tf_op jit(solution)/shard_map/ppermute | solution.py:92
  114.8 30.3 %copy-start.1 = (bf16[32,4096]{1,0:T(8,128)(2,1)S(1)}, bf16[32,4096]{1,0:T(8,128)(2,1)}, u32[]{:S(2)}) copy-start(bf16[32,4096]{1,0:T(8,128)(2,1)} %refs_10_.1) | copy-start | bytes 786436
  114.8 30.3 %copy-start.2 = (f32[4096]{0:T(1024)S(1)}, f32[4096]{0:T(1024)}, u32[]{:S(2)}) copy-start(f32[4096]{0:T(1024)} %param.33) | copy-start | bytes 49156
  119.3 32.4 %copy-start = (bf16[384,4096]{1,0:T(8,128)(2,1)S(1)}, bf16[384,4096]{1,0:T(8,128)(2,1)}, u32[]{:S(2)}) copy-start(bf16[384,4096]{1,0:T(8,128)(2,1)} %shard_map.183) | copy-start | bytes 9437188
  119.3 9.7 %collective-permute-start.4 = (bf16[32,4096]{1,0:T(8,128)(2,1)S(1)}, bf16[32,4096]{1,0:T(8,128)(2,1)S(1)}, u32[]{:S(2)}, u32[]{:S(2)}) collective-permute-start(bf16[32,4096]{1,0:T(8,128)(2,1)S(1)} %get-tuple-element.69), channel_id=1, source_target_pairs={{1,0},{2,1},{3,2},{0,3},{5,4},{6,5},{7,6},{4,7},{9,8},{10,9},{11,1... | collective-permute-start | bytes 786440 | tf_op jit(solution)/shard_map/ppermute | solution.py:96
  122.1 22.6 %collective-permute-start.5 = (bf16[32,4096]{1,0:T(8,128)(2,1)S(1)}, bf16[32,4096]{1,0:T(8,128)(2,1)S(1)}, u32[]{:S(2)}, u32[]{:S(2)}) collective-permute-start(bf16[32,4096]{1,0:T(8,128)(2,1)S(1)} %get-tuple-element.70), channel_id=1, source_target_pairs={{2,0},{3,1},{0,2},{1,3},{6,4},{7,5},{4,6},{5,7},{10,8},{11,9},{8,1... | collective-permute-start | bytes 786440 | tf_op jit(solution)/shard_map/ppermute | solution.py:96
  123.3 21.5 %collective-permute-start.6 = (bf16[32,4096]{1,0:T(8,128)(2,1)S(1)}, bf16[32,4096]{1,0:T(8,128)(2,1)S(1)}, u32[]{:S(2)}, u32[]{:S(2)}) collective-permute-start(bf16[32,4096]{1,0:T(8,128)(2,1)S(1)} %get-tuple-element.71), channel_id=1, source_target_pairs={{3,0},{0,1},{1,2},{2,3},{7,4},{4,5},{5,6},{6,7},{11,8},{8,9},{9,10... | collective-permute-start | bytes 786440 | tf_op jit(solution)/shard_map/ppermute | solution.py:96
  145.3 6.4 %collective-permute-start.10 = (bf16[32,4096]{1,0:T(8,128)(2,1)S(1)}, bf16[32,4096]{1,0:T(8,128)(2,1)S(1)}, u32[]{:S(2)}, u32[]{:S(2)}) collective-permute-start(bf16[32,4096]{1,0:T(8,128)(2,1)S(1)} %add_convert_fusion.1), channel_id=1, source_target_pairs={{0,16},{16,0},{1,17},{17,1},{2,18},{18,2},{3,19},{19,3},{4,20},{20... | collective-permute-start | bytes 786440 | tf_op jit(solution)/shard_map/ppermute | solution.py:92
  145.8 6.9 %collective-permute-start.7 = (bf16[32,4096]{1,0:T(8,128)(2,1)S(1)}, bf16[32,4096]{1,0:T(8,128)(2,1)S(1)}, u32[]{:S(2)}, u32[]{:S(2)}) collective-permute-start(bf16[32,4096]{1,0:T(8,128)(2,1)S(1)} %add_convert_fusion.1), channel_id=1, source_target_pairs={{1,0},{2,1},{3,2},{0,3},{5,4},{6,5},{7,6},{4,7},{9,8},{10,9},{11,1... | collective-permute-start | bytes 786440 | tf_op jit(solution)/shard_map/ppermute | solution.py:96
  145.8 24.0 %collective-permute-start.8 = (bf16[32,4096]{1,0:T(8,128)(2,1)S(1)}, bf16[32,4096]{1,0:T(8,128)(2,1)S(1)}, u32[]{:S(2)}, u32[]{:S(2)}) collective-permute-start(bf16[32,4096]{1,0:T(8,128)(2,1)S(1)} %add_convert_fusion.1), channel_id=1, source_target_pairs={{2,0},{3,1},{0,2},{1,3},{6,4},{7,5},{4,6},{5,7},{10,8},{11,9},{8,1... | collective-permute-start | bytes 786440 | tf_op jit(solution)/shard_map/ppermute | solution.py:96
  147.3 22.5 %collective-permute-start.9 = (bf16[32,4096]{1,0:T(8,128)(2,1)S(1)}, bf16[32,4096]{1,0:T(8,128)(2,1)S(1)}, u32[]{:S(2)}, u32[]{:S(2)}) collective-permute-start(bf16[32,4096]{1,0:T(8,128)(2,1)S(1)} %add_convert_fusion.1), channel_id=1, source_target_pairs={{3,0},{0,1},{1,2},{2,3},{7,4},{4,5},{5,6},{6,7},{11,8},{8,9},{9,10... | collective-permute-start | bytes 786440 | tf_op jit(solution)/shard_map/ppermute | solution.py:96
  151.7 33.5 %collective-permute-start.14 = (bf16[384,4096]{1,0:T(8,128)(2,1)S(1)}, bf16[384,4096]{1,0:T(8,128)(2,1)S(1)}, u32[]{:S(2)}, u32[]{:S(2)}) collective-permute-start(bf16[384,4096]{1,0:T(8,128)(2,1)S(1)} %copy-done), channel_id=1, source_target_pairs={{0,4},{4,0},{1,5},{5,1},{2,6},{6,2},{3,7},{7,3},{8,12},{12,8},{9,1... | collective-permute-start | bytes 9437192 | tf_op jit(solution)/shard_map/ppermute | solution.py:92
  152.8 30.2 %collective-permute-start.12 = (bf16[96,2048]{1,0:T(8,128)(2,1)S(1)}, bf16[96,2048]{1,0:T(8,128)(2,1)S(1)}, u32[]{:S(2)}, u32[]{:S(2)}) collective-permute-start(bf16[96,2048]{1,0:T(8,128)(2,1)S(1)} %get-tuple-element.111), channel_id=1, source_target_pairs={{0,8},{8,0},{1,9},{9,1},{2,10},{10,2},{3,11},{11,3},{4,12},{12,4},... | collective-permute-start | bytes 1179656 | tf_op jit(solution)/shard_map/ppermute | solution.py:92
  183.0 5.9 %collective-permute-start.15 = (bf16[384,4096]{1,0:T(8,128)(2,1)}, bf16[384,4096]{1,0:T(8,128)(2,1)S(1)}, u32[]{:S(2)}, u32[]{:S(2)}) collective-permute-start(bf16[384,4096]{1,0:T(8,128)(2,1)} %collective-permute-done.11.refs_2_), channel_id=1, source_target_pairs={{0,4},{4,0},{1,5},{5,1},{2,6},{6,2},{3,7},{7,3},{8,12},{12,8},{9,1... | collective-permute-start | bytes 9437192 | tf_op jit(solution)/shard_map/ppermute | solution.py:92
  183.0 20.3 %collective-permute-start.16 = (bf16[192,2048]{1,0:T(8,128)(2,1)S(1)}, bf16[192,2048]{1,0:T(8,128)(2,1)S(1)}, u32[]{:S(2)}, u32[]{:S(2)}) collective-permute-start(bf16[192,2048]{1,0:T(8,128)(2,1)S(1)} %collective-permute-done.3.refs_4_), channel_id=1, source_target_pairs={{0,8},{8,0},{1,9},{9,1},{2,10},{10,2},{3,11},{11,3},{4,12},{12,4},... | collective-permute-start | bytes 2359304 | tf_op jit(solution)/shard_map/ppermute | solution.py:92
  184.5 19.7 %collective-permute-start.13 = (bf16[96,4096]{1,0:T(8,128)(2,1)S(1)}, bf16[96,4096]{1,0:T(8,128)(2,1)S(1)}, u32[]{:S(2)}, u32[]{:S(2)}) collective-permute-start(bf16[96,4096]{1,0:T(8,128)(2,1)S(1)} %pad_maximum_fusion.2), channel_id=1, source_target_pairs={{0,16},{16,0},{1,17},{17,1},{2,18},{18,2},{3,19},{19,3},{4,20},{20... | collective-permute-start | bytes 2359304 | tf_op jit(solution)/shard_map/ppermute | solution.py:92
  185.0 27.5 %collective-permute-start.20 = (bf16[192,2048]{1,0:T(8,128)(2,1)S(1)}, bf16[192,2048]{1,0:T(8,128)(2,1)S(1)}, u32[]{:S(2)}, u32[]{:S(2)}) collective-permute-start(bf16[192,2048]{1,0:T(8,128)(2,1)S(1)} %get-tuple-element.89.refs_0_), channel_id=1, source_target_pairs={{0,4},{4,0},{1,5},{5,1},{2,6},{6,2},{3,7},{7,3},{8,12},{12,8},{9,1... | collective-permute-start | bytes 2359304 | tf_op jit(solution)/shard_map/ppermute | solution.py:92
  185.2 26.2 %collective-permute-start.17 = (bf16[96,2048]{1,0:T(8,128)(2,1)S(1)}, bf16[96,2048]{1,0:T(8,128)(2,1)S(1)}, u32[]{:S(2)}, u32[]{:S(2)}) collective-permute-start(bf16[96,2048]{1,0:T(8,128)(2,1)S(1)} %get-tuple-element.110), channel_id=1, source_target_pairs={{0,8},{8,0},{1,9},{9,1},{2,10},{10,2},{3,11},{11,3},{4,12},{12,4},... | collective-permute-start | bytes 1179656 | tf_op jit(solution)/shard_map/ppermute | solution.py:92
  188.9 25.2 %collective-permute-start.22 = (bf16[192,2048]{1,0:T(8,128)(2,1)S(1)}, bf16[192,2048]{1,0:T(8,128)(2,1)S(1)}, u32[]{:S(2)}, u32[]{:S(2)}) collective-permute-start(bf16[192,2048]{1,0:T(8,128)(2,1)S(1)} %collective-permute-done.3.refs_4_), channel_id=1, source_target_pairs={{0,4},{4,0},{1,5},{5,1},{2,6},{6,2},{3,7},{7,3},{8,12},{12,8},{9,1... | collective-permute-start | bytes 2359304 | tf_op jit(solution)/shard_map/ppermute | solution.py:92
  211.4 8.3 %collective-permute-start.21 = (bf16[192,2048]{1,0:T(8,128)(2,1)S(1)}, bf16[192,2048]{1,0:T(8,128)(2,1)S(1)}, u32[]{:S(2)}, u32[]{:S(2)}) collective-permute-start(bf16[192,2048]{1,0:T(8,128)(2,1)S(1)} %constant_dynamic-update-slice_fusion.refs_2_), channel_id=1, source_target_pairs={{0,4},{4,0},{1,5},{5,1},{2,6},{6,2},{3,7},{7,3},{8,12},{12,8},{9,1... | collective-permute-start | bytes 2359304 | tf_op jit(solution)/shard_map/ppermute | solution.py:92
  211.5 8.3 %collective-permute-start.23 = (bf16[192,2048]{1,0:T(8,128)(2,1)S(1)}, bf16[192,2048]{1,0:T(8,128)(2,1)S(1)}, u32[]{:S(2)}, u32[]{:S(2)}) collective-permute-start(bf16[192,2048]{1,0:T(8,128)(2,1)S(1)} %collective-permute-done.16.refs_6_), channel_id=1, source_target_pairs={{0,4},{4,0},{1,5},{5,1},{2,6},{6,2},{3,7},{7,3},{8,12},{12,8},{9,1... | collective-permute-start | bytes 2359304 | tf_op jit(solution)/shard_map/ppermute | solution.py:92
  212.0 7.8 %collective-permute-start.19 = (bf16[128,768]{1,0:T(8,128)(2,1)S(1)}, bf16[128,768]{1,0:T(8,128)(2,1)S(1)}, u32[]{:S(2)}, u32[]{:S(2)}) collective-permute-start(bf16[128,768]{1,0:T(8,128)(2,1)S(1)} %shard_map.185.own), channel_id=1, source_target_pairs={{0,16},{16,0},{1,17},{17,1},{2,18},{18,2},{3,19},{19,3},{4,20},{20... | collective-permute-start | bytes 589832 | tf_op jit(solution)/shard_map/ppermute | solution.py:92
  212.5 10.6 %collective-permute-start.18 = (bf16[128,768]{1,0:T(8,128)(2,1)S(1)}, bf16[128,768]{1,0:T(8,128)(2,1)S(1)}, u32[]{:S(2)}, u32[]{:S(2)}) collective-permute-start(bf16[128,768]{1,0:T(8,128)(2,1)S(1)} %shard_map.186.other), channel_id=1, source_target_pairs={{0,16},{16,0},{1,17},{17,1},{2,18},{18,2},{3,19},{19,3},{4,20},{20... | collective-permute-start | bytes 589832 | tf_op jit(solution)/shard_map/ppermute | solution.py:92
  224.9 31.7 %copy-start.3 = (f32[4096]{0:T(1024)S(1)}, f32[4096]{0:T(1024)}, u32[]{:S(2)}) copy-start(f32[4096]{0:T(1024)} %param.34) | copy-start | bytes 49156
  224.9 10.0 %collective-permute-start.24 = (bf16[64,2048]{1,0:T(8,128)(2,1)S(1)}, bf16[64,2048]{1,0:T(8,128)(2,1)S(1)}, u32[]{:S(2)}, u32[]{:S(2)}) collective-permute-start(bf16[64,2048]{1,0:T(8,128)(2,1)S(1)} %get-tuple-element.100), channel_id=1, source_target_pairs={{1,0},{2,1},{3,2},{0,3},{5,4},{6,5},{7,6},{4,7},{9,8},{10,9},{11,1... | collective-permute-start | bytes 786440 | tf_op jit(solution)/shard_map/ppermute | solution.py:96
  228.1 23.1 %collective-permute-start.25 = (bf16[64,2048]{1,0:T(8,128)(2,1)S(1)}, bf16[64,2048]{1,0:T(8,128)(2,1)S(1)}, u32[]{:S(2)}, u32[]{:S(2)}) collective-permute-start(bf16[64,2048]{1,0:T(8,128)(2,1)S(1)} %get-tuple-element.101), channel_id=1, source_target_pairs={{2,0},{3,1},{0,2},{1,3},{6,4},{7,5},{4,6},{5,7},{10,8},{11,9},{8,1... | collective-permute-start | bytes 786440 | tf_op jit(solution)/shard_map/ppermute | solution.py:96
  228.9 22.3 %collective-permute-start.26 = (bf16[64,2048]{1,0:T(8,128)(2,1)S(1)}, bf16[64,2048]{1,0:T(8,128)(2,1)S(1)}, u32[]{:S(2)}, u32[]{:S(2)}) collective-permute-start(bf16[64,2048]{1,0:T(8,128)(2,1)S(1)} %get-tuple-element.102), channel_id=1, source_target_pairs={{3,0},{0,1},{1,2},{2,3},{7,4},{4,5},{5,6},{6,7},{11,8},{8,9},{9,10... | collective-permute-start | bytes 786440 | tf_op jit(solution)/shard_map/ppermute | solution.py:96
  251.4 5.0 %collective-permute-start.27 = (bf16[32,2048]{1,0:T(8,128)(2,1)S(1)}, bf16[32,2048]{1,0:T(8,128)(2,1)S(1)}, u32[]{:S(2)}, u32[]{:S(2)}) collective-permute-start(bf16[32,2048]{1,0:T(8,128)(2,1)S(1)} %slice.14), channel_id=1, source_target_pairs={{0,16},{16,0},{1,17},{17,1},{2,18},{18,2},{3,19},{19,3},{4,20},{20... | collective-permute-start | bytes 393224 | tf_op jit(solution)/shard_map/ppermute | solution.py:92

commit v11 on v10

--- a/solution.py
+++ b/solution.py
@@ -132,7 +132,7 @@
     return pltpu.with_memory_space_constraint(array, pltpu.HBM)
 
 
-def staged(*groups, space=pltpu.VMEM):
+def staged(*groups):
     groups = [
         [piece if isinstance(piece, tuple) else (piece, 0, piece.shape[0]) for piece in group]
         for group in groups
@@ -169,13 +169,52 @@
     size = sum(rows * columns for rows, columns in outs)
     return pl.pallas_call(
         kernel,
-        out_shape=[space(shape, group[0][0].dtype) for shape, group in zip(outs, groups)],
+        out_shape=[pltpu.VMEM(shape, group[0][0].dtype) for shape, group in zip(outs, groups)],
         in_specs=[pl.BlockSpec(memory_space=pl.ANY)] * len(arrays),
-        out_specs=[pl.BlockSpec(memory_space=space)] * len(groups),
+        out_specs=[pl.BlockSpec(memory_space=pltpu.VMEM)] * len(groups),
         scratch_shapes=[pltpu.SemaphoreType.DMA((count,))],
         compiler_params=pltpu.CompilerParams(vmem_limit_bytes=1 << 20),
         cost_estimate=pl.CostEstimate(flops=0, bytes_accessed=4 * size, transcendentals=0),
     )(*arrays)
+
+
+def stacked(*arrays):
+    rows, columns = arrays[0].shape
+
+    def kernel(*refs):
+        sources, target, buffer, sems_in, sems_out = refs[:-4], *refs[-4:]
+        into = [
+            pltpu.make_async_copy(source, buffer.at[k], sems_in.at[k])
+            for k, source in enumerate(sources)
+        ]
+        out = [
+            pltpu.make_async_copy(
+                buffer.at[k], target.at[pl.ds(k * rows, rows), :], sems_out.at[k]
+            )
+            for k in range(len(sources))
+        ]
+        for copy in into:
+            copy.start()
+        for copy_in, copy_out in zip(into, out):
+            copy_in.wait()
+            copy_out.start()
+        for copy in out:
+            copy.wait()
+
+    count = len(arrays)
+    return pl.pallas_call(
+        kernel,
+        out_shape=pltpu.HBM((count * rows, columns), arrays[0].dtype),
+        in_specs=[pl.BlockSpec(memory_space=pl.ANY)] * count,
+        out_specs=pl.BlockSpec(memory_space=pltpu.HBM),
+        scratch_shapes=[
+            pltpu.VMEM((count, rows, columns), arrays[0].dtype),
+            pltpu.SemaphoreType.DMA((count,)),
+            pltpu.SemaphoreType.DMA((count,)),
+        ],
+        compiler_params=pltpu.CompilerParams(vmem_limit_bytes=8 << 20),
+        cost_estimate=pl.CostEstimate(flops=0, bytes_accessed=1 << 20, transcendentals=0),
+    )(*(in_hbm(array) for array in arrays))
 
 
 NT = (((1,), (1,)), ((), ()))
@@ -294,7 +333,7 @@
     units = gate_rows.shape[0]
     near = lax.dynamic_slice_in_dim(down_rows, y * half, half, axis=1)
     far = exchange(lax.dynamic_slice_in_dim(down_rows, (1 - y) * half, half, axis=1), "y")
-    (gate_up,) = staged([in_hbm(gate_rows), in_hbm(up_rows)], space=pltpu.HBM)
+    gate_up = stacked(gate_rows, up_rows)
     gate_up_x = exchange(gate_up, "x")
     cosine, sine = jnp.cos(angles), jnp.sin(angles)
     block = jax.ShapeDtypeStruct((tok_dev, width), jnp.bfloat16)

time: 258 us -> 164 us (0.64)
  Pallas kernels: 121 us -> 28.1 us
    pallas_call x4, Pallas kernels: 106 us -> 13.2 us  [the longest x3 10.1 us: staged(): pl.pallas_call(kernel, out_shape=[pltpu.VMEM(shape, group[0][0].dtype) fo...]
    ppermute x16, waiting for transfers between devices: 42.2 us -> 35.8 us  [exchange(): return lax.ppermute(block, axis, [(0, 1), (1, 0)])]
    ppermute x12, waiting for transfers between devices: 61.1 us -> 65.6 us  [shift(): return lax.ppermute(block, 'mlp', [((k + hops) % 4, k) for k in range(4)])]
  transfers between devices with their start and end apart: 28 -> 28, of which waited for: 15 -> 16; matrix products, arithmetic and copies ran while one was open for 1% -> 2% of each run, Pallas kernels for 46% -> 16%
where the time goes in v11:
time: 164 us
  waiting for transfers between devices  101 us (62%)
  starting transfers between devices  29.9 us (18%)
  Pallas kernels  28.1 us (17%)
  other arithmetic  2.82 us (2%)
  local copies, waits for them, and re-layouts  1.66 us (1%)
    ppermute x12, waiting for transfers between devices, shift(): return lax.ppermute(block, 'mlp', [((k + hops) % 4, k) for k in range(4)])  65.6 us
    ppermute x16, waiting for transfers between devices, exchange(): return lax.ppermute(block, axis, [(0, 1), (1, 0)])  35.8 us
    ppermute x12, starting transfers between devices, shift(): return lax.ppermute(block, 'mlp', [((k + hops) % 4, k) for k in range(4)])  17.8 us
    pallas_call x4, Pallas kernels, vmem_call(): pl.pallas_call(kernel, out_shape=outs, in_specs=[whole] * len(operands),...  14.9 us
    ppermute x16, starting transfers between devices, exchange(): return lax.ppermute(block, axis, [(0, 1), (1, 0)])  12.1 us
    pallas_call x3, Pallas kernels, staged(): pl.pallas_call(kernel, out_shape=[pltpu.VMEM(shape, group[0][0].dtype) fo...  10.1 us
  transfers between devices with their start and end apart: 28, of which 16 were waited for; matrix products, arithmetic and copies ran while one was open for 2% of the time, Pallas kernels for 16%

profile of v11, /device:TPU:0, one launch (start us, length us, event | category | flops | bytes accessed | tf_op | source)
XLA Modules:
  0.0 164.2 jit_solution(2328128647718852561)
XLA Ops:
  0.0 5.0 %collective-permute-start = (bf16[32,4096]{1,0:T(8,128)(2,1)}, bf16[32,4096]{1,0:T(8,128)(2,1)S(1)}, u32[]{:S(2)}, u32[]{:S(2)}) collective-permute-start(bf16[32,4096]{1,0:T(8,128)(2,1)} %refs_10_.1), channel_id=1, source_target_pairs={{1,0},{2,1},{3,2},{0,3},{5,4},{6,5},{7,6},{4,7},{9,8},{10,9},{11,1... | collective-permute-start | bytes 786440 | tf_op jit(solution)/shard_map/ppermute | solution.py:96
  5.1 1.0 collective-permute-start.2
  6.1 1.5 dynamic-slice_bitcast_fusion
  7.6 1.6 collective-permute-start.3
  9.2 3.1 %shard_map.183 = bf16[384,4096]{1,0:T(8,128)(2,1)} custom-call(bf16[192,4096]{1,0:T(8,128)(2,1)} %bitcast.17, bf16[192,4096]{1,0:T(8,128)(2,1)} %bitcast.19), custom_call_target="tpu_custom_call" | custom-call | bytes 1048576 | tf_op jit(solution)/shard_map/pallas_call | solution.py:205
  12.3 1.6 collective-permute-start.11
  14.2 0.3 fusion.4
  14.7 6.6 %shard_map.181 = (bf16[4096,512]{1,0:T(8,128)(2,1)S(1)}, bf16[4096,512]{1,0:T(8,128)(2,1)S(1)}, bf16[4096,512]{1,0:T(8,128)(2,1)S(1)}, bf16[512,4096]{1,0:T(8,12...) custom-call(bf16[4096,512]{1,0:T(8,128)(2,1)} %refs_0_.1, ...), custom_call_target="tpu_custom_call" | custom-call | bytes 38801408 | tf_op jit(solution)/shard_map/pallas_call | solution.py:170
  21.4 6.1 %collective-permute-done.1.block_2 = bf16[32,4096]{1,0:T(8,128)(2,1)S(1)} collective-permute-done((bf16[32,4096]{1,0:T(8,128)(2,1)}, bf16[32,4096]{1,0:T(8,128)(2,1)S(1)}, u32[]{:S(2)}, u32[]{:S(2)}) %collective-permute-start.1) | collective-permute-done | bytes 262176 | tf_op jit(solution)/shard_map/ppermute | solution.py:96
  27.6 4.5 %shard_map.182 = (bf16[32,4096]{1,0:T(8,128)(2,1)S(1)}, bf16[32,4096]{1,0:T(8,128)(2,1)S(1)}, bf16[32,4096]{1,0:T(8,128)(2,1)S(1)}, bf16[32,4096]{1,0:T(8,128)(2,1)S(1)}) custom-call(bf16[32,4096]{1,0:T(8,128)(2,1)S(1)} %get-tuple-element.54.block_0, bf16[32,4096]{1,0:T(8,128)(2,1)S(1)} %collective-permute-done.block_1, ...), custom_call_target="tpu_custom_call" | custom-call | flops 1048576 | bytes 1048576 | tf_op jit(solution)/shard_map/pallas_call | solution.py:120
  32.1 1.6 collective-permute-start.4
  33.7 1.3 collective-permute-start.5
  35.0 1.9 %collective-permute-start.6 = (bf16[32,4096]{1,0:T(8,128)(2,1)S(1)}, bf16[32,4096]{1,0:T(8,128)(2,1)S(1)}, u32[]{:S(2)}, u32[]{:S(2)}) collective-permute-start(bf16[32,4096]{1,0:T(8,128)(2,1)S(1)} %get-tuple-element.71), channel_id=1, source_target_pairs={{3,0},{0,1},{1,2},{2,3},{7,4},{4,5},{5,6},{6,7},{11,8},{8,9},{9,10... | collective-permute-start | bytes 786440 | tf_op jit(solution)/shard_map/ppermute | solution.py:96
  36.9 3.6 %collective-permute-done.4 = bf16[32,4096]{1,0:T(8,128)(2,1)S(1)} collective-permute-done((bf16[32,4096]{1,0:T(8,128)(2,1)S(1)}, bf16[32,4096]{1,0:T(8,128)(2,1)S(1)}, u32[]{:S(2)}, u32[]{:S(2)}) %collective-permute-start.4) | collective-permute-done | bytes 262176 | tf_op jit(solution)/shard_map/ppermute | solution.py:96
  40.5 17.0 %collective-permute-done.5 = bf16[32,4096]{1,0:T(8,128)(2,1)S(1)} collective-permute-done((bf16[32,4096]{1,0:T(8,128)(2,1)S(1)}, bf16[32,4096]{1,0:T(8,128)(2,1)S(1)}, u32[]{:S(2)}, u32[]{:S(2)}) %collective-permute-start.5) | collective-permute-done | bytes 262176 | tf_op jit(solution)/shard_map/ppermute | solution.py:96
  58.1 1.6 collective-permute-start.10
  59.7 0.6 collective-permute-start.8
  60.2 2.0 %collective-permute-start.9 = (bf16[32,4096]{1,0:T(8,128)(2,1)S(1)}, bf16[32,4096]{1,0:T(8,128)(2,1)S(1)}, u32[]{:S(2)}, u32[]{:S(2)}) collective-permute-start(bf16[32,4096]{1,0:T(8,128)(2,1)S(1)} %add_convert_fusion.1), channel_id=1, source_target_pairs={{3,0},{0,1},{1,2},{2,3},{7,4},{4,5},{5,6},{6,7},{11,8},{8,9},{9,10... | collective-permute-start | bytes 786440 | tf_op jit(solution)/shard_map/ppermute | solution.py:96
  62.3 2.8 %collective-permute-done.10 = bf16[32,4096]{1,0:T(8,128)(2,1)S(1)} collective-permute-done((bf16[32,4096]{1,0:T(8,128)(2,1)S(1)}, bf16[32,4096]{1,0:T(8,128)(2,1)S(1)}, u32[]{:S(2)}, u32[]{:S(2)}) %collective-permute-start.10) | collective-permute-done | bytes 262176 | tf_op jit(solution)/shard_map/ppermute | solution.py:92
  65.1 1.7 %collective-permute-done.7 = bf16[32,4096]{1,0:T(8,128)(2,1)S(1)} collective-permute-done((bf16[32,4096]{1,0:T(8,128)(2,1)S(1)}, bf16[32,4096]{1,0:T(8,128)(2,1)S(1)}, u32[]{:S(2)}, u32[]{:S(2)}) %collective-permute-start.7) | collective-permute-done | bytes 262176 | tf_op jit(solution)/shard_map/ppermute | solution.py:96
  66.8 1.5 collective-permute-start.12
  68.3 15.1 %collective-permute-done.8 = bf16[32,4096]{1,0:T(8,128)(2,1)S(1)} collective-permute-done((bf16[32,4096]{1,0:T(8,128)(2,1)S(1)}, bf16[32,4096]{1,0:T(8,128)(2,1)S(1)}, u32[]{:S(2)}, u32[]{:S(2)}) %collective-permute-start.8) | collective-permute-done | bytes 262176 | tf_op jit(solution)/shard_map/ppermute | solution.py:96
  83.5 6.2 %collective-permute-done.12 = bf16[96,2048]{1,0:T(8,128)(2,1)S(1)} collective-permute-done((bf16[96,2048]{1,0:T(8,128)(2,1)S(1)}, bf16[96,2048]{1,0:T(8,128)(2,1)S(1)}, u32[]{:S(2)}, u32[]{:S(2)}) %collective-permute-start.12) | collective-permute-done | bytes 393248 | tf_op jit(solution)/shard_map/ppermute | solution.py:92
  89.7 1.5 collective-permute-start.16
  91.2 0.5 collective-permute-start.13
  91.9 0.6 collective-permute-start.17
  92.5 3.1 %collective-permute-done.15.refs_3_ = bf16[384,4096]{1,0:T(8,128)(2,1)S(1)} collective-permute-done((bf16[384,4096]{1,0:T(8,128)(2,1)}, bf16[384,4096]{1,0:T(8,128)(2,1)S(1)}, u32[]{:S(2)}, u32[]{:S(2)}) %collective-permute-start.15) | collective-permute-done | bytes 3145760 | tf_op jit(solution)/shard_map/ppermute | solution.py:92
  95.7 3.0 %shard_map.184 = (bf16[768,4096]{1,0:T(8,128)(2,1)S(1)}, bf16[768,4096]{1,0:T(8,128)(2,1)S(1)}) custom-call(bf16[192,4096]{1,0:T(8,128)(2,1)} %bitcast.18, bf16[384,4096]{1,0:T(8,128)(2,1)S(1)} %collective-permute-done.14.refs_1_, bf16[384,4096]{1,0:T(8,128)(2,1)} %collective-permute-done.11.refs_2_, bf16[384,4096]{1,0:T(8,128)(2,1)S(1)} %collective-permute-done.15.refs_3_, ...), custom_call_target="tpu_custom_call" | custom-call | bytes 25165824 | tf_op jit(solution)/shard_map/pallas_call | solution.py:170
  98.7 4.3 %shard_map.185.own = bf16[128,768]{1,0:T(8,128)(2,1)S(1)} custom-call(bf16[128,4096]{1,0:T(8,128)(2,1)S(1)} %pad_maximum_fusion.states, bf16[768,4096]{1,0:T(8,128)(2,1)S(1)} %get-tuple-element.78.gate_rows, bf16[768,4096]{1,0:T(8,128)(2,1)S(1)} %get-tuple-element.79.up_rows), custom_call_target="tpu_custom_call" | custom-call | flops 1048576 | bytes 1048576 | tf_op jit(solution)/shard_map/pallas_call | solution.py:120
  103.0 7.0 %collective-permute-done.16.refs_6_ = bf16[192,2048]{1,0:T(8,128)(2,1)S(1)} collective-permute-done((bf16[192,2048]{1,0:T(8,128)(2,1)S(1)}, bf16[192,2048]{1,0:T(8,128)(2,1)S(1)}, u32[]{:S(2)}, u32[]{:S(2)}) %collective-permute-start.16) | collective-permute-done | bytes 786464 | tf_op jit(solution)/shard_map/ppermute | solution.py:92
  110.1 0.8 collective-permute-done.13
  111.0 4.3 %shard_map.186.other = bf16[128,768]{1,0:T(8,128)(2,1)S(1)} custom-call(bf16[128,4096]{1,0:T(8,128)(2,1)S(1)} %pad_maximum_fusion.1.states, bf16[768,4096]{1,0:T(8,128)(2,1)S(1)} %get-tuple-element.78.gate_rows, bf16[768,4096]{1,0:T(8,128)(2,1)S(1)} %get-tuple-element.79.up_rows), custom_call_target="tpu_custom_call" | custom-call | flops 1048576 | bytes 1048576 | tf_op jit(solution)/shard_map/pallas_call | solution.py:120
  115.3 2.8 %collective-permute-done.17 = bf16[96,2048]{1,0:T(8,128)(2,1)S(1)} collective-permute-done((bf16[96,2048]{1,0:T(8,128)(2,1)S(1)}, bf16[96,2048]{1,0:T(8,128)(2,1)S(1)}, u32[]{:S(2)}, u32[]{:S(2)}) %collective-permute-start.17) | collective-permute-done | bytes 393248 | tf_op jit(solution)/shard_map/ppermute | solution.py:92
  118.2 0.5 collective-permute-start.23
  118.7 0.5 collective-permute-start.19
  119.2 1.5 collective-permute-start.18
  120.7 5.7 %collective-permute-done.19.far_other = bf16[128,768]{1,0:T(8,128)(2,1)S(1)} collective-permute-done((bf16[128,768]{1,0:T(8,128)(2,1)S(1)}, bf16[128,768]{1,0:T(8,128)(2,1)S(1)}, u32[]{:S(2)}, u32[]{:S(2)}) %collective-permute-start.19) | collective-permute-done | bytes 196640 | tf_op jit(solution)/shard_map/ppermute | solution.py:92
  126.5 0.5 shard_map.187
  127.0 2.8 %collective-permute-done.18.far_own = bf16[128,768]{1,0:T(8,128)(2,1)S(1)} collective-permute-done((bf16[128,768]{1,0:T(8,128)(2,1)S(1)}, bf16[128,768]{1,0:T(8,128)(2,1)S(1)}, u32[]{:S(2)}, u32[]{:S(2)}) %collective-permute-start.18) | collective-permute-done | bytes 196640 | tf_op jit(solution)/shard_map/ppermute | solution.py:92
  129.8 1.8 %shard_map.188 = (bf16[64,2048]{1,0:T(8,128)(2,1)S(1)}, bf16[64,2048]{1,0:T(8,128)(2,1)S(1)}, bf16[64,2048]{1,0:T(8,128)(2,1)S(1)}, bf16[64,2048]{1,0:T(8,128)(2,1)S(1)}) custom-call(bf16[128,768]{1,0:T(8,128)(2,1)S(1)} %shard_map.185.own, bf16[128,768]{1,0:T(8,128)(2,1)S(1)} %shard_map.186.other, bf16[128,768]{1,0:T(8,128)(2,1)S(1)} %collective-permute-done.18.far_own, ...), custom_call_target="tpu_custom_call" | custom-call | flops 1048576 | bytes 1048576 | tf_op jit(solution)/shard_map/pallas_call | solution.py:120
  131.6 3.1 %collective-permute-start.24 = (bf16[64,2048]{1,0:T(8,128)(2,1)S(1)}, bf16[64,2048]{1,0:T(8,128)(2,1)S(1)}, u32[]{:S(2)}, u32[]{:S(2)}) collective-permute-start(bf16[64,2048]{1,0:T(8,128)(2,1)S(1)} %get-tuple-element.100), channel_id=1, source_target_pairs={{1,0},{2,1},{3,2},{0,3},{5,4},{6,5},{7,6},{4,7},{9,8},{10,9},{11,1... | collective-permute-start | bytes 786440 | tf_op jit(solution)/shard_map/ppermute | solution.py:96
  134.8 0.8 collective-permute-start.25
  135.6 0.3 collective-permute-start.26
  135.9 5.7 %collective-permute-done.24 = bf16[64,2048]{1,0:T(8,128)(2,1)S(1)} collective-permute-done((bf16[64,2048]{1,0:T(8,128)(2,1)S(1)}, bf16[64,2048]{1,0:T(8,128)(2,1)S(1)}, u32[]{:S(2)}, u32[]{:S(2)}) %collective-permute-start.24) | collective-permute-done | bytes 262176 | tf_op jit(solution)/shard_map/ppermute | solution.py:96
  141.6 16.3 %collective-permute-done.25 = bf16[64,2048]{1,0:T(8,128)(2,1)S(1)} collective-permute-done((bf16[64,2048]{1,0:T(8,128)(2,1)S(1)}, bf16[64,2048]{1,0:T(8,128)(2,1)S(1)}, u32[]{:S(2)}, u32[]{:S(2)}) %collective-permute-start.25) | collective-permute-done | bytes 262176 | tf_op jit(solution)/shard_map/ppermute | solution.py:96
  158.1 0.6 collective-permute-start.27
  158.6 4.5 %collective-permute-done.27 = bf16[32,2048]{1,0:T(8,128)(2,1)S(1)} collective-permute-done((bf16[32,2048]{1,0:T(8,128)(2,1)S(1)}, bf16[32,2048]{1,0:T(8,128)(2,1)S(1)}, u32[]{:S(2)}, u32[]{:S(2)}) %collective-permute-start.27) | collective-permute-done | bytes 131104 | tf_op jit(solution)/shard_map/ppermute | solution.py:92
  163.3 0.9 add_convert_fusion
  (58 shorter events, 2.1 us)
Async XLA Ops:
  0.0 21.4 %collective-permute-start = (bf16[32,4096]{1,0:T(8,128)(2,1)}, bf16[32,4096]{1,0:T(8,128)(2,1)S(1)}, u32[]{:S(2)}, u32[]{:S(2)}) collective-permute-start(bf16[32,4096]{1,0:T(8,128)(2,1)} %refs_10_.1), channel_id=1, source_target_pairs={{1,0},{2,1},{3,2},{0,3},{5,4},{6,5},{7,6},{4,7},{9,8},{10,9},{11,1... | collective-permute-start | bytes 786440 | tf_op jit(solution)/shard_map/ppermute | solution.py:96
  5.0 22.5 %collective-permute-start.1 = (bf16[32,4096]{1,0:T(8,128)(2,1)}, bf16[32,4096]{1,0:T(8,128)(2,1)S(1)}, u32[]{:S(2)}, u32[]{:S(2)}) collective-permute-start(bf16[32,4096]{1,0:T(8,128)(2,1)} %refs_10_.1), channel_id=1, source_target_pairs={{2,0},{3,1},{0,2},{1,3},{6,4},{7,5},{4,6},{5,7},{10,8},{11,9},{8,1... | collective-permute-start | bytes 786440 | tf_op jit(solution)/shard_map/ppermute | solution.py:96
  5.1 22.5 %collective-permute-start.2 = (bf16[32,4096]{1,0:T(8,128)(2,1)}, bf16[32,4096]{1,0:T(8,128)(2,1)S(1)}, u32[]{:S(2)}, u32[]{:S(2)}) collective-permute-start(bf16[32,4096]{1,0:T(8,128)(2,1)} %refs_10_.1), channel_id=1, source_target_pairs={{3,0},{0,1},{1,2},{2,3},{7,4},{4,5},{5,6},{6,7},{11,8},{8,9},{9,10... | collective-permute-start | bytes 786440 | tf_op jit(solution)/shard_map/ppermute | solution.py:96
  7.6 20.0 %collective-permute-start.3 = (bf16[192,2048]{1,0:T(8,128)(2,1)S(1)}, bf16[192,2048]{1,0:T(8,128)(2,1)S(1)}, u32[]{:S(2)}, u32[]{:S(2)}) collective-permute-start(bf16[192,2048]{1,0:T(8,128)(2,1)S(1)} %get-tuple-element.109), channel_id=1, source_target_pairs={{0,16},{16,0},{1,17},{17,1},{2,18},{18,2},{3,19},{19,3},{4,20},{20... | collective-permute-start | bytes 2359304 | tf_op jit(solution)/shard_map/ppermute | solution.py:92
  9.2 4.7 %copy-start.5 = (s32[1,4]{1,0:T(1,128)S(1)}, s32[1,4]{1,0:T(1,128)}, u32[]{:S(2)}) copy-start(s32[1,4]{1,0:T(1,128)} %param.20) | copy-start | bytes 52
  9.2 4.9 %copy-start.4 = (s32[1,4]{1,0:T(1,128)S(1)}, s32[1,4]{1,0:T(1,128)}, u32[]{:S(2)}) copy-start(s32[1,4]{1,0:T(1,128)} %param.21) | copy-start | bytes 52
  9.2 5.3 %copy-start.6 = (s32[8]{0:T(128)S(1)}, s32[8]{0:T(128)}, u32[]{:S(2)}) copy-start(s32[8]{0:T(128)} %param.22) | copy-start | bytes 100
  12.3 77.4 %collective-permute-start.11 = (bf16[384,4096]{1,0:T(8,128)(2,1)}, bf16[384,4096]{1,0:T(8,128)(2,1)}, u32[]{:S(2)}, u32[]{:S(2)}) collective-permute-start(bf16[384,4096]{1,0:T(8,128)(2,1)} %shard_map.183), channel_id=1, source_target_pairs={{0,8},{8,0},{1,9},{9,1},{2,10},{10,2},{3,11},{11,3},{4,12},{12,4},... | collective-permute-start | bytes 9437192 | tf_op jit(solution)/shard_map/ppermute | solution.py:92
  27.6 30.3 %copy-start.1 = (bf16[32,4096]{1,0:T(8,128)(2,1)S(1)}, bf16[32,4096]{1,0:T(8,128)(2,1)}, u32[]{:S(2)}) copy-start(bf16[32,4096]{1,0:T(8,128)(2,1)} %refs_10_.1) | copy-start | bytes 786436
  27.6 30.3 %copy-start.2 = (f32[4096]{0:T(1024)S(1)}, f32[4096]{0:T(1024)}, u32[]{:S(2)}) copy-start(f32[4096]{0:T(1024)} %param.33) | copy-start | bytes 49156
  32.1 33.0 %copy-start = (bf16[384,4096]{1,0:T(8,128)(2,1)S(1)}, bf16[384,4096]{1,0:T(8,128)(2,1)}, u32[]{:S(2)}) copy-start(bf16[384,4096]{1,0:T(8,128)(2,1)} %shard_map.183) | copy-start | bytes 9437188
  32.1 8.4 %collective-permute-start.4 = (bf16[32,4096]{1,0:T(8,128)(2,1)S(1)}, bf16[32,4096]{1,0:T(8,128)(2,1)S(1)}, u32[]{:S(2)}, u32[]{:S(2)}) collective-permute-start(bf16[32,4096]{1,0:T(8,128)(2,1)S(1)} %get-tuple-element.69), channel_id=1, source_target_pairs={{1,0},{2,1},{3,2},{0,3},{5,4},{6,5},{7,6},{4,7},{9,8},{10,9},{11,1... | collective-permute-start | bytes 786440 | tf_op jit(solution)/shard_map/ppermute | solution.py:96
  33.7 23.9 %collective-permute-start.5 = (bf16[32,4096]{1,0:T(8,128)(2,1)S(1)}, bf16[32,4096]{1,0:T(8,128)(2,1)S(1)}, u32[]{:S(2)}, u32[]{:S(2)}) collective-permute-start(bf16[32,4096]{1,0:T(8,128)(2,1)S(1)} %get-tuple-element.70), channel_id=1, source_target_pairs={{2,0},{3,1},{0,2},{1,3},{6,4},{7,5},{4,6},{5,7},{10,8},{11,9},{8,1... | collective-permute-start | bytes 786440 | tf_op jit(solution)/shard_map/ppermute | solution.py:96
  35.0 22.6 %collective-permute-start.6 = (bf16[32,4096]{1,0:T(8,128)(2,1)S(1)}, bf16[32,4096]{1,0:T(8,128)(2,1)S(1)}, u32[]{:S(2)}, u32[]{:S(2)}) collective-permute-start(bf16[32,4096]{1,0:T(8,128)(2,1)S(1)} %get-tuple-element.71), channel_id=1, source_target_pairs={{3,0},{0,1},{1,2},{2,3},{7,4},{4,5},{5,6},{6,7},{11,8},{8,9},{9,10... | collective-permute-start | bytes 786440 | tf_op jit(solution)/shard_map/ppermute | solution.py:96
  58.1 7.0 %collective-permute-start.10 = (bf16[32,4096]{1,0:T(8,128)(2,1)S(1)}, bf16[32,4096]{1,0:T(8,128)(2,1)S(1)}, u32[]{:S(2)}, u32[]{:S(2)}) collective-permute-start(bf16[32,4096]{1,0:T(8,128)(2,1)S(1)} %add_convert_fusion.1), channel_id=1, source_target_pairs={{0,16},{16,0},{1,17},{17,1},{2,18},{18,2},{3,19},{19,3},{4,20},{20... | collective-permute-start | bytes 786440 | tf_op jit(solution)/shard_map/ppermute | solution.py:92
  59.7 7.1 %collective-permute-start.7 = (bf16[32,4096]{1,0:T(8,128)(2,1)S(1)}, bf16[32,4096]{1,0:T(8,128)(2,1)S(1)}, u32[]{:S(2)}, u32[]{:S(2)}) collective-permute-start(bf16[32,4096]{1,0:T(8,128)(2,1)S(1)} %add_convert_fusion.1), channel_id=1, source_target_pairs={{1,0},{2,1},{3,2},{0,3},{5,4},{6,5},{7,6},{4,7},{9,8},{10,9},{11,1... | collective-permute-start | bytes 786440 | tf_op jit(solution)/shard_map/ppermute | solution.py:96
  59.7 23.7 %collective-permute-start.8 = (bf16[32,4096]{1,0:T(8,128)(2,1)S(1)}, bf16[32,4096]{1,0:T(8,128)(2,1)S(1)}, u32[]{:S(2)}, u32[]{:S(2)}) collective-permute-start(bf16[32,4096]{1,0:T(8,128)(2,1)S(1)} %add_convert_fusion.1), channel_id=1, source_target_pairs={{2,0},{3,1},{0,2},{1,3},{6,4},{7,5},{4,6},{5,7},{10,8},{11,9},{8,1... | collective-permute-start | bytes 786440 | tf_op jit(solution)/shard_map/ppermute | solution.py:96
  60.2 23.2 %collective-permute-start.9 = (bf16[32,4096]{1,0:T(8,128)(2,1)S(1)}, bf16[32,4096]{1,0:T(8,128)(2,1)S(1)}, u32[]{:S(2)}, u32[]{:S(2)}) collective-permute-start(bf16[32,4096]{1,0:T(8,128)(2,1)S(1)} %add_convert_fusion.1), channel_id=1, source_target_pairs={{3,0},{0,1},{1,2},{2,3},{7,4},{4,5},{5,6},{6,7},{11,8},{8,9},{9,10... | collective-permute-start | bytes 786440 | tf_op jit(solution)/shard_map/ppermute | solution.py:96
  65.1 26.8 %collective-permute-start.14 = (bf16[384,4096]{1,0:T(8,128)(2,1)S(1)}, bf16[384,4096]{1,0:T(8,128)(2,1)S(1)}, u32[]{:S(2)}, u32[]{:S(2)}) collective-permute-start(bf16[384,4096]{1,0:T(8,128)(2,1)S(1)} %copy-done), channel_id=1, source_target_pairs={{0,4},{4,0},{1,5},{5,1},{2,6},{6,2},{3,7},{7,3},{8,12},{12,8},{9,1... | collective-permute-start | bytes 9437192 | tf_op jit(solution)/shard_map/ppermute | solution.py:92
  66.8 22.9 %collective-permute-start.12 = (bf16[96,2048]{1,0:T(8,128)(2,1)S(1)}, bf16[96,2048]{1,0:T(8,128)(2,1)S(1)}, u32[]{:S(2)}, u32[]{:S(2)}) collective-permute-start(bf16[96,2048]{1,0:T(8,128)(2,1)S(1)} %get-tuple-element.111), channel_id=1, source_target_pairs={{0,8},{8,0},{1,9},{9,1},{2,10},{10,2},{3,11},{11,3},{4,12},{12,4},... | collective-permute-start | bytes 1179656 | tf_op jit(solution)/shard_map/ppermute | solution.py:92
  89.7 5.9 %collective-permute-start.15 = (bf16[384,4096]{1,0:T(8,128)(2,1)}, bf16[384,4096]{1,0:T(8,128)(2,1)S(1)}, u32[]{:S(2)}, u32[]{:S(2)}) collective-permute-start(bf16[384,4096]{1,0:T(8,128)(2,1)} %collective-permute-done.11.refs_2_), channel_id=1, source_target_pairs={{0,4},{4,0},{1,5},{5,1},{2,6},{6,2},{3,7},{7,3},{8,12},{12,8},{9,1... | collective-permute-start | bytes 9437192 | tf_op jit(solution)/shard_map/ppermute | solution.py:92
  89.7 20.3 %collective-permute-start.16 = (bf16[192,2048]{1,0:T(8,128)(2,1)S(1)}, bf16[192,2048]{1,0:T(8,128)(2,1)S(1)}, u32[]{:S(2)}, u32[]{:S(2)}) collective-permute-start(bf16[192,2048]{1,0:T(8,128)(2,1)S(1)} %collective-permute-done.3.refs_4_), channel_id=1, source_target_pairs={{0,8},{8,0},{1,9},{9,1},{2,10},{10,2},{3,11},{11,3},{4,12},{12,4},... | collective-permute-start | bytes 2359304 | tf_op jit(solution)/shard_map/ppermute | solution.py:92
  91.2 19.7 %collective-permute-start.13 = (bf16[96,4096]{1,0:T(8,128)(2,1)S(1)}, bf16[96,4096]{1,0:T(8,128)(2,1)S(1)}, u32[]{:S(2)}, u32[]{:S(2)}) collective-permute-start(bf16[96,4096]{1,0:T(8,128)(2,1)S(1)} %pad_maximum_fusion.2), channel_id=1, source_target_pairs={{0,16},{16,0},{1,17},{17,1},{2,18},{18,2},{3,19},{19,3},{4,20},{20... | collective-permute-start | bytes 2359304 | tf_op jit(solution)/shard_map/ppermute | solution.py:92
  91.7 27.5 %collective-permute-start.20 = (bf16[192,2048]{1,0:T(8,128)(2,1)S(1)}, bf16[192,2048]{1,0:T(8,128)(2,1)S(1)}, u32[]{:S(2)}, u32[]{:S(2)}) collective-permute-start(bf16[192,2048]{1,0:T(8,128)(2,1)S(1)} %get-tuple-element.89.refs_0_), channel_id=1, source_target_pairs={{0,4},{4,0},{1,5},{5,1},{2,6},{6,2},{3,7},{7,3},{8,12},{12,8},{9,1... | collective-permute-start | bytes 2359304 | tf_op jit(solution)/shard_map/ppermute | solution.py:92
  91.9 26.2 %collective-permute-start.17 = (bf16[96,2048]{1,0:T(8,128)(2,1)S(1)}, bf16[96,2048]{1,0:T(8,128)(2,1)S(1)}, u32[]{:S(2)}, u32[]{:S(2)}) collective-permute-start(bf16[96,2048]{1,0:T(8,128)(2,1)S(1)} %get-tuple-element.110), channel_id=1, source_target_pairs={{0,8},{8,0},{1,9},{9,1},{2,10},{10,2},{3,11},{11,3},{4,12},{12,4},... | collective-permute-start | bytes 1179656 | tf_op jit(solution)/shard_map/ppermute | solution.py:92
  95.6 25.2 %collective-permute-start.22 = (bf16[192,2048]{1,0:T(8,128)(2,1)S(1)}, bf16[192,2048]{1,0:T(8,128)(2,1)S(1)}, u32[]{:S(2)}, u32[]{:S(2)}) collective-permute-start(bf16[192,2048]{1,0:T(8,128)(2,1)S(1)} %collective-permute-done.3.refs_4_), channel_id=1, source_target_pairs={{0,4},{4,0},{1,5},{5,1},{2,6},{6,2},{3,7},{7,3},{8,12},{12,8},{9,1... | collective-permute-start | bytes 2359304 | tf_op jit(solution)/shard_map/ppermute | solution.py:92
  118.1 8.3 %collective-permute-start.21 = (bf16[192,2048]{1,0:T(8,128)(2,1)S(1)}, bf16[192,2048]{1,0:T(8,128)(2,1)S(1)}, u32[]{:S(2)}, u32[]{:S(2)}) collective-permute-start(bf16[192,2048]{1,0:T(8,128)(2,1)S(1)} %constant_dynamic-update-slice_fusion.refs_2_), channel_id=1, source_target_pairs={{0,4},{4,0},{1,5},{5,1},{2,6},{6,2},{3,7},{7,3},{8,12},{12,8},{9,1... | collective-permute-start | bytes 2359304 | tf_op jit(solution)/shard_map/ppermute | solution.py:92
  118.2 8.3 %collective-permute-start.23 = (bf16[192,2048]{1,0:T(8,128)(2,1)S(1)}, bf16[192,2048]{1,0:T(8,128)(2,1)S(1)}, u32[]{:S(2)}, u32[]{:S(2)}) collective-permute-start(bf16[192,2048]{1,0:T(8,128)(2,1)S(1)} %collective-permute-done.16.refs_6_), channel_id=1, source_target_pairs={{0,4},{4,0},{1,5},{5,1},{2,6},{6,2},{3,7},{7,3},{8,12},{12,8},{9,1... | collective-permute-start | bytes 2359304 | tf_op jit(solution)/shard_map/ppermute | solution.py:92
  118.7 7.8 %collective-permute-start.19 = (bf16[128,768]{1,0:T(8,128)(2,1)S(1)}, bf16[128,768]{1,0:T(8,128)(2,1)S(1)}, u32[]{:S(2)}, u32[]{:S(2)}) collective-permute-start(bf16[128,768]{1,0:T(8,128)(2,1)S(1)} %shard_map.185.own), channel_id=1, source_target_pairs={{0,16},{16,0},{1,17},{17,1},{2,18},{18,2},{3,19},{19,3},{4,20},{20... | collective-permute-start | bytes 589832 | tf_op jit(solution)/shard_map/ppermute | solution.py:92
  119.2 10.6 %collective-permute-start.18 = (bf16[128,768]{1,0:T(8,128)(2,1)S(1)}, bf16[128,768]{1,0:T(8,128)(2,1)S(1)}, u32[]{:S(2)}, u32[]{:S(2)}) collective-permute-start(bf16[128,768]{1,0:T(8,128)(2,1)S(1)} %shard_map.186.other), channel_id=1, source_target_pairs={{0,16},{16,0},{1,17},{17,1},{2,18},{18,2},{3,19},{19,3},{4,20},{20... | collective-permute-start | bytes 589832 | tf_op jit(solution)/shard_map/ppermute | solution.py:92
  131.6 31.7 %copy-start.3 = (f32[4096]{0:T(1024)S(1)}, f32[4096]{0:T(1024)}, u32[]{:S(2)}) copy-start(f32[4096]{0:T(1024)} %param.34) | copy-start | bytes 49156
  131.6 10.0 %collective-permute-start.24 = (bf16[64,2048]{1,0:T(8,128)(2,1)S(1)}, bf16[64,2048]{1,0:T(8,128)(2,1)S(1)}, u32[]{:S(2)}, u32[]{:S(2)}) collective-permute-start(bf16[64,2048]{1,0:T(8,128)(2,1)S(1)} %get-tuple-element.100), channel_id=1, source_target_pairs={{1,0},{2,1},{3,2},{0,3},{5,4},{6,5},{7,6},{4,7},{9,8},{10,9},{11,1... | collective-permute-start | bytes 786440 | tf_op jit(solution)/shard_map/ppermute | solution.py:96
  134.8 23.1 %collective-permute-start.25 = (bf16[64,2048]{1,0:T(8,128)(2,1)S(1)}, bf16[64,2048]{1,0:T(8,128)(2,1)S(1)}, u32[]{:S(2)}, u32[]{:S(2)}) collective-permute-start(bf16[64,2048]{1,0:T(8,128)(2,1)S(1)} %get-tuple-element.101), channel_id=1, source_target_pairs={{2,0},{3,1},{0,2},{1,3},{6,4},{7,5},{4,6},{5,7},{10,8},{11,9},{8,1... | collective-permute-start | bytes 786440 | tf_op jit(solution)/shard_map/ppermute | solution.py:96
  135.6 22.3 %collective-permute-start.26 = (bf16[64,2048]{1,0:T(8,128)(2,1)S(1)}, bf16[64,2048]{1,0:T(8,128)(2,1)S(1)}, u32[]{:S(2)}, u32[]{:S(2)}) collective-permute-start(bf16[64,2048]{1,0:T(8,128)(2,1)S(1)} %get-tuple-element.102), channel_id=1, source_target_pairs={{3,0},{0,1},{1,2},{2,3},{7,4},{4,5},{5,6},{6,7},{11,8},{8,9},{9,10... | collective-permute-start | bytes 786440 | tf_op jit(solution)/shard_map/ppermute | solution.py:96
  158.1 5.0 %collective-permute-start.27 = (bf16[32,2048]{1,0:T(8,128)(2,1)S(1)}, bf16[32,2048]{1,0:T(8,128)(2,1)S(1)}, u32[]{:S(2)}, u32[]{:S(2)}) collective-permute-start(bf16[32,2048]{1,0:T(8,128)(2,1)S(1)} %slice.14), channel_id=1, source_target_pairs={{0,16},{16,0},{1,17},{17,1},{2,18},{18,2},{3,19},{19,3},{4,20},{20... | collective-permute-start | bytes 393224 | tf_op jit(solution)/shard_map/ppermute | solution.py:92

commit v12 on v11

--- a/solution.py
+++ b/solution.py
@@ -304,19 +304,16 @@
         out[:, at] = hidden.astype(jnp.bfloat16)
 
 
-def down_kernel(own, other, far_own, far_other, near_rows, far_rows, out_0, out_1, out_2, out_3):
-    tok_dev = out_0.shape[0] // 2
+def down_kernel(near, far, near_rows, far_rows, out_0, out_1, out_2, out_3):
+    tok_dev = out_0.shape[0]
     step = 512
     for start in range(0, near_rows.shape[1], step):
         at = slice(start, start + step)
-        for side, (near, far) in enumerate(((own, far_own), (other, far_other))):
-            part = jnp.dot(near[...], near_rows[:, at], preferred_element_type=jnp.float32)
-            part += jnp.dot(far[...], far_rows[:, at], preferred_element_type=jnp.float32)
-            part = part.astype(jnp.bfloat16)
-            for k, out in enumerate((out_0, out_1, out_2, out_3)):
-                out[side * tok_dev : (side + 1) * tok_dev, at] = part[
-                    k * tok_dev : (k + 1) * tok_dev
-                ]
+        part = jnp.dot(near[...], near_rows[:, at], preferred_element_type=jnp.float32)
+        part += jnp.dot(far[...], far_rows[:, at], preferred_element_type=jnp.float32)
+        part = part.astype(jnp.bfloat16)
+        for k, out in enumerate((out_0, out_1, out_2, out_3)):
+            out[:, at] = part[k * tok_dev : (k + 1) * tok_dev]
 
 
 def add_normed(base, added, gain):
@@ -333,14 +330,14 @@
     units = gate_rows.shape[0]
     near = lax.dynamic_slice_in_dim(down_rows, y * half, half, axis=1)
     far = exchange(lax.dynamic_slice_in_dim(down_rows, (1 - y) * half, half, axis=1), "y")
-    gate_up = stacked(gate_rows, up_rows)
+    gate_up, line_input = together(stacked(gate_rows, up_rows), layer_input)
     gate_up_x = exchange(gate_up, "x")
     cosine, sine = jnp.cos(angles), jnp.sin(angles)
     block = jax.ShapeDtypeStruct((tok_dev, width), jnp.bfloat16)
     *staged_rows, own_block = staged(
         *([in_hbm(array)] for array in (*projections, *adapters, *head_gains, layer_input))
     )
-    *blocks, far = together(*line_gather(layer_input)[1:], far)
+    *blocks, far = together(*line_gather(line_input)[1:], far)
     parts = vmem_call(
         attention_kernel,
         [block] * 4,
@@ -383,24 +380,27 @@
 
     line_other = exchange(line, "y")
     hidden_own = hidden_units_of(own, line)
-    line_other, hidden_own, far_x = together(line_other, hidden_own, far_x)
+    line_other, hidden_own, far_x, near_x[1] = together(line_other, hidden_own, far_x, near_x[1])
     from_own = exchange(hidden_own, "y")
     far_pieces = four_pieces(far, far_x)
-    hidden_other, near_x[1] = together(hidden_units_of(other, line_other), near_x[1])
+    hidden_other = hidden_units_of(other, line_other)
     from_other = exchange(hidden_other, "y")
     near_pieces = four_pieces(near, jnp.concatenate(near_x))
-    from_own, *pieces = together(from_own, *near_pieces, *far_pieces)
-    near_all, far_all = staged(pieces[:4], pieces[4:])
-    parts = vmem_call(
-        down_kernel,
-        [jax.ShapeDtypeStruct((2 * tok_dev, half), jnp.bfloat16)] * 4,
-        [],
-        [hidden_own, hidden_other, from_other, from_own, near_all, far_all],
-        8,
-    )
-    summed = line_scatter(parts)
-    own_half = summed[:tok_dev]
-    other_half = exchange(summed[tok_dev:].astype(jnp.bfloat16), "y").astype(jnp.float32)
+    near_all, far_all = staged(near_pieces, far_pieces)
+
+    def summed_down(hidden, from_y):
+        parts = vmem_call(
+            down_kernel,
+            [jax.ShapeDtypeStruct((tok_dev, half), jnp.bfloat16)] * 4,
+            [],
+            [hidden, from_y, near_all, far_all],
+            8,
+        )
+        return line_scatter(parts)
+
+    other_half = exchange(summed_down(hidden_other, from_own).astype(jnp.bfloat16), "y")
+    own_half = summed_down(hidden_own, from_other)
+    other_half = other_half.astype(jnp.float32)
     mlp_own = jnp.concatenate(
         [jnp.where(y == 1, other_half, own_half), jnp.where(y == 1, own_half, other_half)], axis=1
     )

time: 164 us -> 155 us (0.945)
  waiting for transfers between devices: 101 us -> 82.7 us
  starting transfers between devices: 29.9 us -> 39.5 us
    ppermute x16, waiting for transfers between devices: 35.8 us -> 24.6 us  [exchange(): return lax.ppermute(block, axis, [(0, 1), (1, 0)])]
    ppermute x12 -> x15, starting transfers between devices: 17.8 us -> 27.4 us  [shift(): return lax.ppermute(block, 'mlp', [((k + hops) % 4, k) for k in range(4)])]
    ppermute x12 -> x15, waiting for transfers between devices: 65.6 us -> 58.1 us  [shift(): return lax.ppermute(block, 'mlp', [((k + hops) % 4, k) for k in range(4)])]
    pallas_call x4 -> x5, Pallas kernels: 14.9 us -> 15.1 us  [vmem_call(): pl.pallas_call(kernel, out_shape=outs, in_specs=[whole] * len(operands),...]
  transfers between devices with their start and end apart: 28 -> 31, of which waited for: 16 -> 12; matrix products, arithmetic and copies ran while one was open for 2% -> 2% of each run, Pallas kernels for 16% -> 16%
where the time goes in v12:
time: 155 us
  waiting for transfers between devices  82.7 us (53%)
  starting transfers between devices  39.5 us (25%)
  Pallas kernels  28.3 us (18%)
  other arithmetic  2.82 us (2%)
  local copies, waits for them, and re-layouts  1.61 us (1%)
    ppermute x15, waiting for transfers between devices, shift(): return lax.ppermute(block, 'mlp', [((k + hops) % 4, k) for k in range(4)])  58.1 us
    ppermute x15, starting transfers between devices, shift(): return lax.ppermute(block, 'mlp', [((k + hops) % 4, k) for k in range(4)])  27.4 us
    ppermute x16, waiting for transfers between devices, exchange(): return lax.ppermute(block, axis, [(0, 1), (1, 0)])  24.6 us
    pallas_call x5, Pallas kernels, vmem_call(): pl.pallas_call(kernel, out_shape=outs, in_specs=[whole] * len(operands),...  15.1 us
    ppermute x16, starting transfers between devices, exchange(): return lax.ppermute(block, axis, [(0, 1), (1, 0)])  12.1 us
    pallas_call x3, Pallas kernels, staged(): pl.pallas_call(kernel, out_shape=[pltpu.VMEM(shape, group[0][0].dtype) fo...  10.1 us
    pallas_call x1, Pallas kernels, stacked(): pl.pallas_call(kernel, out_shape=pltpu.HBM((count * rows, columns), array...  3.12 us
  transfers between devices with their start and end apart: 31, of which 12 were waited for; matrix products, arithmetic and copies ran while one was open for 2% of the time, Pallas kernels for 16%

profile of v12, /device:TPU:0, one launch (start us, length us, event | category | flops | bytes accessed | tf_op | source)
XLA Modules:
  0.0 155.2 jit_solution(7811977305461610341)
XLA Ops:
  0.0 3.1 %shard_map.182 = bf16[384,4096]{1,0:T(8,128)(2,1)} custom-call(bf16[192,4096]{1,0:T(8,128)(2,1)} %bitcast.17, bf16[192,4096]{1,0:T(8,128)(2,1)} %bitcast.19), custom_call_target="tpu_custom_call" | custom-call | bytes 1048576 | tf_op jit(solution)/shard_map/pallas_call | solution.py:205
  3.2 5.1 %collective-permute-start = (bf16[32,4096]{1,0:T(8,128)(2,1)S(1)}, bf16[32,4096]{1,0:T(8,128)(2,1)S(1)}, u32[]{:S(2)}, u32[]{:S(2)}) collective-permute-start(bf16[32,4096]{1,0:T(8,128)(2,1)S(1)} %copy-done), channel_id=1, source_target_pairs={{1,0},{2,1},{3,2},{0,3},{5,4},{6,5},{7,6},{4,7},{9,8},{10,9},{11,1... | collective-permute-start | bytes 786440 | tf_op jit(solution)/shard_map/ppermute | solution.py:96
  8.3 1.0 collective-permute-start.2
  9.3 1.5 dynamic-slice_bitcast_fusion
  10.8 1.6 %collective-permute-start.3 = (bf16[192,2048]{1,0:T(8,128)(2,1)S(1)}, bf16[192,2048]{1,0:T(8,128)(2,1)S(1)}, u32[]{:S(2)}, u32[]{:S(2)}) collective-permute-start(bf16[192,2048]{1,0:T(8,128)(2,1)S(1)} %get-tuple-element.101), channel_id=1, source_target_pairs={{0,16},{16,0},{1,17},{17,1},{2,18},{18,2},{3,19},{19,3},{4,20},{20... | collective-permute-start | bytes 2359304 | tf_op jit(solution)/shard_map/ppermute | solution.py:92
  12.4 1.5 collective-permute-start.11
  14.2 0.3 fusion.4
  14.7 6.6 %shard_map.181 = (bf16[4096,512]{1,0:T(8,128)(2,1)S(1)}, bf16[4096,512]{1,0:T(8,128)(2,1)S(1)}, bf16[4096,512]{1,0:T(8,128)(2,1)S(1)}, bf16[512,4096]{1,0:T(8,12...) custom-call(bf16[4096,512]{1,0:T(8,128)(2,1)} %refs_0_.1, ...), custom_call_target="tpu_custom_call" | custom-call | bytes 38801408 | tf_op jit(solution)/shard_map/pallas_call | solution.py:170
  21.4 9.2 %collective-permute-done.1.block_2 = bf16[32,4096]{1,0:T(8,128)(2,1)S(1)} collective-permute-done((bf16[32,4096]{1,0:T(8,128)(2,1)S(1)}, bf16[32,4096]{1,0:T(8,128)(2,1)S(1)}, u32[]{:S(2)}, u32[]{:S(2)}) %collective-permute-start.1) | collective-permute-done | bytes 262176 | tf_op jit(solution)/shard_map/ppermute | solution.py:96
  30.6 4.5 %shard_map.183 = (bf16[32,4096]{1,0:T(8,128)(2,1)S(1)}, bf16[32,4096]{1,0:T(8,128)(2,1)S(1)}, bf16[32,4096]{1,0:T(8,128)(2,1)S(1)}, bf16[32,4096]{1,0:T(8,128)(2,1)S(1)}) custom-call(bf16[32,4096]{1,0:T(8,128)(2,1)S(1)} %get-tuple-element.50.block_0, bf16[32,4096]{1,0:T(8,128)(2,1)S(1)} %collective-permute-done.block_1, ...), custom_call_target="tpu_custom_call" | custom-call | flops 1048576 | bytes 1048576 | tf_op jit(solution)/shard_map/pallas_call | solution.py:120
  35.1 1.8 %collective-permute-start.4 = (bf16[32,4096]{1,0:T(8,128)(2,1)S(1)}, bf16[32,4096]{1,0:T(8,128)(2,1)S(1)}, u32[]{:S(2)}, u32[]{:S(2)}) collective-permute-start(bf16[32,4096]{1,0:T(8,128)(2,1)S(1)} %get-tuple-element.66), channel_id=1, source_target_pairs={{1,0},{2,1},{3,2},{0,3},{5,4},{6,5},{7,6},{4,7},{9,8},{10,9},{11,1... | collective-permute-start | bytes 786440 | tf_op jit(solution)/shard_map/ppermute | solution.py:96
  36.9 1.1 collective-permute-start.5
  38.0 1.9 %collective-permute-start.6 = (bf16[32,4096]{1,0:T(8,128)(2,1)S(1)}, bf16[32,4096]{1,0:T(8,128)(2,1)S(1)}, u32[]{:S(2)}, u32[]{:S(2)}) collective-permute-start(bf16[32,4096]{1,0:T(8,128)(2,1)S(1)} %get-tuple-element.68), channel_id=1, source_target_pairs={{3,0},{0,1},{1,2},{2,3},{7,4},{4,5},{5,6},{6,7},{11,8},{8,9},{9,10... | collective-permute-start | bytes 786440 | tf_op jit(solution)/shard_map/ppermute | solution.py:96
  40.0 3.8 %collective-permute-done.4 = bf16[32,4096]{1,0:T(8,128)(2,1)S(1)} collective-permute-done((bf16[32,4096]{1,0:T(8,128)(2,1)S(1)}, bf16[32,4096]{1,0:T(8,128)(2,1)S(1)}, u32[]{:S(2)}, u32[]{:S(2)}) %collective-permute-start.4) | collective-permute-done | bytes 262176 | tf_op jit(solution)/shard_map/ppermute | solution.py:96
  43.7 16.8 %collective-permute-done.5 = bf16[32,4096]{1,0:T(8,128)(2,1)S(1)} collective-permute-done((bf16[32,4096]{1,0:T(8,128)(2,1)S(1)}, bf16[32,4096]{1,0:T(8,128)(2,1)S(1)}, u32[]{:S(2)}, u32[]{:S(2)}) %collective-permute-start.5) | collective-permute-done | bytes 262176 | tf_op jit(solution)/shard_map/ppermute | solution.py:96
  61.1 1.6 %collective-permute-start.10 = (bf16[32,4096]{1,0:T(8,128)(2,1)S(1)}, bf16[32,4096]{1,0:T(8,128)(2,1)S(1)}, u32[]{:S(2)}, u32[]{:S(2)}) collective-permute-start(bf16[32,4096]{1,0:T(8,128)(2,1)S(1)} %add_convert_fusion.1), channel_id=1, source_target_pairs={{0,16},{16,0},{1,17},{17,1},{2,18},{18,2},{3,19},{19,3},{4,20},{20... | collective-permute-start | bytes 786440 | tf_op jit(solution)/shard_map/ppermute | solution.py:92
  62.7 0.8 collective-permute-start.8
  63.5 2.0 %collective-permute-start.9 = (bf16[32,4096]{1,0:T(8,128)(2,1)S(1)}, bf16[32,4096]{1,0:T(8,128)(2,1)S(1)}, u32[]{:S(2)}, u32[]{:S(2)}) collective-permute-start(bf16[32,4096]{1,0:T(8,128)(2,1)S(1)} %add_convert_fusion.1), channel_id=1, source_target_pairs={{3,0},{0,1},{1,2},{2,3},{7,4},{4,5},{5,6},{6,7},{11,8},{8,9},{9,10... | collective-permute-start | bytes 786440 | tf_op jit(solution)/shard_map/ppermute | solution.py:96
  65.5 2.6 %collective-permute-done.10 = bf16[32,4096]{1,0:T(8,128)(2,1)S(1)} collective-permute-done((bf16[32,4096]{1,0:T(8,128)(2,1)S(1)}, bf16[32,4096]{1,0:T(8,128)(2,1)S(1)}, u32[]{:S(2)}, u32[]{:S(2)}) %collective-permute-start.10) | collective-permute-done | bytes 262176 | tf_op jit(solution)/shard_map/ppermute | solution.py:92
  68.1 1.6 %collective-permute-done.7 = bf16[32,4096]{1,0:T(8,128)(2,1)S(1)} collective-permute-done((bf16[32,4096]{1,0:T(8,128)(2,1)S(1)}, bf16[32,4096]{1,0:T(8,128)(2,1)S(1)}, u32[]{:S(2)}, u32[]{:S(2)}) %collective-permute-start.7) | collective-permute-done | bytes 262176 | tf_op jit(solution)/shard_map/ppermute | solution.py:96
  69.7 1.5 collective-permute-start.12
  71.2 15.4 %collective-permute-done.8 = bf16[32,4096]{1,0:T(8,128)(2,1)S(1)} collective-permute-done((bf16[32,4096]{1,0:T(8,128)(2,1)S(1)}, bf16[32,4096]{1,0:T(8,128)(2,1)S(1)}, u32[]{:S(2)}, u32[]{:S(2)}) %collective-permute-start.8) | collective-permute-done | bytes 262176 | tf_op jit(solution)/shard_map/ppermute | solution.py:96
  86.7 3.0 %collective-permute-done.12 = bf16[96,2048]{1,0:T(8,128)(2,1)S(1)} collective-permute-done((bf16[96,2048]{1,0:T(8,128)(2,1)S(1)}, bf16[96,2048]{1,0:T(8,128)(2,1)S(1)}, u32[]{:S(2)}, u32[]{:S(2)}) %collective-permute-start.12) | collective-permute-done | bytes 393248 | tf_op jit(solution)/shard_map/ppermute | solution.py:92
  89.7 1.5 collective-permute-start.16
  91.2 0.5 collective-permute-start.13
  91.7 0.5 collective-permute-start.17
  92.5 3.1 %collective-permute-done.15.refs_3_ = bf16[384,4096]{1,0:T(8,128)(2,1)S(1)} collective-permute-done((bf16[384,4096]{1,0:T(8,128)(2,1)}, bf16[384,4096]{1,0:T(8,128)(2,1)S(1)}, u32[]{:S(2)}, u32[]{:S(2)}) %collective-permute-start.15) | collective-permute-done | bytes 3145760 | tf_op jit(solution)/shard_map/ppermute | solution.py:92
  95.7 3.0 %shard_map.184 = (bf16[768,4096]{1,0:T(8,128)(2,1)S(1)}, bf16[768,4096]{1,0:T(8,128)(2,1)S(1)}) custom-call(bf16[192,4096]{1,0:T(8,128)(2,1)} %bitcast.18, bf16[384,4096]{1,0:T(8,128)(2,1)S(1)} %collective-permute-done.14.refs_1_, bf16[384,4096]{1,0:T(8,128)(2,1)} %collective-permute-done.11.refs_2_, bf16[384,4096]{1,0:T(8,128)(2,1)S(1)} %collective-permute-done.15.refs_3_, ...), custom_call_target="tpu_custom_call" | custom-call | bytes 25165824 | tf_op jit(solution)/shard_map/pallas_call | solution.py:170
  98.7 4.3 %shard_map.185.near = bf16[128,768]{1,0:T(8,128)(2,1)S(1)} custom-call(bf16[128,4096]{1,0:T(8,128)(2,1)S(1)} %pad_maximum_fusion.states, bf16[768,4096]{1,0:T(8,128)(2,1)S(1)} %get-tuple-element.77.gate_rows, bf16[768,4096]{1,0:T(8,128)(2,1)S(1)} %get-tuple-element.78.up_rows), custom_call_target="tpu_custom_call" | custom-call | flops 1048576 | bytes 1048576 | tf_op jit(solution)/shard_map/pallas_call | solution.py:120
  103.0 15.1 %collective-permute-done.17 = bf16[96,2048]{1,0:T(8,128)(2,1)S(1)} collective-permute-done((bf16[96,2048]{1,0:T(8,128)(2,1)S(1)}, bf16[96,2048]{1,0:T(8,128)(2,1)S(1)}, u32[]{:S(2)}, u32[]{:S(2)}) %collective-permute-start.17) | collective-permute-done | bytes 393248 | tf_op jit(solution)/shard_map/ppermute | solution.py:92
  118.2 0.5 collective-permute-start.22
  118.7 0.5 collective-permute-start.18
  119.3 4.3 %shard_map.186.near = bf16[128,768]{1,0:T(8,128)(2,1)S(1)} custom-call(bf16[128,4096]{1,0:T(8,128)(2,1)S(1)} %pad_maximum_fusion.1.states, bf16[768,4096]{1,0:T(8,128)(2,1)S(1)} %get-tuple-element.77.gate_rows, bf16[768,4096]{1,0:T(8,128)(2,1)S(1)} %get-tuple-element.78.up_rows), custom_call_target="tpu_custom_call" | custom-call | flops 1048576 | bytes 1048576 | tf_op jit(solution)/shard_map/pallas_call | solution.py:120
  123.6 1.6 %collective-permute-start.27 = (bf16[128,768]{1,0:T(8,128)(2,1)S(1)}, bf16[128,768]{1,0:T(8,128)(2,1)S(1)}, u32[]{:S(2)}, u32[]{:S(2)}) collective-permute-start(bf16[128,768]{1,0:T(8,128)(2,1)S(1)} %shard_map.186.near), channel_id=1, source_target_pairs={{0,16},{16,0},{1,17},{17,1},{2,18},{18,2},{3,19},{19,3},{4,20},{20... | collective-permute-start | bytes 589832 | tf_op jit(solution)/shard_map/ppermute | solution.py:92
  125.2 0.5 shard_map.187
  125.8 1.0 shard_map.188
  126.8 3.1 %collective-permute-start.23 = (bf16[32,2048]{1,0:T(8,128)(2,1)S(1)}, bf16[32,2048]{1,0:T(8,128)(2,1)S(1)}, u32[]{:S(2)}, u32[]{:S(2)}) collective-permute-start(bf16[32,2048]{1,0:T(8,128)(2,1)S(1)} %get-tuple-element.88), channel_id=1, source_target_pairs={{1,0},{2,1},{3,2},{0,3},{5,4},{6,5},{7,6},{4,7},{9,8},{10,9},{11,1... | collective-permute-start | bytes 393224 | tf_op jit(solution)/shard_map/ppermute | solution.py:96
  129.9 0.8 collective-permute-start.24
  130.8 0.3 collective-permute-start.25
  131.1 1.0 shard_map.189
  132.1 3.6 %collective-permute-start.28 = (bf16[32,2048]{1,0:T(8,128)(2,1)S(1)}, bf16[32,2048]{1,0:T(8,128)(2,1)S(1)}, u32[]{:S(2)}, u32[]{:S(2)}) collective-permute-start(bf16[32,2048]{1,0:T(8,128)(2,1)S(1)} %get-tuple-element.92), channel_id=1, source_target_pairs={{1,0},{2,1},{3,2},{0,3},{5,4},{6,5},{7,6},{4,7},{9,8},{10,9},{11,1... | collective-permute-start | bytes 393224 | tf_op jit(solution)/shard_map/ppermute | solution.py:96
  135.7 0.3 collective-permute-start.29
  135.9 5.5 %collective-permute-start.30 = (bf16[32,2048]{1,0:T(8,128)(2,1)S(1)}, bf16[32,2048]{1,0:T(8,128)(2,1)S(1)}, u32[]{:S(2)}, u32[]{:S(2)}) collective-permute-start(bf16[32,2048]{1,0:T(8,128)(2,1)S(1)} %get-tuple-element.94), channel_id=1, source_target_pairs={{3,0},{0,1},{1,2},{2,3},{7,4},{4,5},{5,6},{6,7},{11,8},{8,9},{9,10... | collective-permute-start | bytes 393224 | tf_op jit(solution)/shard_map/ppermute | solution.py:96
  141.4 7.6 %collective-permute-done.24 = bf16[32,2048]{1,0:T(8,128)(2,1)S(1)} collective-permute-done((bf16[32,2048]{1,0:T(8,128)(2,1)S(1)}, bf16[32,2048]{1,0:T(8,128)(2,1)S(1)}, u32[]{:S(2)}, u32[]{:S(2)}) %collective-permute-start.24) | collective-permute-done | bytes 131104 | tf_op jit(solution)/shard_map/ppermute | solution.py:96
  149.1 0.6 collective-permute-start.26
  149.7 3.7 %collective-permute-done.29 = bf16[32,2048]{1,0:T(8,128)(2,1)S(1)} collective-permute-done((bf16[32,2048]{1,0:T(8,128)(2,1)S(1)}, bf16[32,2048]{1,0:T(8,128)(2,1)S(1)}, u32[]{:S(2)}, u32[]{:S(2)}) %collective-permute-start.29) | collective-permute-done | bytes 131104 | tf_op jit(solution)/shard_map/ppermute | solution.py:96
  153.3 0.8 collective-permute-done.26
  154.4 0.9 add_convert_fusion
  (64 shorter events, 2.1 us)
Async XLA Ops:
  0.0 3.1 %copy-start = (bf16[32,4096]{1,0:T(8,128)(2,1)S(1)}, bf16[32,4096]{1,0:T(8,128)(2,1)}, u32[]{:S(2)}) copy-start(bf16[32,4096]{1,0:T(8,128)(2,1)} %refs_10_.1) | copy-start | bytes 786436
  3.1 10.7 %copy-start.5 = (s32[1,4]{1,0:T(1,128)S(1)}, s32[1,4]{1,0:T(1,128)}, u32[]{:S(2)}) copy-start(s32[1,4]{1,0:T(1,128)} %param.20) | copy-start | bytes 52
  3.2 10.9 %copy-start.4 = (s32[1,4]{1,0:T(1,128)S(1)}, s32[1,4]{1,0:T(1,128)}, u32[]{:S(2)}) copy-start(s32[1,4]{1,0:T(1,128)} %param.21) | copy-start | bytes 52
  3.2 11.3 %copy-start.6 = (s32[8]{0:T(128)S(1)}, s32[8]{0:T(128)}, u32[]{:S(2)}) copy-start(s32[8]{0:T(128)} %param.22) | copy-start | bytes 100
  3.2 18.2 %collective-permute-start = (bf16[32,4096]{1,0:T(8,128)(2,1)S(1)}, bf16[32,4096]{1,0:T(8,128)(2,1)S(1)}, u32[]{:S(2)}, u32[]{:S(2)}) collective-permute-start(bf16[32,4096]{1,0:T(8,128)(2,1)S(1)} %copy-done), channel_id=1, source_target_pairs={{1,0},{2,1},{3,2},{0,3},{5,4},{6,5},{7,6},{4,7},{9,8},{10,9},{11,1... | collective-permute-start | bytes 786440 | tf_op jit(solution)/shard_map/ppermute | solution.py:96
  8.3 22.3 %collective-permute-start.1 = (bf16[32,4096]{1,0:T(8,128)(2,1)S(1)}, bf16[32,4096]{1,0:T(8,128)(2,1)S(1)}, u32[]{:S(2)}, u32[]{:S(2)}) collective-permute-start(bf16[32,4096]{1,0:T(8,128)(2,1)S(1)} %copy-done), channel_id=1, source_target_pairs={{2,0},{3,1},{0,2},{1,3},{6,4},{7,5},{4,6},{5,7},{10,8},{11,9},{8,1... | collective-permute-start | bytes 786440 | tf_op jit(solution)/shard_map/ppermute | solution.py:96
  8.3 22.3 %collective-permute-start.2 = (bf16[32,4096]{1,0:T(8,128)(2,1)S(1)}, bf16[32,4096]{1,0:T(8,128)(2,1)S(1)}, u32[]{:S(2)}, u32[]{:S(2)}) collective-permute-start(bf16[32,4096]{1,0:T(8,128)(2,1)S(1)} %copy-done), channel_id=1, source_target_pairs={{3,0},{0,1},{1,2},{2,3},{7,4},{4,5},{5,6},{6,7},{11,8},{8,9},{9,10... | collective-permute-start | bytes 786440 | tf_op jit(solution)/shard_map/ppermute | solution.py:96
  10.8 19.8 %collective-permute-start.3 = (bf16[192,2048]{1,0:T(8,128)(2,1)S(1)}, bf16[192,2048]{1,0:T(8,128)(2,1)S(1)}, u32[]{:S(2)}, u32[]{:S(2)}) collective-permute-start(bf16[192,2048]{1,0:T(8,128)(2,1)S(1)} %get-tuple-element.101), channel_id=1, source_target_pairs={{0,16},{16,0},{1,17},{17,1},{2,18},{18,2},{3,19},{19,3},{4,20},{20... | collective-permute-start | bytes 2359304 | tf_op jit(solution)/shard_map/ppermute | solution.py:92
  12.4 77.4 %collective-permute-start.11 = (bf16[384,4096]{1,0:T(8,128)(2,1)}, bf16[384,4096]{1,0:T(8,128)(2,1)}, u32[]{:S(2)}, u32[]{:S(2)}) collective-permute-start(bf16[384,4096]{1,0:T(8,128)(2,1)} %shard_map.182), channel_id=1, source_target_pairs={{0,8},{8,0},{1,9},{9,1},{2,10},{10,2},{3,11},{11,3},{4,12},{12,4},... | collective-permute-start | bytes 9437192 | tf_op jit(solution)/shard_map/ppermute | solution.py:92
  30.6 30.3 %copy-start.1 = (bf16[32,4096]{1,0:T(8,128)(2,1)S(1)}, bf16[32,4096]{1,0:T(8,128)(2,1)}, u32[]{:S(2)}) copy-start(bf16[32,4096]{1,0:T(8,128)(2,1)} %refs_10_.1) | copy-start | bytes 786436
  30.6 30.3 %copy-start.2 = (f32[4096]{0:T(1024)S(1)}, f32[4096]{0:T(1024)}, u32[]{:S(2)}) copy-start(f32[4096]{0:T(1024)} %param.33) | copy-start | bytes 49156
  35.1 8.6 %collective-permute-start.4 = (bf16[32,4096]{1,0:T(8,128)(2,1)S(1)}, bf16[32,4096]{1,0:T(8,128)(2,1)S(1)}, u32[]{:S(2)}, u32[]{:S(2)}) collective-permute-start(bf16[32,4096]{1,0:T(8,128)(2,1)S(1)} %get-tuple-element.66), channel_id=1, source_target_pairs={{1,0},{2,1},{3,2},{0,3},{5,4},{6,5},{7,6},{4,7},{9,8},{10,9},{11,1... | collective-permute-start | bytes 786440 | tf_op jit(solution)/shard_map/ppermute | solution.py:96
  36.9 23.7 %collective-permute-start.5 = (bf16[32,4096]{1,0:T(8,128)(2,1)S(1)}, bf16[32,4096]{1,0:T(8,128)(2,1)S(1)}, u32[]{:S(2)}, u32[]{:S(2)}) collective-permute-start(bf16[32,4096]{1,0:T(8,128)(2,1)S(1)} %get-tuple-element.67), channel_id=1, source_target_pairs={{2,0},{3,1},{0,2},{1,3},{6,4},{7,5},{4,6},{5,7},{10,8},{11,9},{8,1... | collective-permute-start | bytes 786440 | tf_op jit(solution)/shard_map/ppermute | solution.py:96
  38.0 22.6 %collective-permute-start.6 = (bf16[32,4096]{1,0:T(8,128)(2,1)S(1)}, bf16[32,4096]{1,0:T(8,128)(2,1)S(1)}, u32[]{:S(2)}, u32[]{:S(2)}) collective-permute-start(bf16[32,4096]{1,0:T(8,128)(2,1)S(1)} %get-tuple-element.68), channel_id=1, source_target_pairs={{3,0},{0,1},{1,2},{2,3},{7,4},{4,5},{5,6},{6,7},{11,8},{8,9},{9,10... | collective-permute-start | bytes 786440 | tf_op jit(solution)/shard_map/ppermute | solution.py:96
  61.1 7.0 %collective-permute-start.10 = (bf16[32,4096]{1,0:T(8,128)(2,1)S(1)}, bf16[32,4096]{1,0:T(8,128)(2,1)S(1)}, u32[]{:S(2)}, u32[]{:S(2)}) collective-permute-start(bf16[32,4096]{1,0:T(8,128)(2,1)S(1)} %add_convert_fusion.1), channel_id=1, source_target_pairs={{0,16},{16,0},{1,17},{17,1},{2,18},{18,2},{3,19},{19,3},{4,20},{20... | collective-permute-start | bytes 786440 | tf_op jit(solution)/shard_map/ppermute | solution.py:92
  62.7 7.0 %collective-permute-start.7 = (bf16[32,4096]{1,0:T(8,128)(2,1)S(1)}, bf16[32,4096]{1,0:T(8,128)(2,1)S(1)}, u32[]{:S(2)}, u32[]{:S(2)}) collective-permute-start(bf16[32,4096]{1,0:T(8,128)(2,1)S(1)} %add_convert_fusion.1), channel_id=1, source_target_pairs={{1,0},{2,1},{3,2},{0,3},{5,4},{6,5},{7,6},{4,7},{9,8},{10,9},{11,1... | collective-permute-start | bytes 786440 | tf_op jit(solution)/shard_map/ppermute | solution.py:96
  62.7 23.9 %collective-permute-start.8 = (bf16[32,4096]{1,0:T(8,128)(2,1)S(1)}, bf16[32,4096]{1,0:T(8,128)(2,1)S(1)}, u32[]{:S(2)}, u32[]{:S(2)}) collective-permute-start(bf16[32,4096]{1,0:T(8,128)(2,1)S(1)} %add_convert_fusion.1), channel_id=1, source_target_pairs={{2,0},{3,1},{0,2},{1,3},{6,4},{7,5},{4,6},{5,7},{10,8},{11,9},{8,1... | collective-permute-start | bytes 786440 | tf_op jit(solution)/shard_map/ppermute | solution.py:96
  63.5 23.2 %collective-permute-start.9 = (bf16[32,4096]{1,0:T(8,128)(2,1)S(1)}, bf16[32,4096]{1,0:T(8,128)(2,1)S(1)}, u32[]{:S(2)}, u32[]{:S(2)}) collective-permute-start(bf16[32,4096]{1,0:T(8,128)(2,1)S(1)} %add_convert_fusion.1), channel_id=1, source_target_pairs={{3,0},{0,1},{1,2},{2,3},{7,4},{4,5},{5,6},{6,7},{11,8},{8,9},{9,10... | collective-permute-start | bytes 786440 | tf_op jit(solution)/shard_map/ppermute | solution.py:96
  68.1 24.3 %collective-permute-start.14 = (bf16[384,4096]{1,0:T(8,128)(2,1)}, bf16[384,4096]{1,0:T(8,128)(2,1)S(1)}, u32[]{:S(2)}, u32[]{:S(2)}) collective-permute-start(bf16[384,4096]{1,0:T(8,128)(2,1)} %shard_map.182), channel_id=1, source_target_pairs={{0,4},{4,0},{1,5},{5,1},{2,6},{6,2},{3,7},{7,3},{8,12},{12,8},{9,1... | collective-permute-start | bytes 9437192 | tf_op jit(solution)/shard_map/ppermute | solution.py:92
  69.7 20.0 %collective-permute-start.12 = (bf16[96,2048]{1,0:T(8,128)(2,1)S(1)}, bf16[96,2048]{1,0:T(8,128)(2,1)S(1)}, u32[]{:S(2)}, u32[]{:S(2)}) collective-permute-start(bf16[96,2048]{1,0:T(8,128)(2,1)S(1)} %get-tuple-element.103), channel_id=1, source_target_pairs={{0,8},{8,0},{1,9},{9,1},{2,10},{10,2},{3,11},{11,3},{4,12},{12,4},... | collective-permute-start | bytes 1179656 | tf_op jit(solution)/shard_map/ppermute | solution.py:92
  89.7 5.9 %collective-permute-start.15 = (bf16[384,4096]{1,0:T(8,128)(2,1)}, bf16[384,4096]{1,0:T(8,128)(2,1)S(1)}, u32[]{:S(2)}, u32[]{:S(2)}) collective-permute-start(bf16[384,4096]{1,0:T(8,128)(2,1)} %collective-permute-done.11.refs_2_), channel_id=1, source_target_pairs={{0,4},{4,0},{1,5},{5,1},{2,6},{6,2},{3,7},{7,3},{8,12},{12,8},{9,1... | collective-permute-start | bytes 9437192 | tf_op jit(solution)/shard_map/ppermute | solution.py:92
  89.7 28.4 %collective-permute-start.16 = (bf16[192,2048]{1,0:T(8,128)(2,1)S(1)}, bf16[192,2048]{1,0:T(8,128)(2,1)S(1)}, u32[]{:S(2)}, u32[]{:S(2)}) collective-permute-start(bf16[192,2048]{1,0:T(8,128)(2,1)S(1)} %collective-permute-done.3.refs_4_), channel_id=1, source_target_pairs={{0,8},{8,0},{1,9},{9,1},{2,10},{10,2},{3,11},{11,3},{4,12},{12,4},... | collective-permute-start | bytes 2359304 | tf_op jit(solution)/shard_map/ppermute | solution.py:92
  91.2 26.9 %collective-permute-start.13 = (bf16[96,4096]{1,0:T(8,128)(2,1)S(1)}, bf16[96,4096]{1,0:T(8,128)(2,1)S(1)}, u32[]{:S(2)}, u32[]{:S(2)}) collective-permute-start(bf16[96,4096]{1,0:T(8,128)(2,1)S(1)} %pad_maximum_fusion.2), channel_id=1, source_target_pairs={{0,16},{16,0},{1,17},{17,1},{2,18},{18,2},{3,19},{19,3},{4,20},{20... | collective-permute-start | bytes 2359304 | tf_op jit(solution)/shard_map/ppermute | solution.py:92
  91.7 26.4 %collective-permute-start.17 = (bf16[96,2048]{1,0:T(8,128)(2,1)S(1)}, bf16[96,2048]{1,0:T(8,128)(2,1)S(1)}, u32[]{:S(2)}, u32[]{:S(2)}) collective-permute-start(bf16[96,2048]{1,0:T(8,128)(2,1)S(1)} %get-tuple-element.102), channel_id=1, source_target_pairs={{0,8},{8,0},{1,9},{9,1},{2,10},{10,2},{3,11},{11,3},{4,12},{12,4},... | collective-permute-start | bytes 1179656 | tf_op jit(solution)/shard_map/ppermute | solution.py:92
  92.4 31.2 %collective-permute-start.19 = (bf16[192,2048]{1,0:T(8,128)(2,1)S(1)}, bf16[192,2048]{1,0:T(8,128)(2,1)S(1)}, u32[]{:S(2)}, u32[]{:S(2)}) collective-permute-start(bf16[192,2048]{1,0:T(8,128)(2,1)S(1)} %get-tuple-element.100.refs_0_), channel_id=1, source_target_pairs={{0,4},{4,0},{1,5},{5,1},{2,6},{6,2},{3,7},{7,3},{8,12},{12,8},{9,1... | collective-permute-start | bytes 2359304 | tf_op jit(solution)/shard_map/ppermute | solution.py:92
  95.6 29.6 %collective-permute-start.21 = (bf16[192,2048]{1,0:T(8,128)(2,1)S(1)}, bf16[192,2048]{1,0:T(8,128)(2,1)S(1)}, u32[]{:S(2)}, u32[]{:S(2)}) collective-permute-start(bf16[192,2048]{1,0:T(8,128)(2,1)S(1)} %collective-permute-done.3.refs_4_), channel_id=1, source_target_pairs={{0,4},{4,0},{1,5},{5,1},{2,6},{6,2},{3,7},{7,3},{8,12},{12,8},{9,1... | collective-permute-start | bytes 2359304 | tf_op jit(solution)/shard_map/ppermute | solution.py:92
  118.1 7.1 %collective-permute-start.20 = (bf16[192,2048]{1,0:T(8,128)(2,1)S(1)}, bf16[192,2048]{1,0:T(8,128)(2,1)S(1)}, u32[]{:S(2)}, u32[]{:S(2)}) collective-permute-start(bf16[192,2048]{1,0:T(8,128)(2,1)S(1)} %constant_dynamic-update-slice_fusion.refs_2_), channel_id=1, source_target_pairs={{0,4},{4,0},{1,5},{5,1},{2,6},{6,2},{3,7},{7,3},{8,12},{12,8},{9,1... | collective-permute-start | bytes 2359304 | tf_op jit(solution)/shard_map/ppermute | solution.py:92
  118.2 7.0 %collective-permute-start.22 = (bf16[192,2048]{1,0:T(8,128)(2,1)S(1)}, bf16[192,2048]{1,0:T(8,128)(2,1)S(1)}, u32[]{:S(2)}, u32[]{:S(2)}) collective-permute-start(bf16[192,2048]{1,0:T(8,128)(2,1)S(1)} %collective-permute-done.16.refs_6_), channel_id=1, source_target_pairs={{0,4},{4,0},{1,5},{5,1},{2,6},{6,2},{3,7},{7,3},{8,12},{12,8},{9,1... | collective-permute-start | bytes 2359304 | tf_op jit(solution)/shard_map/ppermute | solution.py:92
  118.7 7.0 %collective-permute-start.18 = (bf16[128,768]{1,0:T(8,128)(2,1)S(1)}, bf16[128,768]{1,0:T(8,128)(2,1)S(1)}, u32[]{:S(2)}, u32[]{:S(2)}) collective-permute-start(bf16[128,768]{1,0:T(8,128)(2,1)S(1)} %shard_map.185.near), channel_id=1, source_target_pairs={{0,16},{16,0},{1,17},{17,1},{2,18},{18,2},{3,19},{19,3},{4,20},{20... | collective-permute-start | bytes 589832 | tf_op jit(solution)/shard_map/ppermute | solution.py:92
  123.6 7.4 %collective-permute-start.27 = (bf16[128,768]{1,0:T(8,128)(2,1)S(1)}, bf16[128,768]{1,0:T(8,128)(2,1)S(1)}, u32[]{:S(2)}, u32[]{:S(2)}) collective-permute-start(bf16[128,768]{1,0:T(8,128)(2,1)S(1)} %shard_map.186.near), channel_id=1, source_target_pairs={{0,16},{16,0},{1,17},{17,1},{2,18},{18,2},{3,19},{19,3},{4,20},{20... | collective-permute-start | bytes 589832 | tf_op jit(solution)/shard_map/ppermute | solution.py:92
  126.8 9.2 %collective-permute-start.23 = (bf16[32,2048]{1,0:T(8,128)(2,1)S(1)}, bf16[32,2048]{1,0:T(8,128)(2,1)S(1)}, u32[]{:S(2)}, u32[]{:S(2)}) collective-permute-start(bf16[32,2048]{1,0:T(8,128)(2,1)S(1)} %get-tuple-element.88), channel_id=1, source_target_pairs={{1,0},{2,1},{3,2},{0,3},{5,4},{6,5},{7,6},{4,7},{9,8},{10,9},{11,1... | collective-permute-start | bytes 393224 | tf_op jit(solution)/shard_map/ppermute | solution.py:96
  129.9 19.1 %collective-permute-start.24 = (bf16[32,2048]{1,0:T(8,128)(2,1)S(1)}, bf16[32,2048]{1,0:T(8,128)(2,1)S(1)}, u32[]{:S(2)}, u32[]{:S(2)}) collective-permute-start(bf16[32,2048]{1,0:T(8,128)(2,1)S(1)} %get-tuple-element.89), channel_id=1, source_target_pairs={{2,0},{3,1},{0,2},{1,3},{6,4},{7,5},{4,6},{5,7},{10,8},{11,9},{8,1... | collective-permute-start | bytes 393224 | tf_op jit(solution)/shard_map/ppermute | solution.py:96
  130.8 23.6 %copy-start.3 = (f32[4096]{0:T(1024)S(1)}, f32[4096]{0:T(1024)}, u32[]{:S(2)}) copy-start(f32[4096]{0:T(1024)} %param.34) | copy-start | bytes 49156
  130.8 18.2 %collective-permute-start.25 = (bf16[32,2048]{1,0:T(8,128)(2,1)S(1)}, bf16[32,2048]{1,0:T(8,128)(2,1)S(1)}, u32[]{:S(2)}, u32[]{:S(2)}) collective-permute-start(bf16[32,2048]{1,0:T(8,128)(2,1)S(1)} %get-tuple-element.90), channel_id=1, source_target_pairs={{3,0},{0,1},{1,2},{2,3},{7,4},{4,5},{5,6},{6,7},{11,8},{8,9},{9,10... | collective-permute-start | bytes 393224 | tf_op jit(solution)/shard_map/ppermute | solution.py:96
  132.1 17.6 %collective-permute-start.28 = (bf16[32,2048]{1,0:T(8,128)(2,1)S(1)}, bf16[32,2048]{1,0:T(8,128)(2,1)S(1)}, u32[]{:S(2)}, u32[]{:S(2)}) collective-permute-start(bf16[32,2048]{1,0:T(8,128)(2,1)S(1)} %get-tuple-element.92), channel_id=1, source_target_pairs={{1,0},{2,1},{3,2},{0,3},{5,4},{6,5},{7,6},{4,7},{9,8},{10,9},{11,1... | collective-permute-start | bytes 393224 | tf_op jit(solution)/shard_map/ppermute | solution.py:96
  135.7 17.7 %collective-permute-start.29 = (bf16[32,2048]{1,0:T(8,128)(2,1)S(1)}, bf16[32,2048]{1,0:T(8,128)(2,1)S(1)}, u32[]{:S(2)}, u32[]{:S(2)}) collective-permute-start(bf16[32,2048]{1,0:T(8,128)(2,1)S(1)} %get-tuple-element.93), channel_id=1, source_target_pairs={{2,0},{3,1},{0,2},{1,3},{6,4},{7,5},{4,6},{5,7},{10,8},{11,9},{8,1... | collective-permute-start | bytes 393224 | tf_op jit(solution)/shard_map/ppermute | solution.py:96
  135.9 17.4 %collective-permute-start.30 = (bf16[32,2048]{1,0:T(8,128)(2,1)S(1)}, bf16[32,2048]{1,0:T(8,128)(2,1)S(1)}, u32[]{:S(2)}, u32[]{:S(2)}) collective-permute-start(bf16[32,2048]{1,0:T(8,128)(2,1)S(1)} %get-tuple-element.94), channel_id=1, source_target_pairs={{3,0},{0,1},{1,2},{2,3},{7,4},{4,5},{5,6},{6,7},{11,8},{8,9},{9,10... | collective-permute-start | bytes 393224 | tf_op jit(solution)/shard_map/ppermute | solution.py:96
  149.1 5.0 %collective-permute-start.26 = (bf16[32,2048]{1,0:T(8,128)(2,1)S(1)}, bf16[32,2048]{1,0:T(8,128)(2,1)S(1)}, u32[]{:S(2)}, u32[]{:S(2)}) collective-permute-start(bf16[32,2048]{1,0:T(8,128)(2,1)S(1)} %add_convert_fusion.2), channel_id=1, source_target_pairs={{0,16},{16,0},{1,17},{17,1},{2,18},{18,2},{3,19},{19,3},{4,20},{20... | collective-permute-start | bytes 393224 | tf_op jit(solution)/shard_map/ppermute | solution.py:92

commit v13 on v12

--- a/solution.py
+++ b/solution.py
@@ -101,18 +101,22 @@
     return [block, shift(block, 1), across, shift(block, 3)]
 
 
-def line_scatter(parts):
+def line_arrivals(parts):
     across = shift(parts[2], 2)
-    arrived = (parts[0], shift(parts[3], 1), across, shift(parts[1], 3))
-    return sum(part.astype(jnp.float32) for part in arrived)
+    return [shift(parts[3], 1), across, shift(parts[1], 3), parts[0]]
+
+
+def line_sum(arrivals):
+    return sum(part.astype(jnp.float32) for part in arrivals)
 
 
 def together(*values):
     return lax.optimization_barrier(values)
 
 
-def four_pieces(rows, rows_x):
-    return [rows, exchange(rows, "core"), rows_x, exchange(rows_x, "core")]
+def both_halves(*rows):
+    (half,) = staged(rows)
+    return half, pltpu.with_memory_space_constraint(exchange(half, "core"), pltpu.VMEM)
 
 
 def vmem_call(kernel, outs, scratch, operands, vmem_mib):
@@ -176,45 +180,6 @@
         compiler_params=pltpu.CompilerParams(vmem_limit_bytes=1 << 20),
         cost_estimate=pl.CostEstimate(flops=0, bytes_accessed=4 * size, transcendentals=0),
     )(*arrays)
-
-
-def stacked(*arrays):
-    rows, columns = arrays[0].shape
-
-    def kernel(*refs):
-        sources, target, buffer, sems_in, sems_out = refs[:-4], *refs[-4:]
-        into = [
-            pltpu.make_async_copy(source, buffer.at[k], sems_in.at[k])
-            for k, source in enumerate(sources)
-        ]
-        out = [
-            pltpu.make_async_copy(
-                buffer.at[k], target.at[pl.ds(k * rows, rows), :], sems_out.at[k]
-            )
-            for k in range(len(sources))
-        ]
-        for copy in into:
-            copy.start()
-        for copy_in, copy_out in zip(into, out):
-            copy_in.wait()
-            copy_out.start()
-        for copy in out:
-            copy.wait()
-
-    count = len(arrays)
-    return pl.pallas_call(
-        kernel,
-        out_shape=pltpu.HBM((count * rows, columns), arrays[0].dtype),
-        in_specs=[pl.BlockSpec(memory_space=pl.ANY)] * count,
-        out_specs=pl.BlockSpec(memory_space=pltpu.HBM),
-        scratch_shapes=[
-            pltpu.VMEM((count, rows, columns), arrays[0].dtype),
-            pltpu.SemaphoreType.DMA((count,)),
-            pltpu.SemaphoreType.DMA((count,)),
-        ],
-        compiler_params=pltpu.CompilerParams(vmem_limit_bytes=8 << 20),
-        cost_estimate=pl.CostEstimate(flops=0, bytes_accessed=1 << 20, transcendentals=0),
-    )(*(in_hbm(array) for array in arrays))
 
 
 NT = (((1,), (1,)), ((), ()))
@@ -290,27 +255,30 @@
             out[:, at] = part[k * tok_dev : (k + 1) * tok_dev]
 
 
-def hidden_kernel(states, gate_rows, up_rows, out):
-    step = 256
-    for start in range(0, gate_rows.shape[0], step):
+def hidden_kernel(states, gate_0, gate_1, up_0, up_1, out):
+    count = gate_0.shape[0]
+    for k, (gate_rows, up_rows) in enumerate(((gate_0, up_0), (gate_1, up_1))):
+        gate_act = lax.dot_general(
+            states[...], gate_rows[...], NT, preferred_element_type=jnp.float32
+        )
+        up_act = lax.dot_general(states[...], up_rows[...], NT, preferred_element_type=jnp.float32)
+        hidden = gate_act / (1.0 + jnp.exp(-gate_act)) * up_act
+        out[:, k * count : (k + 1) * count] = hidden.astype(jnp.bfloat16)
+
+
+def down_kernel(near, far, near_0, near_1, far_0, far_1, out_0, out_1, out_2, out_3):
+    tok_dev, count = out_0.shape[0], near_0.shape[0]
+    step = 512
+    for start in range(0, near_0.shape[1], step):
         at = slice(start, start + step)
-        gate_act = lax.dot_general(
-            states[...], gate_rows[at, :], NT, preferred_element_type=jnp.float32
-        )
-        up_act = lax.dot_general(
-            states[...], up_rows[at, :], NT, preferred_element_type=jnp.float32
-        )
-        hidden = gate_act / (1.0 + jnp.exp(-gate_act)) * up_act
-        out[:, at] = hidden.astype(jnp.bfloat16)
-
-
-def down_kernel(near, far, near_rows, far_rows, out_0, out_1, out_2, out_3):
-    tok_dev = out_0.shape[0]
-    step = 512
-    for start in range(0, near_rows.shape[1], step):
-        at = slice(start, start + step)
-        part = jnp.dot(near[...], near_rows[:, at], preferred_element_type=jnp.float32)
-        part += jnp.dot(far[...], far_rows[:, at], preferred_element_type=jnp.float32)
+        part = 0.0
+        for hidden, halves in ((near, (near_0, near_1)), (far, (far_0, far_1))):
+            for k, rows in enumerate(halves):
+                part += jnp.dot(
+                    hidden[:, k * count : (k + 1) * count],
+                    rows[:, at],
+                    preferred_element_type=jnp.float32,
+                )
         part = part.astype(jnp.bfloat16)
         for k, out in enumerate((out_0, out_1, out_2, out_3)):
             out[:, at] = part[k * tok_dev : (k + 1) * tok_dev]
@@ -327,17 +295,15 @@
     gate_rows, up_rows, down_rows = ffn_rows
     y = lax.axis_index("y")
     half = width // 2
-    units = gate_rows.shape[0]
     near = lax.dynamic_slice_in_dim(down_rows, y * half, half, axis=1)
     far = exchange(lax.dynamic_slice_in_dim(down_rows, (1 - y) * half, half, axis=1), "y")
-    gate_up, line_input = together(stacked(gate_rows, up_rows), layer_input)
-    gate_up_x = exchange(gate_up, "x")
+    gate_x = exchange(gate_rows, "x")
     cosine, sine = jnp.cos(angles), jnp.sin(angles)
     block = jax.ShapeDtypeStruct((tok_dev, width), jnp.bfloat16)
     *staged_rows, own_block = staged(
         *([in_hbm(array)] for array in (*projections, *adapters, *head_gains, layer_input))
     )
-    *blocks, far = together(*line_gather(line_input)[1:], far)
+    *blocks, far = together(*line_gather(layer_input)[1:], far)
     parts = vmem_call(
         attention_kernel,
         [block] * 4,
@@ -356,24 +322,26 @@
         ],
         8,
     )
-    near_x = [exchange(rows, "x") for rows in jnp.split(near, 2)]
-    attn_own = line_scatter(parts)
+    near_x = [exchange(rows, "x") for rows in jnp.split(near, [near.shape[0] // 6])]
+    arrivals = line_arrivals(parts)
+    arrivals[0], gate_x, up_late = together(arrivals[0], gate_x, up_rows)
+    units = up_late.shape[0]
+    up_parts = jnp.split(up_late, [units * 5 // 12])
+    up_x = [exchange(up_parts[0], "x")]
+    attn_own, up_x[0], up_part = together(line_sum(arrivals), up_x[0], up_parts[1])
+    up_x.append(exchange(up_part, "x"))
     residual_own = add_normed(layer_input, attn_own, gains[0])
     own, *line, other = together(*line_gather(residual_own), exchange(residual_own, "y"))
-    line, gate_up_x, near_x[0] = together(jnp.concatenate(line), gate_up_x, near_x[0])
+    line, gate_x, *up_x, near_x[0] = together(jnp.concatenate(line), gate_x, *up_x, near_x[0])
     far_x = exchange(far, "x")
-    pieces = [exchange(gate_up, "core"), gate_up_x, exchange(gate_up_x, "core")]
-    gate_all, up_all = staged(
-        [in_hbm(gate_rows), *((piece, 0, units) for piece in pieces)],
-        [in_hbm(up_rows), *((piece, units, units) for piece in pieces)],
-    )
+    halves = [*both_halves(in_hbm(gate_rows), gate_x), *both_halves(in_hbm(up_rows), *up_x)]
 
     def hidden_units_of(first, others):
         (hidden,) = vmem_call(
             hidden_kernel,
-            [jax.ShapeDtypeStruct((4 * tok_dev, gate_all.shape[0]), jnp.bfloat16)],
+            [jax.ShapeDtypeStruct((4 * tok_dev, 4 * gate_rows.shape[0]), jnp.bfloat16)],
             [],
-            [jnp.concatenate([first, others]), gate_all, up_all],
+            [jnp.concatenate([first, others]), *halves],
             8,
         )
         return hidden
@@ -382,21 +350,19 @@
     hidden_own = hidden_units_of(own, line)
     line_other, hidden_own, far_x, near_x[1] = together(line_other, hidden_own, far_x, near_x[1])
     from_own = exchange(hidden_own, "y")
-    far_pieces = four_pieces(far, far_x)
     hidden_other = hidden_units_of(other, line_other)
     from_other = exchange(hidden_other, "y")
-    near_pieces = four_pieces(near, jnp.concatenate(near_x))
-    near_all, far_all = staged(near_pieces, far_pieces)
+    down_halves = [*both_halves(near, *near_x), *both_halves(far, far_x)]
 
     def summed_down(hidden, from_y):
         parts = vmem_call(
             down_kernel,
             [jax.ShapeDtypeStruct((tok_dev, half), jnp.bfloat16)] * 4,
             [],
-            [hidden, from_y, near_all, far_all],
+            [hidden, from_y, *down_halves],
             8,
         )
-        return line_scatter(parts)
+        return line_sum(line_arrivals(parts))
 
     other_half = exchange(summed_down(hidden_other, from_own).astype(jnp.bfloat16), "y")
     own_half = summed_down(hidden_own, from_other)

time: 155 us -> 161 us (1.039)
  starting transfers between devices: 39.5 us -> 56 us
  waiting for transfers between devices: 82.7 us -> 74 us
  Pallas kernels: 28.3 us -> 25.6 us
    ppermute x15, waiting for transfers between devices: 58.1 us -> 41.1 us  [shift(): return lax.ppermute(block, 'mlp', [((k + hops) % 4, k) for k in range(4)])]
    ppermute x15, starting transfers between devices: 27.4 us -> 40.2 us  [shift(): return lax.ppermute(block, 'mlp', [((k + hops) % 4, k) for k in range(4)])]
    ppermute x16, waiting for transfers between devices: 24.6 us -> 32.9 us  [exchange(): return lax.ppermute(block, axis, [(0, 1), (1, 0)])]
    ppermute x16, starting transfers between devices: 12.1 us -> 15.8 us  [exchange(): return lax.ppermute(block, axis, [(0, 1), (1, 0)])]
    pallas_call x1 -> x0, Pallas kernels: 3.12 us -> none  [stacked(): pl.pallas_call(kernel, out_shape=pltpu.HBM((count * rows, columns), array...]
    pallas_call x3 -> x5, Pallas kernels: 10.1 us -> 10.1 us  [staged(): pl.pallas_call(kernel, out_shape=[pltpu.VMEM(shape, group[0][0].dtype) fo...]
  transfers between devices with their start and end apart: 31 -> 31, of which waited for: 12 -> 14; matrix products, arithmetic and copies ran while one was open for 2% -> 3% of each run, Pallas kernels for 16% -> 15%
where the time goes in v13:
time: 161 us
  waiting for transfers between devices  74 us (46%)
  starting transfers between devices  56 us (35%)
  Pallas kernels  25.6 us (16%)
  other arithmetic  2.75 us (2%)
  local copies, waits for them, and re-layouts  2.6 us (2%)
    ppermute x15, waiting for transfers between devices, shift(): return lax.ppermute(block, 'mlp', [((k + hops) % 4, k) for k in range(4)])  41.1 us
    ppermute x15, starting transfers between devices, shift(): return lax.ppermute(block, 'mlp', [((k + hops) % 4, k) for k in range(4)])  40.2 us
    ppermute x16, waiting for transfers between devices, exchange(): return lax.ppermute(block, axis, [(0, 1), (1, 0)])  32.9 us
    ppermute x16, starting transfers between devices, exchange(): return lax.ppermute(block, axis, [(0, 1), (1, 0)])  15.8 us
    pallas_call x5, Pallas kernels, vmem_call(): pl.pallas_call(kernel, out_shape=outs, in_specs=[whole] * len(operands),...  15.6 us
    pallas_call x5, Pallas kernels, staged(): pl.pallas_call(kernel, out_shape=[pltpu.VMEM(shape, group[0][0].dtype) fo...  10.1 us
  transfers between devices with their start and end apart: 31, of which 14 were waited for; matrix products, arithmetic and copies ran while one was open for 3% of the time, Pallas kernels for 15%

profile of v13, /device:TPU:0, one launch (start us, length us, event | category | flops | bytes accessed | tf_op | source)
XLA Modules:
  0.0 161.3 jit_solution(5353756986609313481)
XLA Ops:
  0.0 5.1 %collective-permute-start = (bf16[32,4096]{1,0:T(8,128)(2,1)}, bf16[32,4096]{1,0:T(8,128)(2,1)S(1)}, u32[]{:S(2)}, u32[]{:S(2)}) collective-permute-start(bf16[32,4096]{1,0:T(8,128)(2,1)} %refs_10_.1), channel_id=1, source_target_pairs={{1,0},{2,1},{3,2},{0,3},{5,4},{6,5},{7,6},{4,7},{9,8},{10,9},{11,1... | collective-permute-start | bytes 786440 | tf_op jit(solution)/shard_map/ppermute | solution.py:96
  5.1 1.0 collective-permute-start.2
  6.1 2.4 %dynamic-slice_bitcast_fusion = (bf16[192,2048]{1,0:T(8,128)(2,1)S(1)}, bf16[192,2048]{1,0:T(8,128)(2,1)}) fusion(bf16[4096,192]{0,1:T(8,128)(2,1)} %param.37, s32[]{:T(128)S(6)} %select_n.55, s32[]{:T(128)S(6)} %select_n.51), kind=kLoop, calls=%fused_computation.3 | loop fusion | bytes 3145736 | tf_op jit(solution)/shard_map/dynamic_slice | solution.py:298
  8.5 1.5 collective-permute-start.3
  10.1 1.5 collective-permute-start.5
  12.4 6.6 %shard_map.181 = (bf16[4096,512]{1,0:T(8,128)(2,1)S(1)}, bf16[4096,512]{1,0:T(8,128)(2,1)S(1)}, bf16[4096,512]{1,0:T(8,128)(2,1)S(1)}, bf16[512,4096]{1,0:T(8,12...) custom-call(bf16[4096,512]{1,0:T(8,128)(2,1)} %refs_0_.1, ...), custom_call_target="tpu_custom_call" | custom-call | bytes 38801408 | tf_op jit(solution)/shard_map/pallas_call | solution.py:174
  19.1 8.6 %collective-permute-done.1.block_2 = bf16[32,4096]{1,0:T(8,128)(2,1)} collective-permute-done((bf16[32,4096]{1,0:T(8,128)(2,1)}, bf16[32,4096]{1,0:T(8,128)(2,1)}, u32[]{:S(2)}, u32[]{:S(2)}) %collective-permute-start.1) | collective-permute-done | bytes 262176 | tf_op jit(solution)/shard_map/ppermute | solution.py:96
  27.7 5.5 %shard_map.182 = (bf16[32,4096]{1,0:T(8,128)(2,1)S(1)}, bf16[32,4096]{1,0:T(8,128)(2,1)S(1)}, bf16[32,4096]{1,0:T(8,128)(2,1)S(1)}, bf16[32,4096]{1,0:T(8,128)(2,1)S(1)}) custom-call(bf16[32,4096]{1,0:T(8,128)(2,1)S(1)} %get-tuple-element.52.block_0, bf16[32,4096]{1,0:T(8,128)(2,1)S(1)} %collective-permute-done.block_1, ...), custom_call_target="tpu_custom_call" | custom-call | flops 1048576 | bytes 1048576 | tf_op jit(solution)/shard_map/pallas_call | solution.py:124
  33.2 2.6 %collective-permute-start.4 = (bf16[32,4096]{1,0:T(8,128)(2,1)S(1)}, bf16[32,4096]{1,0:T(8,128)(2,1)S(1)}, u32[]{:S(2)}, u32[]{:S(2)}) collective-permute-start(bf16[32,4096]{1,0:T(8,128)(2,1)S(1)} %get-tuple-element.66), channel_id=1, source_target_pairs={{1,0},{2,1},{3,2},{0,3},{5,4},{6,5},{7,6},{4,7},{9,8},{10,9},{11,1... | collective-permute-start | bytes 786440 | tf_op jit(solution)/shard_map/ppermute | solution.py:96
  35.8 0.8 collective-permute-start.6
  36.7 1.4 collective-permute-start.7
  38.1 4.6 %collective-permute-done.4 = bf16[32,4096]{1,0:T(8,128)(2,1)S(1)} collective-permute-done((bf16[32,4096]{1,0:T(8,128)(2,1)S(1)}, bf16[32,4096]{1,0:T(8,128)(2,1)S(1)}, u32[]{:S(2)}, u32[]{:S(2)}) %collective-permute-start.4) | collective-permute-done | bytes 262176 | tf_op jit(solution)/shard_map/ppermute | solution.py:96
  42.7 2.6 %collective-permute-done.5.refs_1_ = bf16[192,4096]{1,0:T(8,128)(2,1)S(1)} collective-permute-done((bf16[192,4096]{1,0:T(8,128)(2,1)}, bf16[192,4096]{1,0:T(8,128)(2,1)S(1)}, u32[]{:S(2)}, u32[]{:S(2)}) %collective-permute-start.5) | collective-permute-done | bytes 1572896 | tf_op jit(solution)/shard_map/ppermute | solution.py:92
  45.4 1.6 collective-permute-start.8
  47.0 11.7 %collective-permute-done.6 = bf16[32,4096]{1,0:T(8,128)(2,1)S(1)} collective-permute-done((bf16[32,4096]{1,0:T(8,128)(2,1)S(1)}, bf16[32,4096]{1,0:T(8,128)(2,1)S(1)}, u32[]{:S(2)}, u32[]{:S(2)}) %collective-permute-start.6) | collective-permute-done | bytes 262176 | tf_op jit(solution)/shard_map/ppermute | solution.py:96
  58.8 1.4 collective-permute-done.8.refs_1_
  60.3 1.5 collective-permute-start.13
  62.0 7.6 %collective-permute-start.10 = (bf16[32,4096]{1,0:T(8,128)(2,1)S(1)}, bf16[32,4096]{1,0:T(8,128)(2,1)S(1)}, u32[]{:S(2)}, u32[]{:S(2)}) collective-permute-start(bf16[32,4096]{1,0:T(8,128)(2,1)S(1)} %add_convert_fusion.1), channel_id=1, source_target_pairs={{2,0},{3,1},{0,2},{1,3},{6,4},{7,5},{4,6},{5,7},{10,8},{11,9},{8,1... | collective-permute-start | bytes 786440 | tf_op jit(solution)/shard_map/ppermute | solution.py:96
  69.6 4.0 %collective-permute-start.11 = (bf16[32,4096]{1,0:T(8,128)(2,1)S(1)}, bf16[32,4096]{1,0:T(8,128)(2,1)S(1)}, u32[]{:S(2)}, u32[]{:S(2)}) collective-permute-start(bf16[32,4096]{1,0:T(8,128)(2,1)S(1)} %add_convert_fusion.1), channel_id=1, source_target_pairs={{3,0},{0,1},{1,2},{2,3},{7,4},{4,5},{5,6},{6,7},{11,8},{8,9},{9,10... | collective-permute-start | bytes 786440 | tf_op jit(solution)/shard_map/ppermute | solution.py:96
  73.7 1.5 collective-permute-start.12
  75.2 2.3 %collective-permute-start.9 = (bf16[32,4096]{1,0:T(8,128)(2,1)S(1)}, bf16[32,4096]{1,0:T(8,128)(2,1)S(1)}, u32[]{:S(2)}, u32[]{:S(2)}) collective-permute-start(bf16[32,4096]{1,0:T(8,128)(2,1)S(1)} %add_convert_fusion.1), channel_id=1, source_target_pairs={{1,0},{2,1},{3,2},{0,3},{5,4},{6,5},{7,6},{4,7},{9,8},{10,9},{11,1... | collective-permute-start | bytes 786440 | tf_op jit(solution)/shard_map/ppermute | solution.py:96
  77.5 0.6 collective-permute-start.14
  78.1 5.2 %collective-permute-done.11 = bf16[32,4096]{1,0:T(8,128)(2,1)S(1)} collective-permute-done((bf16[32,4096]{1,0:T(8,128)(2,1)S(1)}, bf16[32,4096]{1,0:T(8,128)(2,1)S(1)}, u32[]{:S(2)}, u32[]{:S(2)}) %collective-permute-start.11) | collective-permute-done | bytes 262176 | tf_op jit(solution)/shard_map/ppermute | solution.py:96
  83.3 1.1 collective-permute-done.9
  84.4 1.4 shard_map.184.up_0
  86.0 1.4 shard_map.183.gate_0
  87.4 0.6 collective-permute-start.16
  88.0 0.5 collective-permute-start.18
  89.1 1.5 collective-permute-start.19
  90.7 0.9 collective-permute-done.17.up_1
  91.6 4.5 %collective-permute-done.16.gate_1 = bf16[384,4096]{1,0:T(8,128)(2,1)S(1)} collective-permute-done((bf16[384,4096]{1,0:T(8,128)(2,1)S(1)}, bf16[384,4096]{1,0:T(8,128)(2,1)S(1)}, u32[]{:S(2)}, u32[]{:S(2)}) %collective-permute-start.16) | collective-permute-done | bytes 3145760 | tf_op jit(solution)/shard_map/ppermute | solution.py:92
  96.1 3.8 %shard_map.185.near = bf16[128,768]{1,0:T(8,128)(2,1)S(1)} custom-call(bf16[128,4096]{1,0:T(8,128)(2,1)S(1)} %pad_maximum_fusion.states, bf16[384,4096]{1,0:T(8,128)(2,1)S(1)} %shard_map.183.gate_0, bf16[384,4096]{1,0:T(8,128)(2,1)S(1)} %collective-permute-done.16.gate_1, bf16[384,4096]{1,0:T(8,128)(2,1)S(1)} %shard_map.184.up_0, ...), custom_call_target="tpu_custom_call" | custom-call | flops 1048576 | bytes 1048576 | tf_op jit(solution)/shard_map/pallas_call | solution.py:124
  99.9 21.7 %collective-permute-done.19.refs_2_ = bf16[160,2048]{1,0:T(8,128)(2,1)S(1)} collective-permute-done((bf16[160,2048]{1,0:T(8,128)(2,1)S(1)}, bf16[160,2048]{1,0:T(8,128)(2,1)S(1)}, u32[]{:S(2)}, u32[]{:S(2)}) %collective-permute-start.19) | collective-permute-done | bytes 655392 | tf_op jit(solution)/shard_map/ppermute | solution.py:92
  122.2 0.6 collective-permute-start.21
  123.4 3.8 %shard_map.186.near = bf16[128,768]{1,0:T(8,128)(2,1)S(1)} custom-call(bf16[128,4096]{1,0:T(8,128)(2,1)S(1)} %pad_maximum_fusion.1.states, bf16[384,4096]{1,0:T(8,128)(2,1)S(1)} %shard_map.183.gate_0, bf16[384,4096]{1,0:T(8,128)(2,1)S(1)} %collective-permute-done.16.gate_1, bf16[384,4096]{1,0:T(8,128)(2,1)S(1)} %shard_map.184.up_0, ...), custom_call_target="tpu_custom_call" | custom-call | flops 1048576 | bytes 1048576 | tf_op jit(solution)/shard_map/pallas_call | solution.py:124
  127.2 1.6 collective-permute-start.27
  128.7 0.9 collective-permute-done.20.far
  129.7 1.3 shard_map.189
  130.9 3.1 %collective-permute-start.23 = (bf16[32,2048]{1,0:T(8,128)(2,1)S(1)}, bf16[32,2048]{1,0:T(8,128)(2,1)S(1)}, u32[]{:S(2)}, u32[]{:S(2)}) collective-permute-start(bf16[32,2048]{1,0:T(8,128)(2,1)S(1)} %get-tuple-element.91), channel_id=1, source_target_pairs={{1,0},{2,1},{3,2},{0,3},{5,4},{6,5},{7,6},{4,7},{9,8},{10,9},{11,1... | collective-permute-start | bytes 393224 | tf_op jit(solution)/shard_map/ppermute | solution.py:96
  134.1 2.9 %collective-permute-start.24 = (bf16[32,2048]{1,0:T(8,128)(2,1)S(1)}, bf16[32,2048]{1,0:T(8,128)(2,1)S(1)}, u32[]{:S(2)}, u32[]{:S(2)}) collective-permute-start(bf16[32,2048]{1,0:T(8,128)(2,1)S(1)} %get-tuple-element.92), channel_id=1, source_target_pairs={{2,0},{3,1},{0,2},{1,3},{6,4},{7,5},{4,6},{5,7},{10,8},{11,9},{8,1... | collective-permute-start | bytes 393224 | tf_op jit(solution)/shard_map/ppermute | solution.py:96
  137.0 1.3 shard_map.190
  138.3 3.9 %collective-permute-start.28 = (bf16[32,2048]{1,0:T(8,128)(2,1)S(1)}, bf16[32,2048]{1,0:T(8,128)(2,1)S(1)}, u32[]{:S(2)}, u32[]{:S(2)}) collective-permute-start(bf16[32,2048]{1,0:T(8,128)(2,1)S(1)} %get-tuple-element.95), channel_id=1, source_target_pairs={{1,0},{2,1},{3,2},{0,3},{5,4},{6,5},{7,6},{4,7},{9,8},{10,9},{11,1... | collective-permute-start | bytes 393224 | tf_op jit(solution)/shard_map/ppermute | solution.py:96
  142.1 5.4 %collective-permute-start.30 = (bf16[32,2048]{1,0:T(8,128)(2,1)S(1)}, bf16[32,2048]{1,0:T(8,128)(2,1)S(1)}, u32[]{:S(2)}, u32[]{:S(2)}) collective-permute-start(bf16[32,2048]{1,0:T(8,128)(2,1)S(1)} %get-tuple-element.97), channel_id=1, source_target_pairs={{3,0},{0,1},{1,2},{2,3},{7,4},{4,5},{5,6},{6,7},{11,8},{8,9},{9,10... | collective-permute-start | bytes 393224 | tf_op jit(solution)/shard_map/ppermute | solution.py:96
  147.6 7.5 %collective-permute-done.24 = bf16[32,2048]{1,0:T(8,128)(2,1)S(1)} collective-permute-done((bf16[32,2048]{1,0:T(8,128)(2,1)S(1)}, bf16[32,2048]{1,0:T(8,128)(2,1)S(1)}, u32[]{:S(2)}, u32[]{:S(2)}) %collective-permute-start.24) | collective-permute-done | bytes 131104 | tf_op jit(solution)/shard_map/ppermute | solution.py:96
  155.1 1.6 collective-permute-start.26
  156.7 2.5 %collective-permute-done.29 = bf16[32,2048]{1,0:T(8,128)(2,1)S(1)} collective-permute-done((bf16[32,2048]{1,0:T(8,128)(2,1)S(1)}, bf16[32,2048]{1,0:T(8,128)(2,1)S(1)}, u32[]{:S(2)}, u32[]{:S(2)}) %collective-permute-start.29) | collective-permute-done | bytes 131104 | tf_op jit(solution)/shard_map/ppermute | solution.py:96
  159.2 0.9 collective-permute-done.26
  160.4 0.9 add_convert_fusion
  (67 shorter events, 3.9 us)
Async XLA Ops:
  0.0 11.5 %copy-start.5 = (s32[1,4]{1,0:T(1,128)S(1)}, s32[1,4]{1,0:T(1,128)}, u32[]{:S(2)}) copy-start(s32[1,4]{1,0:T(1,128)} %param.20) | copy-start | bytes 52
  0.0 11.7 %copy-start.4 = (s32[1,4]{1,0:T(1,128)S(1)}, s32[1,4]{1,0:T(1,128)}, u32[]{:S(2)}) copy-start(s32[1,4]{1,0:T(1,128)} %param.21) | copy-start | bytes 52
  0.0 11.9 %copy-start.6 = (s32[8]{0:T(128)S(1)}, s32[8]{0:T(128)}, u32[]{:S(2)}) copy-start(s32[8]{0:T(128)} %param.22) | copy-start | bytes 100
  0.0 19.1 %collective-permute-start = (bf16[32,4096]{1,0:T(8,128)(2,1)}, bf16[32,4096]{1,0:T(8,128)(2,1)S(1)}, u32[]{:S(2)}, u32[]{:S(2)}) collective-permute-start(bf16[32,4096]{1,0:T(8,128)(2,1)} %refs_10_.1), channel_id=1, source_target_pairs={{1,0},{2,1},{3,2},{0,3},{5,4},{6,5},{7,6},{4,7},{9,8},{10,9},{11,1... | collective-permute-start | bytes 786440 | tf_op jit(solution)/shard_map/ppermute | solution.py:96
  5.1 22.6 %collective-permute-start.1 = (bf16[32,4096]{1,0:T(8,128)(2,1)}, bf16[32,4096]{1,0:T(8,128)(2,1)}, u32[]{:S(2)}, u32[]{:S(2)}) collective-permute-start(bf16[32,4096]{1,0:T(8,128)(2,1)} %refs_10_.1), channel_id=1, source_target_pairs={{2,0},{3,1},{0,2},{1,3},{6,4},{7,5},{4,6},{5,7},{10,8},{11,9},{8,1... | collective-permute-start | bytes 786440 | tf_op jit(solution)/shard_map/ppermute | solution.py:96
  5.1 22.6 %collective-permute-start.2 = (bf16[32,4096]{1,0:T(8,128)(2,1)}, bf16[32,4096]{1,0:T(8,128)(2,1)}, u32[]{:S(2)}, u32[]{:S(2)}) collective-permute-start(bf16[32,4096]{1,0:T(8,128)(2,1)} %refs_10_.1), channel_id=1, source_target_pairs={{3,0},{0,1},{1,2},{2,3},{7,4},{4,5},{5,6},{6,7},{11,8},{8,9},{9,10... | collective-permute-start | bytes 786440 | tf_op jit(solution)/shard_map/ppermute | solution.py:96
  8.5 19.2 %collective-permute-start.3 = (bf16[192,2048]{1,0:T(8,128)(2,1)}, bf16[192,2048]{1,0:T(8,128)(2,1)S(1)}, u32[]{:S(2)}, u32[]{:S(2)}) collective-permute-start(bf16[192,2048]{1,0:T(8,128)(2,1)} %get-tuple-element.105), channel_id=1, source_target_pairs={{0,16},{16,0},{1,17},{17,1},{2,18},{18,2},{3,19},{19,3},{4,20},{20... | collective-permute-start | bytes 2359304 | tf_op jit(solution)/shard_map/ppermute | solution.py:92
  10.1 35.2 %collective-permute-start.5 = (bf16[192,4096]{1,0:T(8,128)(2,1)}, bf16[192,4096]{1,0:T(8,128)(2,1)S(1)}, u32[]{:S(2)}, u32[]{:S(2)}) collective-permute-start(bf16[192,4096]{1,0:T(8,128)(2,1)} %bitcast.8.refs_0_), channel_id=1, source_target_pairs={{0,8},{8,0},{1,9},{9,1},{2,10},{10,2},{3,11},{11,3},{4,12},{12,4},... | collective-permute-start | bytes 4718600 | tf_op jit(solution)/shard_map/ppermute | solution.py:92
  27.7 17.5 %copy-start = (bf16[4096,192]{0,1:T(8,128)(2,1)S(1)}, bf16[4096,192]{0,1:T(8,128)(2,1)}, u32[]{:S(2)}) copy-start(bf16[4096,192]{0,1:T(8,128)(2,1)} %param.36) | copy-start | bytes 4718596
  33.2 9.4 %collective-permute-start.4 = (bf16[32,4096]{1,0:T(8,128)(2,1)S(1)}, bf16[32,4096]{1,0:T(8,128)(2,1)S(1)}, u32[]{:S(2)}, u32[]{:S(2)}) collective-permute-start(bf16[32,4096]{1,0:T(8,128)(2,1)S(1)} %get-tuple-element.66), channel_id=1, source_target_pairs={{1,0},{2,1},{3,2},{0,3},{5,4},{6,5},{7,6},{4,7},{9,8},{10,9},{11,1... | collective-permute-start | bytes 786440 | tf_op jit(solution)/shard_map/ppermute | solution.py:96
  35.8 22.8 %collective-permute-start.6 = (bf16[32,4096]{1,0:T(8,128)(2,1)S(1)}, bf16[32,4096]{1,0:T(8,128)(2,1)S(1)}, u32[]{:S(2)}, u32[]{:S(2)}) collective-permute-start(bf16[32,4096]{1,0:T(8,128)(2,1)S(1)} %get-tuple-element.68), channel_id=1, source_target_pairs={{2,0},{3,1},{0,2},{1,3},{6,4},{7,5},{4,6},{5,7},{10,8},{11,9},{8,1... | collective-permute-start | bytes 786440 | tf_op jit(solution)/shard_map/ppermute | solution.py:96
  36.7 22.0 %collective-permute-start.7 = (bf16[32,4096]{1,0:T(8,128)(2,1)S(1)}, bf16[32,4096]{1,0:T(8,128)(2,1)S(1)}, u32[]{:S(2)}, u32[]{:S(2)}) collective-permute-start(bf16[32,4096]{1,0:T(8,128)(2,1)S(1)} %get-tuple-element.69), channel_id=1, source_target_pairs={{3,0},{0,1},{1,2},{2,3},{7,4},{4,5},{5,6},{6,7},{11,8},{8,9},{9,10... | collective-permute-start | bytes 786440 | tf_op jit(solution)/shard_map/ppermute | solution.py:96
  45.3 16.5 %copy-start.1 = (bf16[32,4096]{1,0:T(8,128)(2,1)S(1)}, bf16[32,4096]{1,0:T(8,128)(2,1)}, u32[]{:S(2)}) copy-start(bf16[32,4096]{1,0:T(8,128)(2,1)} %refs_10_.1) | copy-start | bytes 786436
  45.3 16.5 %copy-start.2 = (f32[4096]{0:T(1024)S(1)}, f32[4096]{0:T(1024)}, u32[]{:S(2)}) copy-start(f32[4096]{0:T(1024)} %param.33) | copy-start | bytes 49156
  45.4 14.7 %collective-permute-start.8 = (bf16[80,4096]{1,0:T(8,128)(2,1)S(1)}, bf16[80,4096]{1,0:T(8,128)(2,1)S(1)}, u32[]{:S(2)}, u32[]{:S(2)}) collective-permute-start(bf16[80,4096]{1,0:T(8,128)(2,1)S(1)} %split.12), channel_id=1, source_target_pairs={{0,8},{8,0},{1,9},{9,1},{2,10},{10,2},{3,11},{11,3},{4,12},{12,4},... | collective-permute-start | bytes 1966088 | tf_op jit(solution)/shard_map/ppermute | solution.py:92
  60.3 24.1 %collective-permute-start.13 = (bf16[112,4096]{1,0:T(8,128)(2,1)S(1)}, bf16[112,4096]{1,0:T(8,128)(2,1)S(1)}, u32[]{:S(2)}, u32[]{:S(2)}) collective-permute-start(bf16[112,4096]{1,0:T(8,128)(2,1)S(1)} %split.13), channel_id=1, source_target_pairs={{0,8},{8,0},{1,9},{9,1},{2,10},{10,2},{3,11},{11,3},{4,12},{12,4},... | collective-permute-start | bytes 2752520 | tf_op jit(solution)/shard_map/ppermute | solution.py:92
  62.0 15.5 %collective-permute-start.10 = (bf16[32,4096]{1,0:T(8,128)(2,1)S(1)}, bf16[32,4096]{1,0:T(8,128)(2,1)S(1)}, u32[]{:S(2)}, u32[]{:S(2)}) collective-permute-start(bf16[32,4096]{1,0:T(8,128)(2,1)S(1)} %add_convert_fusion.1), channel_id=1, source_target_pairs={{2,0},{3,1},{0,2},{1,3},{6,4},{7,5},{4,6},{5,7},{10,8},{11,9},{8,1... | collective-permute-start | bytes 786440 | tf_op jit(solution)/shard_map/ppermute | solution.py:96
  69.6 13.7 %collective-permute-start.11 = (bf16[32,4096]{1,0:T(8,128)(2,1)S(1)}, bf16[32,4096]{1,0:T(8,128)(2,1)S(1)}, u32[]{:S(2)}, u32[]{:S(2)}) collective-permute-start(bf16[32,4096]{1,0:T(8,128)(2,1)S(1)} %add_convert_fusion.1), channel_id=1, source_target_pairs={{3,0},{0,1},{1,2},{2,3},{7,4},{4,5},{5,6},{6,7},{11,8},{8,9},{9,10... | collective-permute-start | bytes 786440 | tf_op jit(solution)/shard_map/ppermute | solution.py:96
  73.7 9.6 %collective-permute-start.12 = (bf16[32,4096]{1,0:T(8,128)(2,1)S(1)}, bf16[32,4096]{1,0:T(8,128)(2,1)S(1)}, u32[]{:S(2)}, u32[]{:S(2)}) collective-permute-start(bf16[32,4096]{1,0:T(8,128)(2,1)S(1)} %add_convert_fusion.1), channel_id=1, source_target_pairs={{0,16},{16,0},{1,17},{17,1},{2,18},{18,2},{3,19},{19,3},{4,20},{20... | collective-permute-start | bytes 786440 | tf_op jit(solution)/shard_map/ppermute | solution.py:92
  75.2 9.2 %collective-permute-start.9 = (bf16[32,4096]{1,0:T(8,128)(2,1)S(1)}, bf16[32,4096]{1,0:T(8,128)(2,1)S(1)}, u32[]{:S(2)}, u32[]{:S(2)}) collective-permute-start(bf16[32,4096]{1,0:T(8,128)(2,1)S(1)} %add_convert_fusion.1), channel_id=1, source_target_pairs={{1,0},{2,1},{3,2},{0,3},{5,4},{6,5},{7,6},{4,7},{9,8},{10,9},{11,1... | collective-permute-start | bytes 786440 | tf_op jit(solution)/shard_map/ppermute | solution.py:96
  77.5 6.9 %collective-permute-start.14 = (bf16[32,2048]{1,0:T(8,128)(2,1)S(1)}, bf16[32,2048]{1,0:T(8,128)(2,1)S(1)}, u32[]{:S(2)}, u32[]{:S(2)}) collective-permute-start(bf16[32,2048]{1,0:T(8,128)(2,1)S(1)} %split.16), channel_id=1, source_target_pairs={{0,8},{8,0},{1,9},{9,1},{2,10},{10,2},{3,11},{11,3},{4,12},{12,4},... | collective-permute-start | bytes 393224 | tf_op jit(solution)/shard_map/ppermute | solution.py:92
  85.9 5.7 %collective-permute-start.17 = (bf16[384,4096]{1,0:T(8,128)(2,1)S(1)}, bf16[384,4096]{1,0:T(8,128)(2,1)S(1)}, u32[]{:S(2)}, u32[]{:S(2)}) collective-permute-start(bf16[384,4096]{1,0:T(8,128)(2,1)S(1)} %shard_map.184.up_0), channel_id=1, source_target_pairs={{0,4},{4,0},{1,5},{5,1},{2,6},{6,2},{3,7},{7,3},{8,12},{12,8},{9,1... | collective-permute-start | bytes 9437192 | tf_op jit(solution)/shard_map/ppermute | solution.py:92
  87.4 8.7 %collective-permute-start.16 = (bf16[384,4096]{1,0:T(8,128)(2,1)S(1)}, bf16[384,4096]{1,0:T(8,128)(2,1)S(1)}, u32[]{:S(2)}, u32[]{:S(2)}) collective-permute-start(bf16[384,4096]{1,0:T(8,128)(2,1)S(1)} %shard_map.183.gate_0), channel_id=1, source_target_pairs={{0,4},{4,0},{1,5},{5,1},{2,6},{6,2},{3,7},{7,3},{8,12},{12,8},{9,1... | collective-permute-start | bytes 9437192 | tf_op jit(solution)/shard_map/ppermute | solution.py:92
  88.0 33.6 %collective-permute-start.18 = (bf16[192,2048]{1,0:T(8,128)(2,1)S(1)}, bf16[192,2048]{1,0:T(8,128)(2,1)S(1)}, u32[]{:S(2)}, u32[]{:S(2)}) collective-permute-start(bf16[192,2048]{1,0:T(8,128)(2,1)S(1)} %collective-permute-done.3.refs_0_), channel_id=1, source_target_pairs={{0,8},{8,0},{1,9},{9,1},{2,10},{10,2},{3,11},{11,3},{4,12},{12,4},... | collective-permute-start | bytes 2359304 | tf_op jit(solution)/shard_map/ppermute | solution.py:92
  88.5 33.0 %collective-permute-start.15 = (bf16[96,4096]{1,0:T(8,128)(2,1)S(1)}, bf16[96,4096]{1,0:T(8,128)(2,1)S(1)}, u32[]{:S(2)}, u32[]{:S(2)}) collective-permute-start(bf16[96,4096]{1,0:T(8,128)(2,1)S(1)} %pad_maximum_fusion.2), channel_id=1, source_target_pairs={{0,16},{16,0},{1,17},{17,1},{2,18},{18,2},{3,19},{19,3},{4,20},{20... | collective-permute-start | bytes 2359304 | tf_op jit(solution)/shard_map/ppermute | solution.py:92
  89.1 32.5 %collective-permute-start.19 = (bf16[160,2048]{1,0:T(8,128)(2,1)S(1)}, bf16[160,2048]{1,0:T(8,128)(2,1)S(1)}, u32[]{:S(2)}, u32[]{:S(2)}) collective-permute-start(bf16[160,2048]{1,0:T(8,128)(2,1)S(1)} %split.17), channel_id=1, source_target_pairs={{0,8},{8,0},{1,9},{9,1},{2,10},{10,2},{3,11},{11,3},{4,12},{12,4},... | collective-permute-start | bytes 1966088 | tf_op jit(solution)/shard_map/ppermute | solution.py:92
  121.7 8.0 %collective-permute-start.22 = (bf16[384,2048]{1,0:T(8,128)(2,1)S(1)}, bf16[384,2048]{1,0:T(8,128)(2,1)S(1)}, u32[]{:S(2)}, u32[]{:S(2)}) collective-permute-start(bf16[384,2048]{1,0:T(8,128)(2,1)S(1)} %shard_map.188.far_0), channel_id=1, source_target_pairs={{0,4},{4,0},{1,5},{5,1},{2,6},{6,2},{3,7},{7,3},{8,12},{12,8},{9,1... | collective-permute-start | bytes 4718600 | tf_op jit(solution)/shard_map/ppermute | solution.py:92
  122.2 7.4 %collective-permute-start.21 = (bf16[384,2048]{1,0:T(8,128)(2,1)S(1)}, bf16[384,2048]{1,0:T(8,128)(2,1)S(1)}, u32[]{:S(2)}, u32[]{:S(2)}) collective-permute-start(bf16[384,2048]{1,0:T(8,128)(2,1)S(1)} %shard_map.187.near_0), channel_id=1, source_target_pairs={{0,4},{4,0},{1,5},{5,1},{2,6},{6,2},{3,7},{7,3},{8,12},{12,8},{9,1... | collective-permute-start | bytes 4718600 | tf_op jit(solution)/shard_map/ppermute | solution.py:92
  122.8 6.9 %collective-permute-start.20 = (bf16[128,768]{1,0:T(8,128)(2,1)S(1)}, bf16[128,768]{1,0:T(8,128)(2,1)S(1)}, u32[]{:S(2)}, u32[]{:S(2)}) collective-permute-start(bf16[128,768]{1,0:T(8,128)(2,1)S(1)} %shard_map.185.near), channel_id=1, source_target_pairs={{0,16},{16,0},{1,17},{17,1},{2,18},{18,2},{3,19},{19,3},{4,20},{20... | collective-permute-start | bytes 589832 | tf_op jit(solution)/shard_map/ppermute | solution.py:92
  127.2 9.8 %collective-permute-start.27 = (bf16[128,768]{1,0:T(8,128)(2,1)S(1)}, bf16[128,768]{1,0:T(8,128)(2,1)S(1)}, u32[]{:S(2)}, u32[]{:S(2)}) collective-permute-start(bf16[128,768]{1,0:T(8,128)(2,1)S(1)} %shard_map.186.near), channel_id=1, source_target_pairs={{0,16},{16,0},{1,17},{17,1},{2,18},{18,2},{3,19},{19,3},{4,20},{20... | collective-permute-start | bytes 589832 | tf_op jit(solution)/shard_map/ppermute | solution.py:92
  130.9 11.2 %collective-permute-start.23 = (bf16[32,2048]{1,0:T(8,128)(2,1)S(1)}, bf16[32,2048]{1,0:T(8,128)(2,1)S(1)}, u32[]{:S(2)}, u32[]{:S(2)}) collective-permute-start(bf16[32,2048]{1,0:T(8,128)(2,1)S(1)} %get-tuple-element.91), channel_id=1, source_target_pairs={{1,0},{2,1},{3,2},{0,3},{5,4},{6,5},{7,6},{4,7},{9,8},{10,9},{11,1... | collective-permute-start | bytes 393224 | tf_op jit(solution)/shard_map/ppermute | solution.py:96
  134.1 21.0 %collective-permute-start.24 = (bf16[32,2048]{1,0:T(8,128)(2,1)S(1)}, bf16[32,2048]{1,0:T(8,128)(2,1)S(1)}, u32[]{:S(2)}, u32[]{:S(2)}) collective-permute-start(bf16[32,2048]{1,0:T(8,128)(2,1)S(1)} %get-tuple-element.92), channel_id=1, source_target_pairs={{2,0},{3,1},{0,2},{1,3},{6,4},{7,5},{4,6},{5,7},{10,8},{11,9},{8,1... | collective-permute-start | bytes 393224 | tf_op jit(solution)/shard_map/ppermute | solution.py:96
  137.0 18.1 %collective-permute-start.25 = (bf16[32,2048]{1,0:T(8,128)(2,1)S(1)}, bf16[32,2048]{1,0:T(8,128)(2,1)S(1)}, u32[]{:S(2)}, u32[]{:S(2)}) collective-permute-start(bf16[32,2048]{1,0:T(8,128)(2,1)S(1)} %get-tuple-element.93), channel_id=1, source_target_pairs={{3,0},{0,1},{1,2},{2,3},{7,4},{4,5},{5,6},{6,7},{11,8},{8,9},{9,10... | collective-permute-start | bytes 393224 | tf_op jit(solution)/shard_map/ppermute | solution.py:96
  138.2 22.2 %copy-start.3 = (f32[4096]{0:T(1024)S(1)}, f32[4096]{0:T(1024)}, u32[]{:S(2)}) copy-start(f32[4096]{0:T(1024)} %param.34) | copy-start | bytes 49156
  138.3 18.4 %collective-permute-start.28 = (bf16[32,2048]{1,0:T(8,128)(2,1)S(1)}, bf16[32,2048]{1,0:T(8,128)(2,1)S(1)}, u32[]{:S(2)}, u32[]{:S(2)}) collective-permute-start(bf16[32,2048]{1,0:T(8,128)(2,1)S(1)} %get-tuple-element.95), channel_id=1, source_target_pairs={{1,0},{2,1},{3,2},{0,3},{5,4},{6,5},{7,6},{4,7},{9,8},{10,9},{11,1... | collective-permute-start | bytes 393224 | tf_op jit(solution)/shard_map/ppermute | solution.py:96
  142.1 17.1 %collective-permute-start.29 = (bf16[32,2048]{1,0:T(8,128)(2,1)S(1)}, bf16[32,2048]{1,0:T(8,128)(2,1)S(1)}, u32[]{:S(2)}, u32[]{:S(2)}) collective-permute-start(bf16[32,2048]{1,0:T(8,128)(2,1)S(1)} %get-tuple-element.96), channel_id=1, source_target_pairs={{2,0},{3,1},{0,2},{1,3},{6,4},{7,5},{4,6},{5,7},{10,8},{11,9},{8,1... | collective-permute-start | bytes 393224 | tf_op jit(solution)/shard_map/ppermute | solution.py:96
  142.1 17.1 %collective-permute-start.30 = (bf16[32,2048]{1,0:T(8,128)(2,1)S(1)}, bf16[32,2048]{1,0:T(8,128)(2,1)S(1)}, u32[]{:S(2)}, u32[]{:S(2)}) collective-permute-start(bf16[32,2048]{1,0:T(8,128)(2,1)S(1)} %get-tuple-element.97), channel_id=1, source_target_pairs={{3,0},{0,1},{1,2},{2,3},{7,4},{4,5},{5,6},{6,7},{11,8},{8,9},{9,10... | collective-permute-start | bytes 393224 | tf_op jit(solution)/shard_map/ppermute | solution.py:96
  155.1 5.0 %collective-permute-start.26 = (bf16[32,2048]{1,0:T(8,128)(2,1)S(1)}, bf16[32,2048]{1,0:T(8,128)(2,1)S(1)}, u32[]{:S(2)}, u32[]{:S(2)}) collective-permute-start(bf16[32,2048]{1,0:T(8,128)(2,1)S(1)} %add_convert_fusion.2), channel_id=1, source_target_pairs={{0,16},{16,0},{1,17},{17,1},{2,18},{18,2},{3,19},{19,3},{4,20},{20... | collective-permute-start | bytes 393224 | tf_op jit(solution)/shard_map/ppermute | solution.py:92

commit v14 on v13

--- a/solution.py
+++ b/solution.py
@@ -136,7 +136,7 @@
     return pltpu.with_memory_space_constraint(array, pltpu.HBM)
 
 
-def staged(*groups):
+def staged(*groups, weight=4):
     groups = [
         [piece if isinstance(piece, tuple) else (piece, 0, piece.shape[0]) for piece in group]
         for group in groups
@@ -178,7 +178,7 @@
         out_specs=[pl.BlockSpec(memory_space=pltpu.VMEM)] * len(groups),
         scratch_shapes=[pltpu.SemaphoreType.DMA((count,))],
         compiler_params=pltpu.CompilerParams(vmem_limit_bytes=1 << 20),
-        cost_estimate=pl.CostEstimate(flops=0, bytes_accessed=4 * size, transcendentals=0),
+        cost_estimate=pl.CostEstimate(flops=0, bytes_accessed=weight * size, transcendentals=0),
     )(*arrays)
 
 
@@ -295,15 +295,14 @@
     gate_rows, up_rows, down_rows = ffn_rows
     y = lax.axis_index("y")
     half = width // 2
-    near = lax.dynamic_slice_in_dim(down_rows, y * half, half, axis=1)
-    far = exchange(lax.dynamic_slice_in_dim(down_rows, (1 - y) * half, half, axis=1), "y")
     gate_x = exchange(gate_rows, "x")
     cosine, sine = jnp.cos(angles), jnp.sin(angles)
     block = jax.ShapeDtypeStruct((tok_dev, width), jnp.bfloat16)
     *staged_rows, own_block = staged(
-        *([in_hbm(array)] for array in (*projections, *adapters, *head_gains, layer_input))
-    )
-    *blocks, far = together(*line_gather(layer_input)[1:], far)
+        *([in_hbm(array)] for array in (*projections, *adapters, *head_gains, layer_input)),
+        weight=0,
+    )
+    *blocks, own_block, down_rows = together(*line_gather(layer_input)[1:], own_block, down_rows)
     parts = vmem_call(
         attention_kernel,
         [block] * 4,
@@ -322,14 +321,18 @@
         ],
         8,
     )
-    near_x = [exchange(rows, "x") for rows in jnp.split(near, [near.shape[0] // 6])]
+    near = lax.dynamic_slice_in_dim(down_rows, y * half, half, axis=1)
+    far = exchange(lax.dynamic_slice_in_dim(down_rows, (1 - y) * half, half, axis=1), "y")
     arrivals = line_arrivals(parts)
     arrivals[0], gate_x, up_late = together(arrivals[0], gate_x, up_rows)
     units = up_late.shape[0]
     up_parts = jnp.split(up_late, [units * 5 // 12])
     up_x = [exchange(up_parts[0], "x")]
-    attn_own, up_x[0], up_part = together(line_sum(arrivals), up_x[0], up_parts[1])
+    attn_own, up_x[0], up_part, near, far = together(
+        line_sum(arrivals), up_x[0], up_parts[1], near, far
+    )
     up_x.append(exchange(up_part, "x"))
+    near_x = [exchange(rows, "x") for rows in jnp.split(near, [near.shape[0] // 6])]
     residual_own = add_normed(layer_input, attn_own, gains[0])
     own, *line, other = together(*line_gather(residual_own), exchange(residual_own, "y"))
     line, gate_x, *up_x, near_x[0] = together(jnp.concatenate(line), gate_x, *up_x, near_x[0])

time: 161 us -> 160 us (level)
  other arithmetic: 2.75 us -> 5.38 us
  local copies, waits for them, and re-layouts: 2.6 us -> 0.3 us
  waiting for transfers between devices: 74 us -> 72 us
    dynamic_slice x1, local copies, waits for them, and re-layouts: 2.41 us -> 0.1 us  [layer_direct(): lax.dynamic_slice_in_dim(down_rows, (1 - y) * half, half, axis=1)]
    ppermute x16, waiting for transfers between devices: 32.9 us -> 31.1 us  [exchange(): return lax.ppermute(block, axis, [(0, 1), (1, 0)])]
  transfers between devices with their start and end apart: 31 -> 31, of which waited for: 14 -> 13; matrix products, arithmetic and copies ran while one was open for 3% -> 3% of each run, Pallas kernels for 15% -> 14%
where the time goes in v14:
time: 160 us; the launch traced here: 159 us
  waiting for transfers between devices  72 us (45%)
  starting transfers between devices  56.9 us (36%)
  Pallas kernels  24.4 us (15%)
  other arithmetic  5.38 us (3%)
    ppermute x15, starting transfers between devices, shift(): return lax.ppermute(block, 'mlp', [((k + hops) % 4, k) for k in range(4)])  41 us
    ppermute x15, waiting for transfers between devices, shift(): return lax.ppermute(block, 'mlp', [((k + hops) % 4, k) for k in range(4)])  41 us
    ppermute x16, waiting for transfers between devices, exchange(): return lax.ppermute(block, axis, [(0, 1), (1, 0)])  31.1 us
    ppermute x16, starting transfers between devices, exchange(): return lax.ppermute(block, axis, [(0, 1), (1, 0)])  15.8 us
    pallas_call x5, Pallas kernels, vmem_call(): pl.pallas_call(kernel, out_shape=outs, in_specs=[whole] * len(operands),...  14.4 us
    pallas_call x5, Pallas kernels, staged(): pl.pallas_call(kernel, out_shape=[pltpu.VMEM(shape, group[0][0].dtype) fo...  10.1 us
  transfers between devices with their start and end apart: 31, of which 13 were waited for; matrix products, arithmetic and copies ran while one was open for 3% of the time, Pallas kernels for 14%

profile of v14, /device:TPU:0, one launch (start us, length us, event | category | flops | bytes accessed | tf_op | source)
XLA Modules:
  0.0 159.3 jit_solution(13389346211657192490)
XLA Ops:
  0.0 5.0 %collective-permute-start = (bf16[32,4096]{1,0:T(8,128)(2,1)}, bf16[32,4096]{1,0:T(8,128)(2,1)S(1)}, u32[]{:S(2)}, u32[]{:S(2)}) collective-permute-start(bf16[32,4096]{1,0:T(8,128)(2,1)} %refs_10_.1), channel_id=1, source_target_pairs={{1,0},{2,1},{3,2},{0,3},{5,4},{6,5},{7,6},{4,7},{9,8},{10,9},{11,1... | collective-permute-start | bytes 786440 | tf_op jit(solution)/shard_map/ppermute | solution.py:96
  5.1 1.0 collective-permute-start.2
  6.1 1.5 collective-permute-start.4
  7.6 0.8 reduce-window.4
  8.4 0.7 fusion.6
  9.1 0.7 select_reduce_fusion.1
  9.8 0.7 select_reduce_fusion
  11.0 6.6 %shard_map.181 = (bf16[4096,512]{1,0:T(8,128)(2,1)S(1)}, bf16[4096,512]{1,0:T(8,128)(2,1)S(1)}, bf16[4096,512]{1,0:T(8,128)(2,1)S(1)}, bf16[512,4096]{1,0:T(8,12...) custom-call(bf16[4096,512]{1,0:T(8,128)(2,1)} %refs_0_.1, ...), custom_call_target="tpu_custom_call" | custom-call | tf_op jit(solution)/shard_map/pallas_call | solution.py:174
  17.8 9.8 %collective-permute-done.1.block_2 = bf16[32,4096]{1,0:T(8,128)(2,1)S(1)} collective-permute-done((bf16[32,4096]{1,0:T(8,128)(2,1)}, bf16[32,4096]{1,0:T(8,128)(2,1)S(1)}, u32[]{:S(2)}, u32[]{:S(2)}) %collective-permute-start.1) | collective-permute-done | bytes 262176 | tf_op jit(solution)/shard_map/ppermute | solution.py:96
  27.6 4.3 %shard_map.182 = (bf16[32,4096]{1,0:T(8,128)(2,1)S(1)}, bf16[32,4096]{1,0:T(8,128)(2,1)S(1)}, bf16[32,4096]{1,0:T(8,128)(2,1)S(1)}, bf16[32,4096]{1,0:T(8,128)(2,1)S(1)}) custom-call(bf16[32,4096]{1,0:T(8,128)(2,1)S(1)} %get-tuple-element.56.block_0, bf16[32,4096]{1,0:T(8,128)(2,1)S(1)} %collective-permute-done.block_1, ...), custom_call_target="tpu_custom_call" | custom-call | flops 1048576 | bytes 1048576 | tf_op jit(solution)/shard_map/pallas_call | solution.py:124
  32.0 2.9 %collective-permute-start.5 = (bf16[32,4096]{1,0:T(8,128)(2,1)S(1)}, bf16[32,4096]{1,0:T(8,128)(2,1)S(1)}, u32[]{:S(2)}, u32[]{:S(2)}) collective-permute-start(bf16[32,4096]{1,0:T(8,128)(2,1)S(1)} %get-tuple-element.72), channel_id=1, source_target_pairs={{2,0},{3,1},{0,2},{1,3},{6,4},{7,5},{4,6},{5,7},{10,8},{11,9},{8,1... | collective-permute-start | bytes 786440 | tf_op jit(solution)/shard_map/ppermute | solution.py:96
  34.8 1.9 %collective-permute-start.6 = (bf16[32,4096]{1,0:T(8,128)(2,1)S(1)}, bf16[32,4096]{1,0:T(8,128)(2,1)S(1)}, u32[]{:S(2)}, u32[]{:S(2)}) collective-permute-start(bf16[32,4096]{1,0:T(8,128)(2,1)S(1)} %get-tuple-element.73), channel_id=1, source_target_pairs={{3,0},{0,1},{1,2},{2,3},{7,4},{4,5},{5,6},{6,7},{11,8},{8,9},{9,10... | collective-permute-start | bytes 786440 | tf_op jit(solution)/shard_map/ppermute | solution.py:96
  36.9 1.6 collective-permute-start.8
  38.5 0.9 collective-permute-done.3
  39.3 2.2 %collective-permute-done.4.refs_1_ = bf16[192,4096]{1,0:T(8,128)(2,1)S(1)} collective-permute-done((bf16[192,4096]{1,0:T(8,128)(2,1)}, bf16[192,4096]{1,0:T(8,128)(2,1)S(1)}, u32[]{:S(2)}, u32[]{:S(2)}) %collective-permute-start.4) | collective-permute-done | bytes 1572896 | tf_op jit(solution)/shard_map/ppermute | solution.py:92
  41.7 1.6 collective-permute-start.7
  43.3 14.0 %collective-permute-done.5 = bf16[32,4096]{1,0:T(8,128)(2,1)S(1)} collective-permute-done((bf16[32,4096]{1,0:T(8,128)(2,1)S(1)}, bf16[32,4096]{1,0:T(8,128)(2,1)S(1)}, u32[]{:S(2)}, u32[]{:S(2)}) %collective-permute-start.5) | collective-permute-done | bytes 262176 | tf_op jit(solution)/shard_map/ppermute | solution.py:96
  57.6 1.6 collective-permute-start.13
  59.3 1.6 collective-permute-start.10
  60.9 12.0 %collective-permute-start.11 = (bf16[32,4096]{1,0:T(8,128)(2,1)S(1)}, bf16[32,4096]{1,0:T(8,128)(2,1)S(1)}, u32[]{:S(2)}, u32[]{:S(2)}) collective-permute-start(bf16[32,4096]{1,0:T(8,128)(2,1)S(1)} %add_convert_fusion.1), channel_id=1, source_target_pairs={{3,0},{0,1},{1,2},{2,3},{7,4},{4,5},{5,6},{6,7},{11,8},{8,9},{9,10... | collective-permute-start | bytes 786440 | tf_op jit(solution)/shard_map/ppermute | solution.py:96
  72.9 1.5 collective-permute-start.12
  74.5 2.3 %collective-permute-start.9 = (bf16[32,4096]{1,0:T(8,128)(2,1)S(1)}, bf16[32,4096]{1,0:T(8,128)(2,1)S(1)}, u32[]{:S(2)}, u32[]{:S(2)}) collective-permute-start(bf16[32,4096]{1,0:T(8,128)(2,1)S(1)} %add_convert_fusion.1), channel_id=1, source_target_pairs={{1,0},{2,1},{3,2},{0,3},{5,4},{6,5},{7,6},{4,7},{9,8},{10,9},{11,1... | collective-permute-start | bytes 786440 | tf_op jit(solution)/shard_map/ppermute | solution.py:96
  76.8 0.6 collective-permute-start.14
  77.4 5.2 %collective-permute-done.11 = bf16[32,4096]{1,0:T(8,128)(2,1)S(1)} collective-permute-done((bf16[32,4096]{1,0:T(8,128)(2,1)S(1)}, bf16[32,4096]{1,0:T(8,128)(2,1)S(1)}, u32[]{:S(2)}, u32[]{:S(2)}) %collective-permute-start.11) | collective-permute-done | bytes 262176 | tf_op jit(solution)/shard_map/ppermute | solution.py:96
  82.6 1.1 collective-permute-done.9
  83.7 1.4 shard_map.184.up_0
  85.3 1.4 shard_map.183.gate_0
  86.7 0.6 collective-permute-start.16
  88.4 1.6 collective-permute-start.19
  90.0 0.9 collective-permute-done.17.up_1
  90.9 4.5 %collective-permute-done.16.gate_1 = bf16[384,4096]{1,0:T(8,128)(2,1)S(1)} collective-permute-done((bf16[384,4096]{1,0:T(8,128)(2,1)S(1)}, bf16[384,4096]{1,0:T(8,128)(2,1)S(1)}, u32[]{:S(2)}, u32[]{:S(2)}) %collective-permute-start.16) | collective-permute-done | bytes 3145760 | tf_op jit(solution)/shard_map/ppermute | solution.py:92
  95.4 3.8 %shard_map.185.near = bf16[128,768]{1,0:T(8,128)(2,1)S(1)} custom-call(bf16[128,4096]{1,0:T(8,128)(2,1)S(1)} %pad_maximum_fusion.states, bf16[384,4096]{1,0:T(8,128)(2,1)S(1)} %shard_map.183.gate_0, bf16[384,4096]{1,0:T(8,128)(2,1)S(1)} %collective-permute-done.16.gate_1, bf16[384,4096]{1,0:T(8,128)(2,1)S(1)} %shard_map.184.up_0, ...), custom_call_target="tpu_custom_call" | custom-call | flops 1048576 | bytes 1048576 | tf_op jit(solution)/shard_map/pallas_call | solution.py:124
  99.2 21.6 %collective-permute-done.19.refs_2_ = bf16[160,2048]{1,0:T(8,128)(2,1)S(1)} collective-permute-done((bf16[160,2048]{1,0:T(8,128)(2,1)S(1)}, bf16[160,2048]{1,0:T(8,128)(2,1)S(1)}, u32[]{:S(2)}, u32[]{:S(2)}) %collective-permute-start.19) | collective-permute-done | bytes 655392 | tf_op jit(solution)/shard_map/ppermute | solution.py:92
  121.5 0.6 collective-permute-start.21
  122.7 3.8 %shard_map.186.near = bf16[128,768]{1,0:T(8,128)(2,1)S(1)} custom-call(bf16[128,4096]{1,0:T(8,128)(2,1)S(1)} %pad_maximum_fusion.1.states, bf16[384,4096]{1,0:T(8,128)(2,1)S(1)} %shard_map.183.gate_0, bf16[384,4096]{1,0:T(8,128)(2,1)S(1)} %collective-permute-done.16.gate_1, bf16[384,4096]{1,0:T(8,128)(2,1)S(1)} %shard_map.184.up_0, ...), custom_call_target="tpu_custom_call" | custom-call | flops 1048576 | bytes 1048576 | tf_op jit(solution)/shard_map/pallas_call | solution.py:124
  126.4 1.6 collective-permute-start.27
  128.0 0.9 collective-permute-done.20.far
  129.0 1.3 shard_map.189
  130.2 1.6 %collective-permute-start.23 = (bf16[32,2048]{1,0:T(8,128)(2,1)S(1)}, bf16[32,2048]{1,0:T(8,128)(2,1)S(1)}, u32[]{:S(2)}, u32[]{:S(2)}) collective-permute-start(bf16[32,2048]{1,0:T(8,128)(2,1)S(1)} %get-tuple-element.97), channel_id=1, source_target_pairs={{1,0},{2,1},{3,2},{0,3},{5,4},{6,5},{7,6},{4,7},{9,8},{10,9},{11,1... | collective-permute-start | bytes 393224 | tf_op jit(solution)/shard_map/ppermute | solution.py:96
  131.9 3.2 %collective-permute-start.24 = (bf16[32,2048]{1,0:T(8,128)(2,1)S(1)}, bf16[32,2048]{1,0:T(8,128)(2,1)S(1)}, u32[]{:S(2)}, u32[]{:S(2)}) collective-permute-start(bf16[32,2048]{1,0:T(8,128)(2,1)S(1)} %get-tuple-element.98), channel_id=1, source_target_pairs={{2,0},{3,1},{0,2},{1,3},{6,4},{7,5},{4,6},{5,7},{10,8},{11,9},{8,1... | collective-permute-start | bytes 393224 | tf_op jit(solution)/shard_map/ppermute | solution.py:96
  135.1 1.3 shard_map.190
  136.4 3.9 %collective-permute-start.28 = (bf16[32,2048]{1,0:T(8,128)(2,1)S(1)}, bf16[32,2048]{1,0:T(8,128)(2,1)S(1)}, u32[]{:S(2)}, u32[]{:S(2)}) collective-permute-start(bf16[32,2048]{1,0:T(8,128)(2,1)S(1)} %get-tuple-element.101), channel_id=1, source_target_pairs={{1,0},{2,1},{3,2},{0,3},{5,4},{6,5},{7,6},{4,7},{9,8},{10,9},{11,1... | collective-permute-start | bytes 393224 | tf_op jit(solution)/shard_map/ppermute | solution.py:96
  140.3 5.4 %collective-permute-start.30 = (bf16[32,2048]{1,0:T(8,128)(2,1)S(1)}, bf16[32,2048]{1,0:T(8,128)(2,1)S(1)}, u32[]{:S(2)}, u32[]{:S(2)}) collective-permute-start(bf16[32,2048]{1,0:T(8,128)(2,1)S(1)} %get-tuple-element.103), channel_id=1, source_target_pairs={{3,0},{0,1},{1,2},{2,3},{7,4},{4,5},{5,6},{6,7},{11,8},{8,9},{9,10... | collective-permute-start | bytes 393224 | tf_op jit(solution)/shard_map/ppermute | solution.py:96
  145.7 7.4 %collective-permute-done.24 = bf16[32,2048]{1,0:T(8,128)(2,1)S(1)} collective-permute-done((bf16[32,2048]{1,0:T(8,128)(2,1)S(1)}, bf16[32,2048]{1,0:T(8,128)(2,1)S(1)}, u32[]{:S(2)}, u32[]{:S(2)}) %collective-permute-start.24) | collective-permute-done | bytes 131104 | tf_op jit(solution)/shard_map/ppermute | solution.py:96
  153.2 1.6 collective-permute-start.26
  154.8 2.6 %collective-permute-done.29 = bf16[32,2048]{1,0:T(8,128)(2,1)S(1)} collective-permute-done((bf16[32,2048]{1,0:T(8,128)(2,1)S(1)}, bf16[32,2048]{1,0:T(8,128)(2,1)S(1)}, u32[]{:S(2)}, u32[]{:S(2)}) %collective-permute-start.29) | collective-permute-done | bytes 131104 | tf_op jit(solution)/shard_map/ppermute | solution.py:96
  157.4 0.9 collective-permute-done.26
  158.5 0.9 add_convert_fusion
  (63 shorter events, 4.3 us)
Async XLA Ops:
  0.0 17.7 %collective-permute-start = (bf16[32,4096]{1,0:T(8,128)(2,1)}, bf16[32,4096]{1,0:T(8,128)(2,1)S(1)}, u32[]{:S(2)}, u32[]{:S(2)}) collective-permute-start(bf16[32,4096]{1,0:T(8,128)(2,1)} %refs_10_.1), channel_id=1, source_target_pairs={{1,0},{2,1},{3,2},{0,3},{5,4},{6,5},{7,6},{4,7},{9,8},{10,9},{11,1... | collective-permute-start | bytes 786440 | tf_op jit(solution)/shard_map/ppermute | solution.py:96
  5.0 22.5 %collective-permute-start.1 = (bf16[32,4096]{1,0:T(8,128)(2,1)}, bf16[32,4096]{1,0:T(8,128)(2,1)S(1)}, u32[]{:S(2)}, u32[]{:S(2)}) collective-permute-start(bf16[32,4096]{1,0:T(8,128)(2,1)} %refs_10_.1), channel_id=1, source_target_pairs={{2,0},{3,1},{0,2},{1,3},{6,4},{7,5},{4,6},{5,7},{10,8},{11,9},{8,1... | collective-permute-start | bytes 786440 | tf_op jit(solution)/shard_map/ppermute | solution.py:96
  5.1 22.5 %collective-permute-start.2 = (bf16[32,4096]{1,0:T(8,128)(2,1)}, bf16[32,4096]{1,0:T(8,128)(2,1)S(1)}, u32[]{:S(2)}, u32[]{:S(2)}) collective-permute-start(bf16[32,4096]{1,0:T(8,128)(2,1)} %refs_10_.1), channel_id=1, source_target_pairs={{3,0},{0,1},{1,2},{2,3},{7,4},{4,5},{5,6},{6,7},{11,8},{8,9},{9,10... | collective-permute-start | bytes 786440 | tf_op jit(solution)/shard_map/ppermute | solution.py:96
  6.1 35.5 %collective-permute-start.4 = (bf16[192,4096]{1,0:T(8,128)(2,1)}, bf16[192,4096]{1,0:T(8,128)(2,1)S(1)}, u32[]{:S(2)}, u32[]{:S(2)}) collective-permute-start(bf16[192,4096]{1,0:T(8,128)(2,1)} %bitcast.18), channel_id=1, source_target_pairs={{0,8},{8,0},{1,9},{9,1},{2,10},{10,2},{3,11},{11,3},{4,12},{12,4},... | collective-permute-start | bytes 4718600 | tf_op jit(solution)/shard_map/ppermute | solution.py:92
  27.6 9.2 %copy-start.1 = (bf16[4096,192]{0,1:T(8,128)(2,1)S(1)}, bf16[4096,192]{0,1:T(8,128)(2,1)}, u32[]{:S(2)}) copy-start(bf16[4096,192]{0,1:T(8,128)(2,1)} %param.37) | copy-start | bytes 4718596
  31.9 9.7 %copy-start = (bf16[4096,192]{0,1:T(8,128)(2,1)S(1)}, bf16[4096,192]{0,1:T(8,128)(2,1)}, u32[]{:S(2)}) copy-start(bf16[4096,192]{0,1:T(8,128)(2,1)} %param.36) | copy-start | bytes 4718596
  31.9 7.4 %collective-permute-start.3 = (bf16[32,4096]{1,0:T(8,128)(2,1)S(1)}, bf16[32,4096]{1,0:T(8,128)(2,1)S(1)}, u32[]{:S(2)}, u32[]{:S(2)}) collective-permute-start(bf16[32,4096]{1,0:T(8,128)(2,1)S(1)} %get-tuple-element.70), channel_id=1, source_target_pairs={{1,0},{2,1},{3,2},{0,3},{5,4},{6,5},{7,6},{4,7},{9,8},{10,9},{11,1... | collective-permute-start | bytes 786440 | tf_op jit(solution)/shard_map/ppermute | solution.py:96
  32.0 25.3 %collective-permute-start.5 = (bf16[32,4096]{1,0:T(8,128)(2,1)S(1)}, bf16[32,4096]{1,0:T(8,128)(2,1)S(1)}, u32[]{:S(2)}, u32[]{:S(2)}) collective-permute-start(bf16[32,4096]{1,0:T(8,128)(2,1)S(1)} %get-tuple-element.72), channel_id=1, source_target_pairs={{2,0},{3,1},{0,2},{1,3},{6,4},{7,5},{4,6},{5,7},{10,8},{11,9},{8,1... | collective-permute-start | bytes 786440 | tf_op jit(solution)/shard_map/ppermute | solution.py:96
  34.8 22.5 %collective-permute-start.6 = (bf16[32,4096]{1,0:T(8,128)(2,1)S(1)}, bf16[32,4096]{1,0:T(8,128)(2,1)S(1)}, u32[]{:S(2)}, u32[]{:S(2)}) collective-permute-start(bf16[32,4096]{1,0:T(8,128)(2,1)S(1)} %get-tuple-element.73), channel_id=1, source_target_pairs={{3,0},{0,1},{1,2},{2,3},{7,4},{4,5},{5,6},{6,7},{11,8},{8,9},{9,10... | collective-permute-start | bytes 786440 | tf_op jit(solution)/shard_map/ppermute | solution.py:96
  36.9 20.5 %collective-permute-start.8 = (bf16[192,2048]{1,0:T(8,128)(2,1)S(1)}, bf16[192,2048]{1,0:T(8,128)(2,1)S(1)}, u32[]{:S(2)}, u32[]{:S(2)}) collective-permute-start(bf16[192,2048]{1,0:T(8,128)(2,1)S(1)} %get-tuple-element.110), channel_id=1, source_target_pairs={{0,16},{16,0},{1,17},{17,1},{2,18},{18,2},{3,19},{19,3},{4,20},{20... | collective-permute-start | bytes 2359304 | tf_op jit(solution)/shard_map/ppermute | solution.py:92
  41.6 17.6 %copy-start.2 = (bf16[32,4096]{1,0:T(8,128)(2,1)S(1)}, bf16[32,4096]{1,0:T(8,128)(2,1)}, u32[]{:S(2)}) copy-start(bf16[32,4096]{1,0:T(8,128)(2,1)} %refs_10_.1) | copy-start | bytes 786436
  41.6 17.6 %copy-start.3 = (f32[4096]{0:T(1024)S(1)}, f32[4096]{0:T(1024)}, u32[]{:S(2)}) copy-start(f32[4096]{0:T(1024)} %param.33) | copy-start | bytes 49156
  41.7 15.7 %collective-permute-start.7 = (bf16[80,4096]{1,0:T(8,128)(2,1)S(1)}, bf16[80,4096]{1,0:T(8,128)(2,1)S(1)}, u32[]{:S(2)}, u32[]{:S(2)}) collective-permute-start(bf16[80,4096]{1,0:T(8,128)(2,1)S(1)} %split.12), channel_id=1, source_target_pairs={{0,8},{8,0},{1,9},{9,1},{2,10},{10,2},{3,11},{11,3},{4,12},{12,4},... | collective-permute-start | bytes 1966088 | tf_op jit(solution)/shard_map/ppermute | solution.py:92
  57.6 26.1 %collective-permute-start.13 = (bf16[112,4096]{1,0:T(8,128)(2,1)S(1)}, bf16[112,4096]{1,0:T(8,128)(2,1)S(1)}, u32[]{:S(2)}, u32[]{:S(2)}) collective-permute-start(bf16[112,4096]{1,0:T(8,128)(2,1)S(1)} %split.13), channel_id=1, source_target_pairs={{0,8},{8,0},{1,9},{9,1},{2,10},{10,2},{3,11},{11,3},{4,12},{12,4},... | collective-permute-start | bytes 2752520 | tf_op jit(solution)/shard_map/ppermute | solution.py:92
  59.3 17.4 %collective-permute-start.10 = (bf16[32,4096]{1,0:T(8,128)(2,1)S(1)}, bf16[32,4096]{1,0:T(8,128)(2,1)S(1)}, u32[]{:S(2)}, u32[]{:S(2)}) collective-permute-start(bf16[32,4096]{1,0:T(8,128)(2,1)S(1)} %add_convert_fusion.1), channel_id=1, source_target_pairs={{2,0},{3,1},{0,2},{1,3},{6,4},{7,5},{4,6},{5,7},{10,8},{11,9},{8,1... | collective-permute-start | bytes 786440 | tf_op jit(solution)/shard_map/ppermute | solution.py:96
  60.9 21.7 %collective-permute-start.11 = (bf16[32,4096]{1,0:T(8,128)(2,1)S(1)}, bf16[32,4096]{1,0:T(8,128)(2,1)S(1)}, u32[]{:S(2)}, u32[]{:S(2)}) collective-permute-start(bf16[32,4096]{1,0:T(8,128)(2,1)S(1)} %add_convert_fusion.1), channel_id=1, source_target_pairs={{3,0},{0,1},{1,2},{2,3},{7,4},{4,5},{5,6},{6,7},{11,8},{8,9},{9,10... | collective-permute-start | bytes 786440 | tf_op jit(solution)/shard_map/ppermute | solution.py:96
  72.9 9.6 %collective-permute-start.12 = (bf16[32,4096]{1,0:T(8,128)(2,1)S(1)}, bf16[32,4096]{1,0:T(8,128)(2,1)S(1)}, u32[]{:S(2)}, u32[]{:S(2)}) collective-permute-start(bf16[32,4096]{1,0:T(8,128)(2,1)S(1)} %add_convert_fusion.1), channel_id=1, source_target_pairs={{0,16},{16,0},{1,17},{17,1},{2,18},{18,2},{3,19},{19,3},{4,20},{20... | collective-permute-start | bytes 786440 | tf_op jit(solution)/shard_map/ppermute | solution.py:92
  74.5 9.2 %collective-permute-start.9 = (bf16[32,4096]{1,0:T(8,128)(2,1)S(1)}, bf16[32,4096]{1,0:T(8,128)(2,1)S(1)}, u32[]{:S(2)}, u32[]{:S(2)}) collective-permute-start(bf16[32,4096]{1,0:T(8,128)(2,1)S(1)} %add_convert_fusion.1), channel_id=1, source_target_pairs={{1,0},{2,1},{3,2},{0,3},{5,4},{6,5},{7,6},{4,7},{9,8},{10,9},{11,1... | collective-permute-start | bytes 786440 | tf_op jit(solution)/shard_map/ppermute | solution.py:96
  76.8 6.9 %collective-permute-start.14 = (bf16[32,2048]{1,0:T(8,128)(2,1)S(1)}, bf16[32,2048]{1,0:T(8,128)(2,1)S(1)}, u32[]{:S(2)}, u32[]{:S(2)}) collective-permute-start(bf16[32,2048]{1,0:T(8,128)(2,1)S(1)} %split.14), channel_id=1, source_target_pairs={{0,8},{8,0},{1,9},{9,1},{2,10},{10,2},{3,11},{11,3},{4,12},{12,4},... | collective-permute-start | bytes 393224 | tf_op jit(solution)/shard_map/ppermute | solution.py:92
  85.2 5.7 %collective-permute-start.17 = (bf16[384,4096]{1,0:T(8,128)(2,1)S(1)}, bf16[384,4096]{1,0:T(8,128)(2,1)S(1)}, u32[]{:S(2)}, u32[]{:S(2)}) collective-permute-start(bf16[384,4096]{1,0:T(8,128)(2,1)S(1)} %shard_map.184.up_0), channel_id=1, source_target_pairs={{0,4},{4,0},{1,5},{5,1},{2,6},{6,2},{3,7},{7,3},{8,12},{12,8},{9,1... | collective-permute-start | bytes 9437192 | tf_op jit(solution)/shard_map/ppermute | solution.py:92
  86.7 8.7 %collective-permute-start.16 = (bf16[384,4096]{1,0:T(8,128)(2,1)S(1)}, bf16[384,4096]{1,0:T(8,128)(2,1)S(1)}, u32[]{:S(2)}, u32[]{:S(2)}) collective-permute-start(bf16[384,4096]{1,0:T(8,128)(2,1)S(1)} %shard_map.183.gate_0), channel_id=1, source_target_pairs={{0,4},{4,0},{1,5},{5,1},{2,6},{6,2},{3,7},{7,3},{8,12},{12,8},{9,1... | collective-permute-start | bytes 9437192 | tf_op jit(solution)/shard_map/ppermute | solution.py:92
  87.2 33.6 %collective-permute-start.18 = (bf16[192,2048]{1,0:T(8,128)(2,1)S(1)}, bf16[192,2048]{1,0:T(8,128)(2,1)S(1)}, u32[]{:S(2)}, u32[]{:S(2)}) collective-permute-start(bf16[192,2048]{1,0:T(8,128)(2,1)S(1)} %collective-permute-done.8.refs_0_), channel_id=1, source_target_pairs={{0,8},{8,0},{1,9},{9,1},{2,10},{10,2},{3,11},{11,3},{4,12},{12,4},... | collective-permute-start | bytes 2359304 | tf_op jit(solution)/shard_map/ppermute | solution.py:92
  87.8 33.0 %collective-permute-start.15 = (bf16[96,4096]{1,0:T(8,128)(2,1)S(1)}, bf16[96,4096]{1,0:T(8,128)(2,1)S(1)}, u32[]{:S(2)}, u32[]{:S(2)}) collective-permute-start(bf16[96,4096]{1,0:T(8,128)(2,1)S(1)} %pad_maximum_fusion.2), channel_id=1, source_target_pairs={{0,16},{16,0},{1,17},{17,1},{2,18},{18,2},{3,19},{19,3},{4,20},{20... | collective-permute-start | bytes 2359304 | tf_op jit(solution)/shard_map/ppermute | solution.py:92
  88.4 32.5 %collective-permute-start.19 = (bf16[160,2048]{1,0:T(8,128)(2,1)S(1)}, bf16[160,2048]{1,0:T(8,128)(2,1)S(1)}, u32[]{:S(2)}, u32[]{:S(2)}) collective-permute-start(bf16[160,2048]{1,0:T(8,128)(2,1)S(1)} %split.15), channel_id=1, source_target_pairs={{0,8},{8,0},{1,9},{9,1},{2,10},{10,2},{3,11},{11,3},{4,12},{12,4},... | collective-permute-start | bytes 1966088 | tf_op jit(solution)/shard_map/ppermute | solution.py:92
  121.0 8.0 %collective-permute-start.22 = (bf16[384,2048]{1,0:T(8,128)(2,1)S(1)}, bf16[384,2048]{1,0:T(8,128)(2,1)S(1)}, u32[]{:S(2)}, u32[]{:S(2)}) collective-permute-start(bf16[384,2048]{1,0:T(8,128)(2,1)S(1)} %shard_map.188.far_0), channel_id=1, source_target_pairs={{0,4},{4,0},{1,5},{5,1},{2,6},{6,2},{3,7},{7,3},{8,12},{12,8},{9,1... | collective-permute-start | bytes 4718600 | tf_op jit(solution)/shard_map/ppermute | solution.py:92
  121.5 7.4 %collective-permute-start.21 = (bf16[384,2048]{1,0:T(8,128)(2,1)S(1)}, bf16[384,2048]{1,0:T(8,128)(2,1)S(1)}, u32[]{:S(2)}, u32[]{:S(2)}) collective-permute-start(bf16[384,2048]{1,0:T(8,128)(2,1)S(1)} %shard_map.187.near_0), channel_id=1, source_target_pairs={{0,4},{4,0},{1,5},{5,1},{2,6},{6,2},{3,7},{7,3},{8,12},{12,8},{9,1... | collective-permute-start | bytes 4718600 | tf_op jit(solution)/shard_map/ppermute | solution.py:92
  122.1 6.9 %collective-permute-start.20 = (bf16[128,768]{1,0:T(8,128)(2,1)S(1)}, bf16[128,768]{1,0:T(8,128)(2,1)S(1)}, u32[]{:S(2)}, u32[]{:S(2)}) collective-permute-start(bf16[128,768]{1,0:T(8,128)(2,1)S(1)} %shard_map.185.near), channel_id=1, source_target_pairs={{0,16},{16,0},{1,17},{17,1},{2,18},{18,2},{3,19},{19,3},{4,20},{20... | collective-permute-start | bytes 589832 | tf_op jit(solution)/shard_map/ppermute | solution.py:92
  126.4 8.6 %collective-permute-start.27 = (bf16[128,768]{1,0:T(8,128)(2,1)S(1)}, bf16[128,768]{1,0:T(8,128)(2,1)S(1)}, u32[]{:S(2)}, u32[]{:S(2)}) collective-permute-start(bf16[128,768]{1,0:T(8,128)(2,1)S(1)} %shard_map.186.near), channel_id=1, source_target_pairs={{0,16},{16,0},{1,17},{17,1},{2,18},{18,2},{3,19},{19,3},{4,20},{20... | collective-permute-start | bytes 589832 | tf_op jit(solution)/shard_map/ppermute | solution.py:92
  130.2 10.1 %collective-permute-start.23 = (bf16[32,2048]{1,0:T(8,128)(2,1)S(1)}, bf16[32,2048]{1,0:T(8,128)(2,1)S(1)}, u32[]{:S(2)}, u32[]{:S(2)}) collective-permute-start(bf16[32,2048]{1,0:T(8,128)(2,1)S(1)} %get-tuple-element.97), channel_id=1, source_target_pairs={{1,0},{2,1},{3,2},{0,3},{5,4},{6,5},{7,6},{4,7},{9,8},{10,9},{11,1... | collective-permute-start | bytes 393224 | tf_op jit(solution)/shard_map/ppermute | solution.py:96
  131.9 21.3 %collective-permute-start.24 = (bf16[32,2048]{1,0:T(8,128)(2,1)S(1)}, bf16[32,2048]{1,0:T(8,128)(2,1)S(1)}, u32[]{:S(2)}, u32[]{:S(2)}) collective-permute-start(bf16[32,2048]{1,0:T(8,128)(2,1)S(1)} %get-tuple-element.98), channel_id=1, source_target_pairs={{2,0},{3,1},{0,2},{1,3},{6,4},{7,5},{4,6},{5,7},{10,8},{11,9},{8,1... | collective-permute-start | bytes 393224 | tf_op jit(solution)/shard_map/ppermute | solution.py:96
  135.1 18.0 %collective-permute-start.25 = (bf16[32,2048]{1,0:T(8,128)(2,1)S(1)}, bf16[32,2048]{1,0:T(8,128)(2,1)S(1)}, u32[]{:S(2)}, u32[]{:S(2)}) collective-permute-start(bf16[32,2048]{1,0:T(8,128)(2,1)S(1)} %get-tuple-element.99), channel_id=1, source_target_pairs={{3,0},{0,1},{1,2},{2,3},{7,4},{4,5},{5,6},{6,7},{11,8},{8,9},{9,10... | collective-permute-start | bytes 393224 | tf_op jit(solution)/shard_map/ppermute | solution.py:96
  136.3 22.1 %copy-start.4 = (f32[4096]{0:T(1024)S(1)}, f32[4096]{0:T(1024)}, u32[]{:S(2)}) copy-start(f32[4096]{0:T(1024)} %param.34) | copy-start | bytes 49156
  136.4 18.4 %collective-permute-start.28 = (bf16[32,2048]{1,0:T(8,128)(2,1)S(1)}, bf16[32,2048]{1,0:T(8,128)(2,1)S(1)}, u32[]{:S(2)}, u32[]{:S(2)}) collective-permute-start(bf16[32,2048]{1,0:T(8,128)(2,1)S(1)} %get-tuple-element.101), channel_id=1, source_target_pairs={{1,0},{2,1},{3,2},{0,3},{5,4},{6,5},{7,6},{4,7},{9,8},{10,9},{11,1... | collective-permute-start | bytes 393224 | tf_op jit(solution)/shard_map/ppermute | solution.py:96
  140.2 17.1 %collective-permute-start.29 = (bf16[32,2048]{1,0:T(8,128)(2,1)S(1)}, bf16[32,2048]{1,0:T(8,128)(2,1)S(1)}, u32[]{:S(2)}, u32[]{:S(2)}) collective-permute-start(bf16[32,2048]{1,0:T(8,128)(2,1)S(1)} %get-tuple-element.102), channel_id=1, source_target_pairs={{2,0},{3,1},{0,2},{1,3},{6,4},{7,5},{4,6},{5,7},{10,8},{11,9},{8,1... | collective-permute-start | bytes 393224 | tf_op jit(solution)/shard_map/ppermute | solution.py:96
  140.3 17.1 %collective-permute-start.30 = (bf16[32,2048]{1,0:T(8,128)(2,1)S(1)}, bf16[32,2048]{1,0:T(8,128)(2,1)S(1)}, u32[]{:S(2)}, u32[]{:S(2)}) collective-permute-start(bf16[32,2048]{1,0:T(8,128)(2,1)S(1)} %get-tuple-element.103), channel_id=1, source_target_pairs={{3,0},{0,1},{1,2},{2,3},{7,4},{4,5},{5,6},{6,7},{11,8},{8,9},{9,10... | collective-permute-start | bytes 393224 | tf_op jit(solution)/shard_map/ppermute | solution.py:96
  153.2 5.0 %collective-permute-start.26 = (bf16[32,2048]{1,0:T(8,128)(2,1)S(1)}, bf16[32,2048]{1,0:T(8,128)(2,1)S(1)}, u32[]{:S(2)}, u32[]{:S(2)}) collective-permute-start(bf16[32,2048]{1,0:T(8,128)(2,1)S(1)} %add_convert_fusion.2), channel_id=1, source_target_pairs={{0,16},{16,0},{1,17},{17,1},{2,18},{18,2},{3,19},{19,3},{4,20},{20... | collective-permute-start | bytes 393224 | tf_op jit(solution)/shard_map/ppermute | solution.py:92

commit v15 on v14

--- a/solution.py
+++ b/solution.py
@@ -180,6 +180,45 @@
         compiler_params=pltpu.CompilerParams(vmem_limit_bytes=1 << 20),
         cost_estimate=pl.CostEstimate(flops=0, bytes_accessed=weight * size, transcendentals=0),
     )(*arrays)
+
+
+def stacked(*arrays):
+    rows, columns = arrays[0].shape
+
+    def kernel(*refs):
+        sources, target, buffer, sems_in, sems_out = refs[:-4], *refs[-4:]
+        into = [
+            pltpu.make_async_copy(source, buffer.at[k], sems_in.at[k])
+            for k, source in enumerate(sources)
+        ]
+        out = [
+            pltpu.make_async_copy(
+                buffer.at[k], target.at[pl.ds(k * rows, rows), :], sems_out.at[k]
+            )
+            for k in range(len(sources))
+        ]
+        for copy in into:
+            copy.start()
+        for copy_in, copy_out in zip(into, out):
+            copy_in.wait()
+            copy_out.start()
+        for copy in out:
+            copy.wait()
+
+    count = len(arrays)
+    return pl.pallas_call(
+        kernel,
+        out_shape=pltpu.HBM((count * rows, columns), arrays[0].dtype),
+        in_specs=[pl.BlockSpec(memory_space=pl.ANY)] * count,
+        out_specs=pl.BlockSpec(memory_space=pltpu.HBM),
+        scratch_shapes=[
+            pltpu.VMEM((count, rows, columns), arrays[0].dtype),
+            pltpu.SemaphoreType.DMA((count,)),
+            pltpu.SemaphoreType.DMA((count,)),
+        ],
+        compiler_params=pltpu.CompilerParams(vmem_limit_bytes=8 << 20),
+        cost_estimate=pl.CostEstimate(flops=0, bytes_accessed=1 << 20, transcendentals=0),
+    )(*(in_hbm(array) for array in arrays))
 
 
 NT = (((1,), (1,)), ((), ()))
@@ -295,7 +334,8 @@
     gate_rows, up_rows, down_rows = ffn_rows
     y = lax.axis_index("y")
     half = width // 2
-    gate_x = exchange(gate_rows, "x")
+    units = gate_rows.shape[0]
+    gate_up_x = exchange(stacked(gate_rows, up_rows), "x")
     cosine, sine = jnp.cos(angles), jnp.sin(angles)
     block = jax.ShapeDtypeStruct((tok_dev, width), jnp.bfloat16)
     *staged_rows, own_block = staged(
@@ -324,20 +364,16 @@
     near = lax.dynamic_slice_in_dim(down_rows, y * half, half, axis=1)
     far = exchange(lax.dynamic_slice_in_dim(down_rows, (1 - y) * half, half, axis=1), "y")
     arrivals = line_arrivals(parts)
-    arrivals[0], gate_x, up_late = together(arrivals[0], gate_x, up_rows)
-    units = up_late.shape[0]
-    up_parts = jnp.split(up_late, [units * 5 // 12])
-    up_x = [exchange(up_parts[0], "x")]
-    attn_own, up_x[0], up_part, near, far = together(
-        line_sum(arrivals), up_x[0], up_parts[1], near, far
-    )
-    up_x.append(exchange(up_part, "x"))
-    near_x = [exchange(rows, "x") for rows in jnp.split(near, [near.shape[0] // 6])]
+    attn_own, near, far = together(line_sum(arrivals), near, far)
+    near_x = [exchange(rows, "x") for rows in jnp.split(near, 2)]
     residual_own = add_normed(layer_input, attn_own, gains[0])
     own, *line, other = together(*line_gather(residual_own), exchange(residual_own, "y"))
-    line, gate_x, *up_x, near_x[0] = together(jnp.concatenate(line), gate_x, *up_x, near_x[0])
+    line, gate_up_x, near_x[0] = together(jnp.concatenate(line), gate_up_x, near_x[0])
     far_x = exchange(far, "x")
-    halves = [*both_halves(in_hbm(gate_rows), gate_x), *both_halves(in_hbm(up_rows), *up_x)]
+    halves = [
+        *both_halves(in_hbm(gate_rows), (gate_up_x, 0, units)),
+        *both_halves(in_hbm(up_rows), (gate_up_x, units, units)),
+    ]
 
     def hidden_units_of(first, others):
         (hidden,) = vmem_call(
@@ -351,9 +387,10 @@
 
     line_other = exchange(line, "y")
     hidden_own = hidden_units_of(own, line)
-    line_other, hidden_own, far_x, near_x[1] = together(line_other, hidden_own, far_x, near_x[1])
+    line_other, hidden_own = together(line_other, hidden_own)
     from_own = exchange(hidden_own, "y")
     hidden_other = hidden_units_of(other, line_other)
+    hidden_other, from_own, far_x, near_x[1] = together(hidden_other, from_own, far_x, near_x[1])
     from_other = exchange(hidden_other, "y")
     down_halves = [*both_halves(near, *near_x), *both_halves(far, far_x)]
 

time: 160 us -> 156 us (0.975)
  starting transfers between devices: 56.9 us -> 39.7 us
  waiting for transfers between devices: 72 us -> 83 us
  Pallas kernels: 24.4 us -> 28.8 us
  other arithmetic: 5.38 us -> 3.28 us
    ppermute x15, waiting for transfers between devices: 41 us -> 55.9 us  [shift(): return lax.ppermute(block, 'mlp', [((k + hops) % 4, k) for k in range(4)])]
    ppermute x15, starting transfers between devices: 41 us -> 26.2 us  [shift(): return lax.ppermute(block, 'mlp', [((k + hops) % 4, k) for k in range(4)])]
    ppermute x16 -> x14, waiting for transfers between devices: 31.1 us -> 27.1 us  [exchange(): return lax.ppermute(block, axis, [(0, 1), (1, 0)])]
    pallas_call x0 -> x1, Pallas kernels: none -> 3.12 us  [stacked(): pl.pallas_call(kernel, out_shape=pltpu.HBM((count * rows, columns), array...]
    ppermute x16 -> x14, starting transfers between devices: 15.8 us -> 13.5 us  [exchange(): return lax.ppermute(block, axis, [(0, 1), (1, 0)])]
  transfers between devices with their start and end apart: 31 -> 29, of which waited for: 13 -> 16; matrix products, arithmetic and copies ran while one was open for 3% -> 2% of each run, Pallas kernels for 14% -> 17%
where the time goes in v15:
time: 156 us; the launch traced here: 155 us
  waiting for transfers between devices  83 us (53%)
  starting transfers between devices  39.7 us (25%)
  Pallas kernels  28.8 us (18%)
  other arithmetic  3.28 us (2%)
    ppermute x15, waiting for transfers between devices, shift(): return lax.ppermute(block, 'mlp', [((k + hops) % 4, k) for k in range(4)])  55.9 us
    ppermute x14, waiting for transfers between devices, exchange(): return lax.ppermute(block, axis, [(0, 1), (1, 0)])  27.1 us
    ppermute x15, starting transfers between devices, shift(): return lax.ppermute(block, 'mlp', [((k + hops) % 4, k) for k in range(4)])  26.2 us
    pallas_call x5, Pallas kernels, vmem_call(): pl.pallas_call(kernel, out_shape=outs, in_specs=[whole] * len(operands),...  15.7 us
    ppermute x14, starting transfers between devices, exchange(): return lax.ppermute(block, axis, [(0, 1), (1, 0)])  13.5 us
    pallas_call x5, Pallas kernels, staged(): pl.pallas_call(kernel, out_shape=[pltpu.VMEM(shape, group[0][0].dtype) fo...  10 us
  transfers between devices with their start and end apart: 29, of which 16 were waited for; matrix products, arithmetic and copies ran while one was open for 2% of the time, Pallas kernels for 17%

profile of v15, /device:TPU:0, one launch (start us, length us, event | category | flops | bytes accessed | tf_op | source)
XLA Modules:
  0.0 155.3 jit_solution(5097479461238304670)
XLA Ops:
  0.0 5.0 %collective-permute-start = (bf16[32,4096]{1,0:T(8,128)(2,1)}, bf16[32,4096]{1,0:T(8,128)(2,1)S(1)}, u32[]{:S(2)}, u32[]{:S(2)}) collective-permute-start(bf16[32,4096]{1,0:T(8,128)(2,1)} %refs_10_.1), channel_id=1, source_target_pairs={{1,0},{2,1},{3,2},{0,3},{5,4},{6,5},{7,6},{4,7},{9,8},{10,9},{11,1... | collective-permute-start | bytes 786440 | tf_op jit(solution)/shard_map/ppermute | solution.py:96
  5.1 1.0 collective-permute-start.2
  6.1 3.1 %shard_map.183 = bf16[384,4096]{1,0:T(8,128)(2,1)} custom-call(bf16[192,4096]{1,0:T(8,128)(2,1)} %bitcast.14, bf16[192,4096]{1,0:T(8,128)(2,1)} %bitcast.16), custom_call_target="tpu_custom_call" | custom-call | bytes 1048576 | tf_op jit(solution)/shard_map/pallas_call | solution.py:209
  9.2 1.6 %collective-permute-start.11 = (bf16[384,4096]{1,0:T(8,128)(2,1)}, bf16[384,4096]{1,0:T(8,128)(2,1)S(1)}, u32[]{:S(2)}, u32[]{:S(2)}) collective-permute-start(bf16[384,4096]{1,0:T(8,128)(2,1)} %shard_map.183), channel_id=1, source_target_pairs={{0,8},{8,0},{1,9},{9,1},{2,10},{10,2},{3,11},{11,3},{4,12},{12,4},... | collective-permute-start | bytes 9437192 | tf_op jit(solution)/shard_map/ppermute | solution.py:92
  11.6 0.5 and_select_fusion
  12.1 6.6 %shard_map.181 = (bf16[4096,512]{1,0:T(8,128)(2,1)S(1)}, bf16[4096,512]{1,0:T(8,128)(2,1)S(1)}, bf16[4096,512]{1,0:T(8,128)(2,1)S(1)}, bf16[512,4096]{1,0:T(8,12...) custom-call(bf16[4096,512]{1,0:T(8,128)(2,1)} %refs_0_.1, ...), custom_call_target="tpu_custom_call" | custom-call | tf_op jit(solution)/shard_map/pallas_call | solution.py:174
  18.8 8.8 %collective-permute-done.1.block_2 = bf16[32,4096]{1,0:T(8,128)(2,1)} collective-permute-done((bf16[32,4096]{1,0:T(8,128)(2,1)}, bf16[32,4096]{1,0:T(8,128)(2,1)}, u32[]{:S(2)}, u32[]{:S(2)}) %collective-permute-start.1) | collective-permute-done | bytes 262176 | tf_op jit(solution)/shard_map/ppermute | solution.py:96
  27.7 5.6 %shard_map.182 = (bf16[32,4096]{1,0:T(8,128)(2,1)S(1)}, bf16[32,4096]{1,0:T(8,128)(2,1)S(1)}, bf16[32,4096]{1,0:T(8,128)(2,1)S(1)}, bf16[32,4096]{1,0:T(8,128)(2,1)S(1)}) custom-call(bf16[32,4096]{1,0:T(8,128)(2,1)S(1)} %get-tuple-element.51.block_0, bf16[32,4096]{1,0:T(8,128)(2,1)S(1)} %collective-permute-done.block_1, ...), custom_call_target="tpu_custom_call" | custom-call | flops 1048576 | bytes 1048576 | tf_op jit(solution)/shard_map/pallas_call | solution.py:124
  33.3 2.9 %collective-permute-start.4 = (bf16[32,4096]{1,0:T(8,128)(2,1)S(1)}, bf16[32,4096]{1,0:T(8,128)(2,1)S(1)}, u32[]{:S(2)}, u32[]{:S(2)}) collective-permute-start(bf16[32,4096]{1,0:T(8,128)(2,1)S(1)} %get-tuple-element.66), channel_id=1, source_target_pairs={{2,0},{3,1},{0,2},{1,3},{6,4},{7,5},{4,6},{5,7},{10,8},{11,9},{8,1... | collective-permute-start | bytes 786440 | tf_op jit(solution)/shard_map/ppermute | solution.py:96
  36.2 1.9 %collective-permute-start.5 = (bf16[32,4096]{1,0:T(8,128)(2,1)S(1)}, bf16[32,4096]{1,0:T(8,128)(2,1)S(1)}, u32[]{:S(2)}, u32[]{:S(2)}) collective-permute-start(bf16[32,4096]{1,0:T(8,128)(2,1)S(1)} %get-tuple-element.67), channel_id=1, source_target_pairs={{3,0},{0,1},{1,2},{2,3},{7,4},{4,5},{5,6},{6,7},{11,8},{8,9},{9,10... | collective-permute-start | bytes 786440 | tf_op jit(solution)/shard_map/ppermute | solution.py:96
  38.3 1.6 %collective-permute-start.6 = (bf16[192,2048]{1,0:T(8,128)(2,1)S(1)}, bf16[192,2048]{1,0:T(8,128)(2,1)S(1)}, u32[]{:S(2)}, u32[]{:S(2)}) collective-permute-start(bf16[192,2048]{1,0:T(8,128)(2,1)S(1)} %get-tuple-element.100), channel_id=1, source_target_pairs={{0,16},{16,0},{1,17},{17,1},{2,18},{18,2},{3,19},{19,3},{4,20},{20... | collective-permute-start | bytes 2359304 | tf_op jit(solution)/shard_map/ppermute | solution.py:92
  39.9 0.8 collective-permute-done.3
  40.7 18.0 %collective-permute-done.4 = bf16[32,4096]{1,0:T(8,128)(2,1)S(1)} collective-permute-done((bf16[32,4096]{1,0:T(8,128)(2,1)S(1)}, bf16[32,4096]{1,0:T(8,128)(2,1)S(1)}, u32[]{:S(2)}, u32[]{:S(2)}) %collective-permute-start.4) | collective-permute-done | bytes 262176 | tf_op jit(solution)/shard_map/ppermute | solution.py:96
  59.2 1.6 %collective-permute-start.10 = (bf16[32,4096]{1,0:T(8,128)(2,1)S(1)}, bf16[32,4096]{1,0:T(8,128)(2,1)S(1)}, u32[]{:S(2)}, u32[]{:S(2)}) collective-permute-start(bf16[32,4096]{1,0:T(8,128)(2,1)S(1)} %add_convert_fusion.1), channel_id=1, source_target_pairs={{0,16},{16,0},{1,17},{17,1},{2,18},{18,2},{3,19},{19,3},{4,20},{20... | collective-permute-start | bytes 786440 | tf_op jit(solution)/shard_map/ppermute | solution.py:92
  60.8 2.0 %collective-permute-start.9 = (bf16[32,4096]{1,0:T(8,128)(2,1)S(1)}, bf16[32,4096]{1,0:T(8,128)(2,1)S(1)}, u32[]{:S(2)}, u32[]{:S(2)}) collective-permute-start(bf16[32,4096]{1,0:T(8,128)(2,1)S(1)} %add_convert_fusion.1), channel_id=1, source_target_pairs={{3,0},{0,1},{1,2},{2,3},{7,4},{4,5},{5,6},{6,7},{11,8},{8,9},{9,10... | collective-permute-start | bytes 786440 | tf_op jit(solution)/shard_map/ppermute | solution.py:96
  62.9 3.2 %collective-permute-done.10 = bf16[32,4096]{1,0:T(8,128)(2,1)S(1)} collective-permute-done((bf16[32,4096]{1,0:T(8,128)(2,1)S(1)}, bf16[32,4096]{1,0:T(8,128)(2,1)S(1)}, u32[]{:S(2)}, u32[]{:S(2)}) %collective-permute-start.10) | collective-permute-done | bytes 262176 | tf_op jit(solution)/shard_map/ppermute | solution.py:92
  66.0 1.5 collective-permute-start.12
  67.5 0.5 collective-permute-done.7
  68.0 15.7 %collective-permute-done.8 = bf16[32,4096]{1,0:T(8,128)(2,1)S(1)} collective-permute-done((bf16[32,4096]{1,0:T(8,128)(2,1)S(1)}, bf16[32,4096]{1,0:T(8,128)(2,1)S(1)}, u32[]{:S(2)}, u32[]{:S(2)}) %collective-permute-start.8) | collective-permute-done | bytes 262176 | tf_op jit(solution)/shard_map/ppermute | solution.py:96
  83.7 3.1 %collective-permute-done.12.refs_1_ = bf16[96,2048]{1,0:T(8,128)(2,1)S(1)} collective-permute-done((bf16[96,2048]{1,0:T(8,128)(2,1)S(1)}, bf16[96,2048]{1,0:T(8,128)(2,1)S(1)}, u32[]{:S(2)}, u32[]{:S(2)}) %collective-permute-start.12) | collective-permute-done | bytes 393248 | tf_op jit(solution)/shard_map/ppermute | solution.py:92
  86.9 1.4 shard_map.184.gate_0
  88.3 1.4 shard_map.185.up_0
  89.9 0.5 collective-permute-start.15
  90.4 1.5 collective-permute-start.13
  91.9 1.5 collective-permute-start.18
  93.4 0.5 collective-permute-start.17
  94.0 1.5 collective-permute-done.14.gate_1
  95.5 4.5 %collective-permute-done.15.up_1 = bf16[384,4096]{1,0:T(8,128)(2,1)S(1)} collective-permute-done((bf16[384,4096]{1,0:T(8,128)(2,1)S(1)}, bf16[384,4096]{1,0:T(8,128)(2,1)S(1)}, u32[]{:S(2)}, u32[]{:S(2)}) %collective-permute-start.15) | collective-permute-done | bytes 3145760 | tf_op jit(solution)/shard_map/ppermute | solution.py:92
  100.0 3.8 %shard_map.186.near = bf16[128,768]{1,0:T(8,128)(2,1)S(1)} custom-call(bf16[128,4096]{1,0:T(8,128)(2,1)S(1)} %pad_maximum_fusion.states, bf16[384,4096]{1,0:T(8,128)(2,1)S(1)} %shard_map.184.gate_0, bf16[384,4096]{1,0:T(8,128)(2,1)S(1)} %collective-permute-done.14.gate_1, bf16[384,4096]{1,0:T(8,128)(2,1)S(1)} %shard_map.185.up_0, ...), custom_call_target="tpu_custom_call" | custom-call | flops 1048576 | bytes 1048576 | tf_op jit(solution)/shard_map/pallas_call | solution.py:124
  103.8 6.1 %collective-permute-done.13 = bf16[96,4096]{1,0:T(8,128)(2,1)S(1)} collective-permute-done((bf16[96,4096]{1,0:T(8,128)(2,1)S(1)}, bf16[96,4096]{1,0:T(8,128)(2,1)S(1)}, u32[]{:S(2)}, u32[]{:S(2)}) %collective-permute-start.13) | collective-permute-done | bytes 786464 | tf_op jit(solution)/shard_map/ppermute | solution.py:92
  109.9 1.5 collective-permute-start.16
  111.5 3.8 %shard_map.187.near = bf16[128,768]{1,0:T(8,128)(2,1)S(1)} custom-call(bf16[128,4096]{1,0:T(8,128)(2,1)S(1)} %pad_maximum_fusion.1.states, bf16[384,4096]{1,0:T(8,128)(2,1)S(1)} %shard_map.184.gate_0, bf16[384,4096]{1,0:T(8,128)(2,1)S(1)} %collective-permute-done.14.gate_1, bf16[384,4096]{1,0:T(8,128)(2,1)S(1)} %shard_map.185.up_0, ...), custom_call_target="tpu_custom_call" | custom-call | flops 1048576 | bytes 1048576 | tf_op jit(solution)/shard_map/pallas_call | solution.py:124
  115.3 4.2 %collective-permute-done.17.refs_1_ = bf16[192,2048]{1,0:T(8,128)(2,1)S(1)} collective-permute-done((bf16[192,2048]{1,0:T(8,128)(2,1)S(1)}, bf16[192,2048]{1,0:T(8,128)(2,1)S(1)}, u32[]{:S(2)}, u32[]{:S(2)}) %collective-permute-start.17) | collective-permute-done | bytes 786464 | tf_op jit(solution)/shard_map/ppermute | solution.py:92
  119.8 0.5 shard_map.188.near_0
  120.2 0.6 collective-permute-start.19
  120.8 0.5 collective-permute-start.25
  121.3 1.9 %collective-permute-done.20.far_1 = bf16[384,2048]{1,0:T(8,128)(2,1)S(1)} collective-permute-done((bf16[384,2048]{1,0:T(8,128)(2,1)S(1)}, bf16[384,2048]{1,0:T(8,128)(2,1)S(1)}, u32[]{:S(2)}, u32[]{:S(2)}) %collective-permute-start.20) | collective-permute-done | bytes 1572896 | tf_op jit(solution)/shard_map/ppermute | solution.py:92
  123.2 2.2 %collective-permute-done.19.near_1 = bf16[384,2048]{1,0:T(8,128)(2,1)S(1)} collective-permute-done((bf16[384,2048]{1,0:T(8,128)(2,1)S(1)}, bf16[384,2048]{1,0:T(8,128)(2,1)S(1)}, u32[]{:S(2)}, u32[]{:S(2)}) %collective-permute-start.19) | collective-permute-done | bytes 1572896 | tf_op jit(solution)/shard_map/ppermute | solution.py:92
  125.4 1.3 shard_map.190
  126.7 3.1 %collective-permute-start.21 = (bf16[32,2048]{1,0:T(8,128)(2,1)S(1)}, bf16[32,2048]{1,0:T(8,128)(2,1)S(1)}, u32[]{:S(2)}, u32[]{:S(2)}) collective-permute-start(bf16[32,2048]{1,0:T(8,128)(2,1)S(1)} %get-tuple-element.87), channel_id=1, source_target_pairs={{1,0},{2,1},{3,2},{0,3},{5,4},{6,5},{7,6},{4,7},{9,8},{10,9},{11,1... | collective-permute-start | bytes 393224 | tf_op jit(solution)/shard_map/ppermute | solution.py:96
  129.8 0.9 collective-permute-start.22
  131.0 1.3 shard_map.191
  132.2 3.6 %collective-permute-start.26 = (bf16[32,2048]{1,0:T(8,128)(2,1)S(1)}, bf16[32,2048]{1,0:T(8,128)(2,1)S(1)}, u32[]{:S(2)}, u32[]{:S(2)}) collective-permute-start(bf16[32,2048]{1,0:T(8,128)(2,1)S(1)} %get-tuple-element.91), channel_id=1, source_target_pairs={{1,0},{2,1},{3,2},{0,3},{5,4},{6,5},{7,6},{4,7},{9,8},{10,9},{11,1... | collective-permute-start | bytes 393224 | tf_op jit(solution)/shard_map/ppermute | solution.py:96
  136.1 5.1 %collective-permute-start.28 = (bf16[32,2048]{1,0:T(8,128)(2,1)S(1)}, bf16[32,2048]{1,0:T(8,128)(2,1)S(1)}, u32[]{:S(2)}, u32[]{:S(2)}) collective-permute-start(bf16[32,2048]{1,0:T(8,128)(2,1)S(1)} %get-tuple-element.93), channel_id=1, source_target_pairs={{3,0},{0,1},{1,2},{2,3},{7,4},{4,5},{5,6},{6,7},{11,8},{8,9},{9,10... | collective-permute-start | bytes 393224 | tf_op jit(solution)/shard_map/ppermute | solution.py:96
  141.2 7.9 %collective-permute-done.22 = bf16[32,2048]{1,0:T(8,128)(2,1)S(1)} collective-permute-done((bf16[32,2048]{1,0:T(8,128)(2,1)S(1)}, bf16[32,2048]{1,0:T(8,128)(2,1)S(1)}, u32[]{:S(2)}, u32[]{:S(2)}) %collective-permute-start.22) | collective-permute-done | bytes 131104 | tf_op jit(solution)/shard_map/ppermute | solution.py:96
  149.2 0.6 collective-permute-start.24
  149.7 4.1 %collective-permute-done.27 = bf16[32,2048]{1,0:T(8,128)(2,1)S(1)} collective-permute-done((bf16[32,2048]{1,0:T(8,128)(2,1)S(1)}, bf16[32,2048]{1,0:T(8,128)(2,1)S(1)}, u32[]{:S(2)}, u32[]{:S(2)}) %collective-permute-start.27) | collective-permute-done | bytes 131104 | tf_op jit(solution)/shard_map/ppermute | solution.py:96
  154.5 0.9 add_convert_fusion
  (63 shorter events, 3.3 us)
Async XLA Ops:
  0.0 18.8 %collective-permute-start = (bf16[32,4096]{1,0:T(8,128)(2,1)}, bf16[32,4096]{1,0:T(8,128)(2,1)S(1)}, u32[]{:S(2)}, u32[]{:S(2)}) collective-permute-start(bf16[32,4096]{1,0:T(8,128)(2,1)} %refs_10_.1), channel_id=1, source_target_pairs={{1,0},{2,1},{3,2},{0,3},{5,4},{6,5},{7,6},{4,7},{9,8},{10,9},{11,1... | collective-permute-start | bytes 786440 | tf_op jit(solution)/shard_map/ppermute | solution.py:96
  5.0 22.6 %collective-permute-start.1 = (bf16[32,4096]{1,0:T(8,128)(2,1)}, bf16[32,4096]{1,0:T(8,128)(2,1)}, u32[]{:S(2)}, u32[]{:S(2)}) collective-permute-start(bf16[32,4096]{1,0:T(8,128)(2,1)} %refs_10_.1), channel_id=1, source_target_pairs={{2,0},{3,1},{0,2},{1,3},{6,4},{7,5},{4,6},{5,7},{10,8},{11,9},{8,1... | collective-permute-start | bytes 786440 | tf_op jit(solution)/shard_map/ppermute | solution.py:96
  5.1 22.6 %collective-permute-start.2 = (bf16[32,4096]{1,0:T(8,128)(2,1)}, bf16[32,4096]{1,0:T(8,128)(2,1)}, u32[]{:S(2)}, u32[]{:S(2)}) collective-permute-start(bf16[32,4096]{1,0:T(8,128)(2,1)} %refs_10_.1), channel_id=1, source_target_pairs={{3,0},{0,1},{1,2},{2,3},{7,4},{4,5},{5,6},{6,7},{11,8},{8,9},{9,10... | collective-permute-start | bytes 786440 | tf_op jit(solution)/shard_map/ppermute | solution.py:96
  6.1 4.7 %copy-start.6 = (s32[1,4]{1,0:T(1,128)S(1)}, s32[1,4]{1,0:T(1,128)}, u32[]{:S(2)}) copy-start(s32[1,4]{1,0:T(1,128)} %param.20) | copy-start | bytes 52
  6.1 4.9 %copy-start.5 = (s32[1,4]{1,0:T(1,128)S(1)}, s32[1,4]{1,0:T(1,128)}, u32[]{:S(2)}) copy-start(s32[1,4]{1,0:T(1,128)} %param.21) | copy-start | bytes 52
  6.1 5.3 %copy-start.7 = (s32[8]{0:T(128)S(1)}, s32[8]{0:T(128)}, u32[]{:S(2)}) copy-start(s32[8]{0:T(128)} %param.22) | copy-start | bytes 100
  9.2 77.7 %collective-permute-start.11 = (bf16[384,4096]{1,0:T(8,128)(2,1)}, bf16[384,4096]{1,0:T(8,128)(2,1)S(1)}, u32[]{:S(2)}, u32[]{:S(2)}) collective-permute-start(bf16[384,4096]{1,0:T(8,128)(2,1)} %shard_map.183), channel_id=1, source_target_pairs={{0,8},{8,0},{1,9},{9,1},{2,10},{10,2},{3,11},{11,3},{4,12},{12,4},... | collective-permute-start | bytes 9437192 | tf_op jit(solution)/shard_map/ppermute | solution.py:92
  12.1 6.6 %copy-start.4 = (s32[128]{0:T(128)S(1)}, s32[128]{0:T(128)}, u32[]{:S(2)}) copy-start(s32[128]{0:T(128)} %and_select_fusion) | copy-start | bytes 1540
  27.7 10.5 %copy-start = (bf16[4096,192]{0,1:T(8,128)(2,1)S(1)}, bf16[4096,192]{0,1:T(8,128)(2,1)}, u32[]{:S(2)}) copy-start(bf16[4096,192]{0,1:T(8,128)(2,1)} %param.37) | copy-start | bytes 4718596
  33.3 7.4 %collective-permute-start.3 = (bf16[32,4096]{1,0:T(8,128)(2,1)S(1)}, bf16[32,4096]{1,0:T(8,128)(2,1)S(1)}, u32[]{:S(2)}, u32[]{:S(2)}) collective-permute-start(bf16[32,4096]{1,0:T(8,128)(2,1)S(1)} %get-tuple-element.65), channel_id=1, source_target_pairs={{1,0},{2,1},{3,2},{0,3},{5,4},{6,5},{7,6},{4,7},{9,8},{10,9},{11,1... | collective-permute-start | bytes 786440 | tf_op jit(solution)/shard_map/ppermute | solution.py:96
  33.3 25.4 %collective-permute-start.4 = (bf16[32,4096]{1,0:T(8,128)(2,1)S(1)}, bf16[32,4096]{1,0:T(8,128)(2,1)S(1)}, u32[]{:S(2)}, u32[]{:S(2)}) collective-permute-start(bf16[32,4096]{1,0:T(8,128)(2,1)S(1)} %get-tuple-element.66), channel_id=1, source_target_pairs={{2,0},{3,1},{0,2},{1,3},{6,4},{7,5},{4,6},{5,7},{10,8},{11,9},{8,1... | collective-permute-start | bytes 786440 | tf_op jit(solution)/shard_map/ppermute | solution.py:96
  36.2 22.8 %copy-start.1 = (bf16[32,4096]{1,0:T(8,128)(2,1)S(1)}, bf16[32,4096]{1,0:T(8,128)(2,1)}, u32[]{:S(2)}) copy-start(bf16[32,4096]{1,0:T(8,128)(2,1)} %refs_10_.1) | copy-start | bytes 786436
  36.2 22.8 %copy-start.2 = (f32[4096]{0:T(1024)S(1)}, f32[4096]{0:T(1024)}, u32[]{:S(2)}) copy-start(f32[4096]{0:T(1024)} %param.33) | copy-start | bytes 49156
  36.2 22.5 %collective-permute-start.5 = (bf16[32,4096]{1,0:T(8,128)(2,1)S(1)}, bf16[32,4096]{1,0:T(8,128)(2,1)S(1)}, u32[]{:S(2)}, u32[]{:S(2)}) collective-permute-start(bf16[32,4096]{1,0:T(8,128)(2,1)S(1)} %get-tuple-element.67), channel_id=1, source_target_pairs={{3,0},{0,1},{1,2},{2,3},{7,4},{4,5},{5,6},{6,7},{11,8},{8,9},{9,10... | collective-permute-start | bytes 786440 | tf_op jit(solution)/shard_map/ppermute | solution.py:96
  38.3 20.6 %collective-permute-start.6 = (bf16[192,2048]{1,0:T(8,128)(2,1)S(1)}, bf16[192,2048]{1,0:T(8,128)(2,1)S(1)}, u32[]{:S(2)}, u32[]{:S(2)}) collective-permute-start(bf16[192,2048]{1,0:T(8,128)(2,1)S(1)} %get-tuple-element.100), channel_id=1, source_target_pairs={{0,16},{16,0},{1,17},{17,1},{2,18},{18,2},{3,19},{19,3},{4,20},{20... | collective-permute-start | bytes 2359304 | tf_op jit(solution)/shard_map/ppermute | solution.py:92
  59.2 6.9 %collective-permute-start.10 = (bf16[32,4096]{1,0:T(8,128)(2,1)S(1)}, bf16[32,4096]{1,0:T(8,128)(2,1)S(1)}, u32[]{:S(2)}, u32[]{:S(2)}) collective-permute-start(bf16[32,4096]{1,0:T(8,128)(2,1)S(1)} %add_convert_fusion.1), channel_id=1, source_target_pairs={{0,16},{16,0},{1,17},{17,1},{2,18},{18,2},{3,19},{19,3},{4,20},{20... | collective-permute-start | bytes 786440 | tf_op jit(solution)/shard_map/ppermute | solution.py:92
  60.7 7.3 %collective-permute-start.7 = (bf16[32,4096]{1,0:T(8,128)(2,1)S(1)}, bf16[32,4096]{1,0:T(8,128)(2,1)S(1)}, u32[]{:S(2)}, u32[]{:S(2)}) collective-permute-start(bf16[32,4096]{1,0:T(8,128)(2,1)S(1)} %add_convert_fusion.1), channel_id=1, source_target_pairs={{1,0},{2,1},{3,2},{0,3},{5,4},{6,5},{7,6},{4,7},{9,8},{10,9},{11,1... | collective-permute-start | bytes 786440 | tf_op jit(solution)/shard_map/ppermute | solution.py:96
  60.8 22.9 %collective-permute-start.8 = (bf16[32,4096]{1,0:T(8,128)(2,1)S(1)}, bf16[32,4096]{1,0:T(8,128)(2,1)S(1)}, u32[]{:S(2)}, u32[]{:S(2)}) collective-permute-start(bf16[32,4096]{1,0:T(8,128)(2,1)S(1)} %add_convert_fusion.1), channel_id=1, source_target_pairs={{2,0},{3,1},{0,2},{1,3},{6,4},{7,5},{4,6},{5,7},{10,8},{11,9},{8,1... | collective-permute-start | bytes 786440 | tf_op jit(solution)/shard_map/ppermute | solution.py:96
  60.8 22.9 %collective-permute-start.9 = (bf16[32,4096]{1,0:T(8,128)(2,1)S(1)}, bf16[32,4096]{1,0:T(8,128)(2,1)S(1)}, u32[]{:S(2)}, u32[]{:S(2)}) collective-permute-start(bf16[32,4096]{1,0:T(8,128)(2,1)S(1)} %add_convert_fusion.1), channel_id=1, source_target_pairs={{3,0},{0,1},{1,2},{2,3},{7,4},{4,5},{5,6},{6,7},{11,8},{8,9},{9,10... | collective-permute-start | bytes 786440 | tf_op jit(solution)/shard_map/ppermute | solution.py:96
  66.0 20.8 %collective-permute-start.12 = (bf16[96,2048]{1,0:T(8,128)(2,1)S(1)}, bf16[96,2048]{1,0:T(8,128)(2,1)S(1)}, u32[]{:S(2)}, u32[]{:S(2)}) collective-permute-start(bf16[96,2048]{1,0:T(8,128)(2,1)S(1)} %get-tuple-element.103), channel_id=1, source_target_pairs={{0,8},{8,0},{1,9},{9,1},{2,10},{10,2},{3,11},{11,3},{4,12},{12,4},... | collective-permute-start | bytes 1179656 | tf_op jit(solution)/shard_map/ppermute | solution.py:92
  89.8 5.7 %collective-permute-start.14 = (bf16[384,4096]{1,0:T(8,128)(2,1)S(1)}, bf16[384,4096]{1,0:T(8,128)(2,1)S(1)}, u32[]{:S(2)}, u32[]{:S(2)}) collective-permute-start(bf16[384,4096]{1,0:T(8,128)(2,1)S(1)} %shard_map.184.gate_0), channel_id=1, source_target_pairs={{0,4},{4,0},{1,5},{5,1},{2,6},{6,2},{3,7},{7,3},{8,12},{12,8},{9,1... | collective-permute-start | bytes 9437192 | tf_op jit(solution)/shard_map/ppermute | solution.py:92
  89.9 10.1 %collective-permute-start.15 = (bf16[384,4096]{1,0:T(8,128)(2,1)S(1)}, bf16[384,4096]{1,0:T(8,128)(2,1)S(1)}, u32[]{:S(2)}, u32[]{:S(2)}) collective-permute-start(bf16[384,4096]{1,0:T(8,128)(2,1)S(1)} %shard_map.185.up_0), channel_id=1, source_target_pairs={{0,4},{4,0},{1,5},{5,1},{2,6},{6,2},{3,7},{7,3},{8,12},{12,8},{9,1... | collective-permute-start | bytes 9437192 | tf_op jit(solution)/shard_map/ppermute | solution.py:92
  90.4 19.5 %collective-permute-start.13 = (bf16[96,4096]{1,0:T(8,128)(2,1)S(1)}, bf16[96,4096]{1,0:T(8,128)(2,1)S(1)}, u32[]{:S(2)}, u32[]{:S(2)}) collective-permute-start(bf16[96,4096]{1,0:T(8,128)(2,1)S(1)} %pad_maximum_fusion.2), channel_id=1, source_target_pairs={{0,16},{16,0},{1,17},{17,1},{2,18},{18,2},{3,19},{19,3},{4,20},{20... | collective-permute-start | bytes 2359304 | tf_op jit(solution)/shard_map/ppermute | solution.py:92
  91.9 23.4 %collective-permute-start.18 = (bf16[96,2048]{1,0:T(8,128)(2,1)S(1)}, bf16[96,2048]{1,0:T(8,128)(2,1)S(1)}, u32[]{:S(2)}, u32[]{:S(2)}) collective-permute-start(bf16[96,2048]{1,0:T(8,128)(2,1)S(1)} %get-tuple-element.102), channel_id=1, source_target_pairs={{0,8},{8,0},{1,9},{9,1},{2,10},{10,2},{3,11},{11,3},{4,12},{12,4},... | collective-permute-start | bytes 1179656 | tf_op jit(solution)/shard_map/ppermute | solution.py:92
  93.4 26.2 %collective-permute-start.17 = (bf16[192,2048]{1,0:T(8,128)(2,1)S(1)}, bf16[192,2048]{1,0:T(8,128)(2,1)S(1)}, u32[]{:S(2)}, u32[]{:S(2)}) collective-permute-start(bf16[192,2048]{1,0:T(8,128)(2,1)S(1)} %collective-permute-done.6.refs_0_), channel_id=1, source_target_pairs={{0,8},{8,0},{1,9},{9,1},{2,10},{10,2},{3,11},{11,3},{4,12},{12,4},... | collective-permute-start | bytes 2359304 | tf_op jit(solution)/shard_map/ppermute | solution.py:92
  109.9 9.7 %collective-permute-start.16 = (bf16[128,768]{1,0:T(8,128)(2,1)S(1)}, bf16[128,768]{1,0:T(8,128)(2,1)S(1)}, u32[]{:S(2)}, u32[]{:S(2)}) collective-permute-start(bf16[128,768]{1,0:T(8,128)(2,1)S(1)} %shard_map.186.near), channel_id=1, source_target_pairs={{0,16},{16,0},{1,17},{17,1},{2,18},{18,2},{3,19},{19,3},{4,20},{20... | collective-permute-start | bytes 589832 | tf_op jit(solution)/shard_map/ppermute | solution.py:92
  119.7 3.5 %collective-permute-start.20 = (bf16[384,2048]{1,0:T(8,128)(2,1)S(1)}, bf16[384,2048]{1,0:T(8,128)(2,1)S(1)}, u32[]{:S(2)}, u32[]{:S(2)}) collective-permute-start(bf16[384,2048]{1,0:T(8,128)(2,1)S(1)} %shard_map.189.far_0), channel_id=1, source_target_pairs={{0,4},{4,0},{1,5},{5,1},{2,6},{6,2},{3,7},{7,3},{8,12},{12,8},{9,1... | collective-permute-start | bytes 4718600 | tf_op jit(solution)/shard_map/ppermute | solution.py:92
  120.2 5.2 %collective-permute-start.19 = (bf16[384,2048]{1,0:T(8,128)(2,1)S(1)}, bf16[384,2048]{1,0:T(8,128)(2,1)S(1)}, u32[]{:S(2)}, u32[]{:S(2)}) collective-permute-start(bf16[384,2048]{1,0:T(8,128)(2,1)S(1)} %shard_map.188.near_0), channel_id=1, source_target_pairs={{0,4},{4,0},{1,5},{5,1},{2,6},{6,2},{3,7},{7,3},{8,12},{12,8},{9,1... | collective-permute-start | bytes 4718600 | tf_op jit(solution)/shard_map/ppermute | solution.py:92
  120.8 10.2 %collective-permute-start.25 = (bf16[128,768]{1,0:T(8,128)(2,1)S(1)}, bf16[128,768]{1,0:T(8,128)(2,1)S(1)}, u32[]{:S(2)}, u32[]{:S(2)}) collective-permute-start(bf16[128,768]{1,0:T(8,128)(2,1)S(1)} %shard_map.187.near), channel_id=1, source_target_pairs={{0,16},{16,0},{1,17},{17,1},{2,18},{18,2},{3,19},{19,3},{4,20},{20... | collective-permute-start | bytes 589832 | tf_op jit(solution)/shard_map/ppermute | solution.py:92
  126.7 9.4 %collective-permute-start.21 = (bf16[32,2048]{1,0:T(8,128)(2,1)S(1)}, bf16[32,2048]{1,0:T(8,128)(2,1)S(1)}, u32[]{:S(2)}, u32[]{:S(2)}) collective-permute-start(bf16[32,2048]{1,0:T(8,128)(2,1)S(1)} %get-tuple-element.87), channel_id=1, source_target_pairs={{1,0},{2,1},{3,2},{0,3},{5,4},{6,5},{7,6},{4,7},{9,8},{10,9},{11,1... | collective-permute-start | bytes 393224 | tf_op jit(solution)/shard_map/ppermute | solution.py:96
  129.8 19.3 %collective-permute-start.22 = (bf16[32,2048]{1,0:T(8,128)(2,1)S(1)}, bf16[32,2048]{1,0:T(8,128)(2,1)S(1)}, u32[]{:S(2)}, u32[]{:S(2)}) collective-permute-start(bf16[32,2048]{1,0:T(8,128)(2,1)S(1)} %get-tuple-element.88), channel_id=1, source_target_pairs={{2,0},{3,1},{0,2},{1,3},{6,4},{7,5},{4,6},{5,7},{10,8},{11,9},{8,1... | collective-permute-start | bytes 393224 | tf_op jit(solution)/shard_map/ppermute | solution.py:96
  130.7 18.4 %collective-permute-start.23 = (bf16[32,2048]{1,0:T(8,128)(2,1)S(1)}, bf16[32,2048]{1,0:T(8,128)(2,1)S(1)}, u32[]{:S(2)}, u32[]{:S(2)}) collective-permute-start(bf16[32,2048]{1,0:T(8,128)(2,1)S(1)} %get-tuple-element.89), channel_id=1, source_target_pairs={{3,0},{0,1},{1,2},{2,3},{7,4},{4,5},{5,6},{6,7},{11,8},{8,9},{9,10... | collective-permute-start | bytes 393224 | tf_op jit(solution)/shard_map/ppermute | solution.py:96
  132.2 22.2 %copy-start.3 = (f32[4096]{0:T(1024)S(1)}, f32[4096]{0:T(1024)}, u32[]{:S(2)}) copy-start(f32[4096]{0:T(1024)} %param.34) | copy-start | bytes 49156
  132.2 17.5 %collective-permute-start.26 = (bf16[32,2048]{1,0:T(8,128)(2,1)S(1)}, bf16[32,2048]{1,0:T(8,128)(2,1)S(1)}, u32[]{:S(2)}, u32[]{:S(2)}) collective-permute-start(bf16[32,2048]{1,0:T(8,128)(2,1)S(1)} %get-tuple-element.91), channel_id=1, source_target_pairs={{1,0},{2,1},{3,2},{0,3},{5,4},{6,5},{7,6},{4,7},{9,8},{10,9},{11,1... | collective-permute-start | bytes 393224 | tf_op jit(solution)/shard_map/ppermute | solution.py:96
  135.8 18.0 %collective-permute-start.27 = (bf16[32,2048]{1,0:T(8,128)(2,1)S(1)}, bf16[32,2048]{1,0:T(8,128)(2,1)S(1)}, u32[]{:S(2)}, u32[]{:S(2)}) collective-permute-start(bf16[32,2048]{1,0:T(8,128)(2,1)S(1)} %get-tuple-element.92), channel_id=1, source_target_pairs={{2,0},{3,1},{0,2},{1,3},{6,4},{7,5},{4,6},{5,7},{10,8},{11,9},{8,1... | collective-permute-start | bytes 393224 | tf_op jit(solution)/shard_map/ppermute | solution.py:96
  136.1 17.8 %collective-permute-start.28 = (bf16[32,2048]{1,0:T(8,128)(2,1)S(1)}, bf16[32,2048]{1,0:T(8,128)(2,1)S(1)}, u32[]{:S(2)}, u32[]{:S(2)}) collective-permute-start(bf16[32,2048]{1,0:T(8,128)(2,1)S(1)} %get-tuple-element.93), channel_id=1, source_target_pairs={{3,0},{0,1},{1,2},{2,3},{7,4},{4,5},{5,6},{6,7},{11,8},{8,9},{9,10... | collective-permute-start | bytes 393224 | tf_op jit(solution)/shard_map/ppermute | solution.py:96
  149.2 5.0 %collective-permute-start.24 = (bf16[32,2048]{1,0:T(8,128)(2,1)S(1)}, bf16[32,2048]{1,0:T(8,128)(2,1)S(1)}, u32[]{:S(2)}, u32[]{:S(2)}) collective-permute-start(bf16[32,2048]{1,0:T(8,128)(2,1)S(1)} %add_convert_fusion.2), channel_id=1, source_target_pairs={{0,16},{16,0},{1,17},{17,1},{2,18},{18,2},{3,19},{19,3},{4,20},{20... | collective-permute-start | bytes 393224 | tf_op jit(solution)/shard_map/ppermute | solution.py:92

commit v16 on v15

--- a/solution.py
+++ b/solution.py
@@ -184,18 +184,25 @@
 
 def stacked(*arrays):
     rows, columns = arrays[0].shape
+    pieces = 3
+    part = rows // pieces
+    count = len(arrays) * pieces
 
     def kernel(*refs):
         sources, target, buffer, sems_in, sems_out = refs[:-4], *refs[-4:]
         into = [
-            pltpu.make_async_copy(source, buffer.at[k], sems_in.at[k])
-            for k, source in enumerate(sources)
+            pltpu.make_async_copy(
+                sources[k // pieces].at[pl.ds(k % pieces * part, part), :],
+                buffer.at[k],
+                sems_in.at[k],
+            )
+            for k in range(count)
         ]
         out = [
             pltpu.make_async_copy(
-                buffer.at[k], target.at[pl.ds(k * rows, rows), :], sems_out.at[k]
+                buffer.at[k], target.at[pl.ds(k * part, part), :], sems_out.at[k]
             )
-            for k in range(len(sources))
+            for k in range(count)
         ]
         for copy in into:
             copy.start()
@@ -205,14 +212,13 @@
         for copy in out:
             copy.wait()
 
-    count = len(arrays)
     return pl.pallas_call(
         kernel,
-        out_shape=pltpu.HBM((count * rows, columns), arrays[0].dtype),
-        in_specs=[pl.BlockSpec(memory_space=pl.ANY)] * count,
+        out_shape=pltpu.HBM((len(arrays) * rows, columns), arrays[0].dtype),
+        in_specs=[pl.BlockSpec(memory_space=pl.ANY)] * len(arrays),
         out_specs=pl.BlockSpec(memory_space=pltpu.HBM),
         scratch_shapes=[
-            pltpu.VMEM((count, rows, columns), arrays[0].dtype),
+            pltpu.VMEM((count, part, columns), arrays[0].dtype),
             pltpu.SemaphoreType.DMA((count,)),
             pltpu.SemaphoreType.DMA((count,)),
         ],
@@ -387,10 +393,10 @@
 
     line_other = exchange(line, "y")
     hidden_own = hidden_units_of(own, line)
-    line_other, hidden_own = together(line_other, hidden_own)
+    line_other, hidden_own, near_x[1] = together(line_other, hidden_own, near_x[1])
     from_own = exchange(hidden_own, "y")
     hidden_other = hidden_units_of(other, line_other)
-    hidden_other, from_own, far_x, near_x[1] = together(hidden_other, from_own, far_x, near_x[1])
+    hidden_other, from_own, far_x = together(hidden_other, from_own, far_x)
     from_other = exchange(hidden_other, "y")
     down_halves = [*both_halves(near, *near_x), *both_halves(far, far_x)]
 

time: 156 us -> 153 us (0.981)
  waiting for transfers between devices: 83 us -> 81.2 us
    ppermute x14, waiting for transfers between devices: 27.1 us -> 25 us  [exchange(): return lax.ppermute(block, axis, [(0, 1), (1, 0)])]
where the time goes in v16:
time: 153 us
  waiting for transfers between devices  81.2 us (53%)
  starting transfers between devices  39.3 us (26%)
  Pallas kernels  28.5 us (19%)
  other arithmetic  3.28 us (2%)
    ppermute x15, waiting for transfers between devices, shift(): return lax.ppermute(block, 'mlp', [((k + hops) % 4, k) for k in range(4)])  56.2 us
    ppermute x15, starting transfers between devices, shift(): return lax.ppermute(block, 'mlp', [((k + hops) % 4, k) for k in range(4)])  26.2 us
    ppermute x14, waiting for transfers between devices, exchange(): return lax.ppermute(block, axis, [(0, 1), (1, 0)])  25 us
    pallas_call x5, Pallas kernels, vmem_call(): pl.pallas_call(kernel, out_shape=outs, in_specs=[whole] * len(operands),...  15.7 us
    ppermute x14, starting transfers between devices, exchange(): return lax.ppermute(block, axis, [(0, 1), (1, 0)])  13.1 us
    pallas_call x5, Pallas kernels, staged(): pl.pallas_call(kernel, out_shape=[pltpu.VMEM(shape, group[0][0].dtype) fo...  10 us
  transfers between devices with their start and end apart: 29, of which 16 were waited for; matrix products, arithmetic and copies ran while one was open for 2% of the time, Pallas kernels for 17%

profile of v16, /device:TPU:0, one launch (start us, length us, event | category | flops | bytes accessed | tf_op | source)
XLA Modules:
  0.0 152.7 jit_solution(3772407228500196665)
XLA Ops:
  0.0 5.0 %collective-permute-start = (bf16[32,4096]{1,0:T(8,128)(2,1)}, bf16[32,4096]{1,0:T(8,128)(2,1)S(1)}, u32[]{:S(2)}, u32[]{:S(2)}) collective-permute-start(bf16[32,4096]{1,0:T(8,128)(2,1)} %refs_10_.1), channel_id=1, source_target_pairs={{1,0},{2,1},{3,2},{0,3},{5,4},{6,5},{7,6},{4,7},{9,8},{10,9},{11,1... | collective-permute-start | bytes 786440 | tf_op jit(solution)/shard_map/ppermute | solution.py:96
  5.1 1.0 collective-permute-start.2
  6.1 2.8 %shard_map.183 = bf16[384,4096]{1,0:T(8,128)(2,1)} custom-call(bf16[192,4096]{1,0:T(8,128)(2,1)} %bitcast.14, bf16[192,4096]{1,0:T(8,128)(2,1)} %bitcast.16), custom_call_target="tpu_custom_call" | custom-call | bytes 1048576 | tf_op jit(solution)/shard_map/pallas_call | solution.py:215
  8.9 1.6 %collective-permute-start.11 = (bf16[384,4096]{1,0:T(8,128)(2,1)}, bf16[384,4096]{1,0:T(8,128)(2,1)S(1)}, u32[]{:S(2)}, u32[]{:S(2)}) collective-permute-start(bf16[384,4096]{1,0:T(8,128)(2,1)} %shard_map.183), channel_id=1, source_target_pairs={{0,8},{8,0},{1,9},{9,1},{2,10},{10,2},{3,11},{11,3},{4,12},{12,4},... | collective-permute-start | bytes 9437192 | tf_op jit(solution)/shard_map/ppermute | solution.py:92
  10.8 0.3 fusion.4
  11.3 0.5 and_select_fusion
  11.8 6.6 %shard_map.181 = (bf16[4096,512]{1,0:T(8,128)(2,1)S(1)}, bf16[4096,512]{1,0:T(8,128)(2,1)S(1)}, bf16[4096,512]{1,0:T(8,128)(2,1)S(1)}, bf16[512,4096]{1,0:T(8,12...) custom-call(bf16[4096,512]{1,0:T(8,128)(2,1)} %refs_0_.1, ...), custom_call_target="tpu_custom_call" | custom-call | tf_op jit(solution)/shard_map/pallas_call | solution.py:174
  18.6 9.1 %collective-permute-done.1.block_2 = bf16[32,4096]{1,0:T(8,128)(2,1)} collective-permute-done((bf16[32,4096]{1,0:T(8,128)(2,1)}, bf16[32,4096]{1,0:T(8,128)(2,1)}, u32[]{:S(2)}, u32[]{:S(2)}) %collective-permute-start.1) | collective-permute-done | bytes 262176 | tf_op jit(solution)/shard_map/ppermute | solution.py:96
  27.7 5.6 %shard_map.182 = (bf16[32,4096]{1,0:T(8,128)(2,1)S(1)}, bf16[32,4096]{1,0:T(8,128)(2,1)S(1)}, bf16[32,4096]{1,0:T(8,128)(2,1)S(1)}, bf16[32,4096]{1,0:T(8,128)(2,1)S(1)}) custom-call(bf16[32,4096]{1,0:T(8,128)(2,1)S(1)} %get-tuple-element.51.block_0, bf16[32,4096]{1,0:T(8,128)(2,1)S(1)} %collective-permute-done.block_1, ...), custom_call_target="tpu_custom_call" | custom-call | flops 1048576 | bytes 1048576 | tf_op jit(solution)/shard_map/pallas_call | solution.py:124
  33.3 2.9 %collective-permute-start.4 = (bf16[32,4096]{1,0:T(8,128)(2,1)S(1)}, bf16[32,4096]{1,0:T(8,128)(2,1)S(1)}, u32[]{:S(2)}, u32[]{:S(2)}) collective-permute-start(bf16[32,4096]{1,0:T(8,128)(2,1)S(1)} %get-tuple-element.66), channel_id=1, source_target_pairs={{2,0},{3,1},{0,2},{1,3},{6,4},{7,5},{4,6},{5,7},{10,8},{11,9},{8,1... | collective-permute-start | bytes 786440 | tf_op jit(solution)/shard_map/ppermute | solution.py:96
  36.2 1.9 %collective-permute-start.5 = (bf16[32,4096]{1,0:T(8,128)(2,1)S(1)}, bf16[32,4096]{1,0:T(8,128)(2,1)S(1)}, u32[]{:S(2)}, u32[]{:S(2)}) collective-permute-start(bf16[32,4096]{1,0:T(8,128)(2,1)S(1)} %get-tuple-element.67), channel_id=1, source_target_pairs={{3,0},{0,1},{1,2},{2,3},{7,4},{4,5},{5,6},{6,7},{11,8},{8,9},{9,10... | collective-permute-start | bytes 786440 | tf_op jit(solution)/shard_map/ppermute | solution.py:96
  38.3 1.6 %collective-permute-start.6 = (bf16[192,2048]{1,0:T(8,128)(2,1)S(1)}, bf16[192,2048]{1,0:T(8,128)(2,1)S(1)}, u32[]{:S(2)}, u32[]{:S(2)}) collective-permute-start(bf16[192,2048]{1,0:T(8,128)(2,1)S(1)} %get-tuple-element.100), channel_id=1, source_target_pairs={{0,16},{16,0},{1,17},{17,1},{2,18},{18,2},{3,19},{19,3},{4,20},{20... | collective-permute-start | bytes 2359304 | tf_op jit(solution)/shard_map/ppermute | solution.py:92
  39.9 0.8 collective-permute-done.3
  40.7 18.0 %collective-permute-done.4 = bf16[32,4096]{1,0:T(8,128)(2,1)S(1)} collective-permute-done((bf16[32,4096]{1,0:T(8,128)(2,1)S(1)}, bf16[32,4096]{1,0:T(8,128)(2,1)S(1)}, u32[]{:S(2)}, u32[]{:S(2)}) %collective-permute-start.4) | collective-permute-done | bytes 262176 | tf_op jit(solution)/shard_map/ppermute | solution.py:96
  59.2 1.6 %collective-permute-start.10 = (bf16[32,4096]{1,0:T(8,128)(2,1)S(1)}, bf16[32,4096]{1,0:T(8,128)(2,1)S(1)}, u32[]{:S(2)}, u32[]{:S(2)}) collective-permute-start(bf16[32,4096]{1,0:T(8,128)(2,1)S(1)} %add_convert_fusion.1), channel_id=1, source_target_pairs={{0,16},{16,0},{1,17},{17,1},{2,18},{18,2},{3,19},{19,3},{4,20},{20... | collective-permute-start | bytes 786440 | tf_op jit(solution)/shard_map/ppermute | solution.py:92
  60.8 2.0 %collective-permute-start.9 = (bf16[32,4096]{1,0:T(8,128)(2,1)S(1)}, bf16[32,4096]{1,0:T(8,128)(2,1)S(1)}, u32[]{:S(2)}, u32[]{:S(2)}) collective-permute-start(bf16[32,4096]{1,0:T(8,128)(2,1)S(1)} %add_convert_fusion.1), channel_id=1, source_target_pairs={{3,0},{0,1},{1,2},{2,3},{7,4},{4,5},{5,6},{6,7},{11,8},{8,9},{9,10... | collective-permute-start | bytes 786440 | tf_op jit(solution)/shard_map/ppermute | solution.py:96
  62.8 3.2 %collective-permute-done.10 = bf16[32,4096]{1,0:T(8,128)(2,1)S(1)} collective-permute-done((bf16[32,4096]{1,0:T(8,128)(2,1)S(1)}, bf16[32,4096]{1,0:T(8,128)(2,1)S(1)}, u32[]{:S(2)}, u32[]{:S(2)}) %collective-permute-start.10) | collective-permute-done | bytes 262176 | tf_op jit(solution)/shard_map/ppermute | solution.py:92
  66.0 1.5 collective-permute-start.12
  67.5 0.5 collective-permute-done.7
  68.0 15.7 %collective-permute-done.8 = bf16[32,4096]{1,0:T(8,128)(2,1)S(1)} collective-permute-done((bf16[32,4096]{1,0:T(8,128)(2,1)S(1)}, bf16[32,4096]{1,0:T(8,128)(2,1)S(1)}, u32[]{:S(2)}, u32[]{:S(2)}) %collective-permute-start.8) | collective-permute-done | bytes 262176 | tf_op jit(solution)/shard_map/ppermute | solution.py:96
  83.7 2.9 %collective-permute-done.12.refs_1_ = bf16[96,2048]{1,0:T(8,128)(2,1)S(1)} collective-permute-done((bf16[96,2048]{1,0:T(8,128)(2,1)S(1)}, bf16[96,2048]{1,0:T(8,128)(2,1)S(1)}, u32[]{:S(2)}, u32[]{:S(2)}) %collective-permute-start.12) | collective-permute-done | bytes 393248 | tf_op jit(solution)/shard_map/ppermute | solution.py:92
  86.6 1.4 shard_map.184.gate_0
  88.0 1.4 shard_map.185.up_0
  89.6 0.5 collective-permute-start.15
  90.1 1.5 collective-permute-start.13
  91.6 1.5 collective-permute-start.16
  93.1 0.5 collective-permute-start.18
  93.7 1.5 collective-permute-done.14.gate_1
  95.2 4.5 %collective-permute-done.15.up_1 = bf16[384,4096]{1,0:T(8,128)(2,1)S(1)} collective-permute-done((bf16[384,4096]{1,0:T(8,128)(2,1)S(1)}, bf16[384,4096]{1,0:T(8,128)(2,1)S(1)}, u32[]{:S(2)}, u32[]{:S(2)}) %collective-permute-start.15) | collective-permute-done | bytes 3145760 | tf_op jit(solution)/shard_map/ppermute | solution.py:92
  99.7 3.8 %shard_map.186.near = bf16[128,768]{1,0:T(8,128)(2,1)S(1)} custom-call(bf16[128,4096]{1,0:T(8,128)(2,1)S(1)} %pad_maximum_fusion.states, bf16[384,4096]{1,0:T(8,128)(2,1)S(1)} %shard_map.184.gate_0, bf16[384,4096]{1,0:T(8,128)(2,1)S(1)} %collective-permute-done.14.gate_1, bf16[384,4096]{1,0:T(8,128)(2,1)S(1)} %shard_map.185.up_0, ...), custom_call_target="tpu_custom_call" | custom-call | flops 1048576 | bytes 1048576 | tf_op jit(solution)/shard_map/pallas_call | solution.py:124
  103.6 6.0 %collective-permute-done.13 = bf16[96,4096]{1,0:T(8,128)(2,1)S(1)} collective-permute-done((bf16[96,4096]{1,0:T(8,128)(2,1)S(1)}, bf16[96,4096]{1,0:T(8,128)(2,1)S(1)}, u32[]{:S(2)}, u32[]{:S(2)}) %collective-permute-start.13) | collective-permute-done | bytes 786464 | tf_op jit(solution)/shard_map/ppermute | solution.py:92
  109.6 1.5 collective-permute-start.17
  111.1 0.5 shard_map.188.near_0
  111.7 3.8 %shard_map.187.near = bf16[128,768]{1,0:T(8,128)(2,1)S(1)} custom-call(bf16[128,4096]{1,0:T(8,128)(2,1)S(1)} %pad_maximum_fusion.1.states, bf16[384,4096]{1,0:T(8,128)(2,1)S(1)} %shard_map.184.gate_0, bf16[384,4096]{1,0:T(8,128)(2,1)S(1)} %collective-permute-done.14.gate_1, bf16[384,4096]{1,0:T(8,128)(2,1)S(1)} %shard_map.185.up_0, ...), custom_call_target="tpu_custom_call" | custom-call | flops 1048576 | bytes 1048576 | tf_op jit(solution)/shard_map/pallas_call | solution.py:124
  115.5 3.7 %collective-permute-done.18.refs_1_ = bf16[192,2048]{1,0:T(8,128)(2,1)S(1)} collective-permute-done((bf16[192,2048]{1,0:T(8,128)(2,1)S(1)}, bf16[192,2048]{1,0:T(8,128)(2,1)S(1)}, u32[]{:S(2)}, u32[]{:S(2)}) %collective-permute-start.18) | collective-permute-done | bytes 786464 | tf_op jit(solution)/shard_map/ppermute | solution.py:92
  119.5 0.6 collective-permute-start.25
  120.0 2.8 %collective-permute-done.20.far_1 = bf16[384,2048]{1,0:T(8,128)(2,1)S(1)} collective-permute-done((bf16[384,2048]{1,0:T(8,128)(2,1)S(1)}, bf16[384,2048]{1,0:T(8,128)(2,1)S(1)}, u32[]{:S(2)}, u32[]{:S(2)}) %collective-permute-start.20) | collective-permute-done | bytes 1572896 | tf_op jit(solution)/shard_map/ppermute | solution.py:92
  122.9 1.3 shard_map.190
  124.1 3.1 %collective-permute-start.21 = (bf16[32,2048]{1,0:T(8,128)(2,1)S(1)}, bf16[32,2048]{1,0:T(8,128)(2,1)S(1)}, u32[]{:S(2)}, u32[]{:S(2)}) collective-permute-start(bf16[32,2048]{1,0:T(8,128)(2,1)S(1)} %get-tuple-element.87), channel_id=1, source_target_pairs={{1,0},{2,1},{3,2},{0,3},{5,4},{6,5},{7,6},{4,7},{9,8},{10,9},{11,1... | collective-permute-start | bytes 393224 | tf_op jit(solution)/shard_map/ppermute | solution.py:96
  127.3 0.8 collective-permute-start.22
  128.1 0.3 collective-permute-start.23
  128.4 1.2 shard_map.191
  129.7 3.6 %collective-permute-start.26 = (bf16[32,2048]{1,0:T(8,128)(2,1)S(1)}, bf16[32,2048]{1,0:T(8,128)(2,1)S(1)}, u32[]{:S(2)}, u32[]{:S(2)}) collective-permute-start(bf16[32,2048]{1,0:T(8,128)(2,1)S(1)} %get-tuple-element.91), channel_id=1, source_target_pairs={{1,0},{2,1},{3,2},{0,3},{5,4},{6,5},{7,6},{4,7},{9,8},{10,9},{11,1... | collective-permute-start | bytes 393224 | tf_op jit(solution)/shard_map/ppermute | solution.py:96
  133.5 5.1 %collective-permute-start.28 = (bf16[32,2048]{1,0:T(8,128)(2,1)S(1)}, bf16[32,2048]{1,0:T(8,128)(2,1)S(1)}, u32[]{:S(2)}, u32[]{:S(2)}) collective-permute-start(bf16[32,2048]{1,0:T(8,128)(2,1)S(1)} %get-tuple-element.93), channel_id=1, source_target_pairs={{3,0},{0,1},{1,2},{2,3},{7,4},{4,5},{5,6},{6,7},{11,8},{8,9},{9,10... | collective-permute-start | bytes 393224 | tf_op jit(solution)/shard_map/ppermute | solution.py:96
  138.6 7.9 %collective-permute-done.22 = bf16[32,2048]{1,0:T(8,128)(2,1)S(1)} collective-permute-done((bf16[32,2048]{1,0:T(8,128)(2,1)S(1)}, bf16[32,2048]{1,0:T(8,128)(2,1)S(1)}, u32[]{:S(2)}, u32[]{:S(2)}) %collective-permute-start.22) | collective-permute-done | bytes 131104 | tf_op jit(solution)/shard_map/ppermute | solution.py:96
  146.6 0.6 collective-permute-start.24
  147.2 4.2 %collective-permute-done.27 = bf16[32,2048]{1,0:T(8,128)(2,1)S(1)} collective-permute-done((bf16[32,2048]{1,0:T(8,128)(2,1)S(1)}, bf16[32,2048]{1,0:T(8,128)(2,1)S(1)}, u32[]{:S(2)}, u32[]{:S(2)}) %collective-permute-start.27) | collective-permute-done | bytes 131104 | tf_op jit(solution)/shard_map/ppermute | solution.py:96
  151.9 0.9 add_convert_fusion
  (63 shorter events, 2.9 us)
Async XLA Ops:
  0.0 18.5 %collective-permute-start = (bf16[32,4096]{1,0:T(8,128)(2,1)}, bf16[32,4096]{1,0:T(8,128)(2,1)S(1)}, u32[]{:S(2)}, u32[]{:S(2)}) collective-permute-start(bf16[32,4096]{1,0:T(8,128)(2,1)} %refs_10_.1), channel_id=1, source_target_pairs={{1,0},{2,1},{3,2},{0,3},{5,4},{6,5},{7,6},{4,7},{9,8},{10,9},{11,1... | collective-permute-start | bytes 786440 | tf_op jit(solution)/shard_map/ppermute | solution.py:96
  5.0 22.6 %collective-permute-start.1 = (bf16[32,4096]{1,0:T(8,128)(2,1)}, bf16[32,4096]{1,0:T(8,128)(2,1)}, u32[]{:S(2)}, u32[]{:S(2)}) collective-permute-start(bf16[32,4096]{1,0:T(8,128)(2,1)} %refs_10_.1), channel_id=1, source_target_pairs={{2,0},{3,1},{0,2},{1,3},{6,4},{7,5},{4,6},{5,7},{10,8},{11,9},{8,1... | collective-permute-start | bytes 786440 | tf_op jit(solution)/shard_map/ppermute | solution.py:96
  5.1 22.6 %collective-permute-start.2 = (bf16[32,4096]{1,0:T(8,128)(2,1)}, bf16[32,4096]{1,0:T(8,128)(2,1)}, u32[]{:S(2)}, u32[]{:S(2)}) collective-permute-start(bf16[32,4096]{1,0:T(8,128)(2,1)} %refs_10_.1), channel_id=1, source_target_pairs={{3,0},{0,1},{1,2},{2,3},{7,4},{4,5},{5,6},{6,7},{11,8},{8,9},{9,10... | collective-permute-start | bytes 786440 | tf_op jit(solution)/shard_map/ppermute | solution.py:96
  6.1 4.4 %copy-start.6 = (s32[1,4]{1,0:T(1,128)S(1)}, s32[1,4]{1,0:T(1,128)}, u32[]{:S(2)}) copy-start(s32[1,4]{1,0:T(1,128)} %param.20) | copy-start | bytes 52
  6.1 4.6 %copy-start.5 = (s32[1,4]{1,0:T(1,128)S(1)}, s32[1,4]{1,0:T(1,128)}, u32[]{:S(2)}) copy-start(s32[1,4]{1,0:T(1,128)} %param.21) | copy-start | bytes 52
  6.1 5.0 %copy-start.7 = (s32[8]{0:T(128)S(1)}, s32[8]{0:T(128)}, u32[]{:S(2)}) copy-start(s32[8]{0:T(128)} %param.22) | copy-start | bytes 100
  8.9 77.7 %collective-permute-start.11 = (bf16[384,4096]{1,0:T(8,128)(2,1)}, bf16[384,4096]{1,0:T(8,128)(2,1)S(1)}, u32[]{:S(2)}, u32[]{:S(2)}) collective-permute-start(bf16[384,4096]{1,0:T(8,128)(2,1)} %shard_map.183), channel_id=1, source_target_pairs={{0,8},{8,0},{1,9},{9,1},{2,10},{10,2},{3,11},{11,3},{4,12},{12,4},... | collective-permute-start | bytes 9437192 | tf_op jit(solution)/shard_map/ppermute | solution.py:92
  11.8 6.6 %copy-start.4 = (s32[128]{0:T(128)S(1)}, s32[128]{0:T(128)}, u32[]{:S(2)}) copy-start(s32[128]{0:T(128)} %and_select_fusion) | copy-start | bytes 1540
  27.7 10.5 %copy-start = (bf16[4096,192]{0,1:T(8,128)(2,1)S(1)}, bf16[4096,192]{0,1:T(8,128)(2,1)}, u32[]{:S(2)}) copy-start(bf16[4096,192]{0,1:T(8,128)(2,1)} %param.37) | copy-start | bytes 4718596
  33.3 7.4 %collective-permute-start.3 = (bf16[32,4096]{1,0:T(8,128)(2,1)S(1)}, bf16[32,4096]{1,0:T(8,128)(2,1)S(1)}, u32[]{:S(2)}, u32[]{:S(2)}) collective-permute-start(bf16[32,4096]{1,0:T(8,128)(2,1)S(1)} %get-tuple-element.65), channel_id=1, source_target_pairs={{1,0},{2,1},{3,2},{0,3},{5,4},{6,5},{7,6},{4,7},{9,8},{10,9},{11,1... | collective-permute-start | bytes 786440 | tf_op jit(solution)/shard_map/ppermute | solution.py:96
  33.3 25.4 %collective-permute-start.4 = (bf16[32,4096]{1,0:T(8,128)(2,1)S(1)}, bf16[32,4096]{1,0:T(8,128)(2,1)S(1)}, u32[]{:S(2)}, u32[]{:S(2)}) collective-permute-start(bf16[32,4096]{1,0:T(8,128)(2,1)S(1)} %get-tuple-element.66), channel_id=1, source_target_pairs={{2,0},{3,1},{0,2},{1,3},{6,4},{7,5},{4,6},{5,7},{10,8},{11,9},{8,1... | collective-permute-start | bytes 786440 | tf_op jit(solution)/shard_map/ppermute | solution.py:96
  36.2 22.8 %copy-start.1 = (bf16[32,4096]{1,0:T(8,128)(2,1)S(1)}, bf16[32,4096]{1,0:T(8,128)(2,1)}, u32[]{:S(2)}) copy-start(bf16[32,4096]{1,0:T(8,128)(2,1)} %refs_10_.1) | copy-start | bytes 786436
  36.2 22.8 %copy-start.2 = (f32[4096]{0:T(1024)S(1)}, f32[4096]{0:T(1024)}, u32[]{:S(2)}) copy-start(f32[4096]{0:T(1024)} %param.33) | copy-start | bytes 49156
  36.2 22.5 %collective-permute-start.5 = (bf16[32,4096]{1,0:T(8,128)(2,1)S(1)}, bf16[32,4096]{1,0:T(8,128)(2,1)S(1)}, u32[]{:S(2)}, u32[]{:S(2)}) collective-permute-start(bf16[32,4096]{1,0:T(8,128)(2,1)S(1)} %get-tuple-element.67), channel_id=1, source_target_pairs={{3,0},{0,1},{1,2},{2,3},{7,4},{4,5},{5,6},{6,7},{11,8},{8,9},{9,10... | collective-permute-start | bytes 786440 | tf_op jit(solution)/shard_map/ppermute | solution.py:96
  38.3 20.6 %collective-permute-start.6 = (bf16[192,2048]{1,0:T(8,128)(2,1)S(1)}, bf16[192,2048]{1,0:T(8,128)(2,1)S(1)}, u32[]{:S(2)}, u32[]{:S(2)}) collective-permute-start(bf16[192,2048]{1,0:T(8,128)(2,1)S(1)} %get-tuple-element.100), channel_id=1, source_target_pairs={{0,16},{16,0},{1,17},{17,1},{2,18},{18,2},{3,19},{19,3},{4,20},{20... | collective-permute-start | bytes 2359304 | tf_op jit(solution)/shard_map/ppermute | solution.py:92
  59.2 6.9 %collective-permute-start.10 = (bf16[32,4096]{1,0:T(8,128)(2,1)S(1)}, bf16[32,4096]{1,0:T(8,128)(2,1)S(1)}, u32[]{:S(2)}, u32[]{:S(2)}) collective-permute-start(bf16[32,4096]{1,0:T(8,128)(2,1)S(1)} %add_convert_fusion.1), channel_id=1, source_target_pairs={{0,16},{16,0},{1,17},{17,1},{2,18},{18,2},{3,19},{19,3},{4,20},{20... | collective-permute-start | bytes 786440 | tf_op jit(solution)/shard_map/ppermute | solution.py:92
  60.7 7.3 %collective-permute-start.7 = (bf16[32,4096]{1,0:T(8,128)(2,1)S(1)}, bf16[32,4096]{1,0:T(8,128)(2,1)S(1)}, u32[]{:S(2)}, u32[]{:S(2)}) collective-permute-start(bf16[32,4096]{1,0:T(8,128)(2,1)S(1)} %add_convert_fusion.1), channel_id=1, source_target_pairs={{1,0},{2,1},{3,2},{0,3},{5,4},{6,5},{7,6},{4,7},{9,8},{10,9},{11,1... | collective-permute-start | bytes 786440 | tf_op jit(solution)/shard_map/ppermute | solution.py:96
  60.8 22.9 %collective-permute-start.8 = (bf16[32,4096]{1,0:T(8,128)(2,1)S(1)}, bf16[32,4096]{1,0:T(8,128)(2,1)S(1)}, u32[]{:S(2)}, u32[]{:S(2)}) collective-permute-start(bf16[32,4096]{1,0:T(8,128)(2,1)S(1)} %add_convert_fusion.1), channel_id=1, source_target_pairs={{2,0},{3,1},{0,2},{1,3},{6,4},{7,5},{4,6},{5,7},{10,8},{11,9},{8,1... | collective-permute-start | bytes 786440 | tf_op jit(solution)/shard_map/ppermute | solution.py:96
  60.8 22.9 %collective-permute-start.9 = (bf16[32,4096]{1,0:T(8,128)(2,1)S(1)}, bf16[32,4096]{1,0:T(8,128)(2,1)S(1)}, u32[]{:S(2)}, u32[]{:S(2)}) collective-permute-start(bf16[32,4096]{1,0:T(8,128)(2,1)S(1)} %add_convert_fusion.1), channel_id=1, source_target_pairs={{3,0},{0,1},{1,2},{2,3},{7,4},{4,5},{5,6},{6,7},{11,8},{8,9},{9,10... | collective-permute-start | bytes 786440 | tf_op jit(solution)/shard_map/ppermute | solution.py:96
  66.0 20.6 %collective-permute-start.12 = (bf16[96,2048]{1,0:T(8,128)(2,1)S(1)}, bf16[96,2048]{1,0:T(8,128)(2,1)S(1)}, u32[]{:S(2)}, u32[]{:S(2)}) collective-permute-start(bf16[96,2048]{1,0:T(8,128)(2,1)S(1)} %get-tuple-element.103), channel_id=1, source_target_pairs={{0,8},{8,0},{1,9},{9,1},{2,10},{10,2},{3,11},{11,3},{4,12},{12,4},... | collective-permute-start | bytes 1179656 | tf_op jit(solution)/shard_map/ppermute | solution.py:92
  89.5 5.7 %collective-permute-start.14 = (bf16[384,4096]{1,0:T(8,128)(2,1)S(1)}, bf16[384,4096]{1,0:T(8,128)(2,1)S(1)}, u32[]{:S(2)}, u32[]{:S(2)}) collective-permute-start(bf16[384,4096]{1,0:T(8,128)(2,1)S(1)} %shard_map.184.gate_0), channel_id=1, source_target_pairs={{0,4},{4,0},{1,5},{5,1},{2,6},{6,2},{3,7},{7,3},{8,12},{12,8},{9,1... | collective-permute-start | bytes 9437192 | tf_op jit(solution)/shard_map/ppermute | solution.py:92
  89.6 10.1 %collective-permute-start.15 = (bf16[384,4096]{1,0:T(8,128)(2,1)S(1)}, bf16[384,4096]{1,0:T(8,128)(2,1)S(1)}, u32[]{:S(2)}, u32[]{:S(2)}) collective-permute-start(bf16[384,4096]{1,0:T(8,128)(2,1)S(1)} %shard_map.185.up_0), channel_id=1, source_target_pairs={{0,4},{4,0},{1,5},{5,1},{2,6},{6,2},{3,7},{7,3},{8,12},{12,8},{9,1... | collective-permute-start | bytes 9437192 | tf_op jit(solution)/shard_map/ppermute | solution.py:92
  90.1 19.5 %collective-permute-start.13 = (bf16[96,4096]{1,0:T(8,128)(2,1)S(1)}, bf16[96,4096]{1,0:T(8,128)(2,1)S(1)}, u32[]{:S(2)}, u32[]{:S(2)}) collective-permute-start(bf16[96,4096]{1,0:T(8,128)(2,1)S(1)} %pad_maximum_fusion.2), channel_id=1, source_target_pairs={{0,16},{16,0},{1,17},{17,1},{2,18},{18,2},{3,19},{19,3},{4,20},{20... | collective-permute-start | bytes 2359304 | tf_op jit(solution)/shard_map/ppermute | solution.py:92
  91.6 12.0 %collective-permute-start.16 = (bf16[96,2048]{1,0:T(8,128)(2,1)S(1)}, bf16[96,2048]{1,0:T(8,128)(2,1)S(1)}, u32[]{:S(2)}, u32[]{:S(2)}) collective-permute-start(bf16[96,2048]{1,0:T(8,128)(2,1)S(1)} %get-tuple-element.102), channel_id=1, source_target_pairs={{0,8},{8,0},{1,9},{9,1},{2,10},{10,2},{3,11},{11,3},{4,12},{12,4},... | collective-permute-start | bytes 1179656 | tf_op jit(solution)/shard_map/ppermute | solution.py:92
  93.1 26.2 %collective-permute-start.18 = (bf16[192,2048]{1,0:T(8,128)(2,1)S(1)}, bf16[192,2048]{1,0:T(8,128)(2,1)S(1)}, u32[]{:S(2)}, u32[]{:S(2)}) collective-permute-start(bf16[192,2048]{1,0:T(8,128)(2,1)S(1)} %collective-permute-done.6.refs_0_), channel_id=1, source_target_pairs={{0,8},{8,0},{1,9},{9,1},{2,10},{10,2},{3,11},{11,3},{4,12},{12,4},... | collective-permute-start | bytes 2359304 | tf_op jit(solution)/shard_map/ppermute | solution.py:92
  109.6 9.7 %collective-permute-start.17 = (bf16[128,768]{1,0:T(8,128)(2,1)S(1)}, bf16[128,768]{1,0:T(8,128)(2,1)S(1)}, u32[]{:S(2)}, u32[]{:S(2)}) collective-permute-start(bf16[128,768]{1,0:T(8,128)(2,1)S(1)} %shard_map.186.near), channel_id=1, source_target_pairs={{0,16},{16,0},{1,17},{17,1},{2,18},{18,2},{3,19},{19,3},{4,20},{20... | collective-permute-start | bytes 589832 | tf_op jit(solution)/shard_map/ppermute | solution.py:92
  111.6 8.5 %collective-permute-start.19 = (bf16[384,2048]{1,0:T(8,128)(2,1)S(1)}, bf16[384,2048]{1,0:T(8,128)(2,1)S(1)}, u32[]{:S(2)}, u32[]{:S(2)}) collective-permute-start(bf16[384,2048]{1,0:T(8,128)(2,1)S(1)} %shard_map.188.near_0), channel_id=1, source_target_pairs={{0,4},{4,0},{1,5},{5,1},{2,6},{6,2},{3,7},{7,3},{8,12},{12,8},{9,1... | collective-permute-start | bytes 4718600 | tf_op jit(solution)/shard_map/ppermute | solution.py:92
  119.4 3.5 %collective-permute-start.20 = (bf16[384,2048]{1,0:T(8,128)(2,1)S(1)}, bf16[384,2048]{1,0:T(8,128)(2,1)S(1)}, u32[]{:S(2)}, u32[]{:S(2)}) collective-permute-start(bf16[384,2048]{1,0:T(8,128)(2,1)S(1)} %shard_map.189.far_0), channel_id=1, source_target_pairs={{0,4},{4,0},{1,5},{5,1},{2,6},{6,2},{3,7},{7,3},{8,12},{12,8},{9,1... | collective-permute-start | bytes 4718600 | tf_op jit(solution)/shard_map/ppermute | solution.py:92
  119.5 8.9 %collective-permute-start.25 = (bf16[128,768]{1,0:T(8,128)(2,1)S(1)}, bf16[128,768]{1,0:T(8,128)(2,1)S(1)}, u32[]{:S(2)}, u32[]{:S(2)}) collective-permute-start(bf16[128,768]{1,0:T(8,128)(2,1)S(1)} %shard_map.187.near), channel_id=1, source_target_pairs={{0,16},{16,0},{1,17},{17,1},{2,18},{18,2},{3,19},{19,3},{4,20},{20... | collective-permute-start | bytes 589832 | tf_op jit(solution)/shard_map/ppermute | solution.py:92
  124.1 9.4 %collective-permute-start.21 = (bf16[32,2048]{1,0:T(8,128)(2,1)S(1)}, bf16[32,2048]{1,0:T(8,128)(2,1)S(1)}, u32[]{:S(2)}, u32[]{:S(2)}) collective-permute-start(bf16[32,2048]{1,0:T(8,128)(2,1)S(1)} %get-tuple-element.87), channel_id=1, source_target_pairs={{1,0},{2,1},{3,2},{0,3},{5,4},{6,5},{7,6},{4,7},{9,8},{10,9},{11,1... | collective-permute-start | bytes 393224 | tf_op jit(solution)/shard_map/ppermute | solution.py:96
  127.3 19.2 %collective-permute-start.22 = (bf16[32,2048]{1,0:T(8,128)(2,1)S(1)}, bf16[32,2048]{1,0:T(8,128)(2,1)S(1)}, u32[]{:S(2)}, u32[]{:S(2)}) collective-permute-start(bf16[32,2048]{1,0:T(8,128)(2,1)S(1)} %get-tuple-element.88), channel_id=1, source_target_pairs={{2,0},{3,1},{0,2},{1,3},{6,4},{7,5},{4,6},{5,7},{10,8},{11,9},{8,1... | collective-permute-start | bytes 393224 | tf_op jit(solution)/shard_map/ppermute | solution.py:96
  128.1 18.4 %collective-permute-start.23 = (bf16[32,2048]{1,0:T(8,128)(2,1)S(1)}, bf16[32,2048]{1,0:T(8,128)(2,1)S(1)}, u32[]{:S(2)}, u32[]{:S(2)}) collective-permute-start(bf16[32,2048]{1,0:T(8,128)(2,1)S(1)} %get-tuple-element.89), channel_id=1, source_target_pairs={{3,0},{0,1},{1,2},{2,3},{7,4},{4,5},{5,6},{6,7},{11,8},{8,9},{9,10... | collective-permute-start | bytes 393224 | tf_op jit(solution)/shard_map/ppermute | solution.py:96
  129.7 22.2 %copy-start.3 = (f32[4096]{0:T(1024)S(1)}, f32[4096]{0:T(1024)}, u32[]{:S(2)}) copy-start(f32[4096]{0:T(1024)} %param.34) | copy-start | bytes 49156
  129.7 17.5 %collective-permute-start.26 = (bf16[32,2048]{1,0:T(8,128)(2,1)S(1)}, bf16[32,2048]{1,0:T(8,128)(2,1)S(1)}, u32[]{:S(2)}, u32[]{:S(2)}) collective-permute-start(bf16[32,2048]{1,0:T(8,128)(2,1)S(1)} %get-tuple-element.91), channel_id=1, source_target_pairs={{1,0},{2,1},{3,2},{0,3},{5,4},{6,5},{7,6},{4,7},{9,8},{10,9},{11,1... | collective-permute-start | bytes 393224 | tf_op jit(solution)/shard_map/ppermute | solution.py:96
  133.3 18.1 %collective-permute-start.27 = (bf16[32,2048]{1,0:T(8,128)(2,1)S(1)}, bf16[32,2048]{1,0:T(8,128)(2,1)S(1)}, u32[]{:S(2)}, u32[]{:S(2)}) collective-permute-start(bf16[32,2048]{1,0:T(8,128)(2,1)S(1)} %get-tuple-element.92), channel_id=1, source_target_pairs={{2,0},{3,1},{0,2},{1,3},{6,4},{7,5},{4,6},{5,7},{10,8},{11,9},{8,1... | collective-permute-start | bytes 393224 | tf_op jit(solution)/shard_map/ppermute | solution.py:96
  133.5 17.8 %collective-permute-start.28 = (bf16[32,2048]{1,0:T(8,128)(2,1)S(1)}, bf16[32,2048]{1,0:T(8,128)(2,1)S(1)}, u32[]{:S(2)}, u32[]{:S(2)}) collective-permute-start(bf16[32,2048]{1,0:T(8,128)(2,1)S(1)} %get-tuple-element.93), channel_id=1, source_target_pairs={{3,0},{0,1},{1,2},{2,3},{7,4},{4,5},{5,6},{6,7},{11,8},{8,9},{9,10... | collective-permute-start | bytes 393224 | tf_op jit(solution)/shard_map/ppermute | solution.py:96
  146.6 5.0 %collective-permute-start.24 = (bf16[32,2048]{1,0:T(8,128)(2,1)S(1)}, bf16[32,2048]{1,0:T(8,128)(2,1)S(1)}, u32[]{:S(2)}, u32[]{:S(2)}) collective-permute-start(bf16[32,2048]{1,0:T(8,128)(2,1)S(1)} %add_convert_fusion.2), channel_id=1, source_target_pairs={{0,16},{16,0},{1,17},{17,1},{2,18},{18,2},{3,19},{19,3},{4,20},{20... | collective-permute-start | bytes 393224 | tf_op jit(solution)/shard_map/ppermute | solution.py:92

commit v17 on v16

--- a/solution.py
+++ b/solution.py
@@ -114,9 +114,13 @@
     return lax.optimization_barrier(values)
 
 
+def swapped(half):
+    return pltpu.with_memory_space_constraint(exchange(half, "core"), pltpu.VMEM)
+
+
 def both_halves(*rows):
     (half,) = staged(rows)
-    return half, pltpu.with_memory_space_constraint(exchange(half, "core"), pltpu.VMEM)
+    return half, swapped(half)
 
 
 def vmem_call(kernel, outs, scratch, operands, vmem_mib):
@@ -376,10 +380,10 @@
     own, *line, other = together(*line_gather(residual_own), exchange(residual_own, "y"))
     line, gate_up_x, near_x[0] = together(jnp.concatenate(line), gate_up_x, near_x[0])
     far_x = exchange(far, "x")
-    halves = [
-        *both_halves(in_hbm(gate_rows), (gate_up_x, 0, units)),
-        *both_halves(in_hbm(up_rows), (gate_up_x, units, units)),
-    ]
+    gate_half, up_half = staged(
+        [in_hbm(gate_rows), (gate_up_x, 0, units)], [in_hbm(up_rows), (gate_up_x, units, units)]
+    )
+    halves = [gate_half, swapped(gate_half), up_half, swapped(up_half)]
 
     def hidden_units_of(first, others):
         (hidden,) = vmem_call(

time: 153 us -> 152 us (level)
    pallas_call x5 -> x4, Pallas kernels: 10 us -> 9.1 us  [staged(): pl.pallas_call(kernel, out_shape=[pltpu.VMEM(shape, group[0][0].dtype) fo...]
where the time goes in v17:
time: 152 us
  waiting for transfers between devices  81.2 us (53%)
  starting transfers between devices  39.3 us (26%)
  Pallas kernels  27.6 us (18%)
  other arithmetic  3.28 us (2%)
    ppermute x15, waiting for transfers between devices, shift(): return lax.ppermute(block, 'mlp', [((k + hops) % 4, k) for k in range(4)])  56.2 us
    ppermute x15, starting transfers between devices, shift(): return lax.ppermute(block, 'mlp', [((k + hops) % 4, k) for k in range(4)])  26.2 us
    ppermute x14, waiting for transfers between devices, exchange(): return lax.ppermute(block, axis, [(0, 1), (1, 0)])  25 us
    pallas_call x5, Pallas kernels, vmem_call(): pl.pallas_call(kernel, out_shape=outs, in_specs=[whole] * len(operands),...  15.7 us
    ppermute x14, starting transfers between devices, exchange(): return lax.ppermute(block, axis, [(0, 1), (1, 0)])  13.1 us
    pallas_call x4, Pallas kernels, staged(): pl.pallas_call(kernel, out_shape=[pltpu.VMEM(shape, group[0][0].dtype) fo...  9.1 us
  transfers between devices with their start and end apart: 29, of which 16 were waited for; matrix products, arithmetic and copies ran while one was open for 2% of the time, Pallas kernels for 17%

profile of v17, /device:TPU:0, one launch (start us, length us, event | category | flops | bytes accessed | tf_op | source)
XLA Modules:
  0.0 151.8 jit_solution(13159212908145145502)
XLA Ops:
  0.0 5.0 %collective-permute-start = (bf16[32,4096]{1,0:T(8,128)(2,1)}, bf16[32,4096]{1,0:T(8,128)(2,1)S(1)}, u32[]{:S(2)}, u32[]{:S(2)}) collective-permute-start(bf16[32,4096]{1,0:T(8,128)(2,1)} %refs_10_.1), channel_id=1, source_target_pairs={{1,0},{2,1},{3,2},{0,3},{5,4},{6,5},{7,6},{4,7},{9,8},{10,9},{11,1... | collective-permute-start | bytes 786440 | tf_op jit(solution)/shard_map/ppermute | solution.py:96
  5.1 1.0 collective-permute-start.2
  6.1 2.8 %shard_map.183 = bf16[384,4096]{1,0:T(8,128)(2,1)} custom-call(bf16[192,4096]{1,0:T(8,128)(2,1)} %bitcast.14, bf16[192,4096]{1,0:T(8,128)(2,1)} %bitcast.16), custom_call_target="tpu_custom_call" | custom-call | bytes 1048576 | tf_op jit(solution)/shard_map/pallas_call | solution.py:219
  8.9 1.6 %collective-permute-start.11 = (bf16[384,4096]{1,0:T(8,128)(2,1)}, bf16[384,4096]{1,0:T(8,128)(2,1)S(1)}, u32[]{:S(2)}, u32[]{:S(2)}) collective-permute-start(bf16[384,4096]{1,0:T(8,128)(2,1)} %shard_map.183), channel_id=1, source_target_pairs={{0,8},{8,0},{1,9},{9,1},{2,10},{10,2},{3,11},{11,3},{4,12},{12,4},... | collective-permute-start | bytes 9437192 | tf_op jit(solution)/shard_map/ppermute | solution.py:92
  10.8 0.3 fusion.4
  11.3 0.5 and_select_fusion
  11.8 6.6 %shard_map.181 = (bf16[4096,512]{1,0:T(8,128)(2,1)S(1)}, bf16[4096,512]{1,0:T(8,128)(2,1)S(1)}, bf16[4096,512]{1,0:T(8,128)(2,1)S(1)}, bf16[512,4096]{1,0:T(8,12...) custom-call(bf16[4096,512]{1,0:T(8,128)(2,1)} %refs_0_.1, ...), custom_call_target="tpu_custom_call" | custom-call | tf_op jit(solution)/shard_map/pallas_call | solution.py:178
  18.5 9.1 %collective-permute-done.1.block_2 = bf16[32,4096]{1,0:T(8,128)(2,1)} collective-permute-done((bf16[32,4096]{1,0:T(8,128)(2,1)}, bf16[32,4096]{1,0:T(8,128)(2,1)}, u32[]{:S(2)}, u32[]{:S(2)}) %collective-permute-start.1) | collective-permute-done | bytes 262176 | tf_op jit(solution)/shard_map/ppermute | solution.py:96
  27.7 5.6 %shard_map.182 = (bf16[32,4096]{1,0:T(8,128)(2,1)S(1)}, bf16[32,4096]{1,0:T(8,128)(2,1)S(1)}, bf16[32,4096]{1,0:T(8,128)(2,1)S(1)}, bf16[32,4096]{1,0:T(8,128)(2,1)S(1)}) custom-call(bf16[32,4096]{1,0:T(8,128)(2,1)S(1)} %get-tuple-element.53.block_0, bf16[32,4096]{1,0:T(8,128)(2,1)S(1)} %collective-permute-done.block_1, ...), custom_call_target="tpu_custom_call" | custom-call | flops 1048576 | bytes 1048576 | tf_op jit(solution)/shard_map/pallas_call | solution.py:128
  33.3 2.9 %collective-permute-start.4 = (bf16[32,4096]{1,0:T(8,128)(2,1)S(1)}, bf16[32,4096]{1,0:T(8,128)(2,1)S(1)}, u32[]{:S(2)}, u32[]{:S(2)}) collective-permute-start(bf16[32,4096]{1,0:T(8,128)(2,1)S(1)} %get-tuple-element.68), channel_id=1, source_target_pairs={{2,0},{3,1},{0,2},{1,3},{6,4},{7,5},{4,6},{5,7},{10,8},{11,9},{8,1... | collective-permute-start | bytes 786440 | tf_op jit(solution)/shard_map/ppermute | solution.py:96
  36.2 1.9 %collective-permute-start.5 = (bf16[32,4096]{1,0:T(8,128)(2,1)S(1)}, bf16[32,4096]{1,0:T(8,128)(2,1)S(1)}, u32[]{:S(2)}, u32[]{:S(2)}) collective-permute-start(bf16[32,4096]{1,0:T(8,128)(2,1)S(1)} %get-tuple-element.69), channel_id=1, source_target_pairs={{3,0},{0,1},{1,2},{2,3},{7,4},{4,5},{5,6},{6,7},{11,8},{8,9},{9,10... | collective-permute-start | bytes 786440 | tf_op jit(solution)/shard_map/ppermute | solution.py:96
  38.3 1.6 %collective-permute-start.6 = (bf16[192,2048]{1,0:T(8,128)(2,1)S(1)}, bf16[192,2048]{1,0:T(8,128)(2,1)S(1)}, u32[]{:S(2)}, u32[]{:S(2)}) collective-permute-start(bf16[192,2048]{1,0:T(8,128)(2,1)S(1)} %get-tuple-element.104), channel_id=1, source_target_pairs={{0,16},{16,0},{1,17},{17,1},{2,18},{18,2},{3,19},{19,3},{4,20},{20... | collective-permute-start | bytes 2359304 | tf_op jit(solution)/shard_map/ppermute | solution.py:92
  39.9 0.8 collective-permute-done.3
  40.7 18.0 %collective-permute-done.4 = bf16[32,4096]{1,0:T(8,128)(2,1)S(1)} collective-permute-done((bf16[32,4096]{1,0:T(8,128)(2,1)S(1)}, bf16[32,4096]{1,0:T(8,128)(2,1)S(1)}, u32[]{:S(2)}, u32[]{:S(2)}) %collective-permute-start.4) | collective-permute-done | bytes 262176 | tf_op jit(solution)/shard_map/ppermute | solution.py:96
  59.2 1.6 %collective-permute-start.10 = (bf16[32,4096]{1,0:T(8,128)(2,1)S(1)}, bf16[32,4096]{1,0:T(8,128)(2,1)S(1)}, u32[]{:S(2)}, u32[]{:S(2)}) collective-permute-start(bf16[32,4096]{1,0:T(8,128)(2,1)S(1)} %add_convert_fusion.1), channel_id=1, source_target_pairs={{0,16},{16,0},{1,17},{17,1},{2,18},{18,2},{3,19},{19,3},{4,20},{20... | collective-permute-start | bytes 786440 | tf_op jit(solution)/shard_map/ppermute | solution.py:92
  60.8 2.0 %collective-permute-start.9 = (bf16[32,4096]{1,0:T(8,128)(2,1)S(1)}, bf16[32,4096]{1,0:T(8,128)(2,1)S(1)}, u32[]{:S(2)}, u32[]{:S(2)}) collective-permute-start(bf16[32,4096]{1,0:T(8,128)(2,1)S(1)} %add_convert_fusion.1), channel_id=1, source_target_pairs={{3,0},{0,1},{1,2},{2,3},{7,4},{4,5},{5,6},{6,7},{11,8},{8,9},{9,10... | collective-permute-start | bytes 786440 | tf_op jit(solution)/shard_map/ppermute | solution.py:96
  62.8 3.2 %collective-permute-done.10 = bf16[32,4096]{1,0:T(8,128)(2,1)S(1)} collective-permute-done((bf16[32,4096]{1,0:T(8,128)(2,1)S(1)}, bf16[32,4096]{1,0:T(8,128)(2,1)S(1)}, u32[]{:S(2)}, u32[]{:S(2)}) %collective-permute-start.10) | collective-permute-done | bytes 262176 | tf_op jit(solution)/shard_map/ppermute | solution.py:92
  66.0 1.5 collective-permute-start.12
  67.5 0.5 collective-permute-done.7
  68.0 15.7 %collective-permute-done.8 = bf16[32,4096]{1,0:T(8,128)(2,1)S(1)} collective-permute-done((bf16[32,4096]{1,0:T(8,128)(2,1)S(1)}, bf16[32,4096]{1,0:T(8,128)(2,1)S(1)}, u32[]{:S(2)}, u32[]{:S(2)}) %collective-permute-start.8) | collective-permute-done | bytes 262176 | tf_op jit(solution)/shard_map/ppermute | solution.py:96
  83.7 2.9 %collective-permute-done.12.refs_1_ = bf16[96,2048]{1,0:T(8,128)(2,1)S(1)} collective-permute-done((bf16[96,2048]{1,0:T(8,128)(2,1)S(1)}, bf16[96,2048]{1,0:T(8,128)(2,1)S(1)}, u32[]{:S(2)}, u32[]{:S(2)}) %collective-permute-start.12) | collective-permute-done | bytes 393248 | tf_op jit(solution)/shard_map/ppermute | solution.py:92
  86.6 1.9 %shard_map.184 = (bf16[384,4096]{1,0:T(8,128)(2,1)S(1)}, bf16[384,4096]{1,0:T(8,128)(2,1)S(1)}) custom-call(bf16[192,4096]{1,0:T(8,128)(2,1)} %bitcast.15, bf16[384,4096]{1,0:T(8,128)(2,1)S(1)} %collective-permute-done.11.refs_1_, bf16[192,4096]{1,0:T(8,128)(2,1)} %bitcast.17), custom_call_target="tpu_custom_call" | custom-call | bytes 12582912 | tf_op jit(solution)/shard_map/pallas_call | solution.py:178
  88.6 0.5 collective-permute-start.15
  89.1 1.5 %collective-permute-start.13 = (bf16[96,4096]{1,0:T(8,128)(2,1)S(1)}, bf16[96,4096]{1,0:T(8,128)(2,1)S(1)}, u32[]{:S(2)}, u32[]{:S(2)}) collective-permute-start(bf16[96,4096]{1,0:T(8,128)(2,1)S(1)} %pad_maximum_fusion.2), channel_id=1, source_target_pairs={{0,16},{16,0},{1,17},{17,1},{2,18},{18,2},{3,19},{19,3},{4,20},{20... | collective-permute-start | bytes 2359304 | tf_op jit(solution)/shard_map/ppermute | solution.py:92
  90.7 1.5 collective-permute-start.16
  92.1 0.5 collective-permute-start.18
  92.8 1.5 collective-permute-done.14.gate_1
  94.3 4.5 %collective-permute-done.15.up_1 = bf16[384,4096]{1,0:T(8,128)(2,1)S(1)} collective-permute-done((bf16[384,4096]{1,0:T(8,128)(2,1)S(1)}, bf16[384,4096]{1,0:T(8,128)(2,1)S(1)}, u32[]{:S(2)}, u32[]{:S(2)}) %collective-permute-start.15) | collective-permute-done | bytes 3145760 | tf_op jit(solution)/shard_map/ppermute | solution.py:92
  98.8 3.8 %shard_map.185.near = bf16[128,768]{1,0:T(8,128)(2,1)S(1)} custom-call(bf16[128,4096]{1,0:T(8,128)(2,1)S(1)} %pad_maximum_fusion.states, bf16[384,4096]{1,0:T(8,128)(2,1)S(1)} %get-tuple-element.81.gate_0, bf16[384,4096]{1,0:T(8,128)(2,1)S(1)} %collective-permute-done.14.gate_1, bf16[384,4096]{1,0:T(8,128)(2,1)S(1)} %get-tuple-element.82.up_0, ...), custom_call_target="tpu_custom_call" | custom-call | flops 1048576 | bytes 1048576 | tf_op jit(solution)/shard_map/pallas_call | solution.py:128
  102.7 6.0 %collective-permute-done.13 = bf16[96,4096]{1,0:T(8,128)(2,1)S(1)} collective-permute-done((bf16[96,4096]{1,0:T(8,128)(2,1)S(1)}, bf16[96,4096]{1,0:T(8,128)(2,1)S(1)}, u32[]{:S(2)}, u32[]{:S(2)}) %collective-permute-start.13) | collective-permute-done | bytes 786464 | tf_op jit(solution)/shard_map/ppermute | solution.py:92
  108.7 1.5 %collective-permute-start.17 = (bf16[128,768]{1,0:T(8,128)(2,1)S(1)}, bf16[128,768]{1,0:T(8,128)(2,1)S(1)}, u32[]{:S(2)}, u32[]{:S(2)}) collective-permute-start(bf16[128,768]{1,0:T(8,128)(2,1)S(1)} %shard_map.185.near), channel_id=1, source_target_pairs={{0,16},{16,0},{1,17},{17,1},{2,18},{18,2},{3,19},{19,3},{4,20},{20... | collective-permute-start | bytes 589832 | tf_op jit(solution)/shard_map/ppermute | solution.py:92
  110.2 0.5 shard_map.187.near_0
  110.8 3.8 %shard_map.186.near = bf16[128,768]{1,0:T(8,128)(2,1)S(1)} custom-call(bf16[128,4096]{1,0:T(8,128)(2,1)S(1)} %pad_maximum_fusion.1.states, bf16[384,4096]{1,0:T(8,128)(2,1)S(1)} %get-tuple-element.81.gate_0, bf16[384,4096]{1,0:T(8,128)(2,1)S(1)} %collective-permute-done.14.gate_1, bf16[384,4096]{1,0:T(8,128)(2,1)S(1)} %get-tuple-element.82.up_0, ...), custom_call_target="tpu_custom_call" | custom-call | flops 1048576 | bytes 1048576 | tf_op jit(solution)/shard_map/pallas_call | solution.py:128
  114.6 3.7 %collective-permute-done.18.refs_1_ = bf16[192,2048]{1,0:T(8,128)(2,1)S(1)} collective-permute-done((bf16[192,2048]{1,0:T(8,128)(2,1)S(1)}, bf16[192,2048]{1,0:T(8,128)(2,1)S(1)}, u32[]{:S(2)}, u32[]{:S(2)}) %collective-permute-start.18) | collective-permute-done | bytes 786464 | tf_op jit(solution)/shard_map/ppermute | solution.py:92
  118.5 0.6 collective-permute-start.25
  119.1 2.8 %collective-permute-done.20.far_1 = bf16[384,2048]{1,0:T(8,128)(2,1)S(1)} collective-permute-done((bf16[384,2048]{1,0:T(8,128)(2,1)S(1)}, bf16[384,2048]{1,0:T(8,128)(2,1)S(1)}, u32[]{:S(2)}, u32[]{:S(2)}) %collective-permute-start.20) | collective-permute-done | bytes 1572896 | tf_op jit(solution)/shard_map/ppermute | solution.py:92
  121.9 1.3 shard_map.189
  123.2 3.1 %collective-permute-start.21 = (bf16[32,2048]{1,0:T(8,128)(2,1)S(1)}, bf16[32,2048]{1,0:T(8,128)(2,1)S(1)}, u32[]{:S(2)}, u32[]{:S(2)}) collective-permute-start(bf16[32,2048]{1,0:T(8,128)(2,1)S(1)} %get-tuple-element.91), channel_id=1, source_target_pairs={{1,0},{2,1},{3,2},{0,3},{5,4},{6,5},{7,6},{4,7},{9,8},{10,9},{11,1... | collective-permute-start | bytes 393224 | tf_op jit(solution)/shard_map/ppermute | solution.py:96
  126.3 0.8 collective-permute-start.22
  127.2 0.3 collective-permute-start.23
  127.5 1.3 shard_map.190
  128.8 3.6 %collective-permute-start.26 = (bf16[32,2048]{1,0:T(8,128)(2,1)S(1)}, bf16[32,2048]{1,0:T(8,128)(2,1)S(1)}, u32[]{:S(2)}, u32[]{:S(2)}) collective-permute-start(bf16[32,2048]{1,0:T(8,128)(2,1)S(1)} %get-tuple-element.95), channel_id=1, source_target_pairs={{1,0},{2,1},{3,2},{0,3},{5,4},{6,5},{7,6},{4,7},{9,8},{10,9},{11,1... | collective-permute-start | bytes 393224 | tf_op jit(solution)/shard_map/ppermute | solution.py:96
  132.6 5.1 %collective-permute-start.28 = (bf16[32,2048]{1,0:T(8,128)(2,1)S(1)}, bf16[32,2048]{1,0:T(8,128)(2,1)S(1)}, u32[]{:S(2)}, u32[]{:S(2)}) collective-permute-start(bf16[32,2048]{1,0:T(8,128)(2,1)S(1)} %get-tuple-element.97), channel_id=1, source_target_pairs={{3,0},{0,1},{1,2},{2,3},{7,4},{4,5},{5,6},{6,7},{11,8},{8,9},{9,10... | collective-permute-start | bytes 393224 | tf_op jit(solution)/shard_map/ppermute | solution.py:96
  137.7 7.9 %collective-permute-done.22 = bf16[32,2048]{1,0:T(8,128)(2,1)S(1)} collective-permute-done((bf16[32,2048]{1,0:T(8,128)(2,1)S(1)}, bf16[32,2048]{1,0:T(8,128)(2,1)S(1)}, u32[]{:S(2)}, u32[]{:S(2)}) %collective-permute-start.22) | collective-permute-done | bytes 131104 | tf_op jit(solution)/shard_map/ppermute | solution.py:96
  145.7 0.6 collective-permute-start.24
  146.2 4.2 %collective-permute-done.27 = bf16[32,2048]{1,0:T(8,128)(2,1)S(1)} collective-permute-done((bf16[32,2048]{1,0:T(8,128)(2,1)S(1)}, bf16[32,2048]{1,0:T(8,128)(2,1)S(1)}, u32[]{:S(2)}, u32[]{:S(2)}) %collective-permute-start.27) | collective-permute-done | bytes 131104 | tf_op jit(solution)/shard_map/ppermute | solution.py:96
  150.4 0.3 collective-permute-done.24
  151.0 0.9 add_convert_fusion
  (62 shorter events, 2.6 us)
Async XLA Ops:
  0.0 18.5 %collective-permute-start = (bf16[32,4096]{1,0:T(8,128)(2,1)}, bf16[32,4096]{1,0:T(8,128)(2,1)S(1)}, u32[]{:S(2)}, u32[]{:S(2)}) collective-permute-start(bf16[32,4096]{1,0:T(8,128)(2,1)} %refs_10_.1), channel_id=1, source_target_pairs={{1,0},{2,1},{3,2},{0,3},{5,4},{6,5},{7,6},{4,7},{9,8},{10,9},{11,1... | collective-permute-start | bytes 786440 | tf_op jit(solution)/shard_map/ppermute | solution.py:96
  5.0 22.6 %collective-permute-start.1 = (bf16[32,4096]{1,0:T(8,128)(2,1)}, bf16[32,4096]{1,0:T(8,128)(2,1)}, u32[]{:S(2)}, u32[]{:S(2)}) collective-permute-start(bf16[32,4096]{1,0:T(8,128)(2,1)} %refs_10_.1), channel_id=1, source_target_pairs={{2,0},{3,1},{0,2},{1,3},{6,4},{7,5},{4,6},{5,7},{10,8},{11,9},{8,1... | collective-permute-start | bytes 786440 | tf_op jit(solution)/shard_map/ppermute | solution.py:96
  5.1 22.6 %collective-permute-start.2 = (bf16[32,4096]{1,0:T(8,128)(2,1)}, bf16[32,4096]{1,0:T(8,128)(2,1)}, u32[]{:S(2)}, u32[]{:S(2)}) collective-permute-start(bf16[32,4096]{1,0:T(8,128)(2,1)} %refs_10_.1), channel_id=1, source_target_pairs={{3,0},{0,1},{1,2},{2,3},{7,4},{4,5},{5,6},{6,7},{11,8},{8,9},{9,10... | collective-permute-start | bytes 786440 | tf_op jit(solution)/shard_map/ppermute | solution.py:96
  6.1 4.4 %copy-start.6 = (s32[1,4]{1,0:T(1,128)S(1)}, s32[1,4]{1,0:T(1,128)}, u32[]{:S(2)}) copy-start(s32[1,4]{1,0:T(1,128)} %param.20) | copy-start | bytes 52
  6.1 4.6 %copy-start.5 = (s32[1,4]{1,0:T(1,128)S(1)}, s32[1,4]{1,0:T(1,128)}, u32[]{:S(2)}) copy-start(s32[1,4]{1,0:T(1,128)} %param.21) | copy-start | bytes 52
  6.1 5.0 %copy-start.7 = (s32[8]{0:T(128)S(1)}, s32[8]{0:T(128)}, u32[]{:S(2)}) copy-start(s32[8]{0:T(128)} %param.22) | copy-start | bytes 100
  8.9 77.7 %collective-permute-start.11 = (bf16[384,4096]{1,0:T(8,128)(2,1)}, bf16[384,4096]{1,0:T(8,128)(2,1)S(1)}, u32[]{:S(2)}, u32[]{:S(2)}) collective-permute-start(bf16[384,4096]{1,0:T(8,128)(2,1)} %shard_map.183), channel_id=1, source_target_pairs={{0,8},{8,0},{1,9},{9,1},{2,10},{10,2},{3,11},{11,3},{4,12},{12,4},... | collective-permute-start | bytes 9437192 | tf_op jit(solution)/shard_map/ppermute | solution.py:92
  11.8 6.6 %copy-start.4 = (s32[128]{0:T(128)S(1)}, s32[128]{0:T(128)}, u32[]{:S(2)}) copy-start(s32[128]{0:T(128)} %and_select_fusion) | copy-start | bytes 1540
  27.7 10.5 %copy-start = (bf16[4096,192]{0,1:T(8,128)(2,1)S(1)}, bf16[4096,192]{0,1:T(8,128)(2,1)}, u32[]{:S(2)}) copy-start(bf16[4096,192]{0,1:T(8,128)(2,1)} %param.37) | copy-start | bytes 4718596
  33.3 7.4 %collective-permute-start.3 = (bf16[32,4096]{1,0:T(8,128)(2,1)S(1)}, bf16[32,4096]{1,0:T(8,128)(2,1)S(1)}, u32[]{:S(2)}, u32[]{:S(2)}) collective-permute-start(bf16[32,4096]{1,0:T(8,128)(2,1)S(1)} %get-tuple-element.67), channel_id=1, source_target_pairs={{1,0},{2,1},{3,2},{0,3},{5,4},{6,5},{7,6},{4,7},{9,8},{10,9},{11,1... | collective-permute-start | bytes 786440 | tf_op jit(solution)/shard_map/ppermute | solution.py:96
  33.3 25.4 %collective-permute-start.4 = (bf16[32,4096]{1,0:T(8,128)(2,1)S(1)}, bf16[32,4096]{1,0:T(8,128)(2,1)S(1)}, u32[]{:S(2)}, u32[]{:S(2)}) collective-permute-start(bf16[32,4096]{1,0:T(8,128)(2,1)S(1)} %get-tuple-element.68), channel_id=1, source_target_pairs={{2,0},{3,1},{0,2},{1,3},{6,4},{7,5},{4,6},{5,7},{10,8},{11,9},{8,1... | collective-permute-start | bytes 786440 | tf_op jit(solution)/shard_map/ppermute | solution.py:96
  36.2 22.8 %copy-start.1 = (bf16[32,4096]{1,0:T(8,128)(2,1)S(1)}, bf16[32,4096]{1,0:T(8,128)(2,1)}, u32[]{:S(2)}) copy-start(bf16[32,4096]{1,0:T(8,128)(2,1)} %refs_10_.1) | copy-start | bytes 786436
  36.2 22.8 %copy-start.2 = (f32[4096]{0:T(1024)S(1)}, f32[4096]{0:T(1024)}, u32[]{:S(2)}) copy-start(f32[4096]{0:T(1024)} %param.33) | copy-start | bytes 49156
  36.2 22.5 %collective-permute-start.5 = (bf16[32,4096]{1,0:T(8,128)(2,1)S(1)}, bf16[32,4096]{1,0:T(8,128)(2,1)S(1)}, u32[]{:S(2)}, u32[]{:S(2)}) collective-permute-start(bf16[32,4096]{1,0:T(8,128)(2,1)S(1)} %get-tuple-element.69), channel_id=1, source_target_pairs={{3,0},{0,1},{1,2},{2,3},{7,4},{4,5},{5,6},{6,7},{11,8},{8,9},{9,10... | collective-permute-start | bytes 786440 | tf_op jit(solution)/shard_map/ppermute | solution.py:96
  38.3 20.6 %collective-permute-start.6 = (bf16[192,2048]{1,0:T(8,128)(2,1)S(1)}, bf16[192,2048]{1,0:T(8,128)(2,1)S(1)}, u32[]{:S(2)}, u32[]{:S(2)}) collective-permute-start(bf16[192,2048]{1,0:T(8,128)(2,1)S(1)} %get-tuple-element.104), channel_id=1, source_target_pairs={{0,16},{16,0},{1,17},{17,1},{2,18},{18,2},{3,19},{19,3},{4,20},{20... | collective-permute-start | bytes 2359304 | tf_op jit(solution)/shard_map/ppermute | solution.py:92
  59.2 6.9 %collective-permute-start.10 = (bf16[32,4096]{1,0:T(8,128)(2,1)S(1)}, bf16[32,4096]{1,0:T(8,128)(2,1)S(1)}, u32[]{:S(2)}, u32[]{:S(2)}) collective-permute-start(bf16[32,4096]{1,0:T(8,128)(2,1)S(1)} %add_convert_fusion.1), channel_id=1, source_target_pairs={{0,16},{16,0},{1,17},{17,1},{2,18},{18,2},{3,19},{19,3},{4,20},{20... | collective-permute-start | bytes 786440 | tf_op jit(solution)/shard_map/ppermute | solution.py:92
  60.7 7.3 %collective-permute-start.7 = (bf16[32,4096]{1,0:T(8,128)(2,1)S(1)}, bf16[32,4096]{1,0:T(8,128)(2,1)S(1)}, u32[]{:S(2)}, u32[]{:S(2)}) collective-permute-start(bf16[32,4096]{1,0:T(8,128)(2,1)S(1)} %add_convert_fusion.1), channel_id=1, source_target_pairs={{1,0},{2,1},{3,2},{0,3},{5,4},{6,5},{7,6},{4,7},{9,8},{10,9},{11,1... | collective-permute-start | bytes 786440 | tf_op jit(solution)/shard_map/ppermute | solution.py:96
  60.8 22.9 %collective-permute-start.8 = (bf16[32,4096]{1,0:T(8,128)(2,1)S(1)}, bf16[32,4096]{1,0:T(8,128)(2,1)S(1)}, u32[]{:S(2)}, u32[]{:S(2)}) collective-permute-start(bf16[32,4096]{1,0:T(8,128)(2,1)S(1)} %add_convert_fusion.1), channel_id=1, source_target_pairs={{2,0},{3,1},{0,2},{1,3},{6,4},{7,5},{4,6},{5,7},{10,8},{11,9},{8,1... | collective-permute-start | bytes 786440 | tf_op jit(solution)/shard_map/ppermute | solution.py:96
  60.8 22.9 %collective-permute-start.9 = (bf16[32,4096]{1,0:T(8,128)(2,1)S(1)}, bf16[32,4096]{1,0:T(8,128)(2,1)S(1)}, u32[]{:S(2)}, u32[]{:S(2)}) collective-permute-start(bf16[32,4096]{1,0:T(8,128)(2,1)S(1)} %add_convert_fusion.1), channel_id=1, source_target_pairs={{3,0},{0,1},{1,2},{2,3},{7,4},{4,5},{5,6},{6,7},{11,8},{8,9},{9,10... | collective-permute-start | bytes 786440 | tf_op jit(solution)/shard_map/ppermute | solution.py:96
  66.0 20.5 %collective-permute-start.12 = (bf16[96,2048]{1,0:T(8,128)(2,1)S(1)}, bf16[96,2048]{1,0:T(8,128)(2,1)S(1)}, u32[]{:S(2)}, u32[]{:S(2)}) collective-permute-start(bf16[96,2048]{1,0:T(8,128)(2,1)S(1)} %get-tuple-element.107), channel_id=1, source_target_pairs={{0,8},{8,0},{1,9},{9,1},{2,10},{10,2},{3,11},{11,3},{4,12},{12,4},... | collective-permute-start | bytes 1179656 | tf_op jit(solution)/shard_map/ppermute | solution.py:92
  88.6 5.7 %collective-permute-start.14 = (bf16[384,4096]{1,0:T(8,128)(2,1)S(1)}, bf16[384,4096]{1,0:T(8,128)(2,1)S(1)}, u32[]{:S(2)}, u32[]{:S(2)}) collective-permute-start(bf16[384,4096]{1,0:T(8,128)(2,1)S(1)} %get-tuple-element.81.gate_0), channel_id=1, source_target_pairs={{0,4},{4,0},{1,5},{5,1},{2,6},{6,2},{3,7},{7,3},{8,12},{12,8},{9,1... | collective-permute-start | bytes 9437192 | tf_op jit(solution)/shard_map/ppermute | solution.py:92
  88.6 10.1 %collective-permute-start.15 = (bf16[384,4096]{1,0:T(8,128)(2,1)S(1)}, bf16[384,4096]{1,0:T(8,128)(2,1)S(1)}, u32[]{:S(2)}, u32[]{:S(2)}) collective-permute-start(bf16[384,4096]{1,0:T(8,128)(2,1)S(1)} %get-tuple-element.82.up_0), channel_id=1, source_target_pairs={{0,4},{4,0},{1,5},{5,1},{2,6},{6,2},{3,7},{7,3},{8,12},{12,8},{9,1... | collective-permute-start | bytes 9437192 | tf_op jit(solution)/shard_map/ppermute | solution.py:92
  89.1 19.5 %collective-permute-start.13 = (bf16[96,4096]{1,0:T(8,128)(2,1)S(1)}, bf16[96,4096]{1,0:T(8,128)(2,1)S(1)}, u32[]{:S(2)}, u32[]{:S(2)}) collective-permute-start(bf16[96,4096]{1,0:T(8,128)(2,1)S(1)} %pad_maximum_fusion.2), channel_id=1, source_target_pairs={{0,16},{16,0},{1,17},{17,1},{2,18},{18,2},{3,19},{19,3},{4,20},{20... | collective-permute-start | bytes 2359304 | tf_op jit(solution)/shard_map/ppermute | solution.py:92
  90.7 12.0 %collective-permute-start.16 = (bf16[96,2048]{1,0:T(8,128)(2,1)S(1)}, bf16[96,2048]{1,0:T(8,128)(2,1)S(1)}, u32[]{:S(2)}, u32[]{:S(2)}) collective-permute-start(bf16[96,2048]{1,0:T(8,128)(2,1)S(1)} %get-tuple-element.106), channel_id=1, source_target_pairs={{0,8},{8,0},{1,9},{9,1},{2,10},{10,2},{3,11},{11,3},{4,12},{12,4},... | collective-permute-start | bytes 1179656 | tf_op jit(solution)/shard_map/ppermute | solution.py:92
  92.1 26.2 %collective-permute-start.18 = (bf16[192,2048]{1,0:T(8,128)(2,1)S(1)}, bf16[192,2048]{1,0:T(8,128)(2,1)S(1)}, u32[]{:S(2)}, u32[]{:S(2)}) collective-permute-start(bf16[192,2048]{1,0:T(8,128)(2,1)S(1)} %collective-permute-done.6.refs_0_), channel_id=1, source_target_pairs={{0,8},{8,0},{1,9},{9,1},{2,10},{10,2},{3,11},{11,3},{4,12},{12,4},... | collective-permute-start | bytes 2359304 | tf_op jit(solution)/shard_map/ppermute | solution.py:92
  108.7 9.7 %collective-permute-start.17 = (bf16[128,768]{1,0:T(8,128)(2,1)S(1)}, bf16[128,768]{1,0:T(8,128)(2,1)S(1)}, u32[]{:S(2)}, u32[]{:S(2)}) collective-permute-start(bf16[128,768]{1,0:T(8,128)(2,1)S(1)} %shard_map.185.near), channel_id=1, source_target_pairs={{0,16},{16,0},{1,17},{17,1},{2,18},{18,2},{3,19},{19,3},{4,20},{20... | collective-permute-start | bytes 589832 | tf_op jit(solution)/shard_map/ppermute | solution.py:92
  110.6 8.5 %collective-permute-start.19 = (bf16[384,2048]{1,0:T(8,128)(2,1)S(1)}, bf16[384,2048]{1,0:T(8,128)(2,1)S(1)}, u32[]{:S(2)}, u32[]{:S(2)}) collective-permute-start(bf16[384,2048]{1,0:T(8,128)(2,1)S(1)} %shard_map.187.near_0), channel_id=1, source_target_pairs={{0,4},{4,0},{1,5},{5,1},{2,6},{6,2},{3,7},{7,3},{8,12},{12,8},{9,1... | collective-permute-start | bytes 4718600 | tf_op jit(solution)/shard_map/ppermute | solution.py:92
  118.5 3.5 %collective-permute-start.20 = (bf16[384,2048]{1,0:T(8,128)(2,1)S(1)}, bf16[384,2048]{1,0:T(8,128)(2,1)S(1)}, u32[]{:S(2)}, u32[]{:S(2)}) collective-permute-start(bf16[384,2048]{1,0:T(8,128)(2,1)S(1)} %shard_map.188.far_0), channel_id=1, source_target_pairs={{0,4},{4,0},{1,5},{5,1},{2,6},{6,2},{3,7},{7,3},{8,12},{12,8},{9,1... | collective-permute-start | bytes 4718600 | tf_op jit(solution)/shard_map/ppermute | solution.py:92
  118.5 9.0 %collective-permute-start.25 = (bf16[128,768]{1,0:T(8,128)(2,1)S(1)}, bf16[128,768]{1,0:T(8,128)(2,1)S(1)}, u32[]{:S(2)}, u32[]{:S(2)}) collective-permute-start(bf16[128,768]{1,0:T(8,128)(2,1)S(1)} %shard_map.186.near), channel_id=1, source_target_pairs={{0,16},{16,0},{1,17},{17,1},{2,18},{18,2},{3,19},{19,3},{4,20},{20... | collective-permute-start | bytes 589832 | tf_op jit(solution)/shard_map/ppermute | solution.py:92
  123.2 9.4 %collective-permute-start.21 = (bf16[32,2048]{1,0:T(8,128)(2,1)S(1)}, bf16[32,2048]{1,0:T(8,128)(2,1)S(1)}, u32[]{:S(2)}, u32[]{:S(2)}) collective-permute-start(bf16[32,2048]{1,0:T(8,128)(2,1)S(1)} %get-tuple-element.91), channel_id=1, source_target_pairs={{1,0},{2,1},{3,2},{0,3},{5,4},{6,5},{7,6},{4,7},{9,8},{10,9},{11,1... | collective-permute-start | bytes 393224 | tf_op jit(solution)/shard_map/ppermute | solution.py:96
  126.3 19.2 %collective-permute-start.22 = (bf16[32,2048]{1,0:T(8,128)(2,1)S(1)}, bf16[32,2048]{1,0:T(8,128)(2,1)S(1)}, u32[]{:S(2)}, u32[]{:S(2)}) collective-permute-start(bf16[32,2048]{1,0:T(8,128)(2,1)S(1)} %get-tuple-element.92), channel_id=1, source_target_pairs={{2,0},{3,1},{0,2},{1,3},{6,4},{7,5},{4,6},{5,7},{10,8},{11,9},{8,1... | collective-permute-start | bytes 393224 | tf_op jit(solution)/shard_map/ppermute | solution.py:96
  127.2 18.4 %collective-permute-start.23 = (bf16[32,2048]{1,0:T(8,128)(2,1)S(1)}, bf16[32,2048]{1,0:T(8,128)(2,1)S(1)}, u32[]{:S(2)}, u32[]{:S(2)}) collective-permute-start(bf16[32,2048]{1,0:T(8,128)(2,1)S(1)} %get-tuple-element.93), channel_id=1, source_target_pairs={{3,0},{0,1},{1,2},{2,3},{7,4},{4,5},{5,6},{6,7},{11,8},{8,9},{9,10... | collective-permute-start | bytes 393224 | tf_op jit(solution)/shard_map/ppermute | solution.py:96
  128.8 22.2 %copy-start.3 = (f32[4096]{0:T(1024)S(1)}, f32[4096]{0:T(1024)}, u32[]{:S(2)}) copy-start(f32[4096]{0:T(1024)} %param.34) | copy-start | bytes 49156
  128.8 17.5 %collective-permute-start.26 = (bf16[32,2048]{1,0:T(8,128)(2,1)S(1)}, bf16[32,2048]{1,0:T(8,128)(2,1)S(1)}, u32[]{:S(2)}, u32[]{:S(2)}) collective-permute-start(bf16[32,2048]{1,0:T(8,128)(2,1)S(1)} %get-tuple-element.95), channel_id=1, source_target_pairs={{1,0},{2,1},{3,2},{0,3},{5,4},{6,5},{7,6},{4,7},{9,8},{10,9},{11,1... | collective-permute-start | bytes 393224 | tf_op jit(solution)/shard_map/ppermute | solution.py:96
  132.3 18.1 %collective-permute-start.27 = (bf16[32,2048]{1,0:T(8,128)(2,1)S(1)}, bf16[32,2048]{1,0:T(8,128)(2,1)S(1)}, u32[]{:S(2)}, u32[]{:S(2)}) collective-permute-start(bf16[32,2048]{1,0:T(8,128)(2,1)S(1)} %get-tuple-element.96), channel_id=1, source_target_pairs={{2,0},{3,1},{0,2},{1,3},{6,4},{7,5},{4,6},{5,7},{10,8},{11,9},{8,1... | collective-permute-start | bytes 393224 | tf_op jit(solution)/shard_map/ppermute | solution.py:96
  132.6 17.8 %collective-permute-start.28 = (bf16[32,2048]{1,0:T(8,128)(2,1)S(1)}, bf16[32,2048]{1,0:T(8,128)(2,1)S(1)}, u32[]{:S(2)}, u32[]{:S(2)}) collective-permute-start(bf16[32,2048]{1,0:T(8,128)(2,1)S(1)} %get-tuple-element.97), channel_id=1, source_target_pairs={{3,0},{0,1},{1,2},{2,3},{7,4},{4,5},{5,6},{6,7},{11,8},{8,9},{9,10... | collective-permute-start | bytes 393224 | tf_op jit(solution)/shard_map/ppermute | solution.py:96
  145.7 5.0 %collective-permute-start.24 = (bf16[32,2048]{1,0:T(8,128)(2,1)S(1)}, bf16[32,2048]{1,0:T(8,128)(2,1)S(1)}, u32[]{:S(2)}, u32[]{:S(2)}) collective-permute-start(bf16[32,2048]{1,0:T(8,128)(2,1)S(1)} %add_convert_fusion.2), channel_id=1, source_target_pairs={{0,16},{16,0},{1,17},{17,1},{2,18},{18,2},{3,19},{19,3},{4,20},{20... | collective-permute-start | bytes 393224 | tf_op jit(solution)/shard_map/ppermute | solution.py:92

commit v18 on v17

--- a/solution.py
+++ b/solution.py
@@ -397,12 +397,18 @@
 
     line_other = exchange(line, "y")
     hidden_own = hidden_units_of(own, line)
-    line_other, hidden_own, near_x[1] = together(line_other, hidden_own, near_x[1])
+    line_other, hidden_own, near_x[1], far_late = together(
+        line_other, hidden_own, near_x[1], far
+    )
+    far_core = exchange(far_late, "core")
     from_own = exchange(hidden_own, "y")
     hidden_other = hidden_units_of(other, line_other)
-    hidden_other, from_own, far_x = together(hidden_other, from_own, far_x)
+    hidden_other, from_own, far_x, far_core = together(hidden_other, from_own, far_x, far_core)
     from_other = exchange(hidden_other, "y")
-    down_halves = [*both_halves(near, *near_x), *both_halves(far, far_x)]
+    down_halves = [
+        *both_halves(near, *near_x),
+        *staged([far, far_x], [far_core, exchange(far_x, "core")]),
+    ]
 
     def summed_down(hidden, from_y):
         parts = vmem_call(

time: 152 us -> 151 us (level)
    ppermute x14 -> x15, waiting for transfers between devices: 25 us -> 23.6 us  [exchange(): return lax.ppermute(block, axis, [(0, 1), (1, 0)])]
    ppermute x14 -> x15, starting transfers between devices: 13.1 us -> 13.5 us  [exchange(): return lax.ppermute(block, axis, [(0, 1), (1, 0)])]
  transfers between devices with their start and end apart: 29 -> 30, of which waited for: 16 -> 16; matrix products, arithmetic and copies ran while one was open for 2% -> 2% of each run, Pallas kernels for 17% -> 17%
where the time goes in v18:
time: 151 us
  waiting for transfers between devices  79.7 us (53%)
  starting transfers between devices  39.8 us (26%)
  Pallas kernels  27.6 us (18%)
  other arithmetic  3.27 us (2%)
    ppermute x15, waiting for transfers between devices, shift(): return lax.ppermute(block, 'mlp', [((k + hops) % 4, k) for k in range(4)])  56.1 us
    ppermute x15, starting transfers between devices, shift(): return lax.ppermute(block, 'mlp', [((k + hops) % 4, k) for k in range(4)])  26.2 us
    ppermute x15, waiting for transfers between devices, exchange(): return lax.ppermute(block, axis, [(0, 1), (1, 0)])  23.6 us
    pallas_call x5, Pallas kernels, vmem_call(): pl.pallas_call(kernel, out_shape=outs, in_specs=[whole] * len(operands),...  15.5 us
    ppermute x15, starting transfers between devices, exchange(): return lax.ppermute(block, axis, [(0, 1), (1, 0)])  13.5 us
    pallas_call x4, Pallas kernels, staged(): pl.pallas_call(kernel, out_shape=[pltpu.VMEM(shape, group[0][0].dtype) fo...  9.23 us
  transfers between devices with their start and end apart: 30, of which 16 were waited for; matrix products, arithmetic and copies ran while one was open for 2% of the time, Pallas kernels for 17%

profile of v18, /device:TPU:0, one launch (start us, length us, event | category | flops | bytes accessed | tf_op | source)
XLA Modules:
  0.0 150.8 jit_solution(18018707165856247521)
XLA Ops:
  0.0 5.0 %collective-permute-start = (bf16[32,4096]{1,0:T(8,128)(2,1)}, bf16[32,4096]{1,0:T(8,128)(2,1)S(1)}, u32[]{:S(2)}, u32[]{:S(2)}) collective-permute-start(bf16[32,4096]{1,0:T(8,128)(2,1)} %refs_10_.1), channel_id=1, source_target_pairs={{1,0},{2,1},{3,2},{0,3},{5,4},{6,5},{7,6},{4,7},{9,8},{10,9},{11,1... | collective-permute-start | bytes 786440 | tf_op jit(solution)/shard_map/ppermute | solution.py:96
  5.1 1.0 collective-permute-start.2
  6.1 2.8 %shard_map.183 = bf16[384,4096]{1,0:T(8,128)(2,1)} custom-call(bf16[192,4096]{1,0:T(8,128)(2,1)} %bitcast.14, bf16[192,4096]{1,0:T(8,128)(2,1)} %bitcast.16), custom_call_target="tpu_custom_call" | custom-call | bytes 1048576 | tf_op jit(solution)/shard_map/pallas_call | solution.py:219
  8.9 1.6 %collective-permute-start.11 = (bf16[384,4096]{1,0:T(8,128)(2,1)}, bf16[384,4096]{1,0:T(8,128)(2,1)S(1)}, u32[]{:S(2)}, u32[]{:S(2)}) collective-permute-start(bf16[384,4096]{1,0:T(8,128)(2,1)} %shard_map.183), channel_id=1, source_target_pairs={{0,8},{8,0},{1,9},{9,1},{2,10},{10,2},{3,11},{11,3},{4,12},{12,4},... | collective-permute-start | bytes 9437192 | tf_op jit(solution)/shard_map/ppermute | solution.py:92
  10.8 0.3 fusion.4
  11.3 0.5 and_select_fusion
  11.8 6.6 %shard_map.181 = (bf16[4096,512]{1,0:T(8,128)(2,1)S(1)}, bf16[4096,512]{1,0:T(8,128)(2,1)S(1)}, bf16[4096,512]{1,0:T(8,128)(2,1)S(1)}, bf16[512,4096]{1,0:T(8,12...) custom-call(bf16[4096,512]{1,0:T(8,128)(2,1)} %refs_0_.1, ...), custom_call_target="tpu_custom_call" | custom-call | tf_op jit(solution)/shard_map/pallas_call | solution.py:178
  18.6 9.1 %collective-permute-done.1.block_2 = bf16[32,4096]{1,0:T(8,128)(2,1)} collective-permute-done((bf16[32,4096]{1,0:T(8,128)(2,1)}, bf16[32,4096]{1,0:T(8,128)(2,1)}, u32[]{:S(2)}, u32[]{:S(2)}) %collective-permute-start.1) | collective-permute-done | bytes 262176 | tf_op jit(solution)/shard_map/ppermute | solution.py:96
  27.7 5.5 %shard_map.182 = (bf16[32,4096]{1,0:T(8,128)(2,1)S(1)}, bf16[32,4096]{1,0:T(8,128)(2,1)S(1)}, bf16[32,4096]{1,0:T(8,128)(2,1)S(1)}, bf16[32,4096]{1,0:T(8,128)(2,1)S(1)}) custom-call(bf16[32,4096]{1,0:T(8,128)(2,1)S(1)} %get-tuple-element.57.block_0, bf16[32,4096]{1,0:T(8,128)(2,1)S(1)} %collective-permute-done.block_1, ...), custom_call_target="tpu_custom_call" | custom-call | flops 1048576 | bytes 1048576 | tf_op jit(solution)/shard_map/pallas_call | solution.py:128
  33.2 2.9 %collective-permute-start.4 = (bf16[32,4096]{1,0:T(8,128)(2,1)S(1)}, bf16[32,4096]{1,0:T(8,128)(2,1)S(1)}, u32[]{:S(2)}, u32[]{:S(2)}) collective-permute-start(bf16[32,4096]{1,0:T(8,128)(2,1)S(1)} %get-tuple-element.72), channel_id=1, source_target_pairs={{2,0},{3,1},{0,2},{1,3},{6,4},{7,5},{4,6},{5,7},{10,8},{11,9},{8,1... | collective-permute-start | bytes 786440 | tf_op jit(solution)/shard_map/ppermute | solution.py:96
  36.1 1.9 %collective-permute-start.5 = (bf16[32,4096]{1,0:T(8,128)(2,1)S(1)}, bf16[32,4096]{1,0:T(8,128)(2,1)S(1)}, u32[]{:S(2)}, u32[]{:S(2)}) collective-permute-start(bf16[32,4096]{1,0:T(8,128)(2,1)S(1)} %get-tuple-element.73), channel_id=1, source_target_pairs={{3,0},{0,1},{1,2},{2,3},{7,4},{4,5},{5,6},{6,7},{11,8},{8,9},{9,10... | collective-permute-start | bytes 786440 | tf_op jit(solution)/shard_map/ppermute | solution.py:96
  38.2 1.6 %collective-permute-start.6 = (bf16[192,2048]{1,0:T(8,128)(2,1)S(1)}, bf16[192,2048]{1,0:T(8,128)(2,1)S(1)}, u32[]{:S(2)}, u32[]{:S(2)}) collective-permute-start(bf16[192,2048]{1,0:T(8,128)(2,1)S(1)} %get-tuple-element.112), channel_id=1, source_target_pairs={{0,16},{16,0},{1,17},{17,1},{2,18},{18,2},{3,19},{19,3},{4,20},{20... | collective-permute-start | bytes 2359304 | tf_op jit(solution)/shard_map/ppermute | solution.py:92
  39.8 0.8 collective-permute-done.3
  40.6 18.0 %collective-permute-done.4 = bf16[32,4096]{1,0:T(8,128)(2,1)S(1)} collective-permute-done((bf16[32,4096]{1,0:T(8,128)(2,1)S(1)}, bf16[32,4096]{1,0:T(8,128)(2,1)S(1)}, u32[]{:S(2)}, u32[]{:S(2)}) %collective-permute-start.4) | collective-permute-done | bytes 262176 | tf_op jit(solution)/shard_map/ppermute | solution.py:96
  59.0 1.6 %collective-permute-start.10 = (bf16[32,4096]{1,0:T(8,128)(2,1)S(1)}, bf16[32,4096]{1,0:T(8,128)(2,1)S(1)}, u32[]{:S(2)}, u32[]{:S(2)}) collective-permute-start(bf16[32,4096]{1,0:T(8,128)(2,1)S(1)} %add_convert_fusion.1), channel_id=1, source_target_pairs={{0,16},{16,0},{1,17},{17,1},{2,18},{18,2},{3,19},{19,3},{4,20},{20... | collective-permute-start | bytes 786440 | tf_op jit(solution)/shard_map/ppermute | solution.py:92
  60.6 2.0 %collective-permute-start.9 = (bf16[32,4096]{1,0:T(8,128)(2,1)S(1)}, bf16[32,4096]{1,0:T(8,128)(2,1)S(1)}, u32[]{:S(2)}, u32[]{:S(2)}) collective-permute-start(bf16[32,4096]{1,0:T(8,128)(2,1)S(1)} %add_convert_fusion.1), channel_id=1, source_target_pairs={{3,0},{0,1},{1,2},{2,3},{7,4},{4,5},{5,6},{6,7},{11,8},{8,9},{9,10... | collective-permute-start | bytes 786440 | tf_op jit(solution)/shard_map/ppermute | solution.py:96
  62.7 3.2 %collective-permute-done.10 = bf16[32,4096]{1,0:T(8,128)(2,1)S(1)} collective-permute-done((bf16[32,4096]{1,0:T(8,128)(2,1)S(1)}, bf16[32,4096]{1,0:T(8,128)(2,1)S(1)}, u32[]{:S(2)}, u32[]{:S(2)}) %collective-permute-start.10) | collective-permute-done | bytes 262176 | tf_op jit(solution)/shard_map/ppermute | solution.py:92
  65.9 1.5 collective-permute-start.12
  67.4 0.5 collective-permute-done.7
  67.9 15.7 %collective-permute-done.8 = bf16[32,4096]{1,0:T(8,128)(2,1)S(1)} collective-permute-done((bf16[32,4096]{1,0:T(8,128)(2,1)S(1)}, bf16[32,4096]{1,0:T(8,128)(2,1)S(1)}, u32[]{:S(2)}, u32[]{:S(2)}) %collective-permute-start.8) | collective-permute-done | bytes 262176 | tf_op jit(solution)/shard_map/ppermute | solution.py:96
  83.6 3.0 %collective-permute-done.12.refs_1_ = bf16[96,2048]{1,0:T(8,128)(2,1)S(1)} collective-permute-done((bf16[96,2048]{1,0:T(8,128)(2,1)S(1)}, bf16[96,2048]{1,0:T(8,128)(2,1)S(1)}, u32[]{:S(2)}, u32[]{:S(2)}) %collective-permute-start.12) | collective-permute-done | bytes 393248 | tf_op jit(solution)/shard_map/ppermute | solution.py:92
  86.6 1.9 %shard_map.184 = (bf16[384,4096]{1,0:T(8,128)(2,1)S(1)}, bf16[384,4096]{1,0:T(8,128)(2,1)S(1)}) custom-call(bf16[192,4096]{1,0:T(8,128)(2,1)} %bitcast.15, bf16[384,4096]{1,0:T(8,128)(2,1)S(1)} %collective-permute-done.11.refs_1_, bf16[192,4096]{1,0:T(8,128)(2,1)} %bitcast.17), custom_call_target="tpu_custom_call" | custom-call | bytes 12582912 | tf_op jit(solution)/shard_map/pallas_call | solution.py:178
  88.6 0.5 collective-permute-start.15
  89.1 1.5 %collective-permute-start.13 = (bf16[96,4096]{1,0:T(8,128)(2,1)S(1)}, bf16[96,4096]{1,0:T(8,128)(2,1)S(1)}, u32[]{:S(2)}, u32[]{:S(2)}) collective-permute-start(bf16[96,4096]{1,0:T(8,128)(2,1)S(1)} %pad_maximum_fusion.2), channel_id=1, source_target_pairs={{0,16},{16,0},{1,17},{17,1},{2,18},{18,2},{3,19},{19,3},{4,20},{20... | collective-permute-start | bytes 2359304 | tf_op jit(solution)/shard_map/ppermute | solution.py:92
  90.7 1.5 collective-permute-start.16
  92.2 0.5 collective-permute-start.18
  92.8 1.5 %collective-permute-done.14.gate_1 = bf16[384,4096]{1,0:T(8,128)(2,1)S(1)} collective-permute-done((bf16[384,4096]{1,0:T(8,128)(2,1)S(1)}, bf16[384,4096]{1,0:T(8,128)(2,1)S(1)}, u32[]{:S(2)}, u32[]{:S(2)}) %collective-permute-start.14) | collective-permute-done | bytes 3145760 | tf_op jit(solution)/shard_map/ppermute | solution.py:92
  94.3 4.5 %collective-permute-done.15.up_1 = bf16[384,4096]{1,0:T(8,128)(2,1)S(1)} collective-permute-done((bf16[384,4096]{1,0:T(8,128)(2,1)S(1)}, bf16[384,4096]{1,0:T(8,128)(2,1)S(1)}, u32[]{:S(2)}, u32[]{:S(2)}) %collective-permute-start.15) | collective-permute-done | bytes 3145760 | tf_op jit(solution)/shard_map/ppermute | solution.py:92
  98.8 3.8 %shard_map.185.near = bf16[128,768]{1,0:T(8,128)(2,1)S(1)} custom-call(bf16[128,4096]{1,0:T(8,128)(2,1)S(1)} %pad_maximum_fusion.states, bf16[384,4096]{1,0:T(8,128)(2,1)S(1)} %get-tuple-element.85.gate_0, bf16[384,4096]{1,0:T(8,128)(2,1)S(1)} %collective-permute-done.14.gate_1, bf16[384,4096]{1,0:T(8,128)(2,1)S(1)} %get-tuple-element.86.up_0, ...), custom_call_target="tpu_custom_call" | custom-call | flops 1048576 | bytes 1048576 | tf_op jit(solution)/shard_map/pallas_call | solution.py:128
  102.7 6.0 %collective-permute-done.13 = bf16[96,4096]{1,0:T(8,128)(2,1)S(1)} collective-permute-done((bf16[96,4096]{1,0:T(8,128)(2,1)S(1)}, bf16[96,4096]{1,0:T(8,128)(2,1)S(1)}, u32[]{:S(2)}, u32[]{:S(2)}) %collective-permute-start.13) | collective-permute-done | bytes 786464 | tf_op jit(solution)/shard_map/ppermute | solution.py:92
  108.7 0.5 shard_map.187.near_0
  109.1 0.6 collective-permute-start.20
  109.7 1.5 %collective-permute-start.17 = (bf16[128,768]{1,0:T(8,128)(2,1)S(1)}, bf16[128,768]{1,0:T(8,128)(2,1)S(1)}, u32[]{:S(2)}, u32[]{:S(2)}) collective-permute-start(bf16[128,768]{1,0:T(8,128)(2,1)S(1)} %shard_map.185.near), channel_id=1, source_target_pairs={{0,16},{16,0},{1,17},{17,1},{2,18},{18,2},{3,19},{19,3},{4,20},{20... | collective-permute-start | bytes 589832 | tf_op jit(solution)/shard_map/ppermute | solution.py:92
  111.3 3.8 %shard_map.186.near = bf16[128,768]{1,0:T(8,128)(2,1)S(1)} custom-call(bf16[128,4096]{1,0:T(8,128)(2,1)S(1)} %pad_maximum_fusion.1.states, bf16[384,4096]{1,0:T(8,128)(2,1)S(1)} %get-tuple-element.85.gate_0, bf16[384,4096]{1,0:T(8,128)(2,1)S(1)} %collective-permute-done.14.gate_1, bf16[384,4096]{1,0:T(8,128)(2,1)S(1)} %get-tuple-element.86.up_0, ...), custom_call_target="tpu_custom_call" | custom-call | flops 1048576 | bytes 1048576 | tf_op jit(solution)/shard_map/pallas_call | solution.py:128
  115.1 3.2 %collective-permute-done.18.refs_1_ = bf16[192,2048]{1,0:T(8,128)(2,1)S(1)} collective-permute-done((bf16[192,2048]{1,0:T(8,128)(2,1)S(1)}, bf16[192,2048]{1,0:T(8,128)(2,1)S(1)}, u32[]{:S(2)}, u32[]{:S(2)}) %collective-permute-start.18) | collective-permute-done | bytes 786464 | tf_op jit(solution)/shard_map/ppermute | solution.py:92
  118.3 0.6 collective-permute-start.26
  118.9 1.7 %collective-permute-done.21.refs_3_ = bf16[192,2048]{1,0:T(8,128)(2,1)S(1)} collective-permute-done((bf16[192,2048]{1,0:T(8,128)(2,1)S(1)}, bf16[192,2048]{1,0:T(8,128)(2,1)S(1)}, u32[]{:S(2)}, u32[]{:S(2)}) %collective-permute-start.21) | collective-permute-done | bytes 786464 | tf_op jit(solution)/shard_map/ppermute | solution.py:92
  120.9 1.3 shard_map.189
  122.2 3.1 %collective-permute-start.22 = (bf16[32,2048]{1,0:T(8,128)(2,1)S(1)}, bf16[32,2048]{1,0:T(8,128)(2,1)S(1)}, u32[]{:S(2)}, u32[]{:S(2)}) collective-permute-start(bf16[32,2048]{1,0:T(8,128)(2,1)S(1)} %get-tuple-element.99), channel_id=1, source_target_pairs={{1,0},{2,1},{3,2},{0,3},{5,4},{6,5},{7,6},{4,7},{9,8},{10,9},{11,1... | collective-permute-start | bytes 393224 | tf_op jit(solution)/shard_map/ppermute | solution.py:96
  125.3 0.9 collective-permute-start.23
  126.5 1.3 shard_map.190
  127.8 3.6 %collective-permute-start.27 = (bf16[32,2048]{1,0:T(8,128)(2,1)S(1)}, bf16[32,2048]{1,0:T(8,128)(2,1)S(1)}, u32[]{:S(2)}, u32[]{:S(2)}) collective-permute-start(bf16[32,2048]{1,0:T(8,128)(2,1)S(1)} %get-tuple-element.103), channel_id=1, source_target_pairs={{1,0},{2,1},{3,2},{0,3},{5,4},{6,5},{7,6},{4,7},{9,8},{10,9},{11,1... | collective-permute-start | bytes 393224 | tf_op jit(solution)/shard_map/ppermute | solution.py:96
  131.6 5.1 %collective-permute-start.29 = (bf16[32,2048]{1,0:T(8,128)(2,1)S(1)}, bf16[32,2048]{1,0:T(8,128)(2,1)S(1)}, u32[]{:S(2)}, u32[]{:S(2)}) collective-permute-start(bf16[32,2048]{1,0:T(8,128)(2,1)S(1)} %get-tuple-element.105), channel_id=1, source_target_pairs={{3,0},{0,1},{1,2},{2,3},{7,4},{4,5},{5,6},{6,7},{11,8},{8,9},{9,10... | collective-permute-start | bytes 393224 | tf_op jit(solution)/shard_map/ppermute | solution.py:96
  136.7 7.9 %collective-permute-done.23 = bf16[32,2048]{1,0:T(8,128)(2,1)S(1)} collective-permute-done((bf16[32,2048]{1,0:T(8,128)(2,1)S(1)}, bf16[32,2048]{1,0:T(8,128)(2,1)S(1)}, u32[]{:S(2)}, u32[]{:S(2)}) %collective-permute-start.23) | collective-permute-done | bytes 131104 | tf_op jit(solution)/shard_map/ppermute | solution.py:96
  144.7 0.5 collective-permute-start.25
  145.2 4.2 %collective-permute-done.28 = bf16[32,2048]{1,0:T(8,128)(2,1)S(1)} collective-permute-done((bf16[32,2048]{1,0:T(8,128)(2,1)S(1)}, bf16[32,2048]{1,0:T(8,128)(2,1)S(1)}, u32[]{:S(2)}, u32[]{:S(2)}) %collective-permute-start.28) | collective-permute-done | bytes 131104 | tf_op jit(solution)/shard_map/ppermute | solution.py:96
  149.4 0.3 collective-permute-done.25
  150.0 0.9 add_convert_fusion
  (64 shorter events, 3.0 us)
Async XLA Ops:
  0.0 18.5 %collective-permute-start = (bf16[32,4096]{1,0:T(8,128)(2,1)}, bf16[32,4096]{1,0:T(8,128)(2,1)S(1)}, u32[]{:S(2)}, u32[]{:S(2)}) collective-permute-start(bf16[32,4096]{1,0:T(8,128)(2,1)} %refs_10_.1), channel_id=1, source_target_pairs={{1,0},{2,1},{3,2},{0,3},{5,4},{6,5},{7,6},{4,7},{9,8},{10,9},{11,1... | collective-permute-start | bytes 786440 | tf_op jit(solution)/shard_map/ppermute | solution.py:96
  5.0 22.6 %collective-permute-start.1 = (bf16[32,4096]{1,0:T(8,128)(2,1)}, bf16[32,4096]{1,0:T(8,128)(2,1)}, u32[]{:S(2)}, u32[]{:S(2)}) collective-permute-start(bf16[32,4096]{1,0:T(8,128)(2,1)} %refs_10_.1), channel_id=1, source_target_pairs={{2,0},{3,1},{0,2},{1,3},{6,4},{7,5},{4,6},{5,7},{10,8},{11,9},{8,1... | collective-permute-start | bytes 786440 | tf_op jit(solution)/shard_map/ppermute | solution.py:96
  5.1 22.6 %collective-permute-start.2 = (bf16[32,4096]{1,0:T(8,128)(2,1)}, bf16[32,4096]{1,0:T(8,128)(2,1)}, u32[]{:S(2)}, u32[]{:S(2)}) collective-permute-start(bf16[32,4096]{1,0:T(8,128)(2,1)} %refs_10_.1), channel_id=1, source_target_pairs={{3,0},{0,1},{1,2},{2,3},{7,4},{4,5},{5,6},{6,7},{11,8},{8,9},{9,10... | collective-permute-start | bytes 786440 | tf_op jit(solution)/shard_map/ppermute | solution.py:96
  6.1 4.4 %copy-start.6 = (s32[1,4]{1,0:T(1,128)S(1)}, s32[1,4]{1,0:T(1,128)}, u32[]{:S(2)}) copy-start(s32[1,4]{1,0:T(1,128)} %param.20) | copy-start | bytes 52
  6.1 4.6 %copy-start.5 = (s32[1,4]{1,0:T(1,128)S(1)}, s32[1,4]{1,0:T(1,128)}, u32[]{:S(2)}) copy-start(s32[1,4]{1,0:T(1,128)} %param.21) | copy-start | bytes 52
  6.1 5.0 %copy-start.7 = (s32[8]{0:T(128)S(1)}, s32[8]{0:T(128)}, u32[]{:S(2)}) copy-start(s32[8]{0:T(128)} %param.22) | copy-start | bytes 100
  8.9 77.7 %collective-permute-start.11 = (bf16[384,4096]{1,0:T(8,128)(2,1)}, bf16[384,4096]{1,0:T(8,128)(2,1)S(1)}, u32[]{:S(2)}, u32[]{:S(2)}) collective-permute-start(bf16[384,4096]{1,0:T(8,128)(2,1)} %shard_map.183), channel_id=1, source_target_pairs={{0,8},{8,0},{1,9},{9,1},{2,10},{10,2},{3,11},{11,3},{4,12},{12,4},... | collective-permute-start | bytes 9437192 | tf_op jit(solution)/shard_map/ppermute | solution.py:92
  11.8 6.6 %copy-start.4 = (s32[128]{0:T(128)S(1)}, s32[128]{0:T(128)}, u32[]{:S(2)}) copy-start(s32[128]{0:T(128)} %and_select_fusion) | copy-start | bytes 1540
  27.7 10.4 %copy-start = (bf16[4096,192]{0,1:T(8,128)(2,1)S(1)}, bf16[4096,192]{0,1:T(8,128)(2,1)}, u32[]{:S(2)}) copy-start(bf16[4096,192]{0,1:T(8,128)(2,1)} %param.37) | copy-start | bytes 4718596
  33.2 7.4 %collective-permute-start.3 = (bf16[32,4096]{1,0:T(8,128)(2,1)S(1)}, bf16[32,4096]{1,0:T(8,128)(2,1)S(1)}, u32[]{:S(2)}, u32[]{:S(2)}) collective-permute-start(bf16[32,4096]{1,0:T(8,128)(2,1)S(1)} %get-tuple-element.71), channel_id=1, source_target_pairs={{1,0},{2,1},{3,2},{0,3},{5,4},{6,5},{7,6},{4,7},{9,8},{10,9},{11,1... | collective-permute-start | bytes 786440 | tf_op jit(solution)/shard_map/ppermute | solution.py:96
  33.2 25.3 %collective-permute-start.4 = (bf16[32,4096]{1,0:T(8,128)(2,1)S(1)}, bf16[32,4096]{1,0:T(8,128)(2,1)S(1)}, u32[]{:S(2)}, u32[]{:S(2)}) collective-permute-start(bf16[32,4096]{1,0:T(8,128)(2,1)S(1)} %get-tuple-element.72), channel_id=1, source_target_pairs={{2,0},{3,1},{0,2},{1,3},{6,4},{7,5},{4,6},{5,7},{10,8},{11,9},{8,1... | collective-permute-start | bytes 786440 | tf_op jit(solution)/shard_map/ppermute | solution.py:96
  36.1 22.8 %copy-start.1 = (bf16[32,4096]{1,0:T(8,128)(2,1)S(1)}, bf16[32,4096]{1,0:T(8,128)(2,1)}, u32[]{:S(2)}) copy-start(bf16[32,4096]{1,0:T(8,128)(2,1)} %refs_10_.1) | copy-start | bytes 786436
  36.1 22.8 %copy-start.2 = (f32[4096]{0:T(1024)S(1)}, f32[4096]{0:T(1024)}, u32[]{:S(2)}) copy-start(f32[4096]{0:T(1024)} %param.33) | copy-start | bytes 49156
  36.1 22.5 %collective-permute-start.5 = (bf16[32,4096]{1,0:T(8,128)(2,1)S(1)}, bf16[32,4096]{1,0:T(8,128)(2,1)S(1)}, u32[]{:S(2)}, u32[]{:S(2)}) collective-permute-start(bf16[32,4096]{1,0:T(8,128)(2,1)S(1)} %get-tuple-element.73), channel_id=1, source_target_pairs={{3,0},{0,1},{1,2},{2,3},{7,4},{4,5},{5,6},{6,7},{11,8},{8,9},{9,10... | collective-permute-start | bytes 786440 | tf_op jit(solution)/shard_map/ppermute | solution.py:96
  38.2 20.5 %collective-permute-start.6 = (bf16[192,2048]{1,0:T(8,128)(2,1)S(1)}, bf16[192,2048]{1,0:T(8,128)(2,1)S(1)}, u32[]{:S(2)}, u32[]{:S(2)}) collective-permute-start(bf16[192,2048]{1,0:T(8,128)(2,1)S(1)} %get-tuple-element.112), channel_id=1, source_target_pairs={{0,16},{16,0},{1,17},{17,1},{2,18},{18,2},{3,19},{19,3},{4,20},{20... | collective-permute-start | bytes 2359304 | tf_op jit(solution)/shard_map/ppermute | solution.py:92
  59.0 6.9 %collective-permute-start.10 = (bf16[32,4096]{1,0:T(8,128)(2,1)S(1)}, bf16[32,4096]{1,0:T(8,128)(2,1)S(1)}, u32[]{:S(2)}, u32[]{:S(2)}) collective-permute-start(bf16[32,4096]{1,0:T(8,128)(2,1)S(1)} %add_convert_fusion.1), channel_id=1, source_target_pairs={{0,16},{16,0},{1,17},{17,1},{2,18},{18,2},{3,19},{19,3},{4,20},{20... | collective-permute-start | bytes 786440 | tf_op jit(solution)/shard_map/ppermute | solution.py:92
  60.6 7.3 %collective-permute-start.7 = (bf16[32,4096]{1,0:T(8,128)(2,1)S(1)}, bf16[32,4096]{1,0:T(8,128)(2,1)S(1)}, u32[]{:S(2)}, u32[]{:S(2)}) collective-permute-start(bf16[32,4096]{1,0:T(8,128)(2,1)S(1)} %add_convert_fusion.1), channel_id=1, source_target_pairs={{1,0},{2,1},{3,2},{0,3},{5,4},{6,5},{7,6},{4,7},{9,8},{10,9},{11,1... | collective-permute-start | bytes 786440 | tf_op jit(solution)/shard_map/ppermute | solution.py:96
  60.6 22.9 %collective-permute-start.8 = (bf16[32,4096]{1,0:T(8,128)(2,1)S(1)}, bf16[32,4096]{1,0:T(8,128)(2,1)S(1)}, u32[]{:S(2)}, u32[]{:S(2)}) collective-permute-start(bf16[32,4096]{1,0:T(8,128)(2,1)S(1)} %add_convert_fusion.1), channel_id=1, source_target_pairs={{2,0},{3,1},{0,2},{1,3},{6,4},{7,5},{4,6},{5,7},{10,8},{11,9},{8,1... | collective-permute-start | bytes 786440 | tf_op jit(solution)/shard_map/ppermute | solution.py:96
  60.6 22.9 %collective-permute-start.9 = (bf16[32,4096]{1,0:T(8,128)(2,1)S(1)}, bf16[32,4096]{1,0:T(8,128)(2,1)S(1)}, u32[]{:S(2)}, u32[]{:S(2)}) collective-permute-start(bf16[32,4096]{1,0:T(8,128)(2,1)S(1)} %add_convert_fusion.1), channel_id=1, source_target_pairs={{3,0},{0,1},{1,2},{2,3},{7,4},{4,5},{5,6},{6,7},{11,8},{8,9},{9,10... | collective-permute-start | bytes 786440 | tf_op jit(solution)/shard_map/ppermute | solution.py:96
  65.9 20.7 %collective-permute-start.12 = (bf16[96,2048]{1,0:T(8,128)(2,1)S(1)}, bf16[96,2048]{1,0:T(8,128)(2,1)S(1)}, u32[]{:S(2)}, u32[]{:S(2)}) collective-permute-start(bf16[96,2048]{1,0:T(8,128)(2,1)S(1)} %get-tuple-element.115), channel_id=1, source_target_pairs={{0,8},{8,0},{1,9},{9,1},{2,10},{10,2},{3,11},{11,3},{4,12},{12,4},... | collective-permute-start | bytes 1179656 | tf_op jit(solution)/shard_map/ppermute | solution.py:92
  88.6 5.7 %collective-permute-start.14 = (bf16[384,4096]{1,0:T(8,128)(2,1)S(1)}, bf16[384,4096]{1,0:T(8,128)(2,1)S(1)}, u32[]{:S(2)}, u32[]{:S(2)}) collective-permute-start(bf16[384,4096]{1,0:T(8,128)(2,1)S(1)} %get-tuple-element.85.gate_0), channel_id=1, source_target_pairs={{0,4},{4,0},{1,5},{5,1},{2,6},{6,2},{3,7},{7,3},{8,12},{12,8},{9,1... | collective-permute-start | bytes 9437192 | tf_op jit(solution)/shard_map/ppermute | solution.py:92
  88.6 10.1 %collective-permute-start.15 = (bf16[384,4096]{1,0:T(8,128)(2,1)S(1)}, bf16[384,4096]{1,0:T(8,128)(2,1)S(1)}, u32[]{:S(2)}, u32[]{:S(2)}) collective-permute-start(bf16[384,4096]{1,0:T(8,128)(2,1)S(1)} %get-tuple-element.86.up_0), channel_id=1, source_target_pairs={{0,4},{4,0},{1,5},{5,1},{2,6},{6,2},{3,7},{7,3},{8,12},{12,8},{9,1... | collective-permute-start | bytes 9437192 | tf_op jit(solution)/shard_map/ppermute | solution.py:92
  89.1 19.5 %collective-permute-start.13 = (bf16[96,4096]{1,0:T(8,128)(2,1)S(1)}, bf16[96,4096]{1,0:T(8,128)(2,1)S(1)}, u32[]{:S(2)}, u32[]{:S(2)}) collective-permute-start(bf16[96,4096]{1,0:T(8,128)(2,1)S(1)} %pad_maximum_fusion.2), channel_id=1, source_target_pairs={{0,16},{16,0},{1,17},{17,1},{2,18},{18,2},{3,19},{19,3},{4,20},{20... | collective-permute-start | bytes 2359304 | tf_op jit(solution)/shard_map/ppermute | solution.py:92
  90.7 12.0 %collective-permute-start.16 = (bf16[96,2048]{1,0:T(8,128)(2,1)S(1)}, bf16[96,2048]{1,0:T(8,128)(2,1)S(1)}, u32[]{:S(2)}, u32[]{:S(2)}) collective-permute-start(bf16[96,2048]{1,0:T(8,128)(2,1)S(1)} %get-tuple-element.114), channel_id=1, source_target_pairs={{0,8},{8,0},{1,9},{9,1},{2,10},{10,2},{3,11},{11,3},{4,12},{12,4},... | collective-permute-start | bytes 1179656 | tf_op jit(solution)/shard_map/ppermute | solution.py:92
  92.2 26.2 %collective-permute-start.18 = (bf16[192,2048]{1,0:T(8,128)(2,1)S(1)}, bf16[192,2048]{1,0:T(8,128)(2,1)S(1)}, u32[]{:S(2)}, u32[]{:S(2)}) collective-permute-start(bf16[192,2048]{1,0:T(8,128)(2,1)S(1)} %collective-permute-done.6.refs_0_), channel_id=1, source_target_pairs={{0,8},{8,0},{1,9},{9,1},{2,10},{10,2},{3,11},{11,3},{4,12},{12,4},... | collective-permute-start | bytes 2359304 | tf_op jit(solution)/shard_map/ppermute | solution.py:92
  108.7 9.7 %collective-permute-start.19 = (bf16[192,2048]{1,0:T(8,128)(2,1)S(1)}, bf16[192,2048]{1,0:T(8,128)(2,1)S(1)}, u32[]{:S(2)}, u32[]{:S(2)}) collective-permute-start(bf16[192,2048]{1,0:T(8,128)(2,1)S(1)} %collective-permute-done.6.refs_0_), channel_id=1, source_target_pairs={{0,4},{4,0},{1,5},{5,1},{2,6},{6,2},{3,7},{7,3},{8,12},{12,8},{9,1... | collective-permute-start | bytes 2359304 | tf_op jit(solution)/shard_map/ppermute | solution.py:92
  109.1 11.8 %collective-permute-start.20 = (bf16[384,2048]{1,0:T(8,128)(2,1)S(1)}, bf16[384,2048]{1,0:T(8,128)(2,1)S(1)}, u32[]{:S(2)}, u32[]{:S(2)}) collective-permute-start(bf16[384,2048]{1,0:T(8,128)(2,1)S(1)} %shard_map.187.near_0), channel_id=1, source_target_pairs={{0,4},{4,0},{1,5},{5,1},{2,6},{6,2},{3,7},{7,3},{8,12},{12,8},{9,1... | collective-permute-start | bytes 4718600 | tf_op jit(solution)/shard_map/ppermute | solution.py:92
  109.7 8.6 %collective-permute-start.17 = (bf16[128,768]{1,0:T(8,128)(2,1)S(1)}, bf16[128,768]{1,0:T(8,128)(2,1)S(1)}, u32[]{:S(2)}, u32[]{:S(2)}) collective-permute-start(bf16[128,768]{1,0:T(8,128)(2,1)S(1)} %shard_map.185.near), channel_id=1, source_target_pairs={{0,16},{16,0},{1,17},{17,1},{2,18},{18,2},{3,19},{19,3},{4,20},{20... | collective-permute-start | bytes 589832 | tf_op jit(solution)/shard_map/ppermute | solution.py:92
  118.3 2.3 %collective-permute-start.21 = (bf16[192,2048]{1,0:T(8,128)(2,1)S(1)}, bf16[192,2048]{1,0:T(8,128)(2,1)S(1)}, u32[]{:S(2)}, u32[]{:S(2)}) collective-permute-start(bf16[192,2048]{1,0:T(8,128)(2,1)S(1)} %collective-permute-done.18.refs_1_), channel_id=1, source_target_pairs={{0,4},{4,0},{1,5},{5,1},{2,6},{6,2},{3,7},{7,3},{8,12},{12,8},{9,1... | collective-permute-start | bytes 2359304 | tf_op jit(solution)/shard_map/ppermute | solution.py:92
  118.3 8.1 %collective-permute-start.26 = (bf16[128,768]{1,0:T(8,128)(2,1)S(1)}, bf16[128,768]{1,0:T(8,128)(2,1)S(1)}, u32[]{:S(2)}, u32[]{:S(2)}) collective-permute-start(bf16[128,768]{1,0:T(8,128)(2,1)S(1)} %shard_map.186.near), channel_id=1, source_target_pairs={{0,16},{16,0},{1,17},{17,1},{2,18},{18,2},{3,19},{19,3},{4,20},{20... | collective-permute-start | bytes 589832 | tf_op jit(solution)/shard_map/ppermute | solution.py:92
  122.2 9.4 %collective-permute-start.22 = (bf16[32,2048]{1,0:T(8,128)(2,1)S(1)}, bf16[32,2048]{1,0:T(8,128)(2,1)S(1)}, u32[]{:S(2)}, u32[]{:S(2)}) collective-permute-start(bf16[32,2048]{1,0:T(8,128)(2,1)S(1)} %get-tuple-element.99), channel_id=1, source_target_pairs={{1,0},{2,1},{3,2},{0,3},{5,4},{6,5},{7,6},{4,7},{9,8},{10,9},{11,1... | collective-permute-start | bytes 393224 | tf_op jit(solution)/shard_map/ppermute | solution.py:96
  125.3 19.3 %collective-permute-start.23 = (bf16[32,2048]{1,0:T(8,128)(2,1)S(1)}, bf16[32,2048]{1,0:T(8,128)(2,1)S(1)}, u32[]{:S(2)}, u32[]{:S(2)}) collective-permute-start(bf16[32,2048]{1,0:T(8,128)(2,1)S(1)} %get-tuple-element.100), channel_id=1, source_target_pairs={{2,0},{3,1},{0,2},{1,3},{6,4},{7,5},{4,6},{5,7},{10,8},{11,9},{8,1... | collective-permute-start | bytes 393224 | tf_op jit(solution)/shard_map/ppermute | solution.py:96
  126.2 18.4 %collective-permute-start.24 = (bf16[32,2048]{1,0:T(8,128)(2,1)S(1)}, bf16[32,2048]{1,0:T(8,128)(2,1)S(1)}, u32[]{:S(2)}, u32[]{:S(2)}) collective-permute-start(bf16[32,2048]{1,0:T(8,128)(2,1)S(1)} %get-tuple-element.101), channel_id=1, source_target_pairs={{3,0},{0,1},{1,2},{2,3},{7,4},{4,5},{5,6},{6,7},{11,8},{8,9},{9,10... | collective-permute-start | bytes 393224 | tf_op jit(solution)/shard_map/ppermute | solution.py:96
  127.7 22.2 %copy-start.3 = (f32[4096]{0:T(1024)S(1)}, f32[4096]{0:T(1024)}, u32[]{:S(2)}) copy-start(f32[4096]{0:T(1024)} %param.34) | copy-start | bytes 49156
  127.8 17.5 %collective-permute-start.27 = (bf16[32,2048]{1,0:T(8,128)(2,1)S(1)}, bf16[32,2048]{1,0:T(8,128)(2,1)S(1)}, u32[]{:S(2)}, u32[]{:S(2)}) collective-permute-start(bf16[32,2048]{1,0:T(8,128)(2,1)S(1)} %get-tuple-element.103), channel_id=1, source_target_pairs={{1,0},{2,1},{3,2},{0,3},{5,4},{6,5},{7,6},{4,7},{9,8},{10,9},{11,1... | collective-permute-start | bytes 393224 | tf_op jit(solution)/shard_map/ppermute | solution.py:96
  131.3 18.0 %collective-permute-start.28 = (bf16[32,2048]{1,0:T(8,128)(2,1)S(1)}, bf16[32,2048]{1,0:T(8,128)(2,1)S(1)}, u32[]{:S(2)}, u32[]{:S(2)}) collective-permute-start(bf16[32,2048]{1,0:T(8,128)(2,1)S(1)} %get-tuple-element.104), channel_id=1, source_target_pairs={{2,0},{3,1},{0,2},{1,3},{6,4},{7,5},{4,6},{5,7},{10,8},{11,9},{8,1... | collective-permute-start | bytes 393224 | tf_op jit(solution)/shard_map/ppermute | solution.py:96
  131.6 17.8 %collective-permute-start.29 = (bf16[32,2048]{1,0:T(8,128)(2,1)S(1)}, bf16[32,2048]{1,0:T(8,128)(2,1)S(1)}, u32[]{:S(2)}, u32[]{:S(2)}) collective-permute-start(bf16[32,2048]{1,0:T(8,128)(2,1)S(1)} %get-tuple-element.105), channel_id=1, source_target_pairs={{3,0},{0,1},{1,2},{2,3},{7,4},{4,5},{5,6},{6,7},{11,8},{8,9},{9,10... | collective-permute-start | bytes 393224 | tf_op jit(solution)/shard_map/ppermute | solution.py:96
  144.7 5.0 %collective-permute-start.25 = (bf16[32,2048]{1,0:T(8,128)(2,1)S(1)}, bf16[32,2048]{1,0:T(8,128)(2,1)S(1)}, u32[]{:S(2)}, u32[]{:S(2)}) collective-permute-start(bf16[32,2048]{1,0:T(8,128)(2,1)S(1)} %add_convert_fusion.2), channel_id=1, source_target_pairs={{0,16},{16,0},{1,17},{17,1},{2,18},{18,2},{3,19},{19,3},{4,20},{20... | collective-permute-start | bytes 393224 | tf_op jit(solution)/shard_map/ppermute | solution.py:92
